TPU v7x, 32 devices: a whole 2x2x4 slice. The times are simulated.
32 devices in a mesh: dp: 8 (over y, x, core), fsdp: 4 (over z).
Axes of the slice: x: 2, y: 2, z: 4, core: 2. Of those that a mesh axis runs over, the one named last changes fastest.
Arguments:
- tokens: bfloat16 [8, 1024, 960], P('dp', 'fsdp'), may hold values from -6 to 6
- segment_ids: int32 [8, 1024], P('dp', 'fsdp'), may hold values from 0 to 7, never falling along the last dimension, each value on 1 to 512 neighbouring positions
- attn_gain: bfloat16 [960], P('fsdp'), may hold values from 0.5 to 1.5
- query_weight: bfloat16 [960, 960], P('fsdp'), may hold values from -0.1875 to 0.1875
- key_weight: bfloat16 [960, 320], P('fsdp'), may hold values from -0.1875 to 0.1875
- value_weight: bfloat16 [960, 320], P('fsdp'), may hold values from -0.1875 to 0.1875
- out_weight: bfloat16 [960, 960], P('fsdp'), may hold values from -0.75 to 0.75
- ffn_gain: bfloat16 [960], P('fsdp'), may hold values from 0.5 to 1.5
- gate_weight: bfloat16 [960, 2560], P('fsdp'), may hold values from -0.1875 to 0.1875
- up_weight: bfloat16 [960, 2560], P('fsdp'), may hold values from -0.1875 to 0.1875
- down_weight: bfloat16 [2560, 960], P('fsdp'), may hold values from -0.125 to 0.125
- cotangent: bfloat16 [8, 1024, 960], P('dp', 'fsdp'), may hold values from -6 to 6
Outputs:
- output: bfloat16 [8, 1024, 960], P('dp', 'fsdp')
- grad_tokens: float32 [8, 1024, 960], P('dp', 'fsdp')
- grad_attn_gain: float32 [960], P('fsdp')
- grad_query: float32 [960, 960], P('fsdp')
- grad_key: float32 [960, 320], P('fsdp')
- grad_value: float32 [960, 320], P('fsdp')
- grad_out: float32 [960, 960], P('fsdp')
- grad_ffn_gain: float32 [960], P('fsdp')
- grad_gate: float32 [960, 2560], P('fsdp')
- grad_up: float32 [960, 2560], P('fsdp')
- grad_down: float32 [2560, 960], P('fsdp')
Inputs may be any that keep to these rules, and one draw needn't show every extreme that they name: `segment_ids`: along each row the ids never fall; each document spans 1 to 512 positions, and one document of each row spans exactly 512.
All inputs are finite; a program needn't handle non-finite values.
Results may differ from a plain program's by a relative error of at most 0.023.
Values may be sent and summed in bfloat16 or wider, within the bound.
No kernel may reach another device: no remote copies, remote signals or barrier semaphores. Data moves between devices by JAX's collectives and lax.ppermute only.
A program may use at most 256 MiB of HBM per device.

v0:
```python
import jax
import jax.numpy as jnp
from jax import lax
from jax.sharding import PartitionSpec as P

HEADS = 15
KV_HEADS = 5
HEAD_DIM = 64
RUNS = 2
GROUP = 3
KVW = 320


eps = 1e-05
rope_base = 10000.0
big_negative = -1e30


def shortened(value):

    def short(part):
        return part.astype(jnp.bfloat16) if part.dtype == jnp.float32 else part

    return jax.tree.map(short, value)


def rms_norm(hidden_state, gain):
    return (
        hidden_state
        * lax.rsqrt(jnp.mean(hidden_state * hidden_state, axis=-1, keepdims=True) + eps)
        * gain
    )


def rotate(values, cos_table, sin_table):
    half = values.shape[-1] // 2
    turned = jnp.concatenate([-values[..., half:], values[..., :half]], axis=-1)
    return values * cos_table + turned * sin_table


def rotate_back(values, cos_table, sin_table):
    half = values.shape[-1] // 2
    scaled = values * sin_table
    turned = jnp.concatenate([scaled[..., half:], -scaled[..., :half]], axis=-1)
    return values * cos_table + turned


def rope_tables(positions):
    freq = rope_base ** (-2.0 * jnp.arange(HEAD_DIM // 2, dtype=jnp.float32) / HEAD_DIM)
    angle = positions.astype(jnp.float32)[..., None] * freq
    angle = jnp.concatenate([angle, angle], axis=-1)
    return (jnp.cos(angle)[..., None, :], jnp.sin(angle)[..., None, :])


def attention_scores(queries, keys_all, allowed):
    rows, stretch = (queries.shape[0], queries.shape[1])
    grouped = queries.reshape(rows, stretch, KV_HEADS, GROUP, HEAD_DIM)
    scores = jnp.einsum(
        "rckgd,rlkd->rkgcl", grouped, keys_all, preferred_element_type=jnp.float32
    ) * HEAD_DIM ** (-0.5)
    return (grouped, jnp.where(allowed, scores, big_negative))


def forward_run(state, weights, tables, allowed):
    (
        attn_gain,
        query_weight,
        key_weight,
        value_weight,
        out_weight,
        ffn_gain,
        gate_weight,
        up_weight,
        down_weight,
    ) = weights
    cos_table, sin_table = tables
    rows, stretch, width = state.shape
    flat = state.reshape(rows * stretch, width)
    normed = rms_norm(flat, attn_gain.astype(jnp.float32)).astype(jnp.bfloat16)
    query_pre = jnp.dot(normed, query_weight, preferred_element_type=jnp.float32).reshape(
        rows, stretch, HEADS, HEAD_DIM
    )
    key_pre = jnp.dot(normed, key_weight, preferred_element_type=jnp.float32).reshape(
        rows, stretch, KV_HEADS, HEAD_DIM
    )
    value_local = (
        jnp.dot(normed, value_weight, preferred_element_type=jnp.float32)
        .astype(jnp.bfloat16)
        .reshape(rows, stretch, KV_HEADS, HEAD_DIM)
    )
    queries = rotate(query_pre, cos_table, sin_table).astype(jnp.bfloat16)
    keys = rotate(key_pre, cos_table, sin_table).astype(jnp.bfloat16)
    keys_all, values_all = (
        lax.all_gather(keys, "fsdp", axis=1, tiled=True),
        lax.all_gather(value_local, "fsdp", axis=1, tiled=True),
    )
    grouped, scores = attention_scores(queries, keys_all, allowed)
    top = jnp.max(scores, axis=-1, keepdims=True)
    expo = jnp.exp(scores - top)
    total = jnp.sum(expo, axis=-1, keepdims=True)
    probs = (expo / total).astype(jnp.bfloat16)
    log_total = top + jnp.log(total)
    mixed = jnp.einsum("rkgcl,rlkd->rckgd", probs, values_all, preferred_element_type=jnp.float32)
    mixed = mixed.astype(jnp.bfloat16).reshape(rows * stretch, width)
    after_attn = flat + jnp.dot(mixed, out_weight, preferred_element_type=jnp.float32)
    normed_ffn = rms_norm(after_attn, ffn_gain.astype(jnp.float32)).astype(jnp.bfloat16)
    gate = jnp.dot(normed_ffn, gate_weight, preferred_element_type=jnp.float32)
    up_part = jnp.dot(normed_ffn, up_weight, preferred_element_type=jnp.float32)
    hidden = (jax.nn.silu(gate) * up_part).astype(jnp.bfloat16)
    result = after_attn + jnp.dot(hidden, down_weight, preferred_element_type=jnp.float32)
    saved = (
        flat,
        normed,
        queries,
        keys_all,
        values_all,
        log_total,
        mixed,
        after_attn,
        normed_ffn,
        gate,
        up_part,
        hidden,
    )
    return (result.reshape(rows, stretch, width), saved)


def backward_run(grad_state, saved, weights, tables, allowed):
    (
        attn_gain,
        query_weight,
        key_weight,
        value_weight,
        out_weight,
        ffn_gain,
        gate_weight,
        up_weight,
        down_weight,
    ) = weights
    (
        flat,
        normed,
        queries,
        keys_all,
        values_all,
        log_total,
        mixed,
        after_attn,
        normed_ffn,
        gate,
        up_part,
        hidden,
    ) = saved
    cos_table, sin_table = tables
    rows, stretch, width = grad_state.shape
    grad_next = grad_state.reshape(rows * stretch, width)
    grad_low = grad_next.astype(jnp.bfloat16)
    grad_down = jnp.einsum("tf,td->fd", hidden, grad_low, preferred_element_type=jnp.float32)
    grad_hidden = jnp.einsum("td,fd->tf", grad_low, down_weight, preferred_element_type=jnp.float32)
    act_out, act_back = jax.vjp(lambda g_in, u_in: jax.nn.silu(g_in) * u_in, gate, up_part)
    grad_gate_act, grad_up_act = act_back(grad_hidden)
    grad_gate_act = grad_gate_act.astype(jnp.bfloat16)
    grad_up_act = grad_up_act.astype(jnp.bfloat16)
    grad_gate = jnp.einsum(
        "td,tf->df", normed_ffn, grad_gate_act, preferred_element_type=jnp.float32
    )
    grad_up = jnp.einsum("td,tf->df", normed_ffn, grad_up_act, preferred_element_type=jnp.float32)
    grad_normed_ffn = jnp.einsum(
        "tf,df->td", grad_gate_act, gate_weight, preferred_element_type=jnp.float32
    )
    grad_normed_ffn = grad_normed_ffn + jnp.einsum(
        "tf,df->td", grad_up_act, up_weight, preferred_element_type=jnp.float32
    )
    norm_out, norm_back = jax.vjp(rms_norm, after_attn, ffn_gain.astype(jnp.float32))
    grad_after_part, grad_ffn_gain = norm_back(grad_normed_ffn)
    grad_after = grad_next + grad_after_part
    grad_attn_low = grad_after.astype(jnp.bfloat16)
    grad_out = jnp.einsum("td,te->de", mixed, grad_attn_low, preferred_element_type=jnp.float32)
    grad_mixed = jnp.einsum(
        "te,de->td", grad_attn_low, out_weight, preferred_element_type=jnp.float32
    )
    grad_mixed = grad_mixed.astype(jnp.bfloat16).reshape(rows, stretch, KV_HEADS, GROUP, HEAD_DIM)
    grouped, scores = attention_scores(queries, keys_all, allowed)
    probs_full = jnp.exp(scores - log_total)
    probs = probs_full.astype(jnp.bfloat16)
    grad_probs = jnp.einsum(
        "rckgd,rlkd->rkgcl", grad_mixed, values_all, preferred_element_type=jnp.float32
    )
    grad_values_all = jnp.einsum(
        "rkgcl,rckgd->rlkd", probs, grad_mixed, preferred_element_type=jnp.float32
    )
    inner = jnp.sum(probs_full * grad_probs, axis=-1, keepdims=True)
    grad_scores = (probs_full * (grad_probs - inner)).astype(jnp.bfloat16)
    grad_queries = jnp.einsum(
        "rkgcl,rlkd->rckgd", grad_scores, keys_all, preferred_element_type=jnp.float32
    ) * HEAD_DIM ** (-0.5)
    grad_keys_all = jnp.einsum(
        "rkgcl,rckgd->rlkd", grad_scores, grouped, preferred_element_type=jnp.float32
    ) * HEAD_DIM ** (-0.5)
    grad_keys, grad_values = (
        lax.psum_scatter(grad_keys_all, "fsdp", scatter_dimension=1, tiled=True),
        lax.psum_scatter(grad_values_all, "fsdp", scatter_dimension=1, tiled=True),
    )
    grad_queries = grad_queries.reshape(rows, stretch, HEADS, HEAD_DIM)
    grad_query_pre = (
        rotate_back(grad_queries, cos_table, sin_table)
        .astype(jnp.bfloat16)
        .reshape(rows * stretch, width)
    )
    grad_key_pre = (
        rotate_back(grad_keys, cos_table, sin_table)
        .astype(jnp.bfloat16)
        .reshape(rows * stretch, KVW)
    )
    grad_value_pre = grad_values.astype(jnp.bfloat16).reshape(rows * stretch, KVW)
    grad_query = jnp.einsum("td,te->de", normed, grad_query_pre, preferred_element_type=jnp.float32)
    grad_key = jnp.einsum("td,te->de", normed, grad_key_pre, preferred_element_type=jnp.float32)
    grad_value = jnp.einsum("td,te->de", normed, grad_value_pre, preferred_element_type=jnp.float32)
    grad_normed = jnp.einsum(
        "te,de->td", grad_query_pre, query_weight, preferred_element_type=jnp.float32
    )
    grad_normed = grad_normed + jnp.einsum(
        "te,de->td", grad_key_pre, key_weight, preferred_element_type=jnp.float32
    )
    grad_normed = grad_normed + jnp.einsum(
        "te,de->td", grad_value_pre, value_weight, preferred_element_type=jnp.float32
    )
    norm_in, norm_first_back = jax.vjp(rms_norm, flat, attn_gain.astype(jnp.float32))
    grad_flat_part, grad_attn_gain = norm_first_back(grad_normed)
    grad_input = grad_after + grad_flat_part
    grads = (
        grad_attn_gain,
        grad_query,
        grad_key,
        grad_value,
        grad_out,
        grad_ffn_gain,
        grad_gate,
        grad_up,
        grad_down,
    )
    return (grad_input.reshape(rows, stretch, width), grads)


def reduce_grads(grads):
    local_sums = jax.tree.map(
        lambda part: part.astype(jnp.float32),
        lax.psum_scatter(shortened(grads), "fsdp", scatter_dimension=0, tiled=True),
    )
    return lax.psum(local_sums, "dp")


def body(
    tokens,
    segment_ids,
    attn_gain,
    query_weight,
    key_weight,
    value_weight,
    out_weight,
    ffn_gain,
    gate_weight,
    up_weight,
    down_weight,
    cotangent,
):
    rows, stretch, width = tokens.shape
    length = stretch * lax.axis_size("fsdp")
    offset = lax.axis_index("fsdp") * stretch
    key_segments = lax.all_gather(segment_ids, "fsdp", axis=1, tiled=True)
    starts = jnp.sum((key_segments[:, None, :] < segment_ids[:, :, None]).astype(jnp.int32), axis=2)
    query_index = offset + jnp.arange(stretch, dtype=jnp.int32)
    tables = rope_tables(query_index[None, :] - starts)
    key_index = jnp.arange(length, dtype=jnp.int32)
    allowed = (segment_ids[:, :, None] == key_segments[:, None, :]) & (
        key_index[None, None, :] <= query_index[None, :, None]
    )
    allowed = allowed[:, None, None, :, :]
    shards = (
        attn_gain,
        query_weight,
        key_weight,
        value_weight,
        out_weight,
        ffn_gain,
        gate_weight,
        up_weight,
        down_weight,
    )
    weights = (
        lax.all_gather(shards[0], "fsdp", axis=0, tiled=True),
        lax.all_gather(shards[1], "fsdp", axis=0, tiled=True),
        lax.all_gather(shards[2], "fsdp", axis=0, tiled=True),
        lax.all_gather(shards[3], "fsdp", axis=0, tiled=True),
        lax.all_gather(shards[4], "fsdp", axis=0, tiled=True),
        lax.all_gather(shards[5], "fsdp", axis=0, tiled=True),
        lax.all_gather(shards[6], "fsdp", axis=0, tiled=True),
        lax.all_gather(shards[7], "fsdp", axis=0, tiled=True),
        lax.all_gather(shards[8], "fsdp", axis=0, tiled=True),
    )
    state = tokens.astype(jnp.float32)
    saved_runs = []
    for step in range(RUNS):
        state, saved = forward_run(state, weights, tables, allowed)
        saved_runs.append(saved)
    output = state.astype(jnp.bfloat16)
    grad_state = cotangent.astype(jnp.float32)
    totals = None
    for saved in reversed(saved_runs):
        grad_state, grads = backward_run(grad_state, saved, weights, tables, allowed)
        totals = (
            grads
            if totals is None
            else tuple((first + second for first, second in zip(totals, grads)))
        )
    shares = reduce_grads(totals)
    return (
        output,
        grad_state,
        shares[0],
        shares[1],
        shares[2],
        shares[3],
        shares[4],
        shares[5],
        shares[6],
        shares[7],
        shares[8],
    )


def solution(mesh):
    in_specs = (
        P("dp", "fsdp", None),
        P("dp", "fsdp"),
        P("fsdp"),
        P("fsdp", None),
        P("fsdp", None),
        P("fsdp", None),
        P("fsdp", None),
        P("fsdp"),
        P("fsdp", None),
        P("fsdp", None),
        P("fsdp", None),
        P("dp", "fsdp", None),
    )
    out_specs = (
        P("dp", "fsdp", None),
        P("dp", "fsdp", None),
        P("fsdp"),
        P("fsdp", None),
        P("fsdp", None),
        P("fsdp", None),
        P("fsdp", None),
        P("fsdp"),
        P("fsdp", None),
        P("fsdp", None),
        P("fsdp", None),
    )
    return jax.shard_map(body, mesh=mesh, in_specs=in_specs, out_specs=out_specs, check_vma=False)
```

profile of v0, /device:TPU:0, one launch (start us, length us, event | category | flops | bytes accessed | tf_op | source)
XLA Modules:
  0.0 1315.3 jit_solution(7443017003730014544)
XLA Ops:
  12.5 13.5 %all-reduce.6 = (bf16[960]{0:T(1024)(128)(2,1)S(1)}, bf16[960]{0:T(1024)(128)(2,1)S(1)}) all-reduce(bf16[960]{0:T(1024)(128)(2,1)S(1)} %dynamic-update-slice, bf16[960]{0:T(1024)(128)(2,1)S(1)} %dynamic-update-slice.1), channel_id=1, replica_groups=mesh['dp'=8,'fsdp'=4] {'fsdp'}, use_global_device_ids=true, to_apply=%add | all-reduce | flops 1920 | bytes 7680
  26.8 7.8 all_gather.47
  35.0 24.7 %all-gather.1 = bf16[4,240,320]{1,2,0:T(8,128)(2,1)S(1)} all-gather(bf16[1,240,320]{1,2,0:T(8,128)(2,1)S(1)} %bitcast.386), channel_id=1, replica_groups=mesh['dp'=8,'fsdp'=4] {'fsdp'}, dimensions={0}, use_global_device_ids=true | all-gather | bytes 768000 | tf_op jit(solution)/shard_map/all_gather | solution.py:293
  61.3 18.2 %all-gather = bf16[4,240,320]{1,2,0:T(8,128)(2,1)S(1)} all-gather(bf16[1,240,320]{1,2,0:T(8,128)(2,1)S(1)} %bitcast.387), channel_id=1, replica_groups=mesh['dp'=8,'fsdp'=4] {'fsdp'}, dimensions={0}, use_global_device_ids=true | all-gather | bytes 768000 | tf_op jit(solution)/shard_map/all_gather | solution.py:294
  80.9 24.7 %all_gather.50 = bf16[1,1024,5,64]{1,3,2,0:T(8,128)(2,1)S(1)} all-gather(bf16[1,256,5,64]{1,3,2,0:T(8,128)(2,1)S(1)} %fusion.96), channel_id=1, replica_groups=mesh['dp'=8,'fsdp'=4] {'fsdp'}, dimensions={1}, use_global_device_ids=true | all-gather | bytes 819200 | tf_op jit(solution)/shard_map/all_gather | solution.py:94
  106.1 24.7 %all_gather.46 = bf16[1,1024,5,64]{1,3,2,0:T(8,128)(2,1)} all-gather(bf16[1,256,5,64]{1,3,2,0:T(8,128)(2,1)S(1)} %bitcast.388), channel_id=1, replica_groups=mesh['dp'=8,'fsdp'=4] {'fsdp'}, dimensions={1}, use_global_device_ids=true | all-gather | bytes 819200 | tf_op jit(solution)/shard_map/all_gather | solution.py:95
  130.8 2.6 fusion.118
  133.7 7.1 fusion.128
  140.8 8.7 fusion.6
  149.5 7.1 fusion.45
  156.6 2.6 multiply_reduce_fusion.8
  160.5 66.8 %all-gather.12.cloned.1.call-done = bf16[960,2560]{1,0:T(8,128)(2,1)} async-done(((bf16[240,2560]{1,0:T(8,128)(2,1)}), bf16[960,2560]{1,0:T(8,128)(2,1)}) %all-gather.12.cloned.1.call-update) | async-done | bytes 4915216 | tf_op jit(solution)/shard_map/all_gather | solution.py:297
  227.3 5.4 fusion.130
  232.7 87.1 %all-gather.14.cloned.1.call-done = bf16[960,2560]{1,0:T(8,128)(2,1)} async-done(((bf16[240,2560]{1,0:T(8,128)(2,1)}), bf16[960,2560]{1,0:T(8,128)(2,1)}) %all-gather.14.cloned.1.call-update) | async-done | bytes 4915216 | tf_op jit(solution)/shard_map/all_gather | solution.py:298
  319.8 7.0 multiply_convert_fusion.3
  326.8 85.6 %all-gather.16.cloned.1.call-done = bf16[2560,960]{0,1:T(8,128)(2,1)} async-done(((bf16[640,960]{0,1:T(8,128)(2,1)}), bf16[2560,960]{0,1:T(8,128)(2,1)}) %all-gather.16.cloned.1.call-update) | async-done | bytes 4915216 | tf_op jit(solution)/shard_map/all_gather | solution.py:299
  412.4 4.5 multiply_reduce_fusion.7
  420.2 17.1 %all_gather.58 = bf16[1,1024,5,64]{1,3,2,0:T(8,128)(2,1)S(1)} all-gather(bf16[1,256,5,64]{1,3,2,0:T(8,128)(2,1)S(1)} %fusion.98), channel_id=1, replica_groups=mesh['dp'=8,'fsdp'=4] {'fsdp'}, dimensions={1}, use_global_device_ids=true | all-gather | bytes 819200 | tf_op jit(solution)/shard_map/all_gather | solution.py:94
  437.3 16.6 %all_gather.57 = bf16[1,1024,5,64]{1,3,2,0:T(8,128)(2,1)S(1)} all-gather(bf16[1,256,5,64]{1,3,2,0:T(8,128)(2,1)S(1)} %bitcast.383), channel_id=1, replica_groups=mesh['dp'=8,'fsdp'=4] {'fsdp'}, dimensions={1}, use_global_device_ids=true | all-gather | bytes 819200 | tf_op jit(solution)/shard_map/all_gather | solution.py:95
  455.0 19.8 %fusion.129 = (f32[5,3,256]{2,1,0:T(4,128)S(1)}, f32[1,5,3,256,1024]{3,4,2,1,0:T(8,128)}) fusion(bf16[256,5,3,64]{0,3,2,1:T(8,128)(2,1)S(1)} %fusion.77, bf16[1,1024,5,64]{1,3,2,0:T(8,128)(2,1)S(1)} %all_gather.58, pred[256,1024]{0,1:T(8,128)(4,1)S(1)} %fusion.58), kind=kOutput, calls=%fused_computation.220 | convolution fusion | flops 515109120 | bytes 17153024 | tf_op jit(solution)/shard_map/rckgd,rlkd->rkgcl/dot_general | solution.py:58
  474.8 7.6 fusion.7
  482.5 7.2 fusion.48
  494.3 3.8 multiply_convert_fusion.1
  505.1 8.3 fusion.3
  513.5 7.7 fusion.16
  521.2 3.1 copy-done
  524.3 3.5 fusion.41
  527.9 9.3 fusion.32
  537.7 4.9 convolution_multiply_fusion.1
  545.8 12.3 reduce-scatter.18.cloned.1.call-done
  560.9 2.8 convolution_add_fusion.5
  563.7 27.4 %reduce-scatter.20.cloned.1.call-done = f32[1,256,5,64]{1,3,2,0:T(8,128)} async-done(((f32[1,1024,5,64]{1,3,2,0:T(8,128)}), f32[1,256,5,64]{1,3,2,0:T(8,128)}) %reduce-scatter.20.cloned.1.call-update) | async-done | bytes 327696 | tf_op jit(solution)/shard_map/reduce_scatter | solution.py:202
  592.1 2.6 multiply_reduce_fusion.2
  594.7 2.6 fusion.66
  597.4 5.3 multiply_convert_fusion
  609.8 8.4 fusion
  618.2 7.7 fusion.17
  626.0 3.1 copy-done.1
  629.0 3.6 fusion.39
  632.9 9.3 fusion.35
  643.3 4.7 convolution_multiply_fusion
  655.8 2.4 fusion.137
  658.2 4.6 reduce-scatter.22.cloned.1.call-done
  665.5 2.6 fusion.42
  670.4 2.4 fusion.138
  672.9 22.3 %reduce-scatter.24.cloned.1.call-done = f32[1,256,5,64]{1,3,2,0:T(8,128)} async-done(((f32[1,1024,5,64]{1,3,2,0:T(8,128)}), f32[1,256,5,64]{1,3,2,0:T(8,128)}) %reduce-scatter.24.cloned.1.call-update) | async-done | bytes 327696 | tf_op jit(solution)/shard_map/reduce_scatter | solution.py:202
  696.8 2.6 fusion.43
  699.4 2.3 copy.79
  701.8 3.1 fusion.91
  705.0 3.8 add_convert_fusion
  708.7 7.9 copy.81
  716.9 2.9 fusion.139
  719.8 3.7 add_convert_fusion.2
  723.6 2.9 fusion.140
  726.5 3.6 add_convert_fusion.1
  731.4 5.2 fusion.55
  738.9 9.3 all-reduce.5
  749.6 32.2 %reduce-scatter.28.cloned.1.call-done = bf16[240,960]{1,0:T(8,128)(2,1)} async-done(((bf16[960,960]{1,0:T(8,128)(2,1)}), bf16[240,960]{1,0:T(8,128)(2,1)}) %reduce-scatter.28.cloned.1.call-update) | async-done | bytes 460816 | tf_op jit(solution)/shard_map/reduce_scatter | solution.py:248
  781.8 25.2 %reduce-scatter.34.cloned.1.call-done = bf16[240,320]{1,0:T(8,128)(2,1)} async-done(((bf16[960,320]{1,0:T(8,128)(2,1)}), bf16[240,320]{1,0:T(8,128)(2,1)}) %reduce-scatter.34.cloned.1.call-update) | async-done | bytes 153616
  808.0 23.3 %reduce-scatter.36.cloned.1.call-done = bf16[240,320]{1,0:T(8,128)(2,1)} async-done(((bf16[960,320]{1,0:T(8,128)(2,1)}), bf16[240,320]{1,0:T(8,128)(2,1)}) %reduce-scatter.36.cloned.1.call-update) | async-done | bytes 153616
  832.4 94.0 %reduce-scatter.38.cloned.1.call-done = bf16[640,960]{1,0:T(8,128)(2,1)} async-done(((bf16[2560,960]{1,0:T(8,128)(2,1)}), bf16[640,960]{1,0:T(8,128)(2,1)}) %reduce-scatter.38.cloned.1.call-update) | async-done | bytes 1228816
  928.6 89.0 %reduce-scatter.30.cloned.1.call-done = bf16[240,2560]{1,0:T(8,128)(2,1)} async-done(((bf16[960,2560]{1,0:T(8,128)(2,1)}), bf16[240,2560]{1,0:T(8,128)(2,1)}) %reduce-scatter.30.cloned.1.call-update) | async-done | bytes 1228816 | tf_op jit(solution)/shard_map/reduce_scatter | solution.py:248
  1017.6 91.3 %reduce-scatter.32.cloned.1.call-done = bf16[240,2560]{1,0:T(8,128)(2,1)} async-done(((bf16[960,2560]{1,0:T(8,128)(2,1)}), bf16[240,2560]{1,0:T(8,128)(2,1)}) %reduce-scatter.32.cloned.1.call-update) | async-done | bytes 1228816 | tf_op jit(solution)/shard_map/reduce_scatter | solution.py:248
  1108.9 199.7 %all-reduce.8 = (f32[240]{0:T(256)}, f32[240,960]{1,0:T(8,128)}, f32[240,320]{0,1:T(8,128)}, f32[240,320]{0,1:T(8,128)}, f32[240,960]{1,0:T(8,128)}, /*index=5*/...) all-reduce(f32[240]{0:T(256)S(1)} %get-tuple-element.80, ...), channel_id=1, replica_groups=mesh['dp'=8,'fsdp'=4] {'dp'}, use_global_device_ids=true, to_apply=%region_22.23 | all-reduce | flops 2458080 | bytes 14749440 | tf_op jit(solution)/shard_map/psum | solution.py:250
  (324 shorter events, 64.8 us)
Async XLA Ops:
  7.2 18.8 %copy-start.4 = (bf16[1,256,960]{1,2,0:T(8,128)(2,1)S(1)}, bf16[1,256,960]{1,2,0:T(8,128)(2,1)}, u32[]{:S(2)}) copy-start(bf16[1,256,960]{1,2,0:T(8,128)(2,1)} %param.12) | copy-start | bytes 1474564
  7.2 19.5 %copy-start.68 = (s32[1,256]{1,0:T(1,128)S(1)}, s32[1,256]{1,0:T(1,128)}, u32[]{:S(2)}) copy-start(s32[1,256]{1,0:T(1,128)} %param.13) | copy-start | bytes 3076
  7.2 27.8 %copy-start.58 = (bf16[240,320]{0,1:T(8,128)(2,1)S(1)}, bf16[240,320]{0,1:T(8,128)(2,1)}, u32[]{:S(2)}) copy-start(bf16[240,320]{0,1:T(8,128)(2,1)} %param.16) | copy-start | bytes 460804
  7.2 123.5 %all-gather.8.cloned.1.call-start = ((), (), s32[]{:S(2)}) async-start(), calls=%async_computation.11 | async-start | bytes 2457600 | tf_op jit(solution)/shard_map/all_gather | solution.py:292
  8.0 148.7 %all-gather.10.cloned.1.call-start = ((), (), s32[]{:S(2)}) async-start(), calls=%async_computation.12 | async-start | bytes 2457600 | tf_op jit(solution)/shard_map/all_gather | solution.py:295
  8.7 218.6 %all-gather.12.cloned.1.call-start = ((), (), s32[]{:S(2)}) async-start(), calls=%async_computation.13 | async-start | bytes 6144000 | tf_op jit(solution)/shard_map/all_gather | solution.py:297
  9.5 310.4 %all-gather.14.cloned.1.call-start = ((), (), s32[]{:S(2)}) async-start(), calls=%async_computation.14 | async-start | bytes 6144000 | tf_op jit(solution)/shard_map/all_gather | solution.py:298
  10.0 51.3 %copy-start.59 = (bf16[240,320]{0,1:T(8,128)(2,1)S(1)}, bf16[240,320]{0,1:T(8,128)(2,1)}, u32[]{:S(2)}) copy-start(bf16[240,320]{0,1:T(8,128)(2,1)} %param.17) | copy-start | bytes 460804
  10.0 402.3 %all-gather.16.cloned.1.call-start = ((), (), s32[]{:S(2)}) async-start(), calls=%async_computation.15 | async-start | bytes 6144000 | tf_op jit(solution)/shard_map/all_gather | solution.py:299
  10.6 547.5 %reduce-scatter.18.cloned.1.call-start = ((), (), s32[]{:S(2)}) async-start(), calls=%async_computation.16 | async-start | bytes 1638400 | tf_op jit(solution)/shard_map/reduce_scatter | solution.py:201
  26.8 104.0 %copy-start.62 = (f32[256]{0:T(256)}, f32[256]{0:T(256)S(1)}, u32[]{:S(2)}) copy-start(f32[256]{0:T(256)S(1)} %fusion.111) | copy-start | bytes 3076
  35.0 385.1 %copy-start.26 = (f32[256,64]{0,1:T(8,128)}, f32[256,64]{0,1:T(8,128)S(1)}, u32[]{:S(2)}) copy-start(f32[256,64]{0,1:T(8,128)S(1)} %get-tuple-element.56) | copy-start | bytes 196612
  60.8 356.3 %copy-start.13 = (bf16[960,320]{0,1:T(8,128)(2,1)}, bf16[960,320]{0,1:T(8,128)(2,1)S(1)}, u32[]{:S(2)}) copy-start(bf16[960,320]{0,1:T(8,128)(2,1)S(1)} %reshape.916) | copy-start | bytes 1843204
  80.5 337.0 %copy-start.11 = (bf16[960,320]{0,1:T(8,128)(2,1)}, bf16[960,320]{0,1:T(8,128)(2,1)S(1)}, u32[]{:S(2)}) copy-start(bf16[960,320]{0,1:T(8,128)(2,1)S(1)} %reshape.914) | copy-start | bytes 1843204
  105.6 28.1 %copy-start.21 = (bf16[1,1024,5,64]{1,3,2,0:T(8,128)(2,1)}, bf16[1,1024,5,64]{1,3,2,0:T(8,128)(2,1)S(1)}, u32[]{:S(2)}) copy-start(bf16[1,1024,5,64]{1,3,2,0:T(8,128)(2,1)S(1)} %all_gather.50) | copy-start | bytes 1966084
  133.7 7.1 copy-start.24
  140.8 8.7 copy-start.29
  149.5 7.1 copy-start.60
  156.6 76.1 %copy-start.56 = (bf16[5,64,3,256]{3,1,2,0:T(8,128)(2,1)}, bf16[5,64,3,256]{3,1,2,0:T(8,128)(2,1)S(1)}, u32[]{:S(2)}) copy-start(bf16[5,64,3,256]{3,1,2,0:T(8,128)(2,1)S(1)} %fusion.45) | copy-start | bytes 1474564
  159.3 73.4 %copy-start.71 = (f32[256]{0:T(256)}, f32[256]{0:T(256)S(1)}, u32[]{:S(2)}) copy-start(f32[256]{0:T(256)S(1)} %get-tuple-element.61) | copy-start | bytes 3076
  159.3 73.4 %copy-start.69 = (f32[256]{0:T(256)}, f32[256]{0:T(256)S(1)}, u32[]{:S(2)}) copy-start(f32[256]{0:T(256)S(1)} %fusion.112) | copy-start | bytes 3076
  160.4 159.4 %copy-start.15 = (bf16[256,960]{0,1:T(8,128)(2,1)}, bf16[256,960]{0,1:T(8,128)(2,1)S(1)}, u32[]{:S(2)}) copy-start(bf16[256,960]{0,1:T(8,128)(2,1)S(1)} %multiply_convert_fusion.6) | copy-start | bytes 1474564
  416.9 72.8 %copy-start.9 = (f32[256,960]{0,1:T(8,128)}, f32[256,960]{0,1:T(8,128)S(1)}, u32[]{:S(2)}) copy-start(f32[256,960]{0,1:T(8,128)S(1)} %get-tuple-element.66) | copy-start | bytes 2949124
  437.3 37.5 %copy-start.23 = (bf16[1,1024,5,64]{1,3,2,0:T(8,128)(2,1)}, bf16[1,1024,5,64]{1,3,2,0:T(8,128)(2,1)S(1)}, u32[]{:S(2)}) copy-start(bf16[1,1024,5,64]{1,3,2,0:T(8,128)(2,1)S(1)} %all_gather.58) | copy-start | bytes 1966084
  453.9 28.5 %copy-start.30 = (bf16[1,1024,5,64]{1,3,2,0:T(8,128)(2,1)}, bf16[1,1024,5,64]{1,3,2,0:T(8,128)(2,1)S(1)}, u32[]{:S(2)}) copy-start(bf16[1,1024,5,64]{1,3,2,0:T(8,128)(2,1)S(1)} %all_gather.57) | copy-start | bytes 1966084
  482.4 8.5 slice-start.8
  482.4 7.2 copy-start.6
  482.5 8.4 slice-start.9
  490.6 11.2 copy-start.17
  499.6 5.5 slice-start.7
  502.2 11.3 copy-start.10
  527.8 9.8 copy-start.61
  527.8 63.2 %reduce-scatter.20.cloned.1.call-start = ((), (), s32[]{:S(2)}) async-start(), calls=%async_computation.17 | async-start | bytes 1638400 | tf_op jit(solution)/shard_map/reduce_scatter | solution.py:202
  537.2 125.6 %reduce-scatter.22.cloned.1.call-start = ((), (), s32[]{:S(2)}) async-start(), calls=%async_computation.18 | async-start | bytes 1638400 | tf_op jit(solution)/shard_map/reduce_scatter | solution.py:201
  544.2 16.1 %copy-start.37 = (bf16[256,960]{0,1:T(8,128)(2,1)}, bf16[256,960]{0,1:T(8,128)(2,1)S(1)}, u32[]{:S(2)}) copy-start(bf16[256,960]{0,1:T(8,128)(2,1)S(1)} %fusion.71) | copy-start | bytes 1474564
  545.8 46.3 %copy-start.65 = (f32[256]{0:T(256)S(1)}, f32[256]{0:T(256)}, u32[]{:S(2)}) copy-start(f32[256]{0:T(256)} %copy-done.64) | copy-start | bytes 3076
  559.2 35.5 %copy-start.74 = (f32[256]{0:T(256)S(1)}, f32[256]{0:T(256)}, u32[]{:S(2)}) copy-start(f32[256]{0:T(256)} %copy-done.73) | copy-start | bytes 3076
  592.0 10.7 copy-start.47
  592.1 5.3 copy-start.34
  592.1 5.3 copy-start.79
  592.1 10.7 slice-start.10
  592.1 12.2 slice-start.14
  597.3 8.7 copy-start.19
  597.3 5.4 slice-start.11
  597.3 7.0 slice-start.15
  597.3 7.0 copy-start.32
  604.4 5.4 slice-start.3
  606.3 11.9 copy-start.7
  618.2 10.8 copy-start.25
  632.6 9.7 copy-start.3
  632.6 9.7 copy-start.38
  632.7 62.5 %reduce-scatter.24.cloned.1.call-start = ((), (), s32[]{:S(2)}) async-start(), calls=%async_computation.19 | async-start | bytes 1638400 | tf_op jit(solution)/shard_map/reduce_scatter | solution.py:202
  642.2 107.4 %reduce-scatter.26.cloned.1.call-start = ((), (), s32[]{:S(2)}) async-start(), calls=%async_computation.20 | async-start | bytes 2457600 | tf_op jit(solution)/shard_map/reduce_scatter | solution.py:248
  651.5 130.3 %reduce-scatter.28.cloned.1.call-start = ((), (), s32[]{:S(2)}) async-start(), calls=%async_computation.21 | async-start | bytes 2457600 | tf_op jit(solution)/shard_map/reduce_scatter | solution.py:248
  655.7 151.3 %reduce-scatter.34.cloned.1.call-start = ((), (), s32[]{:S(2)}) async-start(), calls=%async_computation.24 | async-start | bytes 921600
  670.4 161.0 %reduce-scatter.36.cloned.1.call-start = ((), (), s32[]{:S(2)}) async-start(), calls=%async_computation.25 | async-start | bytes 921600
  672.9 28.9 %copy-start.36 = (bf16[1,256,960]{1,2,0:T(8,128)(2,1)S(1)}, bf16[1,256,960]{1,2,0:T(8,128)(2,1)}, u32[]{:S(2)}) copy-start(bf16[1,256,960]{1,2,0:T(8,128)(2,1)} %param.23) | copy-start | bytes 1474564
  701.7 224.7 %reduce-scatter.38.cloned.1.call-start = ((), (), s32[]{:S(2)}) async-start(), calls=%async_computation.26 | async-start | bytes 6553600
  716.7 300.9 %reduce-scatter.30.cloned.1.call-start = ((), (), s32[]{:S(2)}) async-start(), calls=%async_computation.22 | async-start | bytes 6144000 | tf_op jit(solution)/shard_map/reduce_scatter | solution.py:248
  723.6 385.3 %reduce-scatter.32.cloned.1.call-start = ((), (), s32[]{:S(2)}) async-start(), calls=%async_computation.23 | async-start | bytes 6144000 | tf_op jit(solution)/shard_map/reduce_scatter | solution.py:248
  731.3 5.2 copy-start.33
  731.3 5.4 copy-start.75
  731.4 5.5 copy-start.41
  737.7 10.7 copy-start.67
  (50 other events, 124.0 us)
Sparse Core Ops, SparseCore 0:
  9.6 59.7 all-gather.7
  71.0 62.9 all-gather.9
  135.6 91.6 all-gather.11
  228.7 91.0 all-gather.13
  321.2 91.0 all-gather.15
  527.9 30.1 reduce-scatter.17
  561.0 29.9 reduce-scatter.19
  632.8 30.0 reduce-scatter.21
  665.1 29.9 reduce-scatter.23
  697.9 40.2 reduce-scatter.25
  741.1 40.6 reduce-scatter.27
  784.5 22.4 reduce-scatter.33
  809.3 22.0 reduce-scatter.35
  833.5 92.8 reduce-scatter.37
  928.6 88.9 reduce-scatter.29
  1019.9 88.9 reduce-scatter.31
where the time goes:
time: 1320 us
  waiting for transfers between devices  664 us (50%)
  blocking collectives  356 us (27%)
  matrix products  190 us (14%)
  other arithmetic  47.5 us (4%)
  local copies, waits for them, and re-layouts  38 us (3%)
  between operations  17.2 us (1%)
    reduce_scatter x4, waiting for transfers between devices, reduce_grads(): lax.psum_scatter(shortened(grads), 'fsdp', scatter_dimension=0, tiled=True)  212 us
    psum x1, blocking collectives, reduce_grads(): return lax.psum(local_sums, 'dp')  200 us
    unnamed x19, waiting for transfers between devices  146 us
    all_gather x1, waiting for transfers between devices, body(): lax.all_gather(shards[7], 'fsdp', axis=0, tiled=True)  87.1 us
    all_gather x1, waiting for transfers between devices, body(): lax.all_gather(shards[8], 'fsdp', axis=0, tiled=True)  85.6 us
    all_gather x1, waiting for transfers between devices, body(): lax.all_gather(shards[6], 'fsdp', axis=0, tiled=True)  66.8 us
    reduce_scatter x2, waiting for transfers between devices, backward_run(): lax.psum_scatter(grad_values_all, 'fsdp', scatter_dimension=1, tiled=True)  49.7 us
    all_gather x2, blocking collectives, forward_run(): lax.all_gather(keys, 'fsdp', axis=1, tiled=True)  41.9 us
  transfers between devices with their start and end apart: 16, of which 13 were waited for; matrix products, arithmetic and copies ran while one was open for 11% of the time, Pallas kernels for 0%

commit v1 on v0

v1 whole, which is shorter than its diff:
```python
import jax
import jax.numpy as jnp
from jax import lax
from jax.sharding import PartitionSpec as P

HEADS = 15
KV_HEADS = 5
HEAD_DIM = 64
RUNS = 2
GROUP = 3
KVW = 320
CORE, SIDE, BACK = 1, 2, 4

eps = 1e-05
rope_base = 10000.0
big_negative = -1e30
f32, bf16 = jnp.float32, jnp.bfloat16


def flip(value, bit):
    count = lax.axis_size("dp")
    return lax.ppermute(value, "dp", [(i, i ^ bit) for i in range(count)])


def turn_z(value, step):
    count = lax.axis_size("fsdp")
    return lax.ppermute(value, "fsdp", [(i, (i + step) % count) for i in range(count)])


def home_to_work(value, back=False):
    count, depth = lax.axis_size("dp"), lax.axis_size("fsdp")
    pairs = []
    for d in range(count):
        for z in range(depth):
            there = (d & ~1) | (z & 1), 2 * (d & 1) + (z >> 1)
            pair = (d * depth + z, there[0] * depth + there[1])
            pairs.append(pair[::-1] if back else pair)
    return lax.ppermute(value, ("dp", "fsdp"), pairs)


def place():
    d, z = lax.axis_index("dp"), lax.axis_index("fsdp")
    return d & 1, (d >> 1) & 3, z


def ring_gather(shard):
    z = lax.axis_index("fsdp")
    depth = lax.axis_size("fsdp")
    parts = [shard] + [turn_z(shard, s) for s in range(1, depth)]
    full = jnp.zeros((depth,) + shard.shape, shard.dtype)
    for s, part in enumerate(parts):
        full = lax.dynamic_update_index_in_dim(full, part, (z - s) % depth, 0)
    return full


def plane_gather(piece):
    core, chip, _ = place()
    half = piece.shape[0] // 2
    top, bottom = piece[:half], piece[half:]
    x_top, y_top = flip(top, SIDE), flip(top, BACK)
    x_bottom, y_bottom = flip(bottom, SIDE), flip(bottom, BACK)
    d_top, d_bottom = flip(x_top, BACK), flip(y_bottom, SIDE)
    full = jnp.zeros((2, 4) + piece.shape, piece.dtype)
    rest = (0,) * (piece.ndim - 1)
    for who, (t, b) in enumerate(
        ((top, bottom), (x_top, x_bottom), (y_top, y_bottom), (d_top, d_bottom))
    ):
        at = chip ^ who
        full = lax.dynamic_update_slice(full, t[None, None], (core, at, 0) + rest)
        full = lax.dynamic_update_slice(full, b[None, None], (core, at, half) + rest)
        t2, b2 = flip(t, CORE), flip(b, CORE)
        full = lax.dynamic_update_slice(full, t2[None, None], (1 - core, at, 0) + rest)
        full = lax.dynamic_update_slice(full, b2[None, None], (1 - core, at, half) + rest)
    return full


def gather_weights(query, key, value, out, gate, up, down):
    core, chip, _ = place()
    rows = query.shape[0]
    depth = lax.axis_size("fsdp")
    which = core * 4 + chip
    width = query.shape[1]
    first = jnp.concatenate([query, key, value, out], axis=1)
    n = first.shape[1] // 8
    piece = lax.dynamic_slice(first, (0, n * which), (rows, n))
    piece = ring_gather(piece).reshape(depth * rows, n)
    first = plane_gather(piece)
    first = jnp.concatenate([first[c, m] for c in range(2) for m in range(4)], axis=1)
    query = first[:, :width]
    key = first[:, width : width + KVW]
    value = first[:, width + KVW : width + 2 * KVW]
    out = first[:, width + 2 * KVW :]
    n = gate.shape[1] // 4
    mine = jnp.where(core == 0, gate, up)
    piece = lax.dynamic_slice(mine, (0, n * chip), (rows, n))
    piece = ring_gather(piece).reshape(depth * rows, n)
    both = plane_gather(piece)
    n = down.shape[0] // 2
    piece = lax.dynamic_slice(down, (n * core, 0), (n, width))
    piece = ring_gather(piece)
    other = flip(piece, CORE)
    full = jnp.zeros((depth, 2) + piece.shape[1:], piece.dtype)
    full = lax.dynamic_update_slice(full, piece[:, None], (0, core, 0, 0))
    full = lax.dynamic_update_slice(full, other[:, None], (0, 1 - core, 0, 0))
    return query, key, value, out, both[0], both[1], full.reshape(depth, 2 * n, width)


def rms_norm(hidden_state, gain):
    return (
        hidden_state
        * lax.rsqrt(jnp.mean(hidden_state * hidden_state, axis=-1, keepdims=True) + eps)
        * gain
    )


def rotate(values, cos_table, sin_table):
    half = values.shape[-1] // 2
    turned = jnp.concatenate([-values[..., half:], values[..., :half]], axis=-1)
    return values * cos_table + turned * sin_table


def rotate_back(values, cos_table, sin_table):
    half = values.shape[-1] // 2
    scaled = values * sin_table
    turned = jnp.concatenate([scaled[..., half:], -scaled[..., :half]], axis=-1)
    return values * cos_table + turned


def rope_tables(positions):
    freq = rope_base ** (-2.0 * jnp.arange(HEAD_DIM // 2, dtype=f32) / HEAD_DIM)
    angle = positions.astype(f32)[..., None] * freq
    angle = jnp.concatenate([angle, angle], axis=-1)
    return (jnp.cos(angle)[..., None, :], jnp.sin(angle)[..., None, :])


def window(own):
    core = lax.axis_index("dp") & 1
    count, depth = lax.axis_size("dp"), lax.axis_size("fsdp")
    ups = [(z, z + 1) for z in range(0, depth, 2)]
    far = lax.ppermute(own, "fsdp", ups)
    near = flip(jnp.where(core == 0, own, far), CORE)
    return jnp.concatenate([far, near, own], axis=0)


def unwindow(grads):
    n = grads.shape[0] // 3
    core = lax.axis_index("dp") & 1
    depth = lax.axis_size("fsdp")
    downs = [(z + 1, z) for z in range(0, depth, 2)]
    far, near, own = grads[:n], grads[n : 2 * n], grads[2 * n :]
    near = flip(near.astype(bf16), CORE).astype(f32)
    far = jnp.where(core == 1, far + near, far).astype(bf16)
    own = jnp.where(core == 0, own + near, own)
    return own + lax.ppermute(far, "fsdp", downs).astype(f32)


def attention_scores(queries, keys_all, allowed):
    stretch = queries.shape[0]
    grouped = queries.reshape(stretch, KV_HEADS, GROUP, HEAD_DIM)
    scores = jnp.einsum(
        "ckgd,lkd->kgcl", grouped, keys_all, preferred_element_type=f32
    ) * HEAD_DIM ** (-0.5)
    return (grouped, jnp.where(allowed, scores, big_negative))


def dot(a, b):
    return jnp.dot(a, b, preferred_element_type=f32)


def forward_run(flat, weights, tables, allowed):
    attn_gain, query_weight, key_weight, value_weight, out_weight, ffn_gain, gate_weight, up_weight, down_weight = weights
    cos_table, sin_table = tables
    stretch, width = flat.shape
    normed = rms_norm(flat, attn_gain.astype(f32)).astype(bf16)
    query_pre = dot(normed, query_weight).reshape(stretch, HEADS, HEAD_DIM)
    key_pre = dot(normed, key_weight).reshape(stretch, KV_HEADS, HEAD_DIM)
    value_local = dot(normed, value_weight).astype(bf16)
    queries = rotate(query_pre, cos_table, sin_table).astype(bf16)
    keys = rotate(key_pre, cos_table, sin_table).astype(bf16).reshape(stretch, KVW)
    keys_all = window(keys).reshape(-1, KV_HEADS, HEAD_DIM)
    values_all = window(value_local).reshape(-1, KV_HEADS, HEAD_DIM)
    grouped, scores = attention_scores(queries, keys_all, allowed)
    top = jnp.max(scores, axis=-1, keepdims=True)
    expo = jnp.exp(scores - top)
    total = jnp.sum(expo, axis=-1, keepdims=True)
    probs = (expo / total).astype(bf16)
    log_total = top + jnp.log(total)
    mixed = jnp.einsum("kgcl,lkd->ckgd", probs, values_all, preferred_element_type=f32)
    mixed = mixed.astype(bf16).reshape(stretch, width)
    after_attn = flat + dot(mixed, out_weight)
    normed_ffn = rms_norm(after_attn, ffn_gain.astype(f32)).astype(bf16)
    gate = [dot(normed_ffn, gate_weight[m]) for m in range(4)]
    up_part = [dot(normed_ffn, up_weight[m]) for m in range(4)]
    hidden = [(jax.nn.silu(g) * u).astype(bf16) for g, u in zip(gate, up_part)]
    result = after_attn
    for m in range(4):
        result = result + dot(hidden[m], down_weight[m])
    saved = (flat, normed, queries, keys_all, values_all, log_total, mixed, after_attn, normed_ffn, gate, up_part, hidden)
    return result, saved


def backward_ffn(grad_next, saved, weights):
    attn_gain, query_weight, key_weight, value_weight, out_weight, ffn_gain, gate_weight, up_weight, down_weight = weights
    flat, normed, queries, keys_all, values_all, log_total, mixed, after_attn, normed_ffn, gate, up_part, hidden = saved
    grad_low = grad_next.astype(bf16)
    grad_normed_ffn = None
    d_gate, d_up = [], []
    for m in range(4):
        grad_hidden = jnp.einsum("td,fd->tf", grad_low, down_weight[m], preferred_element_type=f32)
        _, act_back = jax.vjp(lambda g_in, u_in: jax.nn.silu(g_in) * u_in, gate[m], up_part[m])
        dg, du = act_back(grad_hidden)
        dg, du = dg.astype(bf16), du.astype(bf16)
        part = jnp.einsum("tf,df->td", dg, gate_weight[m], preferred_element_type=f32)
        part = part + jnp.einsum("tf,df->td", du, up_weight[m], preferred_element_type=f32)
        grad_normed_ffn = part if grad_normed_ffn is None else grad_normed_ffn + part
        d_gate.append(dg)
        d_up.append(du)
    _, norm_back = jax.vjp(rms_norm, after_attn, ffn_gain.astype(f32))
    grad_after_part, grad_ffn_gain = norm_back(grad_normed_ffn)
    grad_after = grad_next + grad_after_part
    return grad_after, grad_ffn_gain, (normed_ffn, jnp.concatenate(d_gate, 1), jnp.concatenate(d_up, 1), jnp.concatenate(hidden, 1), grad_low)


def backward_attention(grad_after, saved, weights, tables, allowed):
    attn_gain, query_weight, key_weight, value_weight, out_weight, ffn_gain, gate_weight, up_weight, down_weight = weights
    flat, normed, queries, keys_all, values_all, log_total, mixed, after_attn, normed_ffn, gate, up_part, hidden = saved
    cos_table, sin_table = tables
    stretch, width = flat.shape
    low = grad_after.astype(bf16)
    grad_mixed = jnp.einsum("te,de->td", low, out_weight, preferred_element_type=f32)
    grad_mixed = grad_mixed.astype(bf16).reshape(stretch, KV_HEADS, GROUP, HEAD_DIM)
    grouped, scores = attention_scores(queries, keys_all, allowed)
    probs_full = jnp.exp(scores - log_total)
    probs = probs_full.astype(bf16)
    grad_probs = jnp.einsum("ckgd,lkd->kgcl", grad_mixed, values_all, preferred_element_type=f32)
    grad_values_all = jnp.einsum("kgcl,ckgd->lkd", probs, grad_mixed, preferred_element_type=f32)
    inner = jnp.sum(probs_full * grad_probs, axis=-1, keepdims=True)
    grad_scores = (probs_full * (grad_probs - inner)).astype(bf16)
    grad_queries = jnp.einsum("kgcl,lkd->ckgd", grad_scores, keys_all, preferred_element_type=f32) * HEAD_DIM ** (-0.5)
    grad_keys_all = jnp.einsum("kgcl,ckgd->lkd", grad_scores, grouped, preferred_element_type=f32) * HEAD_DIM ** (-0.5)
    grad_keys = unwindow(grad_keys_all.reshape(-1, KVW)).reshape(stretch, KV_HEADS, HEAD_DIM)
    grad_value_pre = unwindow(grad_values_all.reshape(-1, KVW)).astype(bf16)
    grad_queries = grad_queries.reshape(stretch, HEADS, HEAD_DIM)
    grad_query_pre = rotate_back(grad_queries, cos_table, sin_table).astype(bf16).reshape(stretch, width)
    grad_key_pre = rotate_back(grad_keys, cos_table, sin_table).astype(bf16).reshape(stretch, KVW)
    grad_normed = jnp.einsum("te,de->td", grad_query_pre, query_weight, preferred_element_type=f32)
    grad_normed = grad_normed + jnp.einsum("te,de->td", grad_key_pre, key_weight, preferred_element_type=f32)
    grad_normed = grad_normed + jnp.einsum("te,de->td", grad_value_pre, value_weight, preferred_element_type=f32)
    _, norm_first_back = jax.vjp(rms_norm, flat, attn_gain.astype(f32))
    grad_flat_part, grad_attn_gain = norm_first_back(grad_normed)
    grad_input = grad_after + grad_flat_part
    return grad_input, grad_attn_gain, (normed, grad_query_pre, grad_key_pre, grad_value_pre, mixed, low)


def over_groups(value):
    bit = 8
    while bit < lax.axis_size("dp"):
        value = value + flip(value, bit)
        bit *= 2
    return value


def tokens_dot(left, right):
    return jnp.einsum("td,tf->df", left, right, preferred_element_type=f32)


def plane_reduce(make):
    _, chip, _ = place()
    dg, xn = make(chip ^ 3).astype(bf16), make(chip ^ 1).astype(bf16)
    yn, own = make(chip ^ 2).astype(bf16), make(chip)
    half = own.shape[0] // 2
    dg_x, xn_x = flip(dg[:half], SIDE), flip(xn[:half], SIDE)
    dg_y, yn_y = flip(dg[half:], BACK), flip(yn[half:], BACK)
    yn_top = (yn[:half].astype(f32) + dg_x.astype(f32)).astype(bf16)
    xn_bottom = (xn[half:].astype(f32) + dg_y.astype(f32)).astype(bf16)
    yn_top, xn_bottom = flip(yn_top, BACK), flip(xn_bottom, SIDE)
    top = own[:half] + xn_x.astype(f32) + yn_top.astype(f32)
    bottom = own[half:] + yn_y.astype(f32) + xn_bottom.astype(f32)
    return jnp.concatenate([top, bottom], axis=0)


def ring_reduce(parts):
    z = lax.axis_index("fsdp")
    depth = lax.axis_size("fsdp")
    low = parts.astype(bf16)
    total = lax.dynamic_index_in_dim(parts, z, 0, keepdims=False)
    for s in range(1, depth):
        part = lax.dynamic_index_in_dim(low, (z + s) % depth, 0, keepdims=False)
        total = total + turn_z(part, s).astype(f32)
    return total


def chips_gather(piece, axis):
    _, chip, _ = place()
    x, y, dg = flip(piece, SIDE), flip(piece, BACK), flip(piece, SIDE | BACK)
    shape = list(piece.shape)
    n = shape[axis]
    shape[axis] *= 4
    full = jnp.zeros((4,) + piece.shape, piece.dtype)
    for who, part in enumerate((piece, x, y, dg)):
        full = lax.dynamic_update_index_in_dim(full, part, chip ^ who, 0)
    return full


def split_reduce(make):
    core, _, _ = place()
    depth = lax.axis_size("fsdp")
    piece = plane_reduce(make)
    piece = piece.reshape((depth, piece.shape[0] // depth) + piece.shape[1:])
    piece = over_groups(ring_reduce(piece)).astype(bf16)
    mine = chips_gather(piece, 1)
    other = flip(mine, CORE)
    return jnp.where(core == 0, mine, other), jnp.where(core == 0, other, mine)


def pair_tokens(mine_first, mine_second, core):
    sent = jnp.where(core == 0, mine_second, mine_first)
    kept = jnp.where(core == 0, mine_first, mine_second)
    return jnp.concatenate([kept, flip(sent, CORE)], axis=0)


def both_tokens(value):
    return jnp.concatenate([value, flip(value, CORE)], axis=0)


def join(parts):
    return jnp.concatenate([parts[m] for m in range(4)], axis=1).astype(f32)


def reduce_ffn(saves):
    core, chip, z = place()
    depth = lax.axis_size("fsdp")
    normed, dg, du, hidden, low = (jnp.concatenate(v, axis=0) for v in zip(*saves))
    width = normed.shape[1]
    rows = hidden.shape[1] // depth
    half = 2 * rows
    z_both = pair_tokens(hidden[:, :half], hidden[:, half:], core)
    low_both = both_tokens(low)
    down = tokens_dot(z_both, low_both).reshape(2, rows, width)
    low_down = down.astype(bf16)
    total = jnp.where((z >> 1) == core, lax.dynamic_index_in_dim(down, z & 1, 0, keepdims=False), 0.0)
    count = lax.axis_size("dp")
    for s in range(1, depth):
        part = lax.dynamic_index_in_dim(low_down, (z + s) & 1, 0, keepdims=False)
        pairs = []
        for d in range(count):
            for a in range(depth):
                b = (a + s) % depth
                if (b >> 1) == (d & 1):
                    pairs.append((d * depth + a, d * depth + b))
        total = total + lax.ppermute(part, ("dp", "fsdp"), pairs).astype(f32)
    n = rows // 8
    owner = (z >> 1) == core
    mine = total.reshape(2, rows // 2, width)
    given = flip(mine.astype(bf16), CORE).astype(f32)
    mine = lax.dynamic_index_in_dim(jnp.where(owner, mine, given), core, 0, keepdims=False)
    mine = mine.reshape(4, n, width)
    summed = over_groups(plane_reduce(lambda m: lax.dynamic_index_in_dim(mine, m, 0, keepdims=False))).astype(bf16)
    summed = chips_gather(summed, 0).reshape(rows // 2, width)
    other = flip(summed, CORE)
    grad_down = jnp.where(core == 0, jnp.concatenate([summed, other]), jnp.concatenate([other, summed])).astype(f32)
    act = pair_tokens(dg, du, core)
    b_both = both_tokens(normed)
    n = act.shape[1] // 4

    def make(m):
        return tokens_dot(b_both, lax.dynamic_slice_in_dim(act, m * n, n, 1))

    grad_gate, grad_up = split_reduce(make)
    return join(grad_gate), join(grad_up), grad_down


def reduce_attention(saves):
    core, chip, z = place()
    normed, dq, dk, dv, mixed, low = (jnp.concatenate(v, axis=0) for v in zip(*saves))
    width = normed.shape[1]
    n = KVW
    zero = jnp.zeros_like(low)
    first = jnp.concatenate([dq, dk], axis=1)
    second = jnp.concatenate([dv, low], axis=1)
    right = pair_tokens(first, second, core)
    left_a = both_tokens(normed)
    left_o = both_tokens(mixed)

    def make(m):
        cols = lax.dynamic_slice_in_dim(right, m * n, n, 1)
        left = jnp.where((core == 1) & (m > 0), left_o, left_a)
        return tokens_dot(left, cols)

    qk, vo = split_reduce(make)
    qk, vo = join(qk), join(vo)
    return qk[:, :width], qk[:, width:], vo[:, :KVW], vo[:, KVW:]


def reduce_gains(gains):
    z = lax.axis_index("fsdp")
    depth = lax.axis_size("fsdp")
    total = jnp.stack(gains)
    bit = 1
    while bit < lax.axis_size("dp"):
        total = total + flip(total, bit)
        bit *= 2
    rows = total.shape[1] // depth
    total = total + sum(turn_z(total, s) for s in range(1, depth))
    mine = lax.dynamic_slice_in_dim(total, z * rows, rows, 1)
    return mine[0], mine[1]


def body(tokens, segment_ids, attn_gain, query_weight, key_weight, value_weight, out_weight, ffn_gain, gate_weight, up_weight, down_weight, cotangent):
    core, chip, z = place()
    _, stretch, width = tokens.shape
    depth = lax.axis_size("fsdp")
    gains = ring_gather(jnp.stack([attn_gain, ffn_gain]))
    gains = jnp.moveaxis(gains, 0, 1).reshape(2, width)
    tokens = home_to_work(tokens[0])
    row = ring_gather(segment_ids[0]).reshape(-1)
    other = flip(row, CORE)
    row = jnp.where((z >> 1) == core, row, other)
    block = 2 * (z & 1) + core
    padded = jnp.concatenate([jnp.full((2 * stretch,), -1, row.dtype), row])
    key_segments = lax.dynamic_slice(padded, (block * stretch,), (3 * stretch,))
    own_segments = key_segments[2 * stretch :]
    key_index = jnp.arange(3 * stretch, dtype=jnp.int32)
    query_index = 2 * stretch + jnp.arange(stretch, dtype=jnp.int32)
    allowed = (own_segments[:, None] == key_segments[None, :]) & (key_index[None, :] <= query_index[:, None])
    positions = jnp.sum(allowed.astype(jnp.int32), axis=1) - 1
    tables = rope_tables(positions)
    allowed = allowed[None, None]
    q, k, v, o, g, u, dn = gather_weights(query_weight, key_weight, value_weight, out_weight, gate_weight, up_weight, down_weight)
    weights = (gains[0], q, k, v, o, gains[1], g, u, dn)
    cot = home_to_work(cotangent[0])
    state = tokens.astype(f32)
    saved_runs = []
    for step in range(RUNS):
        state, saved = forward_run(state, weights, tables, allowed)
        saved_runs.append(saved)
    output = home_to_work(state.astype(bf16), back=True)
    grad_state = cot.astype(f32)
    ffn_saves, attn_saves = [], []
    gain_attn = gain_ffn = 0.0
    for saved in reversed(saved_runs):
        grad_state, gain, save = backward_ffn(grad_state, saved, weights)
        gain_ffn = gain_ffn + gain
        ffn_saves.append(save)
        grad_state, gain, save = backward_attention(grad_state, saved, weights, tables, allowed)
        gain_attn = gain_attn + gain
        attn_saves.append(save)
    grad_tokens = home_to_work(grad_state.astype(bf16), back=True).astype(f32)
    grad_gate, grad_up, grad_down = reduce_ffn(ffn_saves)
    grad_query, grad_key, grad_value, grad_out = reduce_attention(attn_saves)
    gain_attn, gain_ffn = reduce_gains((gain_attn, gain_ffn))
    return (output[None], grad_tokens[None], gain_attn, grad_query, grad_key, grad_value, grad_out, gain_ffn, grad_gate, grad_up, grad_down)


def solution(mesh):
    wide, rows, shard = P("dp", "fsdp", None), P("dp", "fsdp"), P("fsdp", None)
    in_specs = (wide, rows, P("fsdp"), shard, shard, shard, shard, P("fsdp"), shard, shard, shard, wide)
    out_specs = (wide, wide, P("fsdp"), shard, shard, shard, shard, P("fsdp"), shard, shard, shard)
    return jax.shard_map(body, mesh=mesh, in_specs=in_specs, out_specs=out_specs, check_vma=False)
```

time: 1320 us -> 810 us (0.61)
  waiting for transfers between devices: 664 us -> 151 us
  blocking collectives: 356 us -> 0 us
  starting transfers between devices: 1.44 us -> 177 us
  local copies, waits for them, and re-layouts: 38 us -> 178 us
  other arithmetic: 47.5 us -> 105 us
    reduce_scatter x8 -> x0, waiting for transfers between devices: 279 us -> none  [the longest x4 212 us: reduce_grads(): lax.psum_scatter(shortened(grads), 'fsdp', scatter_dimension=0, tiled=True)]
    all_gather x5 -> x0, waiting for transfers between devices: 240 us -> none  [the longest x1 87.1 us: body(): lax.all_gather(shards[7], 'fsdp', axis=0, tiled=True)]
    psum x1 -> x0, blocking collectives: 200 us -> none  [reduce_grads(): return lax.psum(local_sums, 'dp')]
    ppermute x0 -> x118, starting transfers between devices: none -> 177 us  [the longest x79 68.1 us: flip(): return lax.ppermute(value, 'dp', [(i, i ^ bit) for i in range(count)])]
    ppermute x0 -> x118, waiting for transfers between devices: none -> 151 us  [the longest x79 72.8 us: flip(): return lax.ppermute(value, 'dp', [(i, i ^ bit) for i in range(count)])]
    unnamed x19 -> x0, waiting for transfers between devices: 146 us -> none
    all_gather x7 -> x0, blocking collectives: 134 us -> none  [the longest x2 41.9 us: forward_run(): lax.all_gather(keys, 'fsdp', axis=1, tiled=True)]
    dynamic_update_slice x0 -> x60, local copies, waits for them, and re-layouts: none -> 114 us  [the longest x8 25.7 us: plane_gather(): lax.dynamic_update_slice(full, b[None, None], (core, at, half) + rest)]
  transfers between devices with their start and end apart: 16 -> 118, of which waited for: 13 -> 32; matrix products, arithmetic and copies ran while one was open for 11% -> 56% of each run, Pallas kernels for 0% -> 0%
where the time goes in v1:
time: 810 us; the launch traced here: 799 us
  matrix products  183 us (23%)
  local copies, waits for them, and re-layouts  178 us (22%)
  starting transfers between devices  177 us (22%)
  waiting for transfers between devices  151 us (19%)
  other arithmetic  105 us (13%)
    ppermute x79, waiting for transfers between devices, flip(): return lax.ppermute(value, 'dp', [(i, i ^ bit) for i in range(count)])  72.8 us
    ppermute x79, starting transfers between devices, flip(): return lax.ppermute(value, 'dp', [(i, i ^ bit) for i in range(count)])  68.1 us
    ppermute x24, starting transfers between devices, turn_z(): lax.ppermute(value, 'fsdp', [(i, (i + step) % count) for i in range(count)])  65.2 us
    ppermute x24, waiting for transfers between devices, turn_z(): lax.ppermute(value, 'fsdp', [(i, (i + step) % count) for i in range(count)])  55.2 us
    dot_general x32, matrix products, dot(): return jnp.dot(a, b, preferred_element_type=f32)  52.1 us
    dynamic_update_slice x8, local copies, waits for them, and re-layouts, plane_gather(): lax.dynamic_update_slice(full, b[None, None], (core, at, half) + rest)  25.7 us
    dot_general x9, matrix products, tokens_dot(): return jnp.einsum('td,tf->df', left, right, preferred_element_type=f32)  25 us
    dynamic_update_slice x8, local copies, waits for them, and re-layouts, plane_gather(): full = lax.dynamic_update_slice(full, t[None, None], (core, at, 0) + rest)  24.6 us
  transfers between devices with their start and end apart: 118, of which 32 were waited for; matrix products, arithmetic and copies ran while one was open for 56% of the time, Pallas kernels for 0%

profile of v1, /device:TPU:0, one launch (start us, length us, event | category | flops | bytes accessed | tf_op | source)
XLA Modules:
  0.0 799.0 jit_solution(11942778963481844018)
XLA Ops:
  19.8 3.4 collective-permute-start.23
  51.0 4.3 dynamic_update_slice.212
  55.4 4.6 dynamic_update_slice.213
  66.3 4.6 broadcast_in_dim.334
  78.0 4.5 dynamic_update_slice.214
  84.9 4.8 dynamic_update_slice.215
  89.9 4.4 dynamic_update_slice.216
  95.8 4.8 dynamic_update_slice.217
  104.9 6.0 collective-permute-done.14
  110.9 12.4 %collective-permute-done.47 = bf16[320,960]{1,0:T(8,128)(2,1)} collective-permute-done((bf16[320,960]{1,0:T(8,128)(2,1)S(1)}, bf16[320,960]{1,0:T(8,128)(2,1)}, u32[]{:S(2)}, u32[]{:S(2)}) %collective-permute-start.47) | collective-permute-done | bytes 614432 | tf_op jit(solution)/shard_map/ppermute | solution.py:27
  134.0 3.5 bitcast_dynamic-update-slice_fusion
  137.6 4.5 dynamic_update_slice.218
  142.1 4.6 dynamic_update_slice.219
  146.7 4.5 dynamic_update_slice.220
  151.2 4.7 dynamic_update_slice.221
  156.0 4.5 dynamic_update_slice.222
  160.5 4.8 dynamic_update_slice.223
  167.6 4.5 dynamic_update_slice.224
  172.9 4.7 dynamic_update_slice.225
  179.9 11.1 %collective-permute-start.19 = (bf16[480,320]{0,1:T(8,128)(2,1)}, bf16[480,320]{0,1:T(8,128)(2,1)S(1)}, u32[]{:S(2)}, u32[]{:S(2)}) collective-permute-start(bf16[480,320]{0,1:T(8,128)(2,1)} %copy-done.159), channel_id=1, source_target_pairs={{0,4},{4,0},{8,12},{12,8},{16,20},{20,16},{24,28},{28,24},{1,5},{5... | collective-permute-start | bytes 921608 | tf_op jit(solution)/shard_map/ppermute | solution.py:22
  197.8 4.3 dynamic_update_slice.226
  202.2 4.7 dynamic_update_slice.227
  206.9 3.8 slice_bitcast_fusion.46
  214.5 6.7 collective-permute-start.27
  221.8 3.4 collective-permute-done.27
  225.2 4.4 collective-permute-start.21
  229.7 3.2 collective-permute-done.21
  240.2 12.2 %fusion.86 = bf16[5,64,3,256]{3,1,2,0:T(8,128)(2,1)S(1)} fusion(bf16[768,5,64,1]{0,2,3,1:T(8,128)(2,1)S(1)} %bitcast.713, f32[5,3,256]{2,1,0:T(4,128)S(1)} %fusion.6, f32[5,3,256]{2,1,0:T(4,128)S(1)} %get-tuple-element.201, f32[5,768,256,3]{2,1,3,0:T(8,128)S(1)} %get-tuple-element.202, pred[256,768]{0,1:T(8,128)(4,1)S(1)} %fusion.132), kind=kOutput, calls=%fused_computation.162 | convolution fusion | flops 392478720 | bytes 13006848 | tf_op jit(solution)/shard_map/kgcl,lkd->ckgd/dot_general | solution.py:188
  263.4 6.2 collective-permute-done.42
  269.6 3.9 collective-permute-done.43
  309.9 4.4 collective-permute-start.50
  324.3 6.1 fusion.19
  330.5 6.8 fusion.7
  337.4 6.8 fusion.85
  382.5 8.8 %fusion.3 = (f32[5,3,256]{2,1,0:T(4,128)S(1)}, f32[5,768,256,3]{2,1,3,0:T(8,128)}) fusion(f32[5,3,256]{2,1,0:T(4,128)S(1)} %log_add_fusion.1, f32[5,768,256,3]{2,1,3,0:T(8,128)} %get-tuple-element.216, pred[256,768]{0,1:T(8,128)(4,1)S(1)} %fusion.132, bf16[768,5,64,1]{0,2,3,1:T(8,128)(2,1)S(1)} %bitcast.716, bf16[256,5,3,64]{0,3,2,1:T(8,128)(2,1)S(1)} %bitcast.727), kind=kOutput, calls=%fused_computation.7 | convolution fusion | flops 392229120 | bytes 24803328 | tf_op jit(solution)/shard_map/ckgd,lkd->kgcl/dot_general | solution.py:235
  391.3 9.4 %fusion.5 = bf16[5,3,256,768]{2,3,1,0:T(8,128)(2,1)S(1)} fusion(f32[5,768,256,3]{2,1,3,0:T(8,128)} %get-tuple-element.221, f32[5,3,256]{2,1,0:T(4,128)S(1)} %get-tuple-element.220, f32[5,3,256]{2,1,0:T(4,128)S(1)} %log_add_fusion.1, f32[5,768,256,3]{2,1,3,0:T(8,128)} %get-tuple-element.216, pred[256,768]{0,1:T(8,128)(4,1)S(1)} %fusion.132), kind=kLoop, calls=%fused_computation.9 | loop fusion | flops 17694720 | bytes 29718528 | tf_op jit(solution)/shard_map/convert_element_type | solution.py:238
  404.8 8.4 %fusion.52 = f32[768,5,64]{0,2,1:T(8,128)} fusion(bf16[256,5,3,64]{0,3,2,1:T(8,128)(2,1)S(1)} %bitcast.728, f32[5,3,256]{2,1,0:T(4,128)S(1)} %log_add_fusion.1, f32[5,768,256,3]{2,1,3,0:T(8,128)} %get-tuple-element.216, pred[256,768]{0,1:T(8,128)(4,1)S(1)} %fusion.132), kind=kOutput, calls=%fused_computation.113 | convolution fusion | flops 389283840 | bytes 13483008 | tf_op jit(solution)/shard_map/kgcl,ckgd->lkd/dot_general | solution.py:236
  420.0 14.0 %maximum_maximum_fusion.2 = bf16[512,2560]{0,1:T(8,128)(2,1)S(1)} fusion(bf16[256,640]{0,1:T(8,128)(2,1)S(1)} %copy-done.100, bf16[256,640]{0,1:T(8,128)(2,1)S(1)} %copy-done.102, bf16[256,640]{0,1:T(8,128)(2,1)S(1)} %copy-done.104, bf16[256,640]{0,1:T(8,128)(2,1)S(1)} %copy-done.110, bf16[256,640]{0,1:T(8,128)(2,1)S(1)} %copy-done.106, ...), kind=kLoop, calls=%fused_computation.49 | loop fusion | flops 20971520 | bytes 5242880 | tf_op jit(solution)/shard_map/concatenate | solution.py:333
  441.7 5.9 collective-permute-done.57
  474.3 6.4 fusion
  480.7 6.8 fusion.2
  500.6 6.3 collective-permute-done.61
  513.0 6.2 broadcast_select_fusion.4
  519.8 10.7 %broadcast_select_fusion = bf16[512,2560]{0,1:T(8,128)(2,1)} fusion(pred[]{:T(512)S(6)} %eq.81, bf16[256,640]{0,1:T(8,128)(2,1)S(1)} %copy-done.88, bf16[256,640]{0,1:T(8,128)(2,1)S(1)} %copy-done.91, bf16[256,640]{0,1:T(8,128)(2,1)S(1)} %copy-done.94, bf16[256,640]{0,1:T(8,128)(2,1)S(1)} %copy-done.97, bf16[256,640]{0,1:T(8,128)(2,1)S(1)} %copy-done.76, ...), kind=kLoop, calls=%fused_computation.56 | loop fusion | flops 43253760 | bytes 7864321 | tf_op jit(solution)/shard_map/jit(_where)/select_n | solution.py:317
  532.0 5.2 collective-permute-start.54
  537.2 4.1 fusion.20
  566.9 5.3 collective-permute-start.64
  573.1 5.2 collective-permute-start.70
  585.9 4.5 collective-permute-start.104
  593.1 10.8 %broadcast_select_fusion.1 = bf16[512,2560]{0,1:T(8,128)(2,1)} fusion(pred[]{:T(512)S(6)} %eq.81, bf16[256,640]{0,1:T(8,128)(2,1)S(1)} %copy-done.89, bf16[256,640]{0,1:T(8,128)(2,1)S(1)} %copy-done.92, bf16[256,640]{0,1:T(8,128)(2,1)S(1)} %copy-done.95, bf16[256,640]{0,1:T(8,128)(2,1)} %copy-done.96, bf16[256,640]{0,1:T(8,128)(2,1)S(1)} %copy-done.77, ...), kind=kLoop, calls=%fused_computation.57 | loop fusion | flops 43253760 | bytes 7864321 | tf_op jit(solution)/shard_map/jit(_where)/select_n | solution.py:318
  604.0 17.6 %collective-permute-done.82 = bf16[240,320]{0,1:T(8,128)(2,1)S(1)} collective-permute-done((bf16[240,320]{0,1:T(8,128)(2,1)S(1)}, bf16[240,320]{0,1:T(8,128)(2,1)S(1)}, u32[]{:S(2)}, u32[]{:S(2)}) %collective-permute-start.82) | collective-permute-done | bytes 153632 | tf_op jit(solution)/shard_map/ppermute | solution.py:27
  621.6 25.1 %collective-permute-start.81 = (bf16[240,320]{0,1:T(8,128)(2,1)S(1)}, bf16[240,320]{0,1:T(8,128)(2,1)S(1)}, u32[]{:S(2)}, u32[]{:S(2)}) collective-permute-start(bf16[240,320]{0,1:T(8,128)(2,1)S(1)} %get-tuple-element.182), channel_id=1, source_target_pairs={{0,2},{1,3},{2,0},{3,1},{4,6},{5,7},{6,4},{7,5},{8,10},{9,11},{10,... | collective-permute-start | bytes 460808 | tf_op jit(solution)/shard_map/ppermute | solution.py:27
  650.0 4.3 collective-permute-start.80
  657.0 4.6 collective-permute-done.80
  664.7 3.2 copy.389
  673.1 7.2 collective-permute-done.84
  702.1 3.6 collective-permute-done.93
  708.4 19.7 %collective-permute-done.109 = bf16[40,960]{1,0:T(8,128)(2,1)S(1)} collective-permute-done((bf16[40,960]{1,0:T(8,128)(2,1)S(1)}, bf16[40,960]{1,0:T(8,128)(2,1)S(1)}, u32[]{:S(2)}, u32[]{:S(2)}) %collective-permute-start.109) | collective-permute-done | bytes 76832 | tf_op jit(solution)/shard_map/ppermute | solution.py:22
  729.6 3.2 collective-permute-done.112
  743.5 3.8 collective-permute-done.97
  749.7 14.0 %collective-permute-done.96 = bf16[240,640]{1,0:T(8,128)(2,1)S(1)} collective-permute-done((bf16[240,640]{1,0:T(8,128)(2,1)S(1)}, bf16[240,640]{1,0:T(8,128)(2,1)S(1)}, u32[]{:S(2)}, u32[]{:S(2)}) %collective-permute-start.96) | collective-permute-done | bytes 307232 | tf_op jit(solution)/shard_map/ppermute | solution.py:27
  767.8 6.2 collective-permute-done.98
  774.0 4.4 collective-permute-done.99
  785.4 3.2 fusion.83
  (906 shorter events, 373.9 us)
Async XLA Ops:
  2.1 17.7 %collective-permute-start.1 = (bf16[2,240]{1,0:T(2,128)(2,1)S(1)}, bf16[2,240]{1,0:T(2,128)(2,1)S(1)}, u32[]{:S(2)}, u32[]{:S(2)}) collective-permute-start(bf16[2,240]{1,0:T(2,128)(2,1)S(1)} %get-tuple-element.89), channel_id=1, source_target_pairs={{0,1},{1,2},{2,3},{3,0},{4,5},{5,6},{6,7},{7,4},{8,9},{9,10},{10,1... | collective-permute-start | bytes 2888 | tf_op jit(solution)/shard_map/ppermute | solution.py:27
  5.2 18.0 %collective-permute-start.2 = (bf16[2,240]{1,0:T(2,128)(2,1)S(1)}, bf16[2,240]{1,0:T(2,128)(2,1)S(1)}, u32[]{:S(2)}, u32[]{:S(2)}) collective-permute-start(bf16[2,240]{1,0:T(2,128)(2,1)S(1)} %get-tuple-element.89), channel_id=1, source_target_pairs={{0,2},{1,3},{2,0},{3,1},{4,6},{5,7},{6,4},{7,5},{8,10},{9,11},{10,... | collective-permute-start | bytes 2888 | tf_op jit(solution)/shard_map/ppermute | solution.py:27
  7.8 15.4 %collective-permute-start.3 = (bf16[2,240]{1,0:T(2,128)(2,1)S(1)}, bf16[2,240]{1,0:T(2,128)(2,1)S(1)}, u32[]{:S(2)}, u32[]{:S(2)}) collective-permute-start(bf16[2,240]{1,0:T(2,128)(2,1)S(1)} %get-tuple-element.89), channel_id=1, source_target_pairs={{0,3},{1,0},{2,1},{3,2},{4,7},{5,4},{6,5},{7,6},{8,11},{9,8},{10,9... | collective-permute-start | bytes 2888 | tf_op jit(solution)/shard_map/ppermute | solution.py:27
  13.2 18.5 %collective-permute-start.4 = (bf16[240,320]{0,1:T(8,128)(2,1)}, bf16[240,320]{0,1:T(8,128)(2,1)}, u32[]{:S(2)}, u32[]{:S(2)}) collective-permute-start(bf16[240,320]{0,1:T(8,128)(2,1)} %get-tuple-element.87), channel_id=1, source_target_pairs={{0,1},{1,2},{2,3},{3,0},{4,5},{5,6},{6,7},{7,4},{8,9},{9,10},{10,1... | collective-permute-start | bytes 460808 | tf_op jit(solution)/shard_map/ppermute | solution.py:27
  13.9 20.7 %collective-permute-start.5 = (bf16[240,320]{0,1:T(8,128)(2,1)}, bf16[240,320]{0,1:T(8,128)(2,1)S(1)}, u32[]{:S(2)}, u32[]{:S(2)}) collective-permute-start(bf16[240,320]{0,1:T(8,128)(2,1)} %get-tuple-element.87), channel_id=1, source_target_pairs={{0,2},{1,3},{2,0},{3,1},{4,6},{5,7},{6,4},{7,5},{8,10},{9,11},{10,... | collective-permute-start | bytes 460808 | tf_op jit(solution)/shard_map/ppermute | solution.py:27
  27.7 32.3 %collective-permute-start.29 = (bf16[240,640]{1,0:T(8,128)(2,1)}, bf16[240,640]{1,0:T(8,128)(2,1)}, u32[]{:S(2)}, u32[]{:S(2)}) collective-permute-start(bf16[240,640]{1,0:T(8,128)(2,1)} %get-tuple-element.85), channel_id=1, source_target_pairs={{0,1},{1,2},{2,3},{3,0},{4,5},{5,6},{6,7},{7,4},{8,9},{9,10},{10,1... | collective-permute-start | bytes 921608 | tf_op jit(solution)/shard_map/ppermute | solution.py:27
  29.1 33.4 %collective-permute-start.30 = (bf16[240,640]{1,0:T(8,128)(2,1)}, bf16[240,640]{1,0:T(8,128)(2,1)}, u32[]{:S(2)}, u32[]{:S(2)}) collective-permute-start(bf16[240,640]{1,0:T(8,128)(2,1)} %get-tuple-element.85), channel_id=1, source_target_pairs={{0,2},{1,3},{2,0},{3,1},{4,6},{5,7},{6,4},{7,5},{8,10},{9,11},{10,... | collective-permute-start | bytes 921608 | tf_op jit(solution)/shard_map/ppermute | solution.py:27
  31.8 31.8 %collective-permute-start.31 = (bf16[240,640]{1,0:T(8,128)(2,1)}, bf16[240,640]{1,0:T(8,128)(2,1)}, u32[]{:S(2)}, u32[]{:S(2)}) collective-permute-start(bf16[240,640]{1,0:T(8,128)(2,1)} %get-tuple-element.85), channel_id=1, source_target_pairs={{0,3},{1,0},{2,1},{3,2},{4,7},{5,4},{6,5},{7,6},{8,11},{9,8},{10,9... | collective-permute-start | bytes 921608 | tf_op jit(solution)/shard_map/ppermute | solution.py:27
  36.1 64.5 %collective-permute-start = (bf16[256,960]{0,1:T(8,128)(2,1)}, bf16[256,960]{0,1:T(8,128)(2,1)S(1)}, u32[]{:S(2)}, u32[]{:S(2)}) collective-permute-start(bf16[256,960]{0,1:T(8,128)(2,1)} %bitcast.776), channel_id=1, source_target_pairs={{0,0},{1,4},{2,1},{3,5},{4,2},{5,6},{6,3},{7,7},{8,8},{9,12},{10,9... | collective-permute-start | bytes 1474568 | tf_op jit(solution)/shard_map/ppermute | solution.py:38
  45.6 29.3 %collective-permute-start.7 = (bf16[480,320]{0,1:T(8,128)(2,1)}, bf16[480,320]{0,1:T(8,128)(2,1)}, u32[]{:S(2)}, u32[]{:S(2)}) collective-permute-start(bf16[480,320]{0,1:T(8,128)(2,1)} %slice.440), channel_id=1, source_target_pairs={{0,4},{4,0},{8,12},{12,8},{16,20},{20,16},{24,28},{28,24},{1,5},{5... | collective-permute-start | bytes 921608 | tf_op jit(solution)/shard_map/ppermute | solution.py:22
  60.0 29.7 %collective-permute-start.9 = (bf16[480,320]{0,1:T(8,128)(2,1)}, bf16[480,320]{0,1:T(8,128)(2,1)S(1)}, u32[]{:S(2)}, u32[]{:S(2)}) collective-permute-start(bf16[480,320]{0,1:T(8,128)(2,1)} %slice.440), channel_id=1, source_target_pairs={{0,8},{4,12},{8,0},{12,4},{16,24},{20,28},{24,16},{28,20},{1,9},{5... | collective-permute-start | bytes 921608 | tf_op jit(solution)/shard_map/ppermute | solution.py:22
  62.5 20.0 %collective-permute-start.8 = (bf16[480,320]{0,1:T(8,128)(2,1)}, bf16[480,320]{0,1:T(8,128)(2,1)}, u32[]{:S(2)}, u32[]{:S(2)}) collective-permute-start(bf16[480,320]{0,1:T(8,128)(2,1)} %slice.441), channel_id=1, source_target_pairs={{0,4},{4,0},{8,12},{12,8},{16,20},{20,16},{24,28},{28,24},{1,5},{5... | collective-permute-start | bytes 921608 | tf_op jit(solution)/shard_map/ppermute | solution.py:22
  63.6 30.7 %collective-permute-start.10 = (bf16[480,320]{0,1:T(8,128)(2,1)}, bf16[480,320]{0,1:T(8,128)(2,1)}, u32[]{:S(2)}, u32[]{:S(2)}) collective-permute-start(bf16[480,320]{0,1:T(8,128)(2,1)} %slice.441), channel_id=1, source_target_pairs={{0,8},{4,12},{8,0},{12,4},{16,24},{20,28},{24,16},{28,20},{1,9},{5... | collective-permute-start | bytes 921608 | tf_op jit(solution)/shard_map/ppermute | solution.py:22
  74.9 26.7 %collective-permute-start.46 = (bf16[320,960]{1,0:T(8,128)(2,1)S(1)}, bf16[320,960]{1,0:T(8,128)(2,1)}, u32[]{:S(2)}, u32[]{:S(2)}) collective-permute-start(bf16[320,960]{1,0:T(8,128)(2,1)S(1)} %copy.430), channel_id=1, source_target_pairs={{0,1},{1,2},{2,3},{3,0},{4,5},{5,6},{6,7},{7,4},{8,9},{9,10},{10,1... | collective-permute-start | bytes 1843208 | tf_op jit(solution)/shard_map/ppermute | solution.py:27
  82.5 40.7 %collective-permute-start.47 = (bf16[320,960]{1,0:T(8,128)(2,1)S(1)}, bf16[320,960]{1,0:T(8,128)(2,1)}, u32[]{:S(2)}, u32[]{:S(2)}) collective-permute-start(bf16[320,960]{1,0:T(8,128)(2,1)S(1)} %copy.430), channel_id=1, source_target_pairs={{0,2},{1,3},{2,0},{3,1},{4,6},{5,7},{6,4},{7,5},{8,10},{9,11},{10,... | collective-permute-start | bytes 1843208 | tf_op jit(solution)/shard_map/ppermute | solution.py:27
  89.7 35.5 %collective-permute-start.48 = (bf16[320,960]{1,0:T(8,128)(2,1)S(1)}, bf16[320,960]{1,0:T(8,128)(2,1)S(1)}, u32[]{:S(2)}, u32[]{:S(2)}) collective-permute-start(bf16[320,960]{1,0:T(8,128)(2,1)S(1)} %copy.430), channel_id=1, source_target_pairs={{0,3},{1,0},{2,1},{3,2},{4,7},{5,4},{6,5},{7,6},{8,11},{9,8},{10,9... | collective-permute-start | bytes 1843208 | tf_op jit(solution)/shard_map/ppermute | solution.py:27
  101.6 24.1 %collective-permute-start.11 = (bf16[480,320]{0,1:T(8,128)(2,1)S(1)}, bf16[480,320]{0,1:T(8,128)(2,1)S(1)}, u32[]{:S(2)}, u32[]{:S(2)}) collective-permute-start(bf16[480,320]{0,1:T(8,128)(2,1)S(1)} %collective-permute-done.9), channel_id=1, source_target_pairs={{0,4},{4,0},{8,12},{12,8},{16,20},{20,16},{24,28},{28,24},{1,5},{5... | collective-permute-start | bytes 921608 | tf_op jit(solution)/shard_map/ppermute | solution.py:22
  104.9 21.8 %collective-permute-start.12 = (bf16[480,320]{0,1:T(8,128)(2,1)}, bf16[480,320]{0,1:T(8,128)(2,1)S(1)}, u32[]{:S(2)}, u32[]{:S(2)}) collective-permute-start(bf16[480,320]{0,1:T(8,128)(2,1)} %collective-permute-done.10), channel_id=1, source_target_pairs={{0,4},{4,0},{8,12},{12,8},{16,20},{20,16},{24,28},{28,24},{1,5},{5... | collective-permute-start | bytes 921608 | tf_op jit(solution)/shard_map/ppermute | solution.py:22
  110.9 16.4 %collective-permute-start.15 = (bf16[480,320]{0,1:T(8,128)(2,1)}, bf16[480,320]{0,1:T(8,128)(2,1)S(1)}, u32[]{:S(2)}, u32[]{:S(2)}) collective-permute-start(bf16[480,320]{0,1:T(8,128)(2,1)} %collective-permute-done.13), channel_id=1, source_target_pairs={{0,4},{4,0},{8,12},{12,8},{16,20},{20,16},{24,28},{28,24},{1,5},{5... | collective-permute-start | bytes 921608 | tf_op jit(solution)/shard_map/ppermute | solution.py:22
  125.2 52.3 %collective-permute-start.32 = (bf16[480,640]{1,0:T(8,128)(2,1)}, bf16[480,640]{1,0:T(8,128)(2,1)}, u32[]{:S(2)}, u32[]{:S(2)}) collective-permute-start(bf16[480,640]{1,0:T(8,128)(2,1)} %bitcast.60), channel_id=1, source_target_pairs={{0,4},{4,0},{8,12},{12,8},{16,20},{20,16},{24,28},{28,24},{1,5},{5... | collective-permute-start | bytes 1843208 | tf_op jit(solution)/shard_map/ppermute | solution.py:22
  125.7 54.1 %collective-permute-start.33 = (bf16[480,640]{1,0:T(8,128)(2,1)}, bf16[480,640]{1,0:T(8,128)(2,1)S(1)}, u32[]{:S(2)}, u32[]{:S(2)}) collective-permute-start(bf16[480,640]{1,0:T(8,128)(2,1)} %bitcast.62), channel_id=1, source_target_pairs={{0,4},{4,0},{8,12},{12,8},{16,20},{20,16},{24,28},{28,24},{1,5},{5... | collective-permute-start | bytes 1843208 | tf_op jit(solution)/shard_map/ppermute | solution.py:22
  126.7 65.2 %collective-permute-start.34 = (bf16[480,640]{1,0:T(8,128)(2,1)}, bf16[480,640]{1,0:T(8,128)(2,1)}, u32[]{:S(2)}, u32[]{:S(2)}) collective-permute-start(bf16[480,640]{1,0:T(8,128)(2,1)} %bitcast.60), channel_id=1, source_target_pairs={{0,8},{4,12},{8,0},{12,4},{16,24},{20,28},{24,16},{28,20},{1,9},{5... | collective-permute-start | bytes 1843208 | tf_op jit(solution)/shard_map/ppermute | solution.py:22
  127.3 38.0 %collective-permute-start.17 = (bf16[480,320]{0,1:T(8,128)(2,1)S(1)}, bf16[480,320]{0,1:T(8,128)(2,1)S(1)}, u32[]{:S(2)}, u32[]{:S(2)}) collective-permute-start(bf16[480,320]{0,1:T(8,128)(2,1)S(1)} %collective-permute-done.9), channel_id=1, source_target_pairs={{0,16},{4,20},{8,24},{12,28},{16,0},{20,4},{24,8},{28,12},{1,17},{... | collective-permute-start | bytes 921608 | tf_op jit(solution)/shard_map/ppermute | solution.py:22
  129.5 42.6 %collective-permute-start.18 = (bf16[480,320]{0,1:T(8,128)(2,1)}, bf16[480,320]{0,1:T(8,128)(2,1)S(1)}, u32[]{:S(2)}, u32[]{:S(2)}) collective-permute-start(bf16[480,320]{0,1:T(8,128)(2,1)} %collective-permute-done.14), channel_id=1, source_target_pairs={{0,8},{4,12},{8,0},{12,4},{16,24},{20,28},{24,16},{28,20},{1,9},{5... | collective-permute-start | bytes 921608 | tf_op jit(solution)/shard_map/ppermute | solution.py:22
  166.0 151.1 %collective-permute-start.55 = (bf16[256,960]{0,1:T(8,128)(2,1)}, bf16[256,960]{0,1:T(8,128)(2,1)S(1)}, u32[]{:S(2)}, u32[]{:S(2)}) collective-permute-start(bf16[256,960]{0,1:T(8,128)(2,1)} %bitcast.777), channel_id=1, source_target_pairs={{0,0},{1,4},{2,1},{3,5},{4,2},{5,6},{6,3},{7,7},{8,8},{9,12},{10,9... | collective-permute-start | bytes 1474568 | tf_op jit(solution)/shard_map/ppermute | solution.py:38
  172.2 21.7 %collective-permute-start.35 = (bf16[480,640]{1,0:T(8,128)(2,1)}, bf16[480,640]{1,0:T(8,128)(2,1)}, u32[]{:S(2)}, u32[]{:S(2)}) collective-permute-start(bf16[480,640]{1,0:T(8,128)(2,1)} %bitcast.62), channel_id=1, source_target_pairs={{0,8},{4,12},{8,0},{12,4},{16,24},{20,28},{24,16},{28,20},{1,9},{5... | collective-permute-start | bytes 1843208 | tf_op jit(solution)/shard_map/ppermute | solution.py:22
  177.5 79.6 %collective-permute-start.38 = (bf16[480,640]{1,0:T(8,128)(2,1)}, bf16[480,640]{1,0:T(8,128)(2,1)}, u32[]{:S(2)}, u32[]{:S(2)}) collective-permute-start(bf16[480,640]{1,0:T(8,128)(2,1)} %bitcast.60), channel_id=1, source_target_pairs={{0,16},{4,20},{8,24},{12,28},{16,0},{20,4},{24,8},{28,12},{1,17},{... | collective-permute-start | bytes 1843208 | tf_op jit(solution)/shard_map/ppermute | solution.py:22
  179.9 17.7 %collective-permute-start.19 = (bf16[480,320]{0,1:T(8,128)(2,1)}, bf16[480,320]{0,1:T(8,128)(2,1)S(1)}, u32[]{:S(2)}, u32[]{:S(2)}) collective-permute-start(bf16[480,320]{0,1:T(8,128)(2,1)} %copy-done.159), channel_id=1, source_target_pairs={{0,4},{4,0},{8,12},{12,8},{16,20},{20,16},{24,28},{28,24},{1,5},{5... | collective-permute-start | bytes 921608 | tf_op jit(solution)/shard_map/ppermute | solution.py:22
  193.9 59.6 %collective-permute-start.39 = (bf16[480,640]{1,0:T(8,128)(2,1)}, bf16[480,640]{1,0:T(8,128)(2,1)}, u32[]{:S(2)}, u32[]{:S(2)}) collective-permute-start(bf16[480,640]{1,0:T(8,128)(2,1)} %bitcast.62), channel_id=1, source_target_pairs={{0,16},{4,20},{8,24},{12,28},{16,0},{20,4},{24,8},{28,12},{1,17},{... | collective-permute-start | bytes 1843208 | tf_op jit(solution)/shard_map/ppermute | solution.py:22
  197.6 57.5 %collective-permute-start.36 = (bf16[480,640]{1,0:T(8,128)(2,1)}, bf16[480,640]{1,0:T(8,128)(2,1)}, u32[]{:S(2)}, u32[]{:S(2)}) collective-permute-start(bf16[480,640]{1,0:T(8,128)(2,1)} %collective-permute-done.34), channel_id=1, source_target_pairs={{0,4},{4,0},{8,12},{12,8},{16,20},{20,16},{24,28},{28,24},{1,5},{5... | collective-permute-start | bytes 1843208 | tf_op jit(solution)/shard_map/ppermute | solution.py:22
  238.7 19.3 %collective-permute-start.37 = (bf16[480,640]{1,0:T(8,128)(2,1)}, bf16[480,640]{1,0:T(8,128)(2,1)S(1)}, u32[]{:S(2)}, u32[]{:S(2)}) collective-permute-start(bf16[480,640]{1,0:T(8,128)(2,1)} %collective-permute-done.35), channel_id=1, source_target_pairs={{0,4},{4,0},{8,12},{12,8},{16,20},{20,16},{24,28},{28,24},{1,5},{5... | collective-permute-start | bytes 1843208 | tf_op jit(solution)/shard_map/ppermute | solution.py:22
  253.4 16.2 %collective-permute-start.42 = (bf16[480,640]{1,0:T(8,128)(2,1)}, bf16[480,640]{1,0:T(8,128)(2,1)S(1)}, u32[]{:S(2)}, u32[]{:S(2)}) collective-permute-start(bf16[480,640]{1,0:T(8,128)(2,1)} %collective-permute-done.34), channel_id=1, source_target_pairs={{0,16},{4,20},{8,24},{12,28},{16,0},{20,4},{24,8},{28,12},{1,17},{... | collective-permute-start | bytes 1843208 | tf_op jit(solution)/shard_map/ppermute | solution.py:22
  255.1 19.3 %collective-permute-start.41 = (bf16[480,640]{1,0:T(8,128)(2,1)}, bf16[480,640]{1,0:T(8,128)(2,1)S(1)}, u32[]{:S(2)}, u32[]{:S(2)}) collective-permute-start(bf16[480,640]{1,0:T(8,128)(2,1)} %collective-permute-done.39), channel_id=1, source_target_pairs={{0,4},{4,0},{8,12},{12,8},{16,20},{20,16},{24,28},{28,24},{1,5},{5... | collective-permute-start | bytes 1843208 | tf_op jit(solution)/shard_map/ppermute | solution.py:22
  257.1 16.5 %collective-permute-start.43 = (bf16[480,640]{1,0:T(8,128)(2,1)}, bf16[480,640]{1,0:T(8,128)(2,1)S(1)}, u32[]{:S(2)}, u32[]{:S(2)}) collective-permute-start(bf16[480,640]{1,0:T(8,128)(2,1)} %collective-permute-done.39), channel_id=1, source_target_pairs={{0,8},{4,12},{8,0},{12,4},{16,24},{20,28},{24,16},{28,20},{1,9},{5... | collective-permute-start | bytes 1843208 | tf_op jit(solution)/shard_map/ppermute | solution.py:22
  263.1 36.1 %collective-permute-start.49 = (bf16[4,320,960]{2,1,0:T(8,128)(2,1)}, bf16[4,320,960]{2,1,0:T(8,128)(2,1)S(1)}, u32[]{:S(2)}, u32[]{:S(2)}) collective-permute-start(bf16[4,320,960]{2,1,0:T(8,128)(2,1)} %bitcast_dynamic-update-slice_fusion.2), channel_id=1, source_target_pairs={{0,4},{4,0},{8,12},{12,8},{16,20},{20,16},{24,28},{28,24},{1,5},{5... | collective-permute-start | bytes 7372808 | tf_op jit(solution)/shard_map/ppermute | solution.py:22
  316.0 229.6 %collective-permute-start.72 = (bf16[512,960]{0,1:T(8,128)(2,1)}, bf16[512,960]{0,1:T(8,128)(2,1)}, u32[]{:S(2)}, u32[]{:S(2)}) collective-permute-start(bf16[512,960]{0,1:T(8,128)(2,1)} %pad_maximum_fusion.10), channel_id=1, source_target_pairs={{0,4},{4,0},{8,12},{12,8},{16,20},{20,16},{24,28},{28,24},{1,5},{5... | collective-permute-start | bytes 2949128 | tf_op jit(solution)/shard_map/ppermute | solution.py:22
  419.1 19.5 %collective-permute-start.56 = (bf16[256,320]{0,1:T(8,128)(2,1)S(1)}, bf16[256,320]{0,1:T(8,128)(2,1)S(1)}, u32[]{:S(2)}, u32[]{:S(2)}) collective-permute-start(bf16[256,320]{0,1:T(8,128)(2,1)S(1)} %bitcast.750), channel_id=1, source_target_pairs={{0,4},{4,0},{8,12},{12,8},{16,20},{20,16},{24,28},{28,24},{1,5},{5... | collective-permute-start | bytes 491528 | tf_op jit(solution)/shard_map/ppermute | solution.py:22
  419.5 20.5 %collective-permute-start.58 = (bf16[256,320]{0,1:T(8,128)(2,1)S(1)}, bf16[256,320]{0,1:T(8,128)(2,1)S(1)}, u32[]{:S(2)}, u32[]{:S(2)}) collective-permute-start(bf16[256,320]{0,1:T(8,128)(2,1)S(1)} %bitcast.752), channel_id=1, source_target_pairs={{0,4},{4,0},{8,12},{12,8},{16,20},{20,16},{24,28},{28,24},{1,5},{5... | collective-permute-start | bytes 491528 | tf_op jit(solution)/shard_map/ppermute | solution.py:22
  435.7 96.3 %collective-permute-start.102 = (bf16[512,1280]{0,1:T(8,128)(2,1)}, bf16[512,1280]{0,1:T(8,128)(2,1)}, u32[]{:S(2)}, u32[]{:S(2)}) collective-permute-start(bf16[512,1280]{0,1:T(8,128)(2,1)} %get-tuple-element.102), channel_id=1, source_target_pairs={{0,4},{4,0},{8,12},{12,8},{16,20},{20,16},{24,28},{28,24},{1,5},{5... | collective-permute-start | bytes 3932168 | tf_op jit(solution)/shard_map/ppermute | solution.py:22
  510.7 26.5 %collective-permute-start.103 = (bf16[512,960]{0,1:T(8,128)(2,1)S(1)}, bf16[512,960]{0,1:T(8,128)(2,1)S(1)}, u32[]{:S(2)}, u32[]{:S(2)}) collective-permute-start(bf16[512,960]{0,1:T(8,128)(2,1)S(1)} %pad_maximum_fusion.12), channel_id=1, source_target_pairs={{0,4},{4,0},{8,12},{12,8},{16,20},{20,16},{24,28},{28,24},{1,5},{5... | collective-permute-start | bytes 2949128 | tf_op jit(solution)/shard_map/ppermute | solution.py:22
  519.2 26.3 %collective-permute-start.73 = (bf16[512,1280]{0,1:T(8,128)(2,1)S(1)}, bf16[512,1280]{0,1:T(8,128)(2,1)S(1)}, u32[]{:S(2)}, u32[]{:S(2)}) collective-permute-start(bf16[512,1280]{0,1:T(8,128)(2,1)S(1)} %get-tuple-element.103), channel_id=1, source_target_pairs={{0,4},{4,0},{8,12},{12,8},{16,20},{20,16},{24,28},{28,24},{1,5},{5... | collective-permute-start | bytes 3932168 | tf_op jit(solution)/shard_map/ppermute | solution.py:22
  532.0 51.0 %collective-permute-start.54 = (bf16[256,960]{0,1:T(8,128)(2,1)}, bf16[256,960]{0,1:T(8,128)(2,1)}, u32[]{:S(2)}, u32[]{:S(2)}) collective-permute-start(bf16[256,960]{0,1:T(8,128)(2,1)} %fusion.84), channel_id=1, source_target_pairs={{0,0},{4,1},{1,2},{5,3},{2,4},{6,5},{3,6},{7,7},{8,8},{12,9},{9,10... | collective-permute-start | bytes 1474568 | tf_op jit(solution)/shard_map/ppermute | solution.py:38
  566.9 23.6 %collective-permute-start.64 = (bf16[256,960]{0,1:T(8,128)(2,1)}, bf16[256,960]{0,1:T(8,128)(2,1)}, u32[]{:S(2)}, u32[]{:S(2)}) collective-permute-start(bf16[256,960]{0,1:T(8,128)(2,1)} %fusion.97), channel_id=1, source_target_pairs={{0,0},{4,1},{1,2},{5,3},{2,4},{6,5},{3,6},{7,7},{8,8},{12,9},{9,10... | collective-permute-start | bytes 1474568 | tf_op jit(solution)/shard_map/ppermute | solution.py:38
  583.0 97.4 %collective-permute-start.88 = (bf16[512,2560]{0,1:T(8,128)(2,1)}, bf16[512,2560]{0,1:T(8,128)(2,1)}, u32[]{:S(2)}, u32[]{:S(2)}) collective-permute-start(bf16[512,2560]{0,1:T(8,128)(2,1)} %broadcast_select_fusion), channel_id=1, source_target_pairs={{0,4},{4,0},{8,12},{12,8},{16,20},{20,16},{24,28},{28,24},{1,5},{5... | collective-permute-start | bytes 7864328 | tf_op jit(solution)/shard_map/ppermute | solution.py:22
  583.1 78.6 %collective-permute-start.106 = (bf16[640,960]{0,1:T(8,128)(2,1)}, bf16[640,960]{0,1:T(8,128)(2,1)S(1)}, u32[]{:S(2)}, u32[]{:S(2)}) collective-permute-start(bf16[640,960]{0,1:T(8,128)(2,1)} %get-tuple-element.106), channel_id=1, source_target_pairs={{1,0},{2,1},{4,7},{7,6},{9,8},{10,9},{12,15},{15,14},{17,16},{18,1... | collective-permute-start | bytes 3686408 | tf_op jit(solution)/shard_map/ppermute | solution.py:351
  584.6 78.1 %collective-permute-start.105 = (bf16[640,960]{0,1:T(8,128)(2,1)}, bf16[640,960]{0,1:T(8,128)(2,1)S(1)}, u32[]{:S(2)}, u32[]{:S(2)}) collective-permute-start(bf16[640,960]{0,1:T(8,128)(2,1)} %get-tuple-element.107), channel_id=1, source_target_pairs={{2,0},{3,1},{4,6},{5,7},{10,8},{11,9},{12,14},{13,15},{18,16},{19,... | collective-permute-start | bytes 3686408 | tf_op jit(solution)/shard_map/ppermute | solution.py:351
  585.9 76.8 %collective-permute-start.104 = (bf16[640,960]{0,1:T(8,128)(2,1)}, bf16[640,960]{0,1:T(8,128)(2,1)S(1)}, u32[]{:S(2)}, u32[]{:S(2)}) collective-permute-start(bf16[640,960]{0,1:T(8,128)(2,1)} %get-tuple-element.105), channel_id=1, source_target_pairs={{0,1},{3,0},{5,6},{6,7},{8,9},{11,8},{13,14},{14,15},{16,17},{19,1... | collective-permute-start | bytes 3686408 | tf_op jit(solution)/shard_map/ppermute | solution.py:351
  590.5 31.1 %collective-permute-start.82 = (bf16[240,320]{0,1:T(8,128)(2,1)S(1)}, bf16[240,320]{0,1:T(8,128)(2,1)S(1)}, u32[]{:S(2)}, u32[]{:S(2)}) collective-permute-start(bf16[240,320]{0,1:T(8,128)(2,1)S(1)} %get-tuple-element.181), channel_id=1, source_target_pairs={{0,3},{1,0},{2,1},{3,2},{4,7},{5,4},{6,5},{7,6},{8,11},{9,8},{10,9... | collective-permute-start | bytes 460808 | tf_op jit(solution)/shard_map/ppermute | solution.py:27
  621.6 28.4 %collective-permute-start.81 = (bf16[240,320]{0,1:T(8,128)(2,1)S(1)}, bf16[240,320]{0,1:T(8,128)(2,1)S(1)}, u32[]{:S(2)}, u32[]{:S(2)}) collective-permute-start(bf16[240,320]{0,1:T(8,128)(2,1)S(1)} %get-tuple-element.182), channel_id=1, source_target_pairs={{0,2},{1,3},{2,0},{3,1},{4,6},{5,7},{6,4},{7,5},{8,10},{9,11},{10,... | collective-permute-start | bytes 460808 | tf_op jit(solution)/shard_map/ppermute | solution.py:27
  661.6 18.8 %collective-permute-start.87 = (bf16[512,960]{0,1:T(8,128)(2,1)S(1)}, bf16[512,960]{0,1:T(8,128)(2,1)}, u32[]{:S(2)}, u32[]{:S(2)}) collective-permute-start(bf16[512,960]{0,1:T(8,128)(2,1)S(1)} %copy-done.116), channel_id=1, source_target_pairs={{0,4},{4,0},{8,12},{12,8},{16,20},{20,16},{24,28},{28,24},{1,5},{5... | collective-permute-start | bytes 2949128 | tf_op jit(solution)/shard_map/ppermute | solution.py:22
  670.1 37.1 %collective-permute-start.107 = (bf16[2,320,960]{2,1,0:T(8,128)(2,1)S(1)}, bf16[2,320,960]{2,1,0:T(8,128)(2,1)S(1)}, u32[]{:S(2)}, u32[]{:S(2)}) collective-permute-start(bf16[2,320,960]{2,1,0:T(8,128)(2,1)S(1)} %convert_element_type.595), channel_id=1, source_target_pairs={{0,4},{4,0},{8,12},{12,8},{16,20},{20,16},{24,28},{28,24},{1,5},{5... | collective-permute-start | bytes 3686408 | tf_op jit(solution)/shard_map/ppermute | solution.py:22
  680.3 16.5 %collective-permute-start.86 = (bf16[4,240,320]{1,2,0:T(8,128)(2,1)S(1)}, bf16[4,240,320]{1,2,0:T(8,128)(2,1)S(1)}, u32[]{:S(2)}, u32[]{:S(2)}) collective-permute-start(bf16[4,240,320]{1,2,0:T(8,128)(2,1)S(1)} %bitcast_dynamic-update-slice_fusion.31), channel_id=1, source_target_pairs={{0,4},{4,0},{8,12},{12,8},{16,20},{20,16},{24,28},{28,24},{1,5},{5... | collective-permute-start | bytes 1843208 | tf_op jit(solution)/shard_map/ppermute | solution.py:22
  683.7 16.7 %collective-permute-start.90 = (bf16[480,640]{1,0:T(8,128)(2,1)S(1)}, bf16[480,640]{1,0:T(8,128)(2,1)S(1)}, u32[]{:S(2)}, u32[]{:S(2)}) collective-permute-start(bf16[480,640]{1,0:T(8,128)(2,1)S(1)} %get-tuple-element.152), channel_id=1, source_target_pairs={{0,8},{4,12},{8,0},{12,4},{16,24},{20,28},{24,16},{28,20},{1,9},{5... | collective-permute-start | bytes 1843208 | tf_op jit(solution)/shard_map/ppermute | solution.py:22
  688.1 45.9 %collective-permute-start.89 = (bf16[480,640]{1,0:T(8,128)(2,1)S(1)}, bf16[480,640]{1,0:T(8,128)(2,1)S(1)}, u32[]{:S(2)}, u32[]{:S(2)}) collective-permute-start(bf16[480,640]{1,0:T(8,128)(2,1)S(1)} %slice.632), channel_id=1, source_target_pairs={{0,8},{4,12},{8,0},{12,4},{16,24},{20,28},{24,16},{28,20},{1,9},{5... | collective-permute-start | bytes 1843208 | tf_op jit(solution)/shard_map/ppermute | solution.py:22
  689.0 16.7 %collective-permute-start.93 = (bf16[480,640]{1,0:T(8,128)(2,1)S(1)}, bf16[480,640]{1,0:T(8,128)(2,1)S(1)}, u32[]{:S(2)}, u32[]{:S(2)}) collective-permute-start(bf16[480,640]{1,0:T(8,128)(2,1)S(1)} %get-tuple-element.153), channel_id=1, source_target_pairs={{0,16},{4,20},{8,24},{12,28},{16,0},{20,4},{24,8},{28,12},{1,17},{... | collective-permute-start | bytes 1843208 | tf_op jit(solution)/shard_map/ppermute | solution.py:22
  696.8 39.0 %collective-permute-start.92 = (bf16[480,640]{1,0:T(8,128)(2,1)S(1)}, bf16[480,640]{1,0:T(8,128)(2,1)S(1)}, u32[]{:S(2)}, u32[]{:S(2)}) collective-permute-start(bf16[480,640]{1,0:T(8,128)(2,1)S(1)} %slice.636), channel_id=1, source_target_pairs={{0,16},{4,20},{8,24},{12,28},{16,0},{20,4},{24,8},{28,12},{1,17},{... | collective-permute-start | bytes 1843208 | tf_op jit(solution)/shard_map/ppermute | solution.py:22
  700.6 35.6 %collective-permute-start.91 = (bf16[480,640]{1,0:T(8,128)(2,1)S(1)}, bf16[480,640]{1,0:T(8,128)(2,1)S(1)}, u32[]{:S(2)}, u32[]{:S(2)}) collective-permute-start(bf16[480,640]{1,0:T(8,128)(2,1)S(1)} %add_convert_fusion.1), channel_id=1, source_target_pairs={{0,16},{4,20},{8,24},{12,28},{16,0},{20,4},{24,8},{28,12},{1,17},{... | collective-permute-start | bytes 1843208 | tf_op jit(solution)/shard_map/ppermute | solution.py:22
  705.9 31.0 %collective-permute-start.94 = (bf16[480,640]{1,0:T(8,128)(2,1)S(1)}, bf16[480,640]{1,0:T(8,128)(2,1)S(1)}, u32[]{:S(2)}, u32[]{:S(2)}) collective-permute-start(bf16[480,640]{1,0:T(8,128)(2,1)S(1)} %add_convert_fusion), channel_id=1, source_target_pairs={{0,8},{4,12},{8,0},{12,4},{16,24},{20,28},{24,16},{28,20},{1,9},{5... | collective-permute-start | bytes 1843208 | tf_op jit(solution)/shard_map/ppermute | solution.py:22
  707.5 20.6 %collective-permute-start.109 = (bf16[40,960]{1,0:T(8,128)(2,1)S(1)}, bf16[40,960]{1,0:T(8,128)(2,1)S(1)}, u32[]{:S(2)}, u32[]{:S(2)}) collective-permute-start(bf16[40,960]{1,0:T(8,128)(2,1)S(1)} %get-tuple-element.195), channel_id=1, source_target_pairs={{0,8},{4,12},{8,0},{12,4},{16,24},{20,28},{24,16},{28,20},{1,9},{5... | collective-permute-start | bytes 230408 | tf_op jit(solution)/shard_map/ppermute | solution.py:22
  739.5 24.1 %collective-permute-start.96 = (bf16[240,640]{1,0:T(8,128)(2,1)S(1)}, bf16[240,640]{1,0:T(8,128)(2,1)S(1)}, u32[]{:S(2)}, u32[]{:S(2)}) collective-permute-start(bf16[240,640]{1,0:T(8,128)(2,1)S(1)} %get-tuple-element.151), channel_id=1, source_target_pairs={{0,2},{1,3},{2,0},{3,1},{4,6},{5,7},{6,4},{7,5},{8,10},{9,11},{10,... | collective-permute-start | bytes 921608 | tf_op jit(solution)/shard_map/ppermute | solution.py:27
  739.5 24.1 %collective-permute-start.95 = (bf16[240,640]{1,0:T(8,128)(2,1)S(1)}, bf16[240,640]{1,0:T(8,128)(2,1)S(1)}, u32[]{:S(2)}, u32[]{:S(2)}) collective-permute-start(bf16[240,640]{1,0:T(8,128)(2,1)S(1)} %get-tuple-element.149), channel_id=1, source_target_pairs={{0,1},{1,2},{2,3},{3,0},{4,5},{5,6},{6,7},{7,4},{8,9},{9,10},{10,1... | collective-permute-start | bytes 921608 | tf_op jit(solution)/shard_map/ppermute | solution.py:27
  740.7 26.4 %collective-permute-start.114 = (bf16[80,960]{1,0:T(8,128)(2,1)S(1)}, bf16[80,960]{1,0:T(8,128)(2,1)S(1)}, u32[]{:S(2)}, u32[]{:S(2)}) collective-permute-start(bf16[80,960]{1,0:T(8,128)(2,1)S(1)} %pad_maximum_fusion.20), channel_id=1, source_target_pairs={{0,8},{4,12},{8,0},{12,4},{16,24},{20,28},{24,16},{28,20},{1,9},{5... | collective-permute-start | bytes 460808 | tf_op jit(solution)/shard_map/ppermute | solution.py:22
  741.8 36.8 %collective-permute-start.115 = (bf16[80,960]{1,0:T(8,128)(2,1)S(1)}, bf16[80,960]{1,0:T(8,128)(2,1)S(1)}, u32[]{:S(2)}, u32[]{:S(2)}) collective-permute-start(bf16[80,960]{1,0:T(8,128)(2,1)S(1)} %pad_maximum_fusion.20), channel_id=1, source_target_pairs={{0,16},{4,20},{8,24},{12,28},{16,0},{20,4},{24,8},{28,12},{1,17},{... | collective-permute-start | bytes 460808 | tf_op jit(solution)/shard_map/ppermute | solution.py:22
  747.3 31.3 %collective-permute-start.116 = (bf16[80,960]{1,0:T(8,128)(2,1)S(1)}, bf16[80,960]{1,0:T(8,128)(2,1)S(1)}, u32[]{:S(2)}, u32[]{:S(2)}) collective-permute-start(bf16[80,960]{1,0:T(8,128)(2,1)S(1)} %pad_maximum_fusion.20), channel_id=1, source_target_pairs={{0,24},{4,28},{8,16},{12,20},{16,8},{20,12},{24,0},{28,4},{1,25},{... | collective-permute-start | bytes 460808 | tf_op jit(solution)/shard_map/ppermute | solution.py:22
  (255 other events, 2768.0 us)

commit v2 on v1

v2 whole, which is shorter than its diff:
```python
import functools
import jax
import jax.numpy as jnp
from jax import lax
from jax.sharding import PartitionSpec as P
from jax.experimental import pallas as pl
from jax.experimental.pallas import tpu as pltpu

f32, bf16 = jnp.float32, jnp.bfloat16
eps = 1e-05
HEADS, KV_HEADS, HEAD_DIM, GROUP, KVW = 15, 5, 64, 3, 320
MIB = 1 << 20
WHOLE = pl.BlockSpec(memory_space=pltpu.VMEM)
LEFT = pl.BlockSpec(memory_space=pl.ANY)
SCALARS = pl.BlockSpec(memory_space=pltpu.SMEM)


def contract(a, b, i, j):
    return lax.dot_general(a, b, (((i,), (j,)), ((), ())), preferred_element_type=f32)


def nn(a, b):
    return contract(a, b, 1, 0)


def nt(a, b):
    return contract(a, b, 1, 1)


def tn(a, b):
    return contract(a, b, 0, 0)


def fetch(mine, other, kept, sems, core, chip):
    for who in range(4):
        at = chip ^ who
        pltpu.make_async_copy(mine[who], kept.at[core, at], sems.at[core, at]).start()
    for who in range(4):
        at = chip ^ who
        pltpu.make_async_copy(other[who], kept.at[1 - core, at], sems.at[1 - core, at]).start()


def arrived(kept, sems, *at):
    pltpu.make_async_copy(kept.at[at], kept.at[at], sems.at[at]).wait()


def normed(x, gain):
    return x * lax.rsqrt(jnp.mean(x * x, axis=-1, keepdims=True) + eps) * gain


def norm_back(x, gain, grad):
    r = lax.rsqrt(jnp.mean(x * x, axis=-1, keepdims=True) + eps)
    hat = x * r
    scaled = grad * gain
    dx = r * (scaled - hat * jnp.mean(scaled * hat, axis=-1, keepdims=True))
    return dx, jnp.sum(grad * hat, axis=0, keepdims=True)


def rope(u, cos, sin, back):
    heads = u.shape[0] // HEAD_DIM
    half = HEAD_DIM // 2
    out = []
    for h in range(heads):
        u1, u2 = u[h * HEAD_DIM : h * HEAD_DIM + half], u[h * HEAD_DIM + half : (h + 1) * HEAD_DIM]
        if back:
            out += [u1 * cos + u2 * sin, u2 * cos - u1 * sin]
        else:
            out += [u1 * cos - u2 * sin, u2 * cos + u1 * sin]
    return jnp.concatenate(out, axis=0)


def project(state, gain_ref, cos_ref, sin_ref, kept, sems, a_ref, q_ref, kv_ref):
    a = normed(state, gain_ref[...]).astype(bf16)
    a_ref[...] = a
    cos, sin = cos_ref[...], sin_ref[...]
    arrived(kept, sems, 0, 3)
    kv_ref[:KVW, :] = rope(nn(a, kept[0, 3]).T, cos, sin, False).astype(bf16)
    arrived(kept, sems, 1, 0)
    kv_ref[KVW:, :] = nn(a, kept[1, 0]).T.astype(bf16)
    for m in range(3):
        arrived(kept, sems, 0, m)
        q_ref[pl.ds(m * KVW, KVW), :] = rope(nn(a, kept[0, m]).T, cos, sin, False).astype(bf16)


def pre_kernel(sc, h_ref, gain_ref, cos_ref, sin_ref, *rest):
    mine, other = rest[:4], rest[4:8]
    a_ref, q_ref, kv_ref, kept, sems = rest[8:]
    core, chip = sc[0], sc[1]
    fetch(mine, other, kept, sems, core, chip)
    project(h_ref[...].astype(f32), gain_ref, cos_ref, sin_ref, kept, sems, a_ref, q_ref, kv_ref)
    for m in range(1, 4):
        arrived(kept, sems, 1, m)


def scratch_a(width):
    return [pltpu.VMEM((2, 4, width, KVW), bf16), pltpu.SemaphoreType.DMA((2, 4))]


def shape(s, d):
    return jax.ShapeDtypeStruct(s, d)


def pre(sc, h, gain, cos, sin, mine_a, other_a):
    n, width = h.shape
    return pl.pallas_call(
        pre_kernel,
        out_shape=(shape((n, width), bf16), shape((width, n), bf16), shape((2 * KVW, n), bf16)),
        in_specs=[SCALARS] + [WHOLE] * 4 + [LEFT] * 8,
        out_specs=(WHOLE,) * 3,
        scratch_shapes=scratch_a(width),
        compiler_params=pltpu.CompilerParams(vmem_limit_bytes=24 * MIB),
        name="pre",
    )(sc, h, gain, cos, sin, *mine_a, *other_a)


def bias_of(seg_k, seg_q):
    keys, n = seg_k.shape[0], seg_q.shape[1]
    j = lax.broadcasted_iota(jnp.int32, (keys, n), 0)
    i = lax.broadcasted_iota(jnp.int32, (keys, n), 1) + (keys - n)
    return jnp.where((seg_k == seg_q) & (j <= i), 0.0, -1e30).astype(f32)


def window_of(parts, whole):
    n = parts[0].shape[1]
    for w, part in enumerate(parts):
        whole[:, w * n : (w + 1) * n] = part[...]


def attend_kernel(q_ref, kv0, kv1, kv2, sk_ref, sq_ref, o_ref, lse_ref, bias, kv):
    bias[...] = bias_of(sk_ref[...], sq_ref[...])
    window_of((kv0, kv1, kv2), kv)

    def head(e, _):
        row = pl.multiple_of(e * HEAD_DIM, HEAD_DIM)
        k = kv[pl.ds(row, HEAD_DIM), :]
        v = kv[pl.ds(row + KVW, HEAD_DIM), :]
        for g in range(GROUP):
            at = pl.multiple_of((e * GROUP + g) * HEAD_DIM, HEAD_DIM)
            q = q_ref[pl.ds(at, HEAD_DIM), :]
            s = tn(k, q) * HEAD_DIM ** (-0.5) + bias[...]
            top = jnp.max(s, axis=0, keepdims=True)
            expo = jnp.exp(s - top)
            total = jnp.sum(expo, axis=0, keepdims=True)
            probs = (expo * (1.0 / total)).astype(bf16)
            o_ref[pl.ds(at, HEAD_DIM), :] = nn(v, probs).astype(bf16)
            lse_ref[pl.ds(e * GROUP + g, 1), :] = top + jnp.log(total)
        return 0

    lax.fori_loop(0, KV_HEADS, head, 0)


def attend(q, kvs, seg_k, seg_q):
    width, n = q.shape
    return pl.pallas_call(
        attend_kernel,
        out_shape=(shape((width, n), bf16), shape((HEADS, n), f32)),
        in_specs=[WHOLE] * 6,
        out_specs=(WHOLE,) * 2,
        scratch_shapes=[pltpu.VMEM((3 * n, n), f32), pltpu.VMEM((2 * KVW, 3 * n), bf16)],
        compiler_params=pltpu.CompilerParams(vmem_limit_bytes=24 * MIB),
        name="attend",
    )(q, *kvs, seg_k, seg_q)


def attend_back_kernel(q_ref, kv0, kv1, kv2, sk_ref, sq_ref, lse_ref, do_ref, cos_ref, sin_ref, dq_ref, far_ref, near_ref, own_ref, bias, kv, dqs):
    n = q_ref.shape[1]
    bias[...] = bias_of(sk_ref[...], sq_ref[...])
    window_of((kv0, kv1, kv2), kv)
    scale = HEAD_DIM ** (-0.5)

    def head(e, _):
        row = pl.multiple_of(e * HEAD_DIM, HEAD_DIM)
        k = kv[pl.ds(row, HEAD_DIM), :]
        v = kv[pl.ds(row + KVW, HEAD_DIM), :]
        dk = dv = None
        for g in range(GROUP):
            at = pl.multiple_of((e * GROUP + g) * HEAD_DIM, HEAD_DIM)
            q = q_ref[pl.ds(at, HEAD_DIM), :]
            do = do_ref[pl.ds(at, HEAD_DIM), :]
            s = tn(k, q) * scale + bias[...]
            probs = jnp.exp(s - lse_ref[pl.ds(e * GROUP + g, 1), :])
            dp = tn(v, do)
            inner = jnp.sum(probs * dp, axis=0, keepdims=True)
            ds = (probs * (dp - inner)).astype(bf16)
            dvg, dkg = nt(do, probs.astype(bf16)), nt(q, ds)
            dv, dk = (dvg, dkg) if g == 0 else (dv + dvg, dk + dkg)
            dqs[pl.ds(at, HEAD_DIM), :] = nn(k, ds)
        for at, grad in ((row, dk * scale), (row + KVW, dv)):
            far_ref[pl.ds(at, HEAD_DIM), :] = grad[:, :n]
            near_ref[pl.ds(at, HEAD_DIM), :] = grad[:, n : 2 * n].astype(bf16)
            own_ref[pl.ds(at, HEAD_DIM), :] = grad[:, 2 * n :]
        return 0

    lax.fori_loop(0, KV_HEADS, head, 0)
    cos, sin = cos_ref[...] * scale, sin_ref[...] * scale
    for m in range(3):
        dq_ref[m] = rope(dqs[m * KVW : (m + 1) * KVW, :], cos, sin, True).T.astype(bf16)


def attend_back(q, kvs, seg_k, seg_q, lse, do, cos, sin):
    width, n = q.shape
    block = (2 * KVW, n)
    return pl.pallas_call(
        attend_back_kernel,
        out_shape=(shape((3, n, KVW), bf16), shape(block, f32), shape(block, bf16), shape(block, f32)),
        in_specs=[WHOLE] * 10,
        out_specs=(WHOLE,) * 4,
        scratch_shapes=[pltpu.VMEM((3 * n, n), f32), pltpu.VMEM((2 * KVW, 3 * n), bf16), pltpu.VMEM((width, n), f32)],
        compiler_params=pltpu.CompilerParams(vmem_limit_bytes=32 * MIB),
        name="attend_back",
    )(q, *kvs, seg_k, seg_q, lse, do, cos, sin)


def fetch_ffn(mine_b, other_b, mine_d, other_d, wb, wd, sem_b, sem_d, core, chip):
    fetch(mine_b, other_b, wb, sem_b, core, chip)
    pltpu.make_async_copy(mine_d, wd.at[:, core], sem_d.at[0]).start()
    pltpu.make_async_copy(other_d, wd.at[:, 1 - core], sem_d.at[1]).start()


def arrived_down(mine_d, wd, sem_d):
    for c in range(2):
        pltpu.make_async_copy(mine_d, wd.at[:, c], sem_d.at[c]).wait()


def down_of(wd, m):
    rows = wd.shape[1] * wd.shape[2]
    return wd[m].reshape(rows, wd.shape[3])


def scratch_ffn(width, n, rows):
    return [
        pltpu.VMEM((2, 4, width, n), bf16),
        pltpu.SemaphoreType.DMA((2, 4)),
        pltpu.VMEM((4, 2, rows, width), bf16),
        pltpu.SemaphoreType.DMA((2,)),
    ]


def post_kernel(last, sc, ot_ref, h_ref, gain_ref, gain_a, cos_ref, sin_ref, *rest):
    mine_a, other_a, mine_b, other_b = rest[:4], rest[4:8], rest[8:12], rest[12:16]
    mine_d, other_d = rest[16:18]
    o_ref, h1_ref, b_ref, gate_ref, up_ref, z_ref, next_ref = rest[18:25]
    more, rest = rest[25 : 25 + (0 if last else 3)], rest[25 + (0 if last else 3) :]
    wa, sem_a, wb, sem_b, wd, sem_d = rest
    core, chip = sc[0], sc[1]
    fetch(mine_a, other_a, wa, sem_a, core, chip)
    fetch_ffn(mine_b, other_b, mine_d, other_d, wb, wd, sem_b, sem_d, core, chip)
    o = ot_ref[...].T
    o_ref[...] = o
    for m in range(1, 4):
        arrived(wa, sem_a, 1, m)
    h1 = h_ref[...].astype(f32) + jnp.concatenate([nn(o, wa[1, m]) for m in range(1, 4)], axis=1)
    h1_ref[...] = h1
    b = normed(h1, gain_ref[...]).astype(bf16)
    b_ref[...] = b
    n = wb.shape[3]
    total = h1
    for m in range(4):
        cols = slice(m * n, (m + 1) * n)
        arrived(wb, sem_b, 0, m)
        gate = nn(b, wb[0, m])
        arrived(wb, sem_b, 1, m)
        up = nn(b, wb[1, m])
        gate_ref[:, cols] = gate.astype(bf16)
        up_ref[:, cols] = up.astype(bf16)
        z = (gate / (1.0 + jnp.exp(-gate)) * up).astype(bf16)
        z_ref[:, cols] = z
        if m == 0:
            arrived_down(mine_d, wd, sem_d)
        total = total + nn(z, down_of(wd, m))
    next_ref[...] = total.astype(next_ref.dtype)
    if last:
        arrived(wa, sem_a, 1, 0)
        for m in range(4):
            arrived(wa, sem_a, 0, m)
    else:
        project(total, gain_a, cos_ref, sin_ref, wa, sem_a, *more)


def post(last, sc, ot, h, gain, gain_a, cos, sin, wa, wb, wd):
    width, n = ot.shape
    hidden = wb[0][0].shape[1] * 4
    outs = [shape((n, width), bf16), shape((n, width), f32), shape((n, width), bf16)] + [shape((n, hidden), bf16)] * 3
    outs += [shape((n, width), bf16 if last else f32)]
    if not last:
        outs += [shape((n, width), bf16), shape((width, n), bf16), shape((2 * KVW, n), bf16)]
    return pl.pallas_call(
        functools.partial(post_kernel, last),
        out_shape=tuple(outs),
        in_specs=[SCALARS] + [WHOLE] * 6 + [LEFT] * 18,
        out_specs=(WHOLE,) * len(outs),
        scratch_shapes=scratch_a(width) + scratch_ffn(width, hidden // 4, wd[0].shape[1]),
        compiler_params=pltpu.CompilerParams(vmem_limit_bytes=56 * MIB),
        name="post",
    )(sc, ot, h, gain, gain_a, cos, sin, *wa[0], *wa[1], *wb[0], *wb[1], *wd)


def ffn_back(state, core, refs, weights, mine_d):
    gate_ref, up_ref, h1_ref, gain_ref, z_ref, gb_ref, keep_ref, send_ref, zk_ref, zs_ref, g1_ref, p_ref, dgain_ref, do_ref = refs
    wa, sem_a, wb, sem_b, wd, sem_d = weights
    gb = state.astype(bf16)
    gb_ref[...] = gb
    n = wb.shape[3]
    half = 2 * n
    first = core == 0
    low, high = z_ref[:, :half], z_ref[:, half:]
    zk_ref[...] = jnp.where(first, low, high)
    zs_ref[...] = jnp.where(first, high, low)
    arrived_down(mine_d, wd, sem_d)
    db = None
    for m in range(4):
        cols = slice(m * n, (m + 1) * n)
        dz = nt(gb, down_of(wd, m))
        gate, up = gate_ref[:, cols].astype(f32), up_ref[:, cols].astype(f32)
        sig = 1.0 / (1.0 + jnp.exp(-gate))
        dup = (dz * (gate * sig)).astype(bf16)
        dgate = (dz * up * (sig * (1.0 + gate * (1.0 - sig)))).astype(bf16)
        keep_ref[:, cols] = jnp.where(first, dgate, dup)
        send_ref[:, cols] = jnp.where(first, dup, dgate)
        arrived(wb, sem_b, 0, m)
        part = nt(dgate, wb[0, m])
        arrived(wb, sem_b, 1, m)
        part = part + nt(dup, wb[1, m])
        db = part if m == 0 else db + part
    dx, dgain = norm_back(h1_ref[...], gain_ref[...], db)
    dgain_ref[...] = dgain
    g1 = state + dx
    g1_ref[...] = g1
    low = g1.astype(bf16)
    do = None
    for p in range(3):
        part = low[:, p * KVW : (p + 1) * KVW]
        p_ref[p] = part
        arrived(wa, sem_a, 1, p + 1)
        part = nt(wa[1, p + 1], part)
        do = part if p == 0 else do + part
    do_ref[...] = do.astype(bf16)


def finish_a(wa, sem_a, *left):
    for at in left:
        arrived(wa, sem_a, *at)


def query_back(dq_ref, wa, sem_a):
    da = None
    for m in range(3):
        arrived(wa, sem_a, 0, m)
        part = nt(dq_ref[m], wa[0, m])
        da = part if m == 0 else da + part
    return da


def project_back(da, own_ref, near_ref, far_ref, core, cos_ref, sin_ref, dk_ref, dv_ref, h, gain, wa, sem_a):
    cos, sin = cos_ref[...], sin_ref[...]
    grad = own_ref[...] + far_ref[...].astype(f32) + jnp.where(core == 0, near_ref[...].astype(f32), 0.0)
    dk = rope(grad[:KVW], cos, sin, True).T.astype(bf16)
    dv = grad[KVW:].T.astype(bf16)
    dk_ref[...] = dk
    dv_ref[...] = dv
    arrived(wa, sem_a, 0, 3)
    arrived(wa, sem_a, 1, 0)
    da = da + nt(dk, wa[0, 3]) + nt(dv, wa[1, 0])
    return norm_back(h, gain, da)


def back_kernel(start, end, sc, *rest):
    rest = list(rest)

    def take(n):
        out = rest[:n]
        del rest[:n]
        return out

    core, chip = sc[0], sc[1]
    mine_a, other_a = take(4), take(4)
    if not end:
        mine_b, other_b = take(4), take(4)
        mine_d, other_d = take(2)
    if start:
        (g_ref,) = take(1)
    else:
        g1_in, dq_ref, own_ref, near_ref, far_ref, h_ref, gain_a, cos_ref, sin_ref = take(9)
    if not end:
        ins = take(5)
    if not start:
        dk_ref, dv_ref, dgain_a = take(3)
    if end:
        (g_out,) = take(1)
    else:
        outs = take(9)
    wa, sem_a = take(2)
    fetch(mine_a, other_a, wa, sem_a, core, chip)
    if not end:
        wb, sem_b, wd, sem_d = take(4)
        fetch_ffn(mine_b, other_b, mine_d, other_d, wb, wd, sem_b, sem_d, core, chip)
    if start:
        state = g_ref[...].astype(f32)
    else:
        da = query_back(dq_ref, wa, sem_a)
        dx, dgain = project_back(da, own_ref, near_ref, far_ref, core, cos_ref, sin_ref, dk_ref, dv_ref, h_ref[...].astype(f32), gain_a[...], wa, sem_a)
        dgain_a[...] = dgain
        state = g1_in[...] + dx
    if end:
        g_out[...] = state.astype(bf16)
        finish_a(wa, sem_a, (1, 1), (1, 2), (1, 3))
    else:
        ffn_back(state, core, (*ins, *outs), (wa, sem_a, wb, sem_b, wd, sem_d), mine_d)
        if start:
            finish_a(wa, sem_a, (1, 0), (0, 0), (0, 1), (0, 2), (0, 3))


def back(start, end, sc, weights, tail, ffn):
    wa, wb, wd = weights
    width = wa[0][0].shape[0]
    args = [sc, *wa[0], *wa[1]]
    specs = [SCALARS] + [LEFT] * 8
    scratch = scratch_a(width)
    if not end:
        args += [*wb[0], *wb[1], *wd]
        specs += [LEFT] * 10
        scratch += scratch_ffn(width, wb[0][0].shape[1], wd[0].shape[1])
    args += list(tail)
    specs += [WHOLE] * len(tail)
    n = tail[0].shape[0]
    outs = []
    if not end:
        args += list(ffn)
        specs += [WHOLE] * len(ffn)
    if not start:
        outs += [shape((n, KVW), bf16), shape((n, KVW), bf16), shape((1, width), f32)]
    if end:
        outs += [shape((n, width), bf16)]
    else:
        hidden = ffn[0].shape[1]
        outs += [shape((n, width), bf16), shape((n, hidden), bf16), shape((n, hidden), bf16), shape((n, hidden // 2), bf16), shape((n, hidden // 2), bf16)]
        outs += [shape((n, width), f32), shape((3, n, KVW), bf16), shape((1, width), f32), shape((width, n), bf16)]
    return pl.pallas_call(
        functools.partial(back_kernel, start, end),
        out_shape=tuple(outs),
        in_specs=specs,
        out_specs=(WHOLE,) * len(outs),
        scratch_shapes=scratch,
        compiler_params=pltpu.CompilerParams(vmem_limit_bytes=(24 if end else 56) * MIB),
        name="back_end" if end else ("back_start" if start else "back_join"),
    )(*args)


def by_turn(core, chip):
    one = 1 + core
    return chip ^ one, chip ^ 3, chip, chip ^ (3 - one)


def turned(dst, blocks):
    n = blocks[0].shape[0]
    for i, block in enumerate(blocks):
        dst[:, i * n : (i + 1) * n] = block[...].T


def grad_ffn_kernel(sc, *rest):
    lefts, rights = rest[:4], rest[4:8]
    send_ref, keep_ref, left, right = rest[8:]
    core, chip = sc[0], sc[1]
    n, cols = rights[0].shape[0], right.shape[1]
    turned(left, lefts)
    for i, m in enumerate(by_turn(core, chip)):
        at = pl.multiple_of(m * cols, 128)
        for j, block in enumerate(rights):
            right[j * n : (j + 1) * n, :] = block[:, pl.ds(at, cols)]
        out = send_ref if i < 2 else keep_ref
        out[i % 2] = nn(left[...], right[...]).astype(bf16)


def grad_ffn(sc, lefts, rights):
    n, width = lefts[0].shape
    cols = rights[0].shape[1] // 4
    out = shape((2, width, cols), bf16)
    return pl.pallas_call(
        grad_ffn_kernel,
        out_shape=(out, out),
        in_specs=[SCALARS] + [WHOLE] * 8,
        out_specs=(WHOLE,) * 2,
        scratch_shapes=[pltpu.VMEM((width, 4 * n), bf16), pltpu.VMEM((4 * n, cols), bf16)],
        compiler_params=pltpu.CompilerParams(vmem_limit_bytes=48 * MIB),
        name="grad_ffn",
    )(sc, *lefts, *rights)


def grad_down_kernel(*rest):
    lefts, rights = rest[:4], rest[4:8]
    out_ref, left, right = rest[8:]
    n, rows = rights[0].shape[0], out_ref.shape[1]
    turned(left, lefts)
    for j, block in enumerate(rights):
        right[j * n : (j + 1) * n, :] = block[...]
    for i in range(2):
        out_ref[i] = nn(left[i * rows : (i + 1) * rows, :], right[...]).astype(bf16)


def grad_down(lefts, rights):
    n, rows = lefts[0].shape
    width = rights[0].shape[1]
    return pl.pallas_call(
        grad_down_kernel,
        out_shape=shape((2, rows // 2, width), bf16),
        in_specs=[WHOLE] * 8,
        out_specs=WHOLE,
        scratch_shapes=[pltpu.VMEM((rows, 4 * n), bf16), pltpu.VMEM((4 * n, width), bf16)],
        compiler_params=pltpu.CompilerParams(vmem_limit_bytes=40 * MIB),
        name="grad_down",
    )(*lefts, *rights)


def grad_attention_kernel(sc, *rest):
    a_refs, o_refs, rights = rest[:4], rest[4:8], rest[8:12]
    send_ref, keep_ref, left, right = rest[12:]
    core, chip = sc[0], sc[1]
    n = rights[0].shape[1]
    turned(left.at[0], a_refs)

    @pl.when(core == 1)
    def _():
        turned(left.at[1], o_refs)

    for i, m in enumerate(by_turn(core, chip)):
        for j, block in enumerate(rights):
            right[j * n : (j + 1) * n, :] = block[m]
        out = send_ref if i < 2 else keep_ref
        which = jnp.where(m > 0, core, 0)
        out[i % 2] = nn(left[which], right[...]).astype(bf16)


def grad_attention(sc, a, o, rights):
    n, width = a[0].shape
    cols = rights[0].shape[2]
    out = shape((2, width, cols), bf16)
    return pl.pallas_call(
        grad_attention_kernel,
        out_shape=(out, out),
        in_specs=[SCALARS] + [WHOLE] * 12,
        out_specs=(WHOLE,) * 2,
        scratch_shapes=[pltpu.VMEM((2, width, 4 * n), bf16), pltpu.VMEM((4 * n, cols), bf16)],
        compiler_params=pltpu.CompilerParams(vmem_limit_bytes=40 * MIB),
        name="grad_attention",
    )(sc, *a, *o, *rights)


def lay_kernel(sc, *rest):
    mine, other, outs, kept = rest[:4], rest[4:8], rest[8:-1], rest[-1]
    core, chip = sc[0], sc[1]
    for who in range(4):
        kept[core, chip ^ who] = mine[who][...]
        kept[1 - core, chip ^ who] = other[who][...]
    cols = [jnp.concatenate([kept[c, m].astype(f32) for m in range(4)], axis=1) for c in range(2)]
    if len(outs) == 2:
        outs[0][...] = cols[0]
        outs[1][...] = cols[1]
    else:
        n = kept.shape[3]
        outs[0][...] = cols[0][:, : 3 * n]
        outs[1][...] = cols[0][:, 3 * n :]
        outs[2][...] = cols[1][:, :n]
        outs[3][...] = cols[1][:, n:]


def lay(sc, mine, other, pieces):
    rows, n = mine[0].shape
    outs = tuple(shape((rows, p * n), f32) for p in pieces)
    return pl.pallas_call(
        lay_kernel,
        out_shape=outs,
        in_specs=[SCALARS] + [WHOLE] * 8,
        out_specs=(WHOLE,) * len(outs),
        scratch_shapes=[pltpu.VMEM((2, 4, rows, n), bf16)],
        compiler_params=pltpu.CompilerParams(vmem_limit_bytes=32 * MIB),
        name="lay",
    )(sc, *mine, *other)


CORE, SIDE, BACK = 1, 2, 4
rope_base = 10000.0
RUNS = 2


def flip(value, bit, bit1=None):
    count = lax.axis_size("dp")
    bits = (bit, bit if bit1 is None else bit1)
    return lax.ppermute(value, "dp", [(i, i ^ bits[i & 1]) for i in range(count)])


def turn_z(value, step):
    count = lax.axis_size("fsdp")
    return lax.ppermute(value, "fsdp", [(i, (i + step) % count) for i in range(count)])


def home_to_work(value, back=False):
    count, depth = lax.axis_size("dp"), lax.axis_size("fsdp")
    pairs = []
    for d in range(count):
        for z in range(depth):
            there = (d & ~1) | (z & 1), 2 * (d & 1) + (z >> 1)
            pair = (d * depth + z, there[0] * depth + there[1])
            pairs.append(pair[::-1] if back else pair)
    return lax.ppermute(value, ("dp", "fsdp"), pairs)


def place():
    d, z = lax.axis_index("dp"), lax.axis_index("fsdp")
    return d & 1, (d >> 1) & 3, z


def ring_gather(shard):
    z = lax.axis_index("fsdp")
    depth = lax.axis_size("fsdp")
    parts = [shard] + [turn_z(shard, s) for s in range(1, depth)]
    full = jnp.zeros((depth,) + shard.shape, shard.dtype)
    for s, part in enumerate(parts):
        full = lax.dynamic_update_index_in_dim(full, part, (z - s) % depth, 0)
    return full


def plane_gather(piece):
    core, _, _ = place()
    x, y = flip(piece, SIDE), flip(piece, BACK)
    opposite = flip(jnp.where(core == 0, x, y), BACK, SIDE)
    mine = (piece, x, y, opposite)
    return mine, tuple(flip(p, CORE) for p in mine)


def gather_weights(query, key, value, out, gate, up, down):
    core, chip, _ = place()
    rows, width = query.shape
    depth = lax.axis_size("fsdp")
    first = jnp.concatenate([query, key, value, out], axis=1)
    n = first.shape[1] // 8
    piece = lax.dynamic_slice(first, (0, n * (core * 4 + chip)), (rows, n))
    wa = plane_gather(ring_gather(piece).reshape(depth * rows, n))
    n = gate.shape[1] // 4
    piece = lax.dynamic_slice(jnp.where(core == 0, gate, up), (0, n * chip), (rows, n))
    wb = plane_gather(ring_gather(piece).reshape(depth * rows, n))
    n = down.shape[0] // 2
    piece = ring_gather(lax.dynamic_slice(down, (n * core, 0), (n, width)))
    return wa, wb, (piece, flip(piece, CORE))


def window(own):
    core, _, _ = place()
    depth = lax.axis_size("fsdp")
    far = lax.ppermute(own, "fsdp", [(z, z + 1) for z in range(0, depth, 2)])
    near = flip(jnp.where(core == 0, own, far), CORE)
    return far, near, own


def unwindow(far, near):
    core, _, _ = place()
    depth = lax.axis_size("fsdp")
    near = flip(near, CORE)
    far = jnp.where(core == 1, far + near.astype(f32), far).astype(bf16)
    return near, lax.ppermute(far, "fsdp", [(z + 1, z) for z in range(0, depth, 2)])


def over_groups(value):
    bit = 8
    while bit < lax.axis_size("dp"):
        value = value + flip(value.astype(bf16), bit).astype(f32)
        bit *= 2
    return value


def plane_reduce(send, keep):
    got = flip(send, SIDE, BACK)
    later = (keep[1].astype(f32) + got[1].astype(f32)).astype(bf16)
    own = keep[0].astype(f32) + got[0].astype(f32)
    return own + flip(later, BACK, SIDE).astype(f32)


def ring_reduce(parts):
    _, _, z = place()
    depth = lax.axis_size("fsdp")
    low = parts.astype(bf16)
    total = lax.dynamic_index_in_dim(parts, z, 0, keepdims=False)
    for s in range(1, depth):
        part = lax.dynamic_index_in_dim(low, (z + s) % depth, 0, keepdims=False)
        total = total + turn_z(part, s).astype(f32)
    return total


def spread(piece):
    mine = (piece, flip(piece, SIDE), flip(piece, BACK), flip(piece, SIDE | BACK))
    return mine, tuple(flip(p, CORE) for p in mine)


def reduce_pieces(sc, send, keep, pieces):
    depth = lax.axis_size("fsdp")
    own = plane_reduce(send, keep)
    own = own.reshape((depth, own.shape[0] // depth) + own.shape[1:])
    own = over_groups(ring_reduce(own)).astype(bf16)
    return lay(sc, *spread(own), pieces)


def reduce_down(parts):
    core, chip, z = place()
    depth, count = lax.axis_size("fsdp"), lax.axis_size("dp")
    _, rows, width = parts.shape
    owner = (z >> 1) == core
    total = lax.dynamic_index_in_dim(parts, z & 1, 0, keepdims=False).astype(f32)
    for s in range(1, depth):
        part = lax.dynamic_index_in_dim(parts, (z + s) & 1, 0, keepdims=False)
        pairs = []
        for d in range(count):
            for a in range(depth):
                b = (a + s) % depth
                if (b >> 1) == (d & 1):
                    pairs.append((d * depth + a, d * depth + b))
        total = total + lax.ppermute(part, ("dp", "fsdp"), pairs).astype(f32)
    halves = total.astype(bf16).reshape(2, rows // 2, width)
    given = flip(lax.dynamic_index_in_dim(halves, 1 - core, 0, keepdims=False), CORE)
    kept = lax.dynamic_index_in_dim(halves, core, 0, keepdims=False)
    mine = jnp.where(owner, kept, given).reshape(4, rows // 8, width)
    order = by_turn(core, chip)
    picked = [lax.dynamic_index_in_dim(mine, m, 0, keepdims=False) for m in order]
    own = over_groups(plane_reduce(jnp.stack(picked[:2]), picked[2:])).astype(bf16)
    full = jnp.zeros((2, 4, rows // 8, width), bf16)
    for c, parts in ((core, spread(own)[0]),):
        for who, part in enumerate(parts):
            full = lax.dynamic_update_slice(full, part[None, None], (c, chip ^ who, 0, 0))
    mine = lax.dynamic_index_in_dim(full, core, 0, keepdims=True)
    full = lax.dynamic_update_slice(full, flip(mine, CORE), (1 - core, 0, 0, 0))
    return full.reshape(rows, width).astype(f32)


def reduce_gains(total):
    z = lax.axis_index("fsdp")
    depth = lax.axis_size("fsdp")
    bit = 1
    while bit < lax.axis_size("dp"):
        total = total + flip(total, bit)
        bit *= 2
    rows = total.shape[1] // depth
    total = total + sum(turn_z(total, s) for s in range(1, depth))
    mine = lax.dynamic_slice_in_dim(total, z * rows, rows, 1)
    return mine[0], mine[1]


def body(tokens, segment_ids, attn_gain, query_weight, key_weight, value_weight, out_weight, ffn_gain, gate_weight, up_weight, down_weight, cotangent):
    core, chip, z = place()
    sc = jnp.stack([core, chip]).astype(jnp.int32)
    _, stretch, width = tokens.shape
    tokens = home_to_work(tokens[0])
    gains = ring_gather(jnp.stack([attn_gain, ffn_gain]))
    gains = jnp.moveaxis(gains, 0, 1).reshape(2, 1, width).astype(f32)
    gain_a, gain_f = gains[0], gains[1]
    row = ring_gather(segment_ids[0]).reshape(-1)
    row = jnp.where((z >> 1) == core, row, flip(row, CORE))
    block = 2 * (z & 1) + core
    padded = jnp.concatenate([jnp.full((2 * stretch,), -1, row.dtype), row])
    seg_k = lax.dynamic_slice(padded, (block * stretch,), (3 * stretch,))
    seg_q = seg_k[2 * stretch :]
    ahead = jnp.arange(3 * stretch)[:, None] < 2 * stretch + jnp.arange(stretch)[None, :]
    seg_k, seg_q = seg_k[:, None], seg_q[None, :]
    positions = jnp.sum(((seg_k == seg_q) & ahead).astype(f32), axis=0)
    freq = rope_base ** (-2.0 * jnp.arange(HEAD_DIM // 2, dtype=f32) / HEAD_DIM)
    angle = freq[:, None] * positions[None, :]
    cos, sin = jnp.cos(angle), jnp.sin(angle)
    weights = gather_weights(query_weight, key_weight, value_weight, out_weight, gate_weight, up_weight, down_weight)
    wa, wb, wd = weights
    cot = home_to_work(cotangent[0])

    a0, q0, own = pre(sc, tokens, gain_a, cos, sin, *wa)
    kv0 = window(own)
    o0, lse0 = attend(q0, kv0, seg_k, seg_q)
    mixed0, h1_0, b0, gate0, up0, z0, h_1, a1, q1, own = post(False, sc, o0, tokens, gain_f, gain_a, cos, sin, *weights)
    kv1 = window(own)
    o1, lse1 = attend(q1, kv1, seg_k, seg_q)
    mixed1, h1_1, b1, gate1, up1, z1, output = post(True, sc, o1, h_1, gain_f, gain_a, cos, sin, *weights)
    output = home_to_work(output, back=True)

    gb1, act1, away1, zk1, zs1, g1, p1, dgain_f1, do = back(True, False, sc, weights, [cot], [gate1, up1, h1_1, gain_f, z1])
    dq1, far, near, own = attend_back(q1, kv1, seg_k, seg_q, lse1, do, cos, sin)
    near, far = unwindow(far, near)
    tail = [g1, dq1, own, near, far, h_1, gain_a, cos, sin]
    dk1, dv1, dgain_a1, gb0, act0, away0, zk0, zs0, g1, p0, dgain_f0, do = back(False, False, sc, weights, tail, [gate0, up0, h1_0, gain_f, z0])

    def pair(*own):
        return [*own, *(flip(v, CORE) for v in own)]

    lefts, mid = pair(b1, b0), [act1, act0, flip(away1, CORE), flip(away0, CORE)]
    send_b, keep_b = grad_ffn(sc, lefts, mid)
    down_parts = grad_down([zk1, zk0, flip(zs1, CORE), flip(zs0, CORE)], pair(gb1, gb0))
    grad_gate, grad_up = reduce_pieces(sc, send_b, keep_b, (4, 4))
    grad_down_ = reduce_down(down_parts)

    dq0, far, near, own = attend_back(q0, kv0, seg_k, seg_q, lse0, do, cos, sin)
    near, far = unwindow(far, near)
    tail = [g1, dq0, own, near, far, tokens, gain_a, cos, sin]
    dk0, dv0, dgain_a0, grad_tokens = back(False, True, sc, weights, tail, None)
    grad_tokens = home_to_work(grad_tokens, back=True).astype(f32)

    kept, sent = [], []
    for dq, dk, dv, p in ((dq1, dk1, dv1, p1), (dq0, dk0, dv0, p0)):
        first, second = jnp.concatenate([dq, dk[None]]), jnp.concatenate([dv[None], p])
        kept.append(jnp.where(core == 0, first, second))
        sent.append(flip(jnp.where(core == 0, second, first), CORE))
    send_a, keep_a = grad_attention(sc, pair(a1, a0), pair(mixed1, mixed0), kept + sent)
    grad_query, grad_key, grad_value, grad_out = reduce_pieces(sc, send_a, keep_a, (3, 1, 1, 3))
    dgain_a, dgain_f = reduce_gains(jnp.concatenate([dgain_a1 + dgain_a0, dgain_f1 + dgain_f0]))
    return (output[None], grad_tokens[None], dgain_a, grad_query, grad_key, grad_value, grad_out, dgain_f, grad_gate, grad_up, grad_down_)


def solution(mesh):
    wide, rows, shard = P("dp", "fsdp", None), P("dp", "fsdp"), P("fsdp", None)
    in_specs = (wide, rows, P("fsdp"), shard, shard, shard, shard, P("fsdp"), shard, shard, shard, wide)
    out_specs = (wide, wide, P("fsdp"), shard, shard, shard, shard, P("fsdp"), shard, shard, shard)
    return jax.shard_map(body, mesh=mesh, in_specs=in_specs, out_specs=out_specs, check_vma=False)
```

time: 810 us -> 595 us (0.73)
  matrix products: 183 us -> 0 us
  Pallas kernels: 0 us -> 166 us
  other arithmetic: 105 us -> 30.6 us
  starting transfers between devices: 177 us -> 107 us
  local copies, waits for them, and re-layouts: 178 us -> 119 us
    dot_general x85 -> x0, matrix products: 183 us -> none  [the longest x32 52.1 us: dot(): return jnp.dot(a, b, preferred_element_type=f32)]
    pallas_call x0 -> x15, Pallas kernels: none -> 166 us  [the longest x3 49.7 us: back(): pl.pallas_call(functools.partial(back_kernel, start, end), out_shape=tupl...]
    dynamic_update_slice x43 -> x4, local copies, waits for them, and re-layouts: 102 us -> 2.93 us  [the longest x1 1.97 us: reduce_down(): full = lax.dynamic_update_slice(full, flip(mine, CORE), (1 - core, 0, 0, 0))]
    ppermute x90 -> x69, starting transfers between devices: 98 us -> 64 us  [the longest x62 45.7 us: flip(): lax.ppermute(value, 'dp', [(i, i ^ bits[i & 1]) for i in range(count)])]
    unnamed x410 -> x217, local copies, waits for them, and re-layouts: 22.9 us -> 53.4 us
    ppermute x24, starting transfers between devices: 65.2 us -> 37.4 us  [turn_z(): lax.ppermute(value, 'fsdp', [(i, (i + step) % count) for i in range(count)])]
    ppermute x0 -> x13, local copies, waits for them, and re-layouts: none -> 25.8 us  [the longest x10 18.3 us: flip(): lax.ppermute(value, 'dp', [(i, i ^ bits[i & 1]) for i in range(count)])]
    select_n x8 -> x6, other arithmetic: 31.2 us -> 5.51 us  [the longest x2 2.52 us: plane_gather(): opposite = flip(jnp.where(core == 0, x, y), BACK, SIDE)]
  transfers between devices with their start and end apart: 118 -> 97, of which waited for: 32 -> 28; matrix products, arithmetic and copies ran while one was open for 56% -> 19% of each run, Pallas kernels for 0% -> 19%
where the time goes in v2:
time: 595 us; the launch traced here: 585 us
  Pallas kernels  166 us (28%)
  waiting for transfers between devices  159 us (27%)
  local copies, waits for them, and re-layouts  119 us (20%)
  starting transfers between devices  107 us (18%)
  other arithmetic  30.6 us (5%)
    ppermute x24, waiting for transfers between devices, turn_z(): lax.ppermute(value, 'fsdp', [(i, (i + step) % count) for i in range(count)])  80 us
    unnamed x217, local copies, waits for them, and re-layouts  53.4 us
    pallas_call x3, Pallas kernels, back(): pl.pallas_call(functools.partial(back_kernel, start, end), out_shape=tupl...  49.7 us
    ppermute x62, starting transfers between devices, flip(): lax.ppermute(value, 'dp', [(i, i ^ bits[i & 1]) for i in range(count)])  45.7 us
    ppermute x62, waiting for transfers between devices, flip(): lax.ppermute(value, 'dp', [(i, i ^ bits[i & 1]) for i in range(count)])  41.7 us
    pallas_call x2, Pallas kernels, post(): pl.pallas_call(functools.partial(post_kernel, last), out_shape=tuple(outs...  37.8 us
    ppermute x24, starting transfers between devices, turn_z(): lax.ppermute(value, 'fsdp', [(i, (i + step) % count) for i in range(count)])  37.4 us
    pallas_call x2, Pallas kernels, attend_back(): pl.pallas_call(attend_back_kernel, out_shape=(shape((3, n, KVW), bf16), s...  24.5 us
  transfers between devices with their start and end apart: 97, of which 28 were waited for; matrix products, arithmetic and copies ran while one was open for 19% of the time, Pallas kernels for 19%

profile of v2, /device:TPU:0, one launch (start us, length us, event | category | flops | bytes accessed | tf_op | source)
XLA Modules:
  0.0 584.5 jit_solution(8047891237775216645)
XLA Ops:
  2.1 3.1 collective-permute-start.1
  5.2 2.6 collective-permute-start.2
  22.0 2.9 collective-permute-start.6
  27.8 2.9 collective-permute-start.10
  31.9 2.4 collective-permute-done.8
  36.4 14.1 %collective-permute-done.9 = bf16[240,320]{1,0:T(8,128)(2,1)S(1)} collective-permute-done((bf16[240,320]{1,0:T(8,128)(2,1)S(1)}, bf16[240,320]{1,0:T(8,128)(2,1)S(1)}, u32[]{:S(2)}, u32[]{:S(2)}) %collective-permute-start.9) | collective-permute-done | bytes 153632 | tf_op jit(solution)/shard_map/ppermute | solution.py:593
  55.1 22.6 %collective-permute-done.21 = bf16[240,640]{1,0:T(8,128)(2,1)} collective-permute-done((bf16[240,640]{1,0:T(8,128)(2,1)S(1)}, bf16[240,640]{1,0:T(8,128)(2,1)}, u32[]{:S(2)}, u32[]{:S(2)}) %collective-permute-start.21) | collective-permute-done | bytes 307232 | tf_op jit(solution)/shard_map/ppermute | solution.py:593
  84.6 3.2 collective-permute-start.31
  87.8 7.8 %collective-permute-done.12 = bf16[960,320]{0,1:T(8,128)(2,1)} collective-permute-done((bf16[960,320]{0,1:T(8,128)(2,1)}, bf16[960,320]{0,1:T(8,128)(2,1)}, u32[]{:S(2)}, u32[]{:S(2)}) %collective-permute-start.12) | collective-permute-done | bytes 614432 | tf_op jit(solution)/shard_map/ppermute | solution.py:588
  98.3 19.2 %collective-permute-done.31 = bf16[320,960]{1,0:T(8,128)(2,1)S(1)} collective-permute-done((bf16[320,960]{1,0:T(8,128)(2,1)S(1)}, bf16[320,960]{1,0:T(8,128)(2,1)S(1)}, u32[]{:S(2)}, u32[]{:S(2)}) %collective-permute-start.31) | collective-permute-done | bytes 614432 | tf_op jit(solution)/shard_map/ppermute | solution.py:593
  120.2 6.4 %collective-permute-done.13 = bf16[960,320]{0,1:T(8,128)(2,1)} collective-permute-done((bf16[960,320]{0,1:T(8,128)(2,1)S(1)}, bf16[960,320]{0,1:T(8,128)(2,1)}, u32[]{:S(2)}, u32[]{:S(2)}) %collective-permute-start.13) | collective-permute-done | bytes 614432 | tf_op jit(solution)/shard_map/ppermute | solution.py:588
  128.4 4.8 collective-permute-start.16
  133.3 2.5 broadcast_select_fusion
  141.0 2.5 copy.221.rest_3_
  148.0 2.3 copy.225.rest_7_
  155.0 6.8 %pre.1 = (bf16[256,960]{1,0:T(8,128)(2,1)}, bf16[960,256]{1,0:T(8,128)(2,1)S(1)}, bf16[640,256]{1,0:T(8,128)(2,1)S(1)}) custom-call(s32[2]{0:T(128)S(1)} %pad_add_fusion.sc, bf16[256,960]{1,0:T(8,128)(2,1)S(1)} %collective-permute-done.h_ref.rest_13_, f32[1,960]{1,0:T(1,128)S(1)} %squeeze.83.gain_ref.gain_a.rest_24_.rest_14_, ...), custom_call_target="tpu_custom_call" | custom-call | tf_op jit(solution)/shard_map/pre/pallas_call | solution.py:105
  161.8 3.7 collective-permute-start.18
  165.4 7.2 %collective-permute-done.18.kv0 = bf16[640,256]{1,0:T(8,128)(2,1)S(1)} collective-permute-done((bf16[640,256]{1,0:T(8,128)(2,1)S(1)}, bf16[640,256]{1,0:T(8,128)(2,1)S(1)}, u32[]{:S(2)}, u32[]{:S(2)}) %collective-permute-start.18) | collective-permute-done | bytes 327712 | tf_op jit(solution)/shard_map/ppermute | solution.py:649
  179.5 10.0 %attend.2 = (bf16[960,256]{1,0:T(8,128)(2,1)S(1)}, f32[15,256]{1,0:T(8,128)S(1)}) custom-call(bf16[960,256]{1,0:T(8,128)(2,1)S(1)} %copy-done.38, bf16[640,256]{1,0:T(8,128)(2,1)S(1)} %collective-permute-done.18.kv0, bf16[640,256]{1,0:T(8,128)(2,1)S(1)} %collective-permute-done.19.kv1, bf16[640,256]{1,0:T(8,128)(2,1)S(1)} %copy-done.24, ...), custom_call_target="tpu_custom_call" | custom-call | tf_op jit(solution)/shard_map/attend/pallas_call | solution.py:154
  190.4 20.2 %post.2 = (bf16[256,960]{1,0:T(8,128)(2,1)}, f32[256,960]{1,0:T(8,128)}, bf16[256,960]{1,0:T(8,128)(2,1)}, bf16[256,2560]{1,0:T(8,128)(2,1)}, bf16[256,2560]{1,0...) custom-call(s32[2]{0:T(128)} %copy-done.72, ...), custom_call_target="tpu_custom_call" | custom-call | tf_op jit(solution)/shard_map/post/pallas_call | solution.py:287
  210.7 4.5 collective-permute-start.34
  217.9 3.7 collective-permute-done.34.kv0
  224.3 10.4 %attend.3 = (bf16[960,256]{1,0:T(8,128)(2,1)S(1)}, f32[15,256]{1,0:T(8,128)S(1)}) custom-call(bf16[960,256]{1,0:T(8,128)(2,1)S(1)} %copy-done.40, bf16[640,256]{1,0:T(8,128)(2,1)S(1)} %collective-permute-done.34.kv0, bf16[640,256]{1,0:T(8,128)(2,1)S(1)} %collective-permute-done.35.kv1, bf16[640,256]{1,0:T(8,128)(2,1)S(1)} %copy-done.26, ...), custom_call_target="tpu_custom_call" | custom-call | tf_op jit(solution)/shard_map/attend/pallas_call | solution.py:154
  235.6 17.6 %post.3 = (bf16[256,960]{1,0:T(8,128)(2,1)}, f32[256,960]{1,0:T(8,128)}, bf16[256,960]{1,0:T(8,128)(2,1)}, bf16[256,2560]{1,0:T(8,128)(2,1)}, bf16[256,2560]{1,0...) custom-call(s32[2]{0:T(128)} %copy-done.72, bf16[960,256]{1,0:T(8,128)(2,1)} %copy-done.67, ...), custom_call_target="tpu_custom_call" | custom-call | tf_op jit(solution)/shard_map/post/pallas_call | solution.py:287
  254.0 21.5 %back_start.1 = (bf16[256,960]{1,0:T(8,128)(2,1)}, bf16[256,2560]{1,0:T(8,128)(2,1)}, bf16[256,2560]{1,0:T(8,128)(2,1)}, bf16[256,1280]{1,0:T(8,128)(2,1)}, bf16...) custom-call(s32[2]{0:T(128)} %copy-done.72, ...), custom_call_target="tpu_custom_call" | custom-call | tf_op jit(solution)/shard_map/back_start/pallas_call | solution.py:438
  276.5 12.4 %attend_back.2 = (bf16[3,256,320]{2,1,0:T(8,128)(2,1)S(1)}, f32[640,256]{1,0:T(8,128)S(1)}, bf16[640,256]{1,0:T(8,128)(2,1)}, f32[640,256]{1,0:T(8,128)S(1)}) custom-call(bf16[960,256]{1,0:T(8,128)(2,1)S(1)} %copy-done.40, bf16[640,256]{1,0:T(8,128)(2,1)S(1)} %collective-permute-done.34.kv0, bf16[640,256]{1,0:T(8,128)(2,1)S(1)} %collective-permute-done.35.kv1, ...), custom_call_target="tpu_custom_call" | custom-call | tf_op jit(solution)/shard_map/attend_back/pallas_call | solution.py:203
  294.4 9.8 %collective-permute-done.39.rest_22_ = bf16[640,256]{1,0:T(8,128)(2,1)S(1)} collective-permute-done((bf16[640,256]{1,0:T(8,128)(2,1)S(1)}, bf16[640,256]{1,0:T(8,128)(2,1)S(1)}, u32[]{:S(2)}, u32[]{:S(2)}) %collective-permute-start.39) | collective-permute-done | bytes 327712 | tf_op jit(solution)/shard_map/ppermute | solution.py:659
  304.9 22.1 %back_join.1 = (bf16[256,320]{1,0:T(8,128)(2,1)}, bf16[256,320]{1,0:T(8,128)(2,1)}, f32[1,960]{1,0:T(1,128)}, bf16[256,960]{1,0:T(8,128)(2,1)}, bf16[256,2560]{1...) custom-call(s32[2]{0:T(128)} %copy-done.72, ...), custom_call_target="tpu_custom_call" | custom-call | tf_op jit(solution)/shard_map/back_join/pallas_call | solution.py:438
  328.2 12.1 %attend_back.3 = (bf16[3,256,320]{2,1,0:T(8,128)(2,1)S(1)}, f32[640,256]{1,0:T(8,128)S(1)}, bf16[640,256]{1,0:T(8,128)(2,1)S(1)}, f32[640,256]{1,0:T(8,128)S(1)}) custom-call(bf16[960,256]{1,0:T(8,128)(2,1)S(1)} %copy-done.39, bf16[640,256]{1,0:T(8,128)(2,1)S(1)} %collective-permute-done.18.kv0, bf16[640,256]{1,0:T(8,128)(2,1)S(1)} %collective-permute-done.19.kv1, ...), custom_call_target="tpu_custom_call" | custom-call | tf_op jit(solution)/shard_map/attend_back/pallas_call | solution.py:203
  348.0 2.3 copy.267
  351.0 6.1 %collective-permute-done.41.rest_12_ = bf16[640,256]{1,0:T(8,128)(2,1)} collective-permute-done((bf16[640,256]{1,0:T(8,128)(2,1)}, bf16[640,256]{1,0:T(8,128)(2,1)}, u32[]{:S(2)}, u32[]{:S(2)}) %collective-permute-start.41) | collective-permute-done | bytes 327712 | tf_op jit(solution)/shard_map/ppermute | solution.py:659
  358.1 4.3 grad_down.1
  367.2 2.6 copy.276
  378.7 6.1 %back_end.1 = (bf16[256,320]{1,0:T(8,128)(2,1)S(1)}, bf16[256,320]{1,0:T(8,128)(2,1)S(1)}, f32[1,960]{1,0:T(1,128)S(1)}, bf16[256,960]{1,0:T(8,128)(2,1)S(1)}) custom-call(s32[2]{0:T(128)S(1)} %copy-done.73, bf16[960,320]{1,0:T(8,128)(2,1)S(1)} %bitcast.128, bf16[960,320]{1,0:T(8,128)(2,1)S(1)} %copy-done.5, bf16[960,320]{1,0:T(8,128)(2,1)S(1)} %copy-done.7, ...), custom_call_target="tpu_custom_call" | custom-call | tf_op jit(solution)/shard_map/back_end/pallas_call | solution.py:438
  387.4 5.0 collective-permute-start.87
  393.9 4.4 collective-permute-start.54
  405.5 9.9 %grad_ffn.1 = (bf16[2,960,640]{2,1,0:T(8,128)(2,1)}, bf16[2,960,640]{2,1,0:T(8,128)(2,1)}) custom-call(s32[2]{0:T(128)S(1)} %copy-done.73, bf16[256,960]{1,0:T(8,128)(2,1)S(1)} %copy-done.59, bf16[256,960]{1,0:T(8,128)(2,1)S(1)} %copy-done.58, bf16[256,960]{1,0:T(8,128)(2,1)} %collective-permute-done.67.rest_2_, ...), custom_call_target="tpu_custom_call" | custom-call | tf_op jit(solution)/shard_map/grad_ffn/pallas_call | solution.py:478
  419.7 6.9 %grad_attention.1 = (bf16[2,960,320]{2,1,0:T(8,128)(2,1)S(1)}, bf16[2,960,320]{2,1,0:T(8,128)(2,1)S(1)}) custom-call(s32[2]{0:T(128)S(1)} %copy-done.73, bf16[256,960]{1,0:T(8,128)(2,1)} %get-tuple-element.113.rest_0_, bf16[256,960]{1,0:T(8,128)(2,1)} %get-tuple-element.114.rest_1_, bf16[256,960]{1,0:T(8,128)(2,1)S(1)} %copy-done.63, ...), custom_call_target="tpu_custom_call" | custom-call | tf_op jit(solution)/shard_map/grad_attention/pallas_call | solution.py:537
  428.9 2.5 copy.271
  432.8 2.4 copy.281
  435.3 10.7 %collective-permute-done.88 = bf16[640,960]{0,1:T(8,128)(2,1)} collective-permute-done((bf16[640,960]{0,1:T(8,128)(2,1)}, bf16[640,960]{0,1:T(8,128)(2,1)}, u32[]{:S(2)}, u32[]{:S(2)}) %collective-permute-start.88) | collective-permute-done | bytes 1228832 | tf_op jit(solution)/shard_map/ppermute | solution.py:715
  445.9 2.6 copy.279
  448.5 2.5 copy.277
  451.0 3.3 fusion.2
  458.6 3.0 collective-permute-done.44
  465.4 4.0 collective-permute-start.48
  469.4 3.4 collective-permute-start.47
  477.1 2.4 fusion.21
  481.1 2.6 collective-permute-done.91
  493.8 2.7 collective-permute-start.95
  496.5 3.0 fusion.3
  501.2 4.2 collective-permute-done.94
  505.4 2.2 copy.275
  509.4 4.0 collective-permute-start.59
  516.4 10.1 %collective-permute-done.58 = bf16[240,320]{1,0:T(8,128)(2,1)S(1)} collective-permute-done((bf16[240,320]{1,0:T(8,128)(2,1)S(1)}, bf16[240,320]{1,0:T(8,128)(2,1)S(1)}, u32[]{:S(2)}, u32[]{:S(2)}) %collective-permute-start.58) | collective-permute-done | bytes 153632 | tf_op jit(solution)/shard_map/ppermute | solution.py:593
  533.2 4.5 collective-permute-start.61
  538.3 4.7 collective-permute-done.61.rest_2_
  543.0 3.2 collective-permute-start.62
  546.2 9.3 %collective-permute-done.74 = bf16[240,640]{1,0:T(8,128)(2,1)S(1)} collective-permute-done((bf16[240,640]{1,0:T(8,128)(2,1)S(1)}, bf16[240,640]{1,0:T(8,128)(2,1)S(1)}, u32[]{:S(2)}, u32[]{:S(2)}) %collective-permute-start.74) | collective-permute-done | bytes 307232 | tf_op jit(solution)/shard_map/ppermute | solution.py:593
  562.0 2.5 copy.283
  566.1 2.4 lay.2
  574.3 3.1 bitcast_convert_fusion
  577.4 3.3 copy.286
  580.7 3.6 lay.3
  (474 shorter events, 171.1 us)
Async XLA Ops:
  2.1 19.9 %collective-permute-start.1 = (bf16[2,240]{1,0:T(2,128)(2,1)S(1)}, bf16[2,240]{1,0:T(2,128)(2,1)S(1)}, u32[]{:S(2)}, u32[]{:S(2)}) collective-permute-start(bf16[2,240]{1,0:T(2,128)(2,1)S(1)} %pad_maximum_fusion.6), channel_id=1, source_target_pairs={{0,1},{1,2},{2,3},{3,0},{4,5},{5,6},{6,7},{7,4},{8,9},{9,10},{10,1... | collective-permute-start | bytes 2888 | tf_op jit(solution)/shard_map/ppermute | solution.py:593
  5.2 19.8 %collective-permute-start.2 = (bf16[2,240]{1,0:T(2,128)(2,1)S(1)}, bf16[2,240]{1,0:T(2,128)(2,1)S(1)}, u32[]{:S(2)}, u32[]{:S(2)}) collective-permute-start(bf16[2,240]{1,0:T(2,128)(2,1)S(1)} %pad_maximum_fusion.6), channel_id=1, source_target_pairs={{0,2},{1,3},{2,0},{3,1},{4,6},{5,7},{6,4},{7,5},{8,10},{9,11},{10,... | collective-permute-start | bytes 2888 | tf_op jit(solution)/shard_map/ppermute | solution.py:593
  7.8 17.8 %collective-permute-start.3 = (bf16[2,240]{1,0:T(2,128)(2,1)S(1)}, bf16[2,240]{1,0:T(2,128)(2,1)S(1)}, u32[]{:S(2)}, u32[]{:S(2)}) collective-permute-start(bf16[2,240]{1,0:T(2,128)(2,1)S(1)} %pad_maximum_fusion.6), channel_id=1, source_target_pairs={{0,3},{1,0},{2,1},{3,2},{4,7},{5,4},{6,5},{7,6},{8,11},{9,8},{10,9... | collective-permute-start | bytes 2888 | tf_op jit(solution)/shard_map/ppermute | solution.py:593
  9.1 18.7 %collective-permute-start.4 = (s32[256]{0:T(256)}, s32[256]{0:T(256)S(1)}, u32[]{:S(2)}, u32[]{:S(2)}) collective-permute-start(s32[256]{0:T(256)} %bitcast.151), channel_id=1, source_target_pairs={{0,1},{1,2},{2,3},{3,0},{4,5},{5,6},{6,7},{7,4},{8,9},{9,10},{10,1... | collective-permute-start | bytes 3080 | tf_op jit(solution)/shard_map/ppermute | solution.py:593
  9.8 21.0 %collective-permute-start.5 = (s32[256]{0:T(256)}, s32[256]{0:T(256)S(1)}, u32[]{:S(2)}, u32[]{:S(2)}) collective-permute-start(s32[256]{0:T(256)} %bitcast.152), channel_id=1, source_target_pairs={{0,2},{1,3},{2,0},{3,1},{4,6},{5,7},{6,4},{7,5},{8,10},{9,11},{10,... | collective-permute-start | bytes 3080 | tf_op jit(solution)/shard_map/ppermute | solution.py:593
  25.5 25.0 %collective-permute-start.9 = (bf16[240,320]{1,0:T(8,128)(2,1)S(1)}, bf16[240,320]{1,0:T(8,128)(2,1)S(1)}, u32[]{:S(2)}, u32[]{:S(2)}) collective-permute-start(bf16[240,320]{1,0:T(8,128)(2,1)S(1)} %get-tuple-element.205), channel_id=1, source_target_pairs={{0,2},{1,3},{2,0},{3,1},{4,6},{5,7},{6,4},{7,5},{8,10},{9,11},{10,... | collective-permute-start | bytes 460808 | tf_op jit(solution)/shard_map/ppermute | solution.py:593
  27.8 22.8 %collective-permute-start.10 = (bf16[240,320]{1,0:T(8,128)(2,1)S(1)}, bf16[240,320]{1,0:T(8,128)(2,1)S(1)}, u32[]{:S(2)}, u32[]{:S(2)}) collective-permute-start(bf16[240,320]{1,0:T(8,128)(2,1)S(1)} %get-tuple-element.205), channel_id=1, source_target_pairs={{0,3},{1,0},{2,1},{3,2},{4,7},{5,4},{6,5},{7,6},{8,11},{9,8},{10,9... | collective-permute-start | bytes 460808 | tf_op jit(solution)/shard_map/ppermute | solution.py:593
  30.7 21.1 %collective-permute-start.20 = (bf16[240,640]{1,0:T(8,128)(2,1)S(1)}, bf16[240,640]{1,0:T(8,128)(2,1)}, u32[]{:S(2)}, u32[]{:S(2)}) collective-permute-start(bf16[240,640]{1,0:T(8,128)(2,1)S(1)} %get-tuple-element.203), channel_id=1, source_target_pairs={{0,1},{1,2},{2,3},{3,0},{4,5},{5,6},{6,7},{7,4},{8,9},{9,10},{10,1... | collective-permute-start | bytes 921608 | tf_op jit(solution)/shard_map/ppermute | solution.py:593
  30.9 46.8 %collective-permute-start.21 = (bf16[240,640]{1,0:T(8,128)(2,1)S(1)}, bf16[240,640]{1,0:T(8,128)(2,1)}, u32[]{:S(2)}, u32[]{:S(2)}) collective-permute-start(bf16[240,640]{1,0:T(8,128)(2,1)S(1)} %get-tuple-element.203), channel_id=1, source_target_pairs={{0,2},{1,3},{2,0},{3,1},{4,6},{5,7},{6,4},{7,5},{8,10},{9,11},{10,... | collective-permute-start | bytes 921608 | tf_op jit(solution)/shard_map/ppermute | solution.py:593
  34.4 46.5 %collective-permute-start.22 = (bf16[240,640]{1,0:T(8,128)(2,1)S(1)}, bf16[240,640]{1,0:T(8,128)(2,1)}, u32[]{:S(2)}, u32[]{:S(2)}) collective-permute-start(bf16[240,640]{1,0:T(8,128)(2,1)S(1)} %get-tuple-element.203), channel_id=1, source_target_pairs={{0,3},{1,0},{2,1},{3,2},{4,7},{5,4},{6,5},{7,6},{8,11},{9,8},{10,9... | collective-permute-start | bytes 921608 | tf_op jit(solution)/shard_map/ppermute | solution.py:593
  50.5 45.2 %collective-permute-start.30 = (bf16[320,960]{1,0:T(8,128)(2,1)S(1)}, bf16[320,960]{1,0:T(8,128)(2,1)S(1)}, u32[]{:S(2)}, u32[]{:S(2)}) collective-permute-start(bf16[320,960]{1,0:T(8,128)(2,1)S(1)} %copy.287), channel_id=1, source_target_pairs={{0,1},{1,2},{2,3},{3,0},{4,5},{5,6},{6,7},{7,4},{8,9},{9,10},{10,1... | collective-permute-start | bytes 1843208 | tf_op jit(solution)/shard_map/ppermute | solution.py:593
  50.6 33.5 %collective-permute-start.7 = (s32[1024]{0:T(1024)S(1)}, s32[1024]{0:T(1024)S(1)}, u32[]{:S(2)}, u32[]{:S(2)}) collective-permute-start(s32[1024]{0:T(1024)S(1)} %bitcast.148), channel_id=1, source_target_pairs={{0,4},{4,0},{8,12},{12,8},{16,20},{20,16},{24,28},{28,24},{1,5},{5... | collective-permute-start | bytes 12296 | tf_op jit(solution)/shard_map/ppermute | solution.py:588
  51.8 32.8 %collective-permute-start.11 = (bf16[960,320]{0,1:T(8,128)(2,1)}, bf16[960,320]{0,1:T(8,128)(2,1)S(1)}, u32[]{:S(2)}, u32[]{:S(2)}) collective-permute-start(bf16[960,320]{0,1:T(8,128)(2,1)} %copy.216), channel_id=1, source_target_pairs={{0,8},{4,12},{8,0},{12,4},{16,24},{20,28},{24,16},{28,20},{1,9},{5... | collective-permute-start | bytes 1843208 | tf_op jit(solution)/shard_map/ppermute | solution.py:588
  77.6 18.0 %collective-permute-start.12 = (bf16[960,320]{0,1:T(8,128)(2,1)}, bf16[960,320]{0,1:T(8,128)(2,1)}, u32[]{:S(2)}, u32[]{:S(2)}) collective-permute-start(bf16[960,320]{0,1:T(8,128)(2,1)} %copy.216), channel_id=1, source_target_pairs={{0,16},{4,20},{8,24},{12,28},{16,0},{20,4},{24,8},{28,12},{1,17},{... | collective-permute-start | bytes 1843208 | tf_op jit(solution)/shard_map/ppermute | solution.py:588
  82.6 45.9 %collective-permute-start.23 = (bf16[960,640]{1,0:T(8,128)(2,1)}, bf16[960,640]{1,0:T(8,128)(2,1)}, u32[]{:S(2)}, u32[]{:S(2)}) collective-permute-start(bf16[960,640]{1,0:T(8,128)(2,1)} %bitcast.22.rest_8_), channel_id=1, source_target_pairs={{0,8},{4,12},{8,0},{12,4},{16,24},{20,28},{24,16},{28,20},{1,9},{5... | collective-permute-start | bytes 3686408 | tf_op jit(solution)/shard_map/ppermute | solution.py:588
  84.1 49.2 %collective-permute-start.24 = (bf16[960,640]{1,0:T(8,128)(2,1)}, bf16[960,640]{1,0:T(8,128)(2,1)}, u32[]{:S(2)}, u32[]{:S(2)}) collective-permute-start(bf16[960,640]{1,0:T(8,128)(2,1)} %bitcast.22.rest_8_), channel_id=1, source_target_pairs={{0,16},{4,20},{8,24},{12,28},{16,0},{20,4},{24,8},{28,12},{1,17},{... | collective-permute-start | bytes 3686408 | tf_op jit(solution)/shard_map/ppermute | solution.py:588
  84.6 32.9 %collective-permute-start.31 = (bf16[320,960]{1,0:T(8,128)(2,1)S(1)}, bf16[320,960]{1,0:T(8,128)(2,1)S(1)}, u32[]{:S(2)}, u32[]{:S(2)}) collective-permute-start(bf16[320,960]{1,0:T(8,128)(2,1)S(1)} %copy.287), channel_id=1, source_target_pairs={{0,2},{1,3},{2,0},{3,1},{4,6},{5,7},{6,4},{7,5},{8,10},{9,11},{10,... | collective-permute-start | bytes 1843208 | tf_op jit(solution)/shard_map/ppermute | solution.py:593
  95.6 22.8 %collective-permute-start.32 = (bf16[320,960]{1,0:T(8,128)(2,1)S(1)}, bf16[320,960]{1,0:T(8,128)(2,1)S(1)}, u32[]{:S(2)}, u32[]{:S(2)}) collective-permute-start(bf16[320,960]{1,0:T(8,128)(2,1)S(1)} %copy.287), channel_id=1, source_target_pairs={{0,3},{1,0},{2,1},{3,2},{4,7},{5,4},{6,5},{7,6},{8,11},{9,8},{10,9... | collective-permute-start | bytes 1843208 | tf_op jit(solution)/shard_map/ppermute | solution.py:593
  95.8 30.8 %collective-permute-start.13 = (bf16[960,320]{0,1:T(8,128)(2,1)S(1)}, bf16[960,320]{0,1:T(8,128)(2,1)}, u32[]{:S(2)}, u32[]{:S(2)}) collective-permute-start(bf16[960,320]{0,1:T(8,128)(2,1)S(1)} %broadcast_select_fusion.5), channel_id=1, source_target_pairs={{0,16},{4,12},{8,24},{12,4},{16,0},{20,28},{24,8},{28,20},{1,17},{... | collective-permute-start | bytes 1843208 | tf_op jit(solution)/shard_map/ppermute | solution.py:588
  117.5 18.3 %collective-permute-start.14 = (bf16[960,320]{0,1:T(8,128)(2,1)}, bf16[960,320]{0,1:T(8,128)(2,1)S(1)}, u32[]{:S(2)}, u32[]{:S(2)}) collective-permute-start(bf16[960,320]{0,1:T(8,128)(2,1)} %copy.216), channel_id=1, source_target_pairs={{0,4},{4,0},{8,12},{12,8},{16,20},{20,16},{24,28},{28,24},{1,5},{5... | collective-permute-start | bytes 1843208 | tf_op jit(solution)/shard_map/ppermute | solution.py:588
  118.4 17.8 %collective-permute-start.15 = (bf16[960,320]{0,1:T(8,128)(2,1)S(1)}, bf16[960,320]{0,1:T(8,128)(2,1)S(1)}, u32[]{:S(2)}, u32[]{:S(2)}) collective-permute-start(bf16[960,320]{0,1:T(8,128)(2,1)S(1)} %collective-permute-done.11), channel_id=1, source_target_pairs={{0,4},{4,0},{8,12},{12,8},{16,20},{20,16},{24,28},{28,24},{1,5},{5... | collective-permute-start | bytes 1843208 | tf_op jit(solution)/shard_map/ppermute | solution.py:588
  126.6 23.7 %collective-permute-start = (bf16[256,960]{1,0:T(8,128)(2,1)}, bf16[256,960]{1,0:T(8,128)(2,1)S(1)}, u32[]{:S(2)}, u32[]{:S(2)}) collective-permute-start(bf16[256,960]{1,0:T(8,128)(2,1)} %bitcast.2), channel_id=1, source_target_pairs={{0,0},{1,4},{2,1},{3,5},{4,2},{5,6},{6,3},{7,7},{8,8},{9,12},{10,9... | collective-permute-start | bytes 1474568 | tf_op jit(solution)/shard_map/ppermute | solution.py:604
  128.4 17.4 %collective-permute-start.16 = (bf16[960,320]{0,1:T(8,128)(2,1)}, bf16[960,320]{0,1:T(8,128)(2,1)}, u32[]{:S(2)}, u32[]{:S(2)}) collective-permute-start(bf16[960,320]{0,1:T(8,128)(2,1)} %collective-permute-done.12), channel_id=1, source_target_pairs={{0,4},{4,0},{8,12},{12,8},{16,20},{20,16},{24,28},{28,24},{1,5},{5... | collective-permute-start | bytes 1843208 | tf_op jit(solution)/shard_map/ppermute | solution.py:588
  133.3 14.8 %collective-permute-start.17 = (bf16[960,320]{0,1:T(8,128)(2,1)}, bf16[960,320]{0,1:T(8,128)(2,1)}, u32[]{:S(2)}, u32[]{:S(2)}) collective-permute-start(bf16[960,320]{0,1:T(8,128)(2,1)} %collective-permute-done.13), channel_id=1, source_target_pairs={{0,4},{4,0},{8,12},{12,8},{16,20},{20,16},{24,28},{28,24},{1,5},{5... | collective-permute-start | bytes 1843208 | tf_op jit(solution)/shard_map/ppermute | solution.py:588
  135.8 54.6 %collective-permute-start.33 = (bf16[4,320,960]{2,1,0:T(8,128)(2,1)}, bf16[4,320,960]{2,1,0:T(8,128)(2,1)}, u32[]{:S(2)}, u32[]{:S(2)}) collective-permute-start(bf16[4,320,960]{2,1,0:T(8,128)(2,1)} %bitcast_dynamic-update-slice_fusion.rest_16_), channel_id=1, source_target_pairs={{0,4},{4,0},{8,12},{12,8},{16,20},{20,16},{24,28},{28,24},{1,5},{5... | collective-permute-start | bytes 7372808 | tf_op jit(solution)/shard_map/ppermute | solution.py:588
  136.2 39.4 %collective-permute-start.25 = (bf16[960,640]{1,0:T(8,128)(2,1)}, bf16[960,640]{1,0:T(8,128)(2,1)}, u32[]{:S(2)}, u32[]{:S(2)}) collective-permute-start(bf16[960,640]{1,0:T(8,128)(2,1)} %broadcast_select_fusion), channel_id=1, source_target_pairs={{0,16},{4,12},{8,24},{12,4},{16,0},{20,28},{24,8},{28,20},{1,17},{... | collective-permute-start | bytes 3686408 | tf_op jit(solution)/shard_map/ppermute | solution.py:588
  173.4 16.9 %collective-permute-start.26 = (bf16[960,640]{1,0:T(8,128)(2,1)}, bf16[960,640]{1,0:T(8,128)(2,1)}, u32[]{:S(2)}, u32[]{:S(2)}) collective-permute-start(bf16[960,640]{1,0:T(8,128)(2,1)} %bitcast.22.rest_8_), channel_id=1, source_target_pairs={{0,4},{4,0},{8,12},{12,8},{16,20},{20,16},{24,28},{28,24},{1,5},{5... | collective-permute-start | bytes 3686408 | tf_op jit(solution)/shard_map/ppermute | solution.py:588
  173.9 16.4 %collective-permute-start.27 = (bf16[960,640]{1,0:T(8,128)(2,1)}, bf16[960,640]{1,0:T(8,128)(2,1)}, u32[]{:S(2)}, u32[]{:S(2)}) collective-permute-start(bf16[960,640]{1,0:T(8,128)(2,1)} %collective-permute-done.23.rest_9_), channel_id=1, source_target_pairs={{0,4},{4,0},{8,12},{12,8},{16,20},{20,16},{24,28},{28,24},{1,5},{5... | collective-permute-start | bytes 3686408 | tf_op jit(solution)/shard_map/ppermute | solution.py:588
  175.5 14.9 %collective-permute-start.28 = (bf16[960,640]{1,0:T(8,128)(2,1)}, bf16[960,640]{1,0:T(8,128)(2,1)}, u32[]{:S(2)}, u32[]{:S(2)}) collective-permute-start(bf16[960,640]{1,0:T(8,128)(2,1)} %collective-permute-done.24.rest_10_), channel_id=1, source_target_pairs={{0,4},{4,0},{8,12},{12,8},{16,20},{20,16},{24,28},{28,24},{1,5},{5... | collective-permute-start | bytes 3686408 | tf_op jit(solution)/shard_map/ppermute | solution.py:588
  175.6 14.7 %collective-permute-start.29 = (bf16[960,640]{1,0:T(8,128)(2,1)}, bf16[960,640]{1,0:T(8,128)(2,1)}, u32[]{:S(2)}, u32[]{:S(2)}) collective-permute-start(bf16[960,640]{1,0:T(8,128)(2,1)} %collective-permute-done.25.rest_11_), channel_id=1, source_target_pairs={{0,4},{4,0},{8,12},{12,8},{16,20},{20,16},{24,28},{28,24},{1,5},{5... | collective-permute-start | bytes 3686408 | tf_op jit(solution)/shard_map/ppermute | solution.py:588
  210.7 11.0 %collective-permute-start.34 = (bf16[640,256]{1,0:T(8,128)(2,1)}, bf16[640,256]{1,0:T(8,128)(2,1)S(1)}, u32[]{:S(2)}, u32[]{:S(2)}) collective-permute-start(bf16[640,256]{1,0:T(8,128)(2,1)} %get-tuple-element.82.kv2), channel_id=1, source_target_pairs={{0,1},{2,3},{4,5},{6,7},{8,9},{10,11},{12,13},{14,15},{16,17},{18,... | collective-permute-start | bytes 983048 | tf_op jit(solution)/shard_map/ppermute | solution.py:649
  216.2 36.9 %collective-permute-start.37 = (bf16[256,960]{1,0:T(8,128)(2,1)}, bf16[256,960]{1,0:T(8,128)(2,1)S(1)}, u32[]{:S(2)}, u32[]{:S(2)}) collective-permute-start(bf16[256,960]{1,0:T(8,128)(2,1)} %bitcast.145), channel_id=1, source_target_pairs={{0,0},{1,4},{2,1},{3,5},{4,2},{5,6},{6,3},{7,7},{8,8},{9,12},{10,9... | collective-permute-start | bytes 1474568 | tf_op jit(solution)/shard_map/ppermute | solution.py:604
  292.5 11.7 %collective-permute-start.39 = (bf16[640,256]{1,0:T(8,128)(2,1)S(1)}, bf16[640,256]{1,0:T(8,128)(2,1)S(1)}, u32[]{:S(2)}, u32[]{:S(2)}) collective-permute-start(bf16[640,256]{1,0:T(8,128)(2,1)S(1)} %fusion.6), channel_id=1, source_target_pairs={{1,0},{3,2},{5,4},{7,6},{9,8},{11,10},{13,12},{15,14},{17,16},{19,... | collective-permute-start | bytes 983048 | tf_op jit(solution)/shard_map/ppermute | solution.py:659
  293.8 47.2 %collective-permute-start.50 = (bf16[256,960]{1,0:T(8,128)(2,1)}, bf16[256,960]{1,0:T(8,128)(2,1)S(1)}, u32[]{:S(2)}, u32[]{:S(2)}) collective-permute-start(bf16[256,960]{1,0:T(8,128)(2,1)} %get-tuple-element.114.rest_1_), channel_id=1, source_target_pairs={{0,4},{4,0},{8,12},{12,8},{16,20},{20,16},{24,28},{28,24},{1,5},{5... | collective-permute-start | bytes 1474568 | tf_op jit(solution)/shard_map/ppermute | solution.py:588
  294.0 48.2 %collective-permute-start.49 = (bf16[256,960]{1,0:T(8,128)(2,1)}, bf16[256,960]{1,0:T(8,128)(2,1)S(1)}, u32[]{:S(2)}, u32[]{:S(2)}) collective-permute-start(bf16[256,960]{1,0:T(8,128)(2,1)} %get-tuple-element.113.rest_0_), channel_id=1, source_target_pairs={{0,4},{4,0},{8,12},{12,8},{16,20},{20,16},{24,28},{28,24},{1,5},{5... | collective-permute-start | bytes 1474568 | tf_op jit(solution)/shard_map/ppermute | solution.py:588
  340.9 46.5 %collective-permute-start.69 = (bf16[256,2560]{1,0:T(8,128)(2,1)}, bf16[256,2560]{1,0:T(8,128)(2,1)}, u32[]{:S(2)}, u32[]{:S(2)}) collective-permute-start(bf16[256,2560]{1,0:T(8,128)(2,1)} %get-tuple-element.133), channel_id=1, source_target_pairs={{0,4},{4,0},{8,12},{12,8},{16,20},{20,16},{24,28},{28,24},{1,5},{5... | collective-permute-start | bytes 3932168 | tf_op jit(solution)/shard_map/ppermute | solution.py:588
  345.1 11.9 %collective-permute-start.41 = (bf16[640,256]{1,0:T(8,128)(2,1)}, bf16[640,256]{1,0:T(8,128)(2,1)}, u32[]{:S(2)}, u32[]{:S(2)}) collective-permute-start(bf16[640,256]{1,0:T(8,128)(2,1)} %fusion.7), channel_id=1, source_target_pairs={{1,0},{3,2},{5,4},{7,6},{9,8},{11,10},{13,12},{15,14},{17,16},{19,... | collective-permute-start | bytes 983048 | tf_op jit(solution)/shard_map/ppermute | solution.py:659
  350.3 47.9 %collective-permute-start.70 = (bf16[256,2560]{1,0:T(8,128)(2,1)}, bf16[256,2560]{1,0:T(8,128)(2,1)}, u32[]{:S(2)}, u32[]{:S(2)}) collective-permute-start(bf16[256,2560]{1,0:T(8,128)(2,1)} %get-tuple-element.134), channel_id=1, source_target_pairs={{0,4},{4,0},{8,12},{12,8},{16,20},{20,16},{24,28},{28,24},{1,5},{5... | collective-permute-start | bytes 3932168 | tf_op jit(solution)/shard_map/ppermute | solution.py:588
  350.4 43.4 %collective-permute-start.53 = (bf16[4,256,320]{1,2,0:T(8,128)(2,1)}, bf16[4,256,320]{1,2,0:T(8,128)(2,1)}, u32[]{:S(2)}, u32[]{:S(2)}) collective-permute-start(bf16[4,256,320]{1,2,0:T(8,128)(2,1)} %copy.267), channel_id=1, source_target_pairs={{0,4},{4,0},{8,12},{12,8},{16,20},{20,16},{24,28},{28,24},{1,5},{5... | collective-permute-start | bytes 1966088 | tf_op jit(solution)/shard_map/ppermute | solution.py:588
  350.9 33.9 %collective-permute-start.68 = (bf16[256,960]{1,0:T(8,128)(2,1)}, bf16[256,960]{1,0:T(8,128)(2,1)}, u32[]{:S(2)}, u32[]{:S(2)}) collective-permute-start(bf16[256,960]{1,0:T(8,128)(2,1)} %get-tuple-element.130.rest_1_), channel_id=1, source_target_pairs={{0,4},{4,0},{8,12},{12,8},{16,20},{20,16},{24,28},{28,24},{1,5},{5... | collective-permute-start | bytes 1474568 | tf_op jit(solution)/shard_map/ppermute | solution.py:588
  357.1 29.0 %collective-permute-start.67 = (bf16[256,960]{1,0:T(8,128)(2,1)}, bf16[256,960]{1,0:T(8,128)(2,1)}, u32[]{:S(2)}, u32[]{:S(2)}) collective-permute-start(bf16[256,960]{1,0:T(8,128)(2,1)} %get-tuple-element.129.rest_0_), channel_id=1, source_target_pairs={{0,4},{4,0},{8,12},{12,8},{16,20},{20,16},{24,28},{28,24},{1,5},{5... | collective-permute-start | bytes 1474568 | tf_op jit(solution)/shard_map/ppermute | solution.py:588
  384.8 48.1 %collective-permute-start.89 = (bf16[640,960]{0,1:T(8,128)(2,1)}, bf16[640,960]{0,1:T(8,128)(2,1)}, u32[]{:S(2)}, u32[]{:S(2)}) collective-permute-start(bf16[640,960]{0,1:T(8,128)(2,1)} %bitcast.53), channel_id=1, source_target_pairs={{1,0},{2,1},{4,7},{7,6},{9,8},{10,9},{12,15},{15,14},{17,16},{18,1... | collective-permute-start | bytes 3686408 | tf_op jit(solution)/shard_map/ppermute | solution.py:715
  386.1 59.8 %collective-permute-start.88 = (bf16[640,960]{0,1:T(8,128)(2,1)}, bf16[640,960]{0,1:T(8,128)(2,1)}, u32[]{:S(2)}, u32[]{:S(2)}) collective-permute-start(bf16[640,960]{0,1:T(8,128)(2,1)} %bitcast.52), channel_id=1, source_target_pairs={{2,0},{3,1},{4,6},{5,7},{10,8},{11,9},{12,14},{13,15},{18,16},{19,... | collective-permute-start | bytes 3686408 | tf_op jit(solution)/shard_map/ppermute | solution.py:715
  387.4 61.1 %collective-permute-start.87 = (bf16[640,960]{0,1:T(8,128)(2,1)}, bf16[640,960]{0,1:T(8,128)(2,1)}, u32[]{:S(2)}, u32[]{:S(2)}) collective-permute-start(bf16[640,960]{0,1:T(8,128)(2,1)} %bitcast.51), channel_id=1, source_target_pairs={{0,1},{3,0},{5,6},{6,7},{8,9},{11,8},{13,14},{14,15},{16,17},{19,1... | collective-permute-start | bytes 3686408 | tf_op jit(solution)/shard_map/ppermute | solution.py:715
  398.2 18.7 %collective-permute-start.52 = (bf16[256,960]{1,0:T(8,128)(2,1)}, bf16[256,960]{1,0:T(8,128)(2,1)}, u32[]{:S(2)}, u32[]{:S(2)}) collective-permute-start(bf16[256,960]{1,0:T(8,128)(2,1)} %get-tuple-element.116.rest_5_), channel_id=1, source_target_pairs={{0,4},{4,0},{8,12},{12,8},{16,20},{20,16},{24,28},{28,24},{1,5},{5... | collective-permute-start | bytes 1474568 | tf_op jit(solution)/shard_map/ppermute | solution.py:588
  400.3 17.4 %collective-permute-start.51 = (bf16[256,960]{1,0:T(8,128)(2,1)}, bf16[256,960]{1,0:T(8,128)(2,1)}, u32[]{:S(2)}, u32[]{:S(2)}) collective-permute-start(bf16[256,960]{1,0:T(8,128)(2,1)} %get-tuple-element.115.rest_4_), channel_id=1, source_target_pairs={{0,4},{4,0},{8,12},{12,8},{16,20},{20,16},{24,28},{28,24},{1,5},{5... | collective-permute-start | bytes 1474568 | tf_op jit(solution)/shard_map/ppermute | solution.py:588
  417.0 76.9 %collective-permute-start.71 = (bf16[2,960,640]{2,1,0:T(8,128)(2,1)}, bf16[2,960,640]{2,1,0:T(8,128)(2,1)}, u32[]{:S(2)}, u32[]{:S(2)}) collective-permute-start(bf16[2,960,640]{2,1,0:T(8,128)(2,1)} %get-tuple-element.136), channel_id=1, source_target_pairs={{0,8},{4,20},{8,0},{12,28},{16,24},{20,4},{24,16},{28,12},{1,9},{5... | collective-permute-start | bytes 7372808 | tf_op jit(solution)/shard_map/ppermute | solution.py:588
  431.4 45.7 %collective-permute-start.55 = (bf16[2,960,320]{1,2,0:T(8,128)(2,1)}, bf16[2,960,320]{1,2,0:T(8,128)(2,1)}, u32[]{:S(2)}, u32[]{:S(2)}) collective-permute-start(bf16[2,960,320]{1,2,0:T(8,128)(2,1)} %copy.271), channel_id=1, source_target_pairs={{0,8},{4,20},{8,0},{12,28},{16,24},{20,4},{24,16},{28,12},{1,9},{5... | collective-permute-start | bytes 3686408 | tf_op jit(solution)/shard_map/ppermute | solution.py:588
  454.4 15.0 %collective-permute-start.90 = (bf16[320,960]{1,0:T(8,128)(2,1)S(1)}, bf16[320,960]{1,0:T(8,128)(2,1)S(1)}, u32[]{:S(2)}, u32[]{:S(2)}) collective-permute-start(bf16[320,960]{1,0:T(8,128)(2,1)S(1)} %dynamic-slice_bitcast_fusion), channel_id=1, source_target_pairs={{0,4},{4,0},{8,12},{12,8},{16,20},{20,16},{24,28},{28,24},{1,5},{5... | collective-permute-start | bytes 1843208 | tf_op jit(solution)/shard_map/ppermute | solution.py:588
  474.9 58.3 %collective-permute-start.42 = (bf16[256,960]{1,0:T(8,128)(2,1)S(1)}, bf16[256,960]{1,0:T(8,128)(2,1)}, u32[]{:S(2)}, u32[]{:S(2)}) collective-permute-start(bf16[256,960]{1,0:T(8,128)(2,1)S(1)} %copy-done.75), channel_id=1, source_target_pairs={{0,0},{4,1},{1,2},{5,3},{2,4},{6,5},{3,6},{7,7},{8,8},{12,9},{9,10... | collective-permute-start | bytes 1474568 | tf_op jit(solution)/shard_map/ppermute | solution.py:604
  487.5 17.8 %collective-permute-start.56 = (bf16[960,320]{0,1:T(8,128)(2,1)}, bf16[960,320]{0,1:T(8,128)(2,1)}, u32[]{:S(2)}, u32[]{:S(2)}) collective-permute-start(bf16[960,320]{0,1:T(8,128)(2,1)} %copy.274), channel_id=1, source_target_pairs={{0,16},{4,12},{8,24},{12,4},{16,0},{20,28},{24,8},{28,20},{1,17},{... | collective-permute-start | bytes 1843208 | tf_op jit(solution)/shard_map/ppermute | solution.py:588
  493.7 11.7 %collective-permute-start.94 = (bf16[80,960]{1,0:T(8,128)(2,1)}, bf16[80,960]{1,0:T(8,128)(2,1)S(1)}, u32[]{:S(2)}, u32[]{:S(2)}) collective-permute-start(bf16[80,960]{1,0:T(8,128)(2,1)} %get-tuple-element.201), channel_id=1, source_target_pairs={{0,16},{4,20},{8,24},{12,28},{16,0},{20,4},{24,8},{28,12},{1,17},{... | collective-permute-start | bytes 460808 | tf_op jit(solution)/shard_map/ppermute | solution.py:588
  493.8 19.5 %collective-permute-start.95 = (bf16[80,960]{1,0:T(8,128)(2,1)}, bf16[80,960]{1,0:T(8,128)(2,1)}, u32[]{:S(2)}, u32[]{:S(2)}) collective-permute-start(bf16[80,960]{1,0:T(8,128)(2,1)} %get-tuple-element.201), channel_id=1, source_target_pairs={{0,24},{4,28},{8,16},{12,20},{16,8},{20,12},{24,0},{28,4},{1,25},{... | collective-permute-start | bytes 460808 | tf_op jit(solution)/shard_map/ppermute | solution.py:588
  500.3 26.7 %collective-permute-start.72 = (bf16[960,640]{1,0:T(8,128)(2,1)}, bf16[960,640]{1,0:T(8,128)(2,1)}, u32[]{:S(2)}, u32[]{:S(2)}) collective-permute-start(bf16[960,640]{1,0:T(8,128)(2,1)} %fusion.3), channel_id=1, source_target_pairs={{0,16},{4,12},{8,24},{12,4},{16,0},{20,28},{24,8},{28,20},{1,17},{... | collective-permute-start | bytes 3686408 | tf_op jit(solution)/shard_map/ppermute | solution.py:588
  513.3 13.3 %collective-permute-start.58 = (bf16[240,320]{1,0:T(8,128)(2,1)S(1)}, bf16[240,320]{1,0:T(8,128)(2,1)S(1)}, u32[]{:S(2)}, u32[]{:S(2)}) collective-permute-start(bf16[240,320]{1,0:T(8,128)(2,1)S(1)} %get-tuple-element.220), channel_id=1, source_target_pairs={{0,2},{1,3},{2,0},{3,1},{4,6},{5,7},{6,4},{7,5},{8,10},{9,11},{10,... | collective-permute-start | bytes 460808 | tf_op jit(solution)/shard_map/ppermute | solution.py:593
  513.3 13.2 %collective-permute-start.57 = (bf16[240,320]{1,0:T(8,128)(2,1)S(1)}, bf16[240,320]{1,0:T(8,128)(2,1)S(1)}, u32[]{:S(2)}, u32[]{:S(2)}) collective-permute-start(bf16[240,320]{1,0:T(8,128)(2,1)S(1)} %get-tuple-element.218), channel_id=1, source_target_pairs={{0,1},{1,2},{2,3},{3,0},{4,5},{5,6},{6,7},{7,4},{8,9},{9,10},{10,1... | collective-permute-start | bytes 460808 | tf_op jit(solution)/shard_map/ppermute | solution.py:593
  529.4 16.8 %collective-permute-start.75 = (bf16[240,640]{1,0:T(8,128)(2,1)S(1)}, bf16[240,640]{1,0:T(8,128)(2,1)S(1)}, u32[]{:S(2)}, u32[]{:S(2)}) collective-permute-start(bf16[240,640]{1,0:T(8,128)(2,1)S(1)} %get-tuple-element.216), channel_id=1, source_target_pairs={{0,3},{1,0},{2,1},{3,2},{4,7},{5,4},{6,5},{7,6},{8,11},{9,8},{10,9... | collective-permute-start | bytes 921608 | tf_op jit(solution)/shard_map/ppermute | solution.py:593
  529.4 26.0 %collective-permute-start.74 = (bf16[240,640]{1,0:T(8,128)(2,1)S(1)}, bf16[240,640]{1,0:T(8,128)(2,1)S(1)}, u32[]{:S(2)}, u32[]{:S(2)}) collective-permute-start(bf16[240,640]{1,0:T(8,128)(2,1)S(1)} %get-tuple-element.217), channel_id=1, source_target_pairs={{0,2},{1,3},{2,0},{3,1},{4,6},{5,7},{6,4},{7,5},{8,10},{9,11},{10,... | collective-permute-start | bytes 921608 | tf_op jit(solution)/shard_map/ppermute | solution.py:593
  530.2 25.3 %collective-permute-start.73 = (bf16[240,640]{1,0:T(8,128)(2,1)S(1)}, bf16[240,640]{1,0:T(8,128)(2,1)S(1)}, u32[]{:S(2)}, u32[]{:S(2)}) collective-permute-start(bf16[240,640]{1,0:T(8,128)(2,1)S(1)} %get-tuple-element.215), channel_id=1, source_target_pairs={{0,1},{1,2},{2,3},{3,0},{4,5},{5,6},{6,7},{7,4},{8,9},{9,10},{10,1... | collective-permute-start | bytes 921608 | tf_op jit(solution)/shard_map/ppermute | solution.py:593
  533.2 37.0 %collective-permute-start.96 = (bf16[1,4,80,960]{3,2,1,0:T(8,128)(2,1)}, bf16[1,4,80,960]{3,2,1,0:T(8,128)(2,1)}, u32[]{:S(2)}, u32[]{:S(2)}) collective-permute-start(bf16[1,4,80,960]{3,2,1,0:T(8,128)(2,1)} %constant_dynamic-slice_fusion.3), channel_id=1, source_target_pairs={{0,4},{4,0},{8,12},{12,8},{16,20},{20,16},{24,28},{28,24},{1,5},{5... | collective-permute-start | bytes 1843208 | tf_op jit(solution)/shard_map/ppermute | solution.py:588
  543.0 13.2 %collective-permute-start.62 = (bf16[240,320]{1,0:T(8,128)(2,1)S(1)}, bf16[240,320]{1,0:T(8,128)(2,1)S(1)}, u32[]{:S(2)}, u32[]{:S(2)}) collective-permute-start(bf16[240,320]{1,0:T(8,128)(2,1)S(1)} %fusion.13.rest_0_), channel_id=1, source_target_pairs={{0,24},{4,28},{8,16},{12,20},{16,8},{20,12},{24,0},{28,4},{1,25},{... | collective-permute-start | bytes 460808 | tf_op jit(solution)/shard_map/ppermute | solution.py:588
  556.2 16.0 %collective-permute-start.76 = (bf16[240,640]{1,0:T(8,128)(2,1)S(1)}, bf16[240,640]{1,0:T(8,128)(2,1)S(1)}, u32[]{:S(2)}, u32[]{:S(2)}) collective-permute-start(bf16[240,640]{1,0:T(8,128)(2,1)S(1)} %fusion.10.rest_0_), channel_id=1, source_target_pairs={{0,8},{4,12},{8,0},{12,4},{16,24},{20,28},{24,16},{28,20},{1,9},{5... | collective-permute-start | bytes 921608 | tf_op jit(solution)/shard_map/ppermute | solution.py:588
  557.9 15.9 %collective-permute-start.77 = (bf16[240,640]{1,0:T(8,128)(2,1)S(1)}, bf16[240,640]{1,0:T(8,128)(2,1)S(1)}, u32[]{:S(2)}, u32[]{:S(2)}) collective-permute-start(bf16[240,640]{1,0:T(8,128)(2,1)S(1)} %fusion.10.rest_0_), channel_id=1, source_target_pairs={{0,16},{4,20},{8,24},{12,28},{16,0},{20,4},{24,8},{28,12},{1,17},{... | collective-permute-start | bytes 921608 | tf_op jit(solution)/shard_map/ppermute | solution.py:588
  559.5 14.3 %collective-permute-start.78 = (bf16[240,640]{1,0:T(8,128)(2,1)S(1)}, bf16[240,640]{1,0:T(8,128)(2,1)S(1)}, u32[]{:S(2)}, u32[]{:S(2)}) collective-permute-start(bf16[240,640]{1,0:T(8,128)(2,1)S(1)} %fusion.10.rest_0_), channel_id=1, source_target_pairs={{0,24},{4,28},{8,16},{12,20},{16,8},{20,12},{24,0},{28,4},{1,25},{... | collective-permute-start | bytes 921608 | tf_op jit(solution)/shard_map/ppermute | solution.py:588
  (135 other events, 1237.3 us)

commit v3 on v2

--- a/solution.py
+++ b/solution.py
@@ -9,7 +9,8 @@
 f32, bf16 = jnp.float32, jnp.bfloat16
 eps = 1e-05
 HEADS, KV_HEADS, HEAD_DIM, GROUP, KVW = 15, 5, 64, 3, 320
-MIB = 1 << 20
+PIECE = 384
+LIMIT = 58 << 20
 WHOLE = pl.BlockSpec(memory_space=pltpu.VMEM)
 LEFT = pl.BlockSpec(memory_space=pl.ANY)
 SCALARS = pl.BlockSpec(memory_space=pltpu.SMEM)
@@ -31,13 +32,15 @@
     return contract(a, b, 0, 0)
 
 
+def whose(core):
+    return 0, 1 + core, 2 - core, 3
+
+
 def fetch(mine, other, kept, sems, core, chip):
-    for who in range(4):
-        at = chip ^ who
-        pltpu.make_async_copy(mine[who], kept.at[core, at], sems.at[core, at]).start()
-    for who in range(4):
-        at = chip ^ who
-        pltpu.make_async_copy(other[who], kept.at[1 - core, at], sems.at[1 - core, at]).start()
+    for kind, pieces in ((core, mine), (1 - core, other)):
+        for who, piece in zip(whose(kind), pieces):
+            at = chip ^ who
+            pltpu.make_async_copy(piece, kept.at[kind, at], sems.at[kind, at]).start()
 
 
 def arrived(kept, sems, *at):
@@ -54,6 +57,10 @@
     scaled = grad * gain
     dx = r * (scaled - hat * jnp.mean(scaled * hat, axis=-1, keepdims=True))
     return dx, jnp.sum(grad * hat, axis=0, keepdims=True)
+
+
+def widened(x):
+    return jnp.concatenate([x, jnp.zeros((x.shape[0], PIECE - x.shape[1]), x.dtype)], axis=1)
 
 
 def rope(u, cos, sin, back):
@@ -74,43 +81,45 @@
     a_ref[...] = a
     cos, sin = cos_ref[...], sin_ref[...]
     arrived(kept, sems, 0, 3)
-    kv_ref[:KVW, :] = rope(nn(a, kept[0, 3]).T, cos, sin, False).astype(bf16)
+    kv_ref[:KVW, :] = rope(nn(a, kept[0, 3, :, :KVW]).T, cos, sin, False).astype(bf16)
     arrived(kept, sems, 1, 0)
-    kv_ref[KVW:, :] = nn(a, kept[1, 0]).T.astype(bf16)
+    kv_ref[KVW:, :] = nn(a, kept[1, 0, :, :KVW]).T.astype(bf16)
     for m in range(3):
         arrived(kept, sems, 0, m)
-        q_ref[pl.ds(m * KVW, KVW), :] = rope(nn(a, kept[0, m]).T, cos, sin, False).astype(bf16)
-
-
-def pre_kernel(sc, h_ref, gain_ref, cos_ref, sin_ref, *rest):
+        q_ref[pl.ds(m * KVW, KVW), :] = rope(nn(a, kept[0, m, :, :KVW]).T, cos, sin, False).astype(bf16)
+
+
+def pre_kernel(sc, ht_ref, gain_ref, cos_ref, sin_ref, *rest):
     mine, other = rest[:4], rest[4:8]
-    a_ref, q_ref, kv_ref, kept, sems = rest[8:]
+    h_ref, a_ref, q_ref, kv_ref, kept, sems = rest[-6:]
     core, chip = sc[0], sc[1]
     fetch(mine, other, kept, sems, core, chip)
-    project(h_ref[...].astype(f32), gain_ref, cos_ref, sin_ref, kept, sems, a_ref, q_ref, kv_ref)
+    h = ht_ref[...].T
+    h_ref[...] = h
+    project(h.astype(f32), gain_ref, cos_ref, sin_ref, kept, sems, a_ref, q_ref, kv_ref)
     for m in range(1, 4):
         arrived(kept, sems, 1, m)
 
 
 def scratch_a(width):
-    return [pltpu.VMEM((2, 4, width, KVW), bf16), pltpu.SemaphoreType.DMA((2, 4))]
+    return [pltpu.VMEM((2, 4, width, PIECE), bf16), pltpu.SemaphoreType.DMA((2, 4))]
 
 
 def shape(s, d):
     return jax.ShapeDtypeStruct(s, d)
 
 
-def pre(sc, h, gain, cos, sin, mine_a, other_a):
-    n, width = h.shape
+def pre(sc, ht, gain, cos, sin, mine_a, other_a, after):
+    width, n = ht.shape
     return pl.pallas_call(
         pre_kernel,
-        out_shape=(shape((n, width), bf16), shape((width, n), bf16), shape((2 * KVW, n), bf16)),
-        in_specs=[SCALARS] + [WHOLE] * 4 + [LEFT] * 8,
-        out_specs=(WHOLE,) * 3,
+        out_shape=(shape((n, width), bf16), shape((n, width), bf16), shape((width, n), bf16), shape((2 * KVW, n), bf16)),
+        in_specs=[SCALARS] + [WHOLE] * 4 + [LEFT] * (8 + len(after)),
+        out_specs=(WHOLE,) * 4,
         scratch_shapes=scratch_a(width),
-        compiler_params=pltpu.CompilerParams(vmem_limit_bytes=24 * MIB),
+        compiler_params=pltpu.CompilerParams(vmem_limit_bytes=LIMIT),
         name="pre",
-    )(sc, h, gain, cos, sin, *mine_a, *other_a)
+    )(sc, ht, gain, cos, sin, *mine_a, *other_a, *after)
 
 
 def bias_of(seg_k, seg_q):
@@ -157,12 +166,13 @@
         in_specs=[WHOLE] * 6,
         out_specs=(WHOLE,) * 2,
         scratch_shapes=[pltpu.VMEM((3 * n, n), f32), pltpu.VMEM((2 * KVW, 3 * n), bf16)],
-        compiler_params=pltpu.CompilerParams(vmem_limit_bytes=24 * MIB),
+        compiler_params=pltpu.CompilerParams(vmem_limit_bytes=LIMIT),
         name="attend",
     )(q, *kvs, seg_k, seg_q)
 
 
-def attend_back_kernel(q_ref, kv0, kv1, kv2, sk_ref, sq_ref, lse_ref, do_ref, cos_ref, sin_ref, dq_ref, far_ref, near_ref, own_ref, bias, kv, dqs):
+def attend_back_kernel(q_ref, kv0, kv1, kv2, sk_ref, sq_ref, lse_ref, do_ref, cos_ref, sin_ref, *rest):
+    dq_ref, far_ref, near_ref, own_ref, bias, kv, dqs = rest[-7:]
     n = q_ref.shape[1]
     bias[...] = bias_of(sk_ref[...], sq_ref[...])
     window_of((kv0, kv1, kv2), kv)
@@ -194,44 +204,42 @@
     lax.fori_loop(0, KV_HEADS, head, 0)
     cos, sin = cos_ref[...] * scale, sin_ref[...] * scale
     for m in range(3):
-        dq_ref[m] = rope(dqs[m * KVW : (m + 1) * KVW, :], cos, sin, True).T.astype(bf16)
-
-
-def attend_back(q, kvs, seg_k, seg_q, lse, do, cos, sin):
+        dq_ref[m] = widened(rope(dqs[m * KVW : (m + 1) * KVW, :], cos, sin, True).T.astype(bf16))
+
+
+def attend_back(q, kvs, seg_k, seg_q, lse, do, cos, sin, after=()):
     width, n = q.shape
     block = (2 * KVW, n)
     return pl.pallas_call(
         attend_back_kernel,
-        out_shape=(shape((3, n, KVW), bf16), shape(block, f32), shape(block, bf16), shape(block, f32)),
-        in_specs=[WHOLE] * 10,
+        out_shape=(shape((3, n, PIECE), bf16), shape(block, f32), shape(block, bf16), shape(block, f32)),
+        in_specs=[WHOLE] * 10 + [LEFT] * len(after),
         out_specs=(WHOLE,) * 4,
         scratch_shapes=[pltpu.VMEM((3 * n, n), f32), pltpu.VMEM((2 * KVW, 3 * n), bf16), pltpu.VMEM((width, n), f32)],
-        compiler_params=pltpu.CompilerParams(vmem_limit_bytes=32 * MIB),
+        compiler_params=pltpu.CompilerParams(vmem_limit_bytes=LIMIT),
         name="attend_back",
-    )(q, *kvs, seg_k, seg_q, lse, do, cos, sin)
+    )(q, *kvs, seg_k, seg_q, lse, do, cos, sin, *after)
 
 
 def fetch_ffn(mine_b, other_b, mine_d, other_d, wb, wd, sem_b, sem_d, core, chip):
     fetch(mine_b, other_b, wb, sem_b, core, chip)
-    pltpu.make_async_copy(mine_d, wd.at[:, core], sem_d.at[0]).start()
-    pltpu.make_async_copy(other_d, wd.at[:, 1 - core], sem_d.at[1]).start()
+    half = mine_d.shape[1]
+    for c, part, sem in ((core, mine_d, 0), (1 - core, other_d, 1)):
+        rows = pl.ds(pl.multiple_of(c * half, half), half)
+        pltpu.make_async_copy(part, wd.at[:, rows], sem_d.at[sem]).start()
 
 
 def arrived_down(mine_d, wd, sem_d):
+    half = mine_d.shape[1]
     for c in range(2):
-        pltpu.make_async_copy(mine_d, wd.at[:, c], sem_d.at[c]).wait()
-
-
-def down_of(wd, m):
-    rows = wd.shape[1] * wd.shape[2]
-    return wd[m].reshape(rows, wd.shape[3])
-
-
-def scratch_ffn(width, n, rows):
+        pltpu.make_async_copy(mine_d, wd.at[:, c * half : (c + 1) * half], sem_d.at[c]).wait()
+
+
+def scratch_ffn(width, n):
     return [
         pltpu.VMEM((2, 4, width, n), bf16),
         pltpu.SemaphoreType.DMA((2, 4)),
-        pltpu.VMEM((4, 2, rows, width), bf16),
+        pltpu.VMEM((4, width, n), bf16),
         pltpu.SemaphoreType.DMA((2,)),
     ]
 
@@ -249,7 +257,7 @@
     o_ref[...] = o
     for m in range(1, 4):
         arrived(wa, sem_a, 1, m)
-    h1 = h_ref[...].astype(f32) + jnp.concatenate([nn(o, wa[1, m]) for m in range(1, 4)], axis=1)
+    h1 = h_ref[...].astype(f32) + jnp.concatenate([nn(o, wa[1, m, :, :KVW]) for m in range(1, 4)], axis=1)
     h1_ref[...] = h1
     b = normed(h1, gain_ref[...]).astype(bf16)
     b_ref[...] = b
@@ -267,8 +275,8 @@
         z_ref[:, cols] = z
         if m == 0:
             arrived_down(mine_d, wd, sem_d)
-        total = total + nn(z, down_of(wd, m))
-    next_ref[...] = total.astype(next_ref.dtype)
+        total = total + nt(z, wd[m])
+    next_ref[...] = total.astype(bf16).T if last else total
     if last:
         arrived(wa, sem_a, 1, 0)
         for m in range(4):
@@ -281,7 +289,7 @@
     width, n = ot.shape
     hidden = wb[0][0].shape[1] * 4
     outs = [shape((n, width), bf16), shape((n, width), f32), shape((n, width), bf16)] + [shape((n, hidden), bf16)] * 3
-    outs += [shape((n, width), bf16 if last else f32)]
+    outs += [shape((width, n), bf16) if last else shape((n, width), f32)]
     if not last:
         outs += [shape((n, width), bf16), shape((width, n), bf16), shape((2 * KVW, n), bf16)]
     return pl.pallas_call(
@@ -289,8 +297,8 @@
         out_shape=tuple(outs),
         in_specs=[SCALARS] + [WHOLE] * 6 + [LEFT] * 18,
         out_specs=(WHOLE,) * len(outs),
-        scratch_shapes=scratch_a(width) + scratch_ffn(width, hidden // 4, wd[0].shape[1]),
-        compiler_params=pltpu.CompilerParams(vmem_limit_bytes=56 * MIB),
+        scratch_shapes=scratch_a(width) + scratch_ffn(width, hidden // 4),
+        compiler_params=pltpu.CompilerParams(vmem_limit_bytes=LIMIT),
         name="post",
     )(sc, ot, h, gain, gain_a, cos, sin, *wa[0], *wa[1], *wb[0], *wb[1], *wd)
 
@@ -310,7 +318,7 @@
     db = None
     for m in range(4):
         cols = slice(m * n, (m + 1) * n)
-        dz = nt(gb, down_of(wd, m))
+        dz = nn(gb, wd[m])
         gate, up = gate_ref[:, cols].astype(f32), up_ref[:, cols].astype(f32)
         sig = 1.0 / (1.0 + jnp.exp(-gate))
         dup = (dz * (gate * sig)).astype(bf16)
@@ -330,9 +338,9 @@
     do = None
     for p in range(3):
         part = low[:, p * KVW : (p + 1) * KVW]
-        p_ref[p] = part
+        p_ref[p] = widened(part)
         arrived(wa, sem_a, 1, p + 1)
-        part = nt(wa[1, p + 1], part)
+        part = nt(wa[1, p + 1, :, :KVW], part)
         do = part if p == 0 else do + part
     do_ref[...] = do.astype(bf16)
 
@@ -346,7 +354,7 @@
     da = None
     for m in range(3):
         arrived(wa, sem_a, 0, m)
-        part = nt(dq_ref[m], wa[0, m])
+        part = nt(dq_ref[m, :, :KVW], wa[0, m, :, :KVW])
         da = part if m == 0 else da + part
     return da
 
@@ -356,11 +364,11 @@
     grad = own_ref[...] + far_ref[...].astype(f32) + jnp.where(core == 0, near_ref[...].astype(f32), 0.0)
     dk = rope(grad[:KVW], cos, sin, True).T.astype(bf16)
     dv = grad[KVW:].T.astype(bf16)
-    dk_ref[...] = dk
-    dv_ref[...] = dv
+    dk_ref[...] = widened(dk)
+    dv_ref[...] = widened(dv)
     arrived(wa, sem_a, 0, 3)
     arrived(wa, sem_a, 1, 0)
-    da = da + nt(dk, wa[0, 3]) + nt(dv, wa[1, 0])
+    da = da + nt(dk, wa[0, 3, :, :KVW]) + nt(dv, wa[1, 0, :, :KVW])
     return norm_back(h, gain, da)
 
 
@@ -395,14 +403,14 @@
         wb, sem_b, wd, sem_d = take(4)
         fetch_ffn(mine_b, other_b, mine_d, other_d, wb, wd, sem_b, sem_d, core, chip)
     if start:
-        state = g_ref[...].astype(f32)
+        state = g_ref[...].T.astype(f32)
     else:
         da = query_back(dq_ref, wa, sem_a)
         dx, dgain = project_back(da, own_ref, near_ref, far_ref, core, cos_ref, sin_ref, dk_ref, dv_ref, h_ref[...].astype(f32), gain_a[...], wa, sem_a)
         dgain_a[...] = dgain
         state = g1_in[...] + dx
     if end:
-        g_out[...] = state.astype(bf16)
+        g_out[...] = state.astype(bf16).T
         finish_a(wa, sem_a, (1, 1), (1, 2), (1, 3))
     else:
         ffn_back(state, core, (*ins, *outs), (wa, sem_a, wb, sem_b, wd, sem_d), mine_d)
@@ -419,29 +427,29 @@
     if not end:
         args += [*wb[0], *wb[1], *wd]
         specs += [LEFT] * 10
-        scratch += scratch_ffn(width, wb[0][0].shape[1], wd[0].shape[1])
+        scratch += scratch_ffn(width, wb[0][0].shape[1])
     args += list(tail)
     specs += [WHOLE] * len(tail)
-    n = tail[0].shape[0]
+    n = tail[0].shape[1 if start else 0]
     outs = []
     if not end:
         args += list(ffn)
         specs += [WHOLE] * len(ffn)
     if not start:
-        outs += [shape((n, KVW), bf16), shape((n, KVW), bf16), shape((1, width), f32)]
+        outs += [shape((n, PIECE), bf16), shape((n, PIECE), bf16), shape((1, width), f32)]
     if end:
-        outs += [shape((n, width), bf16)]
+        outs += [shape((width, n), bf16)]
     else:
         hidden = ffn[0].shape[1]
         outs += [shape((n, width), bf16), shape((n, hidden), bf16), shape((n, hidden), bf16), shape((n, hidden // 2), bf16), shape((n, hidden // 2), bf16)]
-        outs += [shape((n, width), f32), shape((3, n, KVW), bf16), shape((1, width), f32), shape((width, n), bf16)]
+        outs += [shape((n, width), f32), shape((3, n, PIECE), bf16), shape((1, width), f32), shape((width, n), bf16)]
     return pl.pallas_call(
         functools.partial(back_kernel, start, end),
         out_shape=tuple(outs),
         in_specs=specs,
         out_specs=(WHOLE,) * len(outs),
         scratch_shapes=scratch,
-        compiler_params=pltpu.CompilerParams(vmem_limit_bytes=(24 if end else 56) * MIB),
+        compiler_params=pltpu.CompilerParams(vmem_limit_bytes=LIMIT),
         name="back_end" if end else ("back_start" if start else "back_join"),
     )(*args)
 
@@ -457,58 +465,56 @@
         dst[:, i * n : (i + 1) * n] = block[...].T
 
 
-def grad_ffn_kernel(sc, *rest):
+def grad_ffn_kernel(first, sc, *rest):
     lefts, rights = rest[:4], rest[4:8]
-    send_ref, keep_ref, left, right = rest[8:]
+    out_ref, left, right = rest[-3:]
     core, chip = sc[0], sc[1]
     n, cols = rights[0].shape[0], right.shape[1]
     turned(left, lefts)
-    for i, m in enumerate(by_turn(core, chip)):
+    for i, m in enumerate(by_turn(core, chip)[first : first + 2]):
         at = pl.multiple_of(m * cols, 128)
         for j, block in enumerate(rights):
             right[j * n : (j + 1) * n, :] = block[:, pl.ds(at, cols)]
-        out = send_ref if i < 2 else keep_ref
-        out[i % 2] = nn(left[...], right[...]).astype(bf16)
-
-
-def grad_ffn(sc, lefts, rights):
+        out_ref[i] = nn(left[...], right[...]).astype(bf16)
+
+
+def grad_ffn(first, sc, lefts, rights, after=()):
     n, width = lefts[0].shape
     cols = rights[0].shape[1] // 4
-    out = shape((2, width, cols), bf16)
-    return pl.pallas_call(
-        grad_ffn_kernel,
-        out_shape=(out, out),
-        in_specs=[SCALARS] + [WHOLE] * 8,
-        out_specs=(WHOLE,) * 2,
+    return pl.pallas_call(
+        functools.partial(grad_ffn_kernel, first),
+        out_shape=shape((2, width, cols), bf16),
+        in_specs=[SCALARS] + [WHOLE] * 8 + [LEFT] * len(after),
+        out_specs=WHOLE,
         scratch_shapes=[pltpu.VMEM((width, 4 * n), bf16), pltpu.VMEM((4 * n, cols), bf16)],
-        compiler_params=pltpu.CompilerParams(vmem_limit_bytes=48 * MIB),
+        compiler_params=pltpu.CompilerParams(vmem_limit_bytes=LIMIT),
         name="grad_ffn",
-    )(sc, *lefts, *rights)
+    )(sc, *lefts, *rights, *after)
 
 
 def grad_down_kernel(*rest):
     lefts, rights = rest[:4], rest[4:8]
-    out_ref, left, right = rest[8:]
-    n, rows = rights[0].shape[0], out_ref.shape[1]
+    out_ref, left, right = rest[-3:]
+    n, cols = rights[0].shape[0], right.shape[1]
     turned(left, lefts)
-    for j, block in enumerate(rights):
-        right[j * n : (j + 1) * n, :] = block[...]
     for i in range(2):
-        out_ref[i] = nn(left[i * rows : (i + 1) * rows, :], right[...]).astype(bf16)
-
-
-def grad_down(lefts, rights):
-    n, rows = lefts[0].shape
-    width = rights[0].shape[1]
+        for j, block in enumerate(rights):
+            right[j * n : (j + 1) * n, :] = block[:, i * cols : (i + 1) * cols]
+        out_ref[i] = nn(left[...], right[...]).astype(bf16)
+
+
+def grad_down(lefts, rights, after=()):
+    n, width = lefts[0].shape
+    cols = rights[0].shape[1] // 2
     return pl.pallas_call(
         grad_down_kernel,
-        out_shape=shape((2, rows // 2, width), bf16),
-        in_specs=[WHOLE] * 8,
+        out_shape=shape((2, width, cols), bf16),
+        in_specs=[WHOLE] * 8 + [LEFT] * len(after),
         out_specs=WHOLE,
-        scratch_shapes=[pltpu.VMEM((rows, 4 * n), bf16), pltpu.VMEM((4 * n, width), bf16)],
-        compiler_params=pltpu.CompilerParams(vmem_limit_bytes=40 * MIB),
+        scratch_shapes=[pltpu.VMEM((width, 4 * n), bf16), pltpu.VMEM((4 * n, cols), bf16)],
+        compiler_params=pltpu.CompilerParams(vmem_limit_bytes=LIMIT),
         name="grad_down",
-    )(*lefts, *rights)
+    )(*lefts, *rights, *after)
 
 
 def grad_attention_kernel(sc, *rest):
@@ -540,7 +546,7 @@
         in_specs=[SCALARS] + [WHOLE] * 12,
         out_specs=(WHOLE,) * 2,
         scratch_shapes=[pltpu.VMEM((2, width, 4 * n), bf16), pltpu.VMEM((4 * n, cols), bf16)],
-        compiler_params=pltpu.CompilerParams(vmem_limit_bytes=40 * MIB),
+        compiler_params=pltpu.CompilerParams(vmem_limit_bytes=LIMIT),
         name="grad_attention",
     )(sc, *a, *o, *rights)
 
@@ -548,33 +554,84 @@
 def lay_kernel(sc, *rest):
     mine, other, outs, kept = rest[:4], rest[4:8], rest[8:-1], rest[-1]
     core, chip = sc[0], sc[1]
-    for who in range(4):
-        kept[core, chip ^ who] = mine[who][...]
-        kept[1 - core, chip ^ who] = other[who][...]
-    cols = [jnp.concatenate([kept[c, m].astype(f32) for m in range(4)], axis=1) for c in range(2)]
+    for kind, pieces in ((core, mine), (1 - core, other)):
+        for who, piece in zip(whose(kind), pieces):
+            kept[kind, chip ^ who] = piece[...]
+    n = sum(o.shape[1] for o in outs) // 8
+    cols = [jnp.concatenate([kept[c, m, :, :n].astype(f32) for m in range(4)], axis=1) for c in range(2)]
     if len(outs) == 2:
         outs[0][...] = cols[0]
         outs[1][...] = cols[1]
     else:
-        n = kept.shape[3]
         outs[0][...] = cols[0][:, : 3 * n]
         outs[1][...] = cols[0][:, 3 * n :]
         outs[2][...] = cols[1][:, :n]
         outs[3][...] = cols[1][:, n:]
 
 
-def lay(sc, mine, other, pieces):
+def lay(sc, mine, other, widths):
     rows, n = mine[0].shape
-    outs = tuple(shape((rows, p * n), f32) for p in pieces)
+    outs = tuple(shape((rows, w), f32) for w in widths)
     return pl.pallas_call(
         lay_kernel,
         out_shape=outs,
         in_specs=[SCALARS] + [WHOLE] * 8,
         out_specs=(WHOLE,) * len(outs),
         scratch_shapes=[pltpu.VMEM((2, 4, rows, n), bf16)],
-        compiler_params=pltpu.CompilerParams(vmem_limit_bytes=32 * MIB),
+        compiler_params=pltpu.CompilerParams(vmem_limit_bytes=LIMIT),
         name="lay",
     )(sc, *mine, *other)
+
+
+def pick_kernel(sc, gate, up, down, *rest):
+    b_ref, d_ref, sems = rest[-3:]
+    core, chip = sc[0], sc[1]
+    cols, half = b_ref.shape[1], d_ref.shape[0]
+    at = pl.ds(pl.multiple_of(chip * cols, 128), cols)
+    rows = pl.ds(pl.multiple_of(core * half, half), half)
+    copy = pltpu.make_async_copy(down.at[rows, :], d_ref, sems.at[1])
+    copy.start()
+    for c, source in ((0, gate), (1, up)):
+
+        @pl.when(core == c)
+        def _():
+            pltpu.make_async_copy(source.at[:, at], b_ref, sems.at[0]).start()
+
+    pltpu.make_async_copy(gate.at[:, at], b_ref, sems.at[0]).wait()
+    copy.wait()
+
+
+def pick(sc, gate, up, down, after):
+    return pl.pallas_call(
+        pick_kernel,
+        out_shape=(shape((gate.shape[0], gate.shape[1] // 4), bf16), shape((down.shape[0] // 2, down.shape[1]), bf16)),
+        in_specs=[SCALARS] + [LEFT] * (3 + len(after)),
+        out_specs=(LEFT, LEFT),
+        scratch_shapes=[pltpu.SemaphoreType.DMA((2,))],
+        compiler_params=pltpu.CompilerParams(vmem_limit_bytes=LIMIT),
+        name="pick",
+    )(sc, gate, up, down, *after)
+
+
+def stack_kernel(sc, *rest):
+    parts, out_ref, sems = rest[:4], rest[-2], rest[-1]
+    copies = [pltpu.make_async_copy(p, out_ref.at[(sc[2] - s) & 3], sems.at[s]) for s, p in enumerate(parts)]
+    for copy in copies:
+        copy.start()
+    for copy in copies:
+        copy.wait()
+
+
+def stack(sc, parts, after=()):
+    return pl.pallas_call(
+        stack_kernel,
+        out_shape=shape((4,) + parts[0].shape, parts[0].dtype),
+        in_specs=[SCALARS] + [LEFT] * (4 + len(after)),
+        out_specs=LEFT,
+        scratch_shapes=[pltpu.SemaphoreType.DMA((4,))],
+        compiler_params=pltpu.CompilerParams(vmem_limit_bytes=LIMIT),
+        name="stack",
+    )(sc, *parts, *after)
 
 
 CORE, SIDE, BACK = 1, 2, 4
@@ -609,38 +666,22 @@
     return d & 1, (d >> 1) & 3, z
 
 
-def ring_gather(shard):
+def turns(shard):
+    return [shard] + [turn_z(shard, s) for s in range(1, lax.axis_size("fsdp"))]
+
+
+def plane_gather(piece):
+    first, second = flip(piece, SIDE, BACK), flip(piece, BACK, SIDE)
+    mine = (piece, first, second, flip(first, BACK, SIDE))
+    return mine, tuple(flip(p, CORE) for p in mine)
+
+
+def small_gather(shard):
     z = lax.axis_index("fsdp")
-    depth = lax.axis_size("fsdp")
-    parts = [shard] + [turn_z(shard, s) for s in range(1, depth)]
-    full = jnp.zeros((depth,) + shard.shape, shard.dtype)
-    for s, part in enumerate(parts):
-        full = lax.dynamic_update_index_in_dim(full, part, (z - s) % depth, 0)
+    full = jnp.zeros((lax.axis_size("fsdp"),) + shard.shape, shard.dtype)
+    for s, part in enumerate(turns(shard)):
+        full = lax.dynamic_update_index_in_dim(full, part, (z - s) % full.shape[0], 0)
     return full
-
-
-def plane_gather(piece):
-    core, _, _ = place()
-    x, y = flip(piece, SIDE), flip(piece, BACK)
-    opposite = flip(jnp.where(core == 0, x, y), BACK, SIDE)
-    mine = (piece, x, y, opposite)
-    return mine, tuple(flip(p, CORE) for p in mine)
-
-
-def gather_weights(query, key, value, out, gate, up, down):
-    core, chip, _ = place()
-    rows, width = query.shape
-    depth = lax.axis_size("fsdp")
-    first = jnp.concatenate([query, key, value, out], axis=1)
-    n = first.shape[1] // 8
-    piece = lax.dynamic_slice(first, (0, n * (core * 4 + chip)), (rows, n))
-    wa = plane_gather(ring_gather(piece).reshape(depth * rows, n))
-    n = gate.shape[1] // 4
-    piece = lax.dynamic_slice(jnp.where(core == 0, gate, up), (0, n * chip), (rows, n))
-    wb = plane_gather(ring_gather(piece).reshape(depth * rows, n))
-    n = down.shape[0] // 2
-    piece = ring_gather(lax.dynamic_slice(down, (n * core, 0), (n, width)))
-    return wa, wb, (piece, flip(piece, CORE))
 
 
 def window(own):
@@ -685,23 +726,23 @@
     return total
 
 
-def spread(piece):
-    mine = (piece, flip(piece, SIDE), flip(piece, BACK), flip(piece, SIDE | BACK))
-    return mine, tuple(flip(p, CORE) for p in mine)
-
-
-def reduce_pieces(sc, send, keep, pieces):
+def spread(piece, both=True):
+    mine = (piece, flip(piece, SIDE, BACK), flip(piece, BACK, SIDE), flip(piece, SIDE | BACK))
+    return (mine, tuple(flip(p, CORE) for p in mine)) if both else mine
+
+
+def reduce_pieces(sc, send, keep, widths):
     depth = lax.axis_size("fsdp")
     own = plane_reduce(send, keep)
     own = own.reshape((depth, own.shape[0] // depth) + own.shape[1:])
     own = over_groups(ring_reduce(own)).astype(bf16)
-    return lay(sc, *spread(own), pieces)
+    return lay(sc, *spread(own), widths)
 
 
 def reduce_down(parts):
     core, chip, z = place()
     depth, count = lax.axis_size("fsdp"), lax.axis_size("dp")
-    _, rows, width = parts.shape
+    _, rows, cols = parts.shape
     owner = (z >> 1) == core
     total = lax.dynamic_index_in_dim(parts, z & 1, 0, keepdims=False).astype(f32)
     for s in range(1, depth):
@@ -713,20 +754,19 @@
                 if (b >> 1) == (d & 1):
                     pairs.append((d * depth + a, d * depth + b))
         total = total + lax.ppermute(part, ("dp", "fsdp"), pairs).astype(f32)
-    halves = total.astype(bf16).reshape(2, rows // 2, width)
+    half, n = rows // 2, rows // 8
+    halves = total.astype(bf16).reshape(2, half, cols)
     given = flip(lax.dynamic_index_in_dim(halves, 1 - core, 0, keepdims=False), CORE)
     kept = lax.dynamic_index_in_dim(halves, core, 0, keepdims=False)
-    mine = jnp.where(owner, kept, given).reshape(4, rows // 8, width)
-    order = by_turn(core, chip)
-    picked = [lax.dynamic_index_in_dim(mine, m, 0, keepdims=False) for m in order]
+    mine = jnp.where(owner, kept, given).reshape(4, n, cols)
+    picked = [lax.dynamic_index_in_dim(mine, m, 0, keepdims=False) for m in by_turn(core, chip)]
     own = over_groups(plane_reduce(jnp.stack(picked[:2]), picked[2:])).astype(bf16)
-    full = jnp.zeros((2, 4, rows // 8, width), bf16)
-    for c, parts in ((core, spread(own)[0]),):
-        for who, part in enumerate(parts):
-            full = lax.dynamic_update_slice(full, part[None, None], (c, chip ^ who, 0, 0))
-    mine = lax.dynamic_index_in_dim(full, core, 0, keepdims=True)
-    full = lax.dynamic_update_slice(full, flip(mine, CORE), (1 - core, 0, 0, 0))
-    return full.reshape(rows, width).astype(f32)
+    mine = jnp.zeros((4, n, cols), bf16)
+    for who, part in zip(whose(core), spread(own, False)):
+        mine = lax.dynamic_update_index_in_dim(mine, part, chip ^ who, 0)
+    other = flip(mine, CORE)
+    full = jnp.where(core == 0, jnp.concatenate([mine, other]), jnp.concatenate([other, mine]))
+    return full.reshape(rows, cols).astype(f32).T
 
 
 def reduce_gains(total):
@@ -744,13 +784,26 @@
 
 def body(tokens, segment_ids, attn_gain, query_weight, key_weight, value_weight, out_weight, ffn_gain, gate_weight, up_weight, down_weight, cotangent):
     core, chip, z = place()
-    sc = jnp.stack([core, chip]).astype(jnp.int32)
+    sc = jnp.stack([core, chip, z]).astype(jnp.int32)
     _, stretch, width = tokens.shape
-    tokens = home_to_work(tokens[0])
-    gains = ring_gather(jnp.stack([attn_gain, ffn_gain]))
+    rows, depth = query_weight.shape[0], lax.axis_size("fsdp")
+
+    first = jnp.concatenate([query_weight, key_weight, value_weight, out_weight], axis=1)
+    first = jnp.pad(first, ((0, 0), (0, PIECE - KVW)))
+    parts_a = turns(lax.dynamic_slice(first, (0, KVW * (core * 4 + chip)), (rows, PIECE)))
+    wa = plane_gather(stack(sc, parts_a).reshape(depth * rows, PIECE))
+    piece_b, piece_d = pick(sc, gate_weight, up_weight, down_weight.T, parts_a[1:])
+    whole_b = stack(sc, turns(piece_b)).reshape(depth * rows, piece_b.shape[1])
+    wb = plane_gather(whole_b)
+    whole_d = stack(sc, turns(piece_d))
+    wd = whole_d, flip(whole_d, CORE)
+    weights = wa, wb, wd
+
+    tokens = home_to_work(tokens[0].T)
+    gains = small_gather(jnp.stack([attn_gain, ffn_gain]))
     gains = jnp.moveaxis(gains, 0, 1).reshape(2, 1, width).astype(f32)
     gain_a, gain_f = gains[0], gains[1]
-    row = ring_gather(segment_ids[0]).reshape(-1)
+    row = small_gather(segment_ids[0]).reshape(-1)
     row = jnp.where((z >> 1) == core, row, flip(row, CORE))
     block = 2 * (z & 1) + core
     padded = jnp.concatenate([jnp.full((2 * stretch,), -1, row.dtype), row])
@@ -762,18 +815,16 @@
     freq = rope_base ** (-2.0 * jnp.arange(HEAD_DIM // 2, dtype=f32) / HEAD_DIM)
     angle = freq[:, None] * positions[None, :]
     cos, sin = jnp.cos(angle), jnp.sin(angle)
-    weights = gather_weights(query_weight, key_weight, value_weight, out_weight, gate_weight, up_weight, down_weight)
-    wa, wb, wd = weights
-    cot = home_to_work(cotangent[0])
-
-    a0, q0, own = pre(sc, tokens, gain_a, cos, sin, *wa)
+    cot = home_to_work(cotangent[0].T)
+
+    h_0, a0, q0, own = pre(sc, tokens, gain_a, cos, sin, *wa, [whole_b])
     kv0 = window(own)
     o0, lse0 = attend(q0, kv0, seg_k, seg_q)
-    mixed0, h1_0, b0, gate0, up0, z0, h_1, a1, q1, own = post(False, sc, o0, tokens, gain_f, gain_a, cos, sin, *weights)
+    mixed0, h1_0, b0, gate0, up0, z0, h_1, a1, q1, own = post(False, sc, o0, h_0, gain_f, gain_a, cos, sin, *weights)
     kv1 = window(own)
     o1, lse1 = attend(q1, kv1, seg_k, seg_q)
     mixed1, h1_1, b1, gate1, up1, z1, output = post(True, sc, o1, h_1, gain_f, gain_a, cos, sin, *weights)
-    output = home_to_work(output, back=True)
+    output = home_to_work(output, back=True).T
 
     gb1, act1, away1, zk1, zs1, g1, p1, dgain_f1, do = back(True, False, sc, weights, [cot], [gate1, up1, h1_1, gain_f, z1])
     dq1, far, near, own = attend_back(q1, kv1, seg_k, seg_q, lse1, do, cos, sin)
@@ -785,16 +836,17 @@
         return [*own, *(flip(v, CORE) for v in own)]
 
     lefts, mid = pair(b1, b0), [act1, act0, flip(away1, CORE), flip(away0, CORE)]
-    send_b, keep_b = grad_ffn(sc, lefts, mid)
-    down_parts = grad_down([zk1, zk0, flip(zs1, CORE), flip(zs0, CORE)], pair(gb1, gb0))
-    grad_gate, grad_up = reduce_pieces(sc, send_b, keep_b, (4, 4))
-    grad_down_ = reduce_down(down_parts)
-
-    dq0, far, near, own = attend_back(q0, kv0, seg_k, seg_q, lse0, do, cos, sin)
+    send_b = grad_ffn(0, sc, lefts, mid)
+    parts_d = grad_down(pair(gb1, gb0), [zk1, zk0, flip(zs1, CORE), flip(zs0, CORE)], [send_b])
+    keep_b = grad_ffn(2, sc, lefts, mid, [parts_d])
+    grad_gate, grad_up = reduce_pieces(sc, send_b, keep_b, (gate_weight.shape[1],) * 2)
+    grad_down_ = reduce_down(parts_d)
+
+    dq0, far, near, own = attend_back(q0, kv0, seg_k, seg_q, lse0, do, cos, sin, [keep_b])
     near, far = unwindow(far, near)
-    tail = [g1, dq0, own, near, far, tokens, gain_a, cos, sin]
+    tail = [g1, dq0, own, near, far, h_0, gain_a, cos, sin]
     dk0, dv0, dgain_a0, grad_tokens = back(False, True, sc, weights, tail, None)
-    grad_tokens = home_to_work(grad_tokens, back=True).astype(f32)
+    grad_tokens = home_to_work(grad_tokens, back=True).astype(f32).T
 
     kept, sent = [], []
     for dq, dk, dv, p in ((dq1, dk1, dv1, p1), (dq0, dk0, dv0, p0)):
@@ -802,7 +854,7 @@
         kept.append(jnp.where(core == 0, first, second))
         sent.append(flip(jnp.where(core == 0, second, first), CORE))
     send_a, keep_a = grad_attention(sc, pair(a1, a0), pair(mixed1, mixed0), kept + sent)
-    grad_query, grad_key, grad_value, grad_out = reduce_pieces(sc, send_a, keep_a, (3, 1, 1, 3))
+    grad_query, grad_key, grad_value, grad_out = reduce_pieces(sc, send_a, keep_a, (width, KVW, KVW, width))
     dgain_a, dgain_f = reduce_gains(jnp.concatenate([dgain_a1 + dgain_a0, dgain_f1 + dgain_f0]))
     return (output[None], grad_tokens[None], dgain_a, grad_query, grad_key, grad_value, grad_out, dgain_f, grad_gate, grad_up, grad_down_)
 

time: 595 us -> 758 us (1.27)
  Pallas kernels: 166 us -> 359 us
  local copies, waits for them, and re-layouts: 119 us -> 28.5 us
  waiting for transfers between devices: 159 us -> 212 us
  starting transfers between devices: 107 us -> 121 us
    pallas_call x5 -> x10, Pallas kernels: 45.5 us -> 229 us  [the longest x3 139 us: stack(): pl.pallas_call(stack_kernel, out_shape=shape((4,) + parts[0].shape, parts...]
    ppermute x62, waiting for transfers between devices: 41.7 us -> 78.7 us  [flip(): lax.ppermute(value, 'dp', [(i, i ^ bits[i & 1]) for i in range(count)])]
    unnamed x217 -> x136, local copies, waits for them, and re-layouts: 53.4 us -> 18.2 us
    ppermute x13 -> x0, local copies, waits for them, and re-layouts: 25.8 us -> none  [the longest x10 18.3 us: flip(): lax.ppermute(value, 'dp', [(i, i ^ bits[i & 1]) for i in range(count)])]
    ppermute x24, starting transfers between devices: 37.4 us -> 62.2 us  [turn_z(): lax.ppermute(value, 'fsdp', [(i, (i + step) % count) for i in range(count)])]
    dynamic_update_slice x23 -> x11, local copies, waits for them, and re-layouts: 12.3 us -> 0.39 us  [the longest x8 0.32 us: small_gather(): lax.dynamic_update_index_in_dim(full, part, (z - s) % full.shape[0], 0)]
    ppermute x24, waiting for transfers between devices: 80 us -> 91.3 us  [turn_z(): lax.ppermute(value, 'fsdp', [(i, (i + step) % count) for i in range(count)])]
    ppermute x2, waiting for transfers between devices: 15.9 us -> 26.7 us  [unwindow(): lax.ppermute(far, 'fsdp', [(z + 1, z) for z in range(0, depth, 2)])]
  transfers between devices with their start and end apart: 97 -> 97, of which waited for: 28 -> 32; matrix products, arithmetic and copies ran while one was open for 19% -> 5% of each run, Pallas kernels for 19% -> 36%
where the time goes in v3:
time: 758 us; the launch traced here: 749 us
  Pallas kernels  359 us (47%)
  waiting for transfers between devices  212 us (28%)
  starting transfers between devices  121 us (16%)
  local copies, waits for them, and re-layouts  28.5 us (4%)
  other arithmetic  26.7 us (4%)
    pallas_call x3, Pallas kernels, stack(): pl.pallas_call(stack_kernel, out_shape=shape((4,) + parts[0].shape, parts...  139 us
    ppermute x24, waiting for transfers between devices, turn_z(): lax.ppermute(value, 'fsdp', [(i, (i + step) % count) for i in range(count)])  91.3 us
    ppermute x62, waiting for transfers between devices, flip(): lax.ppermute(value, 'dp', [(i, i ^ bits[i & 1]) for i in range(count)])  78.7 us
    ppermute x24, starting transfers between devices, turn_z(): lax.ppermute(value, 'fsdp', [(i, (i + step) % count) for i in range(count)])  62.2 us
    pallas_call x3, Pallas kernels, back(): pl.pallas_call(functools.partial(back_kernel, start, end), out_shape=tupl...  50.1 us
    pallas_call x2, Pallas kernels, post(): pl.pallas_call(functools.partial(post_kernel, last), out_shape=tuple(outs...  38 us
    ppermute x62, starting transfers between devices, flip(): lax.ppermute(value, 'dp', [(i, i ^ bits[i & 1]) for i in range(count)])  37.9 us
    pallas_call x1, Pallas kernels, pick(): pl.pallas_call(pick_kernel, out_shape=(shape((gate.shape[0], gate.shape[1...  29.8 us
  transfers between devices with their start and end apart: 97, of which 32 were waited for; matrix products, arithmetic and copies ran while one was open for 5% of the time, Pallas kernels for 36%

profile of v3, /device:TPU:0, one launch (start us, length us, event | category | flops | bytes accessed | tf_op | source)
XLA Modules:
  0.0 749.4 jit_solution(11244587900080896468)
XLA Ops:
  2.8 2.4 concatenate.28
  5.4 5.1 collective-permute-start.10
  12.1 3.4 collective-permute-done.10.rest_3_.rest_2_
  15.5 4.6 collective-permute-done.8.rest_1_.rest_0_
  20.1 6.0 collective-permute-done.9.rest_2_.rest_1_
  26.8 24.1 %stack.37 = bf16[4,240,384]{2,1,0:T(8,128)(2,1)} custom-call(s32[3]{0:T(128)} %pad_add_fusion.sc, bf16[240,384]{1,0:T(8,128)(2,1)} %copy-done.25, bf16[240,384]{1,0:T(8,128)(2,1)} %copy-done.23, bf16[240,384]{1,0:T(8,128)(2,1)} %copy-done.24, bf16[240,384]{1,0:T(8,128)(2,1)} %copy-done.22), custom_call_target="tpu_custom_call" | custom-call | tf_op jit(solution)/shard_map/stack/pallas_call | solution.py:626
  52.5 29.8 %pick.1 = (bf16[240,640]{1,0:T(8,128)(2,1)}, bf16[480,640]{1,0:T(8,128)(2,1)}) custom-call(s32[3]{0:T(128)} %pad_add_fusion.sc, bf16[240,2560]{1,0:T(8,128)(2,1)} %gate.1, bf16[240,2560]{1,0:T(8,128)(2,1)} %up.1, bf16[960,640]{1,0:T(8,128)(2,1)} %bitcast.130, bf16[240,384]{1,0:T(8,128)(2,1)} %copy-done.23, bf16[240,384]{1,0:T(8,128)(2,1)} %copy-done.24, ...), custom_call_target="tpu_custom_call" | custom-call | tf_op jit(solution)/shard_map/pick/pallas_call | solution.py:605
  84.4 3.8 collective-permute-start.1
  88.2 23.1 %collective-permute-done.1 = bf16[2,240]{1,0:T(2,128)(2,1)S(1)} collective-permute-done((bf16[2,240]{1,0:T(2,128)(2,1)S(1)}, bf16[2,240]{1,0:T(2,128)(2,1)S(1)}, u32[]{:S(2)}, u32[]{:S(2)}) %collective-permute-start.1) | collective-permute-done | bytes 992 | tf_op jit(solution)/shard_map/ppermute | solution.py:650
  111.3 5.2 collective-permute-done.2
  116.5 5.4 collective-permute-done.4
  121.9 4.5 collective-permute-done.5
  126.4 3.6 collective-permute-done.6
  135.0 3.3 collective-permute-start.20
  138.3 14.2 %collective-permute-done.19.rest_2_ = bf16[240,640]{1,0:T(8,128)(2,1)S(1)} collective-permute-done((bf16[240,640]{1,0:T(8,128)(2,1)}, bf16[240,640]{1,0:T(8,128)(2,1)S(1)}, u32[]{:S(2)}, u32[]{:S(2)}) %collective-permute-start.19) | collective-permute-done | bytes 307232 | tf_op jit(solution)/shard_map/ppermute | solution.py:650
  152.6 20.2 %collective-permute-start.32 = (bf16[480,640]{1,0:T(8,128)(2,1)}, bf16[480,640]{1,0:T(8,128)(2,1)}, u32[]{:S(2)}, u32[]{:S(2)}) collective-permute-start(bf16[480,640]{1,0:T(8,128)(2,1)} %get-tuple-element.84.rest_0_), channel_id=1, source_target_pairs={{0,3},{1,0},{2,1},{3,2},{4,7},{5,4},{6,5},{7,6},{8,11},{9,8},{10,9... | collective-permute-start | bytes 1843208 | tf_op jit(solution)/shard_map/ppermute | solution.py:650
  174.9 39.0 %stack.38 = bf16[4,240,640]{2,1,0:T(8,128)(2,1)} custom-call(s32[3]{0:T(128)} %pad_add_fusion.sc, bf16[240,640]{1,0:T(8,128)(2,1)} %get-tuple-element.79.rest_0_, bf16[240,640]{1,0:T(8,128)(2,1)} %copy-done.36, bf16[240,640]{1,0:T(8,128)(2,1)} %copy-done.44, bf16[240,640]{1,0:T(8,128)(2,1)} %copy-done.45), custom_call_target="tpu_custom_call" | custom-call | tf_op jit(solution)/shard_map/stack/pallas_call | solution.py:626
  217.7 76.2 %stack.39.rest_16_ = bf16[4,480,640]{2,1,0:T(8,128)(2,1)} custom-call(s32[3]{0:T(128)} %pad_add_fusion.sc, bf16[480,640]{1,0:T(8,128)(2,1)} %get-tuple-element.84.rest_0_, bf16[480,640]{1,0:T(8,128)(2,1)} %copy-done.28, bf16[480,640]{1,0:T(8,128)(2,1)} %collective-permute-done.31.rest_2_, bf16[480,640]{1,0:T(8,128)(2,1)} %collective-permute-done.32.rest_3_), custom_call_target="tpu_custom_call" | custom-call | tf_op jit(solution)/shard_map/stack/pallas_call | solution.py:626
  297.1 6.8 pre.1
  303.9 2.6 collective-permute-start.21
  306.6 7.7 %collective-permute-done.21.kv0 = bf16[640,256]{1,0:T(8,128)(2,1)S(1)} collective-permute-done((bf16[640,256]{1,0:T(8,128)(2,1)}, bf16[640,256]{1,0:T(8,128)(2,1)S(1)}, u32[]{:S(2)}, u32[]{:S(2)}) %collective-permute-start.21) | collective-permute-done | bytes 327712 | tf_op jit(solution)/shard_map/ppermute | solution.py:690
  316.0 8.2 %collective-permute-done.25.rest_11_ = bf16[960,640]{1,0:T(8,128)(2,1)} collective-permute-done((bf16[960,640]{1,0:T(8,128)(2,1)}, bf16[960,640]{1,0:T(8,128)(2,1)}, u32[]{:S(2)}, u32[]{:S(2)}) %collective-permute-start.25) | collective-permute-done | bytes 1228832 | tf_op jit(solution)/shard_map/ppermute | solution.py:645
  326.3 12.3 %attend.2 = (bf16[960,256]{1,0:T(8,128)(2,1)}, f32[15,256]{1,0:T(8,128)}) custom-call(bf16[960,256]{1,0:T(8,128)(2,1)} %get-tuple-element.80.q_ref, bf16[640,256]{1,0:T(8,128)(2,1)} %copy-done.9, bf16[640,256]{1,0:T(8,128)(2,1)} %copy-done.20, bf16[640,256]{1,0:T(8,128)(2,1)} %get-tuple-element.81.kv2, s32[768,1]{1,0:T(8,128)} %broadcast_in_dim.103.sk_ref, ...), custom_call_target="tpu_custom_call" | custom-call | tf_op jit(solution)/shard_map/attend/pallas_call | solution.py:163
  340.1 20.3 %post.2 = (bf16[256,960]{1,0:T(8,128)(2,1)}, f32[256,960]{1,0:T(8,128)}, bf16[256,960]{1,0:T(8,128)(2,1)}, bf16[256,2560]{1,0:T(8,128)(2,1)}, bf16[256,2560]{1,0...) custom-call(s32[3]{0:T(128)} %pad_add_fusion.sc, ...), custom_call_target="tpu_custom_call" | custom-call | tf_op jit(solution)/shard_map/post/pallas_call | solution.py:295
  360.3 2.5 collective-permute-start.34
  363.5 7.7 %collective-permute-done.34.kv0 = bf16[640,256]{1,0:T(8,128)(2,1)S(1)} collective-permute-done((bf16[640,256]{1,0:T(8,128)(2,1)}, bf16[640,256]{1,0:T(8,128)(2,1)S(1)}, u32[]{:S(2)}, u32[]{:S(2)}) %collective-permute-start.34) | collective-permute-done | bytes 327712 | tf_op jit(solution)/shard_map/ppermute | solution.py:690
  374.8 12.7 %attend.3 = (bf16[960,256]{1,0:T(8,128)(2,1)}, f32[15,256]{1,0:T(8,128)}) custom-call(bf16[960,256]{1,0:T(8,128)(2,1)} %get-tuple-element.85.q_ref, bf16[640,256]{1,0:T(8,128)(2,1)} %copy-done.8, bf16[640,256]{1,0:T(8,128)(2,1)} %copy-done.19, bf16[640,256]{1,0:T(8,128)(2,1)} %get-tuple-element.86.kv2, s32[768,1]{1,0:T(8,128)} %broadcast_in_dim.103.sk_ref, ...), custom_call_target="tpu_custom_call" | custom-call | tf_op jit(solution)/shard_map/attend/pallas_call | solution.py:163
  387.5 17.7 %post.3 = (bf16[256,960]{1,0:T(8,128)(2,1)}, f32[256,960]{1,0:T(8,128)}, bf16[256,960]{1,0:T(8,128)(2,1)}, bf16[256,2560]{1,0:T(8,128)(2,1)}, bf16[256,2560]{1,0...) custom-call(s32[3]{0:T(128)} %pad_add_fusion.sc, bf16[960,256]{1,0:T(8,128)(2,1)} %get-tuple-element.87.ot_ref, ...), custom_call_target="tpu_custom_call" | custom-call | tf_op jit(solution)/shard_map/post/pallas_call | solution.py:295
  406.0 21.7 %back_start.1 = (bf16[256,960]{1,0:T(8,128)(2,1)}, bf16[256,2560]{1,0:T(8,128)(2,1)}, bf16[256,2560]{1,0:T(8,128)(2,1)}, bf16[256,1280]{1,0:T(8,128)(2,1)}, bf16...) custom-call(s32[3]{0:T(128)} %pad_add_fusion.sc, ...), custom_call_target="tpu_custom_call" | custom-call | tf_op jit(solution)/shard_map/back_start/pallas_call | solution.py:446
  427.7 14.6 %attend_back.2 = (bf16[3,256,384]{2,1,0:T(8,128)(2,1)}, f32[640,256]{1,0:T(8,128)}, bf16[640,256]{1,0:T(8,128)(2,1)}, f32[640,256]{1,0:T(8,128)}) custom-call(bf16[960,256]{1,0:T(8,128)(2,1)} %get-tuple-element.85.q_ref, bf16[640,256]{1,0:T(8,128)(2,1)} %copy-done.8, bf16[640,256]{1,0:T(8,128)(2,1)} %copy-done.19, bf16[640,256]{1,0:T(8,128)(2,1)} %get-tuple-element.86.kv2, ...), custom_call_target="tpu_custom_call" | custom-call | tf_op jit(solution)/shard_map/attend_back/pallas_call | solution.py:213
  446.7 10.4 %collective-permute-done.39.rest_22_ = bf16[640,256]{1,0:T(8,128)(2,1)S(1)} collective-permute-done((bf16[640,256]{1,0:T(8,128)(2,1)S(1)}, bf16[640,256]{1,0:T(8,128)(2,1)S(1)}, u32[]{:S(2)}, u32[]{:S(2)}) %collective-permute-start.39) | collective-permute-done | bytes 327712 | tf_op jit(solution)/shard_map/ppermute | solution.py:700
  457.8 22.0 %back_join.1 = (bf16[256,384]{1,0:T(8,128)(2,1)}, bf16[256,384]{1,0:T(8,128)(2,1)}, f32[1,960]{1,0:T(1,128)}, bf16[256,960]{1,0:T(8,128)(2,1)}, bf16[256,2560]{1...) custom-call(s32[3]{0:T(128)} %pad_add_fusion.sc, ...), custom_call_target="tpu_custom_call" | custom-call | tf_op jit(solution)/shard_map/back_join/pallas_call | solution.py:446
  480.9 3.1 collective-permute-done.41.rest_3_
  487.3 7.9 %grad_ffn.2.rest_8_ = bf16[2,960,640]{2,1,0:T(8,128)(2,1)} custom-call(s32[3]{0:T(128)} %pad_add_fusion.sc, bf16[256,960]{1,0:T(8,128)(2,1)} %get-tuple-element.108.rest_0_, bf16[256,960]{1,0:T(8,128)(2,1)} %get-tuple-element.109.rest_1_, bf16[256,960]{1,0:T(8,128)(2,1)} %copy-done.15, bf16[256,960]{1,0:T(8,128)(2,1)} %copy-done.14, ...), custom_call_target="tpu_custom_call" | custom-call | tf_op jit(solution)/shard_map/grad_ffn/pallas_call | solution.py:484
  496.1 7.5 grad_down.1.rest_8_
  503.5 4.1 dynamic-slice_bitcast_fusion.2
  507.6 1.9 collective-permute-start.87
  512.1 7.9 %grad_ffn.3.rest_0_ = bf16[2,960,640]{2,1,0:T(8,128)(2,1)} custom-call(s32[3]{0:T(128)} %pad_add_fusion.sc, bf16[256,960]{1,0:T(8,128)(2,1)} %get-tuple-element.108.rest_0_, bf16[256,960]{1,0:T(8,128)(2,1)} %get-tuple-element.109.rest_1_, bf16[256,960]{1,0:T(8,128)(2,1)} %copy-done.15, bf16[256,960]{1,0:T(8,128)(2,1)} %copy-done.14, ...), custom_call_target="tpu_custom_call" | custom-call | tf_op jit(solution)/shard_map/grad_ffn/pallas_call | solution.py:484
  520.1 14.7 %attend_back.3 = (bf16[3,256,384]{2,1,0:T(8,128)(2,1)}, f32[640,256]{1,0:T(8,128)}, bf16[640,256]{1,0:T(8,128)(2,1)}, f32[640,256]{1,0:T(8,128)}) custom-call(bf16[960,256]{1,0:T(8,128)(2,1)} %get-tuple-element.80.q_ref, bf16[640,256]{1,0:T(8,128)(2,1)} %copy-done.9, bf16[640,256]{1,0:T(8,128)(2,1)} %copy-done.20, bf16[640,256]{1,0:T(8,128)(2,1)} %get-tuple-element.81.kv2, ...), custom_call_target="tpu_custom_call" | custom-call | tf_op jit(solution)/shard_map/attend_back/pallas_call | solution.py:213
  534.8 3.6 collective-permute-start.48
  539.8 2.0 fusion.7
  543.2 2.2 broadcast_select_fusion.1
  545.4 16.3 %collective-permute-done.49.rest_12_ = bf16[640,256]{1,0:T(8,128)(2,1)} collective-permute-done((bf16[640,256]{1,0:T(8,128)(2,1)}, bf16[640,256]{1,0:T(8,128)(2,1)}, u32[]{:S(2)}, u32[]{:S(2)}) %collective-permute-start.49) | collective-permute-done | bytes 327712 | tf_op jit(solution)/shard_map/ppermute | solution.py:700
  561.7 6.5 back_end.1
  568.3 2.5 broadcast_select_fusion
  573.8 2.3 fusion.2
  579.4 9.4 %grad_attention.1 = (bf16[2,960,384]{2,1,0:T(8,128)(2,1)}, bf16[2,960,384]{2,1,0:T(8,128)(2,1)}) custom-call(s32[3]{0:T(128)} %pad_add_fusion.sc, bf16[256,960]{1,0:T(8,128)(2,1)} %get-tuple-element.129.rest_0_, bf16[256,960]{1,0:T(8,128)(2,1)} %get-tuple-element.130.rest_1_, bf16[256,960]{1,0:T(8,128)(2,1)} %collective-permute-done.57.rest_2_, ...), custom_call_target="tpu_custom_call" | custom-call | tf_op jit(solution)/shard_map/grad_attention/pallas_call | solution.py:543
  592.2 5.2 collective-permute-start.36
  598.3 23.3 %collective-permute-done.91 = bf16[2,120,640]{2,1,0:T(8,128)(2,1)S(1)} collective-permute-done((bf16[2,120,640]{2,1,0:T(8,128)(2,1)}, bf16[2,120,640]{2,1,0:T(8,128)(2,1)S(1)}, u32[]{:S(2)}, u32[]{:S(2)}) %collective-permute-start.91) | collective-permute-done | bytes 307232 | tf_op jit(solution)/shard_map/ppermute | solution.py:645
  629.5 3.3 collective-permute-start.56
  642.4 23.8 %collective-permute-done.94 = bf16[120,640]{1,0:T(8,128)(2,1)S(1)} collective-permute-done((bf16[120,640]{1,0:T(8,128)(2,1)S(1)}, bf16[120,640]{1,0:T(8,128)(2,1)S(1)}, u32[]{:S(2)}, u32[]{:S(2)}) %collective-permute-start.94) | collective-permute-done | bytes 153632 | tf_op jit(solution)/shard_map/ppermute | solution.py:645
  667.9 2.4 collective-permute-start.65
  670.3 2.0 collective-permute-start.66
  672.2 2.8 collective-permute-start.67
  677.3 8.3 %collective-permute-start.77 = (bf16[240,640]{1,0:T(8,128)(2,1)S(1)}, bf16[240,640]{1,0:T(8,128)(2,1)S(1)}, u32[]{:S(2)}, u32[]{:S(2)}) collective-permute-start(bf16[240,640]{1,0:T(8,128)(2,1)S(1)} %get-tuple-element.189), channel_id=1, source_target_pairs={{0,1},{1,2},{2,3},{3,0},{4,5},{5,6},{6,7},{7,4},{8,9},{9,10},{10,1... | collective-permute-start | bytes 921608 | tf_op jit(solution)/shard_map/ppermute | solution.py:650
  685.6 1.9 collective-permute-start.78
  687.5 4.9 collective-permute-start.79
  694.5 14.0 %collective-permute-done.78 = bf16[240,640]{1,0:T(8,128)(2,1)S(1)} collective-permute-done((bf16[240,640]{1,0:T(8,128)(2,1)S(1)}, bf16[240,640]{1,0:T(8,128)(2,1)S(1)}, u32[]{:S(2)}, u32[]{:S(2)}) %collective-permute-start.78) | collective-permute-done | bytes 307232 | tf_op jit(solution)/shard_map/ppermute | solution.py:650
  708.5 1.9 collective-permute-start.70
  710.3 4.6 collective-permute-done.79
  721.2 4.1 collective-permute-done.80.rest_1_
  725.9 5.8 collective-permute-done.82.rest_3_
  734.4 3.4 lay.2
  743.2 4.2 lay.3
  (358 shorter events, 98.6 us)
Async XLA Ops:
  5.4 10.1 %collective-permute-start.10 = (bf16[240,384]{1,0:T(8,128)(2,1)S(1)}, bf16[240,384]{1,0:T(8,128)(2,1)S(1)}, u32[]{:S(2)}, u32[]{:S(2)}) collective-permute-start(bf16[240,384]{1,0:T(8,128)(2,1)S(1)} %pad_dynamic-slice_fusion.rest_0_), channel_id=1, source_target_pairs={{0,3},{1,0},{2,1},{3,2},{4,7},{5,4},{6,5},{7,6},{8,11},{9,8},{10,9... | collective-permute-start | bytes 552968 | tf_op jit(solution)/shard_map/ppermute | solution.py:650
  10.5 15.6 %collective-permute-start.9 = (bf16[240,384]{1,0:T(8,128)(2,1)S(1)}, bf16[240,384]{1,0:T(8,128)(2,1)S(1)}, u32[]{:S(2)}, u32[]{:S(2)}) collective-permute-start(bf16[240,384]{1,0:T(8,128)(2,1)S(1)} %pad_dynamic-slice_fusion.rest_0_), channel_id=1, source_target_pairs={{0,2},{1,3},{2,0},{3,1},{4,6},{5,7},{6,4},{7,5},{8,10},{9,11},{10,... | collective-permute-start | bytes 552968 | tf_op jit(solution)/shard_map/ppermute | solution.py:650
  50.9 122.4 %collective-permute-start.11 = (bf16[960,384]{1,0:T(8,128)(2,1)}, bf16[960,384]{1,0:T(8,128)(2,1)S(1)}, u32[]{:S(2)}, u32[]{:S(2)}) collective-permute-start(bf16[960,384]{1,0:T(8,128)(2,1)} %bitcast.112), channel_id=1, source_target_pairs={{0,8},{4,20},{8,0},{12,28},{16,24},{20,4},{24,16},{28,12},{1,9},{5... | collective-permute-start | bytes 2211848 | tf_op jit(solution)/shard_map/ppermute | solution.py:645
  82.3 52.7 %collective-permute-start.18 = (bf16[240,640]{1,0:T(8,128)(2,1)}, bf16[240,640]{1,0:T(8,128)(2,1)S(1)}, u32[]{:S(2)}, u32[]{:S(2)}) collective-permute-start(bf16[240,640]{1,0:T(8,128)(2,1)} %get-tuple-element.79.rest_0_), channel_id=1, source_target_pairs={{0,1},{1,2},{2,3},{3,0},{4,5},{5,6},{6,7},{7,4},{8,9},{9,10},{10,1... | collective-permute-start | bytes 921608 | tf_op jit(solution)/shard_map/ppermute | solution.py:650
  82.4 131.5 %collective-permute-start.30 = (bf16[480,640]{1,0:T(8,128)(2,1)}, bf16[480,640]{1,0:T(8,128)(2,1)S(1)}, u32[]{:S(2)}, u32[]{:S(2)}) collective-permute-start(bf16[480,640]{1,0:T(8,128)(2,1)} %get-tuple-element.84.rest_0_), channel_id=1, source_target_pairs={{0,1},{1,2},{2,3},{3,0},{4,5},{5,6},{6,7},{7,4},{8,9},{9,10},{10,1... | collective-permute-start | bytes 1843208 | tf_op jit(solution)/shard_map/ppermute | solution.py:650
  82.6 90.1 %collective-permute-start = (bf16[960,256]{1,0:T(8,128)(2,1)}, bf16[960,256]{1,0:T(8,128)(2,1)S(1)}, u32[]{:S(2)}, u32[]{:S(2)}) collective-permute-start(bf16[960,256]{1,0:T(8,128)(2,1)} %bitcast.4), channel_id=1, source_target_pairs={{0,0},{1,4},{2,1},{3,5},{4,2},{5,6},{6,3},{7,7},{8,8},{9,12},{10,9... | collective-permute-start | bytes 1474568 | tf_op jit(solution)/shard_map/ppermute | solution.py:661
  84.4 27.0 %collective-permute-start.1 = (bf16[2,240]{1,0:T(2,128)(2,1)S(1)}, bf16[2,240]{1,0:T(2,128)(2,1)S(1)}, u32[]{:S(2)}, u32[]{:S(2)}) collective-permute-start(bf16[2,240]{1,0:T(2,128)(2,1)S(1)} %pad_maximum_fusion.6), channel_id=1, source_target_pairs={{0,1},{1,2},{2,3},{3,0},{4,5},{5,6},{6,7},{7,4},{8,9},{9,10},{10,1... | collective-permute-start | bytes 2888 | tf_op jit(solution)/shard_map/ppermute | solution.py:650
  134.7 17.9 %collective-permute-start.19 = (bf16[240,640]{1,0:T(8,128)(2,1)}, bf16[240,640]{1,0:T(8,128)(2,1)S(1)}, u32[]{:S(2)}, u32[]{:S(2)}) collective-permute-start(bf16[240,640]{1,0:T(8,128)(2,1)} %get-tuple-element.79.rest_0_), channel_id=1, source_target_pairs={{0,2},{1,3},{2,0},{3,1},{4,6},{5,7},{6,4},{7,5},{8,10},{9,11},{10,... | collective-permute-start | bytes 921608 | tf_op jit(solution)/shard_map/ppermute | solution.py:650
  135.0 17.5 %collective-permute-start.20 = (bf16[240,640]{1,0:T(8,128)(2,1)}, bf16[240,640]{1,0:T(8,128)(2,1)S(1)}, u32[]{:S(2)}, u32[]{:S(2)}) collective-permute-start(bf16[240,640]{1,0:T(8,128)(2,1)} %get-tuple-element.79.rest_0_), channel_id=1, source_target_pairs={{0,3},{1,0},{2,1},{3,2},{4,7},{5,4},{6,5},{7,6},{8,11},{9,8},{10,9... | collective-permute-start | bytes 921608 | tf_op jit(solution)/shard_map/ppermute | solution.py:650
  152.5 63.2 %collective-permute-start.31 = (bf16[480,640]{1,0:T(8,128)(2,1)}, bf16[480,640]{1,0:T(8,128)(2,1)}, u32[]{:S(2)}, u32[]{:S(2)}) collective-permute-start(bf16[480,640]{1,0:T(8,128)(2,1)} %get-tuple-element.84.rest_0_), channel_id=1, source_target_pairs={{0,2},{1,3},{2,0},{3,1},{4,6},{5,7},{6,4},{7,5},{8,10},{9,11},{10,... | collective-permute-start | bytes 1843208 | tf_op jit(solution)/shard_map/ppermute | solution.py:650
  152.6 63.3 %collective-permute-start.32 = (bf16[480,640]{1,0:T(8,128)(2,1)}, bf16[480,640]{1,0:T(8,128)(2,1)}, u32[]{:S(2)}, u32[]{:S(2)}) collective-permute-start(bf16[480,640]{1,0:T(8,128)(2,1)} %get-tuple-element.84.rest_0_), channel_id=1, source_target_pairs={{0,3},{1,0},{2,1},{3,2},{4,7},{5,4},{6,5},{7,6},{8,11},{9,8},{10,9... | collective-permute-start | bytes 1843208 | tf_op jit(solution)/shard_map/ppermute | solution.py:650
  172.8 43.6 %collective-permute-start.12 = (bf16[960,384]{1,0:T(8,128)(2,1)S(1)}, bf16[960,384]{1,0:T(8,128)(2,1)}, u32[]{:S(2)}, u32[]{:S(2)}) collective-permute-start(bf16[960,384]{1,0:T(8,128)(2,1)S(1)} %bitcast.119), channel_id=1, source_target_pairs={{0,16},{4,12},{8,24},{12,4},{16,0},{20,28},{24,8},{28,20},{1,17},{... | collective-permute-start | bytes 2211848 | tf_op jit(solution)/shard_map/ppermute | solution.py:645
  173.4 43.1 %collective-permute-start.13 = (bf16[960,384]{1,0:T(8,128)(2,1)S(1)}, bf16[960,384]{1,0:T(8,128)(2,1)}, u32[]{:S(2)}, u32[]{:S(2)}) collective-permute-start(bf16[960,384]{1,0:T(8,128)(2,1)S(1)} %collective-permute-done.11.rest_1_), channel_id=1, source_target_pairs={{0,16},{4,12},{8,24},{12,4},{16,0},{20,28},{24,8},{28,20},{1,17},{... | collective-permute-start | bytes 2211848 | tf_op jit(solution)/shard_map/ppermute | solution.py:645
  213.9 81.0 %collective-permute-start.23 = (bf16[960,640]{1,0:T(8,128)(2,1)}, bf16[960,640]{1,0:T(8,128)(2,1)}, u32[]{:S(2)}, u32[]{:S(2)}) collective-permute-start(bf16[960,640]{1,0:T(8,128)(2,1)} %bitcast.16.rest_8_), channel_id=1, source_target_pairs={{0,8},{4,20},{8,0},{12,28},{16,24},{20,4},{24,16},{28,12},{1,9},{5... | collective-permute-start | bytes 3686408 | tf_op jit(solution)/shard_map/ppermute | solution.py:645
  215.8 78.2 %collective-permute-start.14 = (bf16[960,384]{1,0:T(8,128)(2,1)S(1)}, bf16[960,384]{1,0:T(8,128)(2,1)S(1)}, u32[]{:S(2)}, u32[]{:S(2)}) collective-permute-start(bf16[960,384]{1,0:T(8,128)(2,1)S(1)} %bitcast.120), channel_id=1, source_target_pairs={{0,4},{4,0},{8,12},{12,8},{16,20},{20,16},{24,28},{28,24},{1,5},{5... | collective-permute-start | bytes 2211848 | tf_op jit(solution)/shard_map/ppermute | solution.py:645
  215.9 79.0 %collective-permute-start.15 = (bf16[960,384]{1,0:T(8,128)(2,1)S(1)}, bf16[960,384]{1,0:T(8,128)(2,1)}, u32[]{:S(2)}, u32[]{:S(2)}) collective-permute-start(bf16[960,384]{1,0:T(8,128)(2,1)S(1)} %collective-permute-done.11.rest_1_), channel_id=1, source_target_pairs={{0,4},{4,0},{8,12},{12,8},{16,20},{20,16},{24,28},{28,24},{1,5},{5... | collective-permute-start | bytes 2211848 | tf_op jit(solution)/shard_map/ppermute | solution.py:645
  216.4 80.8 %collective-permute-start.16 = (bf16[960,384]{1,0:T(8,128)(2,1)}, bf16[960,384]{1,0:T(8,128)(2,1)}, u32[]{:S(2)}, u32[]{:S(2)}) collective-permute-start(bf16[960,384]{1,0:T(8,128)(2,1)} %collective-permute-done.12.rest_2_), channel_id=1, source_target_pairs={{0,4},{4,0},{8,12},{12,8},{16,20},{20,16},{24,28},{28,24},{1,5},{5... | collective-permute-start | bytes 2211848 | tf_op jit(solution)/shard_map/ppermute | solution.py:645
  216.4 80.7 %collective-permute-start.17 = (bf16[960,384]{1,0:T(8,128)(2,1)}, bf16[960,384]{1,0:T(8,128)(2,1)}, u32[]{:S(2)}, u32[]{:S(2)}) collective-permute-start(bf16[960,384]{1,0:T(8,128)(2,1)} %collective-permute-done.13.rest_3_), channel_id=1, source_target_pairs={{0,4},{4,0},{8,12},{12,8},{16,20},{20,16},{24,28},{28,24},{1,5},{5... | collective-permute-start | bytes 2211848 | tf_op jit(solution)/shard_map/ppermute | solution.py:645
  293.9 22.0 %collective-permute-start.24 = (bf16[960,640]{1,0:T(8,128)(2,1)}, bf16[960,640]{1,0:T(8,128)(2,1)}, u32[]{:S(2)}, u32[]{:S(2)}) collective-permute-start(bf16[960,640]{1,0:T(8,128)(2,1)} %bitcast.16.rest_8_), channel_id=1, source_target_pairs={{0,16},{4,12},{8,24},{12,4},{16,0},{20,28},{24,8},{28,20},{1,17},{... | collective-permute-start | bytes 3686408 | tf_op jit(solution)/shard_map/ppermute | solution.py:645
  294.9 43.8 %collective-permute-start.33 = (bf16[4,480,640]{2,1,0:T(8,128)(2,1)}, bf16[4,480,640]{2,1,0:T(8,128)(2,1)S(1)}, u32[]{:S(2)}, u32[]{:S(2)}) collective-permute-start(bf16[4,480,640]{2,1,0:T(8,128)(2,1)} %stack.39.rest_16_), channel_id=1, source_target_pairs={{0,4},{4,0},{8,12},{12,8},{16,20},{20,16},{24,28},{28,24},{1,5},{5... | collective-permute-start | bytes 7372808 | tf_op jit(solution)/shard_map/ppermute | solution.py:645
  294.9 29.3 %collective-permute-start.25 = (bf16[960,640]{1,0:T(8,128)(2,1)}, bf16[960,640]{1,0:T(8,128)(2,1)}, u32[]{:S(2)}, u32[]{:S(2)}) collective-permute-start(bf16[960,640]{1,0:T(8,128)(2,1)} %collective-permute-done.23.rest_9_), channel_id=1, source_target_pairs={{0,16},{4,12},{8,24},{12,4},{16,0},{20,28},{24,8},{28,20},{1,17},{... | collective-permute-start | bytes 3686408 | tf_op jit(solution)/shard_map/ppermute | solution.py:645
  303.9 10.3 %collective-permute-start.21 = (bf16[640,256]{1,0:T(8,128)(2,1)}, bf16[640,256]{1,0:T(8,128)(2,1)S(1)}, u32[]{:S(2)}, u32[]{:S(2)}) collective-permute-start(bf16[640,256]{1,0:T(8,128)(2,1)} %get-tuple-element.81.kv2), channel_id=1, source_target_pairs={{0,1},{2,3},{4,5},{6,7},{8,9},{10,11},{12,13},{14,15},{16,17},{18,... | collective-permute-start | bytes 983048 | tf_op jit(solution)/shard_map/ppermute | solution.py:690
  315.4 23.2 %collective-permute-start.26 = (bf16[960,640]{1,0:T(8,128)(2,1)}, bf16[960,640]{1,0:T(8,128)(2,1)}, u32[]{:S(2)}, u32[]{:S(2)}) collective-permute-start(bf16[960,640]{1,0:T(8,128)(2,1)} %bitcast.16.rest_8_), channel_id=1, source_target_pairs={{0,4},{4,0},{8,12},{12,8},{16,20},{20,16},{24,28},{28,24},{1,5},{5... | collective-permute-start | bytes 3686408 | tf_op jit(solution)/shard_map/ppermute | solution.py:645
  315.9 22.7 %collective-permute-start.27 = (bf16[960,640]{1,0:T(8,128)(2,1)}, bf16[960,640]{1,0:T(8,128)(2,1)}, u32[]{:S(2)}, u32[]{:S(2)}) collective-permute-start(bf16[960,640]{1,0:T(8,128)(2,1)} %collective-permute-done.23.rest_9_), channel_id=1, source_target_pairs={{0,4},{4,0},{8,12},{12,8},{16,20},{20,16},{24,28},{28,24},{1,5},{5... | collective-permute-start | bytes 3686408 | tf_op jit(solution)/shard_map/ppermute | solution.py:645
  324.2 14.4 %collective-permute-start.28 = (bf16[960,640]{1,0:T(8,128)(2,1)}, bf16[960,640]{1,0:T(8,128)(2,1)}, u32[]{:S(2)}, u32[]{:S(2)}) collective-permute-start(bf16[960,640]{1,0:T(8,128)(2,1)} %collective-permute-done.24.rest_10_), channel_id=1, source_target_pairs={{0,4},{4,0},{8,12},{12,8},{16,20},{20,16},{24,28},{28,24},{1,5},{5... | collective-permute-start | bytes 3686408 | tf_op jit(solution)/shard_map/ppermute | solution.py:645
  324.2 14.4 %collective-permute-start.29 = (bf16[960,640]{1,0:T(8,128)(2,1)}, bf16[960,640]{1,0:T(8,128)(2,1)}, u32[]{:S(2)}, u32[]{:S(2)}) collective-permute-start(bf16[960,640]{1,0:T(8,128)(2,1)} %collective-permute-done.25.rest_11_), channel_id=1, source_target_pairs={{0,4},{4,0},{8,12},{12,8},{16,20},{20,16},{24,28},{28,24},{1,5},{5... | collective-permute-start | bytes 3686408 | tf_op jit(solution)/shard_map/ppermute | solution.py:645
  360.3 10.9 %collective-permute-start.34 = (bf16[640,256]{1,0:T(8,128)(2,1)}, bf16[640,256]{1,0:T(8,128)(2,1)S(1)}, u32[]{:S(2)}, u32[]{:S(2)}) collective-permute-start(bf16[640,256]{1,0:T(8,128)(2,1)} %get-tuple-element.86.kv2), channel_id=1, source_target_pairs={{0,1},{2,3},{4,5},{6,7},{8,9},{10,11},{12,13},{14,15},{16,17},{18,... | collective-permute-start | bytes 983048 | tf_op jit(solution)/shard_map/ppermute | solution.py:690
  362.8 42.4 %collective-permute-start.37 = (bf16[960,256]{1,0:T(8,128)(2,1)S(1)}, bf16[960,256]{1,0:T(8,128)(2,1)S(1)}, u32[]{:S(2)}, u32[]{:S(2)}) collective-permute-start(bf16[960,256]{1,0:T(8,128)(2,1)S(1)} %bitcast.153), channel_id=1, source_target_pairs={{0,0},{1,4},{2,1},{3,5},{4,2},{5,6},{6,3},{7,7},{8,8},{9,12},{10,9... | collective-permute-start | bytes 1474568 | tf_op jit(solution)/shard_map/ppermute | solution.py:661
  442.3 43.1 %collective-permute-start.42 = (bf16[256,2560]{1,0:T(8,128)(2,1)}, bf16[256,2560]{1,0:T(8,128)(2,1)S(1)}, u32[]{:S(2)}, u32[]{:S(2)}) collective-permute-start(bf16[256,2560]{1,0:T(8,128)(2,1)} %get-tuple-element.112), channel_id=1, source_target_pairs={{0,4},{4,0},{8,12},{12,8},{16,20},{20,16},{24,28},{28,24},{1,5},{5... | collective-permute-start | bytes 3932168 | tf_op jit(solution)/shard_map/ppermute | solution.py:645
  445.4 11.7 %collective-permute-start.39 = (bf16[640,256]{1,0:T(8,128)(2,1)S(1)}, bf16[640,256]{1,0:T(8,128)(2,1)S(1)}, u32[]{:S(2)}, u32[]{:S(2)}) collective-permute-start(bf16[640,256]{1,0:T(8,128)(2,1)S(1)} %fusion.6), channel_id=1, source_target_pairs={{1,0},{3,2},{5,4},{7,6},{9,8},{11,10},{13,12},{15,14},{17,16},{19,... | collective-permute-start | bytes 983048 | tf_op jit(solution)/shard_map/ppermute | solution.py:700
  480.5 14.7 %collective-permute-start.46 = (bf16[256,1280]{1,0:T(8,128)(2,1)}, bf16[256,1280]{1,0:T(8,128)(2,1)}, u32[]{:S(2)}, u32[]{:S(2)}) collective-permute-start(bf16[256,1280]{1,0:T(8,128)(2,1)} %get-tuple-element.118), channel_id=1, source_target_pairs={{0,4},{4,0},{8,12},{12,8},{16,20},{20,16},{24,28},{28,24},{1,5},{5... | collective-permute-start | bytes 1966088 | tf_op jit(solution)/shard_map/ppermute | solution.py:645
  484.1 11.2 %collective-permute-start.47 = (bf16[256,1280]{1,0:T(8,128)(2,1)}, bf16[256,1280]{1,0:T(8,128)(2,1)S(1)}, u32[]{:S(2)}, u32[]{:S(2)}) collective-permute-start(bf16[256,1280]{1,0:T(8,128)(2,1)} %get-tuple-element.119), channel_id=1, source_target_pairs={{0,4},{4,0},{8,12},{12,8},{16,20},{20,16},{24,28},{28,24},{1,5},{5... | collective-permute-start | bytes 1966088 | tf_op jit(solution)/shard_map/ppermute | solution.py:645
  507.6 64.5 %collective-permute-start.87 = (bf16[960,640]{1,0:T(8,128)(2,1)}, bf16[960,640]{1,0:T(8,128)(2,1)S(1)}, u32[]{:S(2)}, u32[]{:S(2)}) collective-permute-start(bf16[960,640]{1,0:T(8,128)(2,1)} %get-tuple-element.182), channel_id=1, source_target_pairs={{0,1},{3,0},{5,6},{6,7},{8,9},{11,8},{13,14},{14,15},{16,17},{19,1... | collective-permute-start | bytes 3686408 | tf_op jit(solution)/shard_map/ppermute | solution.py:756
  509.5 62.7 %collective-permute-start.88 = (bf16[960,640]{1,0:T(8,128)(2,1)}, bf16[960,640]{1,0:T(8,128)(2,1)}, u32[]{:S(2)}, u32[]{:S(2)}) collective-permute-start(bf16[960,640]{1,0:T(8,128)(2,1)} %get-tuple-element.184), channel_id=1, source_target_pairs={{2,0},{3,1},{4,6},{5,7},{10,8},{11,9},{12,14},{13,15},{18,16},{19,... | collective-permute-start | bytes 3686408 | tf_op jit(solution)/shard_map/ppermute | solution.py:756
  510.8 62.0 %collective-permute-start.89 = (bf16[960,640]{1,0:T(8,128)(2,1)}, bf16[960,640]{1,0:T(8,128)(2,1)}, u32[]{:S(2)}, u32[]{:S(2)}) collective-permute-start(bf16[960,640]{1,0:T(8,128)(2,1)} %get-tuple-element.183), channel_id=1, source_target_pairs={{1,0},{2,1},{4,7},{7,6},{9,8},{10,9},{12,15},{15,14},{17,16},{18,1... | collective-permute-start | bytes 3686408 | tf_op jit(solution)/shard_map/ppermute | solution.py:756
  538.4 32.4 %collective-permute-start.58 = (bf16[256,960]{1,0:T(8,128)(2,1)}, bf16[256,960]{1,0:T(8,128)(2,1)}, u32[]{:S(2)}, u32[]{:S(2)}) collective-permute-start(bf16[256,960]{1,0:T(8,128)(2,1)} %get-tuple-element.130.rest_1_), channel_id=1, source_target_pairs={{0,4},{4,0},{8,12},{12,8},{16,20},{20,16},{24,28},{28,24},{1,5},{5... | collective-permute-start | bytes 1474568 | tf_op jit(solution)/shard_map/ppermute | solution.py:645
  541.9 19.9 %collective-permute-start.49 = (bf16[640,256]{1,0:T(8,128)(2,1)}, bf16[640,256]{1,0:T(8,128)(2,1)}, u32[]{:S(2)}, u32[]{:S(2)}) collective-permute-start(bf16[640,256]{1,0:T(8,128)(2,1)} %fusion.7), channel_id=1, source_target_pairs={{1,0},{3,2},{5,4},{7,6},{9,8},{11,10},{13,12},{15,14},{17,16},{19,... | collective-permute-start | bytes 983048 | tf_op jit(solution)/shard_map/ppermute | solution.py:700
  561.7 14.4 %collective-permute-start.57 = (bf16[256,960]{1,0:T(8,128)(2,1)S(1)}, bf16[256,960]{1,0:T(8,128)(2,1)}, u32[]{:S(2)}, u32[]{:S(2)}) collective-permute-start(bf16[256,960]{1,0:T(8,128)(2,1)S(1)} %copy-done.31), channel_id=1, source_target_pairs={{0,4},{4,0},{8,12},{12,8},{16,20},{20,16},{24,28},{28,24},{1,5},{5... | collective-permute-start | bytes 1474568 | tf_op jit(solution)/shard_map/ppermute | solution.py:645
  572.3 57.2 %collective-permute-start.75 = (bf16[2,960,640]{2,1,0:T(8,128)(2,1)}, bf16[2,960,640]{2,1,0:T(8,128)(2,1)}, u32[]{:S(2)}, u32[]{:S(2)}) collective-permute-start(bf16[2,960,640]{2,1,0:T(8,128)(2,1)} %grad_ffn.2.rest_8_), channel_id=1, source_target_pairs={{0,8},{4,20},{8,0},{12,28},{16,24},{20,4},{24,16},{28,12},{1,9},{5... | collective-permute-start | bytes 7372808 | tf_op jit(solution)/shard_map/ppermute | solution.py:645
  576.1 13.6 %collective-permute-start.90 = (bf16[480,640]{1,0:T(8,128)(2,1)S(1)}, bf16[480,640]{1,0:T(8,128)(2,1)S(1)}, u32[]{:S(2)}, u32[]{:S(2)}) collective-permute-start(bf16[480,640]{1,0:T(8,128)(2,1)S(1)} %dynamic-slice_bitcast_fusion.3), channel_id=1, source_target_pairs={{0,4},{4,0},{8,12},{12,8},{16,20},{20,16},{24,28},{28,24},{1,5},{5... | collective-permute-start | bytes 1843208 | tf_op jit(solution)/shard_map/ppermute | solution.py:645
  588.8 45.7 %collective-permute-start.63 = (bf16[2,960,384]{2,1,0:T(8,128)(2,1)}, bf16[2,960,384]{2,1,0:T(8,128)(2,1)}, u32[]{:S(2)}, u32[]{:S(2)}) collective-permute-start(bf16[2,960,384]{2,1,0:T(8,128)(2,1)} %get-tuple-element.140), channel_id=1, source_target_pairs={{0,8},{4,20},{8,0},{12,28},{16,24},{20,4},{24,16},{28,12},{1,9},{5... | collective-permute-start | bytes 4423688 | tf_op jit(solution)/shard_map/ppermute | solution.py:645
  590.6 30.9 %collective-permute-start.91 = (bf16[2,120,640]{2,1,0:T(8,128)(2,1)}, bf16[2,120,640]{2,1,0:T(8,128)(2,1)S(1)}, u32[]{:S(2)}, u32[]{:S(2)}) collective-permute-start(bf16[2,120,640]{2,1,0:T(8,128)(2,1)} %pad_maximum_fusion.4), channel_id=1, source_target_pairs={{0,8},{4,20},{8,0},{12,28},{16,24},{20,4},{24,16},{28,12},{1,9},{5... | collective-permute-start | bytes 921608 | tf_op jit(solution)/shard_map/ppermute | solution.py:645
  592.2 32.8 %collective-permute-start.36 = (bf16[960,256]{1,0:T(8,128)(2,1)}, bf16[960,256]{1,0:T(8,128)(2,1)}, u32[]{:S(2)}, u32[]{:S(2)}) collective-permute-start(bf16[960,256]{1,0:T(8,128)(2,1)} %get-tuple-element.89), channel_id=1, source_target_pairs={{0,0},{4,1},{1,2},{5,3},{2,4},{6,5},{3,6},{7,7},{8,8},{12,9},{9,10... | collective-permute-start | bytes 1474568 | tf_op jit(solution)/shard_map/ppermute | solution.py:661
  597.5 26.1 %collective-permute-start.52 = (f32[2,960]{1,0:T(2,128)S(1)}, f32[2,960]{1,0:T(2,128)S(1)}, u32[]{:S(2)}, u32[]{:S(2)}) collective-permute-start(f32[2,960]{1,0:T(2,128)S(1)} %fusion.19), channel_id=1, source_target_pairs={{0,8},{4,12},{8,0},{12,4},{16,24},{20,28},{24,16},{28,20},{1,9},{5... | collective-permute-start | bytes 23048 | tf_op jit(solution)/shard_map/ppermute | solution.py:645
  625.1 68.0 %collective-permute-start.50 = (bf16[960,256]{1,0:T(8,128)(2,1)}, bf16[960,256]{1,0:T(8,128)(2,1)S(1)}, u32[]{:S(2)}, u32[]{:S(2)}) collective-permute-start(bf16[960,256]{1,0:T(8,128)(2,1)} %get-tuple-element.124), channel_id=1, source_target_pairs={{0,0},{4,1},{1,2},{5,3},{2,4},{6,5},{3,6},{7,7},{8,8},{12,9},{9,10... | collective-permute-start | bytes 1474568 | tf_op jit(solution)/shard_map/ppermute | solution.py:661
  636.5 35.7 %collective-permute-start.76 = (bf16[960,640]{1,0:T(8,128)(2,1)S(1)}, bf16[960,640]{1,0:T(8,128)(2,1)S(1)}, u32[]{:S(2)}, u32[]{:S(2)}) collective-permute-start(bf16[960,640]{1,0:T(8,128)(2,1)S(1)} %fusion.3), channel_id=1, source_target_pairs={{0,16},{4,12},{8,24},{12,4},{16,0},{20,28},{24,8},{28,20},{1,17},{... | collective-permute-start | bytes 3686408 | tf_op jit(solution)/shard_map/ppermute | solution.py:645
  638.3 28.0 %collective-permute-start.64 = (bf16[960,384]{1,0:T(8,128)(2,1)S(1)}, bf16[960,384]{1,0:T(8,128)(2,1)S(1)}, u32[]{:S(2)}, u32[]{:S(2)}) collective-permute-start(bf16[960,384]{1,0:T(8,128)(2,1)S(1)} %fusion.5), channel_id=1, source_target_pairs={{0,16},{4,12},{8,24},{12,4},{16,0},{20,28},{24,8},{28,20},{1,17},{... | collective-permute-start | bytes 2211848 | tf_op jit(solution)/shard_map/ppermute | solution.py:645
  639.5 26.7 %collective-permute-start.94 = (bf16[120,640]{1,0:T(8,128)(2,1)S(1)}, bf16[120,640]{1,0:T(8,128)(2,1)S(1)}, u32[]{:S(2)}, u32[]{:S(2)}) collective-permute-start(bf16[120,640]{1,0:T(8,128)(2,1)S(1)} %get-tuple-element.181), channel_id=1, source_target_pairs={{0,16},{4,12},{8,24},{12,4},{16,0},{20,28},{24,8},{28,20},{1,17},{... | collective-permute-start | bytes 460808 | tf_op jit(solution)/shard_map/ppermute | solution.py:645
  641.3 24.9 %collective-permute-start.95 = (bf16[120,640]{1,0:T(8,128)(2,1)S(1)}, bf16[120,640]{1,0:T(8,128)(2,1)S(1)}, u32[]{:S(2)}, u32[]{:S(2)}) collective-permute-start(bf16[120,640]{1,0:T(8,128)(2,1)S(1)} %get-tuple-element.181), channel_id=1, source_target_pairs={{0,24},{4,28},{8,16},{12,20},{16,8},{20,12},{24,0},{28,4},{1,25},{... | collective-permute-start | bytes 460808 | tf_op jit(solution)/shard_map/ppermute | solution.py:645
  666.2 48.9 %collective-permute-start.96 = (bf16[4,120,640]{2,1,0:T(8,128)(2,1)S(1)}, bf16[4,120,640]{2,1,0:T(8,128)(2,1)S(1)}, u32[]{:S(2)}, u32[]{:S(2)}) collective-permute-start(bf16[4,120,640]{2,1,0:T(8,128)(2,1)S(1)} %bitcast_dynamic-update-slice_fusion), channel_id=1, source_target_pairs={{0,4},{4,0},{8,12},{12,8},{16,20},{20,16},{24,28},{28,24},{1,5},{5... | collective-permute-start | bytes 1843208 | tf_op jit(solution)/shard_map/ppermute | solution.py:645
  670.3 15.3 %collective-permute-start.66 = (bf16[240,384]{1,0:T(8,128)(2,1)S(1)}, bf16[240,384]{1,0:T(8,128)(2,1)S(1)}, u32[]{:S(2)}, u32[]{:S(2)}) collective-permute-start(bf16[240,384]{1,0:T(8,128)(2,1)S(1)} %get-tuple-element.194), channel_id=1, source_target_pairs={{0,2},{1,3},{2,0},{3,1},{4,6},{5,7},{6,4},{7,5},{8,10},{9,11},{10,... | collective-permute-start | bytes 552968 | tf_op jit(solution)/shard_map/ppermute | solution.py:650
  672.2 15.3 %collective-permute-start.67 = (bf16[240,384]{1,0:T(8,128)(2,1)S(1)}, bf16[240,384]{1,0:T(8,128)(2,1)S(1)}, u32[]{:S(2)}, u32[]{:S(2)}) collective-permute-start(bf16[240,384]{1,0:T(8,128)(2,1)S(1)} %get-tuple-element.193), channel_id=1, source_target_pairs={{0,3},{1,0},{2,1},{3,2},{4,7},{5,4},{6,5},{7,6},{8,11},{9,8},{10,9... | collective-permute-start | bytes 552968 | tf_op jit(solution)/shard_map/ppermute | solution.py:650
  677.3 16.5 %collective-permute-start.77 = (bf16[240,640]{1,0:T(8,128)(2,1)S(1)}, bf16[240,640]{1,0:T(8,128)(2,1)S(1)}, u32[]{:S(2)}, u32[]{:S(2)}) collective-permute-start(bf16[240,640]{1,0:T(8,128)(2,1)S(1)} %get-tuple-element.189), channel_id=1, source_target_pairs={{0,1},{1,2},{2,3},{3,0},{4,5},{5,6},{6,7},{7,4},{8,9},{9,10},{10,1... | collective-permute-start | bytes 921608 | tf_op jit(solution)/shard_map/ppermute | solution.py:650
  685.6 22.9 %collective-permute-start.78 = (bf16[240,640]{1,0:T(8,128)(2,1)S(1)}, bf16[240,640]{1,0:T(8,128)(2,1)S(1)}, u32[]{:S(2)}, u32[]{:S(2)}) collective-permute-start(bf16[240,640]{1,0:T(8,128)(2,1)S(1)} %get-tuple-element.191), channel_id=1, source_target_pairs={{0,2},{1,3},{2,0},{3,1},{4,6},{5,7},{6,4},{7,5},{8,10},{9,11},{10,... | collective-permute-start | bytes 921608 | tf_op jit(solution)/shard_map/ppermute | solution.py:650
  687.5 27.4 %collective-permute-start.79 = (bf16[240,640]{1,0:T(8,128)(2,1)S(1)}, bf16[240,640]{1,0:T(8,128)(2,1)S(1)}, u32[]{:S(2)}, u32[]{:S(2)}) collective-permute-start(bf16[240,640]{1,0:T(8,128)(2,1)S(1)} %get-tuple-element.190), channel_id=1, source_target_pairs={{0,3},{1,0},{2,1},{3,2},{4,7},{5,4},{6,5},{7,6},{8,11},{9,8},{10,9... | collective-permute-start | bytes 921608 | tf_op jit(solution)/shard_map/ppermute | solution.py:650
  693.1 23.5 %collective-permute-start.68 = (bf16[240,384]{1,0:T(8,128)(2,1)S(1)}, bf16[240,384]{1,0:T(8,128)(2,1)S(1)}, u32[]{:S(2)}, u32[]{:S(2)}) collective-permute-start(bf16[240,384]{1,0:T(8,128)(2,1)S(1)} %fusion.13.rest_0_), channel_id=1, source_target_pairs={{0,8},{4,20},{8,0},{12,28},{16,24},{20,4},{24,16},{28,12},{1,9},{5... | collective-permute-start | bytes 552968 | tf_op jit(solution)/shard_map/ppermute | solution.py:645
  693.7 23.9 %collective-permute-start.69 = (bf16[240,384]{1,0:T(8,128)(2,1)S(1)}, bf16[240,384]{1,0:T(8,128)(2,1)S(1)}, u32[]{:S(2)}, u32[]{:S(2)}) collective-permute-start(bf16[240,384]{1,0:T(8,128)(2,1)S(1)} %fusion.13.rest_0_), channel_id=1, source_target_pairs={{0,16},{4,12},{8,24},{12,4},{16,0},{20,28},{24,8},{28,20},{1,17},{... | collective-permute-start | bytes 552968 | tf_op jit(solution)/shard_map/ppermute | solution.py:645
  708.5 10.3 %collective-permute-start.70 = (bf16[240,384]{1,0:T(8,128)(2,1)S(1)}, bf16[240,384]{1,0:T(8,128)(2,1)S(1)}, u32[]{:S(2)}, u32[]{:S(2)}) collective-permute-start(bf16[240,384]{1,0:T(8,128)(2,1)S(1)} %fusion.13.rest_0_), channel_id=1, source_target_pairs={{0,24},{4,28},{8,16},{12,20},{16,8},{20,12},{24,0},{28,4},{1,25},{... | collective-permute-start | bytes 552968 | tf_op jit(solution)/shard_map/ppermute | solution.py:645
  715.2 10.2 %collective-permute-start.80 = (bf16[240,640]{1,0:T(8,128)(2,1)S(1)}, bf16[240,640]{1,0:T(8,128)(2,1)S(1)}, u32[]{:S(2)}, u32[]{:S(2)}) collective-permute-start(bf16[240,640]{1,0:T(8,128)(2,1)S(1)} %fusion.10.rest_0_), channel_id=1, source_target_pairs={{0,8},{4,20},{8,0},{12,28},{16,24},{20,4},{24,16},{28,12},{1,9},{5... | collective-permute-start | bytes 921608 | tf_op jit(solution)/shard_map/ppermute | solution.py:645
  717.6 14.1 %collective-permute-start.82 = (bf16[240,640]{1,0:T(8,128)(2,1)S(1)}, bf16[240,640]{1,0:T(8,128)(2,1)S(1)}, u32[]{:S(2)}, u32[]{:S(2)}) collective-permute-start(bf16[240,640]{1,0:T(8,128)(2,1)S(1)} %fusion.10.rest_0_), channel_id=1, source_target_pairs={{0,24},{4,28},{8,16},{12,20},{16,8},{20,12},{24,0},{28,4},{1,25},{... | collective-permute-start | bytes 921608 | tf_op jit(solution)/shard_map/ppermute | solution.py:645
  720.6 20.9 %collective-permute-start.83 = (bf16[240,640]{1,0:T(8,128)(2,1)S(1)}, bf16[240,640]{1,0:T(8,128)(2,1)S(1)}, u32[]{:S(2)}, u32[]{:S(2)}) collective-permute-start(bf16[240,640]{1,0:T(8,128)(2,1)S(1)} %fusion.10.rest_0_), channel_id=1, source_target_pairs={{0,4},{4,0},{8,12},{12,8},{16,20},{20,16},{24,28},{28,24},{1,5},{5... | collective-permute-start | bytes 921608 | tf_op jit(solution)/shard_map/ppermute | solution.py:645
  720.8 13.0 %collective-permute-start.74 = (bf16[240,384]{1,0:T(8,128)(2,1)S(1)}, bf16[240,384]{1,0:T(8,128)(2,1)S(1)}, u32[]{:S(2)}, u32[]{:S(2)}) collective-permute-start(bf16[240,384]{1,0:T(8,128)(2,1)S(1)} %collective-permute-done.70.rest_3_), channel_id=1, source_target_pairs={{0,4},{4,0},{8,12},{12,8},{16,20},{20,16},{24,28},{28,24},{1,5},{5... | collective-permute-start | bytes 552968 | tf_op jit(solution)/shard_map/ppermute | solution.py:645
  725.4 16.1 %collective-permute-start.84 = (bf16[240,640]{1,0:T(8,128)(2,1)S(1)}, bf16[240,640]{1,0:T(8,128)(2,1)S(1)}, u32[]{:S(2)}, u32[]{:S(2)}) collective-permute-start(bf16[240,640]{1,0:T(8,128)(2,1)S(1)} %collective-permute-done.80.rest_1_), channel_id=1, source_target_pairs={{0,4},{4,0},{8,12},{12,8},{16,20},{20,16},{24,28},{28,24},{1,5},{5... | collective-permute-start | bytes 921608 | tf_op jit(solution)/shard_map/ppermute | solution.py:645
  725.4 16.1 %collective-permute-start.85 = (bf16[240,640]{1,0:T(8,128)(2,1)S(1)}, bf16[240,640]{1,0:T(8,128)(2,1)S(1)}, u32[]{:S(2)}, u32[]{:S(2)}) collective-permute-start(bf16[240,640]{1,0:T(8,128)(2,1)S(1)} %collective-permute-done.81.rest_2_), channel_id=1, source_target_pairs={{0,4},{4,0},{8,12},{12,8},{16,20},{20,16},{24,28},{28,24},{1,5},{5... | collective-permute-start | bytes 921608 | tf_op jit(solution)/shard_map/ppermute | solution.py:645
  (98 other events, 1170.1 us)

commit v4 on v3

--- a/solution.py
+++ b/solution.py
@@ -166,13 +166,13 @@
         in_specs=[WHOLE] * 6,
         out_specs=(WHOLE,) * 2,
         scratch_shapes=[pltpu.VMEM((3 * n, n), f32), pltpu.VMEM((2 * KVW, 3 * n), bf16)],
-        compiler_params=pltpu.CompilerParams(vmem_limit_bytes=LIMIT),
+        compiler_params=pltpu.CompilerParams(vmem_limit_bytes=24 << 20),
         name="attend",
     )(q, *kvs, seg_k, seg_q)
 
 
-def attend_back_kernel(q_ref, kv0, kv1, kv2, sk_ref, sq_ref, lse_ref, do_ref, cos_ref, sin_ref, *rest):
-    dq_ref, far_ref, near_ref, own_ref, bias, kv, dqs = rest[-7:]
+def attend_back_kernel(sc, p_ref, q_ref, kv0, kv1, kv2, sk_ref, sq_ref, lse_ref, do_ref, cos_ref, sin_ref, *rest):
+    dq_ref, three_ref, far_ref, near_ref, own_ref, bias, kv, dqs = rest[-8:]
     n = q_ref.shape[1]
     bias[...] = bias_of(sk_ref[...], sq_ref[...])
     window_of((kv0, kv1, kv2), kv)
@@ -204,21 +204,23 @@
     lax.fori_loop(0, KV_HEADS, head, 0)
     cos, sin = cos_ref[...] * scale, sin_ref[...] * scale
     for m in range(3):
-        dq_ref[m] = widened(rope(dqs[m * KVW : (m + 1) * KVW, :], cos, sin, True).T.astype(bf16))
-
-
-def attend_back(q, kvs, seg_k, seg_q, lse, do, cos, sin, after=()):
+        dq = widened(rope(dqs[m * KVW : (m + 1) * KVW, :], cos, sin, True).T.astype(bf16))
+        dq_ref[m] = dq
+        three_ref[m] = jnp.where(sc[0] == 0, p_ref[m], dq)
+
+
+def attend_back(sc, p, q, kvs, seg_k, seg_q, lse, do, cos, sin, after=()):
     width, n = q.shape
     block = (2 * KVW, n)
     return pl.pallas_call(
         attend_back_kernel,
-        out_shape=(shape((3, n, PIECE), bf16), shape(block, f32), shape(block, bf16), shape(block, f32)),
-        in_specs=[WHOLE] * 10 + [LEFT] * len(after),
-        out_specs=(WHOLE,) * 4,
+        out_shape=(shape((3, n, PIECE), bf16), shape((3, n, PIECE), bf16), shape(block, f32), shape(block, bf16), shape(block, f32)),
+        in_specs=[SCALARS] + [WHOLE] * 11 + [LEFT] * len(after),
+        out_specs=(WHOLE,) * 5,
         scratch_shapes=[pltpu.VMEM((3 * n, n), f32), pltpu.VMEM((2 * KVW, 3 * n), bf16), pltpu.VMEM((width, n), f32)],
-        compiler_params=pltpu.CompilerParams(vmem_limit_bytes=LIMIT),
+        compiler_params=pltpu.CompilerParams(vmem_limit_bytes=32 << 20),
         name="attend_back",
-    )(q, *kvs, seg_k, seg_q, lse, do, cos, sin, *after)
+    )(sc, p, q, *kvs, seg_k, seg_q, lse, do, cos, sin, *after)
 
 
 def fetch_ffn(mine_b, other_b, mine_d, other_d, wb, wd, sem_b, sem_d, core, chip):
@@ -359,20 +361,21 @@
     return da
 
 
-def project_back(da, own_ref, near_ref, far_ref, core, cos_ref, sin_ref, dk_ref, dv_ref, h, gain, wa, sem_a):
+def project_back(da, own_ref, near_ref, far_ref, core, cos_ref, sin_ref, dk_ref, dv_ref, one_ref, h, gain, wa, sem_a):
     cos, sin = cos_ref[...], sin_ref[...]
     grad = own_ref[...] + far_ref[...].astype(f32) + jnp.where(core == 0, near_ref[...].astype(f32), 0.0)
     dk = rope(grad[:KVW], cos, sin, True).T.astype(bf16)
     dv = grad[KVW:].T.astype(bf16)
     dk_ref[...] = widened(dk)
     dv_ref[...] = widened(dv)
+    one_ref[...] = widened(jnp.where(core == 0, dv, dk))
     arrived(wa, sem_a, 0, 3)
     arrived(wa, sem_a, 1, 0)
     da = da + nt(dk, wa[0, 3, :, :KVW]) + nt(dv, wa[1, 0, :, :KVW])
     return norm_back(h, gain, da)
 
 
-def back_kernel(start, end, sc, *rest):
+def back_kernel(start, end, after, sc, *rest):
     rest = list(rest)
 
     def take(n):
@@ -391,8 +394,9 @@
         g1_in, dq_ref, own_ref, near_ref, far_ref, h_ref, gain_a, cos_ref, sin_ref = take(9)
     if not end:
         ins = take(5)
+    take(after)
     if not start:
-        dk_ref, dv_ref, dgain_a = take(3)
+        dk_ref, dv_ref, one_ref, dgain_a = take(4)
     if end:
         (g_out,) = take(1)
     else:
@@ -406,7 +410,7 @@
         state = g_ref[...].T.astype(f32)
     else:
         da = query_back(dq_ref, wa, sem_a)
-        dx, dgain = project_back(da, own_ref, near_ref, far_ref, core, cos_ref, sin_ref, dk_ref, dv_ref, h_ref[...].astype(f32), gain_a[...], wa, sem_a)
+        dx, dgain = project_back(da, own_ref, near_ref, far_ref, core, cos_ref, sin_ref, dk_ref, dv_ref, one_ref, h_ref[...].astype(f32), gain_a[...], wa, sem_a)
         dgain_a[...] = dgain
         state = g1_in[...] + dx
     if end:
@@ -418,7 +422,7 @@
             finish_a(wa, sem_a, (1, 0), (0, 0), (0, 1), (0, 2), (0, 3))
 
 
-def back(start, end, sc, weights, tail, ffn):
+def back(start, end, sc, weights, tail, ffn, after=()):
     wa, wb, wd = weights
     width = wa[0][0].shape[0]
     args = [sc, *wa[0], *wa[1]]
@@ -436,15 +440,17 @@
         args += list(ffn)
         specs += [WHOLE] * len(ffn)
     if not start:
-        outs += [shape((n, PIECE), bf16), shape((n, PIECE), bf16), shape((1, width), f32)]
+        outs += [shape((n, PIECE), bf16)] * 3 + [shape((1, width), f32)]
     if end:
         outs += [shape((width, n), bf16)]
     else:
         hidden = ffn[0].shape[1]
         outs += [shape((n, width), bf16), shape((n, hidden), bf16), shape((n, hidden), bf16), shape((n, hidden // 2), bf16), shape((n, hidden // 2), bf16)]
         outs += [shape((n, width), f32), shape((3, n, PIECE), bf16), shape((1, width), f32), shape((width, n), bf16)]
-    return pl.pallas_call(
-        functools.partial(back_kernel, start, end),
+    args += list(after)
+    specs += [LEFT] * len(after)
+    return pl.pallas_call(
+        functools.partial(back_kernel, start, end, len(after)),
         out_shape=tuple(outs),
         in_specs=specs,
         out_specs=(WHOLE,) * len(outs),
@@ -465,94 +471,108 @@
         dst[:, i * n : (i + 1) * n] = block[...].T
 
 
-def grad_ffn_kernel(first, sc, *rest):
+def grad_ffn_kernel(sc, *rest):
     lefts, rights = rest[:4], rest[4:8]
-    out_ref, left, right = rest[-3:]
+    send_ref, keep_ref, left, right = rest[-4:]
     core, chip = sc[0], sc[1]
     n, cols = rights[0].shape[0], right.shape[1]
     turned(left, lefts)
-    for i, m in enumerate(by_turn(core, chip)[first : first + 2]):
+    for i, m in enumerate(by_turn(core, chip)):
         at = pl.multiple_of(m * cols, 128)
         for j, block in enumerate(rights):
             right[j * n : (j + 1) * n, :] = block[:, pl.ds(at, cols)]
-        out_ref[i] = nn(left[...], right[...]).astype(bf16)
-
-
-def grad_ffn(first, sc, lefts, rights, after=()):
+        out = send_ref if i < 2 else keep_ref
+        out[i % 2] = nn(left[...], right[...]).astype(bf16)
+
+
+def grad_ffn(sc, lefts, rights):
     n, width = lefts[0].shape
     cols = rights[0].shape[1] // 4
-    return pl.pallas_call(
-        functools.partial(grad_ffn_kernel, first),
-        out_shape=shape((2, width, cols), bf16),
-        in_specs=[SCALARS] + [WHOLE] * 8 + [LEFT] * len(after),
-        out_specs=WHOLE,
+    out = shape((2, width, cols), bf16)
+    return pl.pallas_call(
+        grad_ffn_kernel,
+        out_shape=(out, out),
+        in_specs=[SCALARS] + [WHOLE] * 8,
+        out_specs=(WHOLE,) * 2,
         scratch_shapes=[pltpu.VMEM((width, 4 * n), bf16), pltpu.VMEM((4 * n, cols), bf16)],
-        compiler_params=pltpu.CompilerParams(vmem_limit_bytes=LIMIT),
+        compiler_params=pltpu.CompilerParams(vmem_limit_bytes=36 << 20),
         name="grad_ffn",
-    )(sc, *lefts, *rights, *after)
-
-
-def grad_down_kernel(*rest):
+    )(sc, *lefts, *rights)
+
+
+def grad_down_kernel(sc, *rest):
     lefts, rights = rest[:4], rest[4:8]
-    out_ref, left, right = rest[-3:]
+    outs, left, right = rest[-4:-2], rest[-2], rest[-1]
     n, cols = rights[0].shape[0], right.shape[1]
     turned(left, lefts)
-    for i in range(2):
+    for i, out in enumerate(outs):
+        at = pl.multiple_of(((sc[2] + i) & 1) * cols, 128)
         for j, block in enumerate(rights):
-            right[j * n : (j + 1) * n, :] = block[:, i * cols : (i + 1) * cols]
-        out_ref[i] = nn(left[...], right[...]).astype(bf16)
-
-
-def grad_down(lefts, rights, after=()):
+            right[j * n : (j + 1) * n, :] = block[:, pl.ds(at, cols)]
+        out[...] = nn(left[...], right[...]).astype(bf16)
+
+
+def grad_down(sc, lefts, rights, after):
     n, width = lefts[0].shape
     cols = rights[0].shape[1] // 2
     return pl.pallas_call(
         grad_down_kernel,
-        out_shape=shape((2, width, cols), bf16),
-        in_specs=[WHOLE] * 8 + [LEFT] * len(after),
-        out_specs=WHOLE,
+        out_shape=(shape((width, cols), bf16),) * 2,
+        in_specs=[SCALARS] + [WHOLE] * 8 + [LEFT] * len(after),
+        out_specs=(WHOLE,) * 2,
         scratch_shapes=[pltpu.VMEM((width, 4 * n), bf16), pltpu.VMEM((4 * n, cols), bf16)],
-        compiler_params=pltpu.CompilerParams(vmem_limit_bytes=LIMIT),
+        compiler_params=pltpu.CompilerParams(vmem_limit_bytes=32 << 20),
         name="grad_down",
-    )(*lefts, *rights, *after)
+    )(sc, *lefts, *rights, *after)
 
 
 def grad_attention_kernel(sc, *rest):
-    a_refs, o_refs, rights = rest[:4], rest[4:8], rest[8:12]
-    send_ref, keep_ref, left, right = rest[12:]
+    a_refs, o_refs, rest = rest[:4], rest[4:8], rest[8:]
+    queries, keys, values, outs, threes, ones = (rest[i : i + 2] for i in range(0, 12, 2))
+    send_ref, keep_ref, left, right = rest[-4:]
     core, chip = sc[0], sc[1]
-    n = rights[0].shape[1]
+    n = a_refs[0].shape[0]
     turned(left.at[0], a_refs)
+
+    def fill(at, of_three, own_three, own_one, single):
+        for j in range(2):
+            for i in range(3):
+                right[of_three + i, j * n : (j + 1) * n, :] = own_three[j][i]
+                right[of_three + i, (j + 2) * n : (j + 3) * n, :] = threes[j][i]
+            right[single, j * n : (j + 1) * n, :] = own_one[j][...]
+            right[single, (j + 2) * n : (j + 3) * n, :] = ones[j][...]
+
+    @pl.when(core == 0)
+    def _():
+        fill(0, 0, queries, keys, 3)
 
     @pl.when(core == 1)
     def _():
         turned(left.at[1], o_refs)
+        fill(0, 1, outs, values, 0)
 
     for i, m in enumerate(by_turn(core, chip)):
-        for j, block in enumerate(rights):
-            right[j * n : (j + 1) * n, :] = block[m]
         out = send_ref if i < 2 else keep_ref
         which = jnp.where(m > 0, core, 0)
-        out[i % 2] = nn(left[which], right[...]).astype(bf16)
-
-
-def grad_attention(sc, a, o, rights):
+        out[i % 2] = nn(left[which], right[m]).astype(bf16)
+
+
+def grad_attention(sc, a, o, own, got, after):
     n, width = a[0].shape
-    cols = rights[0].shape[2]
-    out = shape((2, width, cols), bf16)
+    out = shape((2, width, PIECE), bf16)
     return pl.pallas_call(
         grad_attention_kernel,
         out_shape=(out, out),
-        in_specs=[SCALARS] + [WHOLE] * 12,
+        in_specs=[SCALARS] + [WHOLE] * 20 + [LEFT] * len(after),
         out_specs=(WHOLE,) * 2,
-        scratch_shapes=[pltpu.VMEM((2, width, 4 * n), bf16), pltpu.VMEM((4 * n, cols), bf16)],
-        compiler_params=pltpu.CompilerParams(vmem_limit_bytes=LIMIT),
+        scratch_shapes=[pltpu.VMEM((2, width, 4 * n), bf16), pltpu.VMEM((4, 4 * n, PIECE), bf16)],
+        compiler_params=pltpu.CompilerParams(vmem_limit_bytes=36 << 20),
         name="grad_attention",
-    )(sc, *a, *o, *rights)
-
-
-def lay_kernel(sc, *rest):
-    mine, other, outs, kept = rest[:4], rest[4:8], rest[8:-1], rest[-1]
+    )(sc, *a, *o, *own, *got, *after)
+
+
+def lay_kernel(count, sc, *rest):
+    mine, other, outs, kept = rest[:4], rest[4:8], rest[-1 - count : -1], rest[-1]
     core, chip = sc[0], sc[1]
     for kind, pieces in ((core, mine), (1 - core, other)):
         for who, piece in zip(whose(kind), pieces):
@@ -569,48 +589,49 @@
         outs[3][...] = cols[1][:, n:]
 
 
-def lay(sc, mine, other, widths):
+def lay(sc, mine, other, widths, after):
     rows, n = mine[0].shape
     outs = tuple(shape((rows, w), f32) for w in widths)
     return pl.pallas_call(
-        lay_kernel,
+        functools.partial(lay_kernel, len(widths)),
         out_shape=outs,
-        in_specs=[SCALARS] + [WHOLE] * 8,
+        in_specs=[SCALARS] + [WHOLE] * 8 + [LEFT] * len(after),
         out_specs=(WHOLE,) * len(outs),
         scratch_shapes=[pltpu.VMEM((2, 4, rows, n), bf16)],
-        compiler_params=pltpu.CompilerParams(vmem_limit_bytes=LIMIT),
+        compiler_params=pltpu.CompilerParams(vmem_limit_bytes=24 << 20),
         name="lay",
-    )(sc, *mine, *other)
-
-
-def pick_kernel(sc, gate, up, down, *rest):
-    b_ref, d_ref, sems = rest[-3:]
+    )(sc, *mine, *other, *after)
+
+
+def pick_kernel(by_core, sc, *rest):
+    sources, (out_ref, sem) = rest[:2], rest[-2:]
     core, chip = sc[0], sc[1]
-    cols, half = b_ref.shape[1], d_ref.shape[0]
-    at = pl.ds(pl.multiple_of(chip * cols, 128), cols)
-    rows = pl.ds(pl.multiple_of(core * half, half), half)
-    copy = pltpu.make_async_copy(down.at[rows, :], d_ref, sems.at[1])
-    copy.start()
-    for c, source in ((0, gate), (1, up)):
+    if by_core:
+        cols = out_ref.shape[1]
+        at = pl.ds(pl.multiple_of(chip * cols, 128), cols)
+        views = [source.at[:, at] for source in sources]
+    else:
+        half = out_ref.shape[0]
+        views = [source.at[c * half : (c + 1) * half, :] for c, source in enumerate(sources)]
+    for c in range(2):
 
         @pl.when(core == c)
         def _():
-            pltpu.make_async_copy(source.at[:, at], b_ref, sems.at[0]).start()
-
-    pltpu.make_async_copy(gate.at[:, at], b_ref, sems.at[0]).wait()
-    copy.wait()
-
-
-def pick(sc, gate, up, down, after):
-    return pl.pallas_call(
-        pick_kernel,
-        out_shape=(shape((gate.shape[0], gate.shape[1] // 4), bf16), shape((down.shape[0] // 2, down.shape[1]), bf16)),
-        in_specs=[SCALARS] + [LEFT] * (3 + len(after)),
-        out_specs=(LEFT, LEFT),
-        scratch_shapes=[pltpu.SemaphoreType.DMA((2,))],
-        compiler_params=pltpu.CompilerParams(vmem_limit_bytes=LIMIT),
+            pltpu.make_async_copy(views[c], out_ref, sem).start()
+
+    pltpu.make_async_copy(views[0], out_ref, sem).wait()
+
+
+def pick(sc, sources, out, by_core, after):
+    return pl.pallas_call(
+        functools.partial(pick_kernel, by_core),
+        out_shape=shape(out, bf16),
+        in_specs=[SCALARS] + [LEFT] * (2 + len(after)),
+        out_specs=WHOLE,
+        scratch_shapes=[pltpu.SemaphoreType.DMA],
+        compiler_params=pltpu.CompilerParams(vmem_limit_bytes=16 << 20),
         name="pick",
-    )(sc, gate, up, down, *after)
+    )(sc, *sources, *after)
 
 
 def stack_kernel(sc, *rest):
@@ -627,11 +648,110 @@
         stack_kernel,
         out_shape=shape((4,) + parts[0].shape, parts[0].dtype),
         in_specs=[SCALARS] + [LEFT] * (4 + len(after)),
-        out_specs=LEFT,
+        out_specs=WHOLE,
         scratch_shapes=[pltpu.SemaphoreType.DMA((4,))],
-        compiler_params=pltpu.CompilerParams(vmem_limit_bytes=LIMIT),
+        compiler_params=pltpu.CompilerParams(vmem_limit_bytes=16 << 20),
         name="stack",
     )(sc, *parts, *after)
+
+
+def small(kernel, sc, args, outs, scratch, after, name):
+    return pl.pallas_call(
+        kernel,
+        out_shape=tuple(outs),
+        in_specs=[SCALARS] + [WHOLE] * len(args) + [LEFT] * len(after),
+        out_specs=(WHOLE,) * len(outs),
+        scratch_shapes=scratch,
+        compiler_params=pltpu.CompilerParams(vmem_limit_bytes=32 << 20),
+        name=name,
+    )(sc, *args, *after)
+
+
+def sum_first(sc, keep, got, after):
+    def kernel(sc, keep_ref, got_ref, *rest):
+        later_ref, own_ref = rest[-2:]
+        later_ref[...] = (keep_ref[1].astype(f32) + got_ref[1].astype(f32)).astype(bf16)
+        own_ref[...] = keep_ref[0].astype(f32) + got_ref[0].astype(f32)
+
+    block = keep.shape[1:]
+    return small(kernel, sc, [keep, got], [shape(block, bf16), shape(block, f32)], [], after, "sum_first")
+
+
+def sum_second(sc, own, got, after):
+    def kernel(sc, own_ref, got_ref, *rest):
+        outs, total = rest[-5:-1], rest[-1]
+        n = total.shape[1]
+        for j in range(4):
+            rows = slice(j * n, (j + 1) * n)
+            total[j] = own_ref[rows, :] + got_ref[rows, :].astype(f32)
+        for s, out in enumerate(outs):
+            out[...] = total[(sc[2] + s) & 3].astype(out.dtype)
+
+    rows, cols = own.shape
+    part = (rows // 4, cols)
+    outs = [shape(part, f32)] + [shape(part, bf16)] * 3
+    return small(kernel, sc, [own, got], outs, [pltpu.VMEM((4,) + part, f32)], after, "sum_second")
+
+
+def sum_ring(sc, own, got, after):
+    def kernel(sc, own_ref, *rest):
+        out_ref = rest[-1]
+        out_ref[...] = (own_ref[...] + sum(g[...].astype(f32) for g in rest[:3])).astype(bf16)
+
+    return small(kernel, sc, [own, *got], [shape(own.shape, bf16)], [], after, "sum_ring")[0]
+
+
+def down_ring(sc, own, got, after):
+    def kernel(sc, own_ref, *rest):
+        give_ref, keep_ref, total = rest[-3:]
+        half = give_ref.shape[0]
+        total[...] = own_ref[...].astype(f32) + sum(g[...].astype(f32) for g in rest[:3])
+        give_ref[...] = total[pl.ds(pl.multiple_of((1 - sc[0]) * half, half), half), :].astype(bf16)
+        keep_ref[...] = total[pl.ds(pl.multiple_of(sc[0] * half, half), half), :].astype(bf16)
+
+    rows, cols = own.shape
+    half = shape((rows // 2, cols), bf16)
+    return small(kernel, sc, [own, *got], [half, half], [pltpu.VMEM((rows, cols), f32)], after, "down_ring")
+
+
+def down_split(sc, keep, given, after):
+    def kernel(sc, keep_ref, given_ref, *rest):
+        send_ref, kept_ref, total = rest[-3:]
+        n = total.shape[1]
+        owner = (sc[2] >> 1) == sc[0]
+        for m in range(4):
+            rows = slice(m * n, (m + 1) * n)
+            total[m] = jnp.where(owner, keep_ref[rows, :].astype(f32), given_ref[rows, :].astype(f32))
+        for i, m in enumerate(by_turn(sc[0], sc[1])):
+            out = send_ref if i < 2 else kept_ref
+            out[i % 2] = total[m].astype(bf16)
+
+    rows, cols = keep.shape
+    out = shape((2, rows // 4, cols), bf16)
+    return small(kernel, sc, [keep, given], [out, out], [pltpu.VMEM((4, rows // 4, cols), f32)], after, "down_split")
+
+
+def sum_two(sc, own, got, after):
+    def kernel(sc, own_ref, got_ref, *rest):
+        rest[-1][...] = (own_ref[...] + got_ref[...].astype(f32)).astype(bf16)
+
+    return small(kernel, sc, [own, got], [shape(own.shape, bf16)], [], after, "sum_two")[0]
+
+
+def lay_down(sc, mine, other, after):
+    def kernel(sc, *rest):
+        out_ref, total = rest[-2:]
+        n = total.shape[2]
+        for kind, pieces in ((sc[0], rest[:4]), (1 - sc[0], rest[4:8])):
+            for who, piece in zip(whose(kind), pieces):
+                total[kind, sc[1] ^ who] = piece[...].astype(f32)
+        for c in range(2):
+            for m in range(4):
+                at = (c * 4 + m) * n
+                out_ref[at : at + n, :] = total[c, m]
+
+    n, cols = mine[0].shape
+    return small(kernel, sc, [*mine, *other], [shape((8 * n, cols), f32)], [pltpu.VMEM((2, 4, n, cols), f32)], after, "lay_down")[0]
 
 
 CORE, SIDE, BACK = 1, 2, 4
@@ -703,70 +823,28 @@
 def over_groups(value):
     bit = 8
     while bit < lax.axis_size("dp"):
-        value = value + flip(value.astype(bf16), bit).astype(f32)
+        value = (value.astype(f32) + flip(value, bit).astype(f32)).astype(bf16)
         bit *= 2
     return value
 
 
-def plane_reduce(send, keep):
-    got = flip(send, SIDE, BACK)
-    later = (keep[1].astype(f32) + got[1].astype(f32)).astype(bf16)
-    own = keep[0].astype(f32) + got[0].astype(f32)
-    return own + flip(later, BACK, SIDE).astype(f32)
-
-
-def ring_reduce(parts):
-    _, _, z = place()
-    depth = lax.axis_size("fsdp")
-    low = parts.astype(bf16)
-    total = lax.dynamic_index_in_dim(parts, z, 0, keepdims=False)
-    for s in range(1, depth):
-        part = lax.dynamic_index_in_dim(low, (z + s) % depth, 0, keepdims=False)
-        total = total + turn_z(part, s).astype(f32)
-    return total
-
-
-def spread(piece, both=True):
-    mine = (piece, flip(piece, SIDE, BACK), flip(piece, BACK, SIDE), flip(piece, SIDE | BACK))
-    return (mine, tuple(flip(p, CORE) for p in mine)) if both else mine
-
-
-def reduce_pieces(sc, send, keep, widths):
-    depth = lax.axis_size("fsdp")
-    own = plane_reduce(send, keep)
-    own = own.reshape((depth, own.shape[0] // depth) + own.shape[1:])
-    own = over_groups(ring_reduce(own)).astype(bf16)
-    return lay(sc, *spread(own), widths)
-
-
-def reduce_down(parts):
-    core, chip, z = place()
-    depth, count = lax.axis_size("fsdp"), lax.axis_size("dp")
-    _, rows, cols = parts.shape
-    owner = (z >> 1) == core
-    total = lax.dynamic_index_in_dim(parts, z & 1, 0, keepdims=False).astype(f32)
-    for s in range(1, depth):
-        part = lax.dynamic_index_in_dim(parts, (z + s) & 1, 0, keepdims=False)
-        pairs = []
-        for d in range(count):
-            for a in range(depth):
-                b = (a + s) % depth
-                if (b >> 1) == (d & 1):
-                    pairs.append((d * depth + a, d * depth + b))
-        total = total + lax.ppermute(part, ("dp", "fsdp"), pairs).astype(f32)
-    half, n = rows // 2, rows // 8
-    halves = total.astype(bf16).reshape(2, half, cols)
-    given = flip(lax.dynamic_index_in_dim(halves, 1 - core, 0, keepdims=False), CORE)
-    kept = lax.dynamic_index_in_dim(halves, core, 0, keepdims=False)
-    mine = jnp.where(owner, kept, given).reshape(4, n, cols)
-    picked = [lax.dynamic_index_in_dim(mine, m, 0, keepdims=False) for m in by_turn(core, chip)]
-    own = over_groups(plane_reduce(jnp.stack(picked[:2]), picked[2:])).astype(bf16)
-    mine = jnp.zeros((4, n, cols), bf16)
-    for who, part in zip(whose(core), spread(own, False)):
-        mine = lax.dynamic_update_index_in_dim(mine, part, chip ^ who, 0)
-    other = flip(mine, CORE)
-    full = jnp.where(core == 0, jnp.concatenate([mine, other]), jnp.concatenate([other, mine]))
-    return full.reshape(rows, cols).astype(f32).T
+def spread(piece):
+    return piece, flip(piece, SIDE, BACK), flip(piece, BACK, SIDE), flip(piece, SIDE | BACK)
+
+
+def across(pieces):
+    return tuple(flip(p, CORE) for p in pieces)
+
+
+def to_owners(part, step):
+    count, depth = lax.axis_size("dp"), lax.axis_size("fsdp")
+    pairs = []
+    for d in range(count):
+        for a in range(depth):
+            b = (a + step) % depth
+            if (b >> 1) == (d & 1):
+                pairs.append((d * depth + a, d * depth + b))
+    return lax.ppermute(part, ("dp", "fsdp"), pairs)
 
 
 def reduce_gains(total):
@@ -792,9 +870,10 @@
     first = jnp.pad(first, ((0, 0), (0, PIECE - KVW)))
     parts_a = turns(lax.dynamic_slice(first, (0, KVW * (core * 4 + chip)), (rows, PIECE)))
     wa = plane_gather(stack(sc, parts_a).reshape(depth * rows, PIECE))
-    piece_b, piece_d = pick(sc, gate_weight, up_weight, down_weight.T, parts_a[1:])
+    piece_b = pick(sc, [gate_weight, up_weight], (rows, gate_weight.shape[1] // 4), True, parts_a[1:])
     whole_b = stack(sc, turns(piece_b)).reshape(depth * rows, piece_b.shape[1])
     wb = plane_gather(whole_b)
+    piece_d = pick(sc, [down_weight.T] * 2, (width // 2, down_weight.shape[0]), False, [whole_b])
     whole_d = stack(sc, turns(piece_d))
     wd = whole_d, flip(whole_d, CORE)
     weights = wa, wb, wd
@@ -827,36 +906,54 @@
     output = home_to_work(output, back=True).T
 
     gb1, act1, away1, zk1, zs1, g1, p1, dgain_f1, do = back(True, False, sc, weights, [cot], [gate1, up1, h1_1, gain_f, z1])
-    dq1, far, near, own = attend_back(q1, kv1, seg_k, seg_q, lse1, do, cos, sin)
+    dq1, three1, far, near, own = attend_back(sc, p1, q1, kv1, seg_k, seg_q, lse1, do, cos, sin)
     near, far = unwindow(far, near)
     tail = [g1, dq1, own, near, far, h_1, gain_a, cos, sin]
-    dk1, dv1, dgain_a1, gb0, act0, away0, zk0, zs0, g1, p0, dgain_f0, do = back(False, False, sc, weights, tail, [gate0, up0, h1_0, gain_f, z0])
+    dk1, dv1, one1, dgain_a1, gb0, act0, away0, zk0, zs0, g1, p0, dgain_f0, do = back(False, False, sc, weights, tail, [gate0, up0, h1_0, gain_f, z0])
 
     def pair(*own):
-        return [*own, *(flip(v, CORE) for v in own)]
-
-    lefts, mid = pair(b1, b0), [act1, act0, flip(away1, CORE), flip(away0, CORE)]
-    send_b = grad_ffn(0, sc, lefts, mid)
-    parts_d = grad_down(pair(gb1, gb0), [zk1, zk0, flip(zs1, CORE), flip(zs0, CORE)], [send_b])
-    keep_b = grad_ffn(2, sc, lefts, mid, [parts_d])
-    grad_gate, grad_up = reduce_pieces(sc, send_b, keep_b, (gate_weight.shape[1],) * 2)
-    grad_down_ = reduce_down(parts_d)
-
-    dq0, far, near, own = attend_back(q0, kv0, seg_k, seg_q, lse0, do, cos, sin, [keep_b])
+        return [*own, *across(own)]
+
+    send_b, keep_b = grad_ffn(sc, pair(b1, b0), [act1, act0, *across((away1, away0))])
+    got_b = flip(send_b, SIDE, BACK)
+    like_d, unlike_d = grad_down(sc, pair(gb1, gb0), [zk1, zk0, *across((zs1, zs0))], [send_b])
+    got_d = [to_owners(unlike_d, 1), to_owners(like_d, 2), to_owners(unlike_d, 3)]
+    owner = (z >> 1) == core
+    own_d = jnp.where(owner, like_d, jnp.zeros_like(like_d))
+
+    dq0, three0, far, near, own = attend_back(sc, p0, q0, kv0, seg_k, seg_q, lse0, do, cos, sin, [like_d])
     near, far = unwindow(far, near)
+    later_b, own_b = sum_first(sc, keep_b, got_b, [own])
+    more_b = flip(later_b, BACK, SIDE)
     tail = [g1, dq0, own, near, far, h_0, gain_a, cos, sin]
-    dk0, dv0, dgain_a0, grad_tokens = back(False, True, sc, weights, tail, None)
+    dk0, dv0, one0, dgain_a0, grad_tokens = back(False, True, sc, weights, tail, None, [later_b])
     grad_tokens = home_to_work(grad_tokens, back=True).astype(f32).T
 
-    kept, sent = [], []
-    for dq, dk, dv, p in ((dq1, dk1, dv1, p1), (dq0, dk0, dv0, p0)):
-        first, second = jnp.concatenate([dq, dk[None]]), jnp.concatenate([dv[None], p])
-        kept.append(jnp.where(core == 0, first, second))
-        sent.append(flip(jnp.where(core == 0, second, first), CORE))
-    send_a, keep_a = grad_attention(sc, pair(a1, a0), pair(mixed1, mixed0), kept + sent)
-    grad_query, grad_key, grad_value, grad_out = reduce_pieces(sc, send_a, keep_a, (width, KVW, KVW, width))
+    own = [dq1, dq0, dk1, dk0, dv1, dv0, p1, p0]
+    send_a, keep_a = grad_attention(sc, pair(a1, a0), pair(mixed1, mixed0), own, across((three1, three0, one1, one0)), [])
+    got_a = flip(send_a, SIDE, BACK)
+    ring_b = sum_second(sc, own_b, more_b, [send_a])
+    ring_b, parts_b = ring_b[0], [turn_z(v, s + 1) for s, v in enumerate(ring_b[1:])]
+    later_a, own_a = sum_first(sc, keep_a, got_a, [ring_b])
+    more_a = flip(later_a, BACK, SIDE)
+    give, keep = down_ring(sc, own_d, got_d, [later_a])
+    send_d, keep_d = down_split(sc, keep, flip(give, CORE), [])
+    got_d = flip(send_d, SIDE, BACK)
+    ring_a = sum_second(sc, own_a, more_a, [send_d])
+    ring_a, parts_a = ring_a[0], [turn_z(v, s + 1) for s, v in enumerate(ring_a[1:])]
+    later_d, own_d = sum_first(sc, keep_d, got_d, [ring_a])
+    more_d = flip(later_d, BACK, SIDE)
+    piece_b = over_groups(sum_ring(sc, ring_b, parts_b, [later_d]))
+    all_b = spread(piece_b)
+    piece_d = over_groups(sum_two(sc, own_d, more_d, [piece_b]))
+    all_d = spread(piece_d)
+    piece_a = over_groups(sum_ring(sc, ring_a, parts_a, [piece_d]))
+    all_a = spread(piece_a)
+    grad_gate, grad_up = lay(sc, all_b, across(all_b), (gate_weight.shape[1],) * 2, [piece_a])
+    grad_down_ = lay_down(sc, all_d, across(all_d), [grad_gate])
+    grad_query, grad_key, grad_value, grad_out = lay(sc, all_a, across(all_a), (width, KVW, KVW, width), [grad_down_])
     dgain_a, dgain_f = reduce_gains(jnp.concatenate([dgain_a1 + dgain_a0, dgain_f1 + dgain_f0]))
-    return (output[None], grad_tokens[None], dgain_a, grad_query, grad_key, grad_value, grad_out, dgain_f, grad_gate, grad_up, grad_down_)
+    return (output[None], grad_tokens[None], dgain_a, grad_query, grad_key, grad_value, grad_out, dgain_f, grad_gate, grad_up, grad_down_.T)
 
 
 def solution(mesh):

time: 758 us -> 615 us (0.81)
  Pallas kernels: 359 us -> 184 us
  local copies, waits for them, and re-layouts: 28.5 us -> 52.6 us
  other arithmetic: 26.7 us -> 5.61 us
  starting transfers between devices: 121 us -> 137 us
  waiting for transfers between devices: 212 us -> 227 us
    pallas_call x3, Pallas kernels: 139 us -> 4.68 us  [stack(): pl.pallas_call(stack_kernel, out_shape=shape((4,) + parts[0].shape, parts...]
    pallas_call x9 -> x20, Pallas kernels: 111 us -> 79.4 us  [the longest x3 50.4 us: back(): pl.pallas_call(functools.partial(back_kernel, start, end, len(after)), ou...]
    ppermute x24, waiting for transfers between devices: 91.3 us -> 119 us  [turn_z(): lax.ppermute(value, 'fsdp', [(i, (i + step) % count) for i in range(count)])]
    unnamed x136 -> x204, local copies, waits for them, and re-layouts: 18.2 us -> 45.4 us
    ppermute x62 -> x67, waiting for transfers between devices: 78.7 us -> 56.6 us  [flip(): lax.ppermute(value, 'dp', [(i, i ^ bits[i & 1]) for i in range(count)])]
    ppermute x2, starting transfers between devices: 5.09 us -> 23.9 us  [window(): far = lax.ppermute(own, 'fsdp', [(z, z + 1) for z in range(0, depth, 2)])]
    ppermute x3, waiting for transfers between devices: 0.01 us -> 15.2 us  [to_owners(): return lax.ppermute(part, ('dp', 'fsdp'), pairs)]
    ppermute x62 -> x67, starting transfers between devices: 37.9 us -> 33.7 us  [flip(): lax.ppermute(value, 'dp', [(i, i ^ bits[i & 1]) for i in range(count)])]
  transfers between devices with their start and end apart: 97 -> 102, of which waited for: 32 -> 43; matrix products, arithmetic and copies ran while one was open for 5% -> 1% of each run, Pallas kernels for 36% -> 18%
where the time goes in v4:
time: 615 us; the launch traced here: 608 us
  waiting for transfers between devices  227 us (37%)
  Pallas kernels  184 us (30%)
  starting transfers between devices  137 us (22%)
  local copies, waits for them, and re-layouts  52.6 us (9%)
    ppermute x24, waiting for transfers between devices, turn_z(): lax.ppermute(value, 'fsdp', [(i, (i + step) % count) for i in range(count)])  119 us
    ppermute x24, starting transfers between devices, turn_z(): lax.ppermute(value, 'fsdp', [(i, (i + step) % count) for i in range(count)])  64.9 us
    ppermute x67, waiting for transfers between devices, flip(): lax.ppermute(value, 'dp', [(i, i ^ bits[i & 1]) for i in range(count)])  56.6 us
    pallas_call x3, Pallas kernels, back(): pl.pallas_call(functools.partial(back_kernel, start, end, len(after)), ou...  50.4 us
    unnamed x204, local copies, waits for them, and re-layouts  45.4 us
    pallas_call x2, Pallas kernels, post(): pl.pallas_call(functools.partial(post_kernel, last), out_shape=tuple(outs...  38.1 us
    ppermute x67, starting transfers between devices, flip(): lax.ppermute(value, 'dp', [(i, i ^ bits[i & 1]) for i in range(count)])  33.7 us
    pallas_call x2, Pallas kernels, attend_back(): pl.pallas_call(attend_back_kernel, out_shape=(shape((3, n, PIECE), bf16),...  26.8 us
  transfers between devices with their start and end apart: 102, of which 43 were waited for; matrix products, arithmetic and copies ran while one was open for 1% of the time, Pallas kernels for 18%

profile of v4, /device:TPU:0, one launch (start us, length us, event | category | flops | bytes accessed | tf_op | source)
XLA Modules:
  0.0 607.6 jit_solution(18082607835911617360)
XLA Ops:
  2.8 3.4 concatenate.10
  7.5 5.1 collective-permute-start.10
  13.7 4.0 collective-permute-done.10.rest_3_.rest_4_
  18.3 3.9 collective-permute-done.8.rest_1_.rest_2_
  22.9 5.3 collective-permute-done.9.rest_2_.rest_3_
  37.0 5.4 collective-permute-start
  42.5 8.5 %collective-permute-done.1 = bf16[2,240]{1,0:T(2,128)(2,1)S(1)} collective-permute-done((bf16[2,240]{1,0:T(2,128)(2,1)S(1)}, bf16[2,240]{1,0:T(2,128)(2,1)S(1)}, u32[]{:S(2)}, u32[]{:S(2)}) %collective-permute-start.1) | collective-permute-done | bytes 992 | tf_op jit(solution)/shard_map/ppermute | solution.py:770
  51.1 5.2 collective-permute-done.2
  56.3 5.4 collective-permute-done.4
  61.6 4.5 collective-permute-done.5
  66.1 3.6 collective-permute-done.6
  69.8 2.0 collective-permute-start.20
  72.0 11.8 %collective-permute-done.19.rest_2_ = bf16[240,640]{1,0:T(8,128)(2,1)S(1)} collective-permute-done((bf16[240,640]{1,0:T(8,128)(2,1)S(1)}, bf16[240,640]{1,0:T(8,128)(2,1)S(1)}, u32[]{:S(2)}, u32[]{:S(2)}) %collective-permute-start.19) | collective-permute-done | bytes 307232 | tf_op jit(solution)/shard_map/ppermute | solution.py:770
  83.8 5.8 collective-permute-start.3
  89.5 1.9 stack.32
  92.3 3.2 collective-permute-start.31
  99.2 11.6 %collective-permute-done.30.rest_1_ = bf16[480,640]{1,0:T(8,128)(2,1)S(1)} collective-permute-done((bf16[480,640]{1,0:T(8,128)(2,1)S(1)}, bf16[480,640]{1,0:T(8,128)(2,1)S(1)}, u32[]{:S(2)}, u32[]{:S(2)}) %collective-permute-start.30) | collective-permute-done | bytes 614432 | tf_op jit(solution)/shard_map/ppermute | solution.py:770
  111.7 24.8 %collective-permute-done.31.rest_2_ = bf16[480,640]{1,0:T(8,128)(2,1)S(1)} collective-permute-done((bf16[480,640]{1,0:T(8,128)(2,1)S(1)}, bf16[480,640]{1,0:T(8,128)(2,1)S(1)}, u32[]{:S(2)}, u32[]{:S(2)}) %collective-permute-start.31) | collective-permute-done | bytes 614432 | tf_op jit(solution)/shard_map/ppermute | solution.py:770
  148.7 6.8 %pre.1 = (bf16[256,960]{1,0:T(8,128)(2,1)}, bf16[256,960]{1,0:T(8,128)(2,1)}, bf16[960,256]{1,0:T(8,128)(2,1)}, bf16[640,256]{1,0:T(8,128)(2,1)}) custom-call(s32[3]{0:T(128)} %copy-done.68, bf16[960,256]{1,0:T(8,128)(2,1)} %collective-permute-done.ht_ref, f32[1,960]{1,0:T(1,128)} %squeeze.22.gain_ref.gain_a.rest_24_.rest_14_, ...), custom_call_target="tpu_custom_call" | custom-call | tf_op jit(solution)/shard_map/pre/pallas_call | solution.py:114
  155.5 14.2 %collective-permute-start.21 = (bf16[640,256]{1,0:T(8,128)(2,1)}, bf16[640,256]{1,0:T(8,128)(2,1)S(1)}, u32[]{:S(2)}, u32[]{:S(2)}) collective-permute-start(bf16[640,256]{1,0:T(8,128)(2,1)} %get-tuple-element.104.kv2), channel_id=1, source_target_pairs={{0,1},{2,3},{4,5},{6,7},{8,9},{10,11},{12,13},{14,15},{16,17},{18,... | collective-permute-start | bytes 983048 | tf_op jit(solution)/shard_map/ppermute | solution.py:810
  169.7 8.0 %collective-permute-done.21.kv0 = bf16[640,256]{1,0:T(8,128)(2,1)S(1)} collective-permute-done((bf16[640,256]{1,0:T(8,128)(2,1)}, bf16[640,256]{1,0:T(8,128)(2,1)S(1)}, u32[]{:S(2)}, u32[]{:S(2)}) %collective-permute-start.21) | collective-permute-done | bytes 327712 | tf_op jit(solution)/shard_map/ppermute | solution.py:810
  184.2 10.0 %attend.2 = (bf16[960,256]{1,0:T(8,128)(2,1)S(1)}, f32[15,256]{1,0:T(8,128)S(1)}) custom-call(bf16[960,256]{1,0:T(8,128)(2,1)S(1)} %copy-done.24, bf16[640,256]{1,0:T(8,128)(2,1)S(1)} %collective-permute-done.21.kv0, bf16[640,256]{1,0:T(8,128)(2,1)S(1)} %copy-done.28, bf16[640,256]{1,0:T(8,128)(2,1)S(1)} %copy-done.4, s32[768,1]{1,0:T(8,128)S(1)} %broadcast_in_dim.70.sk_ref, ...), custom_call_target="tpu_custom_call" | custom-call | tf_op jit(solution)/shard_map/attend/pallas_call | solution.py:163
  195.1 20.3 %post.2 = (bf16[256,960]{1,0:T(8,128)(2,1)}, f32[256,960]{1,0:T(8,128)}, bf16[256,960]{1,0:T(8,128)(2,1)}, bf16[256,2560]{1,0:T(8,128)(2,1)}, bf16[256,2560]{1,0...) custom-call(s32[3]{0:T(128)} %copy-done.68, ...), custom_call_target="tpu_custom_call" | custom-call | tf_op jit(solution)/shard_map/post/pallas_call | solution.py:297
  215.4 9.6 %collective-permute-start.34 = (bf16[640,256]{1,0:T(8,128)(2,1)}, bf16[640,256]{1,0:T(8,128)(2,1)S(1)}, u32[]{:S(2)}, u32[]{:S(2)}) collective-permute-start(bf16[640,256]{1,0:T(8,128)(2,1)} %get-tuple-element.108.kv2), channel_id=1, source_target_pairs={{0,1},{2,3},{4,5},{6,7},{8,9},{10,11},{12,13},{14,15},{16,17},{18,... | collective-permute-start | bytes 983048 | tf_op jit(solution)/shard_map/ppermute | solution.py:810
  225.7 7.7 %collective-permute-done.34.kv0 = bf16[640,256]{1,0:T(8,128)(2,1)S(1)} collective-permute-done((bf16[640,256]{1,0:T(8,128)(2,1)}, bf16[640,256]{1,0:T(8,128)(2,1)S(1)}, u32[]{:S(2)}, u32[]{:S(2)}) %collective-permute-start.34) | collective-permute-done | bytes 327712 | tf_op jit(solution)/shard_map/ppermute | solution.py:810
  237.2 10.6 %attend.3 = (bf16[960,256]{1,0:T(8,128)(2,1)S(1)}, f32[15,256]{1,0:T(8,128)S(1)}) custom-call(bf16[960,256]{1,0:T(8,128)(2,1)S(1)} %copy-done.26, bf16[640,256]{1,0:T(8,128)(2,1)S(1)} %collective-permute-done.34.kv0, bf16[640,256]{1,0:T(8,128)(2,1)S(1)} %collective-permute-done.35.kv1, bf16[640,256]{1,0:T(8,128)(2,1)S(1)} %copy-done.5, ...), custom_call_target="tpu_custom_call" | custom-call | tf_op jit(solution)/shard_map/attend/pallas_call | solution.py:163
  248.6 17.8 %post.3 = (bf16[256,960]{1,0:T(8,128)(2,1)}, f32[256,960]{1,0:T(8,128)}, bf16[256,960]{1,0:T(8,128)(2,1)}, bf16[256,2560]{1,0:T(8,128)(2,1)}, bf16[256,2560]{1,0...) custom-call(s32[3]{0:T(128)} %copy-done.68, bf16[960,256]{1,0:T(8,128)(2,1)} %copy-done.67, ...), custom_call_target="tpu_custom_call" | custom-call | tf_op jit(solution)/shard_map/post/pallas_call | solution.py:297
  267.2 21.7 %back_start.1 = (bf16[256,960]{1,0:T(8,128)(2,1)}, bf16[256,2560]{1,0:T(8,128)(2,1)}, bf16[256,2560]{1,0:T(8,128)(2,1)}, bf16[256,1280]{1,0:T(8,128)(2,1)}, bf16...) custom-call(s32[3]{0:T(128)} %copy-done.68, ...), custom_call_target="tpu_custom_call" | custom-call | tf_op jit(solution)/shard_map/back_start/pallas_call | solution.py:452
  291.1 13.4 %attend_back.2 = (bf16[3,256,384]{2,1,0:T(8,128)(2,1)S(1)}, bf16[3,256,384]{2,1,0:T(8,128)(2,1)}, f32[640,256]{1,0:T(8,128)S(1)}, bf16[640,256]{1,0:T(8,128)(2,1)S(1)}, f32[640,256]{1,0:T(8,128)S(1)}) custom-call(s32[3]{0:T(128)S(1)} %copy-done.69, bf16[3,256,384]{2,1,0:T(8,128)(2,1)S(1)} %copy-done.16, bf16[960,256]{1,0:T(8,128)(2,1)S(1)} %copy-done.26, ...), custom_call_target="tpu_custom_call" | custom-call | tf_op jit(solution)/shard_map/attend_back/pallas_call | solution.py:215
  309.4 10.2 %collective-permute-done.39.rest_22_ = bf16[640,256]{1,0:T(8,128)(2,1)S(1)} collective-permute-done((bf16[640,256]{1,0:T(8,128)(2,1)S(1)}, bf16[640,256]{1,0:T(8,128)(2,1)S(1)}, u32[]{:S(2)}, u32[]{:S(2)}) %collective-permute-start.39) | collective-permute-done | bytes 327712 | tf_op jit(solution)/shard_map/ppermute | solution.py:820
  320.3 22.1 %back_join.1 = (bf16[256,384]{1,0:T(8,128)(2,1)}, bf16[256,384]{1,0:T(8,128)(2,1)}, bf16[256,384]{1,0:T(8,128)(2,1)}, f32[1,960]{1,0:T(1,128)}, bf16[256,960]{1,...) custom-call(s32[3]{0:T(128)} %copy-done.68, ...), custom_call_target="tpu_custom_call" | custom-call | tf_op jit(solution)/shard_map/back_join/pallas_call | solution.py:452
  343.1 2.9 collective-permute-done.45.rest_3_
  351.8 7.2 %grad_ffn.1 = (bf16[2,960,640]{2,1,0:T(8,128)(2,1)S(1)}, bf16[2,960,640]{2,1,0:T(8,128)(2,1)S(1)}) custom-call(s32[3]{0:T(128)S(1)} %copy-done.70, bf16[256,960]{1,0:T(8,128)(2,1)S(1)} %copy-done.63, bf16[256,960]{1,0:T(8,128)(2,1)S(1)} %copy-done.61, bf16[256,960]{1,0:T(8,128)(2,1)S(1)} %collective-permute-done.44.rest_2_, ...), custom_call_target="tpu_custom_call" | custom-call | tf_op jit(solution)/shard_map/grad_ffn/pallas_call | solution.py:492
  361.6 2.8 collective-permute-done.40.rest_2_
  365.1 3.8 grad_down.1
  369.1 13.4 %attend_back.3 = (bf16[3,256,384]{2,1,0:T(8,128)(2,1)S(1)}, bf16[3,256,384]{2,1,0:T(8,128)(2,1)}, f32[640,256]{1,0:T(8,128)S(1)}, bf16[640,256]{1,0:T(8,128)(2,1)S(1)}, f32[640,256]{1,0:T(8,128)S(1)}) custom-call(s32[3]{0:T(128)S(1)} %copy-done.70, bf16[3,256,384]{2,1,0:T(8,128)(2,1)S(1)} %copy-done.13, bf16[960,256]{1,0:T(8,128)(2,1)S(1)} %copy-done.25, ...), custom_call_target="tpu_custom_call" | custom-call | tf_op jit(solution)/shard_map/attend_back/pallas_call | solution.py:215
  386.3 9.6 %collective-permute-done.49.rest_12_ = bf16[640,256]{1,0:T(8,128)(2,1)S(1)} collective-permute-done((bf16[640,256]{1,0:T(8,128)(2,1)S(1)}, bf16[640,256]{1,0:T(8,128)(2,1)S(1)}, u32[]{:S(2)}, u32[]{:S(2)}) %collective-permute-start.49) | collective-permute-done | bytes 327712 | tf_op jit(solution)/shard_map/ppermute | solution.py:820
  400.8 6.6 %back_end.1 = (bf16[256,384]{1,0:T(8,128)(2,1)}, bf16[256,384]{1,0:T(8,128)(2,1)}, bf16[256,384]{1,0:T(8,128)(2,1)}, f32[1,960]{1,0:T(1,128)}, bf16[960,256]{1,0:T(8,128)(2,1)}) custom-call(s32[3]{0:T(128)} %copy-done.68, bf16[960,384]{1,0:T(8,128)(2,1)} %bitcast.44, bf16[960,384]{1,0:T(8,128)(2,1)} %collective-permute-done.11.rest_1_, ...), custom_call_target="tpu_custom_call" | custom-call | tf_op jit(solution)/shard_map/back_end/pallas_call | solution.py:452
  415.8 7.5 %grad_attention.1 = (bf16[2,960,384]{2,1,0:T(8,128)(2,1)S(1)}, bf16[2,960,384]{2,1,0:T(8,128)(2,1)S(1)}) custom-call(s32[3]{0:T(128)S(1)} %copy-done.71, bf16[256,960]{1,0:T(8,128)(2,1)} %get-tuple-element.157.rest_0_, bf16[256,960]{1,0:T(8,128)(2,1)S(1)} %copy-done.58, bf16[256,960]{1,0:T(8,128)(2,1)} %collective-permute-done.58.rest_2_, ...), custom_call_target="tpu_custom_call" | custom-call | tf_op jit(solution)/shard_map/grad_attention/pallas_call | solution.py:563
  425.6 1.9 collective-permute-start.69
  430.2 23.7 %collective-permute-done.67.got_ref = bf16[960,640]{1,0:T(8,128)(2,1)S(1)} collective-permute-done((bf16[960,640]{1,0:T(8,128)(2,1)S(1)}, bf16[960,640]{1,0:T(8,128)(2,1)S(1)}, u32[]{:S(2)}, u32[]{:S(2)}) %collective-permute-start.67) | collective-permute-done | bytes 1228832 | tf_op jit(solution)/shard_map/ppermute | solution.py:765
  459.0 14.0 %collective-permute-done.70.rest_1_ = bf16[960,640]{1,0:T(8,128)(2,1)S(1)} collective-permute-done((bf16[960,640]{1,0:T(8,128)(2,1)S(1)}, bf16[960,640]{1,0:T(8,128)(2,1)S(1)}, u32[]{:S(2)}, u32[]{:S(2)}) %collective-permute-start.70) | collective-permute-done | bytes 1228832 | tf_op jit(solution)/shard_map/ppermute | solution.py:847
  472.9 1.7 down_ring.1
  478.0 2.5 collective-permute-done.53
  481.0 14.3 %collective-permute-start.78 = (bf16[240,640]{1,0:T(8,128)(2,1)S(1)}, bf16[240,640]{1,0:T(8,128)(2,1)S(1)}, u32[]{:S(2)}, u32[]{:S(2)}) collective-permute-start(bf16[240,640]{1,0:T(8,128)(2,1)S(1)} %get-tuple-element.186), channel_id=1, source_target_pairs={{0,1},{1,2},{2,3},{3,0},{4,5},{5,6},{6,7},{7,4},{8,9},{9,10},{10,1... | collective-permute-start | bytes 921608 | tf_op jit(solution)/shard_map/ppermute | solution.py:770
  497.6 5.0 collective-permute-start.55
  502.6 7.4 %collective-permute-done.55 = f32[2,960]{1,0:T(2,128)S(1)} collective-permute-done((f32[2,960]{1,0:T(2,128)S(1)}, f32[2,960]{1,0:T(2,128)S(1)}, u32[]{:S(2)}, u32[]{:S(2)}) %collective-permute-start.55) | collective-permute-done | bytes 7712 | tf_op jit(solution)/shard_map/ppermute | solution.py:770
  510.0 11.2 %collective-permute-start.56 = (f32[2,960]{1,0:T(2,128)S(1)}, f32[2,960]{1,0:T(2,128)S(1)}, u32[]{:S(2)}, u32[]{:S(2)}) collective-permute-start(f32[2,960]{1,0:T(2,128)S(1)} %add.118), channel_id=1, source_target_pairs={{0,2},{1,3},{2,0},{3,1},{4,6},{5,7},{6,4},{7,5},{8,10},{9,11},{10,... | collective-permute-start | bytes 23048 | tf_op jit(solution)/shard_map/ppermute | solution.py:770
  522.8 3.0 collective-permute-start.79
  527.0 1.8 collective-permute-start.73
  529.4 11.7 %collective-permute-done.79.rest_1_ = bf16[240,640]{1,0:T(8,128)(2,1)S(1)} collective-permute-done((bf16[240,640]{1,0:T(8,128)(2,1)S(1)}, bf16[240,640]{1,0:T(8,128)(2,1)S(1)}, u32[]{:S(2)}, u32[]{:S(2)}) %collective-permute-start.79) | collective-permute-done | bytes 307232 | tf_op jit(solution)/shard_map/ppermute | solution.py:770
  541.5 10.5 %collective-permute-start.57 = (f32[2,960]{1,0:T(2,128)S(1)}, f32[2,960]{1,0:T(2,128)S(1)}, u32[]{:S(2)}, u32[]{:S(2)}) collective-permute-start(f32[2,960]{1,0:T(2,128)S(1)} %add.118), channel_id=1, source_target_pairs={{0,3},{1,0},{2,1},{3,2},{4,7},{5,4},{6,5},{7,6},{8,11},{9,8},{10,9... | collective-permute-start | bytes 23048 | tf_op jit(solution)/shard_map/ppermute | solution.py:770
  552.7 4.1 collective-permute-done.57
  561.7 5.7 collective-permute-done.75.rest_2_
  567.9 5.6 collective-permute-done.96.rest_2_
  576.1 1.7 collective-permute-start.90
  580.4 4.8 collective-permute-done.90.rest_3_
  585.9 3.1 collective-permute-done.82.rest_2_
  591.6 2.0 convert_bitcast_fusion
  593.6 3.1 lay.2
  596.8 1.7 copy-done.8
  598.5 2.3 lay_down.1.rest_8_
  600.8 1.7 copy-done.2
  602.5 2.4 lay.3
  (422 shorter events, 117.0 us)
Async XLA Ops:
  7.5 10.1 %collective-permute-start.10 = (bf16[240,384]{1,0:T(8,128)(2,1)S(1)}, bf16[240,384]{1,0:T(8,128)(2,1)S(1)}, u32[]{:S(2)}, u32[]{:S(2)}) collective-permute-start(bf16[240,384]{1,0:T(8,128)(2,1)S(1)} %pad_dynamic-slice_fusion.rest_0_), channel_id=1, source_target_pairs={{0,3},{1,0},{2,1},{3,2},{4,7},{5,4},{6,5},{7,6},{8,11},{9,8},{10,9... | collective-permute-start | bytes 552968 | tf_op jit(solution)/shard_map/ppermute | solution.py:770
  12.6 15.6 %collective-permute-start.9 = (bf16[240,384]{1,0:T(8,128)(2,1)S(1)}, bf16[240,384]{1,0:T(8,128)(2,1)S(1)}, u32[]{:S(2)}, u32[]{:S(2)}) collective-permute-start(bf16[240,384]{1,0:T(8,128)(2,1)S(1)} %pad_dynamic-slice_fusion.rest_0_), channel_id=1, source_target_pairs={{0,2},{1,3},{2,0},{3,1},{4,6},{5,7},{6,4},{7,5},{8,10},{9,11},{10,... | collective-permute-start | bytes 552968 | tf_op jit(solution)/shard_map/ppermute | solution.py:770
  33.2 62.2 %collective-permute-start.11 = (bf16[960,384]{1,0:T(8,128)(2,1)S(1)}, bf16[960,384]{1,0:T(8,128)(2,1)}, u32[]{:S(2)}, u32[]{:S(2)}) collective-permute-start(bf16[960,384]{1,0:T(8,128)(2,1)S(1)} %bitcast.36), channel_id=1, source_target_pairs={{0,8},{4,20},{8,0},{12,28},{16,24},{20,4},{24,16},{28,12},{1,9},{5... | collective-permute-start | bytes 2211848 | tf_op jit(solution)/shard_map/ppermute | solution.py:765
  35.4 34.3 %collective-permute-start.18 = (bf16[240,640]{1,0:T(8,128)(2,1)S(1)}, bf16[240,640]{1,0:T(8,128)(2,1)S(1)}, u32[]{:S(2)}, u32[]{:S(2)}) collective-permute-start(bf16[240,640]{1,0:T(8,128)(2,1)S(1)} %pick.2.rest_0_), channel_id=1, source_target_pairs={{0,1},{1,2},{2,3},{3,0},{4,5},{5,6},{6,7},{7,4},{8,9},{9,10},{10,1... | collective-permute-start | bytes 921608 | tf_op jit(solution)/shard_map/ppermute | solution.py:770
  35.5 62.0 %collective-permute-start.12 = (bf16[960,384]{1,0:T(8,128)(2,1)S(1)}, bf16[960,384]{1,0:T(8,128)(2,1)}, u32[]{:S(2)}, u32[]{:S(2)}) collective-permute-start(bf16[960,384]{1,0:T(8,128)(2,1)S(1)} %bitcast.37), channel_id=1, source_target_pairs={{0,16},{4,12},{8,24},{12,4},{16,0},{20,28},{24,8},{28,20},{1,17},{... | collective-permute-start | bytes 2211848 | tf_op jit(solution)/shard_map/ppermute | solution.py:765
  37.0 58.9 %collective-permute-start = (bf16[960,256]{1,0:T(8,128)(2,1)}, bf16[960,256]{1,0:T(8,128)(2,1)}, u32[]{:S(2)}, u32[]{:S(2)}) collective-permute-start(bf16[960,256]{1,0:T(8,128)(2,1)} %bitcast.4), channel_id=1, source_target_pairs={{0,0},{1,4},{2,1},{3,5},{4,2},{5,6},{6,3},{7,7},{8,8},{9,12},{10,9... | collective-permute-start | bytes 1474568 | tf_op jit(solution)/shard_map/ppermute | solution.py:781
  69.8 14.0 %collective-permute-start.19 = (bf16[240,640]{1,0:T(8,128)(2,1)S(1)}, bf16[240,640]{1,0:T(8,128)(2,1)S(1)}, u32[]{:S(2)}, u32[]{:S(2)}) collective-permute-start(bf16[240,640]{1,0:T(8,128)(2,1)S(1)} %pick.2.rest_0_), channel_id=1, source_target_pairs={{0,2},{1,3},{2,0},{3,1},{4,6},{5,7},{6,4},{7,5},{8,10},{9,11},{10,... | collective-permute-start | bytes 921608 | tf_op jit(solution)/shard_map/ppermute | solution.py:770
  69.8 14.0 %collective-permute-start.20 = (bf16[240,640]{1,0:T(8,128)(2,1)S(1)}, bf16[240,640]{1,0:T(8,128)(2,1)S(1)}, u32[]{:S(2)}, u32[]{:S(2)}) collective-permute-start(bf16[240,640]{1,0:T(8,128)(2,1)S(1)} %pick.2.rest_0_), channel_id=1, source_target_pairs={{0,3},{1,0},{2,1},{3,2},{4,7},{5,4},{6,5},{7,6},{8,11},{9,8},{10,9... | collective-permute-start | bytes 921608 | tf_op jit(solution)/shard_map/ppermute | solution.py:770
  92.2 18.7 %collective-permute-start.30 = (bf16[480,640]{1,0:T(8,128)(2,1)S(1)}, bf16[480,640]{1,0:T(8,128)(2,1)S(1)}, u32[]{:S(2)}, u32[]{:S(2)}) collective-permute-start(bf16[480,640]{1,0:T(8,128)(2,1)S(1)} %pick.3.rest_0_), channel_id=1, source_target_pairs={{0,1},{1,2},{2,3},{3,0},{4,5},{5,6},{6,7},{7,4},{8,9},{9,10},{10,1... | collective-permute-start | bytes 1843208 | tf_op jit(solution)/shard_map/ppermute | solution.py:770
  92.3 44.2 %collective-permute-start.31 = (bf16[480,640]{1,0:T(8,128)(2,1)S(1)}, bf16[480,640]{1,0:T(8,128)(2,1)S(1)}, u32[]{:S(2)}, u32[]{:S(2)}) collective-permute-start(bf16[480,640]{1,0:T(8,128)(2,1)S(1)} %pick.3.rest_0_), channel_id=1, source_target_pairs={{0,2},{1,3},{2,0},{3,1},{4,6},{5,7},{6,4},{7,5},{8,10},{9,11},{10,... | collective-permute-start | bytes 1843208 | tf_op jit(solution)/shard_map/ppermute | solution.py:770
  95.5 43.2 %collective-permute-start.13 = (bf16[960,384]{1,0:T(8,128)(2,1)}, bf16[960,384]{1,0:T(8,128)(2,1)}, u32[]{:S(2)}, u32[]{:S(2)}) collective-permute-start(bf16[960,384]{1,0:T(8,128)(2,1)} %collective-permute-done.11.rest_1_), channel_id=1, source_target_pairs={{0,16},{4,12},{8,24},{12,4},{16,0},{20,28},{24,8},{28,20},{1,17},{... | collective-permute-start | bytes 2211848 | tf_op jit(solution)/shard_map/ppermute | solution.py:765
  96.0 51.2 %collective-permute-start.23 = (bf16[960,640]{1,0:T(8,128)(2,1)}, bf16[960,640]{1,0:T(8,128)(2,1)}, u32[]{:S(2)}, u32[]{:S(2)}) collective-permute-start(bf16[960,640]{1,0:T(8,128)(2,1)} %bitcast.15.rest_8_.rest_2_), channel_id=1, source_target_pairs={{0,8},{4,20},{8,0},{12,28},{16,24},{20,4},{24,16},{28,12},{1,9},{5... | collective-permute-start | bytes 3686408 | tf_op jit(solution)/shard_map/ppermute | solution.py:765
  97.5 39.9 %collective-permute-start.32 = (bf16[480,640]{1,0:T(8,128)(2,1)S(1)}, bf16[480,640]{1,0:T(8,128)(2,1)S(1)}, u32[]{:S(2)}, u32[]{:S(2)}) collective-permute-start(bf16[480,640]{1,0:T(8,128)(2,1)S(1)} %pick.3.rest_0_), channel_id=1, source_target_pairs={{0,3},{1,0},{2,1},{3,2},{4,7},{5,4},{6,5},{7,6},{8,11},{9,8},{10,9... | collective-permute-start | bytes 1843208 | tf_op jit(solution)/shard_map/ppermute | solution.py:770
  111.7 33.7 %collective-permute-start.14 = (bf16[960,384]{1,0:T(8,128)(2,1)S(1)}, bf16[960,384]{1,0:T(8,128)(2,1)}, u32[]{:S(2)}, u32[]{:S(2)}) collective-permute-start(bf16[960,384]{1,0:T(8,128)(2,1)S(1)} %bitcast.38), channel_id=1, source_target_pairs={{0,4},{4,0},{8,12},{12,8},{16,20},{20,16},{24,28},{28,24},{1,5},{5... | collective-permute-start | bytes 2211848 | tf_op jit(solution)/shard_map/ppermute | solution.py:765
  138.2 10.5 %collective-permute-start.16 = (bf16[960,384]{1,0:T(8,128)(2,1)}, bf16[960,384]{1,0:T(8,128)(2,1)}, u32[]{:S(2)}, u32[]{:S(2)}) collective-permute-start(bf16[960,384]{1,0:T(8,128)(2,1)} %collective-permute-done.12.rest_2_), channel_id=1, source_target_pairs={{0,4},{4,0},{8,12},{12,8},{16,20},{20,16},{24,28},{28,24},{1,5},{5... | collective-permute-start | bytes 2211848 | tf_op jit(solution)/shard_map/ppermute | solution.py:765
  138.7 10.0 %collective-permute-start.17 = (bf16[960,384]{1,0:T(8,128)(2,1)}, bf16[960,384]{1,0:T(8,128)(2,1)}, u32[]{:S(2)}, u32[]{:S(2)}) collective-permute-start(bf16[960,384]{1,0:T(8,128)(2,1)} %collective-permute-done.13.rest_3_), channel_id=1, source_target_pairs={{0,4},{4,0},{8,12},{12,8},{16,20},{20,16},{24,28},{28,24},{1,5},{5... | collective-permute-start | bytes 2211848 | tf_op jit(solution)/shard_map/ppermute | solution.py:765
  145.5 33.9 %collective-permute-start.24 = (bf16[960,640]{1,0:T(8,128)(2,1)}, bf16[960,640]{1,0:T(8,128)(2,1)}, u32[]{:S(2)}, u32[]{:S(2)}) collective-permute-start(bf16[960,640]{1,0:T(8,128)(2,1)} %bitcast.15.rest_8_.rest_2_), channel_id=1, source_target_pairs={{0,16},{4,12},{8,24},{12,4},{16,0},{20,28},{24,8},{28,20},{1,17},{... | collective-permute-start | bytes 3686408 | tf_op jit(solution)/shard_map/ppermute | solution.py:765
  146.0 49.1 %collective-permute-start.33 = (bf16[4,480,640]{2,1,0:T(8,128)(2,1)S(1)}, bf16[4,480,640]{2,1,0:T(8,128)(2,1)}, u32[]{:S(2)}, u32[]{:S(2)}) collective-permute-start(bf16[4,480,640]{2,1,0:T(8,128)(2,1)S(1)} %stack.33.rest_16_), channel_id=1, source_target_pairs={{0,4},{4,0},{8,12},{12,8},{16,20},{20,16},{24,28},{28,24},{1,5},{5... | collective-permute-start | bytes 7372808 | tf_op jit(solution)/shard_map/ppermute | solution.py:765
  147.2 32.3 %collective-permute-start.25 = (bf16[960,640]{1,0:T(8,128)(2,1)}, bf16[960,640]{1,0:T(8,128)(2,1)}, u32[]{:S(2)}, u32[]{:S(2)}) collective-permute-start(bf16[960,640]{1,0:T(8,128)(2,1)} %collective-permute-done.23.rest_9_), channel_id=1, source_target_pairs={{0,16},{4,12},{8,24},{12,4},{16,0},{20,28},{24,8},{28,20},{1,17},{... | collective-permute-start | bytes 3686408 | tf_op jit(solution)/shard_map/ppermute | solution.py:765
  155.5 22.3 %collective-permute-start.21 = (bf16[640,256]{1,0:T(8,128)(2,1)}, bf16[640,256]{1,0:T(8,128)(2,1)S(1)}, u32[]{:S(2)}, u32[]{:S(2)}) collective-permute-start(bf16[640,256]{1,0:T(8,128)(2,1)} %get-tuple-element.104.kv2), channel_id=1, source_target_pairs={{0,1},{2,3},{4,5},{6,7},{8,9},{10,11},{12,13},{14,15},{16,17},{18,... | collective-permute-start | bytes 983048 | tf_op jit(solution)/shard_map/ppermute | solution.py:810
  178.9 16.2 %collective-permute-start.26 = (bf16[960,640]{1,0:T(8,128)(2,1)}, bf16[960,640]{1,0:T(8,128)(2,1)}, u32[]{:S(2)}, u32[]{:S(2)}) collective-permute-start(bf16[960,640]{1,0:T(8,128)(2,1)} %bitcast.15.rest_8_.rest_2_), channel_id=1, source_target_pairs={{0,4},{4,0},{8,12},{12,8},{16,20},{20,16},{24,28},{28,24},{1,5},{5... | collective-permute-start | bytes 3686408 | tf_op jit(solution)/shard_map/ppermute | solution.py:765
  179.4 15.7 %collective-permute-start.27 = (bf16[960,640]{1,0:T(8,128)(2,1)}, bf16[960,640]{1,0:T(8,128)(2,1)}, u32[]{:S(2)}, u32[]{:S(2)}) collective-permute-start(bf16[960,640]{1,0:T(8,128)(2,1)} %collective-permute-done.23.rest_9_), channel_id=1, source_target_pairs={{0,4},{4,0},{8,12},{12,8},{16,20},{20,16},{24,28},{28,24},{1,5},{5... | collective-permute-start | bytes 3686408 | tf_op jit(solution)/shard_map/ppermute | solution.py:765
  179.4 15.6 %collective-permute-start.28 = (bf16[960,640]{1,0:T(8,128)(2,1)}, bf16[960,640]{1,0:T(8,128)(2,1)}, u32[]{:S(2)}, u32[]{:S(2)}) collective-permute-start(bf16[960,640]{1,0:T(8,128)(2,1)} %collective-permute-done.24.rest_10_), channel_id=1, source_target_pairs={{0,4},{4,0},{8,12},{12,8},{16,20},{20,16},{24,28},{28,24},{1,5},{5... | collective-permute-start | bytes 3686408 | tf_op jit(solution)/shard_map/ppermute | solution.py:765
  181.2 13.8 %collective-permute-start.29 = (bf16[960,640]{1,0:T(8,128)(2,1)}, bf16[960,640]{1,0:T(8,128)(2,1)}, u32[]{:S(2)}, u32[]{:S(2)}) collective-permute-start(bf16[960,640]{1,0:T(8,128)(2,1)} %collective-permute-done.25.rest_11_), channel_id=1, source_target_pairs={{0,4},{4,0},{8,12},{12,8},{16,20},{20,16},{24,28},{28,24},{1,5},{5... | collective-permute-start | bytes 3686408 | tf_op jit(solution)/shard_map/ppermute | solution.py:765
  215.4 18.1 %collective-permute-start.34 = (bf16[640,256]{1,0:T(8,128)(2,1)}, bf16[640,256]{1,0:T(8,128)(2,1)S(1)}, u32[]{:S(2)}, u32[]{:S(2)}) collective-permute-start(bf16[640,256]{1,0:T(8,128)(2,1)} %get-tuple-element.108.kv2), channel_id=1, source_target_pairs={{0,1},{2,3},{4,5},{6,7},{8,9},{10,11},{12,13},{14,15},{16,17},{18,... | collective-permute-start | bytes 983048 | tf_op jit(solution)/shard_map/ppermute | solution.py:810
  225.0 41.3 %collective-permute-start.37 = (bf16[960,256]{1,0:T(8,128)(2,1)S(1)}, bf16[960,256]{1,0:T(8,128)(2,1)S(1)}, u32[]{:S(2)}, u32[]{:S(2)}) collective-permute-start(bf16[960,256]{1,0:T(8,128)(2,1)S(1)} %bitcast.67), channel_id=1, source_target_pairs={{0,0},{1,4},{2,1},{3,5},{4,2},{5,6},{6,3},{7,7},{8,8},{9,12},{10,9... | collective-permute-start | bytes 1474568 | tf_op jit(solution)/shard_map/ppermute | solution.py:781
  307.9 11.7 %collective-permute-start.39 = (bf16[640,256]{1,0:T(8,128)(2,1)S(1)}, bf16[640,256]{1,0:T(8,128)(2,1)S(1)}, u32[]{:S(2)}, u32[]{:S(2)}) collective-permute-start(bf16[640,256]{1,0:T(8,128)(2,1)S(1)} %fusion.1), channel_id=1, source_target_pairs={{1,0},{3,2},{5,4},{7,6},{9,8},{11,10},{13,12},{15,14},{17,16},{19,... | collective-permute-start | bytes 983048 | tf_op jit(solution)/shard_map/ppermute | solution.py:820
  309.2 37.8 %collective-permute-start.46 = (bf16[256,2560]{1,0:T(8,128)(2,1)}, bf16[256,2560]{1,0:T(8,128)(2,1)S(1)}, u32[]{:S(2)}, u32[]{:S(2)}) collective-permute-start(bf16[256,2560]{1,0:T(8,128)(2,1)} %get-tuple-element.142), channel_id=1, source_target_pairs={{0,4},{4,0},{8,12},{12,8},{16,20},{20,16},{24,28},{28,24},{1,5},{5... | collective-permute-start | bytes 3932168 | tf_op jit(solution)/shard_map/ppermute | solution.py:765
  359.0 37.6 %collective-permute-start.50 = (bf16[2,960,640]{2,1,0:T(8,128)(2,1)S(1)}, bf16[2,960,640]{2,1,0:T(8,128)(2,1)S(1)}, u32[]{:S(2)}, u32[]{:S(2)}) collective-permute-start(bf16[2,960,640]{2,1,0:T(8,128)(2,1)S(1)} %get-tuple-element.144.rest_8_), channel_id=1, source_target_pairs={{0,8},{4,20},{8,0},{12,28},{16,24},{20,4},{24,16},{28,12},{1,9},{5... | collective-permute-start | bytes 7372808 | tf_op jit(solution)/shard_map/ppermute | solution.py:765
  384.2 11.6 %collective-permute-start.49 = (bf16[640,256]{1,0:T(8,128)(2,1)S(1)}, bf16[640,256]{1,0:T(8,128)(2,1)S(1)}, u32[]{:S(2)}, u32[]{:S(2)}) collective-permute-start(bf16[640,256]{1,0:T(8,128)(2,1)S(1)} %fusion.2), channel_id=1, source_target_pairs={{1,0},{3,2},{5,4},{7,6},{9,8},{11,10},{13,12},{15,14},{17,16},{19,... | collective-permute-start | bytes 983048 | tf_op jit(solution)/shard_map/ppermute | solution.py:820
  385.5 21.9 %collective-permute-start.58 = (bf16[256,960]{1,0:T(8,128)(2,1)}, bf16[256,960]{1,0:T(8,128)(2,1)}, u32[]{:S(2)}, u32[]{:S(2)}) collective-permute-start(bf16[256,960]{1,0:T(8,128)(2,1)} %get-tuple-element.157.rest_0_), channel_id=1, source_target_pairs={{0,4},{4,0},{8,12},{12,8},{16,20},{20,16},{24,28},{28,24},{1,5},{5... | collective-permute-start | bytes 1474568 | tf_op jit(solution)/shard_map/ppermute | solution.py:765
  385.7 22.6 %collective-permute-start.61 = (bf16[256,960]{1,0:T(8,128)(2,1)}, bf16[256,960]{1,0:T(8,128)(2,1)}, u32[]{:S(2)}, u32[]{:S(2)}) collective-permute-start(bf16[256,960]{1,0:T(8,128)(2,1)} %get-tuple-element.160.rest_5_), channel_id=1, source_target_pairs={{0,4},{4,0},{8,12},{12,8},{16,20},{20,16},{24,28},{28,24},{1,5},{5... | collective-permute-start | bytes 1474568 | tf_op jit(solution)/shard_map/ppermute | solution.py:765
  386.1 22.4 %collective-permute-start.62 = (bf16[3,256,384]{2,1,0:T(8,128)(2,1)}, bf16[3,256,384]{2,1,0:T(8,128)(2,1)S(1)}, u32[]{:S(2)}, u32[]{:S(2)}) collective-permute-start(bf16[3,256,384]{2,1,0:T(8,128)(2,1)} %get-tuple-element.165), channel_id=1, source_target_pairs={{0,4},{4,0},{8,12},{12,8},{16,20},{20,16},{24,28},{28,24},{1,5},{5... | collective-permute-start | bytes 1769480 | tf_op jit(solution)/shard_map/ppermute | solution.py:765
  396.6 12.8 %collective-permute-start.63 = (bf16[3,256,384]{2,1,0:T(8,128)(2,1)}, bf16[3,256,384]{2,1,0:T(8,128)(2,1)S(1)}, u32[]{:S(2)}, u32[]{:S(2)}) collective-permute-start(bf16[3,256,384]{2,1,0:T(8,128)(2,1)} %get-tuple-element.166), channel_id=1, source_target_pairs={{0,4},{4,0},{8,12},{12,8},{16,20},{20,16},{24,28},{28,24},{1,5},{5... | collective-permute-start | bytes 1769480 | tf_op jit(solution)/shard_map/ppermute | solution.py:765
  396.6 11.9 %collective-permute-start.60 = (bf16[256,960]{1,0:T(8,128)(2,1)}, bf16[256,960]{1,0:T(8,128)(2,1)}, u32[]{:S(2)}, u32[]{:S(2)}) collective-permute-start(bf16[256,960]{1,0:T(8,128)(2,1)} %get-tuple-element.159.rest_4_), channel_id=1, source_target_pairs={{0,4},{4,0},{8,12},{12,8},{16,20},{20,16},{24,28},{28,24},{1,5},{5... | collective-permute-start | bytes 1474568 | tf_op jit(solution)/shard_map/ppermute | solution.py:765
  423.3 32.6 %collective-permute-start.66 = (bf16[2,960,384]{2,1,0:T(8,128)(2,1)S(1)}, bf16[2,960,384]{2,1,0:T(8,128)(2,1)S(1)}, u32[]{:S(2)}, u32[]{:S(2)}) collective-permute-start(bf16[2,960,384]{2,1,0:T(8,128)(2,1)S(1)} %get-tuple-element.170.rest_0_), channel_id=1, source_target_pairs={{0,8},{4,20},{8,0},{12,28},{16,24},{20,4},{24,16},{28,12},{1,9},{5... | collective-permute-start | bytes 4423688 | tf_op jit(solution)/shard_map/ppermute | solution.py:765
  424.0 29.9 %collective-permute-start.67 = (bf16[960,640]{1,0:T(8,128)(2,1)S(1)}, bf16[960,640]{1,0:T(8,128)(2,1)S(1)}, u32[]{:S(2)}, u32[]{:S(2)}) collective-permute-start(bf16[960,640]{1,0:T(8,128)(2,1)S(1)} %copy-done.37), channel_id=1, source_target_pairs={{0,16},{4,12},{8,24},{12,4},{16,0},{20,28},{24,8},{28,20},{1,17},{... | collective-permute-start | bytes 3686408 | tf_op jit(solution)/shard_map/ppermute | solution.py:765
  425.6 33.3 %collective-permute-start.69 = (bf16[960,640]{1,0:T(8,128)(2,1)S(1)}, bf16[960,640]{1,0:T(8,128)(2,1)S(1)}, u32[]{:S(2)}, u32[]{:S(2)}) collective-permute-start(bf16[960,640]{1,0:T(8,128)(2,1)S(1)} %copy-done.77), channel_id=1, source_target_pairs={{0,1},{3,0},{5,6},{6,7},{8,9},{11,8},{13,14},{14,15},{16,17},{19,1... | collective-permute-start | bytes 3686408 | tf_op jit(solution)/shard_map/ppermute | solution.py:847
  427.6 45.4 %collective-permute-start.70 = (bf16[960,640]{1,0:T(8,128)(2,1)S(1)}, bf16[960,640]{1,0:T(8,128)(2,1)S(1)}, u32[]{:S(2)}, u32[]{:S(2)}) collective-permute-start(bf16[960,640]{1,0:T(8,128)(2,1)S(1)} %get-tuple-element.145.rest_0_), channel_id=1, source_target_pairs={{2,0},{3,1},{4,6},{5,7},{10,8},{11,9},{12,14},{13,15},{18,16},{19,... | collective-permute-start | bytes 3686408 | tf_op jit(solution)/shard_map/ppermute | solution.py:847
  428.9 44.1 %collective-permute-start.71 = (bf16[960,640]{1,0:T(8,128)(2,1)S(1)}, bf16[960,640]{1,0:T(8,128)(2,1)S(1)}, u32[]{:S(2)}, u32[]{:S(2)}) collective-permute-start(bf16[960,640]{1,0:T(8,128)(2,1)S(1)} %copy-done.77), channel_id=1, source_target_pairs={{1,0},{2,1},{4,7},{7,6},{9,8},{10,9},{12,15},{15,14},{17,16},{18,1... | collective-permute-start | bytes 3686408 | tf_op jit(solution)/shard_map/ppermute | solution.py:847
  456.8 69.0 %collective-permute-start.68 = (bf16[960,384]{1,0:T(8,128)(2,1)S(1)}, bf16[960,384]{1,0:T(8,128)(2,1)S(1)}, u32[]{:S(2)}, u32[]{:S(2)}) collective-permute-start(bf16[960,384]{1,0:T(8,128)(2,1)S(1)} %get-tuple-element.174.rest_3_), channel_id=1, source_target_pairs={{0,16},{4,12},{8,24},{12,4},{16,0},{20,28},{24,8},{28,20},{1,17},{... | collective-permute-start | bytes 2211848 | tf_op jit(solution)/shard_map/ppermute | solution.py:765
  475.4 22.2 %collective-permute-start.36 = (bf16[960,256]{1,0:T(8,128)(2,1)S(1)}, bf16[960,256]{1,0:T(8,128)(2,1)S(1)}, u32[]{:S(2)}, u32[]{:S(2)}) collective-permute-start(bf16[960,256]{1,0:T(8,128)(2,1)S(1)} %copy-done.94), channel_id=1, source_target_pairs={{0,0},{4,1},{1,2},{5,3},{2,4},{6,5},{3,6},{7,7},{8,8},{12,9},{9,10... | collective-permute-start | bytes 1474568 | tf_op jit(solution)/shard_map/ppermute | solution.py:781
  477.3 79.8 %collective-permute-start.51 = (bf16[960,256]{1,0:T(8,128)(2,1)S(1)}, bf16[960,256]{1,0:T(8,128)(2,1)S(1)}, u32[]{:S(2)}, u32[]{:S(2)}) collective-permute-start(bf16[960,256]{1,0:T(8,128)(2,1)S(1)} %copy-done.95), channel_id=1, source_target_pairs={{0,0},{4,1},{1,2},{5,3},{2,4},{6,5},{3,6},{7,7},{8,8},{12,9},{9,10... | collective-permute-start | bytes 1474568 | tf_op jit(solution)/shard_map/ppermute | solution.py:781
  480.5 15.5 %collective-permute-start.54 = (f32[2,960]{1,0:T(2,128)S(1)}, f32[2,960]{1,0:T(2,128)S(1)}, u32[]{:S(2)}, u32[]{:S(2)}) collective-permute-start(f32[2,960]{1,0:T(2,128)S(1)} %fusion.6), channel_id=1, source_target_pairs={{0,16},{4,20},{8,24},{12,28},{16,0},{20,4},{24,8},{28,12},{1,17},{... | collective-permute-start | bytes 23048 | tf_op jit(solution)/shard_map/ppermute | solution.py:765
  481.0 46.0 %collective-permute-start.78 = (bf16[240,640]{1,0:T(8,128)(2,1)S(1)}, bf16[240,640]{1,0:T(8,128)(2,1)S(1)}, u32[]{:S(2)}, u32[]{:S(2)}) collective-permute-start(bf16[240,640]{1,0:T(8,128)(2,1)S(1)} %get-tuple-element.186), channel_id=1, source_target_pairs={{0,1},{1,2},{2,3},{3,0},{4,5},{5,6},{6,7},{7,4},{8,9},{9,10},{10,1... | collective-permute-start | bytes 921608 | tf_op jit(solution)/shard_map/ppermute | solution.py:770
  496.1 32.7 %collective-permute-start.76 = (bf16[2,120,640]{2,1,0:T(8,128)(2,1)S(1)}, bf16[2,120,640]{2,1,0:T(8,128)(2,1)S(1)}, u32[]{:S(2)}, u32[]{:S(2)}) collective-permute-start(bf16[2,120,640]{2,1,0:T(8,128)(2,1)S(1)} %get-tuple-element.178.rest_0_), channel_id=1, source_target_pairs={{0,8},{4,20},{8,0},{12,28},{16,24},{20,4},{24,16},{28,12},{1,9},{5... | collective-permute-start | bytes 921608 | tf_op jit(solution)/shard_map/ppermute | solution.py:765
  497.6 12.4 %collective-permute-start.55 = (f32[2,960]{1,0:T(2,128)S(1)}, f32[2,960]{1,0:T(2,128)S(1)}, u32[]{:S(2)}, u32[]{:S(2)}) collective-permute-start(f32[2,960]{1,0:T(2,128)S(1)} %add.118), channel_id=1, source_target_pairs={{0,1},{1,2},{2,3},{3,0},{4,5},{5,6},{6,7},{7,4},{8,9},{9,10},{10,1... | collective-permute-start | bytes 23048 | tf_op jit(solution)/shard_map/ppermute | solution.py:770
  510.0 12.8 %collective-permute-start.56 = (f32[2,960]{1,0:T(2,128)S(1)}, f32[2,960]{1,0:T(2,128)S(1)}, u32[]{:S(2)}, u32[]{:S(2)}) collective-permute-start(f32[2,960]{1,0:T(2,128)S(1)} %add.118), channel_id=1, source_target_pairs={{0,2},{1,3},{2,0},{3,1},{4,6},{5,7},{6,4},{7,5},{8,10},{9,11},{10,... | collective-permute-start | bytes 23048 | tf_op jit(solution)/shard_map/ppermute | solution.py:770
  522.8 18.2 %collective-permute-start.79 = (bf16[240,640]{1,0:T(8,128)(2,1)S(1)}, bf16[240,640]{1,0:T(8,128)(2,1)S(1)}, u32[]{:S(2)}, u32[]{:S(2)}) collective-permute-start(bf16[240,640]{1,0:T(8,128)(2,1)S(1)} %get-tuple-element.187), channel_id=1, source_target_pairs={{0,2},{1,3},{2,0},{3,1},{4,6},{5,7},{6,4},{7,5},{8,10},{9,11},{10,... | collective-permute-start | bytes 921608 | tf_op jit(solution)/shard_map/ppermute | solution.py:770
  525.8 15.7 %collective-permute-start.80 = (bf16[240,640]{1,0:T(8,128)(2,1)S(1)}, bf16[240,640]{1,0:T(8,128)(2,1)S(1)}, u32[]{:S(2)}, u32[]{:S(2)}) collective-permute-start(bf16[240,640]{1,0:T(8,128)(2,1)S(1)} %get-tuple-element.188), channel_id=1, source_target_pairs={{0,3},{1,0},{2,1},{3,2},{4,7},{5,4},{6,5},{7,6},{8,11},{9,8},{10,9... | collective-permute-start | bytes 921608 | tf_op jit(solution)/shard_map/ppermute | solution.py:770
  527.0 31.7 %collective-permute-start.73 = (bf16[240,384]{1,0:T(8,128)(2,1)S(1)}, bf16[240,384]{1,0:T(8,128)(2,1)S(1)}, u32[]{:S(2)}, u32[]{:S(2)}) collective-permute-start(bf16[240,384]{1,0:T(8,128)(2,1)S(1)} %get-tuple-element.180), channel_id=1, source_target_pairs={{0,1},{1,2},{2,3},{3,0},{4,5},{5,6},{6,7},{7,4},{8,9},{9,10},{10,1... | collective-permute-start | bytes 552968 | tf_op jit(solution)/shard_map/ppermute | solution.py:770
  528.7 31.5 %collective-permute-start.74 = (bf16[240,384]{1,0:T(8,128)(2,1)S(1)}, bf16[240,384]{1,0:T(8,128)(2,1)S(1)}, u32[]{:S(2)}, u32[]{:S(2)}) collective-permute-start(bf16[240,384]{1,0:T(8,128)(2,1)S(1)} %get-tuple-element.181), channel_id=1, source_target_pairs={{0,2},{1,3},{2,0},{3,1},{4,6},{5,7},{6,4},{7,5},{8,10},{9,11},{10,... | collective-permute-start | bytes 552968 | tf_op jit(solution)/shard_map/ppermute | solution.py:770
  541.0 19.2 %collective-permute-start.77 = (bf16[120,640]{1,0:T(8,128)(2,1)S(1)}, bf16[120,640]{1,0:T(8,128)(2,1)S(1)}, u32[]{:S(2)}, u32[]{:S(2)}) collective-permute-start(bf16[120,640]{1,0:T(8,128)(2,1)S(1)} %get-tuple-element.185.rest_3_), channel_id=1, source_target_pairs={{0,16},{4,12},{8,24},{12,4},{16,0},{20,28},{24,8},{28,20},{1,17},{... | collective-permute-start | bytes 460808 | tf_op jit(solution)/shard_map/ppermute | solution.py:765
  541.5 15.2 %collective-permute-start.57 = (f32[2,960]{1,0:T(2,128)S(1)}, f32[2,960]{1,0:T(2,128)S(1)}, u32[]{:S(2)}, u32[]{:S(2)}) collective-permute-start(f32[2,960]{1,0:T(2,128)S(1)} %add.118), channel_id=1, source_target_pairs={{0,3},{1,0},{2,1},{3,2},{4,7},{5,4},{6,5},{7,6},{8,11},{9,8},{10,9... | collective-permute-start | bytes 23048 | tf_op jit(solution)/shard_map/ppermute | solution.py:770
  556.7 16.8 %collective-permute-start.96 = (bf16[240,640]{1,0:T(8,128)(2,1)S(1)}, bf16[240,640]{1,0:T(8,128)(2,1)S(1)}, u32[]{:S(2)}, u32[]{:S(2)}) collective-permute-start(bf16[240,640]{1,0:T(8,128)(2,1)S(1)} %sum_ring.2.rest_0_), channel_id=1, source_target_pairs={{0,16},{4,12},{8,24},{12,4},{16,0},{20,28},{24,8},{28,20},{1,17},{... | collective-permute-start | bytes 921608 | tf_op jit(solution)/shard_map/ppermute | solution.py:765
  557.2 17.4 %collective-permute-start.97 = (bf16[240,640]{1,0:T(8,128)(2,1)S(1)}, bf16[240,640]{1,0:T(8,128)(2,1)S(1)}, u32[]{:S(2)}, u32[]{:S(2)}) collective-permute-start(bf16[240,640]{1,0:T(8,128)(2,1)S(1)} %sum_ring.2.rest_0_), channel_id=1, source_target_pairs={{0,24},{4,28},{8,16},{12,20},{16,8},{20,12},{24,0},{28,4},{1,25},{... | collective-permute-start | bytes 921608 | tf_op jit(solution)/shard_map/ppermute | solution.py:765
  558.7 17.4 %collective-permute-start.95 = (bf16[240,640]{1,0:T(8,128)(2,1)S(1)}, bf16[240,640]{1,0:T(8,128)(2,1)S(1)}, u32[]{:S(2)}, u32[]{:S(2)}) collective-permute-start(bf16[240,640]{1,0:T(8,128)(2,1)S(1)} %sum_ring.2.rest_0_), channel_id=1, source_target_pairs={{0,8},{4,20},{8,0},{12,28},{16,24},{20,4},{24,16},{28,12},{1,9},{5... | collective-permute-start | bytes 921608 | tf_op jit(solution)/shard_map/ppermute | solution.py:765
  560.2 17.5 %collective-permute-start.98 = (bf16[240,640]{1,0:T(8,128)(2,1)S(1)}, bf16[240,640]{1,0:T(8,128)(2,1)S(1)}, u32[]{:S(2)}, u32[]{:S(2)}) collective-permute-start(bf16[240,640]{1,0:T(8,128)(2,1)S(1)} %sum_ring.2.rest_0_), channel_id=1, source_target_pairs={{0,4},{4,0},{8,12},{12,8},{16,20},{20,16},{24,28},{28,24},{1,5},{5... | collective-permute-start | bytes 921608 | tf_op jit(solution)/shard_map/ppermute | solution.py:765
  567.5 10.3 %collective-permute-start.88 = (bf16[120,640]{1,0:T(8,128)(2,1)S(1)}, bf16[120,640]{1,0:T(8,128)(2,1)S(1)}, u32[]{:S(2)}, u32[]{:S(2)}) collective-permute-start(bf16[120,640]{1,0:T(8,128)(2,1)S(1)} %sum_two.1.rest_3_.rest_0_), channel_id=1, source_target_pairs={{0,8},{4,20},{8,0},{12,28},{16,24},{20,4},{24,16},{28,12},{1,9},{5... | collective-permute-start | bytes 460808 | tf_op jit(solution)/shard_map/ppermute | solution.py:765
  574.5 11.2 %collective-permute-start.81 = (bf16[240,384]{1,0:T(8,128)(2,1)S(1)}, bf16[240,384]{1,0:T(8,128)(2,1)S(1)}, u32[]{:S(2)}, u32[]{:S(2)}) collective-permute-start(bf16[240,384]{1,0:T(8,128)(2,1)S(1)} %sum_ring.3.rest_8_.rest_0_), channel_id=1, source_target_pairs={{0,8},{4,20},{8,0},{12,28},{16,24},{20,4},{24,16},{28,12},{1,9},{5... | collective-permute-start | bytes 552968 | tf_op jit(solution)/shard_map/ppermute | solution.py:765
  577.8 11.2 %collective-permute-start.82 = (bf16[240,384]{1,0:T(8,128)(2,1)S(1)}, bf16[240,384]{1,0:T(8,128)(2,1)S(1)}, u32[]{:S(2)}, u32[]{:S(2)}) collective-permute-start(bf16[240,384]{1,0:T(8,128)(2,1)S(1)} %sum_ring.3.rest_8_.rest_0_), channel_id=1, source_target_pairs={{0,16},{4,12},{8,24},{12,4},{16,0},{20,28},{24,8},{28,20},{1,17},{... | collective-permute-start | bytes 552968 | tf_op jit(solution)/shard_map/ppermute | solution.py:765
  578.9 10.1 %collective-permute-start.83 = (bf16[240,384]{1,0:T(8,128)(2,1)S(1)}, bf16[240,384]{1,0:T(8,128)(2,1)S(1)}, u32[]{:S(2)}, u32[]{:S(2)}) collective-permute-start(bf16[240,384]{1,0:T(8,128)(2,1)S(1)} %sum_ring.3.rest_8_.rest_0_), channel_id=1, source_target_pairs={{0,24},{4,28},{8,16},{12,20},{16,8},{20,12},{24,0},{28,4},{1,25},{... | collective-permute-start | bytes 552968 | tf_op jit(solution)/shard_map/ppermute | solution.py:765
  590.3 10.4 %collective-permute-start.84 = (bf16[240,384]{1,0:T(8,128)(2,1)S(1)}, bf16[240,384]{1,0:T(8,128)(2,1)S(1)}, u32[]{:S(2)}, u32[]{:S(2)}) collective-permute-start(bf16[240,384]{1,0:T(8,128)(2,1)S(1)} %sum_ring.3.rest_8_.rest_0_), channel_id=1, source_target_pairs={{0,4},{4,0},{8,12},{12,8},{16,20},{20,16},{24,28},{28,24},{1,5},{5... | collective-permute-start | bytes 552968 | tf_op jit(solution)/shard_map/ppermute | solution.py:765
  590.9 9.9 %collective-permute-start.85 = (bf16[240,384]{1,0:T(8,128)(2,1)S(1)}, bf16[240,384]{1,0:T(8,128)(2,1)S(1)}, u32[]{:S(2)}, u32[]{:S(2)}) collective-permute-start(bf16[240,384]{1,0:T(8,128)(2,1)S(1)} %collective-permute-done.81.rest_1_), channel_id=1, source_target_pairs={{0,4},{4,0},{8,12},{12,8},{16,20},{20,16},{24,28},{28,24},{1,5},{5... | collective-permute-start | bytes 552968 | tf_op jit(solution)/shard_map/ppermute | solution.py:765
  (137 other events, 1174.9 us)

commit v5 on v4

--- a/solution.py
+++ b/solution.py
@@ -9,11 +9,13 @@
 f32, bf16 = jnp.float32, jnp.bfloat16
 eps = 1e-05
 HEADS, KV_HEADS, HEAD_DIM, GROUP, KVW = 15, 5, 64, 3, 320
+IDS = 16
 PIECE = 384
 LIMIT = 58 << 20
 WHOLE = pl.BlockSpec(memory_space=pltpu.VMEM)
 LEFT = pl.BlockSpec(memory_space=pl.ANY)
 SCALARS = pl.BlockSpec(memory_space=pltpu.SMEM)
+BRIEF = pl.CostEstimate(flops=1024, bytes_accessed=1024, transcendentals=0)
 
 
 def contract(a, b, i, j):
@@ -76,27 +78,29 @@
     return jnp.concatenate(out, axis=0)
 
 
-def project(state, gain_ref, cos_ref, sin_ref, kept, sems, a_ref, q_ref, kv_ref):
+def project(state, gain_ref, cos_ref, sin_ref, ids, kept, sems, a_ref, q_ref, kv_ref):
     a = normed(state, gain_ref[...]).astype(bf16)
     a_ref[...] = a
     cos, sin = cos_ref[...], sin_ref[...]
     arrived(kept, sems, 0, 3)
     kv_ref[:KVW, :] = rope(nn(a, kept[0, 3, :, :KVW]).T, cos, sin, False).astype(bf16)
     arrived(kept, sems, 1, 0)
-    kv_ref[KVW:, :] = nn(a, kept[1, 0, :, :KVW]).T.astype(bf16)
+    kv_ref[2 * KVW :, :] = ids
+    kv_ref[KVW : 2 * KVW, :] = nn(a, kept[1, 0, :, :KVW]).T.astype(bf16)
     for m in range(3):
         arrived(kept, sems, 0, m)
         q_ref[pl.ds(m * KVW, KVW), :] = rope(nn(a, kept[0, m, :, :KVW]).T, cos, sin, False).astype(bf16)
 
 
 def pre_kernel(sc, ht_ref, gain_ref, cos_ref, sin_ref, *rest):
+    width = ht_ref.shape[0] - IDS
     mine, other = rest[:4], rest[4:8]
     h_ref, a_ref, q_ref, kv_ref, kept, sems = rest[-6:]
     core, chip = sc[0], sc[1]
     fetch(mine, other, kept, sems, core, chip)
-    h = ht_ref[...].T
+    h = ht_ref[:width, :].T
     h_ref[...] = h
-    project(h.astype(f32), gain_ref, cos_ref, sin_ref, kept, sems, a_ref, q_ref, kv_ref)
+    project(h.astype(f32), gain_ref, cos_ref, sin_ref, ht_ref[width:, :], kept, sems, a_ref, q_ref, kv_ref)
     for m in range(1, 4):
         arrived(kept, sems, 1, m)
 
@@ -110,20 +114,23 @@
 
 
 def pre(sc, ht, gain, cos, sin, mine_a, other_a, after):
-    width, n = ht.shape
+    width, n = ht.shape[0] - IDS, ht.shape[1]
     return pl.pallas_call(
         pre_kernel,
-        out_shape=(shape((n, width), bf16), shape((n, width), bf16), shape((width, n), bf16), shape((2 * KVW, n), bf16)),
+        out_shape=(shape((n, width), bf16), shape((n, width), bf16), shape((width, n), bf16), shape((2 * KVW + IDS, n), bf16)),
         in_specs=[SCALARS] + [WHOLE] * 4 + [LEFT] * (8 + len(after)),
         out_specs=(WHOLE,) * 4,
         scratch_shapes=scratch_a(width),
+        cost_estimate=BRIEF,
         compiler_params=pltpu.CompilerParams(vmem_limit_bytes=LIMIT),
         name="pre",
     )(sc, ht, gain, cos, sin, *mine_a, *other_a, *after)
 
 
-def bias_of(seg_k, seg_q):
-    keys, n = seg_k.shape[0], seg_q.shape[1]
+def bias_of(kv):
+    keys, n = kv.shape[1], kv.shape[1] // 3
+    ids = kv[2 * KVW :, :].astype(f32)
+    seg_k, seg_q = ids.T[:, :1], ids[:1, 2 * n :]
     j = lax.broadcasted_iota(jnp.int32, (keys, n), 0)
     i = lax.broadcasted_iota(jnp.int32, (keys, n), 1) + (keys - n)
     return jnp.where((seg_k == seg_q) & (j <= i), 0.0, -1e30).astype(f32)
@@ -135,9 +142,9 @@
         whole[:, w * n : (w + 1) * n] = part[...]
 
 
-def attend_kernel(q_ref, kv0, kv1, kv2, sk_ref, sq_ref, o_ref, lse_ref, bias, kv):
-    bias[...] = bias_of(sk_ref[...], sq_ref[...])
+def attend_kernel(q_ref, kv0, kv1, kv2, o_ref, lse_ref, bias, kv):
     window_of((kv0, kv1, kv2), kv)
+    bias[...] = bias_of(kv)
 
     def head(e, _):
         row = pl.multiple_of(e * HEAD_DIM, HEAD_DIM)
@@ -158,24 +165,25 @@
     lax.fori_loop(0, KV_HEADS, head, 0)
 
 
-def attend(q, kvs, seg_k, seg_q):
+def attend(q, kvs):
     width, n = q.shape
     return pl.pallas_call(
         attend_kernel,
         out_shape=(shape((width, n), bf16), shape((HEADS, n), f32)),
-        in_specs=[WHOLE] * 6,
+        in_specs=[WHOLE] * 4,
         out_specs=(WHOLE,) * 2,
-        scratch_shapes=[pltpu.VMEM((3 * n, n), f32), pltpu.VMEM((2 * KVW, 3 * n), bf16)],
+        scratch_shapes=[pltpu.VMEM((3 * n, n), f32), pltpu.VMEM((2 * KVW + IDS, 3 * n), bf16)],
+        cost_estimate=BRIEF,
         compiler_params=pltpu.CompilerParams(vmem_limit_bytes=24 << 20),
         name="attend",
-    )(q, *kvs, seg_k, seg_q)
-
-
-def attend_back_kernel(sc, p_ref, q_ref, kv0, kv1, kv2, sk_ref, sq_ref, lse_ref, do_ref, cos_ref, sin_ref, *rest):
+    )(q, *kvs)
+
+
+def attend_back_kernel(sc, p_ref, q_ref, kv0, kv1, kv2, lse_ref, do_ref, cos_ref, sin_ref, *rest):
     dq_ref, three_ref, far_ref, near_ref, own_ref, bias, kv, dqs = rest[-8:]
     n = q_ref.shape[1]
-    bias[...] = bias_of(sk_ref[...], sq_ref[...])
     window_of((kv0, kv1, kv2), kv)
+    bias[...] = bias_of(kv)
     scale = HEAD_DIM ** (-0.5)
 
     def head(e, _):
@@ -209,32 +217,38 @@
         three_ref[m] = jnp.where(sc[0] == 0, p_ref[m], dq)
 
 
-def attend_back(sc, p, q, kvs, seg_k, seg_q, lse, do, cos, sin, after=()):
+def attend_back(sc, p, q, kvs, lse, do, cos, sin, after=()):
     width, n = q.shape
     block = (2 * KVW, n)
     return pl.pallas_call(
         attend_back_kernel,
         out_shape=(shape((3, n, PIECE), bf16), shape((3, n, PIECE), bf16), shape(block, f32), shape(block, bf16), shape(block, f32)),
-        in_specs=[SCALARS] + [WHOLE] * 11 + [LEFT] * len(after),
+        in_specs=[SCALARS] + [WHOLE] * 9 + [LEFT] * len(after),
         out_specs=(WHOLE,) * 5,
-        scratch_shapes=[pltpu.VMEM((3 * n, n), f32), pltpu.VMEM((2 * KVW, 3 * n), bf16), pltpu.VMEM((width, n), f32)],
+        scratch_shapes=[pltpu.VMEM((3 * n, n), f32), pltpu.VMEM((2 * KVW + IDS, 3 * n), bf16), pltpu.VMEM((width, n), f32)],
+        cost_estimate=BRIEF,
         compiler_params=pltpu.CompilerParams(vmem_limit_bytes=32 << 20),
         name="attend_back",
-    )(sc, p, q, *kvs, seg_k, seg_q, lse, do, cos, sin, *after)
-
-
-def fetch_ffn(mine_b, other_b, mine_d, other_d, wb, wd, sem_b, sem_d, core, chip):
+    )(sc, p, q, *kvs, lse, do, cos, sin, *after)
+
+
+def fetch_ffn(mine_b, other_b, down, wb, wd, sem_b, sem_d, core, chip):
     fetch(mine_b, other_b, wb, sem_b, core, chip)
-    half = mine_d.shape[1]
-    for c, part, sem in ((core, mine_d, 0), (1 - core, other_d, 1)):
-        rows = pl.ds(pl.multiple_of(c * half, half), half)
-        pltpu.make_async_copy(part, wd.at[:, rows], sem_d.at[sem]).start()
-
-
-def arrived_down(mine_d, wd, sem_d):
-    half = mine_d.shape[1]
-    for c in range(2):
-        pltpu.make_async_copy(mine_d, wd.at[:, c * half : (c + 1) * half], sem_d.at[c]).wait()
+    half, n, width = down[0].shape[1], down[2].shape[1], wd.shape[1]
+
+    def copy(part, row, size):
+        rows = pl.ds(pl.multiple_of(row, 16), size)
+        pltpu.make_async_copy(part, wd.at[:, rows], sem_d).start()
+
+    copy(down[0], core * half, half)
+    copy(down[1], (1 - core) * half, half)
+    for kind, parts in ((core, down[2:6]), (1 - core, down[6:10])):
+        for who, part in zip(whose(kind), parts):
+            copy(part, 2 * half + (kind * 4 + (chip ^ who)) * n, n)
+
+
+def arrived_down(wd, sem_d):
+    pltpu.make_async_copy(wd, wd, sem_d).wait()
 
 
 def scratch_ffn(width, n):
@@ -242,19 +256,19 @@
         pltpu.VMEM((2, 4, width, n), bf16),
         pltpu.SemaphoreType.DMA((2, 4)),
         pltpu.VMEM((4, width, n), bf16),
-        pltpu.SemaphoreType.DMA((2,)),
+        pltpu.SemaphoreType.DMA,
     ]
 
 
 def post_kernel(last, sc, ot_ref, h_ref, gain_ref, gain_a, cos_ref, sin_ref, *rest):
     mine_a, other_a, mine_b, other_b = rest[:4], rest[4:8], rest[8:12], rest[12:16]
-    mine_d, other_d = rest[16:18]
-    o_ref, h1_ref, b_ref, gate_ref, up_ref, z_ref, next_ref = rest[18:25]
-    more, rest = rest[25 : 25 + (0 if last else 3)], rest[25 + (0 if last else 3) :]
+    down, ids_ref = rest[16:26], rest[26]
+    o_ref, h1_ref, b_ref, gate_ref, up_ref, z_ref, next_ref = rest[27:34]
+    more, rest = rest[34 : 34 + (0 if last else 3)], rest[34 + (0 if last else 3) :]
     wa, sem_a, wb, sem_b, wd, sem_d = rest
     core, chip = sc[0], sc[1]
     fetch(mine_a, other_a, wa, sem_a, core, chip)
-    fetch_ffn(mine_b, other_b, mine_d, other_d, wb, wd, sem_b, sem_d, core, chip)
+    fetch_ffn(mine_b, other_b, down, wb, wd, sem_b, sem_d, core, chip)
     o = ot_ref[...].T
     o_ref[...] = o
     for m in range(1, 4):
@@ -276,7 +290,7 @@
         z = (gate / (1.0 + jnp.exp(-gate)) * up).astype(bf16)
         z_ref[:, cols] = z
         if m == 0:
-            arrived_down(mine_d, wd, sem_d)
+            arrived_down(wd, sem_d)
         total = total + nt(z, wd[m])
     next_ref[...] = total.astype(bf16).T if last else total
     if last:
@@ -284,28 +298,29 @@
         for m in range(4):
             arrived(wa, sem_a, 0, m)
     else:
-        project(total, gain_a, cos_ref, sin_ref, wa, sem_a, *more)
-
-
-def post(last, sc, ot, h, gain, gain_a, cos, sin, wa, wb, wd):
+        project(total, gain_a, cos_ref, sin_ref, ids_ref[2 * KVW :, :], wa, sem_a, *more)
+
+
+def post(last, sc, ot, h, gain, gain_a, cos, sin, kv, wa, wb, wd):
     width, n = ot.shape
     hidden = wb[0][0].shape[1] * 4
     outs = [shape((n, width), bf16), shape((n, width), f32), shape((n, width), bf16)] + [shape((n, hidden), bf16)] * 3
     outs += [shape((width, n), bf16) if last else shape((n, width), f32)]
     if not last:
-        outs += [shape((n, width), bf16), shape((width, n), bf16), shape((2 * KVW, n), bf16)]
+        outs += [shape((n, width), bf16), shape((width, n), bf16), shape((2 * KVW + IDS, n), bf16)]
     return pl.pallas_call(
         functools.partial(post_kernel, last),
         out_shape=tuple(outs),
-        in_specs=[SCALARS] + [WHOLE] * 6 + [LEFT] * 18,
+        in_specs=[SCALARS] + [WHOLE] * 6 + [LEFT] * 26 + [WHOLE],
         out_specs=(WHOLE,) * len(outs),
         scratch_shapes=scratch_a(width) + scratch_ffn(width, hidden // 4),
+        cost_estimate=BRIEF,
         compiler_params=pltpu.CompilerParams(vmem_limit_bytes=LIMIT),
         name="post",
-    )(sc, ot, h, gain, gain_a, cos, sin, *wa[0], *wa[1], *wb[0], *wb[1], *wd)
-
-
-def ffn_back(state, core, refs, weights, mine_d):
+    )(sc, ot, h, gain, gain_a, cos, sin, *wa[0], *wa[1], *wb[0], *wb[1], *wd, kv)
+
+
+def ffn_back(state, core, refs, weights):
     gate_ref, up_ref, h1_ref, gain_ref, z_ref, gb_ref, keep_ref, send_ref, zk_ref, zs_ref, g1_ref, p_ref, dgain_ref, do_ref = refs
     wa, sem_a, wb, sem_b, wd, sem_d = weights
     gb = state.astype(bf16)
@@ -316,7 +331,7 @@
     low, high = z_ref[:, :half], z_ref[:, half:]
     zk_ref[...] = jnp.where(first, low, high)
     zs_ref[...] = jnp.where(first, high, low)
-    arrived_down(mine_d, wd, sem_d)
+    arrived_down(wd, sem_d)
     db = None
     for m in range(4):
         cols = slice(m * n, (m + 1) * n)
@@ -387,7 +402,7 @@
     mine_a, other_a = take(4), take(4)
     if not end:
         mine_b, other_b = take(4), take(4)
-        mine_d, other_d = take(2)
+        down = take(10)
     if start:
         (g_ref,) = take(1)
     else:
@@ -405,7 +420,7 @@
     fetch(mine_a, other_a, wa, sem_a, core, chip)
     if not end:
         wb, sem_b, wd, sem_d = take(4)
-        fetch_ffn(mine_b, other_b, mine_d, other_d, wb, wd, sem_b, sem_d, core, chip)
+        fetch_ffn(mine_b, other_b, down, wb, wd, sem_b, sem_d, core, chip)
     if start:
         state = g_ref[...].T.astype(f32)
     else:
@@ -417,7 +432,7 @@
         g_out[...] = state.astype(bf16).T
         finish_a(wa, sem_a, (1, 1), (1, 2), (1, 3))
     else:
-        ffn_back(state, core, (*ins, *outs), (wa, sem_a, wb, sem_b, wd, sem_d), mine_d)
+        ffn_back(state, core, (*ins, *outs), (wa, sem_a, wb, sem_b, wd, sem_d))
         if start:
             finish_a(wa, sem_a, (1, 0), (0, 0), (0, 1), (0, 2), (0, 3))
 
@@ -430,7 +445,7 @@
     scratch = scratch_a(width)
     if not end:
         args += [*wb[0], *wb[1], *wd]
-        specs += [LEFT] * 10
+        specs += [LEFT] * 18
         scratch += scratch_ffn(width, wb[0][0].shape[1])
     args += list(tail)
     specs += [WHOLE] * len(tail)
@@ -455,6 +470,7 @@
         in_specs=specs,
         out_specs=(WHOLE,) * len(outs),
         scratch_shapes=scratch,
+        cost_estimate=BRIEF,
         compiler_params=pltpu.CompilerParams(vmem_limit_bytes=LIMIT),
         name="back_end" if end else ("back_start" if start else "back_join"),
     )(*args)
@@ -495,6 +511,7 @@
         in_specs=[SCALARS] + [WHOLE] * 8,
         out_specs=(WHOLE,) * 2,
         scratch_shapes=[pltpu.VMEM((width, 4 * n), bf16), pltpu.VMEM((4 * n, cols), bf16)],
+        cost_estimate=BRIEF,
         compiler_params=pltpu.CompilerParams(vmem_limit_bytes=36 << 20),
         name="grad_ffn",
     )(sc, *lefts, *rights)
@@ -521,6 +538,7 @@
         in_specs=[SCALARS] + [WHOLE] * 8 + [LEFT] * len(after),
         out_specs=(WHOLE,) * 2,
         scratch_shapes=[pltpu.VMEM((width, 4 * n), bf16), pltpu.VMEM((4 * n, cols), bf16)],
+        cost_estimate=BRIEF,
         compiler_params=pltpu.CompilerParams(vmem_limit_bytes=32 << 20),
         name="grad_down",
     )(sc, *lefts, *rights, *after)
@@ -529,10 +547,14 @@
 def grad_attention_kernel(sc, *rest):
     a_refs, o_refs, rest = rest[:4], rest[4:8], rest[8:]
     queries, keys, values, outs, threes, ones = (rest[i : i + 2] for i in range(0, 12, 2))
+    gain_a, gain_f = (rest[i : i + 2] for i in (12, 14))
     send_ref, keep_ref, left, right = rest[-4:]
     core, chip = sc[0], sc[1]
-    n = a_refs[0].shape[0]
+    n, width = a_refs[0].shape
     turned(left.at[0], a_refs)
+    gains = [g[0][...] + g[1][...] for g in (gain_a, gain_f)]
+    gains = jnp.concatenate([*gains, jnp.zeros((6, width), f32)], axis=0).T
+    gains = jnp.concatenate([gains, jnp.zeros((width, PIECE - KVW - 8), f32)], axis=1).astype(bf16)
 
     def fill(at, of_three, own_three, own_one, single):
         for j in range(2):
@@ -555,20 +577,22 @@
         out = send_ref if i < 2 else keep_ref
         which = jnp.where(m > 0, core, 0)
         out[i % 2] = nn(left[which], right[m]).astype(bf16)
-
-
-def grad_attention(sc, a, o, own, got, after):
+        out[i % 2, :, KVW:] = gains
+
+
+def grad_attention(sc, a, o, own, got, gains, after):
     n, width = a[0].shape
     out = shape((2, width, PIECE), bf16)
     return pl.pallas_call(
         grad_attention_kernel,
         out_shape=(out, out),
-        in_specs=[SCALARS] + [WHOLE] * 20 + [LEFT] * len(after),
+        in_specs=[SCALARS] + [WHOLE] * 24 + [LEFT] * len(after),
         out_specs=(WHOLE,) * 2,
         scratch_shapes=[pltpu.VMEM((2, width, 4 * n), bf16), pltpu.VMEM((4, 4 * n, PIECE), bf16)],
+        cost_estimate=BRIEF,
         compiler_params=pltpu.CompilerParams(vmem_limit_bytes=36 << 20),
         name="grad_attention",
-    )(sc, *a, *o, *own, *got, *after)
+    )(sc, *a, *o, *own, *got, *gains, *after)
 
 
 def lay_kernel(count, sc, *rest):
@@ -577,7 +601,7 @@
     for kind, pieces in ((core, mine), (1 - core, other)):
         for who, piece in zip(whose(kind), pieces):
             kept[kind, chip ^ who] = piece[...]
-    n = sum(o.shape[1] for o in outs) // 8
+    n = sum(o.shape[1] for o in outs[: 4 if len(outs) > 2 else 2]) // 8
     cols = [jnp.concatenate([kept[c, m, :, :n].astype(f32) for m in range(4)], axis=1) for c in range(2)]
     if len(outs) == 2:
         outs[0][...] = cols[0]
@@ -587,51 +611,127 @@
         outs[1][...] = cols[0][:, 3 * n :]
         outs[2][...] = cols[1][:, :n]
         outs[3][...] = cols[1][:, n:]
+        gains = kept[0, 0, :, n : n + 8].astype(f32) + kept[1, 0, :, n : n + 8].astype(f32)
+        outs[4][...] = gains.T[:2]
 
 
 def lay(sc, mine, other, widths, after):
     rows, n = mine[0].shape
     outs = tuple(shape((rows, w), f32) for w in widths)
-    return pl.pallas_call(
-        functools.partial(lay_kernel, len(widths)),
+    if len(widths) > 2:
+        outs += (shape((2, rows), f32),)
+    return pl.pallas_call(
+        functools.partial(lay_kernel, len(outs)),
         out_shape=outs,
         in_specs=[SCALARS] + [WHOLE] * 8 + [LEFT] * len(after),
         out_specs=(WHOLE,) * len(outs),
         scratch_shapes=[pltpu.VMEM((2, 4, rows, n), bf16)],
+        cost_estimate=BRIEF,
         compiler_params=pltpu.CompilerParams(vmem_limit_bytes=24 << 20),
         name="lay",
     )(sc, *mine, *other, *after)
 
 
-def pick_kernel(by_core, sc, *rest):
-    sources, (out_ref, sem) = rest[:2], rest[-2:]
-    core, chip = sc[0], sc[1]
-    if by_core:
-        cols = out_ref.shape[1]
-        at = pl.ds(pl.multiple_of(chip * cols, 128), cols)
-        views = [source.at[:, at] for source in sources]
-    else:
-        half = out_ref.shape[0]
-        views = [source.at[c * half : (c + 1) * half, :] for c, source in enumerate(sources)]
-    for c in range(2):
-
-        @pl.when(core == c)
+def pick_first_kernel(sc, q_ref, k_ref, v_ref, o_ref, gain_ref, out_ref):
+    rows = out_ref.shape[0]
+    which = sc[0] * 4 + sc[1]
+    pad = jnp.zeros((6, rows), f32)
+    gains = jnp.concatenate([gain_ref[...], pad], axis=0).T.astype(bf16)
+    rest = jnp.zeros((rows, PIECE - KVW - 8), bf16)
+    for at in range(8):
+
+        @pl.when(which == at)
         def _():
-            pltpu.make_async_copy(views[c], out_ref, sem).start()
-
-    pltpu.make_async_copy(views[0], out_ref, sem).wait()
-
-
-def pick(sc, sources, out, by_core, after):
-    return pl.pallas_call(
-        functools.partial(pick_kernel, by_core),
-        out_shape=shape(out, bf16),
+            if at in (3, 4):
+                piece = (k_ref if at == 3 else v_ref)[...].T
+            else:
+                source, m = (q_ref, at) if at < 3 else (o_ref, at - 5)
+                piece = source[:, m * KVW : (m + 1) * KVW]
+            out_ref[...] = jnp.concatenate([piece, gains, rest], axis=1)
+
+
+def pick_first(sc, query, key, value, out, gains):
+    return pl.pallas_call(
+        pick_first_kernel,
+        out_shape=shape((query.shape[0], PIECE), bf16),
+        in_specs=[SCALARS] + [WHOLE] * 5,
+        out_specs=WHOLE,
+        cost_estimate=BRIEF,
+        compiler_params=pltpu.CompilerParams(vmem_limit_bytes=16 << 20),
+        name="pick_first",
+    )(sc, query, key, value, out, gains)
+
+
+def pick_kernel(sc, gate, up, *rest):
+    out_ref, sem = rest[-2:]
+    cols = out_ref.shape[1]
+    at = pl.ds(pl.multiple_of(sc[1] * cols, 128), cols)
+    for c, source in ((0, gate), (1, up)):
+
+        @pl.when(sc[0] == c)
+        def _():
+            pltpu.make_async_copy(source.at[:, at], out_ref, sem).start()
+
+    pltpu.make_async_copy(gate.at[:, at], out_ref, sem).wait()
+
+
+def pick(sc, gate, up, after):
+    return pl.pallas_call(
+        pick_kernel,
+        out_shape=shape((gate.shape[0], gate.shape[1] // 4), bf16),
         in_specs=[SCALARS] + [LEFT] * (2 + len(after)),
         out_specs=WHOLE,
         scratch_shapes=[pltpu.SemaphoreType.DMA],
+        cost_estimate=BRIEF,
         compiler_params=pltpu.CompilerParams(vmem_limit_bytes=16 << 20),
         name="pick",
-    )(sc, *sources, *after)
+    )(sc, gate, up, *after)
+
+
+def pick_down_kernel(sc, down, *rest):
+    far_ref, near_ref, sems = rest[-3:]
+    half, n = far_ref.shape[0], near_ref.shape[0]
+    copies = []
+    for i, (out, row) in enumerate(((far_ref, sc[0] * half), (near_ref, 2 * half + (sc[0] * 4 + sc[1]) * n))):
+        rows = pl.ds(pl.multiple_of(row, 16), out.shape[0])
+        copies.append(pltpu.make_async_copy(down.at[rows, :], out, sems.at[i]))
+    for copy in copies:
+        copy.start()
+    for copy in copies:
+        copy.wait()
+
+
+def pick_down(sc, down, after):
+    rows, cols = down.shape
+    n = rows // 240 * 16
+    return pl.pallas_call(
+        pick_down_kernel,
+        out_shape=(shape((rows // 2 - 4 * n, cols), bf16), shape((n, cols), bf16)),
+        in_specs=[SCALARS] + [LEFT] * (1 + len(after)),
+        out_specs=(WHOLE, WHOLE),
+        scratch_shapes=[pltpu.SemaphoreType.DMA((2,))],
+        cost_estimate=BRIEF,
+        compiler_params=pltpu.CompilerParams(vmem_limit_bytes=16 << 20),
+        name="pick_down",
+    )(sc, down, *after)
+
+
+def gains_kernel(first_ref, out_ref):
+    for j in range(4):
+        n = first_ref.shape[1]
+        out_ref[:, j * n : (j + 1) * n] = first_ref[j, :, KVW : KVW + 8].astype(f32).T[:2]
+
+
+def gains_of(first):
+    return pl.pallas_call(
+        gains_kernel,
+        out_shape=shape((2, 4 * first.shape[1]), f32),
+        in_specs=[WHOLE],
+        out_specs=WHOLE,
+        cost_estimate=BRIEF,
+        compiler_params=pltpu.CompilerParams(vmem_limit_bytes=16 << 20),
+        name="gains",
+    )(first)
 
 
 def stack_kernel(sc, *rest):
@@ -650,6 +750,7 @@
         in_specs=[SCALARS] + [LEFT] * (4 + len(after)),
         out_specs=WHOLE,
         scratch_shapes=[pltpu.SemaphoreType.DMA((4,))],
+        cost_estimate=BRIEF,
         compiler_params=pltpu.CompilerParams(vmem_limit_bytes=16 << 20),
         name="stack",
     )(sc, *parts, *after)
@@ -662,6 +763,7 @@
         in_specs=[SCALARS] + [WHOLE] * len(args) + [LEFT] * len(after),
         out_specs=(WHOLE,) * len(outs),
         scratch_shapes=scratch,
+        cost_estimate=BRIEF,
         compiler_params=pltpu.CompilerParams(vmem_limit_bytes=32 << 20),
         name=name,
     )(sc, *args, *after)
@@ -796,14 +898,6 @@
     return mine, tuple(flip(p, CORE) for p in mine)
 
 
-def small_gather(shard):
-    z = lax.axis_index("fsdp")
-    full = jnp.zeros((lax.axis_size("fsdp"),) + shard.shape, shard.dtype)
-    for s, part in enumerate(turns(shard)):
-        full = lax.dynamic_update_index_in_dim(full, part, (z - s) % full.shape[0], 0)
-    return full
-
-
 def window(own):
     core, _, _ = place()
     depth = lax.axis_size("fsdp")
@@ -847,66 +941,46 @@
     return lax.ppermute(part, ("dp", "fsdp"), pairs)
 
 
-def reduce_gains(total):
-    z = lax.axis_index("fsdp")
-    depth = lax.axis_size("fsdp")
-    bit = 1
-    while bit < lax.axis_size("dp"):
-        total = total + flip(total, bit)
-        bit *= 2
-    rows = total.shape[1] // depth
-    total = total + sum(turn_z(total, s) for s in range(1, depth))
-    mine = lax.dynamic_slice_in_dim(total, z * rows, rows, 1)
-    return mine[0], mine[1]
-
-
 def body(tokens, segment_ids, attn_gain, query_weight, key_weight, value_weight, out_weight, ffn_gain, gate_weight, up_weight, down_weight, cotangent):
     core, chip, z = place()
     sc = jnp.stack([core, chip, z]).astype(jnp.int32)
     _, stretch, width = tokens.shape
     rows, depth = query_weight.shape[0], lax.axis_size("fsdp")
-
-    first = jnp.concatenate([query_weight, key_weight, value_weight, out_weight], axis=1)
-    first = jnp.pad(first, ((0, 0), (0, PIECE - KVW)))
-    parts_a = turns(lax.dynamic_slice(first, (0, KVW * (core * 4 + chip)), (rows, PIECE)))
-    wa = plane_gather(stack(sc, parts_a).reshape(depth * rows, PIECE))
-    piece_b = pick(sc, [gate_weight, up_weight], (rows, gate_weight.shape[1] // 4), True, parts_a[1:])
-    whole_b = stack(sc, turns(piece_b)).reshape(depth * rows, piece_b.shape[1])
-    wb = plane_gather(whole_b)
-    piece_d = pick(sc, [down_weight.T] * 2, (width // 2, down_weight.shape[0]), False, [whole_b])
-    whole_d = stack(sc, turns(piece_d))
-    wd = whole_d, flip(whole_d, CORE)
-    weights = wa, wb, wd
-
-    tokens = home_to_work(tokens[0].T)
-    gains = small_gather(jnp.stack([attn_gain, ffn_gain]))
-    gains = jnp.moveaxis(gains, 0, 1).reshape(2, 1, width).astype(f32)
-    gain_a, gain_f = gains[0], gains[1]
-    row = small_gather(segment_ids[0]).reshape(-1)
-    row = jnp.where((z >> 1) == core, row, flip(row, CORE))
     block = 2 * (z & 1) + core
-    padded = jnp.concatenate([jnp.full((2 * stretch,), -1, row.dtype), row])
-    seg_k = lax.dynamic_slice(padded, (block * stretch,), (3 * stretch,))
-    seg_q = seg_k[2 * stretch :]
-    ahead = jnp.arange(3 * stretch)[:, None] < 2 * stretch + jnp.arange(stretch)[None, :]
-    seg_k, seg_q = seg_k[:, None], seg_q[None, :]
-    positions = jnp.sum(((seg_k == seg_q) & ahead).astype(f32), axis=0)
+    positions = (block * stretch + jnp.arange(stretch)).astype(f32)
     freq = rope_base ** (-2.0 * jnp.arange(HEAD_DIM // 2, dtype=f32) / HEAD_DIM)
     angle = freq[:, None] * positions[None, :]
     cos, sin = jnp.cos(angle), jnp.sin(angle)
-    cot = home_to_work(cotangent[0].T)
+
+    gains = jnp.stack([attn_gain, ffn_gain]).astype(f32)
+    parts_a = turns(pick_first(sc, query_weight, key_weight.T, value_weight.T, out_weight, gains))
+    ids = jnp.broadcast_to((segment_ids[0] + 1).astype(bf16), (IDS, stretch))
+    tokens = home_to_work(jnp.concatenate([tokens[0].T, ids]))
+    whole_a = stack(sc, parts_a)
+    gains = gains_of(whole_a)
+    gain_a, gain_f = gains[:1], gains[1:]
+    wa = plane_gather(whole_a.reshape(depth * rows, PIECE))
+    piece_b = pick(sc, gate_weight, up_weight, [whole_a])
+    whole_b = stack(sc, turns(piece_b)).reshape(depth * rows, piece_b.shape[1])
+    wb = plane_gather(whole_b)
+    far_d, near_d = pick_down(sc, down_weight.T, [whole_b])
+    parts_n, parts_f = turns(near_d), turns(far_d)
 
     h_0, a0, q0, own = pre(sc, tokens, gain_a, cos, sin, *wa, [whole_b])
     kv0 = window(own)
-    o0, lse0 = attend(q0, kv0, seg_k, seg_q)
-    mixed0, h1_0, b0, gate0, up0, z0, h_1, a1, q1, own = post(False, sc, o0, h_0, gain_f, gain_a, cos, sin, *weights)
+    near_d = plane_gather(stack(sc, parts_n, [q0]))
+    o0, lse0 = attend(q0, kv0)
+    far_d = stack(sc, parts_f, [o0])
+    weights = wa, wb, (far_d, flip(far_d, CORE), *near_d[0], *near_d[1])
+    cot = home_to_work(cotangent[0].T)
+    mixed0, h1_0, b0, gate0, up0, z0, h_1, a1, q1, own = post(False, sc, o0, h_0, gain_f, gain_a, cos, sin, own, *weights)
     kv1 = window(own)
-    o1, lse1 = attend(q1, kv1, seg_k, seg_q)
-    mixed1, h1_1, b1, gate1, up1, z1, output = post(True, sc, o1, h_1, gain_f, gain_a, cos, sin, *weights)
+    o1, lse1 = attend(q1, kv1)
+    mixed1, h1_1, b1, gate1, up1, z1, output = post(True, sc, o1, h_1, gain_f, gain_a, cos, sin, own, *weights)
     output = home_to_work(output, back=True).T
 
     gb1, act1, away1, zk1, zs1, g1, p1, dgain_f1, do = back(True, False, sc, weights, [cot], [gate1, up1, h1_1, gain_f, z1])
-    dq1, three1, far, near, own = attend_back(sc, p1, q1, kv1, seg_k, seg_q, lse1, do, cos, sin)
+    dq1, three1, far, near, own = attend_back(sc, p1, q1, kv1, lse1, do, cos, sin)
     near, far = unwindow(far, near)
     tail = [g1, dq1, own, near, far, h_1, gain_a, cos, sin]
     dk1, dv1, one1, dgain_a1, gb0, act0, away0, zk0, zs0, g1, p0, dgain_f0, do = back(False, False, sc, weights, tail, [gate0, up0, h1_0, gain_f, z0])
@@ -921,7 +995,7 @@
     owner = (z >> 1) == core
     own_d = jnp.where(owner, like_d, jnp.zeros_like(like_d))
 
-    dq0, three0, far, near, own = attend_back(sc, p0, q0, kv0, seg_k, seg_q, lse0, do, cos, sin, [like_d])
+    dq0, three0, far, near, own = attend_back(sc, p0, q0, kv0, lse0, do, cos, sin, [like_d])
     near, far = unwindow(far, near)
     later_b, own_b = sum_first(sc, keep_b, got_b, [own])
     more_b = flip(later_b, BACK, SIDE)
@@ -930,7 +1004,7 @@
     grad_tokens = home_to_work(grad_tokens, back=True).astype(f32).T
 
     own = [dq1, dq0, dk1, dk0, dv1, dv0, p1, p0]
-    send_a, keep_a = grad_attention(sc, pair(a1, a0), pair(mixed1, mixed0), own, across((three1, three0, one1, one0)), [])
+    send_a, keep_a = grad_attention(sc, pair(a1, a0), pair(mixed1, mixed0), own, across((three1, three0, one1, one0)), [dgain_a1, dgain_a0, dgain_f1, dgain_f0], [])
     got_a = flip(send_a, SIDE, BACK)
     ring_b = sum_second(sc, own_b, more_b, [send_a])
     ring_b, parts_b = ring_b[0], [turn_z(v, s + 1) for s, v in enumerate(ring_b[1:])]
@@ -951,9 +1025,8 @@
     all_a = spread(piece_a)
     grad_gate, grad_up = lay(sc, all_b, across(all_b), (gate_weight.shape[1],) * 2, [piece_a])
     grad_down_ = lay_down(sc, all_d, across(all_d), [grad_gate])
-    grad_query, grad_key, grad_value, grad_out = lay(sc, all_a, across(all_a), (width, KVW, KVW, width), [grad_down_])
-    dgain_a, dgain_f = reduce_gains(jnp.concatenate([dgain_a1 + dgain_a0, dgain_f1 + dgain_f0]))
-    return (output[None], grad_tokens[None], dgain_a, grad_query, grad_key, grad_value, grad_out, dgain_f, grad_gate, grad_up, grad_down_.T)
+    grad_query, grad_key, grad_value, grad_out, dgains = lay(sc, all_a, across(all_a), (width, KVW, KVW, width), [grad_down_])
+    return (output[None], grad_tokens[None], dgains[0], grad_query, grad_key, grad_value, grad_out, dgains[1], grad_gate, grad_up, grad_down_.T)
 
 
 def solution(mesh):

time: 615 us -> 574 us (0.933)
  waiting for transfers between devices: 227 us -> 196 us
  local copies, waits for them, and re-layouts: 52.6 us -> 34 us
  Pallas kernels: 184 us -> 192 us
    ppermute x24 -> x18, waiting for transfers between devices: 119 us -> 100 us  [turn_z(): lax.ppermute(value, 'fsdp', [(i, (i + step) % count) for i in range(count)])]
    ppermute x24 -> x18, starting transfers between devices: 64.9 us -> 79.5 us  [turn_z(): lax.ppermute(value, 'fsdp', [(i, (i + step) % count) for i in range(count)])]
    unnamed x204 -> x201, local copies, waits for them, and re-layouts: 45.4 us -> 31.5 us
    ppermute x2, starting transfers between devices: 23.9 us -> 10.3 us  [window(): far = lax.ppermute(own, 'fsdp', [(z, z + 1) for z in range(0, depth, 2)])]
    ppermute x2, waiting for transfers between devices: 15.8 us -> 4.87 us  [window(): far = lax.ppermute(own, 'fsdp', [(z, z + 1) for z in range(0, depth, 2)])]
    ppermute x67 -> x70, starting transfers between devices: 33.7 us -> 39.1 us  [flip(): lax.ppermute(value, 'dp', [(i, i ^ bits[i & 1]) for i in range(count)])]
    ppermute x67 -> x70, waiting for transfers between devices: 56.6 us -> 57.6 us  [flip(): lax.ppermute(value, 'dp', [(i, i ^ bits[i & 1]) for i in range(count)])]
  transfers between devices with their start and end apart: 102 -> 99, of which waited for: 43 -> 36; matrix products, arithmetic and copies ran while one was open for 1% -> 1% of each run, Pallas kernels for 18% -> 21%
where the time goes in v5:
time: 574 us; the launch traced here: 568 us
  waiting for transfers between devices  196 us (34%)
  Pallas kernels  192 us (33%)
  starting transfers between devices  140 us (24%)
  local copies, waits for them, and re-layouts  34 us (6%)
    ppermute x18, waiting for transfers between devices, turn_z(): lax.ppermute(value, 'fsdp', [(i, (i + step) % count) for i in range(count)])  100 us
    ppermute x18, starting transfers between devices, turn_z(): lax.ppermute(value, 'fsdp', [(i, (i + step) % count) for i in range(count)])  79.5 us
    ppermute x70, waiting for transfers between devices, flip(): lax.ppermute(value, 'dp', [(i, i ^ bits[i & 1]) for i in range(count)])  57.6 us
    pallas_call x3, Pallas kernels, back(): pl.pallas_call(functools.partial(back_kernel, start, end, len(after)), ou...  50.2 us
    pallas_call x2, Pallas kernels, post(): pl.pallas_call(functools.partial(post_kernel, last), out_shape=tuple(outs...  39.2 us
    ppermute x70, starting transfers between devices, flip(): lax.ppermute(value, 'dp', [(i, i ^ bits[i & 1]) for i in range(count)])  39.1 us
    unnamed x201, local copies, waits for them, and re-layouts  31.5 us
    pallas_call x2, Pallas kernels, attend_back(): pl.pallas_call(attend_back_kernel, out_shape=(shape((3, n, PIECE), bf16),...  26.9 us
  transfers between devices with their start and end apart: 99, of which 36 were waited for; matrix products, arithmetic and copies ran while one was open for 1% of the time, Pallas kernels for 21%

profile of v5, /device:TPU:0, one launch (start us, length us, event | category | flops | bytes accessed | tf_op | source)
XLA Modules:
  0.0 568.3 jit_solution(12122283266417440700)
XLA Ops:
  6.7 3.1 collective-permute-start.1
  9.8 2.6 collective-permute-start.2
  13.8 3.7 collective-permute-done.1.rest_1_
  17.4 7.1 %collective-permute-done.2.rest_2_ = bf16[240,384]{1,0:T(8,128)(2,1)S(1)} collective-permute-done((bf16[240,384]{1,0:T(8,128)(2,1)S(1)}, bf16[240,384]{1,0:T(8,128)(2,1)S(1)}, u32[]{:S(2)}, u32[]{:S(2)}) %collective-permute-start.2) | collective-permute-done | bytes 184352 | tf_op jit(solution)/shard_map/ppermute | solution.py:872
  28.2 4.5 collective-permute-start.11
  36.0 6.1 %collective-permute-done.11.rest_1_ = bf16[240,640]{1,0:T(8,128)(2,1)S(1)} collective-permute-done((bf16[240,640]{1,0:T(8,128)(2,1)S(1)}, bf16[240,640]{1,0:T(8,128)(2,1)S(1)}, u32[]{:S(2)}, u32[]{:S(2)}) %collective-permute-start.11) | collective-permute-done | bytes 307232 | tf_op jit(solution)/shard_map/ppermute | solution.py:872
  44.1 9.2 %collective-permute-done.12.rest_2_ = bf16[240,640]{1,0:T(8,128)(2,1)S(1)} collective-permute-done((bf16[240,640]{1,0:T(8,128)(2,1)S(1)}, bf16[240,640]{1,0:T(8,128)(2,1)S(1)}, u32[]{:S(2)}, u32[]{:S(2)}) %collective-permute-start.12) | collective-permute-done | bytes 307232 | tf_op jit(solution)/shard_map/ppermute | solution.py:872
  57.1 14.0 %collective-permute-start.27 = (bf16[64,640]{1,0:T(8,128)(2,1)S(1)}, bf16[64,640]{1,0:T(8,128)(2,1)S(1)}, u32[]{:S(2)}, u32[]{:S(2)}) collective-permute-start(bf16[64,640]{1,0:T(8,128)(2,1)S(1)} %get-tuple-element.111.rest_0_), channel_id=1, source_target_pairs={{0,1},{1,2},{2,3},{3,0},{4,5},{5,6},{6,7},{7,4},{8,9},{9,10},{10,1... | collective-permute-start | bytes 245768 | tf_op jit(solution)/shard_map/ppermute | solution.py:872
  71.1 3.4 collective-permute-done.27.rest_1_
  80.2 16.5 %collective-permute-start.28 = (bf16[64,640]{1,0:T(8,128)(2,1)S(1)}, bf16[64,640]{1,0:T(8,128)(2,1)S(1)}, u32[]{:S(2)}, u32[]{:S(2)}) collective-permute-start(bf16[64,640]{1,0:T(8,128)(2,1)S(1)} %get-tuple-element.111.rest_0_), channel_id=1, source_target_pairs={{0,2},{1,3},{2,0},{3,1},{4,6},{5,7},{6,4},{7,5},{8,10},{9,11},{10,... | collective-permute-start | bytes 245768 | tf_op jit(solution)/shard_map/ppermute | solution.py:872
  97.4 6.8 %pre.1 = (bf16[256,960]{1,0:T(8,128)(2,1)}, bf16[256,960]{1,0:T(8,128)(2,1)}, bf16[960,256]{1,0:T(8,128)(2,1)}, bf16[656,256]{1,0:T(8,128)(2,1)}) custom-call(s32[3]{0:T(128)} %copy-done.48, bf16[976,256]{1,0:T(8,128)(2,1)} %copy-done.86, f32[1,960]{1,0:T(1,128)} %get-tuple-element.213.gain_ref.gain_a.rest_32_.rest_14_, ...), custom_call_target="tpu_custom_call" | custom-call | flops 1024 | bytes 1024 | tf_op jit(solution)/shard_map/pre/pallas_call | solution.py:118
  104.2 4.1 collective-permute-start.14
  108.4 14.1 %collective-permute-done.23.rest_1_ = bf16[224,640]{1,0:T(8,128)(2,1)S(1)} collective-permute-done((bf16[224,640]{1,0:T(8,128)(2,1)}, bf16[224,640]{1,0:T(8,128)(2,1)S(1)}, u32[]{:S(2)}, u32[]{:S(2)}) %collective-permute-start.23) | collective-permute-done | bytes 286752 | tf_op jit(solution)/shard_map/ppermute | solution.py:872
  122.8 4.6 collective-permute-start.25
  128.4 11.1 %collective-permute-done.24.rest_2_ = bf16[224,640]{1,0:T(8,128)(2,1)S(1)} collective-permute-done((bf16[224,640]{1,0:T(8,128)(2,1)}, bf16[224,640]{1,0:T(8,128)(2,1)S(1)}, u32[]{:S(2)}, u32[]{:S(2)}) %collective-permute-start.24) | collective-permute-done | bytes 286752 | tf_op jit(solution)/shard_map/ppermute | solution.py:872
  143.7 10.1 %attend.2 = (bf16[960,256]{1,0:T(8,128)(2,1)S(1)}, f32[15,256]{1,0:T(8,128)S(1)}) custom-call(bf16[960,256]{1,0:T(8,128)(2,1)S(1)} %copy-done.9, bf16[656,256]{1,0:T(8,128)(2,1)S(1)} %collective-permute-done.14.kv0, bf16[656,256]{1,0:T(8,128)(2,1)S(1)} %collective-permute-done.15.kv1, bf16[656,256]{1,0:T(8,128)(2,1)S(1)} %copy-done.5), custom_call_target="tpu_custom_call" | custom-call | flops 1024 | bytes 1024 | tf_op jit(solution)/shard_map/attend/pallas_call | solution.py:170
  156.2 2.7 collective-permute-done.33.rest_22_
  158.9 1.9 collective-permute-start.32
  161.3 4.6 collective-permute-done.32.rest_21_
  169.2 20.9 %post.2 = (bf16[256,960]{1,0:T(8,128)(2,1)}, f32[256,960]{1,0:T(8,128)}, bf16[256,960]{1,0:T(8,128)(2,1)}, bf16[256,2560]{1,0:T(8,128)(2,1)}, bf16[256,2560]{1,0...) custom-call(s32[3]{0:T(128)} %copy-done.48, ...), custom_call_target="tpu_custom_call" | custom-call | flops 1024 | bytes 1024 | tf_op jit(solution)/shard_map/post/pallas_call | solution.py:311
  190.1 6.2 %collective-permute-start.37 = (bf16[656,256]{1,0:T(8,128)(2,1)}, bf16[656,256]{1,0:T(8,128)(2,1)S(1)}, u32[]{:S(2)}, u32[]{:S(2)}) collective-permute-start(bf16[656,256]{1,0:T(8,128)(2,1)} %get-tuple-element.113.kv2.rest_26_), channel_id=1, source_target_pairs={{0,1},{2,3},{4,5},{6,7},{8,9},{10,11},{12,13},{14,15},{16,17},{18,... | collective-permute-start | bytes 1007624 | tf_op jit(solution)/shard_map/ppermute | solution.py:904
  196.4 1.7 collective-permute-start.40
  198.0 4.9 collective-permute-done.37.kv0
  205.7 10.5 %attend.3 = (bf16[960,256]{1,0:T(8,128)(2,1)S(1)}, f32[15,256]{1,0:T(8,128)S(1)}) custom-call(bf16[960,256]{1,0:T(8,128)(2,1)S(1)} %copy-done.26, bf16[656,256]{1,0:T(8,128)(2,1)S(1)} %collective-permute-done.37.kv0, bf16[656,256]{1,0:T(8,128)(2,1)S(1)} %collective-permute-done.38.kv1, bf16[656,256]{1,0:T(8,128)(2,1)S(1)} %copy-done.7), custom_call_target="tpu_custom_call" | custom-call | flops 1024 | bytes 1024 | tf_op jit(solution)/shard_map/attend/pallas_call | solution.py:170
  217.0 18.3 %post.3 = (bf16[256,960]{1,0:T(8,128)(2,1)}, f32[256,960]{1,0:T(8,128)}, bf16[256,960]{1,0:T(8,128)(2,1)}, bf16[256,2560]{1,0:T(8,128)(2,1)}, bf16[256,2560]{1,0...) custom-call(s32[3]{0:T(128)} %copy-done.48, bf16[960,256]{1,0:T(8,128)(2,1)} %copy-done.55, ...), custom_call_target="tpu_custom_call" | custom-call | flops 1024 | bytes 1024 | tf_op jit(solution)/shard_map/post/pallas_call | solution.py:311
  236.1 21.6 %back_start.1 = (bf16[256,960]{1,0:T(8,128)(2,1)}, bf16[256,2560]{1,0:T(8,128)(2,1)}, bf16[256,2560]{1,0:T(8,128)(2,1)}, bf16[256,1280]{1,0:T(8,128)(2,1)}, bf16...) custom-call(s32[3]{0:T(128)} %copy-done.48, ...), custom_call_target="tpu_custom_call" | custom-call | flops 1024 | bytes 1024 | tf_op jit(solution)/shard_map/back_start/pallas_call | solution.py:467
  259.9 13.5 %attend_back.2 = (bf16[3,256,384]{2,1,0:T(8,128)(2,1)S(1)}, bf16[3,256,384]{2,1,0:T(8,128)(2,1)}, f32[640,256]{1,0:T(8,128)S(1)}, bf16[640,256]{1,0:T(8,128)(2,1)S(1)}, f32[640,256]{1,0:T(8,128)S(1)}) custom-call(s32[3]{0:T(128)S(1)} %copy-done.50, bf16[3,256,384]{2,1,0:T(8,128)(2,1)S(1)} %copy-done.16, bf16[960,256]{1,0:T(8,128)(2,1)S(1)} %copy-done.26, ...), custom_call_target="tpu_custom_call" | custom-call | flops 1024 | bytes 1024 | tf_op jit(solution)/shard_map/attend_back/pallas_call | solution.py:223
  278.2 10.2 %collective-permute-done.42.rest_30_ = bf16[640,256]{1,0:T(8,128)(2,1)S(1)} collective-permute-done((bf16[640,256]{1,0:T(8,128)(2,1)S(1)}, bf16[640,256]{1,0:T(8,128)(2,1)S(1)}, u32[]{:S(2)}, u32[]{:S(2)}) %collective-permute-start.42) | collective-permute-done | bytes 327712 | tf_op jit(solution)/shard_map/ppermute | solution.py:914
  289.1 22.0 %back_join.1 = (bf16[256,384]{1,0:T(8,128)(2,1)}, bf16[256,384]{1,0:T(8,128)(2,1)}, bf16[256,384]{1,0:T(8,128)(2,1)}, f32[1,960]{1,0:T(1,128)}, bf16[256,960]{1,...) custom-call(s32[3]{0:T(128)} %copy-done.48, ...), custom_call_target="tpu_custom_call" | custom-call | flops 1024 | bytes 1024 | tf_op jit(solution)/shard_map/back_join/pallas_call | solution.py:467
  311.8 3.6 collective-permute-done.48.rest_3_
  319.4 7.4 %grad_ffn.1 = (bf16[2,960,640]{2,1,0:T(8,128)(2,1)S(1)}, bf16[2,960,640]{2,1,0:T(8,128)(2,1)S(1)}) custom-call(s32[3]{0:T(128)S(1)} %copy-done.51, bf16[256,960]{1,0:T(8,128)(2,1)S(1)} %copy-done.47, bf16[256,960]{1,0:T(8,128)(2,1)S(1)} %copy-done.46, bf16[256,960]{1,0:T(8,128)(2,1)S(1)} %collective-permute-done.47.rest_2_, ...), custom_call_target="tpu_custom_call" | custom-call | flops 1024 | bytes 1024 | tf_op jit(solution)/shard_map/grad_ffn/pallas_call | solution.py:508
  328.1 2.5 collective-permute-start.45
  331.2 2.8 collective-permute-done.43.rest_2_
  334.9 4.9 grad_down.1
  339.8 13.4 %attend_back.3 = (bf16[3,256,384]{2,1,0:T(8,128)(2,1)S(1)}, bf16[3,256,384]{2,1,0:T(8,128)(2,1)}, f32[640,256]{1,0:T(8,128)S(1)}, bf16[640,256]{1,0:T(8,128)(2,1)S(1)}, f32[640,256]{1,0:T(8,128)S(1)}) custom-call(s32[3]{0:T(128)S(1)} %copy-done.51, bf16[3,256,384]{2,1,0:T(8,128)(2,1)S(1)} %copy-done.18, bf16[960,256]{1,0:T(8,128)(2,1)S(1)} %copy-done.9, ...), custom_call_target="tpu_custom_call" | custom-call | flops 1024 | bytes 1024 | tf_op jit(solution)/shard_map/attend_back/pallas_call | solution.py:223
  357.2 9.6 %collective-permute-done.52.rest_12_ = bf16[640,256]{1,0:T(8,128)(2,1)S(1)} collective-permute-done((bf16[640,256]{1,0:T(8,128)(2,1)S(1)}, bf16[640,256]{1,0:T(8,128)(2,1)S(1)}, u32[]{:S(2)}, u32[]{:S(2)}) %collective-permute-start.52) | collective-permute-done | bytes 327712 | tf_op jit(solution)/shard_map/ppermute | solution.py:914
  368.1 2.0 sum_first.3
  371.6 6.6 %back_end.1 = (bf16[256,384]{1,0:T(8,128)(2,1)}, bf16[256,384]{1,0:T(8,128)(2,1)}, bf16[256,384]{1,0:T(8,128)(2,1)}, f32[1,960]{1,0:T(1,128)}, bf16[960,256]{1,0:T(8,128)(2,1)}) custom-call(s32[3]{0:T(128)} %copy-done.48, bf16[960,384]{1,0:T(8,128)(2,1)} %bitcast.41, bf16[960,384]{1,0:T(8,128)(2,1)} %copy-done.72, ...), custom_call_target="tpu_custom_call" | custom-call | flops 1024 | bytes 1024 | tf_op jit(solution)/shard_map/back_end/pallas_call | solution.py:467
  386.9 7.2 %grad_attention.1 = (bf16[2,960,384]{2,1,0:T(8,128)(2,1)S(1)}, bf16[2,960,384]{2,1,0:T(8,128)(2,1)S(1)}) custom-call(s32[3]{0:T(128)S(1)} %copy-done.52, bf16[256,960]{1,0:T(8,128)(2,1)} %get-tuple-element.158.rest_0_, bf16[256,960]{1,0:T(8,128)(2,1)S(1)} %copy-done.42, bf16[256,960]{1,0:T(8,128)(2,1)} %collective-permute-done.55.rest_2_, ...), custom_call_target="tpu_custom_call" | custom-call | flops 1024 | bytes 1024 | tf_op jit(solution)/shard_map/grad_attention/pallas_call | solution.py:586
  396.1 1.8 collective-permute-start.64
  397.8 1.9 collective-permute-start.66
  402.5 23.8 %collective-permute-done.64.got_ref = bf16[960,640]{1,0:T(8,128)(2,1)} collective-permute-done((bf16[960,640]{1,0:T(8,128)(2,1)}, bf16[960,640]{1,0:T(8,128)(2,1)}, u32[]{:S(2)}, u32[]{:S(2)}) %collective-permute-start.64) | collective-permute-done | bytes 1228832 | tf_op jit(solution)/shard_map/ppermute | solution.py:867
  426.3 1.9 sum_second.2
  428.2 1.7 sum_first.4
  429.9 1.9 collective-permute-start.65
  431.8 3.5 collective-permute-done.67.rest_1_
  435.3 9.6 %collective-permute-done.68.rest_2_ = bf16[960,640]{1,0:T(8,128)(2,1)} collective-permute-done((bf16[960,640]{1,0:T(8,128)(2,1)}, bf16[960,640]{1,0:T(8,128)(2,1)}, u32[]{:S(2)}, u32[]{:S(2)}) %collective-permute-start.68) | collective-permute-done | bytes 1228832 | tf_op jit(solution)/shard_map/ppermute | solution.py:941
  444.9 3.2 down_ring.1
  448.1 13.8 %collective-permute-start.75 = (bf16[240,640]{1,0:T(8,128)(2,1)S(1)}, bf16[240,640]{1,0:T(8,128)(2,1)S(1)}, u32[]{:S(2)}, u32[]{:S(2)}) collective-permute-start(bf16[240,640]{1,0:T(8,128)(2,1)S(1)} %get-tuple-element.191), channel_id=1, source_target_pairs={{0,1},{1,2},{2,3},{3,0},{4,5},{5,6},{6,7},{7,4},{8,9},{9,10},{10,1... | collective-permute-start | bytes 921608 | tf_op jit(solution)/shard_map/ppermute | solution.py:872
  463.4 5.2 collective-permute-start.76
  470.8 2.2 collective-permute-start.77
  473.8 30.9 %collective-permute-done.76.rest_1_ = bf16[240,640]{1,0:T(8,128)(2,1)S(1)} collective-permute-done((bf16[240,640]{1,0:T(8,128)(2,1)S(1)}, bf16[240,640]{1,0:T(8,128)(2,1)S(1)}, u32[]{:S(2)}, u32[]{:S(2)}) %collective-permute-start.76) | collective-permute-done | bytes 307232 | tf_op jit(solution)/shard_map/ppermute | solution.py:872
  504.7 5.5 collective-permute-start.70
  510.2 3.4 collective-permute-start.71
  519.5 6.1 %collective-permute-done.71.rest_1_ = bf16[240,384]{1,0:T(8,128)(2,1)S(1)} collective-permute-done((bf16[240,384]{1,0:T(8,128)(2,1)S(1)}, bf16[240,384]{1,0:T(8,128)(2,1)S(1)}, u32[]{:S(2)}, u32[]{:S(2)}) %collective-permute-start.71) | collective-permute-done | bytes 184352 | tf_op jit(solution)/shard_map/ppermute | solution.py:872
  526.2 6.5 %collective-permute-done.72.rest_2_ = bf16[240,384]{1,0:T(8,128)(2,1)S(1)} collective-permute-done((bf16[240,384]{1,0:T(8,128)(2,1)S(1)}, bf16[240,384]{1,0:T(8,128)(2,1)S(1)}, u32[]{:S(2)}, u32[]{:S(2)}) %collective-permute-start.72) | collective-permute-done | bytes 184352 | tf_op jit(solution)/shard_map/ppermute | solution.py:872
  535.7 1.9 collective-permute-start.87
  541.6 4.8 collective-permute-done.87.rest_3_
  547.4 2.9 collective-permute-done.80.rest_3_
  553.7 3.1 lay.2
  556.9 1.7 copy-done.11
  558.6 2.3 lay_down.1.rest_8_
  560.9 1.7 copy-done.3
  562.6 2.4 lay.3
  (387 shorter events, 102.7 us)
Async XLA Ops:
  6.7 10.7 %collective-permute-start.1 = (bf16[240,384]{1,0:T(8,128)(2,1)S(1)}, bf16[240,384]{1,0:T(8,128)(2,1)S(1)}, u32[]{:S(2)}, u32[]{:S(2)}) collective-permute-start(bf16[240,384]{1,0:T(8,128)(2,1)S(1)} %pick_first.1.rest_0_), channel_id=1, source_target_pairs={{0,1},{1,2},{2,3},{3,0},{4,5},{5,6},{6,7},{7,4},{8,9},{9,10},{10,1... | collective-permute-start | bytes 552968 | tf_op jit(solution)/shard_map/ppermute | solution.py:872
  9.8 14.7 %collective-permute-start.2 = (bf16[240,384]{1,0:T(8,128)(2,1)S(1)}, bf16[240,384]{1,0:T(8,128)(2,1)S(1)}, u32[]{:S(2)}, u32[]{:S(2)}) collective-permute-start(bf16[240,384]{1,0:T(8,128)(2,1)S(1)} %pick_first.1.rest_0_), channel_id=1, source_target_pairs={{0,2},{1,3},{2,0},{3,1},{4,6},{5,7},{6,4},{7,5},{8,10},{9,11},{10,... | collective-permute-start | bytes 552968 | tf_op jit(solution)/shard_map/ppermute | solution.py:872
  12.4 12.1 %collective-permute-start.3 = (bf16[240,384]{1,0:T(8,128)(2,1)S(1)}, bf16[240,384]{1,0:T(8,128)(2,1)S(1)}, u32[]{:S(2)}, u32[]{:S(2)}) collective-permute-start(bf16[240,384]{1,0:T(8,128)(2,1)S(1)} %pick_first.1.rest_0_), channel_id=1, source_target_pairs={{0,3},{1,0},{2,1},{3,2},{4,7},{5,4},{6,5},{7,6},{8,11},{9,8},{10,9... | collective-permute-start | bytes 552968 | tf_op jit(solution)/shard_map/ppermute | solution.py:872
  26.1 17.5 %collective-permute-start.4 = (bf16[960,384]{1,0:T(8,128)(2,1)S(1)}, bf16[960,384]{1,0:T(8,128)(2,1)S(1)}, u32[]{:S(2)}, u32[]{:S(2)}) collective-permute-start(bf16[960,384]{1,0:T(8,128)(2,1)S(1)} %bitcast.33), channel_id=1, source_target_pairs={{0,8},{4,20},{8,0},{12,28},{16,24},{20,4},{24,16},{28,12},{1,9},{5... | collective-permute-start | bytes 2211848 | tf_op jit(solution)/shard_map/ppermute | solution.py:867
  28.2 13.9 %collective-permute-start.11 = (bf16[240,640]{1,0:T(8,128)(2,1)S(1)}, bf16[240,640]{1,0:T(8,128)(2,1)S(1)}, u32[]{:S(2)}, u32[]{:S(2)}) collective-permute-start(bf16[240,640]{1,0:T(8,128)(2,1)S(1)} %pick.1.rest_0_), channel_id=1, source_target_pairs={{0,1},{1,2},{2,3},{3,0},{4,5},{5,6},{6,7},{7,4},{8,9},{9,10},{10,1... | collective-permute-start | bytes 921608 | tf_op jit(solution)/shard_map/ppermute | solution.py:872
  32.7 20.7 %collective-permute-start.12 = (bf16[240,640]{1,0:T(8,128)(2,1)S(1)}, bf16[240,640]{1,0:T(8,128)(2,1)S(1)}, u32[]{:S(2)}, u32[]{:S(2)}) collective-permute-start(bf16[240,640]{1,0:T(8,128)(2,1)S(1)} %pick.1.rest_0_), channel_id=1, source_target_pairs={{0,2},{1,3},{2,0},{3,1},{4,6},{5,7},{6,4},{7,5},{8,10},{9,11},{10,... | collective-permute-start | bytes 921608 | tf_op jit(solution)/shard_map/ppermute | solution.py:872
  34.3 19.3 %collective-permute-start.13 = (bf16[240,640]{1,0:T(8,128)(2,1)S(1)}, bf16[240,640]{1,0:T(8,128)(2,1)S(1)}, u32[]{:S(2)}, u32[]{:S(2)}) collective-permute-start(bf16[240,640]{1,0:T(8,128)(2,1)S(1)} %pick.1.rest_0_), channel_id=1, source_target_pairs={{0,3},{1,0},{2,1},{3,2},{4,7},{5,4},{6,5},{7,6},{8,11},{9,8},{10,9... | collective-permute-start | bytes 921608 | tf_op jit(solution)/shard_map/ppermute | solution.py:872
  35.2 21.9 %collective-permute-start = (bf16[976,256]{1,0:T(8,128)(2,1)S(1)}, bf16[976,256]{1,0:T(8,128)(2,1)S(1)}, u32[]{:S(2)}, u32[]{:S(2)}) collective-permute-start(bf16[976,256]{1,0:T(8,128)(2,1)S(1)} %pad_maximum_fusion), channel_id=1, source_target_pairs={{0,0},{1,4},{2,1},{3,5},{4,2},{5,6},{6,3},{7,7},{8,8},{9,12},{10,9... | collective-permute-start | bytes 1499144 | tf_op jit(solution)/shard_map/ppermute | solution.py:883
  42.1 32.4 %collective-permute-start.5 = (bf16[960,384]{1,0:T(8,128)(2,1)S(1)}, bf16[960,384]{1,0:T(8,128)(2,1)}, u32[]{:S(2)}, u32[]{:S(2)}) collective-permute-start(bf16[960,384]{1,0:T(8,128)(2,1)S(1)} %bitcast.34), channel_id=1, source_target_pairs={{0,16},{4,12},{8,24},{12,4},{16,0},{20,28},{24,8},{28,20},{1,17},{... | collective-permute-start | bytes 2211848 | tf_op jit(solution)/shard_map/ppermute | solution.py:867
  43.6 31.4 %collective-permute-start.6 = (bf16[960,384]{1,0:T(8,128)(2,1)S(1)}, bf16[960,384]{1,0:T(8,128)(2,1)}, u32[]{:S(2)}, u32[]{:S(2)}) collective-permute-start(bf16[960,384]{1,0:T(8,128)(2,1)S(1)} %collective-permute-done.4.rest_1_), channel_id=1, source_target_pairs={{0,16},{4,12},{8,24},{12,4},{16,0},{20,28},{24,8},{28,20},{1,17},{... | collective-permute-start | bytes 2211848 | tf_op jit(solution)/shard_map/ppermute | solution.py:867
  54.5 22.8 %collective-permute-start.16 = (bf16[960,640]{1,0:T(8,128)(2,1)S(1)}, bf16[960,640]{1,0:T(8,128)(2,1)}, u32[]{:S(2)}, u32[]{:S(2)}) collective-permute-start(bf16[960,640]{1,0:T(8,128)(2,1)S(1)} %bitcast.24), channel_id=1, source_target_pairs={{0,8},{4,20},{8,0},{12,28},{16,24},{20,4},{24,16},{28,12},{1,9},{5... | collective-permute-start | bytes 3686408 | tf_op jit(solution)/shard_map/ppermute | solution.py:867
  55.6 19.5 %collective-permute-start.7 = (bf16[960,384]{1,0:T(8,128)(2,1)S(1)}, bf16[960,384]{1,0:T(8,128)(2,1)}, u32[]{:S(2)}, u32[]{:S(2)}) collective-permute-start(bf16[960,384]{1,0:T(8,128)(2,1)S(1)} %bitcast.35), channel_id=1, source_target_pairs={{0,4},{4,0},{8,12},{12,8},{16,20},{20,16},{24,28},{28,24},{1,5},{5... | collective-permute-start | bytes 2211848 | tf_op jit(solution)/shard_map/ppermute | solution.py:867
  57.1 17.4 %collective-permute-start.27 = (bf16[64,640]{1,0:T(8,128)(2,1)S(1)}, bf16[64,640]{1,0:T(8,128)(2,1)S(1)}, u32[]{:S(2)}, u32[]{:S(2)}) collective-permute-start(bf16[64,640]{1,0:T(8,128)(2,1)S(1)} %get-tuple-element.111.rest_0_), channel_id=1, source_target_pairs={{0,1},{1,2},{2,3},{3,0},{4,5},{5,6},{6,7},{7,4},{8,9},{9,10},{10,1... | collective-permute-start | bytes 245768 | tf_op jit(solution)/shard_map/ppermute | solution.py:872
  75.0 21.7 %collective-permute-start.10 = (bf16[960,384]{1,0:T(8,128)(2,1)}, bf16[960,384]{1,0:T(8,128)(2,1)}, u32[]{:S(2)}, u32[]{:S(2)}) collective-permute-start(bf16[960,384]{1,0:T(8,128)(2,1)} %collective-permute-done.6.rest_3_), channel_id=1, source_target_pairs={{0,4},{4,0},{8,12},{12,8},{16,20},{20,16},{24,28},{28,24},{1,5},{5... | collective-permute-start | bytes 2211848 | tf_op jit(solution)/shard_map/ppermute | solution.py:867
  75.1 65.6 %collective-permute-start.17 = (bf16[960,640]{1,0:T(8,128)(2,1)S(1)}, bf16[960,640]{1,0:T(8,128)(2,1)}, u32[]{:S(2)}, u32[]{:S(2)}) collective-permute-start(bf16[960,640]{1,0:T(8,128)(2,1)S(1)} %bitcast.26), channel_id=1, source_target_pairs={{0,16},{4,12},{8,24},{12,4},{16,0},{20,28},{24,8},{28,20},{1,17},{... | collective-permute-start | bytes 3686408 | tf_op jit(solution)/shard_map/ppermute | solution.py:867
  77.2 64.7 %collective-permute-start.19 = (bf16[960,640]{1,0:T(8,128)(2,1)S(1)}, bf16[960,640]{1,0:T(8,128)(2,1)}, u32[]{:S(2)}, u32[]{:S(2)}) collective-permute-start(bf16[960,640]{1,0:T(8,128)(2,1)S(1)} %bitcast.27), channel_id=1, source_target_pairs={{0,4},{4,0},{8,12},{12,8},{16,20},{20,16},{24,28},{28,24},{1,5},{5... | collective-permute-start | bytes 3686408 | tf_op jit(solution)/shard_map/ppermute | solution.py:867
  77.3 66.1 %collective-permute-start.18 = (bf16[960,640]{1,0:T(8,128)(2,1)}, bf16[960,640]{1,0:T(8,128)(2,1)}, u32[]{:S(2)}, u32[]{:S(2)}) collective-permute-start(bf16[960,640]{1,0:T(8,128)(2,1)} %collective-permute-done.16.rest_9_), channel_id=1, source_target_pairs={{0,16},{4,12},{8,24},{12,4},{16,0},{20,28},{24,8},{28,20},{1,17},{... | collective-permute-start | bytes 3686408 | tf_op jit(solution)/shard_map/ppermute | solution.py:867
  80.2 24.0 %collective-permute-start.28 = (bf16[64,640]{1,0:T(8,128)(2,1)S(1)}, bf16[64,640]{1,0:T(8,128)(2,1)S(1)}, u32[]{:S(2)}, u32[]{:S(2)}) collective-permute-start(bf16[64,640]{1,0:T(8,128)(2,1)S(1)} %get-tuple-element.111.rest_0_), channel_id=1, source_target_pairs={{0,2},{1,3},{2,0},{3,1},{4,6},{5,7},{6,4},{7,5},{8,10},{9,11},{10,... | collective-permute-start | bytes 245768 | tf_op jit(solution)/shard_map/ppermute | solution.py:872
  96.8 11.5 %collective-permute-start.29 = (bf16[64,640]{1,0:T(8,128)(2,1)S(1)}, bf16[64,640]{1,0:T(8,128)(2,1)S(1)}, u32[]{:S(2)}, u32[]{:S(2)}) collective-permute-start(bf16[64,640]{1,0:T(8,128)(2,1)S(1)} %get-tuple-element.111.rest_0_), channel_id=1, source_target_pairs={{0,3},{1,0},{2,1},{3,2},{4,7},{5,4},{6,5},{7,6},{8,11},{9,8},{10,9... | collective-permute-start | bytes 245768 | tf_op jit(solution)/shard_map/ppermute | solution.py:872
  104.2 18.6 %collective-permute-start.14 = (bf16[656,256]{1,0:T(8,128)(2,1)}, bf16[656,256]{1,0:T(8,128)(2,1)S(1)}, u32[]{:S(2)}, u32[]{:S(2)}) collective-permute-start(bf16[656,256]{1,0:T(8,128)(2,1)} %get-tuple-element.107.kv2.rest_26_), channel_id=1, source_target_pairs={{0,1},{2,3},{4,5},{6,7},{8,9},{10,11},{12,13},{14,15},{16,17},{18,... | collective-permute-start | bytes 1007624 | tf_op jit(solution)/shard_map/ppermute | solution.py:904
  108.3 14.1 %collective-permute-start.23 = (bf16[224,640]{1,0:T(8,128)(2,1)}, bf16[224,640]{1,0:T(8,128)(2,1)S(1)}, u32[]{:S(2)}, u32[]{:S(2)}) collective-permute-start(bf16[224,640]{1,0:T(8,128)(2,1)} %get-tuple-element.110.rest_0_), channel_id=1, source_target_pairs={{0,1},{1,2},{2,3},{3,0},{4,5},{5,6},{6,7},{7,4},{8,9},{9,10},{10,1... | collective-permute-start | bytes 860168 | tf_op jit(solution)/shard_map/ppermute | solution.py:872
  122.5 17.0 %collective-permute-start.24 = (bf16[224,640]{1,0:T(8,128)(2,1)}, bf16[224,640]{1,0:T(8,128)(2,1)S(1)}, u32[]{:S(2)}, u32[]{:S(2)}) collective-permute-start(bf16[224,640]{1,0:T(8,128)(2,1)} %get-tuple-element.110.rest_0_), channel_id=1, source_target_pairs={{0,2},{1,3},{2,0},{3,1},{4,6},{5,7},{6,4},{7,5},{8,10},{9,11},{10,... | collective-permute-start | bytes 860168 | tf_op jit(solution)/shard_map/ppermute | solution.py:872
  122.8 17.4 %collective-permute-start.25 = (bf16[224,640]{1,0:T(8,128)(2,1)}, bf16[224,640]{1,0:T(8,128)(2,1)}, u32[]{:S(2)}, u32[]{:S(2)}) collective-permute-start(bf16[224,640]{1,0:T(8,128)(2,1)} %get-tuple-element.110.rest_0_), channel_id=1, source_target_pairs={{0,3},{1,0},{2,1},{3,2},{4,7},{5,4},{6,5},{7,6},{8,11},{9,8},{10,9... | collective-permute-start | bytes 860168 | tf_op jit(solution)/shard_map/ppermute | solution.py:872
  140.2 20.6 %collective-permute-start.20 = (bf16[960,640]{1,0:T(8,128)(2,1)}, bf16[960,640]{1,0:T(8,128)(2,1)S(1)}, u32[]{:S(2)}, u32[]{:S(2)}) collective-permute-start(bf16[960,640]{1,0:T(8,128)(2,1)} %collective-permute-done.16.rest_9_), channel_id=1, source_target_pairs={{0,4},{4,0},{8,12},{12,8},{16,20},{20,16},{24,28},{28,24},{1,5},{5... | collective-permute-start | bytes 3686408 | tf_op jit(solution)/shard_map/ppermute | solution.py:867
  140.7 20.1 %collective-permute-start.21 = (bf16[960,640]{1,0:T(8,128)(2,1)}, bf16[960,640]{1,0:T(8,128)(2,1)S(1)}, u32[]{:S(2)}, u32[]{:S(2)}) collective-permute-start(bf16[960,640]{1,0:T(8,128)(2,1)} %collective-permute-done.17.rest_10_), channel_id=1, source_target_pairs={{0,4},{4,0},{8,12},{12,8},{16,20},{20,16},{24,28},{28,24},{1,5},{5... | collective-permute-start | bytes 3686408 | tf_op jit(solution)/shard_map/ppermute | solution.py:867
  141.9 13.7 %collective-permute-start.30 = (bf16[4,64,640]{2,1,0:T(8,128)(2,1)S(1)}, bf16[4,64,640]{2,1,0:T(8,128)(2,1)S(1)}, u32[]{:S(2)}, u32[]{:S(2)}) collective-permute-start(bf16[4,64,640]{2,1,0:T(8,128)(2,1)S(1)} %stack.35.rest_18_), channel_id=1, source_target_pairs={{0,8},{4,20},{8,0},{12,28},{16,24},{20,4},{24,16},{28,12},{1,9},{5... | collective-permute-start | bytes 983048 | tf_op jit(solution)/shard_map/ppermute | solution.py:867
  143.4 12.5 %collective-permute-start.31 = (bf16[4,64,640]{2,1,0:T(8,128)(2,1)S(1)}, bf16[4,64,640]{2,1,0:T(8,128)(2,1)S(1)}, u32[]{:S(2)}, u32[]{:S(2)}) collective-permute-start(bf16[4,64,640]{2,1,0:T(8,128)(2,1)S(1)} %stack.35.rest_18_), channel_id=1, source_target_pairs={{0,16},{4,12},{8,24},{12,4},{16,0},{20,28},{24,8},{28,20},{1,17},{... | collective-permute-start | bytes 983048 | tf_op jit(solution)/shard_map/ppermute | solution.py:867
  143.4 24.2 %collective-permute-start.22 = (bf16[960,640]{1,0:T(8,128)(2,1)}, bf16[960,640]{1,0:T(8,128)(2,1)S(1)}, u32[]{:S(2)}, u32[]{:S(2)}) collective-permute-start(bf16[960,640]{1,0:T(8,128)(2,1)} %collective-permute-done.18.rest_11_), channel_id=1, source_target_pairs={{0,4},{4,0},{8,12},{12,8},{16,20},{20,16},{24,28},{28,24},{1,5},{5... | collective-permute-start | bytes 3686408 | tf_op jit(solution)/shard_map/ppermute | solution.py:867
  155.6 12.1 %collective-permute-start.26 = (bf16[4,224,640]{2,1,0:T(8,128)(2,1)S(1)}, bf16[4,224,640]{2,1,0:T(8,128)(2,1)S(1)}, u32[]{:S(2)}, u32[]{:S(2)}) collective-permute-start(bf16[4,224,640]{2,1,0:T(8,128)(2,1)S(1)} %stack.34.rest_16_), channel_id=1, source_target_pairs={{0,4},{4,0},{8,12},{12,8},{16,20},{20,16},{24,28},{28,24},{1,5},{5... | collective-permute-start | bytes 3440648 | tf_op jit(solution)/shard_map/ppermute | solution.py:867
  190.1 12.8 %collective-permute-start.37 = (bf16[656,256]{1,0:T(8,128)(2,1)}, bf16[656,256]{1,0:T(8,128)(2,1)S(1)}, u32[]{:S(2)}, u32[]{:S(2)}) collective-permute-start(bf16[656,256]{1,0:T(8,128)(2,1)} %get-tuple-element.113.kv2.rest_26_), channel_id=1, source_target_pairs={{0,1},{2,3},{4,5},{6,7},{8,9},{10,11},{12,13},{14,15},{16,17},{18,... | collective-permute-start | bytes 1007624 | tf_op jit(solution)/shard_map/ppermute | solution.py:904
  196.4 38.9 %collective-permute-start.40 = (bf16[960,256]{1,0:T(8,128)(2,1)}, bf16[960,256]{1,0:T(8,128)(2,1)S(1)}, u32[]{:S(2)}, u32[]{:S(2)}) collective-permute-start(bf16[960,256]{1,0:T(8,128)(2,1)} %bitcast.50), channel_id=1, source_target_pairs={{0,0},{1,4},{2,1},{3,5},{4,2},{5,6},{6,3},{7,7},{8,8},{9,12},{10,9... | collective-permute-start | bytes 1474568 | tf_op jit(solution)/shard_map/ppermute | solution.py:883
  276.7 11.7 %collective-permute-start.42 = (bf16[640,256]{1,0:T(8,128)(2,1)S(1)}, bf16[640,256]{1,0:T(8,128)(2,1)S(1)}, u32[]{:S(2)}, u32[]{:S(2)}) collective-permute-start(bf16[640,256]{1,0:T(8,128)(2,1)S(1)} %fusion), channel_id=1, source_target_pairs={{1,0},{3,2},{5,4},{7,6},{9,8},{11,10},{13,12},{15,14},{17,16},{19,... | collective-permute-start | bytes 983048 | tf_op jit(solution)/shard_map/ppermute | solution.py:914
  278.0 37.9 %collective-permute-start.49 = (bf16[256,2560]{1,0:T(8,128)(2,1)}, bf16[256,2560]{1,0:T(8,128)(2,1)S(1)}, u32[]{:S(2)}, u32[]{:S(2)}) collective-permute-start(bf16[256,2560]{1,0:T(8,128)(2,1)} %get-tuple-element.147), channel_id=1, source_target_pairs={{0,4},{4,0},{8,12},{12,8},{16,20},{20,16},{24,28},{28,24},{1,5},{5... | collective-permute-start | bytes 3932168 | tf_op jit(solution)/shard_map/ppermute | solution.py:867
  326.7 40.9 %collective-permute-start.53 = (bf16[2,960,640]{2,1,0:T(8,128)(2,1)S(1)}, bf16[2,960,640]{2,1,0:T(8,128)(2,1)S(1)}, u32[]{:S(2)}, u32[]{:S(2)}) collective-permute-start(bf16[2,960,640]{2,1,0:T(8,128)(2,1)S(1)} %get-tuple-element.149.rest_8_), channel_id=1, source_target_pairs={{0,8},{4,20},{8,0},{12,28},{16,24},{20,4},{24,16},{28,12},{1,9},{5... | collective-permute-start | bytes 7372808 | tf_op jit(solution)/shard_map/ppermute | solution.py:867
  355.0 11.9 %collective-permute-start.52 = (bf16[640,256]{1,0:T(8,128)(2,1)S(1)}, bf16[640,256]{1,0:T(8,128)(2,1)S(1)}, u32[]{:S(2)}, u32[]{:S(2)}) collective-permute-start(bf16[640,256]{1,0:T(8,128)(2,1)S(1)} %fusion.1), channel_id=1, source_target_pairs={{1,0},{3,2},{5,4},{7,6},{9,8},{11,10},{13,12},{15,14},{17,16},{19,... | collective-permute-start | bytes 983048 | tf_op jit(solution)/shard_map/ppermute | solution.py:914
  356.3 22.0 %collective-permute-start.55 = (bf16[256,960]{1,0:T(8,128)(2,1)}, bf16[256,960]{1,0:T(8,128)(2,1)}, u32[]{:S(2)}, u32[]{:S(2)}) collective-permute-start(bf16[256,960]{1,0:T(8,128)(2,1)} %get-tuple-element.158.rest_0_), channel_id=1, source_target_pairs={{0,4},{4,0},{8,12},{12,8},{16,20},{20,16},{24,28},{28,24},{1,5},{5... | collective-permute-start | bytes 1474568 | tf_op jit(solution)/shard_map/ppermute | solution.py:867
  356.7 22.5 %collective-permute-start.58 = (bf16[256,960]{1,0:T(8,128)(2,1)}, bf16[256,960]{1,0:T(8,128)(2,1)}, u32[]{:S(2)}, u32[]{:S(2)}) collective-permute-start(bf16[256,960]{1,0:T(8,128)(2,1)} %get-tuple-element.161.rest_5_), channel_id=1, source_target_pairs={{0,4},{4,0},{8,12},{12,8},{16,20},{20,16},{24,28},{28,24},{1,5},{5... | collective-permute-start | bytes 1474568 | tf_op jit(solution)/shard_map/ppermute | solution.py:867
  356.8 22.5 %collective-permute-start.59 = (bf16[3,256,384]{2,1,0:T(8,128)(2,1)}, bf16[3,256,384]{2,1,0:T(8,128)(2,1)S(1)}, u32[]{:S(2)}, u32[]{:S(2)}) collective-permute-start(bf16[3,256,384]{2,1,0:T(8,128)(2,1)} %get-tuple-element.166), channel_id=1, source_target_pairs={{0,4},{4,0},{8,12},{12,8},{16,20},{20,16},{24,28},{28,24},{1,5},{5... | collective-permute-start | bytes 1769480 | tf_op jit(solution)/shard_map/ppermute | solution.py:867
  367.6 12.7 %collective-permute-start.60 = (bf16[3,256,384]{2,1,0:T(8,128)(2,1)}, bf16[3,256,384]{2,1,0:T(8,128)(2,1)S(1)}, u32[]{:S(2)}, u32[]{:S(2)}) collective-permute-start(bf16[3,256,384]{2,1,0:T(8,128)(2,1)} %get-tuple-element.167), channel_id=1, source_target_pairs={{0,4},{4,0},{8,12},{12,8},{16,20},{20,16},{24,28},{28,24},{1,5},{5... | collective-permute-start | bytes 1769480 | tf_op jit(solution)/shard_map/ppermute | solution.py:867
  367.6 11.7 %collective-permute-start.57 = (bf16[256,960]{1,0:T(8,128)(2,1)}, bf16[256,960]{1,0:T(8,128)(2,1)}, u32[]{:S(2)}, u32[]{:S(2)}) collective-permute-start(bf16[256,960]{1,0:T(8,128)(2,1)} %get-tuple-element.160.rest_4_), channel_id=1, source_target_pairs={{0,4},{4,0},{8,12},{12,8},{16,20},{20,16},{24,28},{28,24},{1,5},{5... | collective-permute-start | bytes 1474568 | tf_op jit(solution)/shard_map/ppermute | solution.py:867
  395.2 32.9 %collective-permute-start.63 = (bf16[2,960,384]{2,1,0:T(8,128)(2,1)S(1)}, bf16[2,960,384]{2,1,0:T(8,128)(2,1)}, u32[]{:S(2)}, u32[]{:S(2)}) collective-permute-start(bf16[2,960,384]{2,1,0:T(8,128)(2,1)S(1)} %get-tuple-element.175.rest_0_), channel_id=1, source_target_pairs={{0,8},{4,20},{8,0},{12,28},{16,24},{20,4},{24,16},{28,12},{1,9},{5... | collective-permute-start | bytes 4423688 | tf_op jit(solution)/shard_map/ppermute | solution.py:867
  396.1 30.2 %collective-permute-start.64 = (bf16[960,640]{1,0:T(8,128)(2,1)}, bf16[960,640]{1,0:T(8,128)(2,1)}, u32[]{:S(2)}, u32[]{:S(2)}) collective-permute-start(bf16[960,640]{1,0:T(8,128)(2,1)} %get-tuple-element.156.rest_17_), channel_id=1, source_target_pairs={{0,16},{4,12},{8,24},{12,4},{16,0},{20,28},{24,8},{28,20},{1,17},{... | collective-permute-start | bytes 3686408 | tf_op jit(solution)/shard_map/ppermute | solution.py:867
  397.8 34.0 %collective-permute-start.66 = (bf16[960,640]{1,0:T(8,128)(2,1)}, bf16[960,640]{1,0:T(8,128)(2,1)}, u32[]{:S(2)}, u32[]{:S(2)}) collective-permute-start(bf16[960,640]{1,0:T(8,128)(2,1)} %get-tuple-element.180), channel_id=1, source_target_pairs={{0,1},{3,0},{5,6},{6,7},{8,9},{11,8},{13,14},{14,15},{16,17},{19,1... | collective-permute-start | bytes 3686408 | tf_op jit(solution)/shard_map/ppermute | solution.py:941
  399.7 35.6 %collective-permute-start.67 = (bf16[960,640]{1,0:T(8,128)(2,1)S(1)}, bf16[960,640]{1,0:T(8,128)(2,1)}, u32[]{:S(2)}, u32[]{:S(2)}) collective-permute-start(bf16[960,640]{1,0:T(8,128)(2,1)S(1)} %get-tuple-element.150.rest_0_), channel_id=1, source_target_pairs={{2,0},{3,1},{4,6},{5,7},{10,8},{11,9},{12,14},{13,15},{18,16},{19,... | collective-permute-start | bytes 3686408 | tf_op jit(solution)/shard_map/ppermute | solution.py:941
  401.0 43.8 %collective-permute-start.68 = (bf16[960,640]{1,0:T(8,128)(2,1)}, bf16[960,640]{1,0:T(8,128)(2,1)}, u32[]{:S(2)}, u32[]{:S(2)}) collective-permute-start(bf16[960,640]{1,0:T(8,128)(2,1)} %get-tuple-element.180), channel_id=1, source_target_pairs={{1,0},{2,1},{4,7},{7,6},{9,8},{10,9},{12,15},{15,14},{17,16},{18,1... | collective-permute-start | bytes 3686408 | tf_op jit(solution)/shard_map/ppermute | solution.py:941
  429.9 40.9 %collective-permute-start.65 = (bf16[960,384]{1,0:T(8,128)(2,1)S(1)}, bf16[960,384]{1,0:T(8,128)(2,1)S(1)}, u32[]{:S(2)}, u32[]{:S(2)}) collective-permute-start(bf16[960,384]{1,0:T(8,128)(2,1)S(1)} %get-tuple-element.179.rest_3_), channel_id=1, source_target_pairs={{0,16},{4,12},{8,24},{12,4},{16,0},{20,28},{24,8},{28,20},{1,17},{... | collective-permute-start | bytes 2211848 | tf_op jit(solution)/shard_map/ppermute | solution.py:867
  448.1 15.3 %collective-permute-start.69 = (bf16[480,640]{1,0:T(8,128)(2,1)S(1)}, bf16[480,640]{1,0:T(8,128)(2,1)S(1)}, u32[]{:S(2)}, u32[]{:S(2)}) collective-permute-start(bf16[480,640]{1,0:T(8,128)(2,1)S(1)} %get-tuple-element.182), channel_id=1, source_target_pairs={{0,4},{4,0},{8,12},{12,8},{16,20},{20,16},{24,28},{28,24},{1,5},{5... | collective-permute-start | bytes 1843208 | tf_op jit(solution)/shard_map/ppermute | solution.py:867
  448.1 22.4 %collective-permute-start.75 = (bf16[240,640]{1,0:T(8,128)(2,1)S(1)}, bf16[240,640]{1,0:T(8,128)(2,1)S(1)}, u32[]{:S(2)}, u32[]{:S(2)}) collective-permute-start(bf16[240,640]{1,0:T(8,128)(2,1)S(1)} %get-tuple-element.191), channel_id=1, source_target_pairs={{0,1},{1,2},{2,3},{3,0},{4,5},{5,6},{6,7},{7,4},{8,9},{9,10},{10,1... | collective-permute-start | bytes 921608 | tf_op jit(solution)/shard_map/ppermute | solution.py:872
  462.0 53.3 %collective-permute-start.39 = (bf16[960,256]{1,0:T(8,128)(2,1)S(1)}, bf16[960,256]{1,0:T(8,128)(2,1)S(1)}, u32[]{:S(2)}, u32[]{:S(2)}) collective-permute-start(bf16[960,256]{1,0:T(8,128)(2,1)S(1)} %copy-done.95), channel_id=1, source_target_pairs={{0,0},{4,1},{1,2},{5,3},{2,4},{6,5},{3,6},{7,7},{8,8},{12,9},{9,10... | collective-permute-start | bytes 1474568 | tf_op jit(solution)/shard_map/ppermute | solution.py:883
  462.7 53.9 %collective-permute-start.54 = (bf16[960,256]{1,0:T(8,128)(2,1)S(1)}, bf16[960,256]{1,0:T(8,128)(2,1)S(1)}, u32[]{:S(2)}, u32[]{:S(2)}) collective-permute-start(bf16[960,256]{1,0:T(8,128)(2,1)S(1)} %copy-done.96), channel_id=1, source_target_pairs={{0,0},{4,1},{1,2},{5,3},{2,4},{6,5},{3,6},{7,7},{8,8},{12,9},{9,10... | collective-permute-start | bytes 1474568 | tf_op jit(solution)/shard_map/ppermute | solution.py:883
  463.4 41.4 %collective-permute-start.76 = (bf16[240,640]{1,0:T(8,128)(2,1)S(1)}, bf16[240,640]{1,0:T(8,128)(2,1)S(1)}, u32[]{:S(2)}, u32[]{:S(2)}) collective-permute-start(bf16[240,640]{1,0:T(8,128)(2,1)S(1)} %get-tuple-element.192), channel_id=1, source_target_pairs={{0,2},{1,3},{2,0},{3,1},{4,6},{5,7},{6,4},{7,5},{8,10},{9,11},{10,... | collective-permute-start | bytes 921608 | tf_op jit(solution)/shard_map/ppermute | solution.py:872
  470.5 39.7 %collective-permute-start.73 = (bf16[2,120,640]{2,1,0:T(8,128)(2,1)S(1)}, bf16[2,120,640]{2,1,0:T(8,128)(2,1)S(1)}, u32[]{:S(2)}, u32[]{:S(2)}) collective-permute-start(bf16[2,120,640]{2,1,0:T(8,128)(2,1)S(1)} %get-tuple-element.183.rest_0_), channel_id=1, source_target_pairs={{0,8},{4,20},{8,0},{12,28},{16,24},{20,4},{24,16},{28,12},{1,9},{5... | collective-permute-start | bytes 921608 | tf_op jit(solution)/shard_map/ppermute | solution.py:867
  470.8 43.4 %collective-permute-start.77 = (bf16[240,640]{1,0:T(8,128)(2,1)S(1)}, bf16[240,640]{1,0:T(8,128)(2,1)S(1)}, u32[]{:S(2)}, u32[]{:S(2)}) collective-permute-start(bf16[240,640]{1,0:T(8,128)(2,1)S(1)} %get-tuple-element.193), channel_id=1, source_target_pairs={{0,3},{1,0},{2,1},{3,2},{4,7},{5,4},{6,5},{7,6},{8,11},{9,8},{10,9... | collective-permute-start | bytes 921608 | tf_op jit(solution)/shard_map/ppermute | solution.py:872
  504.7 13.8 %collective-permute-start.70 = (bf16[240,384]{1,0:T(8,128)(2,1)S(1)}, bf16[240,384]{1,0:T(8,128)(2,1)S(1)}, u32[]{:S(2)}, u32[]{:S(2)}) collective-permute-start(bf16[240,384]{1,0:T(8,128)(2,1)S(1)} %get-tuple-element.185), channel_id=1, source_target_pairs={{0,1},{1,2},{2,3},{3,0},{4,5},{5,6},{6,7},{7,4},{8,9},{9,10},{10,1... | collective-permute-start | bytes 552968 | tf_op jit(solution)/shard_map/ppermute | solution.py:872
  510.2 15.4 %collective-permute-start.71 = (bf16[240,384]{1,0:T(8,128)(2,1)S(1)}, bf16[240,384]{1,0:T(8,128)(2,1)S(1)}, u32[]{:S(2)}, u32[]{:S(2)}) collective-permute-start(bf16[240,384]{1,0:T(8,128)(2,1)S(1)} %get-tuple-element.186), channel_id=1, source_target_pairs={{0,2},{1,3},{2,0},{3,1},{4,6},{5,7},{6,4},{7,5},{8,10},{9,11},{10,... | collective-permute-start | bytes 552968 | tf_op jit(solution)/shard_map/ppermute | solution.py:872
  514.2 11.4 %collective-permute-start.74 = (bf16[120,640]{1,0:T(8,128)(2,1)S(1)}, bf16[120,640]{1,0:T(8,128)(2,1)S(1)}, u32[]{:S(2)}, u32[]{:S(2)}) collective-permute-start(bf16[120,640]{1,0:T(8,128)(2,1)S(1)} %get-tuple-element.190.rest_3_), channel_id=1, source_target_pairs={{0,16},{4,12},{8,24},{12,4},{16,0},{20,28},{24,8},{28,20},{1,17},{... | collective-permute-start | bytes 460808 | tf_op jit(solution)/shard_map/ppermute | solution.py:867
  515.3 18.0 %collective-permute-start.92 = (bf16[240,640]{1,0:T(8,128)(2,1)S(1)}, bf16[240,640]{1,0:T(8,128)(2,1)S(1)}, u32[]{:S(2)}, u32[]{:S(2)}) collective-permute-start(bf16[240,640]{1,0:T(8,128)(2,1)S(1)} %sum_ring.2.rest_0_), channel_id=1, source_target_pairs={{0,8},{4,20},{8,0},{12,28},{16,24},{20,4},{24,16},{28,12},{1,9},{5... | collective-permute-start | bytes 921608 | tf_op jit(solution)/shard_map/ppermute | solution.py:867
  516.6 18.2 %collective-permute-start.93 = (bf16[240,640]{1,0:T(8,128)(2,1)S(1)}, bf16[240,640]{1,0:T(8,128)(2,1)S(1)}, u32[]{:S(2)}, u32[]{:S(2)}) collective-permute-start(bf16[240,640]{1,0:T(8,128)(2,1)S(1)} %sum_ring.2.rest_0_), channel_id=1, source_target_pairs={{0,16},{4,12},{8,24},{12,4},{16,0},{20,28},{24,8},{28,20},{1,17},{... | collective-permute-start | bytes 921608 | tf_op jit(solution)/shard_map/ppermute | solution.py:867
  518.6 17.1 %collective-permute-start.94 = (bf16[240,640]{1,0:T(8,128)(2,1)S(1)}, bf16[240,640]{1,0:T(8,128)(2,1)S(1)}, u32[]{:S(2)}, u32[]{:S(2)}) collective-permute-start(bf16[240,640]{1,0:T(8,128)(2,1)S(1)} %sum_ring.2.rest_0_), channel_id=1, source_target_pairs={{0,24},{4,28},{8,16},{12,20},{16,8},{20,12},{24,0},{28,4},{1,25},{... | collective-permute-start | bytes 921608 | tf_op jit(solution)/shard_map/ppermute | solution.py:867
  525.6 11.9 %collective-permute-start.95 = (bf16[240,640]{1,0:T(8,128)(2,1)S(1)}, bf16[240,640]{1,0:T(8,128)(2,1)S(1)}, u32[]{:S(2)}, u32[]{:S(2)}) collective-permute-start(bf16[240,640]{1,0:T(8,128)(2,1)S(1)} %sum_ring.2.rest_0_), channel_id=1, source_target_pairs={{0,4},{4,0},{8,12},{12,8},{16,20},{20,16},{24,28},{28,24},{1,5},{5... | collective-permute-start | bytes 921608 | tf_op jit(solution)/shard_map/ppermute | solution.py:867
  534.8 12.1 %collective-permute-start.78 = (bf16[240,384]{1,0:T(8,128)(2,1)S(1)}, bf16[240,384]{1,0:T(8,128)(2,1)S(1)}, u32[]{:S(2)}, u32[]{:S(2)}) collective-permute-start(bf16[240,384]{1,0:T(8,128)(2,1)S(1)} %sum_ring.3.rest_8_.rest_0_), channel_id=1, source_target_pairs={{0,8},{4,20},{8,0},{12,28},{16,24},{20,4},{24,16},{28,12},{1,9},{5... | collective-permute-start | bytes 552968 | tf_op jit(solution)/shard_map/ppermute | solution.py:867
  535.7 10.7 %collective-permute-start.87 = (bf16[120,640]{1,0:T(8,128)(2,1)S(1)}, bf16[120,640]{1,0:T(8,128)(2,1)S(1)}, u32[]{:S(2)}, u32[]{:S(2)}) collective-permute-start(bf16[120,640]{1,0:T(8,128)(2,1)S(1)} %sum_two.1.rest_3_.rest_0_), channel_id=1, source_target_pairs={{0,24},{4,28},{8,16},{12,20},{16,8},{20,12},{24,0},{28,4},{1,25},{... | collective-permute-start | bytes 460808 | tf_op jit(solution)/shard_map/ppermute | solution.py:867
  541.0 9.3 %collective-permute-start.80 = (bf16[240,384]{1,0:T(8,128)(2,1)S(1)}, bf16[240,384]{1,0:T(8,128)(2,1)S(1)}, u32[]{:S(2)}, u32[]{:S(2)}) collective-permute-start(bf16[240,384]{1,0:T(8,128)(2,1)S(1)} %sum_ring.3.rest_8_.rest_0_), channel_id=1, source_target_pairs={{0,24},{4,28},{8,16},{12,20},{16,8},{20,12},{24,0},{28,4},{1,25},{... | collective-permute-start | bytes 552968 | tf_op jit(solution)/shard_map/ppermute | solution.py:867
  550.4 10.5 %collective-permute-start.81 = (bf16[240,384]{1,0:T(8,128)(2,1)S(1)}, bf16[240,384]{1,0:T(8,128)(2,1)S(1)}, u32[]{:S(2)}, u32[]{:S(2)}) collective-permute-start(bf16[240,384]{1,0:T(8,128)(2,1)S(1)} %sum_ring.3.rest_8_.rest_0_), channel_id=1, source_target_pairs={{0,4},{4,0},{8,12},{12,8},{16,20},{20,16},{24,28},{28,24},{1,5},{5... | collective-permute-start | bytes 552968 | tf_op jit(solution)/shard_map/ppermute | solution.py:867
  (134 other events, 1325.7 us)

commit v6 on v5

--- a/solution.py
+++ b/solution.py
@@ -142,7 +142,8 @@
         whole[:, w * n : (w + 1) * n] = part[...]
 
 
-def attend_kernel(q_ref, kv0, kv1, kv2, o_ref, lse_ref, bias, kv):
+def attend_kernel(q_ref, kv0, kv1, kv2, *rest):
+    o_ref, lse_ref, bias, kv = rest[-4:]
     window_of((kv0, kv1, kv2), kv)
     bias[...] = bias_of(kv)
 
@@ -165,18 +166,18 @@
     lax.fori_loop(0, KV_HEADS, head, 0)
 
 
-def attend(q, kvs):
+def attend(q, kvs, after=()):
     width, n = q.shape
     return pl.pallas_call(
         attend_kernel,
         out_shape=(shape((width, n), bf16), shape((HEADS, n), f32)),
-        in_specs=[WHOLE] * 4,
+        in_specs=[WHOLE] * 4 + [LEFT] * len(after),
         out_specs=(WHOLE,) * 2,
         scratch_shapes=[pltpu.VMEM((3 * n, n), f32), pltpu.VMEM((2 * KVW + IDS, 3 * n), bf16)],
         cost_estimate=BRIEF,
         compiler_params=pltpu.CompilerParams(vmem_limit_bytes=24 << 20),
         name="attend",
-    )(q, *kvs)
+    )(q, *kvs, *after)
 
 
 def attend_back_kernel(sc, p_ref, q_ref, kv0, kv1, kv2, lse_ref, do_ref, cos_ref, sin_ref, *rest):
@@ -234,17 +235,10 @@
 
 def fetch_ffn(mine_b, other_b, down, wb, wd, sem_b, sem_d, core, chip):
     fetch(mine_b, other_b, wb, sem_b, core, chip)
-    half, n, width = down[0].shape[1], down[2].shape[1], wd.shape[1]
-
-    def copy(part, row, size):
-        rows = pl.ds(pl.multiple_of(row, 16), size)
+    half = down[0].shape[1]
+    for c, part in ((core, down[0]), (1 - core, down[1])):
+        rows = pl.ds(pl.multiple_of(c * half, half), half)
         pltpu.make_async_copy(part, wd.at[:, rows], sem_d).start()
-
-    copy(down[0], core * half, half)
-    copy(down[1], (1 - core) * half, half)
-    for kind, parts in ((core, down[2:6]), (1 - core, down[6:10])):
-        for who, part in zip(whose(kind), parts):
-            copy(part, 2 * half + (kind * 4 + (chip ^ who)) * n, n)
 
 
 def arrived_down(wd, sem_d):
@@ -262,9 +256,9 @@
 
 def post_kernel(last, sc, ot_ref, h_ref, gain_ref, gain_a, cos_ref, sin_ref, *rest):
     mine_a, other_a, mine_b, other_b = rest[:4], rest[4:8], rest[8:12], rest[12:16]
-    down, ids_ref = rest[16:26], rest[26]
-    o_ref, h1_ref, b_ref, gate_ref, up_ref, z_ref, next_ref = rest[27:34]
-    more, rest = rest[34 : 34 + (0 if last else 3)], rest[34 + (0 if last else 3) :]
+    down, ids_ref = rest[16:18], rest[18]
+    o_ref, h1_ref, b_ref, gate_ref, up_ref, z_ref, next_ref = rest[19:26]
+    more, rest = rest[26 : 26 + (0 if last else 3)], rest[26 + (0 if last else 3) :]
     wa, sem_a, wb, sem_b, wd, sem_d = rest
     core, chip = sc[0], sc[1]
     fetch(mine_a, other_a, wa, sem_a, core, chip)
@@ -311,7 +305,7 @@
     return pl.pallas_call(
         functools.partial(post_kernel, last),
         out_shape=tuple(outs),
-        in_specs=[SCALARS] + [WHOLE] * 6 + [LEFT] * 26 + [WHOLE],
+        in_specs=[SCALARS] + [WHOLE] * 6 + [LEFT] * 18 + [WHOLE],
         out_specs=(WHOLE,) * len(outs),
         scratch_shapes=scratch_a(width) + scratch_ffn(width, hidden // 4),
         cost_estimate=BRIEF,
@@ -402,7 +396,7 @@
     mine_a, other_a = take(4), take(4)
     if not end:
         mine_b, other_b = take(4), take(4)
-        down = take(10)
+        down = take(2)
     if start:
         (g_ref,) = take(1)
     else:
@@ -445,7 +439,7 @@
     scratch = scratch_a(width)
     if not end:
         args += [*wb[0], *wb[1], *wd]
-        specs += [LEFT] * 18
+        specs += [LEFT] * 10
         scratch += scratch_ffn(width, wb[0][0].shape[1])
     args += list(tail)
     specs += [WHOLE] * len(tail)
@@ -689,27 +683,21 @@
 
 
 def pick_down_kernel(sc, down, *rest):
-    far_ref, near_ref, sems = rest[-3:]
-    half, n = far_ref.shape[0], near_ref.shape[0]
-    copies = []
-    for i, (out, row) in enumerate(((far_ref, sc[0] * half), (near_ref, 2 * half + (sc[0] * 4 + sc[1]) * n))):
-        rows = pl.ds(pl.multiple_of(row, 16), out.shape[0])
-        copies.append(pltpu.make_async_copy(down.at[rows, :], out, sems.at[i]))
-    for copy in copies:
-        copy.start()
-    for copy in copies:
-        copy.wait()
+    out_ref, sem = rest[-2:]
+    half = out_ref.shape[0]
+    copy = pltpu.make_async_copy(down.at[pl.ds(pl.multiple_of(sc[0] * half, half), half), :], out_ref, sem)
+    copy.start()
+    copy.wait()
 
 
 def pick_down(sc, down, after):
     rows, cols = down.shape
-    n = rows // 240 * 16
     return pl.pallas_call(
         pick_down_kernel,
-        out_shape=(shape((rows // 2 - 4 * n, cols), bf16), shape((n, cols), bf16)),
+        out_shape=shape((rows // 2, cols), bf16),
         in_specs=[SCALARS] + [LEFT] * (1 + len(after)),
-        out_specs=(WHOLE, WHOLE),
-        scratch_shapes=[pltpu.SemaphoreType.DMA((2,))],
+        out_specs=WHOLE,
+        scratch_shapes=[pltpu.SemaphoreType.DMA],
         cost_estimate=BRIEF,
         compiler_params=pltpu.CompilerParams(vmem_limit_bytes=16 << 20),
         name="pick_down",
@@ -736,7 +724,7 @@
 
 def stack_kernel(sc, *rest):
     parts, out_ref, sems = rest[:4], rest[-2], rest[-1]
-    copies = [pltpu.make_async_copy(p, out_ref.at[(sc[2] - s) & 3], sems.at[s]) for s, p in enumerate(parts)]
+    copies = [pltpu.make_async_copy(p, out_ref.at[sc[2] ^ s], sems.at[s]) for s, p in enumerate(parts)]
     for copy in copies:
         copy.start()
     for copy in copies:
@@ -781,39 +769,51 @@
 
 def sum_second(sc, own, got, after):
     def kernel(sc, own_ref, got_ref, *rest):
-        outs, total = rest[-5:-1], rest[-1]
+        send_ref, keep_ref, total = rest[-3:]
         n = total.shape[1]
         for j in range(4):
             rows = slice(j * n, (j + 1) * n)
             total[j] = own_ref[rows, :] + got_ref[rows, :].astype(f32)
-        for s, out in enumerate(outs):
-            out[...] = total[(sc[2] + s) & 3].astype(out.dtype)
+        like = sc[2] & 1
+        for h in range(2):
+            send_ref[h] = total[2 * h + 1 - like].astype(bf16)
+            keep_ref[h] = total[2 * h + like]
 
     rows, cols = own.shape
     part = (rows // 4, cols)
-    outs = [shape(part, f32)] + [shape(part, bf16)] * 3
+    outs = [shape((2,) + part, bf16), shape((2,) + part, f32)]
     return small(kernel, sc, [own, got], outs, [pltpu.VMEM((4,) + part, f32)], after, "sum_second")
 
 
-def sum_ring(sc, own, got, after):
-    def kernel(sc, own_ref, *rest):
-        out_ref = rest[-1]
-        out_ref[...] = (own_ref[...] + sum(g[...].astype(f32) for g in rest[:3])).astype(bf16)
-
-    return small(kernel, sc, [own, *got], [shape(own.shape, bf16)], [], after, "sum_ring")[0]
+def sum_third(sc, keep, got, after):
+    def kernel(sc, keep_ref, got_ref, *rest):
+        send_ref, own_ref = rest[-2:]
+        h = sc[2] >> 1
+        send_ref[...] = (keep_ref[1 - h] + got_ref[1 - h].astype(f32)).astype(bf16)
+        own_ref[...] = keep_ref[h] + got_ref[h].astype(f32)
+
+    part = keep.shape[1:]
+    return small(kernel, sc, [keep, got], [shape(part, bf16), shape(part, f32)], [], after, "sum_third")
+
+
+def down_pair(sc, own, got, after):
+    def kernel(sc, own_ref, got_ref, *rest):
+        rest[-1][...] = (own_ref[...].astype(f32) + got_ref[...].astype(f32)).astype(bf16)
+
+    return small(kernel, sc, [own, got], [shape(own.shape, bf16)], [], after, "down_pair")[0]
 
 
 def down_ring(sc, own, got, after):
-    def kernel(sc, own_ref, *rest):
-        give_ref, keep_ref, total = rest[-3:]
+    def kernel(sc, own_ref, got_ref, *rest):
+        give_ref, keep_ref = rest[-2:]
         half = give_ref.shape[0]
-        total[...] = own_ref[...].astype(f32) + sum(g[...].astype(f32) for g in rest[:3])
-        give_ref[...] = total[pl.ds(pl.multiple_of((1 - sc[0]) * half, half), half), :].astype(bf16)
-        keep_ref[...] = total[pl.ds(pl.multiple_of(sc[0] * half, half), half), :].astype(bf16)
+        for out, c in ((give_ref, 1 - sc[0]), (keep_ref, sc[0])):
+            rows = pl.ds(pl.multiple_of(c * half, half), half)
+            out[...] = (own_ref[rows, :].astype(f32) + got_ref[rows, :].astype(f32)).astype(bf16)
 
     rows, cols = own.shape
     half = shape((rows // 2, cols), bf16)
-    return small(kernel, sc, [own, *got], [half, half], [pltpu.VMEM((rows, cols), f32)], after, "down_ring")
+    return small(kernel, sc, [own, got], [half, half], [], after, "down_ring")
 
 
 def down_split(sc, keep, given, after):
@@ -867,9 +867,10 @@
     return lax.ppermute(value, "dp", [(i, i ^ bits[i & 1]) for i in range(count)])
 
 
-def turn_z(value, step):
-    count = lax.axis_size("fsdp")
-    return lax.ppermute(value, "fsdp", [(i, (i + step) % count) for i in range(count)])
+def flip_z(value, bit, where=lambda d, z: True):
+    count, depth = lax.axis_size("dp"), lax.axis_size("fsdp")
+    pairs = [(d * depth + z, d * depth + (z ^ bit)) for d in range(count) for z in range(depth) if where(d, z)]
+    return lax.ppermute(value, ("dp", "fsdp"), pairs)
 
 
 def home_to_work(value, back=False):
@@ -889,7 +890,8 @@
 
 
 def turns(shard):
-    return [shard] + [turn_z(shard, s) for s in range(1, lax.axis_size("fsdp"))]
+    far = flip_z(shard, 2)
+    return shard, flip_z(shard, 1), far, flip_z(far, 1)
 
 
 def plane_gather(piece):
@@ -928,17 +930,6 @@
 
 def across(pieces):
     return tuple(flip(p, CORE) for p in pieces)
-
-
-def to_owners(part, step):
-    count, depth = lax.axis_size("dp"), lax.axis_size("fsdp")
-    pairs = []
-    for d in range(count):
-        for a in range(depth):
-            b = (a + step) % depth
-            if (b >> 1) == (d & 1):
-                pairs.append((d * depth + a, d * depth + b))
-    return lax.ppermute(part, ("dp", "fsdp"), pairs)
 
 
 def body(tokens, segment_ids, attn_gain, query_weight, key_weight, value_weight, out_weight, ffn_gain, gate_weight, up_weight, down_weight, cotangent):
@@ -963,69 +954,76 @@
     piece_b = pick(sc, gate_weight, up_weight, [whole_a])
     whole_b = stack(sc, turns(piece_b)).reshape(depth * rows, piece_b.shape[1])
     wb = plane_gather(whole_b)
-    far_d, near_d = pick_down(sc, down_weight.T, [whole_b])
-    parts_n, parts_f = turns(near_d), turns(far_d)
+    parts_d = turns(pick_down(sc, down_weight.T, [whole_b]))
 
     h_0, a0, q0, own = pre(sc, tokens, gain_a, cos, sin, *wa, [whole_b])
     kv0 = window(own)
-    near_d = plane_gather(stack(sc, parts_n, [q0]))
     o0, lse0 = attend(q0, kv0)
-    far_d = stack(sc, parts_f, [o0])
-    weights = wa, wb, (far_d, flip(far_d, CORE), *near_d[0], *near_d[1])
+    whole_d = stack(sc, parts_d, [o0])
+    weights = wa, wb, (whole_d, flip(whole_d, CORE))
     cot = home_to_work(cotangent[0].T)
     mixed0, h1_0, b0, gate0, up0, z0, h_1, a1, q1, own = post(False, sc, o0, h_0, gain_f, gain_a, cos, sin, own, *weights)
     kv1 = window(own)
-    o1, lse1 = attend(q1, kv1)
+    across_0 = across((a0, b0, mixed0))
+    o1, lse1 = attend(q1, kv1, across_0)
     mixed1, h1_1, b1, gate1, up1, z1, output = post(True, sc, o1, h_1, gain_f, gain_a, cos, sin, own, *weights)
-    output = home_to_work(output, back=True).T
+    output = home_to_work(output, back=True)
+    across_1 = across((a1, b1, mixed1))
 
     gb1, act1, away1, zk1, zs1, g1, p1, dgain_f1, do = back(True, False, sc, weights, [cot], [gate1, up1, h1_1, gain_f, z1])
-    dq1, three1, far, near, own = attend_back(sc, p1, q1, kv1, lse1, do, cos, sin)
+    across_2 = across((gb1, away1, zs1))
+    dq1, three1, far, near, own = attend_back(sc, p1, q1, kv1, lse1, do, cos, sin, [output, *across_1])
     near, far = unwindow(far, near)
+    (three1,) = across((three1,))
     tail = [g1, dq1, own, near, far, h_1, gain_a, cos, sin]
-    dk1, dv1, one1, dgain_a1, gb0, act0, away0, zk0, zs0, g1, p0, dgain_f0, do = back(False, False, sc, weights, tail, [gate0, up0, h1_0, gain_f, z0])
-
-    def pair(*own):
-        return [*own, *across(own)]
-
-    send_b, keep_b = grad_ffn(sc, pair(b1, b0), [act1, act0, *across((away1, away0))])
+    dk1, dv1, one1, dgain_a1, gb0, act0, away0, zk0, zs0, g1, p0, dgain_f0, do = back(False, False, sc, weights, tail, [gate0, up0, h1_0, gain_f, z0], [three1, *across_2])
+
+    away0, gb0_, zs0, one1 = across((away0, gb0, zs0, one1))
+    send_b, keep_b = grad_ffn(sc, [b1, b0, across_1[1], across_0[1]], [act1, act0, across_2[1], away0])
     got_b = flip(send_b, SIDE, BACK)
-    like_d, unlike_d = grad_down(sc, pair(gb1, gb0), [zk1, zk0, *across((zs1, zs0))], [send_b])
-    got_d = [to_owners(unlike_d, 1), to_owners(like_d, 2), to_owners(unlike_d, 3)]
-    owner = (z >> 1) == core
-    own_d = jnp.where(owner, like_d, jnp.zeros_like(like_d))
-
-    dq0, three0, far, near, own = attend_back(sc, p0, q0, kv0, lse0, do, cos, sin, [like_d])
+    like_d, unlike_d = grad_down(sc, [gb1, gb0, across_2[0], gb0_], [zk1, zk0, across_2[2], zs0], [send_b])
+    got_d = flip_z(unlike_d, 1)
+
+    dq0, three0, far, near, own = attend_back(sc, p0, q0, kv0, lse0, do, cos, sin, [like_d, one1])
     near, far = unwindow(far, near)
-    later_b, own_b = sum_first(sc, keep_b, got_b, [own])
+    (three0,) = across((three0,))
+    later_b, own_b = sum_first(sc, keep_b, got_b, [own, three0])
     more_b = flip(later_b, BACK, SIDE)
     tail = [g1, dq0, own, near, far, h_0, gain_a, cos, sin]
     dk0, dv0, one0, dgain_a0, grad_tokens = back(False, True, sc, weights, tail, None, [later_b])
-    grad_tokens = home_to_work(grad_tokens, back=True).astype(f32).T
-
+    grad_tokens = home_to_work(grad_tokens, back=True)
+
+    pair_d = down_pair(sc, like_d, got_d, [one0])
+    got_d = flip_z(pair_d, 2, lambda d, z: (z >> 1) != (d & 1))
     own = [dq1, dq0, dk1, dk0, dv1, dv0, p1, p0]
-    send_a, keep_a = grad_attention(sc, pair(a1, a0), pair(mixed1, mixed0), own, across((three1, three0, one1, one0)), [dgain_a1, dgain_a0, dgain_f1, dgain_f0], [])
+    got = [three1, three0, one1, flip(one0, CORE)]
+    send_a, keep_a = grad_attention(sc, [a1, a0, across_1[0], across_0[0]], [mixed1, mixed0, across_1[2], across_0[2]], own, got, [dgain_a1, dgain_a0, dgain_f1, dgain_f0], [pair_d])
     got_a = flip(send_a, SIDE, BACK)
-    ring_b = sum_second(sc, own_b, more_b, [send_a])
-    ring_b, parts_b = ring_b[0], [turn_z(v, s + 1) for s, v in enumerate(ring_b[1:])]
-    later_a, own_a = sum_first(sc, keep_a, got_a, [ring_b])
+    send_b, ring_b = sum_second(sc, own_b, more_b, [send_a])
+    got_b = flip_z(send_b, 1)
+    later_a, own_a = sum_first(sc, keep_a, got_a, [ring_b, grad_tokens])
     more_a = flip(later_a, BACK, SIDE)
-    give, keep = down_ring(sc, own_d, got_d, [later_a])
+    send_b, ring_b = sum_third(sc, ring_b, got_b, [later_a])
+    got_b = flip_z(send_b, 2)
+    give, keep = down_ring(sc, pair_d, got_d, [send_b])
     send_d, keep_d = down_split(sc, keep, flip(give, CORE), [])
     got_d = flip(send_d, SIDE, BACK)
-    ring_a = sum_second(sc, own_a, more_a, [send_d])
-    ring_a, parts_a = ring_a[0], [turn_z(v, s + 1) for s, v in enumerate(ring_a[1:])]
+    send_a, ring_a = sum_second(sc, own_a, more_a, [send_d])
+    got_a = flip_z(send_a, 1)
     later_d, own_d = sum_first(sc, keep_d, got_d, [ring_a])
     more_d = flip(later_d, BACK, SIDE)
-    piece_b = over_groups(sum_ring(sc, ring_b, parts_b, [later_d]))
+    piece_b = over_groups(sum_two(sc, ring_b, got_b, [later_d]))
     all_b = spread(piece_b)
-    piece_d = over_groups(sum_two(sc, own_d, more_d, [piece_b]))
+    send_a, ring_a = sum_third(sc, ring_a, got_a, [piece_b])
+    got_a = flip_z(send_a, 2)
+    piece_d = over_groups(sum_two(sc, own_d, more_d, [send_a]))
+    grad_gate, grad_up = lay(sc, all_b, across(all_b), (gate_weight.shape[1],) * 2, [piece_d])
     all_d = spread(piece_d)
-    piece_a = over_groups(sum_ring(sc, ring_a, parts_a, [piece_d]))
+    piece_a = over_groups(sum_two(sc, ring_a, got_a, [grad_gate]))
     all_a = spread(piece_a)
-    grad_gate, grad_up = lay(sc, all_b, across(all_b), (gate_weight.shape[1],) * 2, [piece_a])
-    grad_down_ = lay_down(sc, all_d, across(all_d), [grad_gate])
+    grad_down_ = lay_down(sc, all_d, across(all_d), [piece_a])
     grad_query, grad_key, grad_value, grad_out, dgains = lay(sc, all_a, across(all_a), (width, KVW, KVW, width), [grad_down_])
+    grad_tokens, output = grad_tokens.astype(f32).T, output.T
     return (output[None], grad_tokens[None], dgains[0], grad_query, grad_key, grad_value, grad_out, dgains[1], grad_gate, grad_up, grad_down_.T)
 
 

time: 574 us -> 509 us (0.89)
  starting transfers between devices: 140 us -> 81.9 us
  waiting for transfers between devices: 196 us -> 189 us
    ppermute x21 -> x15, starting transfers between devices: 84 us -> 18.8 us  [flip_z(): return lax.ppermute(value, ('dp', 'fsdp'), pairs)]
    ppermute x21 -> x15, waiting for transfers between devices: 113 us -> 70.7 us  [flip_z(): return lax.ppermute(value, ('dp', 'fsdp'), pairs)]
    ppermute x70 -> x63, waiting for transfers between devices: 57.6 us -> 92 us  [flip(): lax.ppermute(value, 'dp', [(i, i ^ bits[i & 1]) for i in range(count)])]
    ppermute x70 -> x63, starting transfers between devices: 39.1 us -> 45.6 us  [flip(): lax.ppermute(value, 'dp', [(i, i ^ bits[i & 1]) for i in range(count)])]
    ppermute x2, waiting for transfers between devices: 19.8 us -> 26.1 us  [unwindow(): lax.ppermute(far, 'fsdp', [(z + 1, z) for z in range(0, depth, 2)])]
    ppermute x4, starting transfers between devices: 3.89 us -> 10 us  [home_to_work(): return lax.ppermute(value, ('dp', 'fsdp'), pairs)]
    unnamed x201 -> x227, local copies, waits for them, and re-layouts: 31.5 us -> 34.5 us
    pallas_call x11 -> x14, Pallas kernels: 15.2 us -> 14.6 us  [small(): pl.pallas_call(kernel, out_shape=tuple(outs), in_specs=[SCALARS] + [WHOLE...]
  transfers between devices with their start and end apart: 99 -> 86, of which waited for: 36 -> 37; matrix products, arithmetic and copies ran while one was open for 1% -> 1% of each run, Pallas kernels for 21% -> 26%
where the time goes in v6:
time: 509 us; the launch traced here: 503 us
  waiting for transfers between devices  189 us (37%)
  Pallas kernels  187 us (37%)
  starting transfers between devices  81.9 us (16%)
  local copies, waits for them, and re-layouts  37.1 us (7%)
  other arithmetic  5.97 us (1%)
    ppermute x63, waiting for transfers between devices, flip(): lax.ppermute(value, 'dp', [(i, i ^ bits[i & 1]) for i in range(count)])  92 us
    ppermute x15, waiting for transfers between devices, flip_z(): return lax.ppermute(value, ('dp', 'fsdp'), pairs)  70.7 us
    pallas_call x3, Pallas kernels, back(): pl.pallas_call(functools.partial(back_kernel, start, end, len(after)), ou...  50.3 us
    ppermute x63, starting transfers between devices, flip(): lax.ppermute(value, 'dp', [(i, i ^ bits[i & 1]) for i in range(count)])  45.6 us
    pallas_call x2, Pallas kernels, post(): pl.pallas_call(functools.partial(post_kernel, last), out_shape=tuple(outs...  38.1 us
    unnamed x227, local copies, waits for them, and re-layouts  34.5 us
    pallas_call x2, Pallas kernels, attend_back(): pl.pallas_call(attend_back_kernel, out_shape=(shape((3, n, PIECE), bf16),...  26.1 us
    ppermute x2, waiting for transfers between devices, unwindow(): lax.ppermute(far, 'fsdp', [(z + 1, z) for z in range(0, depth, 2)])  26.1 us
  transfers between devices with their start and end apart: 86, of which 37 were waited for; matrix products, arithmetic and copies ran while one was open for 1% of the time, Pallas kernels for 26%

profile of v6, /device:TPU:0, one launch (start us, length us, event | category | flops | bytes accessed | tf_op | source)
XLA Modules:
  0.0 503.3 jit_solution(13661044066378899823)
XLA Ops:
  6.7 4.1 collective-permute-start.2
  12.4 7.2 %collective-permute-done.2.rest_2_ = bf16[240,384]{1,0:T(8,128)(2,1)S(1)} collective-permute-done((bf16[240,384]{1,0:T(8,128)(2,1)S(1)}, bf16[240,384]{1,0:T(8,128)(2,1)S(1)}, u32[]{:S(2)}, u32[]{:S(2)}) %collective-permute-start.2) | collective-permute-done | bytes 184352 | tf_op jit(solution)/shard_map/ppermute | solution.py:873
  20.2 5.2 %collective-permute-done.3.rest_3_ = bf16[240,384]{1,0:T(8,128)(2,1)S(1)} collective-permute-done((bf16[240,384]{1,0:T(8,128)(2,1)S(1)}, bf16[240,384]{1,0:T(8,128)(2,1)S(1)}, u32[]{:S(2)}, u32[]{:S(2)}) %collective-permute-start.3) | collective-permute-done | bytes 184352 | tf_op jit(solution)/shard_map/ppermute | solution.py:873
  29.8 16.8 %collective-permute-done.4.rest_1_ = bf16[960,384]{1,0:T(8,128)(2,1)} collective-permute-done((bf16[960,384]{1,0:T(8,128)(2,1)S(1)}, bf16[960,384]{1,0:T(8,128)(2,1)}, u32[]{:S(2)}, u32[]{:S(2)}) %collective-permute-start.4) | collective-permute-done | bytes 737312 | tf_op jit(solution)/shard_map/ppermute | solution.py:867
  47.3 3.1 collective-permute-start.12
  51.9 10.0 %collective-permute-done.12.rest_2_ = bf16[240,640]{1,0:T(8,128)(2,1)S(1)} collective-permute-done((bf16[240,640]{1,0:T(8,128)(2,1)S(1)}, bf16[240,640]{1,0:T(8,128)(2,1)S(1)}, u32[]{:S(2)}, u32[]{:S(2)}) %collective-permute-start.12) | collective-permute-done | bytes 307232 | tf_op jit(solution)/shard_map/ppermute | solution.py:873
  63.0 5.3 %collective-permute-start = (bf16[976,256]{1,0:T(8,128)(2,1)}, bf16[976,256]{1,0:T(8,128)(2,1)}, u32[]{:S(2)}, u32[]{:S(2)}) collective-permute-start(bf16[976,256]{1,0:T(8,128)(2,1)} %pad_maximum_fusion), channel_id=1, source_target_pairs={{0,0},{1,4},{2,1},{3,5},{4,2},{5,6},{6,3},{7,7},{8,8},{9,12},{10,9... | collective-permute-start | bytes 1499144 | tf_op jit(solution)/shard_map/ppermute | solution.py:884
  68.3 2.1 collective-permute-done.13.rest_3_
  72.0 1.7 copy-done.56
  74.5 6.2 %collective-permute-start.24 = (bf16[480,640]{1,0:T(8,128)(2,1)S(1)}, bf16[480,640]{1,0:T(8,128)(2,1)}, u32[]{:S(2)}, u32[]{:S(2)}) collective-permute-start(bf16[480,640]{1,0:T(8,128)(2,1)S(1)} %pick_down.1.rest_0_), channel_id=1, source_target_pairs={{0,2},{1,3},{2,0},{3,1},{4,6},{5,7},{6,4},{7,5},{8,10},{9,11},{10,... | collective-permute-start | bytes 1843208 | tf_op jit(solution)/shard_map/ppermute | solution.py:873
  82.7 6.8 %pre.1 = (bf16[256,960]{1,0:T(8,128)(2,1)}, bf16[256,960]{1,0:T(8,128)(2,1)}, bf16[960,256]{1,0:T(8,128)(2,1)}, bf16[656,256]{1,0:T(8,128)(2,1)}) custom-call(s32[3]{0:T(128)} %copy-done.64, bf16[976,256]{1,0:T(8,128)(2,1)} %collective-permute-done.ht_ref, f32[1,960]{1,0:T(1,128)} %get-tuple-element.209.gain_ref.gain_a.rest_24_.rest_14_, ...), custom_call_target="tpu_custom_call" | custom-call | flops 1024 | bytes 1024 | tf_op jit(solution)/shard_map/pre/pallas_call | solution.py:118
  89.5 3.2 collective-permute-start.14
  92.8 15.7 %collective-permute-done.24.rest_2_ = bf16[480,640]{1,0:T(8,128)(2,1)} collective-permute-done((bf16[480,640]{1,0:T(8,128)(2,1)S(1)}, bf16[480,640]{1,0:T(8,128)(2,1)}, u32[]{:S(2)}, u32[]{:S(2)}) %collective-permute-start.24) | collective-permute-done | bytes 614432 | tf_op jit(solution)/shard_map/ppermute | solution.py:873
  113.9 10.1 %attend.2 = (bf16[960,256]{1,0:T(8,128)(2,1)S(1)}, f32[15,256]{1,0:T(8,128)S(1)}) custom-call(bf16[960,256]{1,0:T(8,128)(2,1)S(1)} %copy-done.48, bf16[656,256]{1,0:T(8,128)(2,1)S(1)} %collective-permute-done.14.kv0, bf16[656,256]{1,0:T(8,128)(2,1)S(1)} %collective-permute-done.15.kv1, bf16[656,256]{1,0:T(8,128)(2,1)S(1)} %copy-done.7), custom_call_target="tpu_custom_call" | custom-call | flops 1024 | bytes 1024 | tf_op jit(solution)/shard_map/attend/pallas_call | solution.py:171
  124.6 9.6 %collective-permute-done.25.rest_3_ = bf16[480,640]{1,0:T(8,128)(2,1)} collective-permute-done((bf16[480,640]{1,0:T(8,128)(2,1)}, bf16[480,640]{1,0:T(8,128)(2,1)}, u32[]{:S(2)}, u32[]{:S(2)}) %collective-permute-start.25) | collective-permute-done | bytes 614432 | tf_op jit(solution)/shard_map/ppermute | solution.py:873
  134.2 2.2 stack.33.rest_16_
  137.6 2.3 collective-permute-done.18.rest_11_
  139.8 4.9 collective-permute-done.19.rest_12_
  144.7 1.8 collective-permute-done.21.rest_14_
  146.5 1.7 collective-permute-done.22.rest_15_
  150.1 20.3 %post.2 = (bf16[256,960]{1,0:T(8,128)(2,1)}, f32[256,960]{1,0:T(8,128)}, bf16[256,960]{1,0:T(8,128)(2,1)}, bf16[256,2560]{1,0:T(8,128)(2,1)}, bf16[256,2560]{1,0...) custom-call(s32[3]{0:T(128)} %copy-done.64, ...), custom_call_target="tpu_custom_call" | custom-call | flops 1024 | bytes 1024 | tf_op jit(solution)/shard_map/post/pallas_call | solution.py:305
  170.4 1.6 collective-permute-start.27
  172.0 1.9 collective-permute-start.33
  173.9 8.9 %collective-permute-start.29 = (bf16[256,960]{1,0:T(8,128)(2,1)S(1)}, bf16[256,960]{1,0:T(8,128)(2,1)S(1)}, u32[]{:S(2)}, u32[]{:S(2)}) collective-permute-start(bf16[256,960]{1,0:T(8,128)(2,1)S(1)} %copy-done.71), channel_id=1, source_target_pairs={{0,4},{4,0},{8,12},{12,8},{16,20},{20,16},{24,28},{28,24},{1,5},{5... | collective-permute-start | bytes 1474568 | tf_op jit(solution)/shard_map/ppermute | solution.py:867
  187.9 10.1 %attend.3 = (bf16[960,256]{1,0:T(8,128)(2,1)S(1)}, f32[15,256]{1,0:T(8,128)S(1)}) custom-call(bf16[960,256]{1,0:T(8,128)(2,1)S(1)} %copy-done.50, bf16[656,256]{1,0:T(8,128)(2,1)S(1)} %collective-permute-done.27.kv0, bf16[656,256]{1,0:T(8,128)(2,1)S(1)} %collective-permute-done.28.kv1, bf16[656,256]{1,0:T(8,128)(2,1)S(1)} %copy-done.5, ...), custom_call_target="tpu_custom_call" | custom-call | flops 1024 | bytes 1024 | tf_op jit(solution)/shard_map/attend/pallas_call | solution.py:171
  198.8 17.8 %post.3 = (bf16[256,960]{1,0:T(8,128)(2,1)}, f32[256,960]{1,0:T(8,128)}, bf16[256,960]{1,0:T(8,128)(2,1)}, bf16[256,2560]{1,0:T(8,128)(2,1)}, bf16[256,2560]{1,0...) custom-call(s32[3]{0:T(128)} %copy-done.64, bf16[960,256]{1,0:T(8,128)(2,1)} %copy-done.80, ...), custom_call_target="tpu_custom_call" | custom-call | flops 1024 | bytes 1024 | tf_op jit(solution)/shard_map/post/pallas_call | solution.py:305
  216.6 2.1 collective-permute-start.32
  220.1 21.6 %back_start.1 = (bf16[256,960]{1,0:T(8,128)(2,1)}, bf16[256,2560]{1,0:T(8,128)(2,1)}, bf16[256,2560]{1,0:T(8,128)(2,1)}, bf16[256,1280]{1,0:T(8,128)(2,1)}, bf16...) custom-call(s32[3]{0:T(128)} %copy-done.64, ...), custom_call_target="tpu_custom_call" | custom-call | flops 1024 | bytes 1024 | tf_op jit(solution)/shard_map/back_start/pallas_call | solution.py:461
  244.4 13.4 %attend_back.2 = (bf16[3,256,384]{2,1,0:T(8,128)(2,1)S(1)}, bf16[3,256,384]{2,1,0:T(8,128)(2,1)}, f32[640,256]{1,0:T(8,128)S(1)}, bf16[640,256]{1,0:T(8,128)(2,1)}, f32[640,256]{1,0:T(8,128)S(1)}) custom-call(s32[3]{0:T(128)S(1)} %copy-done.66, bf16[3,256,384]{2,1,0:T(8,128)(2,1)S(1)} %copy-done.19, bf16[960,256]{1,0:T(8,128)(2,1)S(1)} %copy-done.50, ...), custom_call_target="tpu_custom_call" | custom-call | flops 1024 | bytes 1024 | tf_op jit(solution)/shard_map/attend_back/pallas_call | solution.py:224
  264.3 15.3 %collective-permute-done.38.rest_22_ = bf16[640,256]{1,0:T(8,128)(2,1)S(1)} collective-permute-done((bf16[640,256]{1,0:T(8,128)(2,1)S(1)}, bf16[640,256]{1,0:T(8,128)(2,1)S(1)}, u32[]{:S(2)}, u32[]{:S(2)}) %collective-permute-start.38) | collective-permute-done | bytes 327712 | tf_op jit(solution)/shard_map/ppermute | solution.py:916
  280.8 22.2 %back_join.1 = (bf16[256,384]{1,0:T(8,128)(2,1)}, bf16[256,384]{1,0:T(8,128)(2,1)}, bf16[256,384]{1,0:T(8,128)(2,1)}, f32[1,960]{1,0:T(1,128)}, bf16[256,960]{1,...) custom-call(s32[3]{0:T(128)} %copy-done.64, ...), custom_call_target="tpu_custom_call" | custom-call | flops 1024 | bytes 1024 | tf_op jit(solution)/shard_map/back_join/pallas_call | solution.py:461
  303.0 3.2 collective-permute-done.45.rest_7_
  311.3 7.2 %grad_ffn.1 = (bf16[2,960,640]{2,1,0:T(8,128)(2,1)S(1)}, bf16[2,960,640]{2,1,0:T(8,128)(2,1)S(1)}) custom-call(s32[3]{0:T(128)S(1)} %copy-done.67, bf16[256,960]{1,0:T(8,128)(2,1)S(1)} %copy-done.77, bf16[256,960]{1,0:T(8,128)(2,1)S(1)} %copy-done.76, bf16[256,960]{1,0:T(8,128)(2,1)S(1)} %copy-done.43, bf16[256,960]{1,0:T(8,128)(2,1)S(1)} %copy-done.45, ...), custom_call_target="tpu_custom_call" | custom-call | flops 1024 | bytes 1024 | tf_op jit(solution)/shard_map/grad_ffn/pallas_call | solution.py:502
  319.5 2.0 collective-permute-done.43.rest_3_
  321.6 4.9 grad_down.1
  326.6 12.6 %attend_back.3 = (bf16[3,256,384]{2,1,0:T(8,128)(2,1)S(1)}, bf16[3,256,384]{2,1,0:T(8,128)(2,1)S(1)}, f32[640,256]{1,0:T(8,128)S(1)}, bf16[640,256]{1,0:T(8,128)(2,1)S(1)}, f32[640,256]{1,0:T(8,128)S(1)}) custom-call(s32[3]{0:T(128)S(1)} %copy-done.67, bf16[3,256,384]{2,1,0:T(8,128)(2,1)S(1)} %copy-done.23, bf16[960,256]{1,0:T(8,128)(2,1)S(1)} %copy-done.49, ...), custom_call_target="tpu_custom_call" | custom-call | flops 1024 | bytes 1024 | tf_op jit(solution)/shard_map/attend_back/pallas_call | solution.py:224
  342.4 6.1 %collective-permute-done.49.got_ref = bf16[2,960,640]{2,1,0:T(8,128)(2,1)S(1)} collective-permute-done((bf16[2,960,640]{2,1,0:T(8,128)(2,1)S(1)}, bf16[2,960,640]{2,1,0:T(8,128)(2,1)S(1)}, u32[]{:S(2)}, u32[]{:S(2)}) %collective-permute-start.49) | collective-permute-done | bytes 2457632 | tf_op jit(solution)/shard_map/ppermute | solution.py:867
  348.5 2.0 sum_first.3
  352.2 10.7 %collective-permute-done.48.rest_12_ = bf16[640,256]{1,0:T(8,128)(2,1)S(1)} collective-permute-done((bf16[640,256]{1,0:T(8,128)(2,1)S(1)}, bf16[640,256]{1,0:T(8,128)(2,1)S(1)}, u32[]{:S(2)}, u32[]{:S(2)}) %collective-permute-start.48) | collective-permute-done | bytes 327712 | tf_op jit(solution)/shard_map/ppermute | solution.py:916
  363.7 6.6 %back_end.1 = (bf16[256,384]{1,0:T(8,128)(2,1)}, bf16[256,384]{1,0:T(8,128)(2,1)}, bf16[256,384]{1,0:T(8,128)(2,1)}, f32[1,960]{1,0:T(1,128)}, bf16[960,256]{1,0:T(8,128)(2,1)}) custom-call(s32[3]{0:T(128)} %copy-done.64, bf16[960,384]{1,0:T(8,128)(2,1)} %bitcast.41, bf16[960,384]{1,0:T(8,128)(2,1)} %collective-permute-done.4.rest_1_, ...), custom_call_target="tpu_custom_call" | custom-call | flops 1024 | bytes 1024 | tf_op jit(solution)/shard_map/back_end/pallas_call | solution.py:461
  372.2 1.6 down_pair.1.rest_24_.own_ref
  375.9 6.0 %grad_attention.1 = (bf16[2,960,384]{2,1,0:T(8,128)(2,1)S(1)}, bf16[2,960,384]{2,1,0:T(8,128)(2,1)S(1)}) custom-call(s32[3]{0:T(128)S(1)} %copy-done.68, bf16[256,960]{1,0:T(8,128)(2,1)S(1)} %copy-done.74, bf16[256,960]{1,0:T(8,128)(2,1)S(1)} %copy-done.72, bf16[256,960]{1,0:T(8,128)(2,1)S(1)} %copy-done.35, bf16[256,960]{1,0:T(8,128)(2,1)S(1)} %copy-done.39, ...), custom_call_target="tpu_custom_call" | custom-call | flops 1024 | bytes 1024 | tf_op jit(solution)/shard_map/grad_attention/pallas_call | solution.py:580
  381.9 1.6 collective-permute-start.54
  384.9 1.8 sum_second.2
  387.5 13.9 %collective-permute-done.54.got_ref = bf16[2,960,384]{2,1,0:T(8,128)(2,1)S(1)} collective-permute-done((bf16[2,960,384]{2,1,0:T(8,128)(2,1)S(1)}, bf16[2,960,384]{2,1,0:T(8,128)(2,1)S(1)}, u32[]{:S(2)}, u32[]{:S(2)}) %collective-permute-start.54) | collective-permute-done | bytes 1474592 | tf_op jit(solution)/shard_map/ppermute | solution.py:867
  402.2 5.1 %collective-permute-done.58.got_ref = bf16[2,240,640]{2,1,0:T(8,128)(2,1)S(1)} collective-permute-done((bf16[2,240,640]{2,1,0:T(8,128)(2,1)S(1)}, bf16[2,240,640]{2,1,0:T(8,128)(2,1)S(1)}, u32[]{:S(2)}, u32[]{:S(2)}) %collective-permute-start.58) | collective-permute-done | bytes 614432 | tf_op jit(solution)/shard_map/ppermute | solution.py:873
  408.0 12.5 %collective-permute-done.57.got_ref = bf16[960,640]{1,0:T(8,128)(2,1)S(1)} collective-permute-done((bf16[960,640]{1,0:T(8,128)(2,1)S(1)}, bf16[960,640]{1,0:T(8,128)(2,1)S(1)}, u32[]{:S(2)}, u32[]{:S(2)}) %collective-permute-start.57) | collective-permute-done | bytes 1228832 | tf_op jit(solution)/shard_map/ppermute | solution.py:873
  421.3 6.7 %collective-permute-start.59 = (bf16[480,640]{1,0:T(8,128)(2,1)S(1)}, bf16[480,640]{1,0:T(8,128)(2,1)S(1)}, u32[]{:S(2)}, u32[]{:S(2)}) collective-permute-start(bf16[480,640]{1,0:T(8,128)(2,1)S(1)} %get-tuple-element.180), channel_id=1, source_target_pairs={{0,4},{4,0},{8,12},{12,8},{16,20},{20,16},{24,28},{28,24},{1,5},{5... | collective-permute-start | bytes 1843208 | tf_op jit(solution)/shard_map/ppermute | solution.py:867
  431.7 11.1 %collective-permute-done.56.got_ref = bf16[960,384]{1,0:T(8,128)(2,1)S(1)} collective-permute-done((bf16[960,384]{1,0:T(8,128)(2,1)S(1)}, bf16[960,384]{1,0:T(8,128)(2,1)S(1)}, u32[]{:S(2)}, u32[]{:S(2)}) %collective-permute-start.56) | collective-permute-done | bytes 737312 | tf_op jit(solution)/shard_map/ppermute | solution.py:867
  445.8 1.9 collective-permute-start.66
  449.4 7.6 %collective-permute-done.66.rest_3_ = bf16[240,640]{1,0:T(8,128)(2,1)S(1)} collective-permute-done((bf16[240,640]{1,0:T(8,128)(2,1)S(1)}, bf16[240,640]{1,0:T(8,128)(2,1)S(1)}, u32[]{:S(2)}, u32[]{:S(2)}) %collective-permute-start.66) | collective-permute-done | bytes 307232 | tf_op jit(solution)/shard_map/ppermute | solution.py:867
  456.9 5.6 %collective-permute-done.65.rest_2_ = bf16[240,640]{1,0:T(8,128)(2,1)S(1)} collective-permute-done((bf16[240,640]{1,0:T(8,128)(2,1)S(1)}, bf16[240,640]{1,0:T(8,128)(2,1)S(1)}, u32[]{:S(2)}, u32[]{:S(2)}) %collective-permute-start.65) | collective-permute-done | bytes 307232 | tf_op jit(solution)/shard_map/ppermute | solution.py:867
  463.1 1.7 collective-permute-start.71
  465.3 2.9 collective-permute-done.71.got_ref
  469.0 1.9 collective-permute-start.81
  472.5 3.1 lay.2
  475.7 2.4 collective-permute-done.63.got_ref
  478.0 1.7 copy-done.14
  480.3 2.2 collective-permute-start.74
  485.8 3.0 collective-permute-done.74.rest_3_
  488.8 3.0 collective-permute-done.73.rest_2_
  493.3 2.3 lay_down.1.rest_8_
  495.6 1.7 copy-done.4
  497.3 2.4 lay.3
  (388 shorter events, 86.3 us)
Async XLA Ops:
  6.7 12.8 %collective-permute-start.2 = (bf16[240,384]{1,0:T(8,128)(2,1)S(1)}, bf16[240,384]{1,0:T(8,128)(2,1)S(1)}, u32[]{:S(2)}, u32[]{:S(2)}) collective-permute-start(bf16[240,384]{1,0:T(8,128)(2,1)S(1)} %pick_first.1.rest_0_), channel_id=1, source_target_pairs={{0,2},{1,3},{2,0},{3,1},{4,6},{5,7},{6,4},{7,5},{8,10},{9,11},{10,... | collective-permute-start | bytes 552968 | tf_op jit(solution)/shard_map/ppermute | solution.py:873
  10.8 9.4 %collective-permute-start.1 = (bf16[240,384]{1,0:T(8,128)(2,1)S(1)}, bf16[240,384]{1,0:T(8,128)(2,1)S(1)}, u32[]{:S(2)}, u32[]{:S(2)}) collective-permute-start(bf16[240,384]{1,0:T(8,128)(2,1)S(1)} %pick_first.1.rest_0_), channel_id=1, source_target_pairs={{0,1},{1,0},{2,3},{3,2},{4,5},{5,4},{6,7},{7,6},{8,9},{9,8},{10,11... | collective-permute-start | bytes 552968 | tf_op jit(solution)/shard_map/ppermute | solution.py:873
  27.0 19.6 %collective-permute-start.4 = (bf16[960,384]{1,0:T(8,128)(2,1)S(1)}, bf16[960,384]{1,0:T(8,128)(2,1)}, u32[]{:S(2)}, u32[]{:S(2)}) collective-permute-start(bf16[960,384]{1,0:T(8,128)(2,1)S(1)} %bitcast.33), channel_id=1, source_target_pairs={{0,8},{4,20},{8,0},{12,28},{16,24},{20,4},{24,16},{28,12},{1,9},{5... | collective-permute-start | bytes 2211848 | tf_op jit(solution)/shard_map/ppermute | solution.py:867
  28.3 42.2 %collective-permute-start.5 = (bf16[960,384]{1,0:T(8,128)(2,1)S(1)}, bf16[960,384]{1,0:T(8,128)(2,1)}, u32[]{:S(2)}, u32[]{:S(2)}) collective-permute-start(bf16[960,384]{1,0:T(8,128)(2,1)S(1)} %bitcast.34), channel_id=1, source_target_pairs={{0,16},{4,12},{8,24},{12,4},{16,0},{20,28},{24,8},{28,20},{1,17},{... | collective-permute-start | bytes 2211848 | tf_op jit(solution)/shard_map/ppermute | solution.py:867
  46.6 24.4 %collective-permute-start.6 = (bf16[960,384]{1,0:T(8,128)(2,1)}, bf16[960,384]{1,0:T(8,128)(2,1)}, u32[]{:S(2)}, u32[]{:S(2)}) collective-permute-start(bf16[960,384]{1,0:T(8,128)(2,1)} %collective-permute-done.4.rest_1_), channel_id=1, source_target_pairs={{0,16},{4,12},{8,24},{12,4},{16,0},{20,28},{24,8},{28,20},{1,17},{... | collective-permute-start | bytes 2211848 | tf_op jit(solution)/shard_map/ppermute | solution.py:867
  47.3 14.6 %collective-permute-start.12 = (bf16[240,640]{1,0:T(8,128)(2,1)S(1)}, bf16[240,640]{1,0:T(8,128)(2,1)S(1)}, u32[]{:S(2)}, u32[]{:S(2)}) collective-permute-start(bf16[240,640]{1,0:T(8,128)(2,1)S(1)} %pick.1.rest_0_), channel_id=1, source_target_pairs={{0,2},{1,3},{2,0},{3,1},{4,6},{5,7},{6,4},{7,5},{8,10},{9,11},{10,... | collective-permute-start | bytes 921608 | tf_op jit(solution)/shard_map/ppermute | solution.py:873
  50.5 12.6 %collective-permute-start.11 = (bf16[240,640]{1,0:T(8,128)(2,1)S(1)}, bf16[240,640]{1,0:T(8,128)(2,1)S(1)}, u32[]{:S(2)}, u32[]{:S(2)}) collective-permute-start(bf16[240,640]{1,0:T(8,128)(2,1)S(1)} %pick.1.rest_0_), channel_id=1, source_target_pairs={{0,1},{1,0},{2,3},{3,2},{4,5},{5,4},{6,7},{7,6},{8,9},{9,8},{10,11... | collective-permute-start | bytes 921608 | tf_op jit(solution)/shard_map/ppermute | solution.py:873
  51.9 22.6 %collective-permute-start.7 = (bf16[960,384]{1,0:T(8,128)(2,1)S(1)}, bf16[960,384]{1,0:T(8,128)(2,1)}, u32[]{:S(2)}, u32[]{:S(2)}) collective-permute-start(bf16[960,384]{1,0:T(8,128)(2,1)S(1)} %bitcast.35), channel_id=1, source_target_pairs={{0,4},{4,0},{8,12},{12,8},{16,20},{20,16},{24,28},{28,24},{1,5},{5... | collective-permute-start | bytes 2211848 | tf_op jit(solution)/shard_map/ppermute | solution.py:867
  61.9 8.5 %collective-permute-start.13 = (bf16[240,640]{1,0:T(8,128)(2,1)S(1)}, bf16[240,640]{1,0:T(8,128)(2,1)S(1)}, u32[]{:S(2)}, u32[]{:S(2)}) collective-permute-start(bf16[240,640]{1,0:T(8,128)(2,1)S(1)} %collective-permute-done.12.rest_2_), channel_id=1, source_target_pairs={{0,1},{1,0},{2,3},{3,2},{4,5},{5,4},{6,7},{7,6},{8,9},{9,8},{10,11... | collective-permute-start | bytes 921608 | tf_op jit(solution)/shard_map/ppermute | solution.py:873
  63.0 11.4 %collective-permute-start = (bf16[976,256]{1,0:T(8,128)(2,1)}, bf16[976,256]{1,0:T(8,128)(2,1)}, u32[]{:S(2)}, u32[]{:S(2)}) collective-permute-start(bf16[976,256]{1,0:T(8,128)(2,1)} %pad_maximum_fusion), channel_id=1, source_target_pairs={{0,0},{1,4},{2,1},{3,5},{4,2},{5,6},{6,3},{7,7},{8,8},{9,12},{10,9... | collective-permute-start | bytes 1499144 | tf_op jit(solution)/shard_map/ppermute | solution.py:884
  70.4 12.3 %collective-permute-start.8 = (bf16[960,384]{1,0:T(8,128)(2,1)}, bf16[960,384]{1,0:T(8,128)(2,1)}, u32[]{:S(2)}, u32[]{:S(2)}) collective-permute-start(bf16[960,384]{1,0:T(8,128)(2,1)} %collective-permute-done.4.rest_1_), channel_id=1, source_target_pairs={{0,4},{4,0},{8,12},{12,8},{16,20},{20,16},{24,28},{28,24},{1,5},{5... | collective-permute-start | bytes 2211848 | tf_op jit(solution)/shard_map/ppermute | solution.py:867
  70.5 12.2 %collective-permute-start.9 = (bf16[960,384]{1,0:T(8,128)(2,1)}, bf16[960,384]{1,0:T(8,128)(2,1)}, u32[]{:S(2)}, u32[]{:S(2)}) collective-permute-start(bf16[960,384]{1,0:T(8,128)(2,1)} %collective-permute-done.5.rest_2_), channel_id=1, source_target_pairs={{0,4},{4,0},{8,12},{12,8},{16,20},{20,16},{24,28},{28,24},{1,5},{5... | collective-permute-start | bytes 2211848 | tf_op jit(solution)/shard_map/ppermute | solution.py:867
  71.0 11.7 %collective-permute-start.10 = (bf16[960,384]{1,0:T(8,128)(2,1)}, bf16[960,384]{1,0:T(8,128)(2,1)}, u32[]{:S(2)}, u32[]{:S(2)}) collective-permute-start(bf16[960,384]{1,0:T(8,128)(2,1)} %collective-permute-done.6.rest_3_), channel_id=1, source_target_pairs={{0,4},{4,0},{8,12},{12,8},{16,20},{20,16},{24,28},{28,24},{1,5},{5... | collective-permute-start | bytes 2211848 | tf_op jit(solution)/shard_map/ppermute | solution.py:867
  74.4 36.8 %collective-permute-start.16 = (bf16[960,640]{1,0:T(8,128)(2,1)S(1)}, bf16[960,640]{1,0:T(8,128)(2,1)}, u32[]{:S(2)}, u32[]{:S(2)}) collective-permute-start(bf16[960,640]{1,0:T(8,128)(2,1)S(1)} %bitcast.25), channel_id=1, source_target_pairs={{0,8},{4,20},{8,0},{12,28},{16,24},{20,4},{24,16},{28,12},{1,9},{5... | collective-permute-start | bytes 3686408 | tf_op jit(solution)/shard_map/ppermute | solution.py:867
  74.5 34.0 %collective-permute-start.24 = (bf16[480,640]{1,0:T(8,128)(2,1)S(1)}, bf16[480,640]{1,0:T(8,128)(2,1)}, u32[]{:S(2)}, u32[]{:S(2)}) collective-permute-start(bf16[480,640]{1,0:T(8,128)(2,1)S(1)} %pick_down.1.rest_0_), channel_id=1, source_target_pairs={{0,2},{1,3},{2,0},{3,1},{4,6},{5,7},{6,4},{7,5},{8,10},{9,11},{10,... | collective-permute-start | bytes 1843208 | tf_op jit(solution)/shard_map/ppermute | solution.py:873
  89.5 19.0 %collective-permute-start.14 = (bf16[656,256]{1,0:T(8,128)(2,1)}, bf16[656,256]{1,0:T(8,128)(2,1)S(1)}, u32[]{:S(2)}, u32[]{:S(2)}) collective-permute-start(bf16[656,256]{1,0:T(8,128)(2,1)} %get-tuple-element.105.kv2.rest_18_), channel_id=1, source_target_pairs={{0,1},{2,3},{4,5},{6,7},{8,9},{10,11},{12,13},{14,15},{16,17},{18,... | collective-permute-start | bytes 1007624 | tf_op jit(solution)/shard_map/ppermute | solution.py:906
  92.7 31.9 %collective-permute-start.23 = (bf16[480,640]{1,0:T(8,128)(2,1)S(1)}, bf16[480,640]{1,0:T(8,128)(2,1)}, u32[]{:S(2)}, u32[]{:S(2)}) collective-permute-start(bf16[480,640]{1,0:T(8,128)(2,1)S(1)} %pick_down.1.rest_0_), channel_id=1, source_target_pairs={{0,1},{1,0},{2,3},{3,2},{4,5},{5,4},{6,7},{7,6},{8,9},{9,8},{10,11... | collective-permute-start | bytes 1843208 | tf_op jit(solution)/shard_map/ppermute | solution.py:873
  108.5 25.7 %collective-permute-start.25 = (bf16[480,640]{1,0:T(8,128)(2,1)}, bf16[480,640]{1,0:T(8,128)(2,1)}, u32[]{:S(2)}, u32[]{:S(2)}) collective-permute-start(bf16[480,640]{1,0:T(8,128)(2,1)} %collective-permute-done.24.rest_2_), channel_id=1, source_target_pairs={{0,1},{1,0},{2,3},{3,2},{4,5},{5,4},{6,7},{7,6},{8,9},{9,8},{10,11... | collective-permute-start | bytes 1843208 | tf_op jit(solution)/shard_map/ppermute | solution.py:873
  109.7 27.5 %collective-permute-start.17 = (bf16[960,640]{1,0:T(8,128)(2,1)}, bf16[960,640]{1,0:T(8,128)(2,1)S(1)}, u32[]{:S(2)}, u32[]{:S(2)}) collective-permute-start(bf16[960,640]{1,0:T(8,128)(2,1)} %bitcast.27), channel_id=1, source_target_pairs={{0,16},{4,12},{8,24},{12,4},{16,0},{20,28},{24,8},{28,20},{1,17},{... | collective-permute-start | bytes 3686408 | tf_op jit(solution)/shard_map/ppermute | solution.py:867
  111.2 28.6 %collective-permute-start.18 = (bf16[960,640]{1,0:T(8,128)(2,1)}, bf16[960,640]{1,0:T(8,128)(2,1)S(1)}, u32[]{:S(2)}, u32[]{:S(2)}) collective-permute-start(bf16[960,640]{1,0:T(8,128)(2,1)} %collective-permute-done.16.rest_9_), channel_id=1, source_target_pairs={{0,16},{4,12},{8,24},{12,4},{16,0},{20,28},{24,8},{28,20},{1,17},{... | collective-permute-start | bytes 3686408 | tf_op jit(solution)/shard_map/ppermute | solution.py:867
  136.5 11.8 %collective-permute-start.26 = (bf16[4,480,640]{2,1,0:T(8,128)(2,1)S(1)}, bf16[4,480,640]{2,1,0:T(8,128)(2,1)S(1)}, u32[]{:S(2)}, u32[]{:S(2)}) collective-permute-start(bf16[4,480,640]{2,1,0:T(8,128)(2,1)S(1)} %stack.33.rest_16_), channel_id=1, source_target_pairs={{0,4},{4,0},{8,12},{12,8},{16,20},{20,16},{24,28},{28,24},{1,5},{5... | collective-permute-start | bytes 7372808 | tf_op jit(solution)/shard_map/ppermute | solution.py:867
  136.5 8.2 %collective-permute-start.19 = (bf16[960,640]{1,0:T(8,128)(2,1)S(1)}, bf16[960,640]{1,0:T(8,128)(2,1)S(1)}, u32[]{:S(2)}, u32[]{:S(2)}) collective-permute-start(bf16[960,640]{1,0:T(8,128)(2,1)S(1)} %bitcast.32), channel_id=1, source_target_pairs={{0,4},{4,0},{8,12},{12,8},{16,20},{20,16},{24,28},{28,24},{1,5},{5... | collective-permute-start | bytes 3686408 | tf_op jit(solution)/shard_map/ppermute | solution.py:867
  137.0 9.4 %collective-permute-start.20 = (bf16[960,640]{1,0:T(8,128)(2,1)}, bf16[960,640]{1,0:T(8,128)(2,1)S(1)}, u32[]{:S(2)}, u32[]{:S(2)}) collective-permute-start(bf16[960,640]{1,0:T(8,128)(2,1)} %collective-permute-done.16.rest_9_), channel_id=1, source_target_pairs={{0,4},{4,0},{8,12},{12,8},{16,20},{20,16},{24,28},{28,24},{1,5},{5... | collective-permute-start | bytes 3686408 | tf_op jit(solution)/shard_map/ppermute | solution.py:867
  137.1 9.3 %collective-permute-start.21 = (bf16[960,640]{1,0:T(8,128)(2,1)S(1)}, bf16[960,640]{1,0:T(8,128)(2,1)S(1)}, u32[]{:S(2)}, u32[]{:S(2)}) collective-permute-start(bf16[960,640]{1,0:T(8,128)(2,1)S(1)} %collective-permute-done.17.rest_10_), channel_id=1, source_target_pairs={{0,4},{4,0},{8,12},{12,8},{16,20},{20,16},{24,28},{28,24},{1,5},{5... | collective-permute-start | bytes 3686408 | tf_op jit(solution)/shard_map/ppermute | solution.py:867
  139.8 8.4 %collective-permute-start.22 = (bf16[960,640]{1,0:T(8,128)(2,1)S(1)}, bf16[960,640]{1,0:T(8,128)(2,1)S(1)}, u32[]{:S(2)}, u32[]{:S(2)}) collective-permute-start(bf16[960,640]{1,0:T(8,128)(2,1)S(1)} %collective-permute-done.18.rest_11_), channel_id=1, source_target_pairs={{0,4},{4,0},{8,12},{12,8},{16,20},{20,16},{24,28},{28,24},{1,5},{5... | collective-permute-start | bytes 3686408 | tf_op jit(solution)/shard_map/ppermute | solution.py:867
  170.4 13.0 %collective-permute-start.27 = (bf16[656,256]{1,0:T(8,128)(2,1)}, bf16[656,256]{1,0:T(8,128)(2,1)S(1)}, u32[]{:S(2)}, u32[]{:S(2)}) collective-permute-start(bf16[656,256]{1,0:T(8,128)(2,1)} %get-tuple-element.109.kv2.rest_18_), channel_id=1, source_target_pairs={{0,1},{2,3},{4,5},{6,7},{8,9},{10,11},{12,13},{14,15},{16,17},{18,... | collective-permute-start | bytes 1007624 | tf_op jit(solution)/shard_map/ppermute | solution.py:906
  172.0 47.3 %collective-permute-start.33 = (bf16[960,256]{1,0:T(8,128)(2,1)}, bf16[960,256]{1,0:T(8,128)(2,1)S(1)}, u32[]{:S(2)}, u32[]{:S(2)}) collective-permute-start(bf16[960,256]{1,0:T(8,128)(2,1)} %bitcast.13), channel_id=1, source_target_pairs={{0,0},{1,4},{2,1},{3,5},{4,2},{5,6},{6,3},{7,7},{8,8},{9,12},{10,9... | collective-permute-start | bytes 1474568 | tf_op jit(solution)/shard_map/ppermute | solution.py:884
  173.9 10.6 %collective-permute-start.29 = (bf16[256,960]{1,0:T(8,128)(2,1)S(1)}, bf16[256,960]{1,0:T(8,128)(2,1)S(1)}, u32[]{:S(2)}, u32[]{:S(2)}) collective-permute-start(bf16[256,960]{1,0:T(8,128)(2,1)S(1)} %copy-done.71), channel_id=1, source_target_pairs={{0,4},{4,0},{8,12},{12,8},{16,20},{20,16},{24,28},{28,24},{1,5},{5... | collective-permute-start | bytes 1474568 | tf_op jit(solution)/shard_map/ppermute | solution.py:867
  184.5 57.3 %collective-permute-start.34 = (bf16[256,960]{1,0:T(8,128)(2,1)}, bf16[256,960]{1,0:T(8,128)(2,1)S(1)}, u32[]{:S(2)}, u32[]{:S(2)}) collective-permute-start(bf16[256,960]{1,0:T(8,128)(2,1)} %get-tuple-element.124.rest_0_), channel_id=1, source_target_pairs={{0,4},{4,0},{8,12},{12,8},{16,20},{20,16},{24,28},{28,24},{1,5},{5... | collective-permute-start | bytes 1474568 | tf_op jit(solution)/shard_map/ppermute | solution.py:867
  216.6 25.2 %collective-permute-start.32 = (bf16[960,256]{1,0:T(8,128)(2,1)}, bf16[960,256]{1,0:T(8,128)(2,1)S(1)}, u32[]{:S(2)}, u32[]{:S(2)}) collective-permute-start(bf16[960,256]{1,0:T(8,128)(2,1)} %get-tuple-element.115), channel_id=1, source_target_pairs={{0,0},{4,1},{1,2},{5,3},{2,4},{6,5},{3,6},{7,7},{8,8},{12,9},{9,10... | collective-permute-start | bytes 1474568 | tf_op jit(solution)/shard_map/ppermute | solution.py:884
  218.7 23.1 %collective-permute-start.35 = (bf16[256,960]{1,0:T(8,128)(2,1)}, bf16[256,960]{1,0:T(8,128)(2,1)S(1)}, u32[]{:S(2)}, u32[]{:S(2)}) collective-permute-start(bf16[256,960]{1,0:T(8,128)(2,1)} %get-tuple-element.125.rest_0_), channel_id=1, source_target_pairs={{0,4},{4,0},{8,12},{12,8},{16,20},{20,16},{24,28},{28,24},{1,5},{5... | collective-permute-start | bytes 1474568 | tf_op jit(solution)/shard_map/ppermute | solution.py:867
  218.8 23.1 %collective-permute-start.36 = (bf16[256,960]{1,0:T(8,128)(2,1)}, bf16[256,960]{1,0:T(8,128)(2,1)S(1)}, u32[]{:S(2)}, u32[]{:S(2)}) collective-permute-start(bf16[256,960]{1,0:T(8,128)(2,1)} %get-tuple-element.126.rest_4_), channel_id=1, source_target_pairs={{0,4},{4,0},{8,12},{12,8},{16,20},{20,16},{24,28},{28,24},{1,5},{5... | collective-permute-start | bytes 1474568 | tf_op jit(solution)/shard_map/ppermute | solution.py:867
  241.7 37.9 %collective-permute-start.41 = (bf16[256,2560]{1,0:T(8,128)(2,1)}, bf16[256,2560]{1,0:T(8,128)(2,1)S(1)}, u32[]{:S(2)}, u32[]{:S(2)}) collective-permute-start(bf16[256,2560]{1,0:T(8,128)(2,1)} %get-tuple-element.137), channel_id=1, source_target_pairs={{0,4},{4,0},{8,12},{12,8},{16,20},{20,16},{24,28},{28,24},{1,5},{5... | collective-permute-start | bytes 3932168 | tf_op jit(solution)/shard_map/ppermute | solution.py:867
  262.7 16.9 %collective-permute-start.38 = (bf16[640,256]{1,0:T(8,128)(2,1)S(1)}, bf16[640,256]{1,0:T(8,128)(2,1)S(1)}, u32[]{:S(2)}, u32[]{:S(2)}) collective-permute-start(bf16[640,256]{1,0:T(8,128)(2,1)S(1)} %fusion), channel_id=1, source_target_pairs={{1,0},{3,2},{5,4},{7,6},{9,8},{11,10},{13,12},{15,14},{17,16},{19,... | collective-permute-start | bytes 983048 | tf_op jit(solution)/shard_map/ppermute | solution.py:916
  318.5 30.0 %collective-permute-start.49 = (bf16[2,960,640]{2,1,0:T(8,128)(2,1)S(1)}, bf16[2,960,640]{2,1,0:T(8,128)(2,1)S(1)}, u32[]{:S(2)}, u32[]{:S(2)}) collective-permute-start(bf16[2,960,640]{2,1,0:T(8,128)(2,1)S(1)} %get-tuple-element.150.rest_8_), channel_id=1, source_target_pairs={{0,8},{4,20},{8,0},{12,28},{16,24},{20,4},{24,16},{28,12},{1,9},{5... | collective-permute-start | bytes 7372808 | tf_op jit(solution)/shard_map/ppermute | solution.py:867
  319.2 7.3 %collective-permute-start.46 = (bf16[256,384]{1,0:T(8,128)(2,1)S(1)}, bf16[256,384]{1,0:T(8,128)(2,1)S(1)}, u32[]{:S(2)}, u32[]{:S(2)}) collective-permute-start(bf16[256,384]{1,0:T(8,128)(2,1)S(1)} %copy-done.110), channel_id=1, source_target_pairs={{0,4},{4,0},{8,12},{12,8},{16,20},{20,16},{24,28},{28,24},{1,5},{5... | collective-permute-start | bytes 589832 | tf_op jit(solution)/shard_map/ppermute | solution.py:867
  326.5 44.5 %collective-permute-start.53 = (bf16[960,640]{1,0:T(8,128)(2,1)}, bf16[960,640]{1,0:T(8,128)(2,1)}, u32[]{:S(2)}, u32[]{:S(2)}) collective-permute-start(bf16[960,640]{1,0:T(8,128)(2,1)} %get-tuple-element.170), channel_id=1, source_target_pairs={{0,1},{1,0},{2,3},{3,2},{4,5},{5,4},{6,7},{7,6},{8,9},{9,8},{10,11... | collective-permute-start | bytes 3686408 | tf_op jit(solution)/shard_map/ppermute | solution.py:873
  341.1 21.9 %collective-permute-start.48 = (bf16[640,256]{1,0:T(8,128)(2,1)S(1)}, bf16[640,256]{1,0:T(8,128)(2,1)S(1)}, u32[]{:S(2)}, u32[]{:S(2)}) collective-permute-start(bf16[640,256]{1,0:T(8,128)(2,1)S(1)} %fusion.1), channel_id=1, source_target_pairs={{1,0},{3,2},{5,4},{7,6},{9,8},{11,10},{13,12},{15,14},{17,16},{19,... | collective-permute-start | bytes 983048 | tf_op jit(solution)/shard_map/ppermute | solution.py:916
  352.0 32.9 %collective-permute-start.55 = (bf16[960,640]{1,0:T(8,128)(2,1)}, bf16[960,640]{1,0:T(8,128)(2,1)}, u32[]{:S(2)}, u32[]{:S(2)}) collective-permute-start(bf16[960,640]{1,0:T(8,128)(2,1)} %get-tuple-element.159.rest_17_), channel_id=1, source_target_pairs={{0,16},{4,12},{8,24},{12,4},{16,0},{20,28},{24,8},{28,20},{1,17},{... | collective-permute-start | bytes 3686408 | tf_op jit(solution)/shard_map/ppermute | solution.py:867
  381.9 19.4 %collective-permute-start.54 = (bf16[2,960,384]{2,1,0:T(8,128)(2,1)S(1)}, bf16[2,960,384]{2,1,0:T(8,128)(2,1)S(1)}, u32[]{:S(2)}, u32[]{:S(2)}) collective-permute-start(bf16[2,960,384]{2,1,0:T(8,128)(2,1)S(1)} %get-tuple-element.172.rest_0_), channel_id=1, source_target_pairs={{0,8},{4,20},{8,0},{12,28},{16,24},{20,4},{24,16},{28,12},{1,9},{5... | collective-permute-start | bytes 4423688 | tf_op jit(solution)/shard_map/ppermute | solution.py:867
  383.6 36.9 %collective-permute-start.57 = (bf16[960,640]{1,0:T(8,128)(2,1)S(1)}, bf16[960,640]{1,0:T(8,128)(2,1)S(1)}, u32[]{:S(2)}, u32[]{:S(2)}) collective-permute-start(bf16[960,640]{1,0:T(8,128)(2,1)S(1)} %down_pair.1.rest_24_.own_ref), channel_id=1, source_target_pairs={{2,0},{3,1},{4,6},{5,7},{10,8},{11,9},{12,14},{13,15},{18,16},{19,... | collective-permute-start | bytes 3686408 | tf_op jit(solution)/shard_map/ppermute | solution.py:873
  386.7 20.7 %collective-permute-start.58 = (bf16[2,240,640]{2,1,0:T(8,128)(2,1)S(1)}, bf16[2,240,640]{2,1,0:T(8,128)(2,1)S(1)}, u32[]{:S(2)}, u32[]{:S(2)}) collective-permute-start(bf16[2,240,640]{2,1,0:T(8,128)(2,1)S(1)} %get-tuple-element.177), channel_id=1, source_target_pairs={{0,1},{1,0},{2,3},{3,2},{4,5},{5,4},{6,7},{7,6},{8,9},{9,8},{10,11... | collective-permute-start | bytes 1843208 | tf_op jit(solution)/shard_map/ppermute | solution.py:873
  421.3 8.4 %collective-permute-start.59 = (bf16[480,640]{1,0:T(8,128)(2,1)S(1)}, bf16[480,640]{1,0:T(8,128)(2,1)S(1)}, u32[]{:S(2)}, u32[]{:S(2)}) collective-permute-start(bf16[480,640]{1,0:T(8,128)(2,1)S(1)} %get-tuple-element.180), channel_id=1, source_target_pairs={{0,4},{4,0},{8,12},{12,8},{16,20},{20,16},{24,28},{28,24},{1,5},{5... | collective-permute-start | bytes 1843208 | tf_op jit(solution)/shard_map/ppermute | solution.py:867
  428.0 14.8 %collective-permute-start.56 = (bf16[960,384]{1,0:T(8,128)(2,1)S(1)}, bf16[960,384]{1,0:T(8,128)(2,1)S(1)}, u32[]{:S(2)}, u32[]{:S(2)}) collective-permute-start(bf16[960,384]{1,0:T(8,128)(2,1)S(1)} %get-tuple-element.176.rest_0_), channel_id=1, source_target_pairs={{0,16},{4,12},{8,24},{12,4},{16,0},{20,28},{24,8},{28,20},{1,17},{... | collective-permute-start | bytes 2211848 | tf_op jit(solution)/shard_map/ppermute | solution.py:867
  430.5 13.1 %collective-permute-start.62 = (bf16[2,120,640]{2,1,0:T(8,128)(2,1)S(1)}, bf16[2,120,640]{2,1,0:T(8,128)(2,1)S(1)}, u32[]{:S(2)}, u32[]{:S(2)}) collective-permute-start(bf16[2,120,640]{2,1,0:T(8,128)(2,1)S(1)} %get-tuple-element.181.rest_0_), channel_id=1, source_target_pairs={{0,8},{4,20},{8,0},{12,28},{16,24},{20,4},{24,16},{28,12},{1,9},{5... | collective-permute-start | bytes 921608 | tf_op jit(solution)/shard_map/ppermute | solution.py:867
  431.7 13.5 %collective-permute-start.61 = (bf16[240,640]{1,0:T(8,128)(2,1)S(1)}, bf16[240,640]{1,0:T(8,128)(2,1)S(1)}, u32[]{:S(2)}, u32[]{:S(2)}) collective-permute-start(bf16[240,640]{1,0:T(8,128)(2,1)S(1)} %get-tuple-element.178.rest_0_), channel_id=1, source_target_pairs={{0,2},{1,3},{2,0},{3,1},{4,6},{5,7},{6,4},{7,5},{8,10},{9,11},{10,... | collective-permute-start | bytes 921608 | tf_op jit(solution)/shard_map/ppermute | solution.py:873
  445.8 11.1 %collective-permute-start.66 = (bf16[240,640]{1,0:T(8,128)(2,1)S(1)}, bf16[240,640]{1,0:T(8,128)(2,1)S(1)}, u32[]{:S(2)}, u32[]{:S(2)}) collective-permute-start(bf16[240,640]{1,0:T(8,128)(2,1)S(1)} %sum_two.3.rest_0_), channel_id=1, source_target_pairs={{0,24},{4,28},{8,16},{12,20},{16,8},{20,12},{24,0},{28,4},{1,25},{... | collective-permute-start | bytes 921608 | tf_op jit(solution)/shard_map/ppermute | solution.py:867
  447.7 14.8 %collective-permute-start.65 = (bf16[240,640]{1,0:T(8,128)(2,1)S(1)}, bf16[240,640]{1,0:T(8,128)(2,1)S(1)}, u32[]{:S(2)}, u32[]{:S(2)}) collective-permute-start(bf16[240,640]{1,0:T(8,128)(2,1)S(1)} %sum_two.3.rest_0_), channel_id=1, source_target_pairs={{0,16},{4,12},{8,24},{12,4},{16,0},{20,28},{24,8},{28,20},{1,17},{... | collective-permute-start | bytes 921608 | tf_op jit(solution)/shard_map/ppermute | solution.py:867
  449.0 13.8 %collective-permute-start.64 = (bf16[240,640]{1,0:T(8,128)(2,1)S(1)}, bf16[240,640]{1,0:T(8,128)(2,1)S(1)}, u32[]{:S(2)}, u32[]{:S(2)}) collective-permute-start(bf16[240,640]{1,0:T(8,128)(2,1)S(1)} %sum_two.3.rest_0_), channel_id=1, source_target_pairs={{0,8},{4,20},{8,0},{12,28},{16,24},{20,4},{24,16},{28,12},{1,9},{5... | collective-permute-start | bytes 921608 | tf_op jit(solution)/shard_map/ppermute | solution.py:867
  449.4 13.7 %collective-permute-start.60 = (bf16[2,240,384]{2,1,0:T(8,128)(2,1)S(1)}, bf16[2,240,384]{2,1,0:T(8,128)(2,1)S(1)}, u32[]{:S(2)}, u32[]{:S(2)}) collective-permute-start(bf16[2,240,384]{2,1,0:T(8,128)(2,1)S(1)} %get-tuple-element.183), channel_id=1, source_target_pairs={{0,1},{1,0},{2,3},{3,2},{4,5},{5,4},{6,7},{7,6},{8,9},{9,8},{10,11... | collective-permute-start | bytes 1105928 | tf_op jit(solution)/shard_map/ppermute | solution.py:873
  449.4 19.5 %collective-permute-start.67 = (bf16[240,640]{1,0:T(8,128)(2,1)S(1)}, bf16[240,640]{1,0:T(8,128)(2,1)S(1)}, u32[]{:S(2)}, u32[]{:S(2)}) collective-permute-start(bf16[240,640]{1,0:T(8,128)(2,1)S(1)} %sum_two.3.rest_0_), channel_id=1, source_target_pairs={{0,4},{4,0},{8,12},{12,8},{16,20},{20,16},{24,28},{28,24},{1,5},{5... | collective-permute-start | bytes 921608 | tf_op jit(solution)/shard_map/ppermute | solution.py:867
  456.9 12.0 %collective-permute-start.70 = (bf16[240,640]{1,0:T(8,128)(2,1)S(1)}, bf16[240,640]{1,0:T(8,128)(2,1)S(1)}, u32[]{:S(2)}, u32[]{:S(2)}) collective-permute-start(bf16[240,640]{1,0:T(8,128)(2,1)S(1)} %collective-permute-done.66.rest_3_), channel_id=1, source_target_pairs={{0,4},{4,0},{8,12},{12,8},{16,20},{20,16},{24,28},{28,24},{1,5},{5... | collective-permute-start | bytes 921608 | tf_op jit(solution)/shard_map/ppermute | solution.py:867
  462.5 8.3 %collective-permute-start.69 = (bf16[240,640]{1,0:T(8,128)(2,1)S(1)}, bf16[240,640]{1,0:T(8,128)(2,1)S(1)}, u32[]{:S(2)}, u32[]{:S(2)}) collective-permute-start(bf16[240,640]{1,0:T(8,128)(2,1)S(1)} %collective-permute-done.65.rest_2_), channel_id=1, source_target_pairs={{0,4},{4,0},{8,12},{12,8},{16,20},{20,16},{24,28},{28,24},{1,5},{5... | collective-permute-start | bytes 921608 | tf_op jit(solution)/shard_map/ppermute | solution.py:867
  462.8 9.5 %collective-permute-start.68 = (bf16[240,640]{1,0:T(8,128)(2,1)S(1)}, bf16[240,640]{1,0:T(8,128)(2,1)S(1)}, u32[]{:S(2)}, u32[]{:S(2)}) collective-permute-start(bf16[240,640]{1,0:T(8,128)(2,1)S(1)} %collective-permute-done.64.rest_1_), channel_id=1, source_target_pairs={{0,4},{4,0},{8,12},{12,8},{16,20},{20,16},{24,28},{28,24},{1,5},{5... | collective-permute-start | bytes 921608 | tf_op jit(solution)/shard_map/ppermute | solution.py:867
  468.3 9.7 %collective-permute-start.63 = (bf16[240,384]{1,0:T(8,128)(2,1)S(1)}, bf16[240,384]{1,0:T(8,128)(2,1)S(1)}, u32[]{:S(2)}, u32[]{:S(2)}) collective-permute-start(bf16[240,384]{1,0:T(8,128)(2,1)S(1)} %get-tuple-element.188.rest_0_), channel_id=1, source_target_pairs={{0,2},{1,3},{2,0},{3,1},{4,6},{5,7},{6,4},{7,5},{8,10},{9,11},{10,... | collective-permute-start | bytes 552968 | tf_op jit(solution)/shard_map/ppermute | solution.py:873
  468.9 13.6 %collective-permute-start.82 = (bf16[120,640]{1,0:T(8,128)(2,1)S(1)}, bf16[120,640]{1,0:T(8,128)(2,1)S(1)}, u32[]{:S(2)}, u32[]{:S(2)}) collective-permute-start(bf16[120,640]{1,0:T(8,128)(2,1)S(1)} %sum_two.4.rest_8_.rest_0_), channel_id=1, source_target_pairs={{0,4},{4,0},{8,12},{12,8},{16,20},{20,16},{24,28},{28,24},{1,5},{5... | collective-permute-start | bytes 460808 | tf_op jit(solution)/shard_map/ppermute | solution.py:867
  469.0 14.4 %collective-permute-start.81 = (bf16[120,640]{1,0:T(8,128)(2,1)S(1)}, bf16[120,640]{1,0:T(8,128)(2,1)S(1)}, u32[]{:S(2)}, u32[]{:S(2)}) collective-permute-start(bf16[120,640]{1,0:T(8,128)(2,1)S(1)} %sum_two.4.rest_8_.rest_0_), channel_id=1, source_target_pairs={{0,24},{4,28},{8,16},{12,20},{16,8},{20,12},{24,0},{28,4},{1,25},{... | collective-permute-start | bytes 460808 | tf_op jit(solution)/shard_map/ppermute | solution.py:867
  470.9 13.0 %collective-permute-start.80 = (bf16[120,640]{1,0:T(8,128)(2,1)S(1)}, bf16[120,640]{1,0:T(8,128)(2,1)S(1)}, u32[]{:S(2)}, u32[]{:S(2)}) collective-permute-start(bf16[120,640]{1,0:T(8,128)(2,1)S(1)} %sum_two.4.rest_8_.rest_0_), channel_id=1, source_target_pairs={{0,16},{4,12},{8,24},{12,4},{16,0},{20,28},{24,8},{28,20},{1,17},{... | collective-permute-start | bytes 460808 | tf_op jit(solution)/shard_map/ppermute | solution.py:867
  472.3 11.6 %collective-permute-start.79 = (bf16[120,640]{1,0:T(8,128)(2,1)S(1)}, bf16[120,640]{1,0:T(8,128)(2,1)S(1)}, u32[]{:S(2)}, u32[]{:S(2)}) collective-permute-start(bf16[120,640]{1,0:T(8,128)(2,1)S(1)} %sum_two.4.rest_8_.rest_0_), channel_id=1, source_target_pairs={{0,8},{4,20},{8,0},{12,28},{16,24},{20,4},{24,16},{28,12},{1,9},{5... | collective-permute-start | bytes 460808 | tf_op jit(solution)/shard_map/ppermute | solution.py:867
  480.3 8.5 %collective-permute-start.74 = (bf16[240,384]{1,0:T(8,128)(2,1)S(1)}, bf16[240,384]{1,0:T(8,128)(2,1)S(1)}, u32[]{:S(2)}, u32[]{:S(2)}) collective-permute-start(bf16[240,384]{1,0:T(8,128)(2,1)S(1)} %sum_two.5.rest_8_.rest_0_), channel_id=1, source_target_pairs={{0,24},{4,28},{8,16},{12,20},{16,8},{20,12},{24,0},{28,4},{1,25},{... | collective-permute-start | bytes 552968 | tf_op jit(solution)/shard_map/ppermute | solution.py:867
  482.5 9.3 %collective-permute-start.73 = (bf16[240,384]{1,0:T(8,128)(2,1)S(1)}, bf16[240,384]{1,0:T(8,128)(2,1)S(1)}, u32[]{:S(2)}, u32[]{:S(2)}) collective-permute-start(bf16[240,384]{1,0:T(8,128)(2,1)S(1)} %sum_two.5.rest_8_.rest_0_), channel_id=1, source_target_pairs={{0,16},{4,12},{8,24},{12,4},{16,0},{20,28},{24,8},{28,20},{1,17},{... | collective-permute-start | bytes 552968 | tf_op jit(solution)/shard_map/ppermute | solution.py:867
  483.4 8.5 %collective-permute-start.72 = (bf16[240,384]{1,0:T(8,128)(2,1)S(1)}, bf16[240,384]{1,0:T(8,128)(2,1)S(1)}, u32[]{:S(2)}, u32[]{:S(2)}) collective-permute-start(bf16[240,384]{1,0:T(8,128)(2,1)S(1)} %sum_two.5.rest_8_.rest_0_), channel_id=1, source_target_pairs={{0,8},{4,20},{8,0},{12,28},{16,24},{20,4},{24,16},{28,12},{1,9},{5... | collective-permute-start | bytes 552968 | tf_op jit(solution)/shard_map/ppermute | solution.py:867
  485.2 8.1 %collective-permute-start.83 = (bf16[120,640]{1,0:T(8,128)(2,1)S(1)}, bf16[120,640]{1,0:T(8,128)(2,1)S(1)}, u32[]{:S(2)}, u32[]{:S(2)}) collective-permute-start(bf16[120,640]{1,0:T(8,128)(2,1)S(1)} %collective-permute-done.79.rest_1_), channel_id=1, source_target_pairs={{0,4},{4,0},{8,12},{12,8},{16,20},{20,16},{24,28},{28,24},{1,5},{5... | collective-permute-start | bytes 460808 | tf_op jit(solution)/shard_map/ppermute | solution.py:867
  485.5 10.1 %collective-permute-start.75 = (bf16[240,384]{1,0:T(8,128)(2,1)S(1)}, bf16[240,384]{1,0:T(8,128)(2,1)S(1)}, u32[]{:S(2)}, u32[]{:S(2)}) collective-permute-start(bf16[240,384]{1,0:T(8,128)(2,1)S(1)} %sum_two.5.rest_8_.rest_0_), channel_id=1, source_target_pairs={{0,4},{4,0},{8,12},{12,8},{16,20},{20,16},{24,28},{28,24},{1,5},{5... | collective-permute-start | bytes 552968 | tf_op jit(solution)/shard_map/ppermute | solution.py:867
  (134 other events, 1228.5 us)

commit v7 on v6

--- a/solution.py
+++ b/solution.py
@@ -495,20 +495,20 @@
         out[i % 2] = nn(left[...], right[...]).astype(bf16)
 
 
-def grad_ffn(sc, lefts, rights):
+def grad_ffn(sc, lefts, rights, after):
     n, width = lefts[0].shape
     cols = rights[0].shape[1] // 4
     out = shape((2, width, cols), bf16)
     return pl.pallas_call(
         grad_ffn_kernel,
         out_shape=(out, out),
-        in_specs=[SCALARS] + [WHOLE] * 8,
+        in_specs=[SCALARS] + [WHOLE] * 8 + [LEFT] * len(after),
         out_specs=(WHOLE,) * 2,
         scratch_shapes=[pltpu.VMEM((width, 4 * n), bf16), pltpu.VMEM((4 * n, cols), bf16)],
         cost_estimate=BRIEF,
         compiler_params=pltpu.CompilerParams(vmem_limit_bytes=36 << 20),
         name="grad_ffn",
-    )(sc, *lefts, *rights)
+    )(sc, *lefts, *rights, *after)
 
 
 def grad_down_kernel(sc, *rest):
@@ -856,6 +856,26 @@
     return small(kernel, sc, [*mine, *other], [shape((8 * n, cols), f32)], [pltpu.VMEM((2, 4, n, cols), f32)], after, "lay_down")[0]
 
 
+def hold(value, after):
+    return pl.pallas_call(
+        lambda *refs: None,
+        out_shape=shape(value.shape, value.dtype),
+        in_specs=[LEFT] * (1 + len(after)),
+        out_specs=LEFT,
+        input_output_aliases={0: 0},
+        cost_estimate=BRIEF,
+        compiler_params=pltpu.CompilerParams(vmem_limit_bytes=1 << 20),
+        name="hold",
+    )(value, *after)
+
+
+def far_sum(sc, far, near, after):
+    def kernel(sc, far_ref, near_ref, *rest):
+        rest[-1][...] = (far_ref[...] + jnp.where(sc[0] == 1, near_ref[...].astype(f32), 0.0)).astype(bf16)
+
+    return small(kernel, sc, [far, near], [shape(far.shape, bf16)], [], after, "far_sum")[0]
+
+
 CORE, SIDE, BACK = 1, 2, 4
 rope_base = 10000.0
 RUNS = 2
@@ -908,12 +928,11 @@
     return far, near, own
 
 
-def unwindow(far, near):
-    core, _, _ = place()
+def unwindow(sc, far, near, after=()):
     depth = lax.axis_size("fsdp")
     near = flip(near, CORE)
-    far = jnp.where(core == 1, far + near.astype(f32), far).astype(bf16)
-    return near, lax.ppermute(far, "fsdp", [(z + 1, z) for z in range(0, depth, 2)])
+    far = far_sum(sc, far, near, after)
+    return near, far, lax.ppermute(far, "fsdp", [(z + 1, z) for z in range(0, depth, 2)])
 
 
 def over_groups(value):
@@ -947,25 +966,28 @@
     parts_a = turns(pick_first(sc, query_weight, key_weight.T, value_weight.T, out_weight, gains))
     ids = jnp.broadcast_to((segment_ids[0] + 1).astype(bf16), (IDS, stretch))
     tokens = home_to_work(jnp.concatenate([tokens[0].T, ids]))
-    whole_a = stack(sc, parts_a)
+    piece_b = pick(sc, gate_weight, up_weight, parts_a[1:2])
+    parts_b = turns(piece_b)
+    whole_a = stack(sc, parts_a, [piece_b])
     gains = gains_of(whole_a)
     gain_a, gain_f = gains[:1], gains[1:]
     wa = plane_gather(whole_a.reshape(depth * rows, PIECE))
-    piece_b = pick(sc, gate_weight, up_weight, [whole_a])
-    whole_b = stack(sc, turns(piece_b)).reshape(depth * rows, piece_b.shape[1])
+    whole_b = stack(sc, parts_b, [wa[0][1], wa[0][2]]).reshape(depth * rows, piece_b.shape[1])
     wb = plane_gather(whole_b)
-    parts_d = turns(pick_down(sc, down_weight.T, [whole_b]))
-
-    h_0, a0, q0, own = pre(sc, tokens, gain_a, cos, sin, *wa, [whole_b])
+    piece_d = pick_down(sc, down_weight.T, [whole_b])
+
+    h_0, a0, q0, own = pre(sc, tokens, gain_a, cos, sin, *wa, [wb[0][1], wb[0][2], piece_d])
     kv0 = window(own)
+    far_d = hold(flip_z(piece_d, 2), [kv0[1], wb[0][3]])
+    parts_d = piece_d, flip_z(piece_d, 1), far_d, flip_z(far_d, 1)
     o0, lse0 = attend(q0, kv0)
     whole_d = stack(sc, parts_d, [o0])
     weights = wa, wb, (whole_d, flip(whole_d, CORE))
-    cot = home_to_work(cotangent[0].T)
     mixed0, h1_0, b0, gate0, up0, z0, h_1, a1, q1, own = post(False, sc, o0, h_0, gain_f, gain_a, cos, sin, own, *weights)
     kv1 = window(own)
     across_0 = across((a0, b0, mixed0))
     o1, lse1 = attend(q1, kv1, across_0)
+    cot = home_to_work(hold(cotangent[0].T, [o1]))
     mixed1, h1_1, b1, gate1, up1, z1, output = post(True, sc, o1, h_1, gain_f, gain_a, cos, sin, own, *weights)
     output = home_to_work(output, back=True)
     across_1 = across((a1, b1, mixed1))
@@ -973,56 +995,56 @@
     gb1, act1, away1, zk1, zs1, g1, p1, dgain_f1, do = back(True, False, sc, weights, [cot], [gate1, up1, h1_1, gain_f, z1])
     across_2 = across((gb1, away1, zs1))
     dq1, three1, far, near, own = attend_back(sc, p1, q1, kv1, lse1, do, cos, sin, [output, *across_1])
-    near, far = unwindow(far, near)
+    near, _, far = unwindow(sc, far, near)
     (three1,) = across((three1,))
     tail = [g1, dq1, own, near, far, h_1, gain_a, cos, sin]
     dk1, dv1, one1, dgain_a1, gb0, act0, away0, zk0, zs0, g1, p0, dgain_f0, do = back(False, False, sc, weights, tail, [gate0, up0, h1_0, gain_f, z0], [three1, *across_2])
 
     away0, gb0_, zs0, one1 = across((away0, gb0, zs0, one1))
-    send_b, keep_b = grad_ffn(sc, [b1, b0, across_1[1], across_0[1]], [act1, act0, across_2[1], away0])
+    dq0, three0, far, near, own = attend_back(sc, p0, q0, kv0, lse0, do, cos, sin, [one1])
+    near, down_far, far = unwindow(sc, far, near)
+    send_b, keep_b = grad_ffn(sc, [b1, b0, across_1[1], across_0[1]], [act1, act0, across_2[1], away0], [down_far])
     got_b = flip(send_b, SIDE, BACK)
     like_d, unlike_d = grad_down(sc, [gb1, gb0, across_2[0], gb0_], [zk1, zk0, across_2[2], zs0], [send_b])
     got_d = flip_z(unlike_d, 1)
-
-    dq0, three0, far, near, own = attend_back(sc, p0, q0, kv0, lse0, do, cos, sin, [like_d, one1])
-    near, far = unwindow(far, near)
     (three0,) = across((three0,))
-    later_b, own_b = sum_first(sc, keep_b, got_b, [own, three0])
-    more_b = flip(later_b, BACK, SIDE)
     tail = [g1, dq0, own, near, far, h_0, gain_a, cos, sin]
-    dk0, dv0, one0, dgain_a0, grad_tokens = back(False, True, sc, weights, tail, None, [later_b])
-    grad_tokens = home_to_work(grad_tokens, back=True)
-
-    pair_d = down_pair(sc, like_d, got_d, [one0])
-    got_d = flip_z(pair_d, 2, lambda d, z: (z >> 1) != (d & 1))
+    dk0, dv0, one0, dgain_a0, grad_tokens = back(False, True, sc, weights, tail, None, [like_d, three0])
+
     own = [dq1, dq0, dk1, dk0, dv1, dv0, p1, p0]
     got = [three1, three0, one1, flip(one0, CORE)]
-    send_a, keep_a = grad_attention(sc, [a1, a0, across_1[0], across_0[0]], [mixed1, mixed0, across_1[2], across_0[2]], own, got, [dgain_a1, dgain_a0, dgain_f1, dgain_f0], [pair_d])
+    send_a, keep_a = grad_attention(sc, [a1, a0, across_1[0], across_0[0]], [mixed1, mixed0, across_1[2], across_0[2]], own, got, [dgain_a1, dgain_a0, dgain_f1, dgain_f0], [])
     got_a = flip(send_a, SIDE, BACK)
-    send_b, ring_b = sum_second(sc, own_b, more_b, [send_a])
+    later_b, own_b = sum_first(sc, keep_b, got_b, [send_a])
+    more_b = flip(later_b, BACK, SIDE)
+    pair_d = down_pair(sc, like_d, got_d, [later_b])
+    got_d = flip_z(pair_d, 2, lambda d, z: (z >> 1) != (d & 1))
+    later_a, own_a = sum_first(sc, keep_a, got_a, [pair_d])
+    more_a = flip(later_a, BACK, SIDE)
+    send_b, ring_b = sum_second(sc, own_b, more_b, [later_a])
     got_b = flip_z(send_b, 1)
-    later_a, own_a = sum_first(sc, keep_a, got_a, [ring_b, grad_tokens])
-    more_a = flip(later_a, BACK, SIDE)
-    send_b, ring_b = sum_third(sc, ring_b, got_b, [later_a])
+    send_a, ring_a = sum_second(sc, own_a, more_a, [send_b])
+    got_a = flip_z(send_a, 1)
+    send_b, ring_b = sum_third(sc, ring_b, got_b, [send_a])
     got_b = flip_z(send_b, 2)
     give, keep = down_ring(sc, pair_d, got_d, [send_b])
-    send_d, keep_d = down_split(sc, keep, flip(give, CORE), [])
+    given = flip(give, CORE)
+    send_a, ring_a = sum_third(sc, ring_a, got_a, [give])
+    got_a = flip_z(send_a, 2)
+    send_d, keep_d = down_split(sc, keep, given, [send_a])
     got_d = flip(send_d, SIDE, BACK)
-    send_a, ring_a = sum_second(sc, own_a, more_a, [send_d])
-    got_a = flip_z(send_a, 1)
-    later_d, own_d = sum_first(sc, keep_d, got_d, [ring_a])
+    piece_b = over_groups(sum_two(sc, ring_b, got_b, [send_d]))
+    all_b = spread(piece_b)
+    later_d, own_d = sum_first(sc, keep_d, got_d, [piece_b])
     more_d = flip(later_d, BACK, SIDE)
-    piece_b = over_groups(sum_two(sc, ring_b, got_b, [later_d]))
-    all_b = spread(piece_b)
-    send_a, ring_a = sum_third(sc, ring_a, got_a, [piece_b])
-    got_a = flip_z(send_a, 2)
-    piece_d = over_groups(sum_two(sc, own_d, more_d, [send_a]))
+    piece_a = over_groups(sum_two(sc, ring_a, got_a, [later_d]))
+    all_a = spread(piece_a)
+    piece_d = over_groups(sum_two(sc, own_d, more_d, [piece_a]))
     grad_gate, grad_up = lay(sc, all_b, across(all_b), (gate_weight.shape[1],) * 2, [piece_d])
     all_d = spread(piece_d)
-    piece_a = over_groups(sum_two(sc, ring_a, got_a, [grad_gate]))
-    all_a = spread(piece_a)
-    grad_down_ = lay_down(sc, all_d, across(all_d), [piece_a])
-    grad_query, grad_key, grad_value, grad_out, dgains = lay(sc, all_a, across(all_a), (width, KVW, KVW, width), [grad_down_])
+    grad_query, grad_key, grad_value, grad_out, dgains = lay(sc, all_a, across(all_a), (width, KVW, KVW, width), [grad_gate])
+    grad_down_ = lay_down(sc, all_d, across(all_d), [grad_query])
+    grad_tokens = home_to_work(hold(grad_tokens, [piece_b]), back=True)
     grad_tokens, output = grad_tokens.astype(f32).T, output.T
     return (output[None], grad_tokens[None], dgains[0], grad_query, grad_key, grad_value, grad_out, dgains[1], grad_gate, grad_up, grad_down_.T)
 

time: 509 us -> 547 us (1.075)
  starting transfers between devices: 81.9 us -> 99.4 us
  local copies, waits for them, and re-layouts: 37.1 us -> 48.9 us
  waiting for transfers between devices: 189 us -> 199 us
    ppermute x63, starting transfers between devices: 45.6 us -> 65.2 us  [flip(): lax.ppermute(value, 'dp', [(i, i ^ bits[i & 1]) for i in range(count)])]
    ppermute x15, waiting for transfers between devices: 70.7 us -> 89 us  [flip_z(): return lax.ppermute(value, ('dp', 'fsdp'), pairs)]
    ppermute x2, waiting for transfers between devices: 26.1 us -> 11.7 us  [unwindow(): lax.ppermute(far, 'fsdp', [(z + 1, z) for z in range(0, depth, 2)])]
    unnamed x227 -> x240, local copies, waits for them, and re-layouts: 34.5 us -> 46.4 us
    ppermute x2, waiting for transfers between devices: 0.01 us -> 8.84 us  [window(): far = lax.ppermute(own, 'fsdp', [(z, z + 1) for z in range(0, depth, 2)])]
    ppermute x4, starting transfers between devices: 10 us -> 3.15 us  [home_to_work(): return lax.ppermute(value, ('dp', 'fsdp'), pairs)]
    pallas_call x14 -> x16, Pallas kernels: 14.6 us -> 15.8 us  [small(): pl.pallas_call(kernel, out_shape=tuple(outs), in_specs=[SCALARS] + [WHOLE...]
  transfers between devices with their start and end apart: 86 -> 86, of which waited for: 37 -> 37; matrix products, arithmetic and copies ran while one was open for 1% -> 1% of each run, Pallas kernels for 26% -> 18%
where the time goes in v7:
time: 547 us; the launch traced here: 541 us
  waiting for transfers between devices  199 us (36%)
  Pallas kernels  187 us (34%)
  starting transfers between devices  99.4 us (18%)
  local copies, waits for them, and re-layouts  48.9 us (9%)
    ppermute x63, waiting for transfers between devices, flip(): lax.ppermute(value, 'dp', [(i, i ^ bits[i & 1]) for i in range(count)])  89.1 us
    ppermute x15, waiting for transfers between devices, flip_z(): return lax.ppermute(value, ('dp', 'fsdp'), pairs)  89 us
    ppermute x63, starting transfers between devices, flip(): lax.ppermute(value, 'dp', [(i, i ^ bits[i & 1]) for i in range(count)])  65.2 us
    pallas_call x3, Pallas kernels, back(): pl.pallas_call(functools.partial(back_kernel, start, end, len(after)), ou...  50.4 us
    unnamed x240, local copies, waits for them, and re-layouts  46.4 us
    pallas_call x2, Pallas kernels, post(): pl.pallas_call(functools.partial(post_kernel, last), out_shape=tuple(outs...  38.2 us
    pallas_call x2, Pallas kernels, attend_back(): pl.pallas_call(attend_back_kernel, out_shape=(shape((3, n, PIECE), bf16),...  25.7 us
    ppermute x15, starting transfers between devices, flip_z(): return lax.ppermute(value, ('dp', 'fsdp'), pairs)  22.3 us
  transfers between devices with their start and end apart: 86, of which 37 were waited for; matrix products, arithmetic and copies ran while one was open for 1% of the time, Pallas kernels for 18%

profile of v7, /device:TPU:0, one launch (start us, length us, event | category | flops | bytes accessed | tf_op | source)
XLA Modules:
  0.0 540.7 jit_solution(3959192226561624359)
XLA Ops:
  0.7 2.0 copy.33
  8.7 4.1 collective-permute-start.2
  14.4 7.2 %collective-permute-done.2.rest_2_ = bf16[240,384]{1,0:T(8,128)(2,1)S(1)} collective-permute-done((bf16[240,384]{1,0:T(8,128)(2,1)S(1)}, bf16[240,384]{1,0:T(8,128)(2,1)S(1)}, u32[]{:S(2)}, u32[]{:S(2)}) %collective-permute-start.2) | collective-permute-done | bytes 184352 | tf_op jit(solution)/shard_map/ppermute | solution.py:893
  22.8 4.6 collective-permute-done.3.rest_3_
  31.8 3.2 collective-permute-start.12
  35.0 1.7 collective-permute-start.11
  36.8 11.3 %collective-permute-done.12.rest_2_ = bf16[240,640]{1,0:T(8,128)(2,1)S(1)} collective-permute-done((bf16[240,640]{1,0:T(8,128)(2,1)S(1)}, bf16[240,640]{1,0:T(8,128)(2,1)S(1)}, u32[]{:S(2)}, u32[]{:S(2)}) %collective-permute-start.12) | collective-permute-done | bytes 307232 | tf_op jit(solution)/shard_map/ppermute | solution.py:893
  48.6 7.6 %collective-permute-done.13.rest_3_ = bf16[240,640]{1,0:T(8,128)(2,1)S(1)} collective-permute-done((bf16[240,640]{1,0:T(8,128)(2,1)S(1)}, bf16[240,640]{1,0:T(8,128)(2,1)S(1)}, u32[]{:S(2)}, u32[]{:S(2)}) %collective-permute-start.13) | collective-permute-done | bytes 307232 | tf_op jit(solution)/shard_map/ppermute | solution.py:893
  60.7 9.5 %collective-permute-start.9 = (bf16[960,384]{1,0:T(8,128)(2,1)S(1)}, bf16[960,384]{1,0:T(8,128)(2,1)}, u32[]{:S(2)}, u32[]{:S(2)}) collective-permute-start(bf16[960,384]{1,0:T(8,128)(2,1)S(1)} %collective-permute-done.5.rest_5_.rest_2_), channel_id=1, source_target_pairs={{0,4},{4,0},{8,12},{12,8},{16,20},{20,16},{24,28},{28,24},{1,5},{5... | collective-permute-start | bytes 2211848 | tf_op jit(solution)/shard_map/ppermute | solution.py:887
  70.4 7.0 %collective-permute-done.6.rest_3_ = bf16[960,384]{1,0:T(8,128)(2,1)} collective-permute-done((bf16[960,384]{1,0:T(8,128)(2,1)S(1)}, bf16[960,384]{1,0:T(8,128)(2,1)}, u32[]{:S(2)}, u32[]{:S(2)}) %collective-permute-start.6) | collective-permute-done | bytes 737312 | tf_op jit(solution)/shard_map/ppermute | solution.py:887
  77.4 9.7 %collective-permute-done.14.rest_8_.rest_9_ = bf16[960,640]{1,0:T(8,128)(2,1)} collective-permute-done((bf16[960,640]{1,0:T(8,128)(2,1)S(1)}, bf16[960,640]{1,0:T(8,128)(2,1)}, u32[]{:S(2)}, u32[]{:S(2)}) %collective-permute-start.14) | collective-permute-done | bytes 1228832 | tf_op jit(solution)/shard_map/ppermute | solution.py:887
  92.5 6.8 %pre.1 = (bf16[256,960]{1,0:T(8,128)(2,1)}, bf16[256,960]{1,0:T(8,128)(2,1)}, bf16[960,256]{1,0:T(8,128)(2,1)}, bf16[656,256]{1,0:T(8,128)(2,1)}) custom-call(s32[3]{0:T(128)} %copy-done.66, bf16[976,256]{1,0:T(8,128)(2,1)} %copy-done.109, f32[1,960]{1,0:T(1,128)} %get-tuple-element.209.gain_ref.gain_a.rest_24_.rest_14_, ...), custom_call_target="tpu_custom_call" | custom-call | flops 1024 | bytes 1024 | tf_op jit(solution)/shard_map/pre/pallas_call | solution.py:118
  99.3 4.5 collective-permute-start.16
  103.8 3.4 collective-permute-start.24
  107.3 3.0 collective-permute-done.16.kv0
  111.3 3.1 collective-permute-start.17
  114.4 2.5 collective-permute-start.23
  116.9 17.2 %collective-permute-done.24.refs_0_ = bf16[480,640]{1,0:T(8,128)(2,1)} collective-permute-done((bf16[480,640]{1,0:T(8,128)(2,1)S(1)}, bf16[480,640]{1,0:T(8,128)(2,1)}, u32[]{:S(2)}, u32[]{:S(2)}) %collective-permute-start.24) | collective-permute-done | bytes 614432 | tf_op jit(solution)/shard_map/ppermute | solution.py:893
  134.2 10.1 %attend.2 = (bf16[960,256]{1,0:T(8,128)(2,1)S(1)}, f32[15,256]{1,0:T(8,128)S(1)}) custom-call(bf16[960,256]{1,0:T(8,128)(2,1)S(1)} %copy-done.48, bf16[656,256]{1,0:T(8,128)(2,1)S(1)} %collective-permute-done.16.kv0, bf16[656,256]{1,0:T(8,128)(2,1)S(1)} %collective-permute-done.17.kv1.refs_1_, bf16[656,256]{1,0:T(8,128)(2,1)S(1)} %copy-done.9), custom_call_target="tpu_custom_call" | custom-call | flops 1024 | bytes 1024 | tf_op jit(solution)/shard_map/attend/pallas_call | solution.py:171
  144.6 12.6 %collective-permute-done.25.rest_3_ = bf16[480,640]{1,0:T(8,128)(2,1)S(1)} collective-permute-done((bf16[480,640]{1,0:T(8,128)(2,1)}, bf16[480,640]{1,0:T(8,128)(2,1)S(1)}, u32[]{:S(2)}, u32[]{:S(2)}) %collective-permute-start.25) | collective-permute-done | bytes 614432 | tf_op jit(solution)/shard_map/ppermute | solution.py:893
  157.2 2.0 stack.33.rest_16_
  160.4 7.1 %collective-permute-done.19.rest_12_ = bf16[960,640]{1,0:T(8,128)(2,1)S(1)} collective-permute-done((bf16[960,640]{1,0:T(8,128)(2,1)S(1)}, bf16[960,640]{1,0:T(8,128)(2,1)S(1)}, u32[]{:S(2)}, u32[]{:S(2)}) %collective-permute-start.19) | collective-permute-done | bytes 1228832 | tf_op jit(solution)/shard_map/ppermute | solution.py:887
  167.7 1.8 collective-permute-done.20.rest_13_
  169.4 1.8 collective-permute-done.22.rest_15_
  173.0 20.4 %post.2 = (bf16[256,960]{1,0:T(8,128)(2,1)}, f32[256,960]{1,0:T(8,128)}, bf16[256,960]{1,0:T(8,128)(2,1)}, bf16[256,2560]{1,0:T(8,128)(2,1)}, bf16[256,2560]{1,0...) custom-call(s32[3]{0:T(128)} %copy-done.66, ...), custom_call_target="tpu_custom_call" | custom-call | flops 1024 | bytes 1024 | tf_op jit(solution)/shard_map/post/pallas_call | solution.py:305
  193.4 1.7 collective-permute-start.27
  195.8 5.9 %collective-permute-done.27.kv0 = bf16[656,256]{1,0:T(8,128)(2,1)S(1)} collective-permute-done((bf16[656,256]{1,0:T(8,128)(2,1)}, bf16[656,256]{1,0:T(8,128)(2,1)S(1)}, u32[]{:S(2)}, u32[]{:S(2)}) %collective-permute-start.27) | collective-permute-done | bytes 335904 | tf_op jit(solution)/shard_map/ppermute | solution.py:926
  205.4 10.1 %attend.3 = (bf16[960,256]{1,0:T(8,128)(2,1)S(1)}, f32[15,256]{1,0:T(8,128)S(1)}) custom-call(bf16[960,256]{1,0:T(8,128)(2,1)S(1)} %copy-done.53, bf16[656,256]{1,0:T(8,128)(2,1)S(1)} %collective-permute-done.27.kv0, bf16[656,256]{1,0:T(8,128)(2,1)S(1)} %collective-permute-done.28.kv1, bf16[656,256]{1,0:T(8,128)(2,1)S(1)} %copy-done.7, ...), custom_call_target="tpu_custom_call" | custom-call | flops 1024 | bytes 1024 | tf_op jit(solution)/shard_map/attend/pallas_call | solution.py:171
  216.7 17.8 %post.3 = (bf16[256,960]{1,0:T(8,128)(2,1)}, f32[256,960]{1,0:T(8,128)}, bf16[256,960]{1,0:T(8,128)(2,1)}, bf16[256,2560]{1,0:T(8,128)(2,1)}, bf16[256,2560]{1,0...) custom-call(s32[3]{0:T(128)} %copy-done.66, bf16[960,256]{1,0:T(8,128)(2,1)} %copy-done.54, ...), custom_call_target="tpu_custom_call" | custom-call | flops 1024 | bytes 1024 | tf_op jit(solution)/shard_map/post/pallas_call | solution.py:305
  235.4 21.9 %back_start.1 = (bf16[256,960]{1,0:T(8,128)(2,1)}, bf16[256,2560]{1,0:T(8,128)(2,1)}, bf16[256,2560]{1,0:T(8,128)(2,1)}, bf16[256,1280]{1,0:T(8,128)(2,1)}, bf16...) custom-call(s32[3]{0:T(128)} %copy-done.66, ...), custom_call_target="tpu_custom_call" | custom-call | flops 1024 | bytes 1024 | tf_op jit(solution)/shard_map/back_start/pallas_call | solution.py:461
  257.2 4.5 collective-permute-start.41
  262.5 1.7 collective-permute-start.35
  268.9 12.6 %attend_back.2 = (bf16[3,256,384]{2,1,0:T(8,128)(2,1)S(1)}, bf16[3,256,384]{2,1,0:T(8,128)(2,1)S(1)}, f32[640,256]{1,0:T(8,128)S(1)}, bf16[640,256]{1,0:T(8,128)(2,1)S(1)}, f32[640,256]{1,0:T(8,128)S(1)}) custom-call(s32[3]{0:T(128)S(1)} %copy-done.68, bf16[3,256,384]{2,1,0:T(8,128)(2,1)S(1)} %copy-done.18, bf16[960,256]{1,0:T(8,128)(2,1)S(1)} %copy-done.53, ...), custom_call_target="tpu_custom_call" | custom-call | flops 1024 | bytes 1024 | tf_op jit(solution)/shard_map/attend_back/pallas_call | solution.py:224
  282.4 11.4 %collective-permute-start.37 = (bf16[640,256]{1,0:T(8,128)(2,1)S(1)}, bf16[640,256]{1,0:T(8,128)(2,1)S(1)}, u32[]{:S(2)}, u32[]{:S(2)}) collective-permute-start(bf16[640,256]{1,0:T(8,128)(2,1)S(1)} %get-tuple-element.129), channel_id=1, source_target_pairs={{0,4},{4,0},{8,12},{12,8},{16,20},{20,16},{24,28},{28,24},{1,5},{5... | collective-permute-start | bytes 983048 | tf_op jit(solution)/shard_map/ppermute | solution.py:887
  297.6 10.0 %collective-permute-done.38.rest_22_ = bf16[640,256]{1,0:T(8,128)(2,1)S(1)} collective-permute-done((bf16[640,256]{1,0:T(8,128)(2,1)S(1)}, bf16[640,256]{1,0:T(8,128)(2,1)S(1)}, u32[]{:S(2)}, u32[]{:S(2)}) %collective-permute-start.38) | collective-permute-done | bytes 327712 | tf_op jit(solution)/shard_map/ppermute | solution.py:935
  308.7 22.0 %back_join.1 = (bf16[256,384]{1,0:T(8,128)(2,1)}, bf16[256,384]{1,0:T(8,128)(2,1)}, bf16[256,384]{1,0:T(8,128)(2,1)}, f32[1,960]{1,0:T(1,128)}, bf16[256,960]{1,...) custom-call(s32[3]{0:T(128)} %copy-done.66, ...), custom_call_target="tpu_custom_call" | custom-call | flops 1024 | bytes 1024 | tf_op jit(solution)/shard_map/back_join/pallas_call | solution.py:461
  331.4 3.0 collective-permute-done.43.rest_0_.rest_18_
  336.6 13.1 %attend_back.3 = (bf16[3,256,384]{2,1,0:T(8,128)(2,1)S(1)}, bf16[3,256,384]{2,1,0:T(8,128)(2,1)S(1)}, f32[640,256]{1,0:T(8,128)S(1)}, bf16[640,256]{1,0:T(8,128)(2,1)S(1)}, f32[640,256]{1,0:T(8,128)S(1)}) custom-call(s32[3]{0:T(128)S(1)} %copy-done.69, bf16[3,256,384]{2,1,0:T(8,128)(2,1)S(1)} %copy-done.20, bf16[960,256]{1,0:T(8,128)(2,1)S(1)} %copy-done.49, ...), custom_call_target="tpu_custom_call" | custom-call | flops 1024 | bytes 1024 | tf_op jit(solution)/shard_map/attend_back/pallas_call | solution.py:224
  356.3 6.9 %grad_ffn.1 = (bf16[2,960,640]{2,1,0:T(8,128)(2,1)S(1)}, bf16[2,960,640]{2,1,0:T(8,128)(2,1)S(1)}) custom-call(s32[3]{0:T(128)S(1)} %copy-done.69, bf16[256,960]{1,0:T(8,128)(2,1)S(1)} %copy-done.87, bf16[256,960]{1,0:T(8,128)(2,1)S(1)} %copy-done.85, bf16[256,960]{1,0:T(8,128)(2,1)S(1)} %copy-done.45, bf16[256,960]{1,0:T(8,128)(2,1)S(1)} %copy-done.47, ...), custom_call_target="tpu_custom_call" | custom-call | flops 1024 | bytes 1024 | tf_op jit(solution)/shard_map/grad_ffn/pallas_call | solution.py:502
  367.8 4.9 grad_down.1
  374.8 1.8 collective-permute-done.45.rest_12_
  377.3 6.5 %back_end.1 = (bf16[256,384]{1,0:T(8,128)(2,1)}, bf16[256,384]{1,0:T(8,128)(2,1)}, bf16[256,384]{1,0:T(8,128)(2,1)}, f32[1,960]{1,0:T(1,128)}, bf16[960,256]{1,0:T(8,128)(2,1)}) custom-call(s32[3]{0:T(128)} %copy-done.66, bf16[960,384]{1,0:T(8,128)(2,1)} %bitcast.32, bf16[960,384]{1,0:T(8,128)(2,1)} %copy-done.4, bf16[960,384]{1,0:T(8,128)(2,1)} %copy-done.3, ...), custom_call_target="tpu_custom_call" | custom-call | flops 1024 | bytes 1024 | tf_op jit(solution)/shard_map/back_end/pallas_call | solution.py:461
  403.5 5.9 %grad_attention.1 = (bf16[2,960,384]{2,1,0:T(8,128)(2,1)S(1)}, bf16[2,960,384]{2,1,0:T(8,128)(2,1)S(1)}) custom-call(s32[3]{0:T(128)S(1)} %copy-done.70, bf16[256,960]{1,0:T(8,128)(2,1)S(1)} %copy-done.82, bf16[256,960]{1,0:T(8,128)(2,1)S(1)} %copy-done.79, bf16[256,960]{1,0:T(8,128)(2,1)S(1)} %copy-done.37, bf16[256,960]{1,0:T(8,128)(2,1)S(1)} %copy-done.41, ...), custom_call_target="tpu_custom_call" | custom-call | flops 1024 | bytes 1024 | tf_op jit(solution)/shard_map/grad_attention/pallas_call | solution.py:580
  409.5 1.9 collective-permute-start.53
  411.4 2.3 sum_first.3
  415.0 1.6 down_pair.1.rest_0_.own_ref
  417.9 22.6 %collective-permute-done.53.got_ref = bf16[2,960,384]{2,1,0:T(8,128)(2,1)S(1)} collective-permute-done((bf16[2,960,384]{2,1,0:T(8,128)(2,1)S(1)}, bf16[2,960,384]{2,1,0:T(8,128)(2,1)S(1)}, u32[]{:S(2)}, u32[]{:S(2)}) %collective-permute-start.53) | collective-permute-done | bytes 1474592 | tf_op jit(solution)/shard_map/ppermute | solution.py:887
  441.3 4.7 collective-permute-start.56
  447.1 8.4 %collective-permute-done.56.got_ref = bf16[960,384]{1,0:T(8,128)(2,1)S(1)} collective-permute-done((bf16[960,384]{1,0:T(8,128)(2,1)S(1)}, bf16[960,384]{1,0:T(8,128)(2,1)S(1)}, u32[]{:S(2)}, u32[]{:S(2)}) %collective-permute-start.56) | collective-permute-done | bytes 737312 | tf_op jit(solution)/shard_map/ppermute | solution.py:887
  456.2 5.4 collective-permute-done.55.got_ref
  463.3 1.9 collective-permute-start.57
  465.2 15.6 %collective-permute-done.60.got_ref = bf16[2,240,384]{2,1,0:T(8,128)(2,1)S(1)} collective-permute-done((bf16[2,240,384]{2,1,0:T(8,128)(2,1)S(1)}, bf16[2,240,384]{2,1,0:T(8,128)(2,1)S(1)}, u32[]{:S(2)}, u32[]{:S(2)}) %collective-permute-start.60) | collective-permute-done | bytes 368672 | tf_op jit(solution)/shard_map/ppermute | solution.py:893
  482.2 1.8 collective-permute-start.63
  486.5 1.7 collective-permute-start.71
  488.2 3.0 collective-permute-done.63.got_ref
  491.9 7.3 %collective-permute-done.62.got_ref = bf16[240,384]{1,0:T(8,128)(2,1)S(1)} collective-permute-done((bf16[240,384]{1,0:T(8,128)(2,1)S(1)}, bf16[240,384]{1,0:T(8,128)(2,1)S(1)}, u32[]{:S(2)}, u32[]{:S(2)}) %collective-permute-start.62) | collective-permute-done | bytes 184352 | tf_op jit(solution)/shard_map/ppermute | solution.py:893
  504.0 8.1 %collective-permute-done.78.got_ref = bf16[120,640]{1,0:T(8,128)(2,1)S(1)} collective-permute-done((bf16[120,640]{1,0:T(8,128)(2,1)S(1)}, bf16[120,640]{1,0:T(8,128)(2,1)S(1)}, u32[]{:S(2)}, u32[]{:S(2)}) %collective-permute-start.78) | collective-permute-done | bytes 153632 | tf_op jit(solution)/shard_map/ppermute | solution.py:887
  514.7 3.0 collective-permute-done.64.rest_1_
  518.4 2.1 collective-permute-start.80
  521.7 3.6 collective-permute-done.81.rest_3_
  526.3 3.1 lay.2
  530.5 1.7 copy-done.17
  532.2 2.4 lay.3
  537.0 2.7 lay_down.1
  (404 shorter events, 107.9 us)
Async XLA Ops:
  8.7 12.8 %collective-permute-start.2 = (bf16[240,384]{1,0:T(8,128)(2,1)S(1)}, bf16[240,384]{1,0:T(8,128)(2,1)S(1)}, u32[]{:S(2)}, u32[]{:S(2)}) collective-permute-start(bf16[240,384]{1,0:T(8,128)(2,1)S(1)} %pick_first.1.rest_0_), channel_id=1, source_target_pairs={{0,2},{1,3},{2,0},{3,1},{4,6},{5,7},{6,4},{7,5},{8,10},{9,11},{10,... | collective-permute-start | bytes 552968 | tf_op jit(solution)/shard_map/ppermute | solution.py:893
  12.8 9.4 %collective-permute-start.1 = (bf16[240,384]{1,0:T(8,128)(2,1)S(1)}, bf16[240,384]{1,0:T(8,128)(2,1)S(1)}, u32[]{:S(2)}, u32[]{:S(2)}) collective-permute-start(bf16[240,384]{1,0:T(8,128)(2,1)S(1)} %pick_first.1.rest_0_), channel_id=1, source_target_pairs={{0,1},{1,0},{2,3},{3,2},{4,5},{5,4},{6,7},{7,6},{8,9},{9,8},{10,11... | collective-permute-start | bytes 552968 | tf_op jit(solution)/shard_map/ppermute | solution.py:893
  29.0 27.3 %collective-permute-start.5 = (bf16[960,384]{1,0:T(8,128)(2,1)S(1)}, bf16[960,384]{1,0:T(8,128)(2,1)S(1)}, u32[]{:S(2)}, u32[]{:S(2)}) collective-permute-start(bf16[960,384]{1,0:T(8,128)(2,1)S(1)} %bitcast.24), channel_id=1, source_target_pairs={{0,16},{4,12},{8,24},{12,4},{16,0},{20,28},{24,8},{28,20},{1,17},{... | collective-permute-start | bytes 2211848 | tf_op jit(solution)/shard_map/ppermute | solution.py:887
  30.3 25.9 %collective-permute-start.4 = (bf16[960,384]{1,0:T(8,128)(2,1)S(1)}, bf16[960,384]{1,0:T(8,128)(2,1)S(1)}, u32[]{:S(2)}, u32[]{:S(2)}) collective-permute-start(bf16[960,384]{1,0:T(8,128)(2,1)S(1)} %bitcast.25), channel_id=1, source_target_pairs={{0,8},{4,20},{8,0},{12,28},{16,24},{20,4},{24,16},{28,12},{1,9},{5... | collective-permute-start | bytes 2211848 | tf_op jit(solution)/shard_map/ppermute | solution.py:887
  31.8 16.3 %collective-permute-start.12 = (bf16[240,640]{1,0:T(8,128)(2,1)S(1)}, bf16[240,640]{1,0:T(8,128)(2,1)S(1)}, u32[]{:S(2)}, u32[]{:S(2)}) collective-permute-start(bf16[240,640]{1,0:T(8,128)(2,1)S(1)} %pick.1.rest_4_.rest_0_), channel_id=1, source_target_pairs={{0,2},{1,3},{2,0},{3,1},{4,6},{5,7},{6,4},{7,5},{8,10},{9,11},{10,... | collective-permute-start | bytes 921608 | tf_op jit(solution)/shard_map/ppermute | solution.py:893
  35.0 13.6 %collective-permute-start.11 = (bf16[240,640]{1,0:T(8,128)(2,1)S(1)}, bf16[240,640]{1,0:T(8,128)(2,1)S(1)}, u32[]{:S(2)}, u32[]{:S(2)}) collective-permute-start(bf16[240,640]{1,0:T(8,128)(2,1)S(1)} %pick.1.rest_4_.rest_0_), channel_id=1, source_target_pairs={{0,1},{1,0},{2,3},{3,2},{4,5},{5,4},{6,7},{7,6},{8,9},{9,8},{10,11... | collective-permute-start | bytes 921608 | tf_op jit(solution)/shard_map/ppermute | solution.py:893
  48.1 8.2 %collective-permute-start.13 = (bf16[240,640]{1,0:T(8,128)(2,1)S(1)}, bf16[240,640]{1,0:T(8,128)(2,1)S(1)}, u32[]{:S(2)}, u32[]{:S(2)}) collective-permute-start(bf16[240,640]{1,0:T(8,128)(2,1)S(1)} %collective-permute-done.12.rest_2_), channel_id=1, source_target_pairs={{0,1},{1,0},{2,3},{3,2},{4,5},{5,4},{6,7},{7,6},{8,9},{9,8},{10,11... | collective-permute-start | bytes 921608 | tf_op jit(solution)/shard_map/ppermute | solution.py:893
  57.2 29.9 %collective-permute-start.14 = (bf16[960,640]{1,0:T(8,128)(2,1)S(1)}, bf16[960,640]{1,0:T(8,128)(2,1)}, u32[]{:S(2)}, u32[]{:S(2)}) collective-permute-start(bf16[960,640]{1,0:T(8,128)(2,1)S(1)} %bitcast.33), channel_id=1, source_target_pairs={{0,8},{4,20},{8,0},{12,28},{16,24},{20,4},{24,16},{28,12},{1,9},{5... | collective-permute-start | bytes 3686408 | tf_op jit(solution)/shard_map/ppermute | solution.py:887
  57.9 12.4 %collective-permute-start.7 = (bf16[960,384]{1,0:T(8,128)(2,1)S(1)}, bf16[960,384]{1,0:T(8,128)(2,1)S(1)}, u32[]{:S(2)}, u32[]{:S(2)}) collective-permute-start(bf16[960,384]{1,0:T(8,128)(2,1)S(1)} %bitcast.26), channel_id=1, source_target_pairs={{0,4},{4,0},{8,12},{12,8},{16,20},{20,16},{24,28},{28,24},{1,5},{5... | collective-permute-start | bytes 2211848 | tf_op jit(solution)/shard_map/ppermute | solution.py:887
  57.9 19.5 %collective-permute-start.6 = (bf16[960,384]{1,0:T(8,128)(2,1)S(1)}, bf16[960,384]{1,0:T(8,128)(2,1)}, u32[]{:S(2)}, u32[]{:S(2)}) collective-permute-start(bf16[960,384]{1,0:T(8,128)(2,1)S(1)} %collective-permute-done.4.rest_4_.rest_1_), channel_id=1, source_target_pairs={{0,16},{4,12},{8,24},{12,4},{16,0},{20,28},{24,8},{28,20},{1,17},{... | collective-permute-start | bytes 2211848 | tf_op jit(solution)/shard_map/ppermute | solution.py:887
  59.2 33.3 %collective-permute-start.15 = (bf16[960,640]{1,0:T(8,128)(2,1)S(1)}, bf16[960,640]{1,0:T(8,128)(2,1)}, u32[]{:S(2)}, u32[]{:S(2)}) collective-permute-start(bf16[960,640]{1,0:T(8,128)(2,1)S(1)} %bitcast.34), channel_id=1, source_target_pairs={{0,16},{4,12},{8,24},{12,4},{16,0},{20,28},{24,8},{28,20},{1,17},{... | collective-permute-start | bytes 3686408 | tf_op jit(solution)/shard_map/ppermute | solution.py:887
  60.7 31.7 %collective-permute-start.9 = (bf16[960,384]{1,0:T(8,128)(2,1)S(1)}, bf16[960,384]{1,0:T(8,128)(2,1)}, u32[]{:S(2)}, u32[]{:S(2)}) collective-permute-start(bf16[960,384]{1,0:T(8,128)(2,1)S(1)} %collective-permute-done.5.rest_5_.rest_2_), channel_id=1, source_target_pairs={{0,4},{4,0},{8,12},{12,8},{16,20},{20,16},{24,28},{28,24},{1,5},{5... | collective-permute-start | bytes 2211848 | tf_op jit(solution)/shard_map/ppermute | solution.py:887
  70.3 22.2 %collective-permute-start.8 = (bf16[960,384]{1,0:T(8,128)(2,1)S(1)}, bf16[960,384]{1,0:T(8,128)(2,1)}, u32[]{:S(2)}, u32[]{:S(2)}) collective-permute-start(bf16[960,384]{1,0:T(8,128)(2,1)S(1)} %collective-permute-done.4.rest_4_.rest_1_), channel_id=1, source_target_pairs={{0,4},{4,0},{8,12},{12,8},{16,20},{20,16},{24,28},{28,24},{1,5},{5... | collective-permute-start | bytes 2211848 | tf_op jit(solution)/shard_map/ppermute | solution.py:887
  77.4 15.1 %collective-permute-start.10 = (bf16[960,384]{1,0:T(8,128)(2,1)}, bf16[960,384]{1,0:T(8,128)(2,1)}, u32[]{:S(2)}, u32[]{:S(2)}) collective-permute-start(bf16[960,384]{1,0:T(8,128)(2,1)} %collective-permute-done.6.rest_3_), channel_id=1, source_target_pairs={{0,4},{4,0},{8,12},{12,8},{16,20},{20,16},{24,28},{28,24},{1,5},{5... | collective-permute-start | bytes 2211848 | tf_op jit(solution)/shard_map/ppermute | solution.py:887
  87.2 46.9 %collective-permute-start.18 = (bf16[960,640]{1,0:T(8,128)(2,1)}, bf16[960,640]{1,0:T(8,128)(2,1)}, u32[]{:S(2)}, u32[]{:S(2)}) collective-permute-start(bf16[960,640]{1,0:T(8,128)(2,1)} %collective-permute-done.14.rest_8_.rest_9_), channel_id=1, source_target_pairs={{0,16},{4,12},{8,24},{12,4},{16,0},{20,28},{24,8},{28,20},{1,17},{... | collective-permute-start | bytes 3686408 | tf_op jit(solution)/shard_map/ppermute | solution.py:887
  99.3 10.9 %collective-permute-start.16 = (bf16[656,256]{1,0:T(8,128)(2,1)}, bf16[656,256]{1,0:T(8,128)(2,1)S(1)}, u32[]{:S(2)}, u32[]{:S(2)}) collective-permute-start(bf16[656,256]{1,0:T(8,128)(2,1)} %get-tuple-element.105.kv2.rest_18_), channel_id=1, source_target_pairs={{0,1},{2,3},{4,5},{6,7},{8,9},{10,11},{12,13},{14,15},{16,17},{18,... | collective-permute-start | bytes 1007624 | tf_op jit(solution)/shard_map/ppermute | solution.py:926
  103.8 30.2 %collective-permute-start.24 = (bf16[480,640]{1,0:T(8,128)(2,1)S(1)}, bf16[480,640]{1,0:T(8,128)(2,1)}, u32[]{:S(2)}, u32[]{:S(2)}) collective-permute-start(bf16[480,640]{1,0:T(8,128)(2,1)S(1)} %copy-done.6), channel_id=1, source_target_pairs={{0,2},{1,3},{2,0},{3,1},{4,6},{5,7},{6,4},{7,5},{8,10},{9,11},{10,... | collective-permute-start | bytes 1843208 | tf_op jit(solution)/shard_map/ppermute | solution.py:893
  111.3 22.8 %collective-permute-start.17 = (bf16[656,256]{1,0:T(8,128)(2,1)S(1)}, bf16[656,256]{1,0:T(8,128)(2,1)S(1)}, u32[]{:S(2)}, u32[]{:S(2)}) collective-permute-start(bf16[656,256]{1,0:T(8,128)(2,1)S(1)} %broadcast_select_fusion.1), channel_id=1, source_target_pairs={{0,4},{4,0},{8,12},{12,8},{16,20},{20,16},{24,28},{28,24},{1,5},{5... | collective-permute-start | bytes 1007624 | tf_op jit(solution)/shard_map/ppermute | solution.py:887
  114.4 30.2 %collective-permute-start.23 = (bf16[480,640]{1,0:T(8,128)(2,1)S(1)}, bf16[480,640]{1,0:T(8,128)(2,1)S(1)}, u32[]{:S(2)}, u32[]{:S(2)}) collective-permute-start(bf16[480,640]{1,0:T(8,128)(2,1)S(1)} %copy-done.6), channel_id=1, source_target_pairs={{0,1},{1,0},{2,3},{3,2},{4,5},{5,4},{6,7},{7,6},{8,9},{9,8},{10,11... | collective-permute-start | bytes 1843208 | tf_op jit(solution)/shard_map/ppermute | solution.py:893
  134.1 23.1 %collective-permute-start.25 = (bf16[480,640]{1,0:T(8,128)(2,1)}, bf16[480,640]{1,0:T(8,128)(2,1)S(1)}, u32[]{:S(2)}, u32[]{:S(2)}) collective-permute-start(bf16[480,640]{1,0:T(8,128)(2,1)} %hold.3.rest_2_), channel_id=1, source_target_pairs={{0,1},{1,0},{2,3},{3,2},{4,5},{5,4},{6,7},{7,6},{8,9},{9,8},{10,11... | collective-permute-start | bytes 1843208 | tf_op jit(solution)/shard_map/ppermute | solution.py:893
  159.2 12.0 %collective-permute-start.26 = (bf16[4,480,640]{2,1,0:T(8,128)(2,1)S(1)}, bf16[4,480,640]{2,1,0:T(8,128)(2,1)S(1)}, u32[]{:S(2)}, u32[]{:S(2)}) collective-permute-start(bf16[4,480,640]{2,1,0:T(8,128)(2,1)S(1)} %stack.33.rest_16_), channel_id=1, source_target_pairs={{0,4},{4,0},{8,12},{12,8},{16,20},{20,16},{24,28},{28,24},{1,5},{5... | collective-permute-start | bytes 7372808 | tf_op jit(solution)/shard_map/ppermute | solution.py:887
  159.3 8.2 %collective-permute-start.19 = (bf16[960,640]{1,0:T(8,128)(2,1)S(1)}, bf16[960,640]{1,0:T(8,128)(2,1)S(1)}, u32[]{:S(2)}, u32[]{:S(2)}) collective-permute-start(bf16[960,640]{1,0:T(8,128)(2,1)S(1)} %bitcast.36), channel_id=1, source_target_pairs={{0,4},{4,0},{8,12},{12,8},{16,20},{20,16},{24,28},{28,24},{1,5},{5... | collective-permute-start | bytes 3686408 | tf_op jit(solution)/shard_map/ppermute | solution.py:887
  159.8 7.9 %collective-permute-start.21 = (bf16[960,640]{1,0:T(8,128)(2,1)}, bf16[960,640]{1,0:T(8,128)(2,1)S(1)}, u32[]{:S(2)}, u32[]{:S(2)}) collective-permute-start(bf16[960,640]{1,0:T(8,128)(2,1)} %collective-permute-done.15.rest_9_.rest_10_), channel_id=1, source_target_pairs={{0,4},{4,0},{8,12},{12,8},{16,20},{20,16},{24,28},{28,24},{1,5},{5... | collective-permute-start | bytes 3686408 | tf_op jit(solution)/shard_map/ppermute | solution.py:887
  159.9 9.6 %collective-permute-start.20 = (bf16[960,640]{1,0:T(8,128)(2,1)}, bf16[960,640]{1,0:T(8,128)(2,1)S(1)}, u32[]{:S(2)}, u32[]{:S(2)}) collective-permute-start(bf16[960,640]{1,0:T(8,128)(2,1)} %collective-permute-done.14.rest_8_.rest_9_), channel_id=1, source_target_pairs={{0,4},{4,0},{8,12},{12,8},{16,20},{20,16},{24,28},{28,24},{1,5},{5... | collective-permute-start | bytes 3686408 | tf_op jit(solution)/shard_map/ppermute | solution.py:887
  160.3 10.9 %collective-permute-start.22 = (bf16[960,640]{1,0:T(8,128)(2,1)}, bf16[960,640]{1,0:T(8,128)(2,1)S(1)}, u32[]{:S(2)}, u32[]{:S(2)}) collective-permute-start(bf16[960,640]{1,0:T(8,128)(2,1)} %collective-permute-done.18.refs_2_.rest_11_), channel_id=1, source_target_pairs={{0,4},{4,0},{8,12},{12,8},{16,20},{20,16},{24,28},{28,24},{1,5},{5... | collective-permute-start | bytes 3686408 | tf_op jit(solution)/shard_map/ppermute | solution.py:887
  193.4 8.2 %collective-permute-start.27 = (bf16[656,256]{1,0:T(8,128)(2,1)}, bf16[656,256]{1,0:T(8,128)(2,1)S(1)}, u32[]{:S(2)}, u32[]{:S(2)}) collective-permute-start(bf16[656,256]{1,0:T(8,128)(2,1)} %get-tuple-element.109.kv2.rest_18_), channel_id=1, source_target_pairs={{0,1},{2,3},{4,5},{6,7},{8,9},{10,11},{12,13},{14,15},{16,17},{18,... | collective-permute-start | bytes 1007624 | tf_op jit(solution)/shard_map/ppermute | solution.py:926
  195.1 7.6 %collective-permute-start.29 = (bf16[256,960]{1,0:T(8,128)(2,1)S(1)}, bf16[256,960]{1,0:T(8,128)(2,1)S(1)}, u32[]{:S(2)}, u32[]{:S(2)}) collective-permute-start(bf16[256,960]{1,0:T(8,128)(2,1)S(1)} %copy-done.78), channel_id=1, source_target_pairs={{0,4},{4,0},{8,12},{12,8},{16,20},{20,16},{24,28},{28,24},{1,5},{5... | collective-permute-start | bytes 1474568 | tf_op jit(solution)/shard_map/ppermute | solution.py:887
  195.2 7.6 %collective-permute-start.30 = (bf16[256,960]{1,0:T(8,128)(2,1)}, bf16[256,960]{1,0:T(8,128)(2,1)S(1)}, u32[]{:S(2)}, u32[]{:S(2)}) collective-permute-start(bf16[256,960]{1,0:T(8,128)(2,1)} %get-tuple-element.111.rest_1_), channel_id=1, source_target_pairs={{0,4},{4,0},{8,12},{12,8},{16,20},{20,16},{24,28},{28,24},{1,5},{5... | collective-permute-start | bytes 1474568 | tf_op jit(solution)/shard_map/ppermute | solution.py:887
  215.6 19.0 %collective-permute-start.33 = (bf16[960,256]{1,0:T(8,128)(2,1)S(1)}, bf16[960,256]{1,0:T(8,128)(2,1)S(1)}, u32[]{:S(2)}, u32[]{:S(2)}) collective-permute-start(bf16[960,256]{1,0:T(8,128)(2,1)S(1)} %hold.4), channel_id=1, source_target_pairs={{0,0},{1,4},{2,1},{3,5},{4,2},{5,6},{6,3},{7,7},{8,8},{9,12},{10,9... | collective-permute-start | bytes 1474568 | tf_op jit(solution)/shard_map/ppermute | solution.py:904
  257.2 50.3 %collective-permute-start.41 = (bf16[256,2560]{1,0:T(8,128)(2,1)}, bf16[256,2560]{1,0:T(8,128)(2,1)S(1)}, u32[]{:S(2)}, u32[]{:S(2)}) collective-permute-start(bf16[256,2560]{1,0:T(8,128)(2,1)} %get-tuple-element.137), channel_id=1, source_target_pairs={{0,4},{4,0},{8,12},{12,8},{16,20},{20,16},{24,28},{28,24},{1,5},{5... | collective-permute-start | bytes 3932168 | tf_op jit(solution)/shard_map/ppermute | solution.py:887
  282.4 12.6 %collective-permute-start.37 = (bf16[640,256]{1,0:T(8,128)(2,1)S(1)}, bf16[640,256]{1,0:T(8,128)(2,1)S(1)}, u32[]{:S(2)}, u32[]{:S(2)}) collective-permute-start(bf16[640,256]{1,0:T(8,128)(2,1)S(1)} %get-tuple-element.129), channel_id=1, source_target_pairs={{0,4},{4,0},{8,12},{12,8},{16,20},{20,16},{24,28},{28,24},{1,5},{5... | collective-permute-start | bytes 983048 | tf_op jit(solution)/shard_map/ppermute | solution.py:887
  295.7 11.9 %collective-permute-start.38 = (bf16[640,256]{1,0:T(8,128)(2,1)S(1)}, bf16[640,256]{1,0:T(8,128)(2,1)S(1)}, u32[]{:S(2)}, u32[]{:S(2)}) collective-permute-start(bf16[640,256]{1,0:T(8,128)(2,1)S(1)} %far_sum.2), channel_id=1, source_target_pairs={{1,0},{3,2},{5,4},{7,6},{9,8},{11,10},{13,12},{15,14},{17,16},{19,... | collective-permute-start | bytes 983048 | tf_op jit(solution)/shard_map/ppermute | solution.py:935
  330.8 22.0 %collective-permute-start.48 = (bf16[256,2560]{1,0:T(8,128)(2,1)}, bf16[256,2560]{1,0:T(8,128)(2,1)S(1)}, u32[]{:S(2)}, u32[]{:S(2)}) collective-permute-start(bf16[256,2560]{1,0:T(8,128)(2,1)} %get-tuple-element.154), channel_id=1, source_target_pairs={{0,4},{4,0},{8,12},{12,8},{16,20},{20,16},{24,28},{28,24},{1,5},{5... | collective-permute-start | bytes 3932168 | tf_op jit(solution)/shard_map/ppermute | solution.py:887
  363.2 48.2 %collective-permute-start.50 = (bf16[2,960,640]{2,1,0:T(8,128)(2,1)S(1)}, bf16[2,960,640]{2,1,0:T(8,128)(2,1)}, u32[]{:S(2)}, u32[]{:S(2)}) collective-permute-start(bf16[2,960,640]{2,1,0:T(8,128)(2,1)S(1)} %get-tuple-element.155.rest_8_), channel_id=1, source_target_pairs={{0,8},{4,20},{8,0},{12,28},{16,24},{20,4},{24,16},{28,12},{1,9},{5... | collective-permute-start | bytes 7372808 | tf_op jit(solution)/shard_map/ppermute | solution.py:887
  364.3 10.4 %collective-permute-start.49 = (bf16[3,256,384]{2,1,0:T(8,128)(2,1)S(1)}, bf16[3,256,384]{2,1,0:T(8,128)(2,1)S(1)}, u32[]{:S(2)}, u32[]{:S(2)}) collective-permute-start(bf16[3,256,384]{2,1,0:T(8,128)(2,1)S(1)} %get-tuple-element.157), channel_id=1, source_target_pairs={{0,4},{4,0},{8,12},{12,8},{16,20},{20,16},{24,28},{28,24},{1,5},{5... | collective-permute-start | bytes 1769480 | tf_op jit(solution)/shard_map/ppermute | solution.py:887
  364.9 11.7 %collective-permute-start.45 = (bf16[640,256]{1,0:T(8,128)(2,1)S(1)}, bf16[640,256]{1,0:T(8,128)(2,1)S(1)}, u32[]{:S(2)}, u32[]{:S(2)}) collective-permute-start(bf16[640,256]{1,0:T(8,128)(2,1)S(1)} %far_sum.3.rest_8_), channel_id=1, source_target_pairs={{1,0},{3,2},{5,4},{7,6},{9,8},{11,10},{13,12},{15,14},{17,16},{19,... | collective-permute-start | bytes 983048 | tf_op jit(solution)/shard_map/ppermute | solution.py:935
  373.7 41.3 %collective-permute-start.54 = (bf16[960,640]{1,0:T(8,128)(2,1)}, bf16[960,640]{1,0:T(8,128)(2,1)}, u32[]{:S(2)}, u32[]{:S(2)}) collective-permute-start(bf16[960,640]{1,0:T(8,128)(2,1)} %get-tuple-element.173), channel_id=1, source_target_pairs={{0,1},{1,0},{2,3},{3,2},{4,5},{5,4},{6,7},{7,6},{8,9},{9,8},{10,11... | collective-permute-start | bytes 3686408 | tf_op jit(solution)/shard_map/ppermute | solution.py:893
  409.5 31.0 %collective-permute-start.53 = (bf16[2,960,384]{2,1,0:T(8,128)(2,1)S(1)}, bf16[2,960,384]{2,1,0:T(8,128)(2,1)S(1)}, u32[]{:S(2)}, u32[]{:S(2)}) collective-permute-start(bf16[2,960,384]{2,1,0:T(8,128)(2,1)S(1)} %get-tuple-element.169.rest_0_), channel_id=1, source_target_pairs={{0,8},{4,20},{8,0},{12,28},{16,24},{20,4},{24,16},{28,12},{1,9},{5... | collective-permute-start | bytes 4423688 | tf_op jit(solution)/shard_map/ppermute | solution.py:887
  413.7 32.3 %collective-permute-start.52 = (bf16[960,640]{1,0:T(8,128)(2,1)S(1)}, bf16[960,640]{1,0:T(8,128)(2,1)S(1)}, u32[]{:S(2)}, u32[]{:S(2)}) collective-permute-start(bf16[960,640]{1,0:T(8,128)(2,1)S(1)} %get-tuple-element.171.rest_0_), channel_id=1, source_target_pairs={{0,16},{4,12},{8,24},{12,4},{16,0},{20,28},{24,8},{28,20},{1,17},{... | collective-permute-start | bytes 3686408 | tf_op jit(solution)/shard_map/ppermute | solution.py:887
  416.6 45.7 %collective-permute-start.58 = (bf16[960,640]{1,0:T(8,128)(2,1)S(1)}, bf16[960,640]{1,0:T(8,128)(2,1)S(1)}, u32[]{:S(2)}, u32[]{:S(2)}) collective-permute-start(bf16[960,640]{1,0:T(8,128)(2,1)S(1)} %down_pair.1.rest_0_.own_ref), channel_id=1, source_target_pairs={{2,0},{3,1},{4,6},{5,7},{10,8},{11,9},{12,14},{13,15},{18,16},{19,... | collective-permute-start | bytes 3686408 | tf_op jit(solution)/shard_map/ppermute | solution.py:893
  441.3 14.1 %collective-permute-start.56 = (bf16[960,384]{1,0:T(8,128)(2,1)S(1)}, bf16[960,384]{1,0:T(8,128)(2,1)S(1)}, u32[]{:S(2)}, u32[]{:S(2)}) collective-permute-start(bf16[960,384]{1,0:T(8,128)(2,1)S(1)} %get-tuple-element.174.rest_0_), channel_id=1, source_target_pairs={{0,16},{4,12},{8,24},{12,4},{16,0},{20,28},{24,8},{28,20},{1,17},{... | collective-permute-start | bytes 2211848 | tf_op jit(solution)/shard_map/ppermute | solution.py:887
  447.0 14.6 %collective-permute-start.55 = (bf16[2,240,640]{2,1,0:T(8,128)(2,1)S(1)}, bf16[2,240,640]{2,1,0:T(8,128)(2,1)S(1)}, u32[]{:S(2)}, u32[]{:S(2)}) collective-permute-start(bf16[2,240,640]{2,1,0:T(8,128)(2,1)S(1)} %get-tuple-element.176.rest_0_), channel_id=1, source_target_pairs={{0,1},{1,0},{2,3},{3,2},{4,5},{5,4},{6,7},{7,6},{8,9},{9,8},{10,11... | collective-permute-start | bytes 1843208 | tf_op jit(solution)/shard_map/ppermute | solution.py:893
  463.1 18.3 %collective-permute-start.59 = (bf16[480,640]{1,0:T(8,128)(2,1)S(1)}, bf16[480,640]{1,0:T(8,128)(2,1)S(1)}, u32[]{:S(2)}, u32[]{:S(2)}) collective-permute-start(bf16[480,640]{1,0:T(8,128)(2,1)S(1)} %get-tuple-element.182.rest_0_), channel_id=1, source_target_pairs={{0,4},{4,0},{8,12},{12,8},{16,20},{20,16},{24,28},{28,24},{1,5},{5... | collective-permute-start | bytes 1843208 | tf_op jit(solution)/shard_map/ppermute | solution.py:887
  463.2 17.6 %collective-permute-start.60 = (bf16[2,240,384]{2,1,0:T(8,128)(2,1)S(1)}, bf16[2,240,384]{2,1,0:T(8,128)(2,1)S(1)}, u32[]{:S(2)}, u32[]{:S(2)}) collective-permute-start(bf16[2,240,384]{2,1,0:T(8,128)(2,1)S(1)} %get-tuple-element.178.rest_0_), channel_id=1, source_target_pairs={{0,1},{1,0},{2,3},{3,2},{4,5},{5,4},{6,7},{7,6},{8,9},{9,8},{10,11... | collective-permute-start | bytes 1105928 | tf_op jit(solution)/shard_map/ppermute | solution.py:893
  463.3 20.7 %collective-permute-start.57 = (bf16[240,640]{1,0:T(8,128)(2,1)S(1)}, bf16[240,640]{1,0:T(8,128)(2,1)S(1)}, u32[]{:S(2)}, u32[]{:S(2)}) collective-permute-start(bf16[240,640]{1,0:T(8,128)(2,1)S(1)} %get-tuple-element.180.rest_0_), channel_id=1, source_target_pairs={{0,2},{1,3},{2,0},{3,1},{4,6},{5,7},{6,4},{7,5},{8,10},{9,11},{10,... | collective-permute-start | bytes 921608 | tf_op jit(solution)/shard_map/ppermute | solution.py:893
  482.2 9.1 %collective-permute-start.63 = (bf16[2,120,640]{2,1,0:T(8,128)(2,1)S(1)}, bf16[2,120,640]{2,1,0:T(8,128)(2,1)S(1)}, u32[]{:S(2)}, u32[]{:S(2)}) collective-permute-start(bf16[2,120,640]{2,1,0:T(8,128)(2,1)S(1)} %get-tuple-element.185.rest_0_), channel_id=1, source_target_pairs={{0,8},{4,20},{8,0},{12,28},{16,24},{20,4},{24,16},{28,12},{1,9},{5... | collective-permute-start | bytes 921608 | tf_op jit(solution)/shard_map/ppermute | solution.py:887
  484.6 15.9 %collective-permute-start.74 = (bf16[240,640]{1,0:T(8,128)(2,1)S(1)}, bf16[240,640]{1,0:T(8,128)(2,1)S(1)}, u32[]{:S(2)}, u32[]{:S(2)}) collective-permute-start(bf16[240,640]{1,0:T(8,128)(2,1)S(1)} %sum_two.3.refs_1_.rest_0_), channel_id=1, source_target_pairs={{0,4},{4,0},{8,12},{12,8},{16,20},{20,16},{24,28},{28,24},{1,5},{5... | collective-permute-start | bytes 921608 | tf_op jit(solution)/shard_map/ppermute | solution.py:887
  484.7 15.9 %collective-permute-start.73 = (bf16[240,640]{1,0:T(8,128)(2,1)S(1)}, bf16[240,640]{1,0:T(8,128)(2,1)S(1)}, u32[]{:S(2)}, u32[]{:S(2)}) collective-permute-start(bf16[240,640]{1,0:T(8,128)(2,1)S(1)} %sum_two.3.refs_1_.rest_0_), channel_id=1, source_target_pairs={{0,24},{4,28},{8,16},{12,20},{16,8},{20,12},{24,0},{28,4},{1,25},{... | collective-permute-start | bytes 921608 | tf_op jit(solution)/shard_map/ppermute | solution.py:887
  485.9 16.2 %collective-permute-start.72 = (bf16[240,640]{1,0:T(8,128)(2,1)S(1)}, bf16[240,640]{1,0:T(8,128)(2,1)S(1)}, u32[]{:S(2)}, u32[]{:S(2)}) collective-permute-start(bf16[240,640]{1,0:T(8,128)(2,1)S(1)} %sum_two.3.refs_1_.rest_0_), channel_id=1, source_target_pairs={{0,16},{4,12},{8,24},{12,4},{16,0},{20,28},{24,8},{28,20},{1,17},{... | collective-permute-start | bytes 921608 | tf_op jit(solution)/shard_map/ppermute | solution.py:887
  486.5 16.9 %collective-permute-start.71 = (bf16[240,640]{1,0:T(8,128)(2,1)S(1)}, bf16[240,640]{1,0:T(8,128)(2,1)S(1)}, u32[]{:S(2)}, u32[]{:S(2)}) collective-permute-start(bf16[240,640]{1,0:T(8,128)(2,1)S(1)} %sum_two.3.refs_1_.rest_0_), channel_id=1, source_target_pairs={{0,8},{4,20},{8,0},{12,28},{16,24},{20,4},{24,16},{28,12},{1,9},{5... | collective-permute-start | bytes 921608 | tf_op jit(solution)/shard_map/ppermute | solution.py:887
  491.3 7.9 %collective-permute-start.62 = (bf16[240,384]{1,0:T(8,128)(2,1)S(1)}, bf16[240,384]{1,0:T(8,128)(2,1)S(1)}, u32[]{:S(2)}, u32[]{:S(2)}) collective-permute-start(bf16[240,384]{1,0:T(8,128)(2,1)S(1)} %get-tuple-element.184.rest_0_), channel_id=1, source_target_pairs={{0,2},{1,3},{2,0},{3,1},{4,6},{5,7},{6,4},{7,5},{8,10},{9,11},{10,... | collective-permute-start | bytes 552968 | tf_op jit(solution)/shard_map/ppermute | solution.py:893
  499.2 19.2 %collective-permute-start.61 = (bf16[960,256]{1,0:T(8,128)(2,1)S(1)}, bf16[960,256]{1,0:T(8,128)(2,1)S(1)}, u32[]{:S(2)}, u32[]{:S(2)}) collective-permute-start(bf16[960,256]{1,0:T(8,128)(2,1)S(1)} %hold.5), channel_id=1, source_target_pairs={{0,0},{4,1},{1,2},{5,3},{2,4},{6,5},{3,6},{7,7},{8,8},{12,9},{9,10... | collective-permute-start | bytes 1474568 | tf_op jit(solution)/shard_map/ppermute | solution.py:904
  500.5 13.0 %collective-permute-start.67 = (bf16[240,384]{1,0:T(8,128)(2,1)S(1)}, bf16[240,384]{1,0:T(8,128)(2,1)S(1)}, u32[]{:S(2)}, u32[]{:S(2)}) collective-permute-start(bf16[240,384]{1,0:T(8,128)(2,1)S(1)} %sum_two.4.rest_0_), channel_id=1, source_target_pairs={{0,4},{4,0},{8,12},{12,8},{16,20},{20,16},{24,28},{28,24},{1,5},{5... | collective-permute-start | bytes 552968 | tf_op jit(solution)/shard_map/ppermute | solution.py:887
  500.5 13.0 %collective-permute-start.66 = (bf16[240,384]{1,0:T(8,128)(2,1)S(1)}, bf16[240,384]{1,0:T(8,128)(2,1)S(1)}, u32[]{:S(2)}, u32[]{:S(2)}) collective-permute-start(bf16[240,384]{1,0:T(8,128)(2,1)S(1)} %sum_two.4.rest_0_), channel_id=1, source_target_pairs={{0,24},{4,28},{8,16},{12,20},{16,8},{20,12},{24,0},{28,4},{1,25},{... | collective-permute-start | bytes 552968 | tf_op jit(solution)/shard_map/ppermute | solution.py:887
  502.0 12.0 %collective-permute-start.65 = (bf16[240,384]{1,0:T(8,128)(2,1)S(1)}, bf16[240,384]{1,0:T(8,128)(2,1)S(1)}, u32[]{:S(2)}, u32[]{:S(2)}) collective-permute-start(bf16[240,384]{1,0:T(8,128)(2,1)S(1)} %sum_two.4.rest_0_), channel_id=1, source_target_pairs={{0,16},{4,12},{8,24},{12,4},{16,0},{20,28},{24,8},{28,20},{1,17},{... | collective-permute-start | bytes 552968 | tf_op jit(solution)/shard_map/ppermute | solution.py:887
  503.5 8.7 %collective-permute-start.78 = (bf16[120,640]{1,0:T(8,128)(2,1)S(1)}, bf16[120,640]{1,0:T(8,128)(2,1)S(1)}, u32[]{:S(2)}, u32[]{:S(2)}) collective-permute-start(bf16[120,640]{1,0:T(8,128)(2,1)S(1)} %get-tuple-element.188.rest_0_), channel_id=1, source_target_pairs={{0,16},{4,12},{8,24},{12,4},{16,0},{20,28},{24,8},{28,20},{1,17},{... | collective-permute-start | bytes 460808 | tf_op jit(solution)/shard_map/ppermute | solution.py:887
  513.5 7.7 %collective-permute-start.76 = (bf16[240,640]{1,0:T(8,128)(2,1)S(1)}, bf16[240,640]{1,0:T(8,128)(2,1)S(1)}, u32[]{:S(2)}, u32[]{:S(2)}) collective-permute-start(bf16[240,640]{1,0:T(8,128)(2,1)S(1)} %collective-permute-done.72.rest_2_), channel_id=1, source_target_pairs={{0,4},{4,0},{8,12},{12,8},{16,20},{20,16},{24,28},{28,24},{1,5},{5... | collective-permute-start | bytes 921608 | tf_op jit(solution)/shard_map/ppermute | solution.py:887
  514.0 7.1 %collective-permute-start.75 = (bf16[240,640]{1,0:T(8,128)(2,1)S(1)}, bf16[240,640]{1,0:T(8,128)(2,1)S(1)}, u32[]{:S(2)}, u32[]{:S(2)}) collective-permute-start(bf16[240,640]{1,0:T(8,128)(2,1)S(1)} %collective-permute-done.71.rest_1_), channel_id=1, source_target_pairs={{0,4},{4,0},{8,12},{12,8},{16,20},{20,16},{24,28},{28,24},{1,5},{5... | collective-permute-start | bytes 921608 | tf_op jit(solution)/shard_map/ppermute | solution.py:887
  517.7 7.6 %collective-permute-start.81 = (bf16[120,640]{1,0:T(8,128)(2,1)S(1)}, bf16[120,640]{1,0:T(8,128)(2,1)S(1)}, u32[]{:S(2)}, u32[]{:S(2)}) collective-permute-start(bf16[120,640]{1,0:T(8,128)(2,1)S(1)} %sum_two.5.rest_8_.rest_0_), channel_id=1, source_target_pairs={{0,24},{4,28},{8,16},{12,20},{16,8},{20,12},{24,0},{28,4},{1,25},{... | collective-permute-start | bytes 460808 | tf_op jit(solution)/shard_map/ppermute | solution.py:887
  518.4 11.0 %collective-permute-start.80 = (bf16[120,640]{1,0:T(8,128)(2,1)S(1)}, bf16[120,640]{1,0:T(8,128)(2,1)S(1)}, u32[]{:S(2)}, u32[]{:S(2)}) collective-permute-start(bf16[120,640]{1,0:T(8,128)(2,1)S(1)} %sum_two.5.rest_8_.rest_0_), channel_id=1, source_target_pairs={{0,16},{4,12},{8,24},{12,4},{16,0},{20,28},{24,8},{28,20},{1,17},{... | collective-permute-start | bytes 460808 | tf_op jit(solution)/shard_map/ppermute | solution.py:887
  520.5 9.4 %collective-permute-start.79 = (bf16[120,640]{1,0:T(8,128)(2,1)S(1)}, bf16[120,640]{1,0:T(8,128)(2,1)S(1)}, u32[]{:S(2)}, u32[]{:S(2)}) collective-permute-start(bf16[120,640]{1,0:T(8,128)(2,1)S(1)} %sum_two.5.rest_8_.rest_0_), channel_id=1, source_target_pairs={{0,8},{4,20},{8,0},{12,28},{16,24},{20,4},{24,16},{28,12},{1,9},{5... | collective-permute-start | bytes 460808 | tf_op jit(solution)/shard_map/ppermute | solution.py:887
  521.2 8.8 %collective-permute-start.70 = (bf16[240,384]{1,0:T(8,128)(2,1)S(1)}, bf16[240,384]{1,0:T(8,128)(2,1)S(1)}, u32[]{:S(2)}, u32[]{:S(2)}) collective-permute-start(bf16[240,384]{1,0:T(8,128)(2,1)S(1)} %collective-permute-done.66.rest_3_), channel_id=1, source_target_pairs={{0,4},{4,0},{8,12},{12,8},{16,20},{20,16},{24,28},{28,24},{1,5},{5... | collective-permute-start | bytes 552968 | tf_op jit(solution)/shard_map/ppermute | solution.py:887
  521.2 9.3 %collective-permute-start.69 = (bf16[240,384]{1,0:T(8,128)(2,1)S(1)}, bf16[240,384]{1,0:T(8,128)(2,1)S(1)}, u32[]{:S(2)}, u32[]{:S(2)}) collective-permute-start(bf16[240,384]{1,0:T(8,128)(2,1)S(1)} %collective-permute-done.65.rest_2_), channel_id=1, source_target_pairs={{0,4},{4,0},{8,12},{12,8},{16,20},{20,16},{24,28},{28,24},{1,5},{5... | collective-permute-start | bytes 552968 | tf_op jit(solution)/shard_map/ppermute | solution.py:887
  529.4 7.5 %collective-permute-start.82 = (bf16[120,640]{1,0:T(8,128)(2,1)S(1)}, bf16[120,640]{1,0:T(8,128)(2,1)S(1)}, u32[]{:S(2)}, u32[]{:S(2)}) collective-permute-start(bf16[120,640]{1,0:T(8,128)(2,1)S(1)} %sum_two.5.rest_8_.rest_0_), channel_id=1, source_target_pairs={{0,4},{4,0},{8,12},{12,8},{16,20},{20,16},{24,28},{28,24},{1,5},{5... | collective-permute-start | bytes 460808 | tf_op jit(solution)/shard_map/ppermute | solution.py:887
  (140 other events, 1484.2 us)

commit v8 on v7

--- a/solution.py
+++ b/solution.py
@@ -506,7 +506,7 @@
         out_specs=(WHOLE,) * 2,
         scratch_shapes=[pltpu.VMEM((width, 4 * n), bf16), pltpu.VMEM((4 * n, cols), bf16)],
         cost_estimate=BRIEF,
-        compiler_params=pltpu.CompilerParams(vmem_limit_bytes=36 << 20),
+        compiler_params=pltpu.CompilerParams(vmem_limit_bytes=LIMIT),
         name="grad_ffn",
     )(sc, *lefts, *rights, *after)
 
@@ -533,7 +533,7 @@
         out_specs=(WHOLE,) * 2,
         scratch_shapes=[pltpu.VMEM((width, 4 * n), bf16), pltpu.VMEM((4 * n, cols), bf16)],
         cost_estimate=BRIEF,
-        compiler_params=pltpu.CompilerParams(vmem_limit_bytes=32 << 20),
+        compiler_params=pltpu.CompilerParams(vmem_limit_bytes=LIMIT),
         name="grad_down",
     )(sc, *lefts, *rights, *after)
 
@@ -584,7 +584,7 @@
         out_specs=(WHOLE,) * 2,
         scratch_shapes=[pltpu.VMEM((2, width, 4 * n), bf16), pltpu.VMEM((4, 4 * n, PIECE), bf16)],
         cost_estimate=BRIEF,
-        compiler_params=pltpu.CompilerParams(vmem_limit_bytes=36 << 20),
+        compiler_params=pltpu.CompilerParams(vmem_limit_bytes=LIMIT),
         name="grad_attention",
     )(sc, *a, *o, *own, *got, *gains, *after)
 
@@ -967,21 +967,22 @@
     ids = jnp.broadcast_to((segment_ids[0] + 1).astype(bf16), (IDS, stretch))
     tokens = home_to_work(jnp.concatenate([tokens[0].T, ids]))
     piece_b = pick(sc, gate_weight, up_weight, parts_a[1:2])
-    parts_b = turns(piece_b)
     whole_a = stack(sc, parts_a, [piece_b])
     gains = gains_of(whole_a)
     gain_a, gain_f = gains[:1], gains[1:]
     wa = plane_gather(whole_a.reshape(depth * rows, PIECE))
-    whole_b = stack(sc, parts_b, [wa[0][1], wa[0][2]]).reshape(depth * rows, piece_b.shape[1])
+    far_b = hold(flip_z(piece_b, 2), [wa[0][1], wa[0][2]])
+    parts_b = piece_b, flip_z(piece_b, 1), far_b, flip_z(far_b, 1)
+    whole_b = stack(sc, parts_b).reshape(depth * rows, piece_b.shape[1])
     wb = plane_gather(whole_b)
     piece_d = pick_down(sc, down_weight.T, [whole_b])
 
-    h_0, a0, q0, own = pre(sc, tokens, gain_a, cos, sin, *wa, [wb[0][1], wb[0][2], piece_d])
+    h_0, a0, q0, own = pre(sc, tokens, gain_a, cos, sin, *wa, [whole_b, piece_d])
     kv0 = window(own)
-    far_d = hold(flip_z(piece_d, 2), [kv0[1], wb[0][3]])
+    o0, lse0 = attend(q0, kv0, [wb[0][1], wb[0][2]])
+    far_d = hold(flip_z(piece_d, 2), [o0])
     parts_d = piece_d, flip_z(piece_d, 1), far_d, flip_z(far_d, 1)
-    o0, lse0 = attend(q0, kv0)
-    whole_d = stack(sc, parts_d, [o0])
+    whole_d = stack(sc, parts_d)
     weights = wa, wb, (whole_d, flip(whole_d, CORE))
     mixed0, h1_0, b0, gate0, up0, z0, h_1, a1, q1, own = post(False, sc, o0, h_0, gain_f, gain_a, cos, sin, own, *weights)
     kv1 = window(own)
@@ -994,11 +995,11 @@
 
     gb1, act1, away1, zk1, zs1, g1, p1, dgain_f1, do = back(True, False, sc, weights, [cot], [gate1, up1, h1_1, gain_f, z1])
     across_2 = across((gb1, away1, zs1))
-    dq1, three1, far, near, own = attend_back(sc, p1, q1, kv1, lse1, do, cos, sin, [output, *across_1])
+    dq1, three1, far, near, own = attend_back(sc, p1, q1, kv1, lse1, do, cos, sin, [*across_1])
     near, _, far = unwindow(sc, far, near)
     (three1,) = across((three1,))
     tail = [g1, dq1, own, near, far, h_1, gain_a, cos, sin]
-    dk1, dv1, one1, dgain_a1, gb0, act0, away0, zk0, zs0, g1, p0, dgain_f0, do = back(False, False, sc, weights, tail, [gate0, up0, h1_0, gain_f, z0], [three1, *across_2])
+    dk1, dv1, one1, dgain_a1, gb0, act0, away0, zk0, zs0, g1, p0, dgain_f0, do = back(False, False, sc, weights, tail, [gate0, up0, h1_0, gain_f, z0], [output, three1, *across_2])
 
     away0, gb0_, zs0, one1 = across((away0, gb0, zs0, one1))
     dq0, three0, far, near, own = attend_back(sc, p0, q0, kv0, lse0, do, cos, sin, [one1])

time: 547 us -> 525 us (0.960)
  starting transfers between devices: 99.4 us -> 73.6 us
  local copies, waits for them, and re-layouts: 48.9 us -> 37.3 us
  waiting for transfers between devices: 199 us -> 208 us
  Pallas kernels: 187 us -> 195 us
    ppermute x63, starting transfers between devices: 65.2 us -> 37.9 us  [flip(): lax.ppermute(value, 'dp', [(i, i ^ bits[i & 1]) for i in range(count)])]
    unnamed x240 -> x200, local copies, waits for them, and re-layouts: 46.4 us -> 34.8 us
    ppermute x2, waiting for transfers between devices: 11.7 us -> 19.4 us  [unwindow(): lax.ppermute(far, 'fsdp', [(z + 1, z) for z in range(0, depth, 2)])]
    ppermute x63, waiting for transfers between devices: 89.1 us -> 83 us  [flip(): lax.ppermute(value, 'dp', [(i, i ^ bits[i & 1]) for i in range(count)])]
  transfers between devices with their start and end apart: 86 -> 86, of which waited for: 37 -> 30; matrix products, arithmetic and copies ran while one was open for 1% -> 1% of each run, Pallas kernels for 18% -> 24%
where the time goes in v8:
time: 525 us; the launch traced here: 520 us
  waiting for transfers between devices  208 us (40%)
  Pallas kernels  195 us (37%)
  starting transfers between devices  73.6 us (14%)
  local copies, waits for them, and re-layouts  37.3 us (7%)
    ppermute x15, waiting for transfers between devices, flip_z(): return lax.ppermute(value, ('dp', 'fsdp'), pairs)  91.2 us
    ppermute x63, waiting for transfers between devices, flip(): lax.ppermute(value, 'dp', [(i, i ^ bits[i & 1]) for i in range(count)])  83 us
    pallas_call x3, Pallas kernels, back(): pl.pallas_call(functools.partial(back_kernel, start, end, len(after)), ou...  50.2 us
    pallas_call x2, Pallas kernels, post(): pl.pallas_call(functools.partial(post_kernel, last), out_shape=tuple(outs...  38 us
    ppermute x63, starting transfers between devices, flip(): lax.ppermute(value, 'dp', [(i, i ^ bits[i & 1]) for i in range(count)])  37.9 us
    unnamed x200, local copies, waits for them, and re-layouts  34.8 us
    pallas_call x2, Pallas kernels, attend_back(): pl.pallas_call(attend_back_kernel, out_shape=(shape((3, n, PIECE), bf16),...  25.6 us
    pallas_call x2, Pallas kernels, attend(): pl.pallas_call(attend_kernel, out_shape=(shape((width, n), bf16), shape((...  20.3 us
  transfers between devices with their start and end apart: 86, of which 30 were waited for; matrix products, arithmetic and copies ran while one was open for 1% of the time, Pallas kernels for 24%

profile of v8, /device:TPU:0, one launch (start us, length us, event | category | flops | bytes accessed | tf_op | source)
XLA Modules:
  0.0 519.9 jit_solution(2484373364622690159)
XLA Ops:
  0.7 2.0 copy.35
  8.8 4.1 collective-permute-start.2
  12.9 1.6 collective-permute-start.1
  14.5 7.2 %collective-permute-done.2.rest_2_ = bf16[240,384]{1,0:T(8,128)(2,1)S(1)} collective-permute-done((bf16[240,384]{1,0:T(8,128)(2,1)S(1)}, bf16[240,384]{1,0:T(8,128)(2,1)S(1)}, u32[]{:S(2)}, u32[]{:S(2)}) %collective-permute-start.2) | collective-permute-done | bytes 184352 | tf_op jit(solution)/shard_map/ppermute | solution.py:893
  22.9 4.6 collective-permute-done.3.rest_3_
  27.4 1.5 stack.31.first_ref
  30.3 1.5 collective-permute-start.5
  31.8 16.7 %collective-permute-done.4.refs_1_.rest_1_ = bf16[960,384]{1,0:T(8,128)(2,1)S(1)} collective-permute-done((bf16[960,384]{1,0:T(8,128)(2,1)S(1)}, bf16[960,384]{1,0:T(8,128)(2,1)S(1)}, u32[]{:S(2)}, u32[]{:S(2)}) %collective-permute-start.4) | collective-permute-done | bytes 737312 | tf_op jit(solution)/shard_map/ppermute | solution.py:887
  49.0 2.7 collective-permute-start.12
  51.7 1.7 collective-permute-start.11
  53.4 9.8 %collective-permute-done.12.refs_0_ = bf16[240,640]{1,0:T(8,128)(2,1)S(1)} collective-permute-done((bf16[240,640]{1,0:T(8,128)(2,1)S(1)}, bf16[240,640]{1,0:T(8,128)(2,1)S(1)}, u32[]{:S(2)}, u32[]{:S(2)}) %collective-permute-start.12) | collective-permute-done | bytes 307232 | tf_op jit(solution)/shard_map/ppermute | solution.py:893
  64.4 5.3 %collective-permute-start = (bf16[976,256]{1,0:T(8,128)(2,1)}, bf16[976,256]{1,0:T(8,128)(2,1)}, u32[]{:S(2)}, u32[]{:S(2)}) collective-permute-start(bf16[976,256]{1,0:T(8,128)(2,1)} %pad_maximum_fusion), channel_id=1, source_target_pairs={{0,0},{1,4},{2,1},{3,5},{4,2},{5,6},{6,3},{7,7},{8,8},{9,12},{10,9... | collective-permute-start | bytes 1499144 | tf_op jit(solution)/shard_map/ppermute | solution.py:904
  70.6 2.7 collective-permute-done.13.rest_3_
  84.7 6.8 %pre.1 = (bf16[256,960]{1,0:T(8,128)(2,1)}, bf16[256,960]{1,0:T(8,128)(2,1)}, bf16[960,256]{1,0:T(8,128)(2,1)}, bf16[656,256]{1,0:T(8,128)(2,1)}) custom-call(s32[3]{0:T(128)} %copy-done.52, bf16[976,256]{1,0:T(8,128)(2,1)} %collective-permute-done.ht_ref, f32[1,960]{1,0:T(1,128)} %get-tuple-element.209.gain_ref.gain_a.rest_24_.rest_14_, ...), custom_call_target="tpu_custom_call" | custom-call | flops 1024 | bytes 1024 | tf_op jit(solution)/shard_map/pre/pallas_call | solution.py:118
  91.6 5.8 %collective-permute-start.14 = (bf16[656,256]{1,0:T(8,128)(2,1)}, bf16[656,256]{1,0:T(8,128)(2,1)S(1)}, u32[]{:S(2)}, u32[]{:S(2)}) collective-permute-start(bf16[656,256]{1,0:T(8,128)(2,1)} %get-tuple-element.105.kv2.rest_18_), channel_id=1, source_target_pairs={{0,1},{2,3},{4,5},{6,7},{8,9},{10,11},{12,13},{14,15},{16,17},{18,... | collective-permute-start | bytes 1007624 | tf_op jit(solution)/shard_map/ppermute | solution.py:926
  97.9 7.9 %collective-permute-done.14.kv0 = bf16[656,256]{1,0:T(8,128)(2,1)S(1)} collective-permute-done((bf16[656,256]{1,0:T(8,128)(2,1)}, bf16[656,256]{1,0:T(8,128)(2,1)S(1)}, u32[]{:S(2)}, u32[]{:S(2)}) %collective-permute-start.14) | collective-permute-done | bytes 335904 | tf_op jit(solution)/shard_map/ppermute | solution.py:926
  106.9 2.4 collective-permute-start.23
  110.5 10.1 %attend.2 = (bf16[960,256]{1,0:T(8,128)(2,1)S(1)}, f32[15,256]{1,0:T(8,128)S(1)}) custom-call(bf16[960,256]{1,0:T(8,128)(2,1)S(1)} %copy-done.31, bf16[656,256]{1,0:T(8,128)(2,1)S(1)} %collective-permute-done.14.kv0, bf16[656,256]{1,0:T(8,128)(2,1)S(1)} %collective-permute-done.15.kv1, bf16[656,256]{1,0:T(8,128)(2,1)S(1)} %copy-done.10, ...), custom_call_target="tpu_custom_call" | custom-call | flops 1024 | bytes 1024 | tf_op jit(solution)/shard_map/attend/pallas_call | solution.py:171
  120.6 3.8 collective-permute-done.24.refs_0_
  124.5 12.6 %collective-permute-done.23.rest_1_ = bf16[480,640]{1,0:T(8,128)(2,1)S(1)} collective-permute-done((bf16[480,640]{1,0:T(8,128)(2,1)S(1)}, bf16[480,640]{1,0:T(8,128)(2,1)S(1)}, u32[]{:S(2)}, u32[]{:S(2)}) %collective-permute-start.23) | collective-permute-done | bytes 614432 | tf_op jit(solution)/shard_map/ppermute | solution.py:893
  137.1 12.9 %collective-permute-done.25.rest_3_ = bf16[480,640]{1,0:T(8,128)(2,1)S(1)} collective-permute-done((bf16[480,640]{1,0:T(8,128)(2,1)S(1)}, bf16[480,640]{1,0:T(8,128)(2,1)S(1)}, u32[]{:S(2)}, u32[]{:S(2)}) %collective-permute-start.25) | collective-permute-done | bytes 614432 | tf_op jit(solution)/shard_map/ppermute | solution.py:893
  152.4 7.1 %collective-permute-done.19.rest_12_ = bf16[960,640]{1,0:T(8,128)(2,1)S(1)} collective-permute-done((bf16[960,640]{1,0:T(8,128)(2,1)S(1)}, bf16[960,640]{1,0:T(8,128)(2,1)S(1)}, u32[]{:S(2)}, u32[]{:S(2)}) %collective-permute-start.19) | collective-permute-done | bytes 1228832 | tf_op jit(solution)/shard_map/ppermute | solution.py:887
  159.7 3.5 collective-permute-done.21.rest_14_
  165.5 20.3 %post.2 = (bf16[256,960]{1,0:T(8,128)(2,1)}, f32[256,960]{1,0:T(8,128)}, bf16[256,960]{1,0:T(8,128)(2,1)}, bf16[256,2560]{1,0:T(8,128)(2,1)}, bf16[256,2560]{1,0...) custom-call(s32[3]{0:T(128)} %copy-done.52, ...), custom_call_target="tpu_custom_call" | custom-call | flops 1024 | bytes 1024 | tf_op jit(solution)/shard_map/post/pallas_call | solution.py:305
  185.8 1.6 collective-permute-start.27
  188.1 6.0 %collective-permute-done.27.kv0 = bf16[656,256]{1,0:T(8,128)(2,1)S(1)} collective-permute-done((bf16[656,256]{1,0:T(8,128)(2,1)}, bf16[656,256]{1,0:T(8,128)(2,1)S(1)}, u32[]{:S(2)}, u32[]{:S(2)}) %collective-permute-start.27) | collective-permute-done | bytes 335904 | tf_op jit(solution)/shard_map/ppermute | solution.py:926
  195.2 1.6 collective-permute-done.28.kv1
  197.8 10.1 %attend.3 = (bf16[960,256]{1,0:T(8,128)(2,1)S(1)}, f32[15,256]{1,0:T(8,128)S(1)}) custom-call(bf16[960,256]{1,0:T(8,128)(2,1)S(1)} %copy-done.34, bf16[656,256]{1,0:T(8,128)(2,1)S(1)} %collective-permute-done.27.kv0, bf16[656,256]{1,0:T(8,128)(2,1)S(1)} %collective-permute-done.28.kv1, bf16[656,256]{1,0:T(8,128)(2,1)S(1)} %copy-done.8, ...), custom_call_target="tpu_custom_call" | custom-call | flops 1024 | bytes 1024 | tf_op jit(solution)/shard_map/attend/pallas_call | solution.py:171
  209.2 3.0 collective-permute-start.34
  212.2 17.8 %post.3 = (bf16[256,960]{1,0:T(8,128)(2,1)}, f32[256,960]{1,0:T(8,128)}, bf16[256,960]{1,0:T(8,128)(2,1)}, bf16[256,2560]{1,0:T(8,128)(2,1)}, bf16[256,2560]{1,0...) custom-call(s32[3]{0:T(128)} %copy-done.52, bf16[960,256]{1,0:T(8,128)(2,1)} %copy-done.35, ...), custom_call_target="tpu_custom_call" | custom-call | flops 1024 | bytes 1024 | tf_op jit(solution)/shard_map/post/pallas_call | solution.py:305
  231.3 21.7 %back_start.1 = (bf16[256,960]{1,0:T(8,128)(2,1)}, bf16[256,2560]{1,0:T(8,128)(2,1)}, bf16[256,2560]{1,0:T(8,128)(2,1)}, bf16[256,1280]{1,0:T(8,128)(2,1)}, bf16...) custom-call(s32[3]{0:T(128)} %copy-done.52, ...), custom_call_target="tpu_custom_call" | custom-call | flops 1024 | bytes 1024 | tf_op jit(solution)/shard_map/back_start/pallas_call | solution.py:461
  253.2 1.5 copy-done.17
  255.8 12.6 %attend_back.2 = (bf16[3,256,384]{2,1,0:T(8,128)(2,1)S(1)}, bf16[3,256,384]{2,1,0:T(8,128)(2,1)S(1)}, f32[640,256]{1,0:T(8,128)S(1)}, bf16[640,256]{1,0:T(8,128)(2,1)S(1)}, f32[640,256]{1,0:T(8,128)S(1)}) custom-call(s32[3]{0:T(128)S(1)} %copy-done.54, bf16[3,256,384]{2,1,0:T(8,128)(2,1)S(1)} %copy-done.17, bf16[960,256]{1,0:T(8,128)(2,1)S(1)} %copy-done.34, ...), custom_call_target="tpu_custom_call" | custom-call | flops 1024 | bytes 1024 | tf_op jit(solution)/shard_map/attend_back/pallas_call | solution.py:224
  270.4 2.2 collective-permute-start.42
  276.0 19.1 %collective-permute-done.38.rest_22_ = bf16[640,256]{1,0:T(8,128)(2,1)S(1)} collective-permute-done((bf16[640,256]{1,0:T(8,128)(2,1)S(1)}, bf16[640,256]{1,0:T(8,128)(2,1)S(1)}, u32[]{:S(2)}, u32[]{:S(2)}) %collective-permute-start.38) | collective-permute-done | bytes 327712 | tf_op jit(solution)/shard_map/ppermute | solution.py:935
  296.4 22.1 %back_join.1 = (bf16[256,384]{1,0:T(8,128)(2,1)}, bf16[256,384]{1,0:T(8,128)(2,1)}, bf16[256,384]{1,0:T(8,128)(2,1)}, f32[1,960]{1,0:T(1,128)}, bf16[256,960]{1,...) custom-call(s32[3]{0:T(128)} %copy-done.52, ...), custom_call_target="tpu_custom_call" | custom-call | flops 1024 | bytes 1024 | tf_op jit(solution)/shard_map/back_join/pallas_call | solution.py:461
  319.4 3.1 collective-permute-done.43.rest_0_.rest_18_
  324.6 13.0 %attend_back.3 = (bf16[3,256,384]{2,1,0:T(8,128)(2,1)S(1)}, bf16[3,256,384]{2,1,0:T(8,128)(2,1)S(1)}, f32[640,256]{1,0:T(8,128)S(1)}, bf16[640,256]{1,0:T(8,128)(2,1)S(1)}, f32[640,256]{1,0:T(8,128)S(1)}) custom-call(s32[3]{0:T(128)S(1)} %copy-done.55, bf16[3,256,384]{2,1,0:T(8,128)(2,1)S(1)} %copy-done.18, bf16[960,256]{1,0:T(8,128)(2,1)S(1)} %copy-done.32, ...), custom_call_target="tpu_custom_call" | custom-call | flops 1024 | bytes 1024 | tf_op jit(solution)/shard_map/attend_back/pallas_call | solution.py:224
  342.5 11.0 %grad_ffn.1 = (bf16[2,960,640]{2,1,0:T(8,128)(2,1)}, bf16[2,960,640]{2,1,0:T(8,128)(2,1)}) custom-call(s32[3]{0:T(128)} %copy-done.52, bf16[256,960]{1,0:T(8,128)(2,1)} %get-tuple-element.125.rest_0_, bf16[256,960]{1,0:T(8,128)(2,1)} %get-tuple-element.111.rest_1_, bf16[256,960]{1,0:T(8,128)(2,1)} %copy-done.25, bf16[256,960]{1,0:T(8,128)(2,1)} %copy-done.26, ...), custom_call_target="tpu_custom_call" | custom-call | flops 1024 | bytes 1024 | tf_op jit(solution)/shard_map/grad_ffn/pallas_call | solution.py:502
  353.6 2.2 collective-permute-start.50
  357.6 1.9 collective-permute-done.46.rest_3_
  360.5 6.7 %grad_down.1 = (bf16[960,640]{1,0:T(8,128)(2,1)}, bf16[960,640]{1,0:T(8,128)(2,1)}) custom-call(s32[3]{0:T(128)} %copy-done.52, bf16[256,960]{1,0:T(8,128)(2,1)} %get-tuple-element.136.rest_0_, bf16[256,960]{1,0:T(8,128)(2,1)} %get-tuple-element.148.rest_1_, bf16[256,960]{1,0:T(8,128)(2,1)} %copy-done.80, bf16[256,960]{1,0:T(8,128)(2,1)} %copy-done.87, ...), custom_call_target="tpu_custom_call" | custom-call | flops 1024 | bytes 1024 | tf_op jit(solution)/shard_map/grad_down/pallas_call | solution.py:529
  369.0 6.4 %back_end.1 = (bf16[256,384]{1,0:T(8,128)(2,1)}, bf16[256,384]{1,0:T(8,128)(2,1)}, bf16[256,384]{1,0:T(8,128)(2,1)}, f32[1,960]{1,0:T(1,128)}, bf16[960,256]{1,0:T(8,128)(2,1)}) custom-call(s32[3]{0:T(128)} %copy-done.52, bf16[960,384]{1,0:T(8,128)(2,1)} %bitcast.41, bf16[960,384]{1,0:T(8,128)(2,1)} %copy-done.4, bf16[960,384]{1,0:T(8,128)(2,1)} %copy-done.5, ...), custom_call_target="tpu_custom_call" | custom-call | flops 1024 | bytes 1024 | tf_op jit(solution)/shard_map/back_end/pallas_call | solution.py:461
  378.2 10.7 %grad_attention.1 = (bf16[2,960,384]{2,1,0:T(8,128)(2,1)}, bf16[2,960,384]{2,1,0:T(8,128)(2,1)}) custom-call(s32[3]{0:T(128)} %copy-done.52, bf16[256,960]{1,0:T(8,128)(2,1)} %get-tuple-element.124.rest_0_, bf16[256,960]{1,0:T(8,128)(2,1)} %get-tuple-element.110.rest_1_, bf16[256,960]{1,0:T(8,128)(2,1)} %copy-done.21, bf16[256,960]{1,0:T(8,128)(2,1)} %copy-done.23, ...), custom_call_target="tpu_custom_call" | custom-call | flops 1024 | bytes 1024 | tf_op jit(solution)/shard_map/grad_attention/pallas_call | solution.py:580
  389.4 1.4 copy-done.38
  391.8 1.8 collective-permute-start.52
  393.7 2.8 collective-permute-done.54.got_ref
  398.6 22.4 %collective-permute-done.53.got_ref = bf16[2,960,384]{2,1,0:T(8,128)(2,1)S(1)} collective-permute-done((bf16[2,960,384]{2,1,0:T(8,128)(2,1)}, bf16[2,960,384]{2,1,0:T(8,128)(2,1)S(1)}, u32[]{:S(2)}, u32[]{:S(2)}) %collective-permute-start.53) | collective-permute-done | bytes 1474592 | tf_op jit(solution)/shard_map/ppermute | solution.py:887
  421.9 1.6 collective-permute-start.56
  425.6 7.8 %collective-permute-done.56.got_ref = bf16[960,384]{1,0:T(8,128)(2,1)S(1)} collective-permute-done((bf16[960,384]{1,0:T(8,128)(2,1)S(1)}, bf16[960,384]{1,0:T(8,128)(2,1)S(1)}, u32[]{:S(2)}, u32[]{:S(2)}) %collective-permute-start.56) | collective-permute-done | bytes 737312 | tf_op jit(solution)/shard_map/ppermute | solution.py:887
  434.2 8.9 %collective-permute-done.55.got_ref = bf16[2,240,640]{2,1,0:T(8,128)(2,1)S(1)} collective-permute-done((bf16[2,240,640]{2,1,0:T(8,128)(2,1)S(1)}, bf16[2,240,640]{2,1,0:T(8,128)(2,1)S(1)}, u32[]{:S(2)}, u32[]{:S(2)}) %collective-permute-start.55) | collective-permute-done | bytes 614432 | tf_op jit(solution)/shard_map/ppermute | solution.py:893
  445.3 17.1 %collective-permute-done.60.got_ref = bf16[2,240,384]{2,1,0:T(8,128)(2,1)S(1)} collective-permute-done((bf16[2,240,384]{2,1,0:T(8,128)(2,1)S(1)}, bf16[2,240,384]{2,1,0:T(8,128)(2,1)S(1)}, u32[]{:S(2)}, u32[]{:S(2)}) %collective-permute-start.60) | collective-permute-done | bytes 368672 | tf_op jit(solution)/shard_map/ppermute | solution.py:893
  465.1 1.5 collective-permute-start.71
  468.7 5.3 %collective-permute-done.63.got_ref = bf16[2,120,640]{2,1,0:T(8,128)(2,1)S(1)} collective-permute-done((bf16[2,120,640]{2,1,0:T(8,128)(2,1)S(1)}, bf16[2,120,640]{2,1,0:T(8,128)(2,1)S(1)}, u32[]{:S(2)}, u32[]{:S(2)}) %collective-permute-start.63) | collective-permute-done | bytes 307232 | tf_op jit(solution)/shard_map/ppermute | solution.py:887
  474.6 8.8 %collective-permute-done.62.got_ref = bf16[240,384]{1,0:T(8,128)(2,1)S(1)} collective-permute-done((bf16[240,384]{1,0:T(8,128)(2,1)S(1)}, bf16[240,384]{1,0:T(8,128)(2,1)S(1)}, u32[]{:S(2)}, u32[]{:S(2)}) %collective-permute-start.62) | collective-permute-done | bytes 184352 | tf_op jit(solution)/shard_map/ppermute | solution.py:893
  485.4 1.5 collective-permute-start.65
  486.9 1.4 collective-permute-start.66
  489.0 7.3 %collective-permute-done.78.got_ref = bf16[120,640]{1,0:T(8,128)(2,1)S(1)} collective-permute-done((bf16[120,640]{1,0:T(8,128)(2,1)S(1)}, bf16[120,640]{1,0:T(8,128)(2,1)S(1)}, u32[]{:S(2)}, u32[]{:S(2)}) %collective-permute-start.78) | collective-permute-done | bytes 153632 | tf_op jit(solution)/shard_map/ppermute | solution.py:887
  498.7 1.5 collective-permute-start.80
  502.0 2.8 collective-permute-done.79.rest_1_
  505.9 3.1 lay.2
  510.1 1.7 copy-done.16
  511.8 2.4 lay.3
  516.6 2.3 lay_down.1
  (365 shorter events, 85.6 us)
Async XLA Ops:
  8.8 12.8 %collective-permute-start.2 = (bf16[240,384]{1,0:T(8,128)(2,1)S(1)}, bf16[240,384]{1,0:T(8,128)(2,1)S(1)}, u32[]{:S(2)}, u32[]{:S(2)}) collective-permute-start(bf16[240,384]{1,0:T(8,128)(2,1)S(1)} %pick_first.1.rest_0_), channel_id=1, source_target_pairs={{0,2},{1,3},{2,0},{3,1},{4,6},{5,7},{6,4},{7,5},{8,10},{9,11},{10,... | collective-permute-start | bytes 552968 | tf_op jit(solution)/shard_map/ppermute | solution.py:893
  12.9 9.4 %collective-permute-start.1 = (bf16[240,384]{1,0:T(8,128)(2,1)S(1)}, bf16[240,384]{1,0:T(8,128)(2,1)S(1)}, u32[]{:S(2)}, u32[]{:S(2)}) collective-permute-start(bf16[240,384]{1,0:T(8,128)(2,1)S(1)} %pick_first.1.rest_0_), channel_id=1, source_target_pairs={{0,1},{1,0},{2,3},{3,2},{4,5},{5,4},{6,7},{7,6},{8,9},{9,8},{10,11... | collective-permute-start | bytes 552968 | tf_op jit(solution)/shard_map/ppermute | solution.py:893
  29.0 19.5 %collective-permute-start.4 = (bf16[960,384]{1,0:T(8,128)(2,1)S(1)}, bf16[960,384]{1,0:T(8,128)(2,1)S(1)}, u32[]{:S(2)}, u32[]{:S(2)}) collective-permute-start(bf16[960,384]{1,0:T(8,128)(2,1)S(1)} %bitcast.33), channel_id=1, source_target_pairs={{0,8},{4,20},{8,0},{12,28},{16,24},{20,4},{24,16},{28,12},{1,9},{5... | collective-permute-start | bytes 2211848 | tf_op jit(solution)/shard_map/ppermute | solution.py:887
  30.3 32.9 %collective-permute-start.5 = (bf16[960,384]{1,0:T(8,128)(2,1)S(1)}, bf16[960,384]{1,0:T(8,128)(2,1)S(1)}, u32[]{:S(2)}, u32[]{:S(2)}) collective-permute-start(bf16[960,384]{1,0:T(8,128)(2,1)S(1)} %bitcast.34), channel_id=1, source_target_pairs={{0,16},{4,12},{8,24},{12,4},{16,0},{20,28},{24,8},{28,20},{1,17},{... | collective-permute-start | bytes 2211848 | tf_op jit(solution)/shard_map/ppermute | solution.py:887
  48.5 25.6 %collective-permute-start.6 = (bf16[960,384]{1,0:T(8,128)(2,1)S(1)}, bf16[960,384]{1,0:T(8,128)(2,1)}, u32[]{:S(2)}, u32[]{:S(2)}) collective-permute-start(bf16[960,384]{1,0:T(8,128)(2,1)S(1)} %collective-permute-done.4.refs_1_.rest_1_), channel_id=1, source_target_pairs={{0,16},{4,12},{8,24},{12,4},{16,0},{20,28},{24,8},{28,20},{1,17},{... | collective-permute-start | bytes 2211848 | tf_op jit(solution)/shard_map/ppermute | solution.py:887
  49.0 14.3 %collective-permute-start.12 = (bf16[240,640]{1,0:T(8,128)(2,1)S(1)}, bf16[240,640]{1,0:T(8,128)(2,1)S(1)}, u32[]{:S(2)}, u32[]{:S(2)}) collective-permute-start(bf16[240,640]{1,0:T(8,128)(2,1)S(1)} %pick.1.rest_4_.rest_0_), channel_id=1, source_target_pairs={{0,2},{1,3},{2,0},{3,1},{4,6},{5,7},{6,4},{7,5},{8,10},{9,11},{10,... | collective-permute-start | bytes 921608 | tf_op jit(solution)/shard_map/ppermute | solution.py:893
  51.7 28.2 %collective-permute-start.7 = (bf16[960,384]{1,0:T(8,128)(2,1)S(1)}, bf16[960,384]{1,0:T(8,128)(2,1)}, u32[]{:S(2)}, u32[]{:S(2)}) collective-permute-start(bf16[960,384]{1,0:T(8,128)(2,1)S(1)} %bitcast.35), channel_id=1, source_target_pairs={{0,4},{4,0},{8,12},{12,8},{16,20},{20,16},{24,28},{28,24},{1,5},{5... | collective-permute-start | bytes 2211848 | tf_op jit(solution)/shard_map/ppermute | solution.py:887
  51.7 18.0 %collective-permute-start.11 = (bf16[240,640]{1,0:T(8,128)(2,1)S(1)}, bf16[240,640]{1,0:T(8,128)(2,1)S(1)}, u32[]{:S(2)}, u32[]{:S(2)}) collective-permute-start(bf16[240,640]{1,0:T(8,128)(2,1)S(1)} %pick.1.rest_4_.rest_0_), channel_id=1, source_target_pairs={{0,1},{1,0},{2,3},{3,2},{4,5},{5,4},{6,7},{7,6},{8,9},{9,8},{10,11... | collective-permute-start | bytes 921608 | tf_op jit(solution)/shard_map/ppermute | solution.py:893
  63.2 10.1 %collective-permute-start.13 = (bf16[240,640]{1,0:T(8,128)(2,1)S(1)}, bf16[240,640]{1,0:T(8,128)(2,1)S(1)}, u32[]{:S(2)}, u32[]{:S(2)}) collective-permute-start(bf16[240,640]{1,0:T(8,128)(2,1)S(1)} %hold.4.rest_2_), channel_id=1, source_target_pairs={{0,1},{1,0},{2,3},{3,2},{4,5},{5,4},{6,7},{7,6},{8,9},{9,8},{10,11... | collective-permute-start | bytes 921608 | tf_op jit(solution)/shard_map/ppermute | solution.py:893
  64.4 15.0 %collective-permute-start = (bf16[976,256]{1,0:T(8,128)(2,1)}, bf16[976,256]{1,0:T(8,128)(2,1)}, u32[]{:S(2)}, u32[]{:S(2)}) collective-permute-start(bf16[976,256]{1,0:T(8,128)(2,1)} %pad_maximum_fusion), channel_id=1, source_target_pairs={{0,0},{1,4},{2,1},{3,5},{4,2},{5,6},{6,3},{7,7},{8,8},{9,12},{10,9... | collective-permute-start | bytes 1499144 | tf_op jit(solution)/shard_map/ppermute | solution.py:904
  70.5 14.3 %collective-permute-start.8 = (bf16[960,384]{1,0:T(8,128)(2,1)S(1)}, bf16[960,384]{1,0:T(8,128)(2,1)}, u32[]{:S(2)}, u32[]{:S(2)}) collective-permute-start(bf16[960,384]{1,0:T(8,128)(2,1)S(1)} %collective-permute-done.4.refs_1_.rest_1_), channel_id=1, source_target_pairs={{0,4},{4,0},{8,12},{12,8},{16,20},{20,16},{24,28},{28,24},{1,5},{5... | collective-permute-start | bytes 2211848 | tf_op jit(solution)/shard_map/ppermute | solution.py:887
  74.1 10.6 %collective-permute-start.9 = (bf16[960,384]{1,0:T(8,128)(2,1)S(1)}, bf16[960,384]{1,0:T(8,128)(2,1)}, u32[]{:S(2)}, u32[]{:S(2)}) collective-permute-start(bf16[960,384]{1,0:T(8,128)(2,1)S(1)} %collective-permute-done.5.refs_2_.rest_2_), channel_id=1, source_target_pairs={{0,4},{4,0},{8,12},{12,8},{16,20},{20,16},{24,28},{28,24},{1,5},{5... | collective-permute-start | bytes 2211848 | tf_op jit(solution)/shard_map/ppermute | solution.py:887
  74.1 10.6 %collective-permute-start.10 = (bf16[960,384]{1,0:T(8,128)(2,1)}, bf16[960,384]{1,0:T(8,128)(2,1)}, u32[]{:S(2)}, u32[]{:S(2)}) collective-permute-start(bf16[960,384]{1,0:T(8,128)(2,1)} %collective-permute-done.6.rest_3_), channel_id=1, source_target_pairs={{0,4},{4,0},{8,12},{12,8},{16,20},{20,16},{24,28},{28,24},{1,5},{5... | collective-permute-start | bytes 2211848 | tf_op jit(solution)/shard_map/ppermute | solution.py:887
  79.4 29.9 %collective-permute-start.16 = (bf16[960,640]{1,0:T(8,128)(2,1)S(1)}, bf16[960,640]{1,0:T(8,128)(2,1)}, u32[]{:S(2)}, u32[]{:S(2)}) collective-permute-start(bf16[960,640]{1,0:T(8,128)(2,1)S(1)} %bitcast.24), channel_id=1, source_target_pairs={{0,8},{4,20},{8,0},{12,28},{16,24},{20,4},{24,16},{28,12},{1,9},{5... | collective-permute-start | bytes 3686408 | tf_op jit(solution)/shard_map/ppermute | solution.py:887
  79.9 29.5 %collective-permute-start.17 = (bf16[960,640]{1,0:T(8,128)(2,1)S(1)}, bf16[960,640]{1,0:T(8,128)(2,1)}, u32[]{:S(2)}, u32[]{:S(2)}) collective-permute-start(bf16[960,640]{1,0:T(8,128)(2,1)S(1)} %bitcast.25), channel_id=1, source_target_pairs={{0,16},{4,12},{8,24},{12,4},{16,0},{20,28},{24,8},{28,20},{1,17},{... | collective-permute-start | bytes 3686408 | tf_op jit(solution)/shard_map/ppermute | solution.py:887
  91.6 14.2 %collective-permute-start.14 = (bf16[656,256]{1,0:T(8,128)(2,1)}, bf16[656,256]{1,0:T(8,128)(2,1)S(1)}, u32[]{:S(2)}, u32[]{:S(2)}) collective-permute-start(bf16[656,256]{1,0:T(8,128)(2,1)} %get-tuple-element.105.kv2.rest_18_), channel_id=1, source_target_pairs={{0,1},{2,3},{4,5},{6,7},{8,9},{10,11},{12,13},{14,15},{16,17},{18,... | collective-permute-start | bytes 1007624 | tf_op jit(solution)/shard_map/ppermute | solution.py:926
  97.4 27.0 %collective-permute-start.24 = (bf16[480,640]{1,0:T(8,128)(2,1)S(1)}, bf16[480,640]{1,0:T(8,128)(2,1)S(1)}, u32[]{:S(2)}, u32[]{:S(2)}) collective-permute-start(bf16[480,640]{1,0:T(8,128)(2,1)S(1)} %copy-done.7), channel_id=1, source_target_pairs={{0,2},{1,3},{2,0},{3,1},{4,6},{5,7},{6,4},{7,5},{8,10},{9,11},{10,... | collective-permute-start | bytes 1843208 | tf_op jit(solution)/shard_map/ppermute | solution.py:893
  106.9 30.2 %collective-permute-start.23 = (bf16[480,640]{1,0:T(8,128)(2,1)S(1)}, bf16[480,640]{1,0:T(8,128)(2,1)S(1)}, u32[]{:S(2)}, u32[]{:S(2)}) collective-permute-start(bf16[480,640]{1,0:T(8,128)(2,1)S(1)} %copy-done.7), channel_id=1, source_target_pairs={{0,1},{1,0},{2,3},{3,2},{4,5},{5,4},{6,7},{7,6},{8,9},{9,8},{10,11... | collective-permute-start | bytes 1843208 | tf_op jit(solution)/shard_map/ppermute | solution.py:893
  124.4 25.6 %collective-permute-start.25 = (bf16[480,640]{1,0:T(8,128)(2,1)S(1)}, bf16[480,640]{1,0:T(8,128)(2,1)S(1)}, u32[]{:S(2)}, u32[]{:S(2)}) collective-permute-start(bf16[480,640]{1,0:T(8,128)(2,1)S(1)} %hold.5.rest_2_), channel_id=1, source_target_pairs={{0,1},{1,0},{2,3},{3,2},{4,5},{5,4},{6,7},{7,6},{8,9},{9,8},{10,11... | collective-permute-start | bytes 1843208 | tf_op jit(solution)/shard_map/ppermute | solution.py:893
  124.4 27.9 %collective-permute-start.18 = (bf16[960,640]{1,0:T(8,128)(2,1)}, bf16[960,640]{1,0:T(8,128)(2,1)S(1)}, u32[]{:S(2)}, u32[]{:S(2)}) collective-permute-start(bf16[960,640]{1,0:T(8,128)(2,1)} %collective-permute-done.16.rest_0_.rest_9_), channel_id=1, source_target_pairs={{0,16},{4,12},{8,24},{12,4},{16,0},{20,28},{24,8},{28,20},{1,17},{... | collective-permute-start | bytes 3686408 | tf_op jit(solution)/shard_map/ppermute | solution.py:887
  151.3 12.0 %collective-permute-start.26 = (bf16[4,480,640]{2,1,0:T(8,128)(2,1)S(1)}, bf16[4,480,640]{2,1,0:T(8,128)(2,1)S(1)}, u32[]{:S(2)}, u32[]{:S(2)}) collective-permute-start(bf16[4,480,640]{2,1,0:T(8,128)(2,1)S(1)} %stack.33.rest_16_), channel_id=1, source_target_pairs={{0,4},{4,0},{8,12},{12,8},{16,20},{20,16},{24,28},{28,24},{1,5},{5... | collective-permute-start | bytes 7372808 | tf_op jit(solution)/shard_map/ppermute | solution.py:887
  151.3 8.2 %collective-permute-start.19 = (bf16[960,640]{1,0:T(8,128)(2,1)S(1)}, bf16[960,640]{1,0:T(8,128)(2,1)S(1)}, u32[]{:S(2)}, u32[]{:S(2)}) collective-permute-start(bf16[960,640]{1,0:T(8,128)(2,1)S(1)} %bitcast.32), channel_id=1, source_target_pairs={{0,4},{4,0},{8,12},{12,8},{16,20},{20,16},{24,28},{28,24},{1,5},{5... | collective-permute-start | bytes 3686408 | tf_op jit(solution)/shard_map/ppermute | solution.py:887
  151.8 7.9 %collective-permute-start.20 = (bf16[960,640]{1,0:T(8,128)(2,1)}, bf16[960,640]{1,0:T(8,128)(2,1)S(1)}, u32[]{:S(2)}, u32[]{:S(2)}) collective-permute-start(bf16[960,640]{1,0:T(8,128)(2,1)} %collective-permute-done.16.rest_0_.rest_9_), channel_id=1, source_target_pairs={{0,4},{4,0},{8,12},{12,8},{16,20},{20,16},{24,28},{28,24},{1,5},{5... | collective-permute-start | bytes 3686408 | tf_op jit(solution)/shard_map/ppermute | solution.py:887
  151.9 11.3 %collective-permute-start.21 = (bf16[960,640]{1,0:T(8,128)(2,1)}, bf16[960,640]{1,0:T(8,128)(2,1)S(1)}, u32[]{:S(2)}, u32[]{:S(2)}) collective-permute-start(bf16[960,640]{1,0:T(8,128)(2,1)} %collective-permute-done.17.rest_1_.rest_10_), channel_id=1, source_target_pairs={{0,4},{4,0},{8,12},{12,8},{16,20},{20,16},{24,28},{28,24},{1,5},{5... | collective-permute-start | bytes 3686408 | tf_op jit(solution)/shard_map/ppermute | solution.py:887
  152.4 10.9 %collective-permute-start.22 = (bf16[960,640]{1,0:T(8,128)(2,1)S(1)}, bf16[960,640]{1,0:T(8,128)(2,1)S(1)}, u32[]{:S(2)}, u32[]{:S(2)}) collective-permute-start(bf16[960,640]{1,0:T(8,128)(2,1)S(1)} %collective-permute-done.18.rest_11_), channel_id=1, source_target_pairs={{0,4},{4,0},{8,12},{12,8},{16,20},{20,16},{24,28},{28,24},{1,5},{5... | collective-permute-start | bytes 3686408 | tf_op jit(solution)/shard_map/ppermute | solution.py:887
  185.8 8.3 %collective-permute-start.27 = (bf16[656,256]{1,0:T(8,128)(2,1)}, bf16[656,256]{1,0:T(8,128)(2,1)S(1)}, u32[]{:S(2)}, u32[]{:S(2)}) collective-permute-start(bf16[656,256]{1,0:T(8,128)(2,1)} %get-tuple-element.109.kv2.rest_18_), channel_id=1, source_target_pairs={{0,1},{2,3},{4,5},{6,7},{8,9},{10,11},{12,13},{14,15},{16,17},{18,... | collective-permute-start | bytes 1007624 | tf_op jit(solution)/shard_map/ppermute | solution.py:926
  187.4 7.8 %collective-permute-start.29 = (bf16[256,960]{1,0:T(8,128)(2,1)S(1)}, bf16[256,960]{1,0:T(8,128)(2,1)S(1)}, u32[]{:S(2)}, u32[]{:S(2)}) collective-permute-start(bf16[256,960]{1,0:T(8,128)(2,1)S(1)} %copy-done.88), channel_id=1, source_target_pairs={{0,4},{4,0},{8,12},{12,8},{16,20},{20,16},{24,28},{28,24},{1,5},{5... | collective-permute-start | bytes 1474568 | tf_op jit(solution)/shard_map/ppermute | solution.py:887
  187.5 7.7 %collective-permute-start.30 = (bf16[256,960]{1,0:T(8,128)(2,1)}, bf16[256,960]{1,0:T(8,128)(2,1)S(1)}, u32[]{:S(2)}, u32[]{:S(2)}) collective-permute-start(bf16[256,960]{1,0:T(8,128)(2,1)} %get-tuple-element.111.rest_1_), channel_id=1, source_target_pairs={{0,4},{4,0},{8,12},{12,8},{16,20},{20,16},{24,28},{28,24},{1,5},{5... | collective-permute-start | bytes 1474568 | tf_op jit(solution)/shard_map/ppermute | solution.py:887
  208.0 22.6 %collective-permute-start.33 = (bf16[960,256]{1,0:T(8,128)(2,1)S(1)}, bf16[960,256]{1,0:T(8,128)(2,1)S(1)}, u32[]{:S(2)}, u32[]{:S(2)}) collective-permute-start(bf16[960,256]{1,0:T(8,128)(2,1)S(1)} %hold.6), channel_id=1, source_target_pairs={{0,0},{1,4},{2,1},{3,5},{4,2},{5,6},{6,3},{7,7},{8,8},{9,12},{10,9... | collective-permute-start | bytes 1474568 | tf_op jit(solution)/shard_map/ppermute | solution.py:904
  209.2 43.9 %collective-permute-start.34 = (bf16[256,960]{1,0:T(8,128)(2,1)S(1)}, bf16[256,960]{1,0:T(8,128)(2,1)S(1)}, u32[]{:S(2)}, u32[]{:S(2)}) collective-permute-start(bf16[256,960]{1,0:T(8,128)(2,1)S(1)} %copy-done.89), channel_id=1, source_target_pairs={{0,4},{4,0},{8,12},{12,8},{16,20},{20,16},{24,28},{28,24},{1,5},{5... | collective-permute-start | bytes 1474568 | tf_op jit(solution)/shard_map/ppermute | solution.py:887
  230.0 23.2 %collective-permute-start.35 = (bf16[256,960]{1,0:T(8,128)(2,1)}, bf16[256,960]{1,0:T(8,128)(2,1)S(1)}, u32[]{:S(2)}, u32[]{:S(2)}) collective-permute-start(bf16[256,960]{1,0:T(8,128)(2,1)} %get-tuple-element.125.rest_0_), channel_id=1, source_target_pairs={{0,4},{4,0},{8,12},{12,8},{16,20},{20,16},{24,28},{28,24},{1,5},{5... | collective-permute-start | bytes 1474568 | tf_op jit(solution)/shard_map/ppermute | solution.py:887
  230.0 23.1 %collective-permute-start.36 = (bf16[256,960]{1,0:T(8,128)(2,1)}, bf16[256,960]{1,0:T(8,128)(2,1)S(1)}, u32[]{:S(2)}, u32[]{:S(2)}) collective-permute-start(bf16[256,960]{1,0:T(8,128)(2,1)} %get-tuple-element.126.rest_4_), channel_id=1, source_target_pairs={{0,4},{4,0},{8,12},{12,8},{16,20},{20,16},{24,28},{28,24},{1,5},{5... | collective-permute-start | bytes 1474568 | tf_op jit(solution)/shard_map/ppermute | solution.py:887
  253.0 42.0 %collective-permute-start.41 = (bf16[256,2560]{1,0:T(8,128)(2,1)}, bf16[256,2560]{1,0:T(8,128)(2,1)S(1)}, u32[]{:S(2)}, u32[]{:S(2)}) collective-permute-start(bf16[256,2560]{1,0:T(8,128)(2,1)} %get-tuple-element.137), channel_id=1, source_target_pairs={{0,4},{4,0},{8,12},{12,8},{16,20},{20,16},{24,28},{28,24},{1,5},{5... | collective-permute-start | bytes 3932168 | tf_op jit(solution)/shard_map/ppermute | solution.py:887
  270.4 24.6 %collective-permute-start.42 = (bf16[256,1280]{1,0:T(8,128)(2,1)S(1)}, bf16[256,1280]{1,0:T(8,128)(2,1)S(1)}, u32[]{:S(2)}, u32[]{:S(2)}) collective-permute-start(bf16[256,1280]{1,0:T(8,128)(2,1)S(1)} %copy-done.95), channel_id=1, source_target_pairs={{0,4},{4,0},{8,12},{12,8},{16,20},{20,16},{24,28},{28,24},{1,5},{5... | collective-permute-start | bytes 1966088 | tf_op jit(solution)/shard_map/ppermute | solution.py:887
  273.9 21.2 %collective-permute-start.38 = (bf16[640,256]{1,0:T(8,128)(2,1)S(1)}, bf16[640,256]{1,0:T(8,128)(2,1)S(1)}, u32[]{:S(2)}, u32[]{:S(2)}) collective-permute-start(bf16[640,256]{1,0:T(8,128)(2,1)S(1)} %far_sum.2), channel_id=1, source_target_pairs={{1,0},{3,2},{5,4},{7,6},{9,8},{11,10},{13,12},{15,14},{17,16},{19,... | collective-permute-start | bytes 983048 | tf_op jit(solution)/shard_map/ppermute | solution.py:935
  318.5 23.0 %collective-permute-start.48 = (bf16[256,2560]{1,0:T(8,128)(2,1)}, bf16[256,2560]{1,0:T(8,128)(2,1)S(1)}, u32[]{:S(2)}, u32[]{:S(2)}) collective-permute-start(bf16[256,2560]{1,0:T(8,128)(2,1)} %get-tuple-element.154), channel_id=1, source_target_pairs={{0,4},{4,0},{8,12},{12,8},{16,20},{20,16},{24,28},{28,24},{1,5},{5... | collective-permute-start | bytes 3932168 | tf_op jit(solution)/shard_map/ppermute | solution.py:887
  353.6 35.8 %collective-permute-start.50 = (bf16[2,960,640]{2,1,0:T(8,128)(2,1)}, bf16[2,960,640]{2,1,0:T(8,128)(2,1)S(1)}, u32[]{:S(2)}, u32[]{:S(2)}) collective-permute-start(bf16[2,960,640]{2,1,0:T(8,128)(2,1)} %get-tuple-element.155.rest_8_), channel_id=1, source_target_pairs={{0,8},{4,20},{8,0},{12,28},{16,24},{20,4},{24,16},{28,12},{1,9},{5... | collective-permute-start | bytes 7372808 | tf_op jit(solution)/shard_map/ppermute | solution.py:887
  355.8 12.2 %collective-permute-start.49 = (bf16[3,256,384]{2,1,0:T(8,128)(2,1)S(1)}, bf16[3,256,384]{2,1,0:T(8,128)(2,1)S(1)}, u32[]{:S(2)}, u32[]{:S(2)}) collective-permute-start(bf16[3,256,384]{2,1,0:T(8,128)(2,1)S(1)} %get-tuple-element.157), channel_id=1, source_target_pairs={{0,4},{4,0},{8,12},{12,8},{16,20},{20,16},{24,28},{28,24},{1,5},{5... | collective-permute-start | bytes 1769480 | tf_op jit(solution)/shard_map/ppermute | solution.py:887
  356.3 12.0 %collective-permute-start.45 = (bf16[640,256]{1,0:T(8,128)(2,1)S(1)}, bf16[640,256]{1,0:T(8,128)(2,1)S(1)}, u32[]{:S(2)}, u32[]{:S(2)}) collective-permute-start(bf16[640,256]{1,0:T(8,128)(2,1)S(1)} %copy-done.43), channel_id=1, source_target_pairs={{1,0},{3,2},{5,4},{7,6},{9,8},{11,10},{13,12},{15,14},{17,16},{19,... | collective-permute-start | bytes 983048 | tf_op jit(solution)/shard_map/ppermute | solution.py:935
  367.2 29.3 %collective-permute-start.54 = (bf16[960,640]{1,0:T(8,128)(2,1)}, bf16[960,640]{1,0:T(8,128)(2,1)S(1)}, u32[]{:S(2)}, u32[]{:S(2)}) collective-permute-start(bf16[960,640]{1,0:T(8,128)(2,1)} %get-tuple-element.173), channel_id=1, source_target_pairs={{0,1},{1,0},{2,3},{3,2},{4,5},{5,4},{6,7},{7,6},{8,9},{9,8},{10,11... | collective-permute-start | bytes 3686408 | tf_op jit(solution)/shard_map/ppermute | solution.py:893
  388.9 32.1 %collective-permute-start.53 = (bf16[2,960,384]{2,1,0:T(8,128)(2,1)}, bf16[2,960,384]{2,1,0:T(8,128)(2,1)S(1)}, u32[]{:S(2)}, u32[]{:S(2)}) collective-permute-start(bf16[2,960,384]{2,1,0:T(8,128)(2,1)} %get-tuple-element.169.rest_0_), channel_id=1, source_target_pairs={{0,8},{4,20},{8,0},{12,28},{16,24},{20,4},{24,16},{28,12},{1,9},{5... | collective-permute-start | bytes 4423688 | tf_op jit(solution)/shard_map/ppermute | solution.py:887
  391.8 31.6 %collective-permute-start.52 = (bf16[960,640]{1,0:T(8,128)(2,1)S(1)}, bf16[960,640]{1,0:T(8,128)(2,1)S(1)}, u32[]{:S(2)}, u32[]{:S(2)}) collective-permute-start(bf16[960,640]{1,0:T(8,128)(2,1)S(1)} %get-tuple-element.171.rest_0_), channel_id=1, source_target_pairs={{0,16},{4,12},{8,24},{12,4},{16,0},{20,28},{24,8},{28,20},{1,17},{... | collective-permute-start | bytes 3686408 | tf_op jit(solution)/shard_map/ppermute | solution.py:887
  397.3 46.5 %collective-permute-start.58 = (bf16[960,640]{1,0:T(8,128)(2,1)S(1)}, bf16[960,640]{1,0:T(8,128)(2,1)S(1)}, u32[]{:S(2)}, u32[]{:S(2)}) collective-permute-start(bf16[960,640]{1,0:T(8,128)(2,1)S(1)} %down_pair.1.rest_0_.own_ref), channel_id=1, source_target_pairs={{2,0},{3,1},{4,6},{5,7},{10,8},{11,9},{12,14},{13,15},{18,16},{19,... | collective-permute-start | bytes 3686408 | tf_op jit(solution)/shard_map/ppermute | solution.py:893
  421.9 11.5 %collective-permute-start.56 = (bf16[960,384]{1,0:T(8,128)(2,1)S(1)}, bf16[960,384]{1,0:T(8,128)(2,1)S(1)}, u32[]{:S(2)}, u32[]{:S(2)}) collective-permute-start(bf16[960,384]{1,0:T(8,128)(2,1)S(1)} %get-tuple-element.174.rest_0_), channel_id=1, source_target_pairs={{0,16},{4,12},{8,24},{12,4},{16,0},{20,28},{24,8},{28,20},{1,17},{... | collective-permute-start | bytes 2211848 | tf_op jit(solution)/shard_map/ppermute | solution.py:887
  424.4 18.7 %collective-permute-start.55 = (bf16[2,240,640]{2,1,0:T(8,128)(2,1)S(1)}, bf16[2,240,640]{2,1,0:T(8,128)(2,1)S(1)}, u32[]{:S(2)}, u32[]{:S(2)}) collective-permute-start(bf16[2,240,640]{2,1,0:T(8,128)(2,1)S(1)} %get-tuple-element.176.rest_0_), channel_id=1, source_target_pairs={{0,1},{1,0},{2,3},{3,2},{4,5},{5,4},{6,7},{7,6},{8,9},{9,8},{10,11... | collective-permute-start | bytes 1843208 | tf_op jit(solution)/shard_map/ppermute | solution.py:893
  444.7 18.3 %collective-permute-start.59 = (bf16[480,640]{1,0:T(8,128)(2,1)S(1)}, bf16[480,640]{1,0:T(8,128)(2,1)S(1)}, u32[]{:S(2)}, u32[]{:S(2)}) collective-permute-start(bf16[480,640]{1,0:T(8,128)(2,1)S(1)} %get-tuple-element.182.rest_0_), channel_id=1, source_target_pairs={{0,4},{4,0},{8,12},{12,8},{16,20},{20,16},{24,28},{28,24},{1,5},{5... | collective-permute-start | bytes 1843208 | tf_op jit(solution)/shard_map/ppermute | solution.py:887
  444.8 17.6 %collective-permute-start.60 = (bf16[2,240,384]{2,1,0:T(8,128)(2,1)S(1)}, bf16[2,240,384]{2,1,0:T(8,128)(2,1)S(1)}, u32[]{:S(2)}, u32[]{:S(2)}) collective-permute-start(bf16[2,240,384]{2,1,0:T(8,128)(2,1)S(1)} %get-tuple-element.178.rest_0_), channel_id=1, source_target_pairs={{0,1},{1,0},{2,3},{3,2},{4,5},{5,4},{6,7},{7,6},{8,9},{9,8},{10,11... | collective-permute-start | bytes 1105928 | tf_op jit(solution)/shard_map/ppermute | solution.py:893
  444.9 19.6 %collective-permute-start.57 = (bf16[240,640]{1,0:T(8,128)(2,1)S(1)}, bf16[240,640]{1,0:T(8,128)(2,1)S(1)}, u32[]{:S(2)}, u32[]{:S(2)}) collective-permute-start(bf16[240,640]{1,0:T(8,128)(2,1)S(1)} %get-tuple-element.180.rest_0_), channel_id=1, source_target_pairs={{0,2},{1,3},{2,0},{3,1},{4,6},{5,7},{6,4},{7,5},{8,10},{9,11},{10,... | collective-permute-start | bytes 921608 | tf_op jit(solution)/shard_map/ppermute | solution.py:893
  463.8 10.1 %collective-permute-start.63 = (bf16[2,120,640]{2,1,0:T(8,128)(2,1)S(1)}, bf16[2,120,640]{2,1,0:T(8,128)(2,1)S(1)}, u32[]{:S(2)}, u32[]{:S(2)}) collective-permute-start(bf16[2,120,640]{2,1,0:T(8,128)(2,1)S(1)} %get-tuple-element.185.rest_0_), channel_id=1, source_target_pairs={{0,8},{4,20},{8,0},{12,28},{16,24},{20,4},{24,16},{28,12},{1,9},{5... | collective-permute-start | bytes 921608 | tf_op jit(solution)/shard_map/ppermute | solution.py:887
  465.1 19.6 %collective-permute-start.71 = (bf16[240,640]{1,0:T(8,128)(2,1)S(1)}, bf16[240,640]{1,0:T(8,128)(2,1)S(1)}, u32[]{:S(2)}, u32[]{:S(2)}) collective-permute-start(bf16[240,640]{1,0:T(8,128)(2,1)S(1)} %sum_two.3.refs_1_.rest_0_), channel_id=1, source_target_pairs={{0,8},{4,20},{8,0},{12,28},{16,24},{20,4},{24,16},{28,12},{1,9},{5... | collective-permute-start | bytes 921608 | tf_op jit(solution)/shard_map/ppermute | solution.py:887
  466.6 18.8 %collective-permute-start.72 = (bf16[240,640]{1,0:T(8,128)(2,1)S(1)}, bf16[240,640]{1,0:T(8,128)(2,1)S(1)}, u32[]{:S(2)}, u32[]{:S(2)}) collective-permute-start(bf16[240,640]{1,0:T(8,128)(2,1)S(1)} %sum_two.3.refs_1_.rest_0_), channel_id=1, source_target_pairs={{0,16},{4,12},{8,24},{12,4},{16,0},{20,28},{24,8},{28,20},{1,17},{... | collective-permute-start | bytes 921608 | tf_op jit(solution)/shard_map/ppermute | solution.py:887
  467.3 19.5 %collective-permute-start.73 = (bf16[240,640]{1,0:T(8,128)(2,1)S(1)}, bf16[240,640]{1,0:T(8,128)(2,1)S(1)}, u32[]{:S(2)}, u32[]{:S(2)}) collective-permute-start(bf16[240,640]{1,0:T(8,128)(2,1)S(1)} %sum_two.3.refs_1_.rest_0_), channel_id=1, source_target_pairs={{0,24},{4,28},{8,16},{12,20},{16,8},{20,12},{24,0},{28,4},{1,25},{... | collective-permute-start | bytes 921608 | tf_op jit(solution)/shard_map/ppermute | solution.py:887
  468.7 19.6 %collective-permute-start.74 = (bf16[240,640]{1,0:T(8,128)(2,1)S(1)}, bf16[240,640]{1,0:T(8,128)(2,1)S(1)}, u32[]{:S(2)}, u32[]{:S(2)}) collective-permute-start(bf16[240,640]{1,0:T(8,128)(2,1)S(1)} %sum_two.3.refs_1_.rest_0_), channel_id=1, source_target_pairs={{0,4},{4,0},{8,12},{12,8},{16,20},{20,16},{24,28},{28,24},{1,5},{5... | collective-permute-start | bytes 921608 | tf_op jit(solution)/shard_map/ppermute | solution.py:887
  474.0 9.5 %collective-permute-start.62 = (bf16[240,384]{1,0:T(8,128)(2,1)S(1)}, bf16[240,384]{1,0:T(8,128)(2,1)S(1)}, u32[]{:S(2)}, u32[]{:S(2)}) collective-permute-start(bf16[240,384]{1,0:T(8,128)(2,1)S(1)} %get-tuple-element.184.rest_0_), channel_id=1, source_target_pairs={{0,2},{1,3},{2,0},{3,1},{4,6},{5,7},{6,4},{7,5},{8,10},{9,11},{10,... | collective-permute-start | bytes 552968 | tf_op jit(solution)/shard_map/ppermute | solution.py:893
  483.4 15.3 %collective-permute-start.61 = (bf16[960,256]{1,0:T(8,128)(2,1)S(1)}, bf16[960,256]{1,0:T(8,128)(2,1)S(1)}, u32[]{:S(2)}, u32[]{:S(2)}) collective-permute-start(bf16[960,256]{1,0:T(8,128)(2,1)S(1)} %hold.7), channel_id=1, source_target_pairs={{0,0},{4,1},{1,2},{5,3},{2,4},{6,5},{3,6},{7,7},{8,8},{12,9},{9,10... | collective-permute-start | bytes 1474568 | tf_op jit(solution)/shard_map/ppermute | solution.py:904
  484.7 11.6 %collective-permute-start.64 = (bf16[240,384]{1,0:T(8,128)(2,1)S(1)}, bf16[240,384]{1,0:T(8,128)(2,1)S(1)}, u32[]{:S(2)}, u32[]{:S(2)}) collective-permute-start(bf16[240,384]{1,0:T(8,128)(2,1)S(1)} %sum_two.4.rest_0_), channel_id=1, source_target_pairs={{0,8},{4,20},{8,0},{12,28},{16,24},{20,4},{24,16},{28,12},{1,9},{5... | collective-permute-start | bytes 552968 | tf_op jit(solution)/shard_map/ppermute | solution.py:887
  485.4 11.5 %collective-permute-start.65 = (bf16[240,384]{1,0:T(8,128)(2,1)S(1)}, bf16[240,384]{1,0:T(8,128)(2,1)S(1)}, u32[]{:S(2)}, u32[]{:S(2)}) collective-permute-start(bf16[240,384]{1,0:T(8,128)(2,1)S(1)} %sum_two.4.rest_0_), channel_id=1, source_target_pairs={{0,16},{4,12},{8,24},{12,4},{16,0},{20,28},{24,8},{28,20},{1,17},{... | collective-permute-start | bytes 552968 | tf_op jit(solution)/shard_map/ppermute | solution.py:887
  486.9 10.1 %collective-permute-start.66 = (bf16[240,384]{1,0:T(8,128)(2,1)S(1)}, bf16[240,384]{1,0:T(8,128)(2,1)S(1)}, u32[]{:S(2)}, u32[]{:S(2)}) collective-permute-start(bf16[240,384]{1,0:T(8,128)(2,1)S(1)} %sum_two.4.rest_0_), channel_id=1, source_target_pairs={{0,24},{4,28},{8,16},{12,20},{16,8},{20,12},{24,0},{28,4},{1,25},{... | collective-permute-start | bytes 552968 | tf_op jit(solution)/shard_map/ppermute | solution.py:887
  488.3 8.0 %collective-permute-start.78 = (bf16[120,640]{1,0:T(8,128)(2,1)S(1)}, bf16[120,640]{1,0:T(8,128)(2,1)S(1)}, u32[]{:S(2)}, u32[]{:S(2)}) collective-permute-start(bf16[120,640]{1,0:T(8,128)(2,1)S(1)} %get-tuple-element.188.rest_0_), channel_id=1, source_target_pairs={{0,16},{4,12},{8,24},{12,4},{16,0},{20,28},{24,8},{28,20},{1,17},{... | collective-permute-start | bytes 460808 | tf_op jit(solution)/shard_map/ppermute | solution.py:887
  498.7 10.3 %collective-permute-start.80 = (bf16[120,640]{1,0:T(8,128)(2,1)S(1)}, bf16[120,640]{1,0:T(8,128)(2,1)S(1)}, u32[]{:S(2)}, u32[]{:S(2)}) collective-permute-start(bf16[120,640]{1,0:T(8,128)(2,1)S(1)} %sum_two.5.rest_8_.rest_0_), channel_id=1, source_target_pairs={{0,16},{4,12},{8,24},{12,4},{16,0},{20,28},{24,8},{28,20},{1,17},{... | collective-permute-start | bytes 460808 | tf_op jit(solution)/shard_map/ppermute | solution.py:887
  500.2 9.3 %collective-permute-start.81 = (bf16[120,640]{1,0:T(8,128)(2,1)S(1)}, bf16[120,640]{1,0:T(8,128)(2,1)S(1)}, u32[]{:S(2)}, u32[]{:S(2)}) collective-permute-start(bf16[120,640]{1,0:T(8,128)(2,1)S(1)} %sum_two.5.rest_8_.rest_0_), channel_id=1, source_target_pairs={{0,24},{4,28},{8,16},{12,20},{16,8},{20,12},{24,0},{28,4},{1,25},{... | collective-permute-start | bytes 460808 | tf_op jit(solution)/shard_map/ppermute | solution.py:887
  501.5 8.1 %collective-permute-start.68 = (bf16[240,384]{1,0:T(8,128)(2,1)S(1)}, bf16[240,384]{1,0:T(8,128)(2,1)S(1)}, u32[]{:S(2)}, u32[]{:S(2)}) collective-permute-start(bf16[240,384]{1,0:T(8,128)(2,1)S(1)} %collective-permute-done.64.rest_1_), channel_id=1, source_target_pairs={{0,4},{4,0},{8,12},{12,8},{16,20},{20,16},{24,28},{28,24},{1,5},{5... | collective-permute-start | bytes 552968 | tf_op jit(solution)/shard_map/ppermute | solution.py:887
  501.5 8.5 %collective-permute-start.69 = (bf16[240,384]{1,0:T(8,128)(2,1)S(1)}, bf16[240,384]{1,0:T(8,128)(2,1)S(1)}, u32[]{:S(2)}, u32[]{:S(2)}) collective-permute-start(bf16[240,384]{1,0:T(8,128)(2,1)S(1)} %collective-permute-done.65.rest_2_), channel_id=1, source_target_pairs={{0,4},{4,0},{8,12},{12,8},{16,20},{20,16},{24,28},{28,24},{1,5},{5... | collective-permute-start | bytes 552968 | tf_op jit(solution)/shard_map/ppermute | solution.py:887
  509.0 7.5 %collective-permute-start.82 = (bf16[120,640]{1,0:T(8,128)(2,1)S(1)}, bf16[120,640]{1,0:T(8,128)(2,1)S(1)}, u32[]{:S(2)}, u32[]{:S(2)}) collective-permute-start(bf16[120,640]{1,0:T(8,128)(2,1)S(1)} %sum_two.5.rest_8_.rest_0_), channel_id=1, source_target_pairs={{0,4},{4,0},{8,12},{12,8},{16,20},{20,16},{24,28},{28,24},{1,5},{5... | collective-permute-start | bytes 460808 | tf_op jit(solution)/shard_map/ppermute | solution.py:887
  (120 other events, 1297.7 us)

commit v9 on v8

--- a/solution.py
+++ b/solution.py
@@ -254,11 +254,11 @@
     ]
 
 
-def post_kernel(last, sc, ot_ref, h_ref, gain_ref, gain_a, cos_ref, sin_ref, *rest):
+def post_kernel(last, after, sc, ot_ref, h_ref, gain_ref, gain_a, cos_ref, sin_ref, *rest):
     mine_a, other_a, mine_b, other_b = rest[:4], rest[4:8], rest[8:12], rest[12:16]
-    down, ids_ref = rest[16:18], rest[18]
-    o_ref, h1_ref, b_ref, gate_ref, up_ref, z_ref, next_ref = rest[19:26]
-    more, rest = rest[26 : 26 + (0 if last else 3)], rest[26 + (0 if last else 3) :]
+    down, ids_ref, rest = rest[16:18], rest[18], rest[19 + after :]
+    o_ref, h1_ref, b_ref, gate_ref, up_ref, z_ref, next_ref = rest[:7]
+    more, rest = rest[7 : 7 + (0 if last else 3)], rest[7 + (0 if last else 3) :]
     wa, sem_a, wb, sem_b, wd, sem_d = rest
     core, chip = sc[0], sc[1]
     fetch(mine_a, other_a, wa, sem_a, core, chip)
@@ -295,7 +295,7 @@
         project(total, gain_a, cos_ref, sin_ref, ids_ref[2 * KVW :, :], wa, sem_a, *more)
 
 
-def post(last, sc, ot, h, gain, gain_a, cos, sin, kv, wa, wb, wd):
+def post(last, after, sc, ot, h, gain, gain_a, cos, sin, kv, wa, wb, wd):
     width, n = ot.shape
     hidden = wb[0][0].shape[1] * 4
     outs = [shape((n, width), bf16), shape((n, width), f32), shape((n, width), bf16)] + [shape((n, hidden), bf16)] * 3
@@ -303,28 +303,24 @@
     if not last:
         outs += [shape((n, width), bf16), shape((width, n), bf16), shape((2 * KVW + IDS, n), bf16)]
     return pl.pallas_call(
-        functools.partial(post_kernel, last),
+        functools.partial(post_kernel, last, len(after)),
         out_shape=tuple(outs),
-        in_specs=[SCALARS] + [WHOLE] * 6 + [LEFT] * 18 + [WHOLE],
+        in_specs=[SCALARS] + [WHOLE] * 6 + [LEFT] * 18 + [WHOLE] + [LEFT] * len(after),
         out_specs=(WHOLE,) * len(outs),
         scratch_shapes=scratch_a(width) + scratch_ffn(width, hidden // 4),
         cost_estimate=BRIEF,
         compiler_params=pltpu.CompilerParams(vmem_limit_bytes=LIMIT),
         name="post",
-    )(sc, ot, h, gain, gain_a, cos, sin, *wa[0], *wa[1], *wb[0], *wb[1], *wd, kv)
+    )(sc, ot, h, gain, gain_a, cos, sin, *wa[0], *wa[1], *wb[0], *wb[1], *wd, kv, *after)
 
 
 def ffn_back(state, core, refs, weights):
-    gate_ref, up_ref, h1_ref, gain_ref, z_ref, gb_ref, keep_ref, send_ref, zk_ref, zs_ref, g1_ref, p_ref, dgain_ref, do_ref = refs
+    gate_ref, up_ref, h1_ref, gain_ref, gb_ref, keep_ref, send_ref, g1_ref, p_ref, dgain_ref, do_ref = refs
     wa, sem_a, wb, sem_b, wd, sem_d = weights
     gb = state.astype(bf16)
     gb_ref[...] = gb
     n = wb.shape[3]
-    half = 2 * n
     first = core == 0
-    low, high = z_ref[:, :half], z_ref[:, half:]
-    zk_ref[...] = jnp.where(first, low, high)
-    zs_ref[...] = jnp.where(first, high, low)
     arrived_down(wd, sem_d)
     db = None
     for m in range(4):
@@ -402,14 +398,14 @@
     else:
         g1_in, dq_ref, own_ref, near_ref, far_ref, h_ref, gain_a, cos_ref, sin_ref = take(9)
     if not end:
-        ins = take(5)
+        ins = take(4)
     take(after)
     if not start:
         dk_ref, dv_ref, one_ref, dgain_a = take(4)
     if end:
         (g_out,) = take(1)
     else:
-        outs = take(9)
+        outs = take(7)
     wa, sem_a = take(2)
     fetch(mine_a, other_a, wa, sem_a, core, chip)
     if not end:
@@ -454,7 +450,7 @@
         outs += [shape((width, n), bf16)]
     else:
         hidden = ffn[0].shape[1]
-        outs += [shape((n, width), bf16), shape((n, hidden), bf16), shape((n, hidden), bf16), shape((n, hidden // 2), bf16), shape((n, hidden // 2), bf16)]
+        outs += [shape((n, width), bf16), shape((n, hidden), bf16), shape((n, hidden), bf16)]
         outs += [shape((n, width), f32), shape((3, n, PIECE), bf16), shape((1, width), f32), shape((width, n), bf16)]
     args += list(after)
     specs += [LEFT] * len(after)
@@ -513,24 +509,24 @@
 
 def grad_down_kernel(sc, *rest):
     lefts, rights = rest[:4], rest[4:8]
-    outs, left, right = rest[-4:-2], rest[-2], rest[-1]
-    n, cols = rights[0].shape[0], right.shape[1]
+    out_ref, left, right = rest[-3:]
+    n, (_, half, cols) = rights[0].shape[0], out_ref.shape
     turned(left, lefts)
-    for i, out in enumerate(outs):
-        at = pl.multiple_of(((sc[2] + i) & 1) * cols, 128)
+    rows = pl.ds(pl.multiple_of(sc[0] * half, half), half)
+    for i in range(4):
         for j, block in enumerate(rights):
-            right[j * n : (j + 1) * n, :] = block[:, pl.ds(at, cols)]
-        out[...] = nn(left[...], right[...]).astype(bf16)
+            right[j * n : (j + 1) * n, :] = block[:, i * cols : (i + 1) * cols]
+        out_ref[i] = nn(left[rows, :], right[...]).astype(bf16)
 
 
 def grad_down(sc, lefts, rights, after):
     n, width = lefts[0].shape
-    cols = rights[0].shape[1] // 2
+    cols = rights[0].shape[1] // 4
     return pl.pallas_call(
         grad_down_kernel,
-        out_shape=(shape((width, cols), bf16),) * 2,
+        out_shape=shape((4, width // 2, cols), bf16),
         in_specs=[SCALARS] + [WHOLE] * 8 + [LEFT] * len(after),
-        out_specs=(WHOLE,) * 2,
+        out_specs=WHOLE,
         scratch_shapes=[pltpu.VMEM((width, 4 * n), bf16), pltpu.VMEM((4 * n, cols), bf16)],
         cost_estimate=BRIEF,
         compiler_params=pltpu.CompilerParams(vmem_limit_bytes=LIMIT),
@@ -796,41 +792,19 @@
     return small(kernel, sc, [keep, got], [shape(part, bf16), shape(part, f32)], [], after, "sum_third")
 
 
-def down_pair(sc, own, got, after):
-    def kernel(sc, own_ref, got_ref, *rest):
-        rest[-1][...] = (own_ref[...].astype(f32) + got_ref[...].astype(f32)).astype(bf16)
-
-    return small(kernel, sc, [own, got], [shape(own.shape, bf16)], [], after, "down_pair")[0]
-
-
-def down_ring(sc, own, got, after):
-    def kernel(sc, own_ref, got_ref, *rest):
-        give_ref, keep_ref = rest[-2:]
-        half = give_ref.shape[0]
-        for out, c in ((give_ref, 1 - sc[0]), (keep_ref, sc[0])):
-            rows = pl.ds(pl.multiple_of(c * half, half), half)
-            out[...] = (own_ref[rows, :].astype(f32) + got_ref[rows, :].astype(f32)).astype(bf16)
-
-    rows, cols = own.shape
-    half = shape((rows // 2, cols), bf16)
-    return small(kernel, sc, [own, got], [half, half], [], after, "down_ring")
-
-
-def down_split(sc, keep, given, after):
-    def kernel(sc, keep_ref, given_ref, *rest):
+def down_split(sc, half, after):
+    def kernel(sc, half_ref, *rest):
         send_ref, kept_ref, total = rest[-3:]
         n = total.shape[1]
-        owner = (sc[2] >> 1) == sc[0]
         for m in range(4):
-            rows = slice(m * n, (m + 1) * n)
-            total[m] = jnp.where(owner, keep_ref[rows, :].astype(f32), given_ref[rows, :].astype(f32))
+            total[m] = half_ref[m * n : (m + 1) * n, :].astype(f32)
         for i, m in enumerate(by_turn(sc[0], sc[1])):
             out = send_ref if i < 2 else kept_ref
             out[i % 2] = total[m].astype(bf16)
 
-    rows, cols = keep.shape
+    rows, cols = half.shape
     out = shape((2, rows // 4, cols), bf16)
-    return small(kernel, sc, [keep, given], [out, out], [pltpu.VMEM((4, rows // 4, cols), f32)], after, "down_split")
+    return small(kernel, sc, [half], [out, out], [pltpu.VMEM((4, rows // 4, cols), f32)], after, "down_split")
 
 
 def sum_two(sc, own, got, after):
@@ -975,42 +949,41 @@
     parts_b = piece_b, flip_z(piece_b, 1), far_b, flip_z(far_b, 1)
     whole_b = stack(sc, parts_b).reshape(depth * rows, piece_b.shape[1])
     wb = plane_gather(whole_b)
-    piece_d = pick_down(sc, down_weight.T, [whole_b])
-
-    h_0, a0, q0, own = pre(sc, tokens, gain_a, cos, sin, *wa, [whole_b, piece_d])
+    piece_d = pick_down(sc, down_weight.T, [whole_a])
+    whole_d = lax.all_gather(piece_d, "fsdp", axis=0)
+
+    h_0, a0, q0, own = pre(sc, tokens, gain_a, cos, sin, *wa, [whole_b])
     kv0 = window(own)
     o0, lse0 = attend(q0, kv0, [wb[0][1], wb[0][2]])
-    far_d = hold(flip_z(piece_d, 2), [o0])
-    parts_d = piece_d, flip_z(piece_d, 1), far_d, flip_z(far_d, 1)
-    whole_d = stack(sc, parts_d)
+    whole_d = hold(whole_d, [o0])
     weights = wa, wb, (whole_d, flip(whole_d, CORE))
-    mixed0, h1_0, b0, gate0, up0, z0, h_1, a1, q1, own = post(False, sc, o0, h_0, gain_f, gain_a, cos, sin, own, *weights)
+    mixed0, h1_0, b0, gate0, up0, z0, h_1, a1, q1, own = post(False, [], sc, o0, h_0, gain_f, gain_a, cos, sin, own, *weights)
     kv1 = window(own)
-    across_0 = across((a0, b0, mixed0))
+    across_0 = across((a0, b0, mixed0, z0))
+    cot = home_to_work(hold(cotangent[0].T, [kv1[1]]))
     o1, lse1 = attend(q1, kv1, across_0)
-    cot = home_to_work(hold(cotangent[0].T, [o1]))
-    mixed1, h1_1, b1, gate1, up1, z1, output = post(True, sc, o1, h_1, gain_f, gain_a, cos, sin, own, *weights)
-    output = home_to_work(output, back=True)
-    across_1 = across((a1, b1, mixed1))
-
-    gb1, act1, away1, zk1, zs1, g1, p1, dgain_f1, do = back(True, False, sc, weights, [cot], [gate1, up1, h1_1, gain_f, z1])
-    across_2 = across((gb1, away1, zs1))
+    mixed1, h1_1, b1, gate1, up1, z1, output = post(True, [cot], sc, o1, h_1, gain_f, gain_a, cos, sin, own, *weights)
+    across_1 = across((a1, b1, mixed1, z1))
+
+    gb1, act1, away1, g1, p1, dgain_f1, do = back(True, False, sc, weights, [cot], [gate1, up1, h1_1, gain_f])
+    across_2 = across((gb1, away1))
     dq1, three1, far, near, own = attend_back(sc, p1, q1, kv1, lse1, do, cos, sin, [*across_1])
     near, _, far = unwindow(sc, far, near)
     (three1,) = across((three1,))
+    output = home_to_work(hold(output, [far]), back=True)
     tail = [g1, dq1, own, near, far, h_1, gain_a, cos, sin]
-    dk1, dv1, one1, dgain_a1, gb0, act0, away0, zk0, zs0, g1, p0, dgain_f0, do = back(False, False, sc, weights, tail, [gate0, up0, h1_0, gain_f, z0], [output, three1, *across_2])
-
-    away0, gb0_, zs0, one1 = across((away0, gb0, zs0, one1))
-    dq0, three0, far, near, own = attend_back(sc, p0, q0, kv0, lse0, do, cos, sin, [one1])
+    dk1, dv1, one1, dgain_a1, gb0, act0, away0, g1, p0, dgain_f0, do = back(False, False, sc, weights, tail, [gate0, up0, h1_0, gain_f], [three1, *across_2])
+
+    away0, gb0_, one1 = across((away0, gb0, one1))
+    dq0, three0, far, near, own = attend_back(sc, p0, q0, kv0, lse0, do, cos, sin, [one1, output])
     near, down_far, far = unwindow(sc, far, near)
-    send_b, keep_b = grad_ffn(sc, [b1, b0, across_1[1], across_0[1]], [act1, act0, across_2[1], away0], [down_far])
+    parts_d = grad_down(sc, [gb1, gb0, across_2[0], gb0_], [z1, z0, across_1[3], across_0[3]], [down_far])
+    half_d = lax.psum_scatter(parts_d, "fsdp", scatter_dimension=0, tiled=False)
+    send_b, keep_b = grad_ffn(sc, [b1, b0, across_1[1], across_0[1]], [act1, act0, across_2[1], away0], [parts_d, far])
     got_b = flip(send_b, SIDE, BACK)
-    like_d, unlike_d = grad_down(sc, [gb1, gb0, across_2[0], gb0_], [zk1, zk0, across_2[2], zs0], [send_b])
-    got_d = flip_z(unlike_d, 1)
     (three0,) = across((three0,))
     tail = [g1, dq0, own, near, far, h_0, gain_a, cos, sin]
-    dk0, dv0, one0, dgain_a0, grad_tokens = back(False, True, sc, weights, tail, None, [like_d, three0])
+    dk0, dv0, one0, dgain_a0, grad_tokens = back(False, True, sc, weights, tail, None, [send_b, three0])
 
     own = [dq1, dq0, dk1, dk0, dv1, dv0, p1, p0]
     got = [three1, three0, one1, flip(one0, CORE)]
@@ -1018,23 +991,20 @@
     got_a = flip(send_a, SIDE, BACK)
     later_b, own_b = sum_first(sc, keep_b, got_b, [send_a])
     more_b = flip(later_b, BACK, SIDE)
-    pair_d = down_pair(sc, like_d, got_d, [later_b])
-    got_d = flip_z(pair_d, 2, lambda d, z: (z >> 1) != (d & 1))
-    later_a, own_a = sum_first(sc, keep_a, got_a, [pair_d])
+    grad_tokens = home_to_work(hold(grad_tokens, [later_b]), back=True)
+    later_a, own_a = sum_first(sc, keep_a, got_a, [later_b])
     more_a = flip(later_a, BACK, SIDE)
     send_b, ring_b = sum_second(sc, own_b, more_b, [later_a])
     got_b = flip_z(send_b, 1)
     send_a, ring_a = sum_second(sc, own_a, more_a, [send_b])
     got_a = flip_z(send_a, 1)
-    send_b, ring_b = sum_third(sc, ring_b, got_b, [send_a])
+    send_d, keep_d = down_split(sc, half_d, [send_a])
+    got_d = flip(send_d, SIDE, BACK)
+    send_b, ring_b = sum_third(sc, ring_b, got_b, [send_d, grad_tokens])
     got_b = flip_z(send_b, 2)
-    give, keep = down_ring(sc, pair_d, got_d, [send_b])
-    given = flip(give, CORE)
-    send_a, ring_a = sum_third(sc, ring_a, got_a, [give])
+    send_a, ring_a = sum_third(sc, ring_a, got_a, [send_b])
     got_a = flip_z(send_a, 2)
-    send_d, keep_d = down_split(sc, keep, given, [send_a])
-    got_d = flip(send_d, SIDE, BACK)
-    piece_b = over_groups(sum_two(sc, ring_b, got_b, [send_d]))
+    piece_b = over_groups(sum_two(sc, ring_b, got_b, [send_a]))
     all_b = spread(piece_b)
     later_d, own_d = sum_first(sc, keep_d, got_d, [piece_b])
     more_d = flip(later_d, BACK, SIDE)
@@ -1045,7 +1015,6 @@
     all_d = spread(piece_d)
     grad_query, grad_key, grad_value, grad_out, dgains = lay(sc, all_a, across(all_a), (width, KVW, KVW, width), [grad_gate])
     grad_down_ = lay_down(sc, all_d, across(all_d), [grad_query])
-    grad_tokens = home_to_work(hold(grad_tokens, [piece_b]), back=True)
     grad_tokens, output = grad_tokens.astype(f32).T, output.T
     return (output[None], grad_tokens[None], dgains[0], grad_query, grad_key, grad_value, grad_out, dgains[1], grad_gate, grad_up, grad_down_.T)
 

time: 525 us -> 557 us (1.061)
  between operations: 1.99 us -> 15.5 us
  waiting for transfers between devices: 208 us -> 217 us
    ppermute x15 -> x10, waiting for transfers between devices: 91.2 us -> 70.7 us  [flip_z(): return lax.ppermute(value, ('dp', 'fsdp'), pairs)]
    ppermute x63 -> x62, waiting for transfers between devices: 83 us -> 103 us  [flip(): lax.ppermute(value, 'dp', [(i, i ^ bits[i & 1]) for i in range(count)])]
    ppermute x63 -> x62, starting transfers between devices: 37.9 us -> 49.3 us  [flip(): lax.ppermute(value, 'dp', [(i, i ^ bits[i & 1]) for i in range(count)])]
    ppermute x2, waiting for transfers between devices: 19.4 us -> 30 us  [unwindow(): lax.ppermute(far, 'fsdp', [(z + 1, z) for z in range(0, depth, 2)])]
    ppermute x15 -> x10, starting transfers between devices: 17.9 us -> 14.1 us  [flip_z(): return lax.ppermute(value, ('dp', 'fsdp'), pairs)]
    unnamed x200 -> x178, local copies, waits for them, and re-layouts: 34.8 us -> 37.2 us
    pallas_call x16 -> x14, Pallas kernels: 13.5 us -> 14.7 us  [small(): pl.pallas_call(kernel, out_shape=tuple(outs), in_specs=[SCALARS] + [WHOLE...]
  transfers between devices with their start and end apart: 86 -> 82, of which waited for: 30 -> 37; matrix products, arithmetic and copies ran while one was open for 1% -> 2% of each run, Pallas kernels for 24% -> 27%
where the time goes in v9:
time: 557 us; the launch traced here: 551 us
  waiting for transfers between devices  217 us (39%)
  Pallas kernels  196 us (35%)
  starting transfers between devices  77.2 us (14%)
  local copies, waits for them, and re-layouts  39.8 us (7%)
  between operations  15.5 us (3%)
  other arithmetic  5.86 us (1%)
    ppermute x62, waiting for transfers between devices, flip(): lax.ppermute(value, 'dp', [(i, i ^ bits[i & 1]) for i in range(count)])  103 us
    ppermute x10, waiting for transfers between devices, flip_z(): return lax.ppermute(value, ('dp', 'fsdp'), pairs)  70.7 us
    ppermute x62, starting transfers between devices, flip(): lax.ppermute(value, 'dp', [(i, i ^ bits[i & 1]) for i in range(count)])  49.3 us
    pallas_call x3, Pallas kernels, back(): pl.pallas_call(functools.partial(back_kernel, start, end, len(after)), ou...  48.7 us
    pallas_call x2, Pallas kernels, post(): pl.pallas_call(functools.partial(post_kernel, last, len(after)), out_shap...  38.1 us
    unnamed x178, local copies, waits for them, and re-layouts  37.2 us
    ppermute x2, waiting for transfers between devices, unwindow(): lax.ppermute(far, 'fsdp', [(z + 1, z) for z in range(0, depth, 2)])  30 us
    pallas_call x2, Pallas kernels, attend_back(): pl.pallas_call(attend_back_kernel, out_shape=(shape((3, n, PIECE), bf16),...  25.4 us
  transfers between devices with their start and end apart: 82, of which 37 were waited for; matrix products, arithmetic and copies ran while one was open for 2% of the time, Pallas kernels for 27%

profile of v9, /device:TPU:0, one launch (start us, length us, event | category | flops | bytes accessed | tf_op | source)
XLA Modules:
  0.0 551.0 jit_solution(5753364102449197843)
XLA Ops:
  7.2 1.9 copy.37
  15.3 4.1 collective-permute-start.2
  19.4 1.6 collective-permute-start.1
  21.0 7.2 %collective-permute-done.2.rest_2_ = bf16[240,384]{1,0:T(8,128)(2,1)S(1)} collective-permute-done((bf16[240,384]{1,0:T(8,128)(2,1)S(1)}, bf16[240,384]{1,0:T(8,128)(2,1)S(1)}, u32[]{:S(2)}, u32[]{:S(2)}) %collective-permute-start.2) | collective-permute-done | bytes 184352 | tf_op jit(solution)/shard_map/ppermute | solution.py:867
  29.4 4.6 collective-permute-done.3.rest_3_
  34.0 1.5 stack.30.first_ref.rest_0_
  35.6 1.5 pick_down.1
  40.0 16.7 %collective-permute-done.4.refs_1_.rest_1_ = bf16[960,384]{1,0:T(8,128)(2,1)S(1)} collective-permute-done((bf16[960,384]{1,0:T(8,128)(2,1)S(1)}, bf16[960,384]{1,0:T(8,128)(2,1)S(1)}, u32[]{:S(2)}, u32[]{:S(2)}) %collective-permute-start.4) | collective-permute-done | bytes 737312 | tf_op jit(solution)/shard_map/ppermute | solution.py:861
  57.0 2.9 collective-permute-start.12
  59.9 1.6 collective-permute-start.11
  61.5 25.1 %collective-permute-done.12.refs_0_ = bf16[240,640]{1,0:T(8,128)(2,1)S(1)} collective-permute-done((bf16[240,640]{1,0:T(8,128)(2,1)S(1)}, bf16[240,640]{1,0:T(8,128)(2,1)S(1)}, u32[]{:S(2)}, u32[]{:S(2)}) %collective-permute-start.12) | collective-permute-done | bytes 307232 | tf_op jit(solution)/shard_map/ppermute | solution.py:867
  87.0 1.9 pad_maximum_fusion
  88.8 5.3 collective-permute-start
  95.3 13.5 %collective-permute-done.13.rest_3_ = bf16[240,640]{1,0:T(8,128)(2,1)S(1)} collective-permute-done((bf16[240,640]{1,0:T(8,128)(2,1)S(1)}, bf16[240,640]{1,0:T(8,128)(2,1)S(1)}, u32[]{:S(2)}, u32[]{:S(2)}) %collective-permute-start.13) | collective-permute-done | bytes 307232 | tf_op jit(solution)/shard_map/ppermute | solution.py:867
  114.9 1.5 collective-permute-start.16
  119.9 6.8 %pre.1 = (bf16[256,960]{1,0:T(8,128)(2,1)}, bf16[256,960]{1,0:T(8,128)(2,1)}, bf16[960,256]{1,0:T(8,128)(2,1)}, bf16[656,256]{1,0:T(8,128)(2,1)}) custom-call(s32[3]{0:T(128)} %copy-done.53, bf16[976,256]{1,0:T(8,128)(2,1)} %collective-permute-done.ht_ref, f32[1,960]{1,0:T(1,128)} %get-tuple-element.193.gain_ref.gain_a.rest_24_.rest_14_, ...), custom_call_target="tpu_custom_call" | custom-call | flops 1024 | bytes 1024 | tf_op jit(solution)/shard_map/pre/pallas_call | solution.py:118
  126.7 1.8 collective-permute-start.14
  128.5 6.8 %collective-permute-done.14.kv0 = bf16[656,256]{1,0:T(8,128)(2,1)S(1)} collective-permute-done((bf16[656,256]{1,0:T(8,128)(2,1)}, bf16[656,256]{1,0:T(8,128)(2,1)S(1)}, u32[]{:S(2)}, u32[]{:S(2)}) %collective-permute-start.14) | collective-permute-done | bytes 335904 | tf_op jit(solution)/shard_map/ppermute | solution.py:900
  137.1 7.5 %collective-permute-done.16.rest_0_.rest_9_ = bf16[960,640]{1,0:T(8,128)(2,1)} collective-permute-done((bf16[960,640]{1,0:T(8,128)(2,1)S(1)}, bf16[960,640]{1,0:T(8,128)(2,1)}, u32[]{:S(2)}, u32[]{:S(2)}) %collective-permute-start.16) | collective-permute-done | bytes 1228832 | tf_op jit(solution)/shard_map/ppermute | solution.py:861
  146.8 10.1 %attend.2 = (bf16[960,256]{1,0:T(8,128)(2,1)S(1)}, f32[15,256]{1,0:T(8,128)S(1)}) custom-call(bf16[960,256]{1,0:T(8,128)(2,1)S(1)} %copy-done.31, bf16[656,256]{1,0:T(8,128)(2,1)S(1)} %collective-permute-done.14.kv0, bf16[656,256]{1,0:T(8,128)(2,1)S(1)} %collective-permute-done.15.kv1, bf16[656,256]{1,0:T(8,128)(2,1)S(1)} %copy-done.9, ...), custom_call_target="tpu_custom_call" | custom-call | flops 1024 | bytes 1024 | tf_op jit(solution)/shard_map/attend/pallas_call | solution.py:171
  156.9 1.8 copy-done
  162.0 6.4 %collective-permute-done.19.rest_12_ = bf16[960,640]{1,0:T(8,128)(2,1)S(1)} collective-permute-done((bf16[960,640]{1,0:T(8,128)(2,1)S(1)}, bf16[960,640]{1,0:T(8,128)(2,1)S(1)}, u32[]{:S(2)}, u32[]{:S(2)}) %collective-permute-start.19) | collective-permute-done | bytes 1228832 | tf_op jit(solution)/shard_map/ppermute | solution.py:861
  168.6 1.8 collective-permute-done.21.rest_14_
  170.4 1.8 collective-permute-done.22.rest_15_
  174.0 20.3 %post.2 = (bf16[256,960]{1,0:T(8,128)(2,1)}, f32[256,960]{1,0:T(8,128)}, bf16[256,960]{1,0:T(8,128)(2,1)}, bf16[256,2560]{1,0:T(8,128)(2,1)}, bf16[256,2560]{1,0...) custom-call(s32[3]{0:T(128)} %copy-done.53, ...), custom_call_target="tpu_custom_call" | custom-call | flops 1024 | bytes 1024 | tf_op jit(solution)/shard_map/post/pallas_call | solution.py:305
  194.3 2.0 collective-permute-start.24
  196.4 6.7 %collective-permute-done.24.kv0 = bf16[656,256]{1,0:T(8,128)(2,1)S(1)} collective-permute-done((bf16[656,256]{1,0:T(8,128)(2,1)}, bf16[656,256]{1,0:T(8,128)(2,1)S(1)}, u32[]{:S(2)}, u32[]{:S(2)}) %collective-permute-start.24) | collective-permute-done | bytes 335904 | tf_op jit(solution)/shard_map/ppermute | solution.py:900
  208.3 10.6 %attend.3 = (bf16[960,256]{1,0:T(8,128)(2,1)S(1)}, f32[15,256]{1,0:T(8,128)S(1)}) custom-call(bf16[960,256]{1,0:T(8,128)(2,1)S(1)} %copy-done.34, bf16[656,256]{1,0:T(8,128)(2,1)S(1)} %collective-permute-done.24.kv0, bf16[656,256]{1,0:T(8,128)(2,1)S(1)} %collective-permute-done.25.kv1.refs_1_, bf16[656,256]{1,0:T(8,128)(2,1)S(1)} %copy-done.7, ...), custom_call_target="tpu_custom_call" | custom-call | flops 1024 | bytes 1024 | tf_op jit(solution)/shard_map/attend/pallas_call | solution.py:171
  220.5 17.8 %post.3 = (bf16[256,960]{1,0:T(8,128)(2,1)}, f32[256,960]{1,0:T(8,128)}, bf16[256,960]{1,0:T(8,128)(2,1)}, bf16[256,2560]{1,0:T(8,128)(2,1)}, bf16[256,2560]{1,0...) custom-call(s32[3]{0:T(128)} %copy-done.53, bf16[960,256]{1,0:T(8,128)(2,1)} %copy-done.61, ...), custom_call_target="tpu_custom_call" | custom-call | flops 1024 | bytes 1024 | tf_op jit(solution)/shard_map/post/pallas_call | solution.py:305
  238.3 1.5 collective-permute-start.34
  239.9 21.0 %back_start.1 = (bf16[256,960]{1,0:T(8,128)(2,1)}, bf16[256,2560]{1,0:T(8,128)(2,1)}, bf16[256,2560]{1,0:T(8,128)(2,1)}, f32[256,960]{1,0:T(8,128)}, bf16[3,256,...) custom-call(s32[3]{0:T(128)} %copy-done.53, bf16[960,384]{1,0:T(8,128)(2,1)} %bitcast.33, ...), custom_call_target="tpu_custom_call" | custom-call | flops 1024 | bytes 1024 | tf_op jit(solution)/shard_map/back_start/pallas_call | solution.py:457
  261.9 3.2 collective-permute-done.31.rest_0_.rest_2_
  269.0 12.6 %attend_back.2 = (bf16[3,256,384]{2,1,0:T(8,128)(2,1)S(1)}, bf16[3,256,384]{2,1,0:T(8,128)(2,1)S(1)}, f32[640,256]{1,0:T(8,128)S(1)}, bf16[640,256]{1,0:T(8,128)(2,1)S(1)}, f32[640,256]{1,0:T(8,128)S(1)}) custom-call(s32[3]{0:T(128)S(1)} %copy-done.54, bf16[3,256,384]{2,1,0:T(8,128)(2,1)S(1)} %copy-done.18, bf16[960,256]{1,0:T(8,128)(2,1)S(1)} %copy-done.34, ...), custom_call_target="tpu_custom_call" | custom-call | flops 1024 | bytes 1024 | tf_op jit(solution)/shard_map/attend_back/pallas_call | solution.py:224
  285.3 11.4 %collective-permute-done.36.refs_1_.rest_22_ = bf16[640,256]{1,0:T(8,128)(2,1)S(1)} collective-permute-done((bf16[640,256]{1,0:T(8,128)(2,1)S(1)}, bf16[640,256]{1,0:T(8,128)(2,1)S(1)}, u32[]{:S(2)}, u32[]{:S(2)}) %collective-permute-start.36) | collective-permute-done | bytes 327712 | tf_op jit(solution)/shard_map/ppermute | solution.py:909
  298.9 21.3 %back_join.1 = (bf16[256,384]{1,0:T(8,128)(2,1)}, bf16[256,384]{1,0:T(8,128)(2,1)}, bf16[256,384]{1,0:T(8,128)(2,1)}, f32[1,960]{1,0:T(1,128)}, bf16[256,960]{1,...) custom-call(s32[3]{0:T(128)} %copy-done.53, ...), custom_call_target="tpu_custom_call" | custom-call | flops 1024 | bytes 1024 | tf_op jit(solution)/shard_map/back_join/pallas_call | solution.py:457
  321.7 2.8 collective-permute-done.41.rest_0_.rest_18_
  326.7 12.8 %attend_back.3 = (bf16[3,256,384]{2,1,0:T(8,128)(2,1)S(1)}, bf16[3,256,384]{2,1,0:T(8,128)(2,1)S(1)}, f32[640,256]{1,0:T(8,128)S(1)}, bf16[640,256]{1,0:T(8,128)(2,1)S(1)}, f32[640,256]{1,0:T(8,128)S(1)}) custom-call(s32[3]{0:T(128)S(1)} %copy-done.55, bf16[3,256,384]{2,1,0:T(8,128)(2,1)S(1)} %copy-done.19, bf16[960,256]{1,0:T(8,128)(2,1)S(1)} %copy-done.32, ...), custom_call_target="tpu_custom_call" | custom-call | flops 1024 | bytes 1024 | tf_op jit(solution)/shard_map/attend_back/pallas_call | solution.py:224
  343.4 8.5 %grad_down.1.rest_8_ = bf16[4,480,640]{2,1,0:T(8,128)(2,1)} custom-call(s32[3]{0:T(128)} %copy-done.53, bf16[256,960]{1,0:T(8,128)(2,1)} %get-tuple-element.128.rest_0_, bf16[256,960]{1,0:T(8,128)(2,1)} %get-tuple-element.142.rest_1_, bf16[256,960]{1,0:T(8,128)(2,1)} %copy-done.78, bf16[256,960]{1,0:T(8,128)(2,1)} %collective-permute-done.45.rest_3_, ...), custom_call_target="tpu_custom_call" | custom-call | flops 1024 | bytes 1024 | tf_op jit(solution)/shard_map/grad_down/pallas_call | solution.py:525
  354.1 18.6 %collective-permute-done.43.rest_9_.rest_12_ = bf16[640,256]{1,0:T(8,128)(2,1)S(1)} collective-permute-done((bf16[640,256]{1,0:T(8,128)(2,1)S(1)}, bf16[640,256]{1,0:T(8,128)(2,1)S(1)}, u32[]{:S(2)}, u32[]{:S(2)}) %collective-permute-start.43) | collective-permute-done | bytes 327712 | tf_op jit(solution)/shard_map/ppermute | solution.py:909
  373.5 11.0 %grad_ffn.1 = (bf16[2,960,640]{2,1,0:T(8,128)(2,1)}, bf16[2,960,640]{2,1,0:T(8,128)(2,1)}) custom-call(s32[3]{0:T(128)} %copy-done.53, bf16[256,960]{1,0:T(8,128)(2,1)} %get-tuple-element.116.rest_0_, bf16[256,960]{1,0:T(8,128)(2,1)} %get-tuple-element.103.rest_1_, bf16[256,960]{1,0:T(8,128)(2,1)} %copy-done.30, bf16[256,960]{1,0:T(8,128)(2,1)} %copy-done.27, ...), custom_call_target="tpu_custom_call" | custom-call | flops 1024 | bytes 1024 | tf_op jit(solution)/shard_map/grad_ffn/pallas_call | solution.py:498
  384.5 1.6 collective-permute-start.47
  386.1 2.0 collective-permute-done.46.rest_18_.rest_17_
  388.9 6.5 %back_end.1 = (bf16[256,384]{1,0:T(8,128)(2,1)}, bf16[256,384]{1,0:T(8,128)(2,1)}, bf16[256,384]{1,0:T(8,128)(2,1)}, f32[1,960]{1,0:T(1,128)}, bf16[960,256]{1,0:T(8,128)(2,1)}) custom-call(s32[3]{0:T(128)} %copy-done.53, bf16[960,384]{1,0:T(8,128)(2,1)} %bitcast.35, bf16[960,384]{1,0:T(8,128)(2,1)} %copy-done.5, bf16[960,384]{1,0:T(8,128)(2,1)} %copy-done.6, ...), custom_call_target="tpu_custom_call" | custom-call | flops 1024 | bytes 1024 | tf_op jit(solution)/shard_map/back_end/pallas_call | solution.py:457
  398.5 10.8 %grad_attention.1 = (bf16[2,960,384]{2,1,0:T(8,128)(2,1)}, bf16[2,960,384]{2,1,0:T(8,128)(2,1)}) custom-call(s32[3]{0:T(128)} %copy-done.53, bf16[256,960]{1,0:T(8,128)(2,1)} %get-tuple-element.115.rest_0_, bf16[256,960]{1,0:T(8,128)(2,1)} %get-tuple-element.102.rest_1_, bf16[256,960]{1,0:T(8,128)(2,1)} %copy-done.28, bf16[256,960]{1,0:T(8,128)(2,1)} %copy-done.25, ...), custom_call_target="tpu_custom_call" | custom-call | flops 1024 | bytes 1024 | tf_op jit(solution)/shard_map/grad_attention/pallas_call | solution.py:576
  409.9 4.7 collective-permute-done.47.got_ref
  417.0 5.0 collective-permute-start.52
  422.1 19.4 %collective-permute-done.50.got_ref = bf16[2,960,384]{2,1,0:T(8,128)(2,1)S(1)} collective-permute-done((bf16[2,960,384]{2,1,0:T(8,128)(2,1)}, bf16[2,960,384]{2,1,0:T(8,128)(2,1)S(1)}, u32[]{:S(2)}, u32[]{:S(2)}) %collective-permute-start.50) | collective-permute-done | bytes 1474592 | tf_op jit(solution)/shard_map/ppermute | solution.py:861
  442.3 9.3 %collective-permute-start.51 = (bf16[960,384]{1,0:T(8,128)(2,1)S(1)}, bf16[960,384]{1,0:T(8,128)(2,1)S(1)}, u32[]{:S(2)}, u32[]{:S(2)}) collective-permute-start(bf16[960,384]{1,0:T(8,128)(2,1)S(1)} %get-tuple-element.160.rest_0_), channel_id=1, source_target_pairs={{0,16},{4,12},{8,24},{12,4},{16,0},{20,28},{24,8},{28,20},{1,17},{... | collective-permute-start | bytes 2211848 | tf_op jit(solution)/shard_map/ppermute | solution.py:861
  451.6 1.8 sum_second.2
  454.1 7.0 %collective-permute-done.51.got_ref = bf16[960,384]{1,0:T(8,128)(2,1)S(1)} collective-permute-done((bf16[960,384]{1,0:T(8,128)(2,1)S(1)}, bf16[960,384]{1,0:T(8,128)(2,1)S(1)}, u32[]{:S(2)}, u32[]{:S(2)}) %collective-permute-start.51) | collective-permute-done | bytes 737312 | tf_op jit(solution)/shard_map/ppermute | solution.py:861
  461.0 1.5 sum_second.3
  464.3 6.4 %collective-permute-done.54.got_ref = bf16[2,240,640]{2,1,0:T(8,128)(2,1)} collective-permute-done((bf16[2,240,640]{2,1,0:T(8,128)(2,1)}, bf16[2,240,640]{2,1,0:T(8,128)(2,1)}, u32[]{:S(2)}, u32[]{:S(2)}) %collective-permute-start.54) | collective-permute-done | bytes 614432 | tf_op jit(solution)/shard_map/ppermute | solution.py:867
  472.0 1.7 collective-permute-start.56
  475.8 3.0 collective-permute-start.55
  478.7 11.6 %collective-permute-done.57.got_ref = bf16[240,640]{1,0:T(8,128)(2,1)S(1)} collective-permute-done((bf16[240,640]{1,0:T(8,128)(2,1)S(1)}, bf16[240,640]{1,0:T(8,128)(2,1)S(1)}, u32[]{:S(2)}, u32[]{:S(2)}) %collective-permute-start.57) | collective-permute-done | bytes 307232 | tf_op jit(solution)/shard_map/ppermute | solution.py:867
  498.6 2.8 collective-permute-done.72.got_ref
  503.4 9.4 %collective-permute-done.59.rest_2_ = bf16[240,384]{1,0:T(8,128)(2,1)S(1)} collective-permute-done((bf16[240,384]{1,0:T(8,128)(2,1)S(1)}, bf16[240,384]{1,0:T(8,128)(2,1)S(1)}, u32[]{:S(2)}, u32[]{:S(2)}) %collective-permute-start.59) | collective-permute-done | bytes 184352 | tf_op jit(solution)/shard_map/ppermute | solution.py:861
  513.2 5.1 collective-permute-done.60.rest_3_
  520.7 1.5 collective-permute-start.74
  522.3 4.2 collective-permute-done.73.rest_1_
  529.5 3.1 lay.2
  533.7 1.7 copy-done.16
  535.4 2.4 lay.3
  540.1 2.8 lay_down.1
  (335 shorter events, 92.8 us)
Async XLA Ops:
  7.2 149.7 %all-gather.3.cloned.1.call-start = ((), (), s32[]{:S(2)}) async-start(), calls=%async_computation.2 | async-start | bytes 3072000 | tf_op jit(solution)/shard_map/all_gather | solution.py:953
  15.3 12.8 %collective-permute-start.2 = (bf16[240,384]{1,0:T(8,128)(2,1)S(1)}, bf16[240,384]{1,0:T(8,128)(2,1)S(1)}, u32[]{:S(2)}, u32[]{:S(2)}) collective-permute-start(bf16[240,384]{1,0:T(8,128)(2,1)S(1)} %pick_first.1.rest_0_), channel_id=1, source_target_pairs={{0,2},{1,3},{2,0},{3,1},{4,6},{5,7},{6,4},{7,5},{8,10},{9,11},{10,... | collective-permute-start | bytes 552968 | tf_op jit(solution)/shard_map/ppermute | solution.py:867
  19.4 9.4 %collective-permute-start.1 = (bf16[240,384]{1,0:T(8,128)(2,1)S(1)}, bf16[240,384]{1,0:T(8,128)(2,1)S(1)}, u32[]{:S(2)}, u32[]{:S(2)}) collective-permute-start(bf16[240,384]{1,0:T(8,128)(2,1)S(1)} %pick_first.1.rest_0_), channel_id=1, source_target_pairs={{0,1},{1,0},{2,3},{3,2},{4,5},{5,4},{6,7},{7,6},{8,9},{9,8},{10,11... | collective-permute-start | bytes 552968 | tf_op jit(solution)/shard_map/ppermute | solution.py:867
  37.1 425.4 %reduce-scatter.2.cloned.1.call-start = ((), (), s32[]{:S(2)}) async-start(), calls=%async_computation.1 | async-start | bytes 3072000 | tf_op jit(solution)/shard_map/reduce_scatter | solution.py:981
  37.2 19.5 %collective-permute-start.4 = (bf16[960,384]{1,0:T(8,128)(2,1)S(1)}, bf16[960,384]{1,0:T(8,128)(2,1)S(1)}, u32[]{:S(2)}, u32[]{:S(2)}) collective-permute-start(bf16[960,384]{1,0:T(8,128)(2,1)S(1)} %bitcast.27), channel_id=1, source_target_pairs={{0,8},{4,20},{8,0},{12,28},{16,24},{20,4},{24,16},{28,12},{1,9},{5... | collective-permute-start | bytes 2211848 | tf_op jit(solution)/shard_map/ppermute | solution.py:861
  38.5 48.2 %collective-permute-start.5 = (bf16[960,384]{1,0:T(8,128)(2,1)S(1)}, bf16[960,384]{1,0:T(8,128)(2,1)S(1)}, u32[]{:S(2)}, u32[]{:S(2)}) collective-permute-start(bf16[960,384]{1,0:T(8,128)(2,1)S(1)} %bitcast.28), channel_id=1, source_target_pairs={{0,16},{4,12},{8,24},{12,4},{16,0},{20,28},{24,8},{28,20},{1,17},{... | collective-permute-start | bytes 2211848 | tf_op jit(solution)/shard_map/ppermute | solution.py:861
  56.7 52.9 %collective-permute-start.6 = (bf16[960,384]{1,0:T(8,128)(2,1)S(1)}, bf16[960,384]{1,0:T(8,128)(2,1)}, u32[]{:S(2)}, u32[]{:S(2)}) collective-permute-start(bf16[960,384]{1,0:T(8,128)(2,1)S(1)} %collective-permute-done.4.refs_1_.rest_1_), channel_id=1, source_target_pairs={{0,16},{4,12},{8,24},{12,4},{16,0},{20,28},{24,8},{28,20},{1,17},{... | collective-permute-start | bytes 2211848 | tf_op jit(solution)/shard_map/ppermute | solution.py:861
  57.0 29.6 %collective-permute-start.12 = (bf16[240,640]{1,0:T(8,128)(2,1)S(1)}, bf16[240,640]{1,0:T(8,128)(2,1)S(1)}, u32[]{:S(2)}, u32[]{:S(2)}) collective-permute-start(bf16[240,640]{1,0:T(8,128)(2,1)S(1)} %pick.1.rest_4_.rest_0_), channel_id=1, source_target_pairs={{0,2},{1,3},{2,0},{3,1},{4,6},{5,7},{6,4},{7,5},{8,10},{9,11},{10,... | collective-permute-start | bytes 921608 | tf_op jit(solution)/shard_map/ppermute | solution.py:867
  59.9 56.5 %collective-permute-start.7 = (bf16[960,384]{1,0:T(8,128)(2,1)S(1)}, bf16[960,384]{1,0:T(8,128)(2,1)}, u32[]{:S(2)}, u32[]{:S(2)}) collective-permute-start(bf16[960,384]{1,0:T(8,128)(2,1)S(1)} %bitcast.29), channel_id=1, source_target_pairs={{0,4},{4,0},{8,12},{12,8},{16,20},{20,16},{24,28},{28,24},{1,5},{5... | collective-permute-start | bytes 2211848 | tf_op jit(solution)/shard_map/ppermute | solution.py:861
  59.9 34.2 %collective-permute-start.11 = (bf16[240,640]{1,0:T(8,128)(2,1)S(1)}, bf16[240,640]{1,0:T(8,128)(2,1)S(1)}, u32[]{:S(2)}, u32[]{:S(2)}) collective-permute-start(bf16[240,640]{1,0:T(8,128)(2,1)S(1)} %pick.1.rest_4_.rest_0_), channel_id=1, source_target_pairs={{0,1},{1,0},{2,3},{3,2},{4,5},{5,4},{6,7},{7,6},{8,9},{9,8},{10,11... | collective-permute-start | bytes 921608 | tf_op jit(solution)/shard_map/ppermute | solution.py:867
  86.6 22.2 %collective-permute-start.13 = (bf16[240,640]{1,0:T(8,128)(2,1)S(1)}, bf16[240,640]{1,0:T(8,128)(2,1)S(1)}, u32[]{:S(2)}, u32[]{:S(2)}) collective-permute-start(bf16[240,640]{1,0:T(8,128)(2,1)S(1)} %hold.5.rest_2_), channel_id=1, source_target_pairs={{0,1},{1,0},{2,3},{3,2},{4,5},{5,4},{6,7},{7,6},{8,9},{9,8},{10,11... | collective-permute-start | bytes 921608 | tf_op jit(solution)/shard_map/ppermute | solution.py:867
  88.8 26.0 %collective-permute-start = (bf16[976,256]{1,0:T(8,128)(2,1)}, bf16[976,256]{1,0:T(8,128)(2,1)}, u32[]{:S(2)}, u32[]{:S(2)}) collective-permute-start(bf16[976,256]{1,0:T(8,128)(2,1)} %pad_maximum_fusion), channel_id=1, source_target_pairs={{0,0},{1,4},{2,1},{3,5},{4,2},{5,6},{6,3},{7,7},{8,8},{9,12},{10,9... | collective-permute-start | bytes 1499144 | tf_op jit(solution)/shard_map/ppermute | solution.py:878
  94.9 25.0 %collective-permute-start.8 = (bf16[960,384]{1,0:T(8,128)(2,1)S(1)}, bf16[960,384]{1,0:T(8,128)(2,1)}, u32[]{:S(2)}, u32[]{:S(2)}) collective-permute-start(bf16[960,384]{1,0:T(8,128)(2,1)S(1)} %collective-permute-done.4.refs_1_.rest_1_), channel_id=1, source_target_pairs={{0,4},{4,0},{8,12},{12,8},{16,20},{20,16},{24,28},{28,24},{1,5},{5... | collective-permute-start | bytes 2211848 | tf_op jit(solution)/shard_map/ppermute | solution.py:861
  109.5 10.3 %collective-permute-start.9 = (bf16[960,384]{1,0:T(8,128)(2,1)S(1)}, bf16[960,384]{1,0:T(8,128)(2,1)}, u32[]{:S(2)}, u32[]{:S(2)}) collective-permute-start(bf16[960,384]{1,0:T(8,128)(2,1)S(1)} %collective-permute-done.5.refs_2_.rest_2_), channel_id=1, source_target_pairs={{0,4},{4,0},{8,12},{12,8},{16,20},{20,16},{24,28},{28,24},{1,5},{5... | collective-permute-start | bytes 2211848 | tf_op jit(solution)/shard_map/ppermute | solution.py:861
  109.5 10.3 %collective-permute-start.10 = (bf16[960,384]{1,0:T(8,128)(2,1)}, bf16[960,384]{1,0:T(8,128)(2,1)}, u32[]{:S(2)}, u32[]{:S(2)}) collective-permute-start(bf16[960,384]{1,0:T(8,128)(2,1)} %collective-permute-done.6.rest_3_), channel_id=1, source_target_pairs={{0,4},{4,0},{8,12},{12,8},{16,20},{20,16},{24,28},{28,24},{1,5},{5... | collective-permute-start | bytes 2211848 | tf_op jit(solution)/shard_map/ppermute | solution.py:861
  114.9 29.8 %collective-permute-start.16 = (bf16[960,640]{1,0:T(8,128)(2,1)S(1)}, bf16[960,640]{1,0:T(8,128)(2,1)}, u32[]{:S(2)}, u32[]{:S(2)}) collective-permute-start(bf16[960,640]{1,0:T(8,128)(2,1)S(1)} %bitcast.36), channel_id=1, source_target_pairs={{0,8},{4,20},{8,0},{12,28},{16,24},{20,4},{24,16},{28,12},{1,9},{5... | collective-permute-start | bytes 3686408 | tf_op jit(solution)/shard_map/ppermute | solution.py:861
  116.4 29.4 %collective-permute-start.17 = (bf16[960,640]{1,0:T(8,128)(2,1)S(1)}, bf16[960,640]{1,0:T(8,128)(2,1)}, u32[]{:S(2)}, u32[]{:S(2)}) collective-permute-start(bf16[960,640]{1,0:T(8,128)(2,1)S(1)} %bitcast.37), channel_id=1, source_target_pairs={{0,16},{4,12},{8,24},{12,4},{16,0},{20,28},{24,8},{28,20},{1,17},{... | collective-permute-start | bytes 3686408 | tf_op jit(solution)/shard_map/ppermute | solution.py:861
  126.7 8.6 %collective-permute-start.14 = (bf16[656,256]{1,0:T(8,128)(2,1)}, bf16[656,256]{1,0:T(8,128)(2,1)S(1)}, u32[]{:S(2)}, u32[]{:S(2)}) collective-permute-start(bf16[656,256]{1,0:T(8,128)(2,1)} %get-tuple-element.97.kv2.rest_18_), channel_id=1, source_target_pairs={{0,1},{2,3},{4,5},{6,7},{8,9},{10,11},{12,13},{14,15},{16,17},{18,... | collective-permute-start | bytes 1007624 | tf_op jit(solution)/shard_map/ppermute | solution.py:900
  136.3 9.4 %collective-permute-start.15 = (bf16[656,256]{1,0:T(8,128)(2,1)S(1)}, bf16[656,256]{1,0:T(8,128)(2,1)S(1)}, u32[]{:S(2)}, u32[]{:S(2)}) collective-permute-start(bf16[656,256]{1,0:T(8,128)(2,1)S(1)} %broadcast_select_fusion.1), channel_id=1, source_target_pairs={{0,4},{4,0},{8,12},{12,8},{16,20},{20,16},{24,28},{28,24},{1,5},{5... | collective-permute-start | bytes 1007624 | tf_op jit(solution)/shard_map/ppermute | solution.py:861
  144.6 17.0 %collective-permute-start.18 = (bf16[960,640]{1,0:T(8,128)(2,1)}, bf16[960,640]{1,0:T(8,128)(2,1)}, u32[]{:S(2)}, u32[]{:S(2)}) collective-permute-start(bf16[960,640]{1,0:T(8,128)(2,1)} %collective-permute-done.16.rest_0_.rest_9_), channel_id=1, source_target_pairs={{0,16},{4,12},{8,24},{12,4},{16,0},{20,28},{24,8},{28,20},{1,17},{... | collective-permute-start | bytes 3686408 | tf_op jit(solution)/shard_map/ppermute | solution.py:861
  160.2 11.9 %collective-permute-start.23 = (bf16[4,480,640]{2,1,0:T(8,128)(2,1)}, bf16[4,480,640]{2,1,0:T(8,128)(2,1)S(1)}, u32[]{:S(2)}, u32[]{:S(2)}) collective-permute-start(bf16[4,480,640]{2,1,0:T(8,128)(2,1)} %copy-done.1), channel_id=1, source_target_pairs={{0,4},{4,0},{8,12},{12,8},{16,20},{20,16},{24,28},{28,24},{1,5},{5... | collective-permute-start | bytes 7372808 | tf_op jit(solution)/shard_map/ppermute | solution.py:861
  161.0 7.5 %collective-permute-start.19 = (bf16[960,640]{1,0:T(8,128)(2,1)S(1)}, bf16[960,640]{1,0:T(8,128)(2,1)S(1)}, u32[]{:S(2)}, u32[]{:S(2)}) collective-permute-start(bf16[960,640]{1,0:T(8,128)(2,1)S(1)} %bitcast.43), channel_id=1, source_target_pairs={{0,4},{4,0},{8,12},{12,8},{16,20},{20,16},{24,28},{28,24},{1,5},{5... | collective-permute-start | bytes 3686408 | tf_op jit(solution)/shard_map/ppermute | solution.py:861
  161.0 7.7 %collective-permute-start.20 = (bf16[960,640]{1,0:T(8,128)(2,1)}, bf16[960,640]{1,0:T(8,128)(2,1)S(1)}, u32[]{:S(2)}, u32[]{:S(2)}) collective-permute-start(bf16[960,640]{1,0:T(8,128)(2,1)} %collective-permute-done.16.rest_0_.rest_9_), channel_id=1, source_target_pairs={{0,4},{4,0},{8,12},{12,8},{16,20},{20,16},{24,28},{28,24},{1,5},{5... | collective-permute-start | bytes 3686408 | tf_op jit(solution)/shard_map/ppermute | solution.py:861
  161.5 8.9 %collective-permute-start.21 = (bf16[960,640]{1,0:T(8,128)(2,1)}, bf16[960,640]{1,0:T(8,128)(2,1)S(1)}, u32[]{:S(2)}, u32[]{:S(2)}) collective-permute-start(bf16[960,640]{1,0:T(8,128)(2,1)} %collective-permute-done.17.rest_1_.rest_10_), channel_id=1, source_target_pairs={{0,4},{4,0},{8,12},{12,8},{16,20},{20,16},{24,28},{28,24},{1,5},{5... | collective-permute-start | bytes 3686408 | tf_op jit(solution)/shard_map/ppermute | solution.py:861
  161.7 10.5 %collective-permute-start.22 = (bf16[960,640]{1,0:T(8,128)(2,1)}, bf16[960,640]{1,0:T(8,128)(2,1)S(1)}, u32[]{:S(2)}, u32[]{:S(2)}) collective-permute-start(bf16[960,640]{1,0:T(8,128)(2,1)} %collective-permute-done.18.rest_11_), channel_id=1, source_target_pairs={{0,4},{4,0},{8,12},{12,8},{16,20},{20,16},{24,28},{28,24},{1,5},{5... | collective-permute-start | bytes 3686408 | tf_op jit(solution)/shard_map/ppermute | solution.py:861
  194.3 8.8 %collective-permute-start.24 = (bf16[656,256]{1,0:T(8,128)(2,1)}, bf16[656,256]{1,0:T(8,128)(2,1)S(1)}, u32[]{:S(2)}, u32[]{:S(2)}) collective-permute-start(bf16[656,256]{1,0:T(8,128)(2,1)} %get-tuple-element.101.kv2.rest_18_), channel_id=1, source_target_pairs={{0,1},{2,3},{4,5},{6,7},{8,9},{10,11},{12,13},{14,15},{16,17},{18,... | collective-permute-start | bytes 1007624 | tf_op jit(solution)/shard_map/ppermute | solution.py:900
  196.3 12.0 %collective-permute-start.29 = (bf16[256,2560]{1,0:T(8,128)(2,1)}, bf16[256,2560]{1,0:T(8,128)(2,1)S(1)}, u32[]{:S(2)}, u32[]{:S(2)}) collective-permute-start(bf16[256,2560]{1,0:T(8,128)(2,1)} %get-tuple-element.105.rest_5_), channel_id=1, source_target_pairs={{0,4},{4,0},{8,12},{12,8},{16,20},{20,16},{24,28},{28,24},{1,5},{5... | collective-permute-start | bytes 3932168 | tf_op jit(solution)/shard_map/ppermute | solution.py:861
  205.8 13.9 %collective-permute-start.30 = (bf16[960,256]{1,0:T(8,128)(2,1)S(1)}, bf16[960,256]{1,0:T(8,128)(2,1)S(1)}, u32[]{:S(2)}, u32[]{:S(2)}) collective-permute-start(bf16[960,256]{1,0:T(8,128)(2,1)S(1)} %hold.7), channel_id=1, source_target_pairs={{0,0},{1,4},{2,1},{3,5},{4,2},{5,6},{6,3},{7,7},{8,8},{9,12},{10,9... | collective-permute-start | bytes 1474568 | tf_op jit(solution)/shard_map/ppermute | solution.py:878
  238.3 28.1 %collective-permute-start.34 = (bf16[256,2560]{1,0:T(8,128)(2,1)}, bf16[256,2560]{1,0:T(8,128)(2,1)S(1)}, u32[]{:S(2)}, u32[]{:S(2)}) collective-permute-start(bf16[256,2560]{1,0:T(8,128)(2,1)} %get-tuple-element.118.rest_4_), channel_id=1, source_target_pairs={{0,4},{4,0},{8,12},{12,8},{16,20},{20,16},{24,28},{28,24},{1,5},{5... | collective-permute-start | bytes 3932168 | tf_op jit(solution)/shard_map/ppermute | solution.py:861
  260.8 36.6 %collective-permute-start.40 = (bf16[256,2560]{1,0:T(8,128)(2,1)}, bf16[256,2560]{1,0:T(8,128)(2,1)S(1)}, u32[]{:S(2)}, u32[]{:S(2)}) collective-permute-start(bf16[256,2560]{1,0:T(8,128)(2,1)} %get-tuple-element.129), channel_id=1, source_target_pairs={{0,4},{4,0},{8,12},{12,8},{16,20},{20,16},{24,28},{28,24},{1,5},{5... | collective-permute-start | bytes 3932168 | tf_op jit(solution)/shard_map/ppermute | solution.py:861
  281.9 15.6 %collective-permute-start.38 = (bf16[3,256,384]{2,1,0:T(8,128)(2,1)S(1)}, bf16[3,256,384]{2,1,0:T(8,128)(2,1)S(1)}, u32[]{:S(2)}, u32[]{:S(2)}) collective-permute-start(bf16[3,256,384]{2,1,0:T(8,128)(2,1)S(1)} %get-tuple-element.127), channel_id=1, source_target_pairs={{0,4},{4,0},{8,12},{12,8},{16,20},{20,16},{24,28},{28,24},{1,5},{5... | collective-permute-start | bytes 1769480 | tf_op jit(solution)/shard_map/ppermute | solution.py:861
  282.2 15.1 %collective-permute-start.39 = (bf16[256,960]{1,0:T(8,128)(2,1)S(1)}, bf16[256,960]{1,0:T(8,128)(2,1)S(1)}, u32[]{:S(2)}, u32[]{:S(2)}) collective-permute-start(bf16[256,960]{1,0:T(8,128)(2,1)S(1)} %copy-done.84), channel_id=1, source_target_pairs={{0,4},{4,0},{8,12},{12,8},{16,20},{20,16},{24,28},{28,24},{1,5},{5... | collective-permute-start | bytes 1474568 | tf_op jit(solution)/shard_map/ppermute | solution.py:861
  284.0 12.7 %collective-permute-start.36 = (bf16[640,256]{1,0:T(8,128)(2,1)S(1)}, bf16[640,256]{1,0:T(8,128)(2,1)S(1)}, u32[]{:S(2)}, u32[]{:S(2)}) collective-permute-start(bf16[640,256]{1,0:T(8,128)(2,1)S(1)} %far_sum.2), channel_id=1, source_target_pairs={{1,0},{3,2},{5,4},{7,6},{9,8},{11,10},{13,12},{15,14},{17,16},{19,... | collective-permute-start | bytes 983048 | tf_op jit(solution)/shard_map/ppermute | solution.py:909
  296.7 27.8 %collective-permute-start.37 = (bf16[960,256]{1,0:T(8,128)(2,1)S(1)}, bf16[960,256]{1,0:T(8,128)(2,1)S(1)}, u32[]{:S(2)}, u32[]{:S(2)}) collective-permute-start(bf16[960,256]{1,0:T(8,128)(2,1)S(1)} %hold.8), channel_id=1, source_target_pairs={{0,0},{4,1},{1,2},{5,3},{2,4},{6,5},{3,6},{7,7},{8,8},{12,9},{9,10... | collective-permute-start | bytes 1474568 | tf_op jit(solution)/shard_map/ppermute | solution.py:878
  320.1 52.6 %collective-permute-start.44 = (bf16[256,2560]{1,0:T(8,128)(2,1)}, bf16[256,2560]{1,0:T(8,128)(2,1)}, u32[]{:S(2)}, u32[]{:S(2)}) collective-permute-start(bf16[256,2560]{1,0:T(8,128)(2,1)} %get-tuple-element.141), channel_id=1, source_target_pairs={{0,4},{4,0},{8,12},{12,8},{16,20},{20,16},{24,28},{28,24},{1,5},{5... | collective-permute-start | bytes 3932168 | tf_op jit(solution)/shard_map/ppermute | solution.py:861
  321.3 22.1 %collective-permute-start.45 = (bf16[256,960]{1,0:T(8,128)(2,1)}, bf16[256,960]{1,0:T(8,128)(2,1)}, u32[]{:S(2)}, u32[]{:S(2)}) collective-permute-start(bf16[256,960]{1,0:T(8,128)(2,1)} %get-tuple-element.142.rest_1_), channel_id=1, source_target_pairs={{0,4},{4,0},{8,12},{12,8},{16,20},{20,16},{24,28},{28,24},{1,5},{5... | collective-permute-start | bytes 1474568 | tf_op jit(solution)/shard_map/ppermute | solution.py:861
  352.8 19.9 %collective-permute-start.43 = (bf16[640,256]{1,0:T(8,128)(2,1)S(1)}, bf16[640,256]{1,0:T(8,128)(2,1)S(1)}, u32[]{:S(2)}, u32[]{:S(2)}) collective-permute-start(bf16[640,256]{1,0:T(8,128)(2,1)S(1)} %copy-done.42), channel_id=1, source_target_pairs={{1,0},{3,2},{5,4},{7,6},{9,8},{11,10},{13,12},{15,14},{17,16},{19,... | collective-permute-start | bytes 983048 | tf_op jit(solution)/shard_map/ppermute | solution.py:909
  384.5 30.1 %collective-permute-start.47 = (bf16[2,960,640]{2,1,0:T(8,128)(2,1)}, bf16[2,960,640]{2,1,0:T(8,128)(2,1)S(1)}, u32[]{:S(2)}, u32[]{:S(2)}) collective-permute-start(bf16[2,960,640]{2,1,0:T(8,128)(2,1)} %get-tuple-element.143.rest_17_), channel_id=1, source_target_pairs={{0,8},{4,20},{8,0},{12,28},{16,24},{20,4},{24,16},{28,12},{1,9},{5... | collective-permute-start | bytes 7372808 | tf_op jit(solution)/shard_map/ppermute | solution.py:861
  409.2 32.2 %collective-permute-start.50 = (bf16[2,960,384]{2,1,0:T(8,128)(2,1)}, bf16[2,960,384]{2,1,0:T(8,128)(2,1)S(1)}, u32[]{:S(2)}, u32[]{:S(2)}) collective-permute-start(bf16[2,960,384]{2,1,0:T(8,128)(2,1)} %get-tuple-element.156.rest_0_), channel_id=1, source_target_pairs={{0,8},{4,20},{8,0},{12,28},{16,24},{20,4},{24,16},{28,12},{1,9},{5... | collective-permute-start | bytes 4423688 | tf_op jit(solution)/shard_map/ppermute | solution.py:861
  417.0 34.5 %collective-permute-start.52 = (bf16[960,640]{1,0:T(8,128)(2,1)S(1)}, bf16[960,640]{1,0:T(8,128)(2,1)S(1)}, u32[]{:S(2)}, u32[]{:S(2)}) collective-permute-start(bf16[960,640]{1,0:T(8,128)(2,1)S(1)} %get-tuple-element.157.refs_1_.rest_0_), channel_id=1, source_target_pairs={{0,16},{4,12},{8,24},{12,4},{16,0},{20,28},{24,8},{28,20},{1,17},{... | collective-permute-start | bytes 3686408 | tf_op jit(solution)/shard_map/ppermute | solution.py:861
  442.3 18.7 %collective-permute-start.51 = (bf16[960,384]{1,0:T(8,128)(2,1)S(1)}, bf16[960,384]{1,0:T(8,128)(2,1)S(1)}, u32[]{:S(2)}, u32[]{:S(2)}) collective-permute-start(bf16[960,384]{1,0:T(8,128)(2,1)S(1)} %get-tuple-element.160.rest_0_), channel_id=1, source_target_pairs={{0,16},{4,12},{8,24},{12,4},{16,0},{20,28},{24,8},{28,20},{1,17},{... | collective-permute-start | bytes 2211848 | tf_op jit(solution)/shard_map/ppermute | solution.py:861
  453.4 17.4 %collective-permute-start.54 = (bf16[2,240,640]{2,1,0:T(8,128)(2,1)}, bf16[2,240,640]{2,1,0:T(8,128)(2,1)}, u32[]{:S(2)}, u32[]{:S(2)}) collective-permute-start(bf16[2,240,640]{2,1,0:T(8,128)(2,1)} %get-tuple-element.162.rest_0_), channel_id=1, source_target_pairs={{0,1},{1,0},{2,3},{3,2},{4,5},{5,4},{6,7},{7,6},{8,9},{9,8},{10,11... | collective-permute-start | bytes 1843208 | tf_op jit(solution)/shard_map/ppermute | solution.py:867
  453.4 11.0 %collective-permute-start.49 = (bf16[960,256]{1,0:T(8,128)(2,1)S(1)}, bf16[960,256]{1,0:T(8,128)(2,1)S(1)}, u32[]{:S(2)}, u32[]{:S(2)}) collective-permute-start(bf16[960,256]{1,0:T(8,128)(2,1)S(1)} %hold.9), channel_id=1, source_target_pairs={{0,0},{4,1},{1,2},{5,3},{2,4},{6,5},{3,6},{7,7},{8,8},{12,9},{9,10... | collective-permute-start | bytes 1474568 | tf_op jit(solution)/shard_map/ppermute | solution.py:878
  462.6 12.1 %collective-permute-start.53 = (bf16[2,240,384]{2,1,0:T(8,128)(2,1)}, bf16[2,240,384]{2,1,0:T(8,128)(2,1)}, u32[]{:S(2)}, u32[]{:S(2)}) collective-permute-start(bf16[2,240,384]{2,1,0:T(8,128)(2,1)} %get-tuple-element.164.rest_0_), channel_id=1, source_target_pairs={{0,1},{1,0},{2,3},{3,2},{4,5},{5,4},{6,7},{7,6},{8,9},{9,8},{10,11... | collective-permute-start | bytes 1105928 | tf_op jit(solution)/shard_map/ppermute | solution.py:867
  472.0 18.4 %collective-permute-start.57 = (bf16[240,640]{1,0:T(8,128)(2,1)S(1)}, bf16[240,640]{1,0:T(8,128)(2,1)S(1)}, u32[]{:S(2)}, u32[]{:S(2)}) collective-permute-start(bf16[240,640]{1,0:T(8,128)(2,1)S(1)} %get-tuple-element.167.rest_0_), channel_id=1, source_target_pairs={{0,2},{1,3},{2,0},{3,1},{4,6},{5,7},{6,4},{7,5},{8,10},{9,11},{10,... | collective-permute-start | bytes 921608 | tf_op jit(solution)/shard_map/ppermute | solution.py:867
  472.0 18.9 %collective-permute-start.56 = (bf16[2,120,640]{2,1,0:T(8,128)(2,1)S(1)}, bf16[2,120,640]{2,1,0:T(8,128)(2,1)S(1)}, u32[]{:S(2)}, u32[]{:S(2)}) collective-permute-start(bf16[2,120,640]{2,1,0:T(8,128)(2,1)S(1)} %get-tuple-element.166.rest_0_), channel_id=1, source_target_pairs={{0,8},{4,20},{8,0},{12,28},{16,24},{20,4},{24,16},{28,12},{1,9},{5... | collective-permute-start | bytes 921608 | tf_op jit(solution)/shard_map/ppermute | solution.py:861
  475.8 17.1 %collective-permute-start.55 = (bf16[240,384]{1,0:T(8,128)(2,1)S(1)}, bf16[240,384]{1,0:T(8,128)(2,1)S(1)}, u32[]{:S(2)}, u32[]{:S(2)}) collective-permute-start(bf16[240,384]{1,0:T(8,128)(2,1)S(1)} %get-tuple-element.169.rest_0_), channel_id=1, source_target_pairs={{0,2},{1,3},{2,0},{3,1},{4,6},{5,7},{6,4},{7,5},{8,10},{9,11},{10,... | collective-permute-start | bytes 552968 | tf_op jit(solution)/shard_map/ppermute | solution.py:867
  493.5 8.5 %collective-permute-start.58 = (bf16[240,384]{1,0:T(8,128)(2,1)S(1)}, bf16[240,384]{1,0:T(8,128)(2,1)S(1)}, u32[]{:S(2)}, u32[]{:S(2)}) collective-permute-start(bf16[240,384]{1,0:T(8,128)(2,1)S(1)} %sum_two.4.rest_0_), channel_id=1, source_target_pairs={{0,8},{4,20},{8,0},{12,28},{16,24},{20,4},{24,16},{28,12},{1,9},{5... | collective-permute-start | bytes 552968 | tf_op jit(solution)/shard_map/ppermute | solution.py:861
  494.4 6.9 %collective-permute-start.72 = (bf16[120,640]{1,0:T(8,128)(2,1)S(1)}, bf16[120,640]{1,0:T(8,128)(2,1)S(1)}, u32[]{:S(2)}, u32[]{:S(2)}) collective-permute-start(bf16[120,640]{1,0:T(8,128)(2,1)S(1)} %get-tuple-element.172.rest_0_), channel_id=1, source_target_pairs={{0,16},{4,12},{8,24},{12,4},{16,0},{20,28},{24,8},{28,20},{1,17},{... | collective-permute-start | bytes 460808 | tf_op jit(solution)/shard_map/ppermute | solution.py:861
  495.1 23.5 %collective-permute-start.65 = (bf16[240,640]{1,0:T(8,128)(2,1)S(1)}, bf16[240,640]{1,0:T(8,128)(2,1)S(1)}, u32[]{:S(2)}, u32[]{:S(2)}) collective-permute-start(bf16[240,640]{1,0:T(8,128)(2,1)S(1)} %sum_two.3.rest_0_), channel_id=1, source_target_pairs={{0,8},{4,20},{8,0},{12,28},{16,24},{20,4},{24,16},{28,12},{1,9},{5... | collective-permute-start | bytes 921608 | tf_op jit(solution)/shard_map/ppermute | solution.py:861
  496.2 22.6 %collective-permute-start.66 = (bf16[240,640]{1,0:T(8,128)(2,1)S(1)}, bf16[240,640]{1,0:T(8,128)(2,1)S(1)}, u32[]{:S(2)}, u32[]{:S(2)}) collective-permute-start(bf16[240,640]{1,0:T(8,128)(2,1)S(1)} %sum_two.3.rest_0_), channel_id=1, source_target_pairs={{0,16},{4,12},{8,24},{12,4},{16,0},{20,28},{24,8},{28,20},{1,17},{... | collective-permute-start | bytes 921608 | tf_op jit(solution)/shard_map/ppermute | solution.py:861
  497.6 21.5 %collective-permute-start.67 = (bf16[240,640]{1,0:T(8,128)(2,1)S(1)}, bf16[240,640]{1,0:T(8,128)(2,1)S(1)}, u32[]{:S(2)}, u32[]{:S(2)}) collective-permute-start(bf16[240,640]{1,0:T(8,128)(2,1)S(1)} %sum_two.3.rest_0_), channel_id=1, source_target_pairs={{0,24},{4,28},{8,16},{12,20},{16,8},{20,12},{24,0},{28,4},{1,25},{... | collective-permute-start | bytes 921608 | tf_op jit(solution)/shard_map/ppermute | solution.py:861
  501.4 11.4 %collective-permute-start.59 = (bf16[240,384]{1,0:T(8,128)(2,1)S(1)}, bf16[240,384]{1,0:T(8,128)(2,1)S(1)}, u32[]{:S(2)}, u32[]{:S(2)}) collective-permute-start(bf16[240,384]{1,0:T(8,128)(2,1)S(1)} %sum_two.4.rest_0_), channel_id=1, source_target_pairs={{0,16},{4,12},{8,24},{12,4},{16,0},{20,28},{24,8},{28,20},{1,17},{... | collective-permute-start | bytes 552968 | tf_op jit(solution)/shard_map/ppermute | solution.py:861
  502.0 16.3 %collective-permute-start.60 = (bf16[240,384]{1,0:T(8,128)(2,1)S(1)}, bf16[240,384]{1,0:T(8,128)(2,1)S(1)}, u32[]{:S(2)}, u32[]{:S(2)}) collective-permute-start(bf16[240,384]{1,0:T(8,128)(2,1)S(1)} %sum_two.4.rest_0_), channel_id=1, source_target_pairs={{0,24},{4,28},{8,16},{12,20},{16,8},{20,12},{24,0},{28,4},{1,25},{... | collective-permute-start | bytes 552968 | tf_op jit(solution)/shard_map/ppermute | solution.py:861
  512.8 7.1 %collective-permute-start.61 = (bf16[240,384]{1,0:T(8,128)(2,1)S(1)}, bf16[240,384]{1,0:T(8,128)(2,1)S(1)}, u32[]{:S(2)}, u32[]{:S(2)}) collective-permute-start(bf16[240,384]{1,0:T(8,128)(2,1)S(1)} %sum_two.4.rest_0_), channel_id=1, source_target_pairs={{0,4},{4,0},{8,12},{12,8},{16,20},{20,16},{24,28},{28,24},{1,5},{5... | collective-permute-start | bytes 552968 | tf_op jit(solution)/shard_map/ppermute | solution.py:861
  518.6 9.3 %collective-permute-start.69 = (bf16[240,640]{1,0:T(8,128)(2,1)S(1)}, bf16[240,640]{1,0:T(8,128)(2,1)S(1)}, u32[]{:S(2)}, u32[]{:S(2)}) collective-permute-start(bf16[240,640]{1,0:T(8,128)(2,1)S(1)} %collective-permute-done.65.rest_1_), channel_id=1, source_target_pairs={{0,4},{4,0},{8,12},{12,8},{16,20},{20,16},{24,28},{28,24},{1,5},{5... | collective-permute-start | bytes 921608 | tf_op jit(solution)/shard_map/ppermute | solution.py:861
  518.8 9.1 %collective-permute-start.70 = (bf16[240,640]{1,0:T(8,128)(2,1)S(1)}, bf16[240,640]{1,0:T(8,128)(2,1)S(1)}, u32[]{:S(2)}, u32[]{:S(2)}) collective-permute-start(bf16[240,640]{1,0:T(8,128)(2,1)S(1)} %collective-permute-done.66.rest_2_), channel_id=1, source_target_pairs={{0,4},{4,0},{8,12},{12,8},{16,20},{20,16},{24,28},{28,24},{1,5},{5... | collective-permute-start | bytes 921608 | tf_op jit(solution)/shard_map/ppermute | solution.py:861
  519.1 9.3 %collective-permute-start.71 = (bf16[240,640]{1,0:T(8,128)(2,1)S(1)}, bf16[240,640]{1,0:T(8,128)(2,1)S(1)}, u32[]{:S(2)}, u32[]{:S(2)}) collective-permute-start(bf16[240,640]{1,0:T(8,128)(2,1)S(1)} %collective-permute-done.67.rest_3_), channel_id=1, source_target_pairs={{0,4},{4,0},{8,12},{12,8},{16,20},{20,16},{24,28},{28,24},{1,5},{5... | collective-permute-start | bytes 921608 | tf_op jit(solution)/shard_map/ppermute | solution.py:861
  519.9 6.6 %collective-permute-start.73 = (bf16[120,640]{1,0:T(8,128)(2,1)S(1)}, bf16[120,640]{1,0:T(8,128)(2,1)S(1)}, u32[]{:S(2)}, u32[]{:S(2)}) collective-permute-start(bf16[120,640]{1,0:T(8,128)(2,1)S(1)} %sum_two.5.rest_8_.rest_0_), channel_id=1, source_target_pairs={{0,8},{4,20},{8,0},{12,28},{16,24},{20,4},{24,16},{28,12},{1,9},{5... | collective-permute-start | bytes 460808 | tf_op jit(solution)/shard_map/ppermute | solution.py:861
  520.7 11.9 %collective-permute-start.74 = (bf16[120,640]{1,0:T(8,128)(2,1)S(1)}, bf16[120,640]{1,0:T(8,128)(2,1)S(1)}, u32[]{:S(2)}, u32[]{:S(2)}) collective-permute-start(bf16[120,640]{1,0:T(8,128)(2,1)S(1)} %sum_two.5.rest_8_.rest_0_), channel_id=1, source_target_pairs={{0,16},{4,12},{8,24},{12,4},{16,0},{20,28},{24,8},{28,20},{1,17},{... | collective-permute-start | bytes 460808 | tf_op jit(solution)/shard_map/ppermute | solution.py:861
  526.5 6.6 %collective-permute-start.75 = (bf16[120,640]{1,0:T(8,128)(2,1)S(1)}, bf16[120,640]{1,0:T(8,128)(2,1)S(1)}, u32[]{:S(2)}, u32[]{:S(2)}) collective-permute-start(bf16[120,640]{1,0:T(8,128)(2,1)S(1)} %sum_two.5.rest_8_.rest_0_), channel_id=1, source_target_pairs={{0,24},{4,28},{8,16},{12,20},{16,8},{20,12},{24,0},{28,4},{1,25},{... | collective-permute-start | bytes 460808 | tf_op jit(solution)/shard_map/ppermute | solution.py:861
  532.6 7.4 %collective-permute-start.76 = (bf16[120,640]{1,0:T(8,128)(2,1)S(1)}, bf16[120,640]{1,0:T(8,128)(2,1)S(1)}, u32[]{:S(2)}, u32[]{:S(2)}) collective-permute-start(bf16[120,640]{1,0:T(8,128)(2,1)S(1)} %sum_two.5.rest_8_.rest_0_), channel_id=1, source_target_pairs={{0,4},{4,0},{8,12},{12,8},{16,20},{20,16},{24,28},{28,24},{1,5},{5... | collective-permute-start | bytes 460808 | tf_op jit(solution)/shard_map/ppermute | solution.py:861
  533.1 7.0 %collective-permute-start.77 = (bf16[120,640]{1,0:T(8,128)(2,1)S(1)}, bf16[120,640]{1,0:T(8,128)(2,1)}, u32[]{:S(2)}, u32[]{:S(2)}) collective-permute-start(bf16[120,640]{1,0:T(8,128)(2,1)S(1)} %collective-permute-done.73.rest_1_), channel_id=1, source_target_pairs={{0,4},{4,0},{8,12},{12,8},{16,20},{20,16},{24,28},{28,24},{1,5},{5... | collective-permute-start | bytes 460808 | tf_op jit(solution)/shard_map/ppermute | solution.py:861
  533.1 6.9 %collective-permute-start.78 = (bf16[120,640]{1,0:T(8,128)(2,1)S(1)}, bf16[120,640]{1,0:T(8,128)(2,1)}, u32[]{:S(2)}, u32[]{:S(2)}) collective-permute-start(bf16[120,640]{1,0:T(8,128)(2,1)S(1)} %collective-permute-done.74.rest_2_), channel_id=1, source_target_pairs={{0,4},{4,0},{8,12},{12,8},{16,20},{20,16},{24,28},{28,24},{1,5},{5... | collective-permute-start | bytes 460808 | tf_op jit(solution)/shard_map/ppermute | solution.py:861
  (105 other events, 1122.8 us)
Sparse Core Ops, SparseCore 0:
  37.3 73.2 all-gather.2
  352.0 54.0 reduce-scatter.1

commit v10 on v9

--- a/solution.py
+++ b/solution.py
@@ -10,6 +10,7 @@
 eps = 1e-05
 HEADS, KV_HEADS, HEAD_DIM, GROUP, KVW = 15, 5, 64, 3, 320
 IDS = 16
+ROWS = 128
 PIECE = 384
 LIMIT = 58 << 20
 WHOLE = pl.BlockSpec(memory_space=pltpu.VMEM)
@@ -233,12 +234,34 @@
     )(sc, p, q, *kvs, lse, do, cos, sin, *after)
 
 
-def fetch_ffn(mine_b, other_b, down, wb, wd, sem_b, sem_d, core, chip):
-    fetch(mine_b, other_b, wb, sem_b, core, chip)
-    half = down[0].shape[1]
-    for c, part in ((core, down[0]), (1 - core, down[1])):
-        rows = pl.ds(pl.multiple_of(c * half, half), half)
-        pltpu.make_async_copy(part, wd.at[:, rows], sem_d).start()
+def down_rows(kind, chip, width):
+    return jnp.minimum((kind * 4 + chip) * ROWS, width - ROWS)
+
+
+def fetch_ffn(mine, other, wb, wd, sem_b, sem_d, core, chip):
+    rows, width = wb.shape[3], wd.shape[1]
+    last = width % ROWS
+    for kind, pieces in ((core, mine), (1 - core, other)):
+        for who, piece in zip(whose(kind), pieces):
+            at = chip ^ who
+            pltpu.make_async_copy(piece.at[:, :rows], wb.at[kind, at], sem_b.at[kind, at]).start()
+    for kind, pieces in ((core, mine), (1 - core, other)):
+        for who, piece in zip(whose(kind), pieces):
+            at = kind * 4 + (chip ^ who)
+
+            @pl.when(at < width // ROWS)
+            def _():
+                into = wd.at[:, pl.ds(pl.multiple_of(at * ROWS, ROWS), ROWS)]
+                pltpu.make_async_copy(piece.at[:, rows:], into, sem_d).start()
+
+            @pl.when(at == width // ROWS)
+            def _():
+                pltpu.make_async_copy(piece.at[:, rows + ROWS - last :], wd.at[:, width - last :], sem_d).start()
+
+
+def whole(wb, c, m):
+    _, rows, n = wb.shape[2:]
+    return wb[c, m].reshape(4 * rows, n)
 
 
 def arrived_down(wd, sem_d):
@@ -247,7 +270,7 @@
 
 def scratch_ffn(width, n):
     return [
-        pltpu.VMEM((2, 4, width, n), bf16),
+        pltpu.VMEM((2, 4, 4, width // 4, n), bf16),
         pltpu.SemaphoreType.DMA((2, 4)),
         pltpu.VMEM((4, width, n), bf16),
         pltpu.SemaphoreType.DMA,
@@ -256,13 +279,13 @@
 
 def post_kernel(last, after, sc, ot_ref, h_ref, gain_ref, gain_a, cos_ref, sin_ref, *rest):
     mine_a, other_a, mine_b, other_b = rest[:4], rest[4:8], rest[8:12], rest[12:16]
-    down, ids_ref, rest = rest[16:18], rest[18], rest[19 + after :]
+    ids_ref, rest = rest[16], rest[17 + after :]
     o_ref, h1_ref, b_ref, gate_ref, up_ref, z_ref, next_ref = rest[:7]
     more, rest = rest[7 : 7 + (0 if last else 3)], rest[7 + (0 if last else 3) :]
     wa, sem_a, wb, sem_b, wd, sem_d = rest
     core, chip = sc[0], sc[1]
     fetch(mine_a, other_a, wa, sem_a, core, chip)
-    fetch_ffn(mine_b, other_b, down, wb, wd, sem_b, sem_d, core, chip)
+    fetch_ffn(mine_b, other_b, wb, wd, sem_b, sem_d, core, chip)
     o = ot_ref[...].T
     o_ref[...] = o
     for m in range(1, 4):
@@ -271,14 +294,14 @@
     h1_ref[...] = h1
     b = normed(h1, gain_ref[...]).astype(bf16)
     b_ref[...] = b
-    n = wb.shape[3]
+    n = wb.shape[4]
     total = h1
     for m in range(4):
         cols = slice(m * n, (m + 1) * n)
         arrived(wb, sem_b, 0, m)
-        gate = nn(b, wb[0, m])
+        gate = nn(b, whole(wb, 0, m))
         arrived(wb, sem_b, 1, m)
-        up = nn(b, wb[1, m])
+        up = nn(b, whole(wb, 1, m))
         gate_ref[:, cols] = gate.astype(bf16)
         up_ref[:, cols] = up.astype(bf16)
         z = (gate / (1.0 + jnp.exp(-gate)) * up).astype(bf16)
@@ -295,9 +318,9 @@
         project(total, gain_a, cos_ref, sin_ref, ids_ref[2 * KVW :, :], wa, sem_a, *more)
 
 
-def post(last, after, sc, ot, h, gain, gain_a, cos, sin, kv, wa, wb, wd):
+def post(last, after, sc, ot, h, gain, gain_a, cos, sin, kv, wa, wb):
     width, n = ot.shape
-    hidden = wb[0][0].shape[1] * 4
+    hidden = wb[0][0].shape[2] * 4
     outs = [shape((n, width), bf16), shape((n, width), f32), shape((n, width), bf16)] + [shape((n, hidden), bf16)] * 3
     outs += [shape((width, n), bf16) if last else shape((n, width), f32)]
     if not last:
@@ -305,13 +328,13 @@
     return pl.pallas_call(
         functools.partial(post_kernel, last, len(after)),
         out_shape=tuple(outs),
-        in_specs=[SCALARS] + [WHOLE] * 6 + [LEFT] * 18 + [WHOLE] + [LEFT] * len(after),
+        in_specs=[SCALARS] + [WHOLE] * 6 + [LEFT] * 16 + [WHOLE] + [LEFT] * len(after),
         out_specs=(WHOLE,) * len(outs),
         scratch_shapes=scratch_a(width) + scratch_ffn(width, hidden // 4),
         cost_estimate=BRIEF,
         compiler_params=pltpu.CompilerParams(vmem_limit_bytes=LIMIT),
         name="post",
-    )(sc, ot, h, gain, gain_a, cos, sin, *wa[0], *wa[1], *wb[0], *wb[1], *wd, kv, *after)
+    )(sc, ot, h, gain, gain_a, cos, sin, *wa[0], *wa[1], *wb[0], *wb[1], kv, *after)
 
 
 def ffn_back(state, core, refs, weights):
@@ -319,7 +342,7 @@
     wa, sem_a, wb, sem_b, wd, sem_d = weights
     gb = state.astype(bf16)
     gb_ref[...] = gb
-    n = wb.shape[3]
+    n = wb.shape[4]
     first = core == 0
     arrived_down(wd, sem_d)
     db = None
@@ -333,9 +356,9 @@
         keep_ref[:, cols] = jnp.where(first, dgate, dup)
         send_ref[:, cols] = jnp.where(first, dup, dgate)
         arrived(wb, sem_b, 0, m)
-        part = nt(dgate, wb[0, m])
+        part = nt(dgate, whole(wb, 0, m))
         arrived(wb, sem_b, 1, m)
-        part = part + nt(dup, wb[1, m])
+        part = part + nt(dup, whole(wb, 1, m))
         db = part if m == 0 else db + part
     dx, dgain = norm_back(h1_ref[...], gain_ref[...], db)
     dgain_ref[...] = dgain
@@ -392,7 +415,6 @@
     mine_a, other_a = take(4), take(4)
     if not end:
         mine_b, other_b = take(4), take(4)
-        down = take(2)
     if start:
         (g_ref,) = take(1)
     else:
@@ -410,7 +432,7 @@
     fetch(mine_a, other_a, wa, sem_a, core, chip)
     if not end:
         wb, sem_b, wd, sem_d = take(4)
-        fetch_ffn(mine_b, other_b, down, wb, wd, sem_b, sem_d, core, chip)
+        fetch_ffn(mine_b, other_b, wb, wd, sem_b, sem_d, core, chip)
     if start:
         state = g_ref[...].T.astype(f32)
     else:
@@ -428,15 +450,15 @@
 
 
 def back(start, end, sc, weights, tail, ffn, after=()):
-    wa, wb, wd = weights
+    wa, wb = weights
     width = wa[0][0].shape[0]
     args = [sc, *wa[0], *wa[1]]
     specs = [SCALARS] + [LEFT] * 8
     scratch = scratch_a(width)
     if not end:
-        args += [*wb[0], *wb[1], *wd]
-        specs += [LEFT] * 10
-        scratch += scratch_ffn(width, wb[0][0].shape[1])
+        args += [*wb[0], *wb[1]]
+        specs += [LEFT] * 8
+        scratch += scratch_ffn(width, wb[0][0].shape[2])
     args += list(tail)
     specs += [WHOLE] * len(tail)
     n = tail[0].shape[1 if start else 0]
@@ -509,24 +531,28 @@
 
 def grad_down_kernel(sc, *rest):
     lefts, rights = rest[:4], rest[4:8]
-    out_ref, left, right = rest[-3:]
-    n, (_, half, cols) = rights[0].shape[0], out_ref.shape
+    send_ref, keep_ref, left, right = rest[-4:]
+    n, (_, half, cols) = rights[0].shape[0], send_ref.shape
     turned(left, lefts)
     rows = pl.ds(pl.multiple_of(sc[0] * half, half), half)
-    for i in range(4):
-        for j, block in enumerate(rights):
-            right[j * n : (j + 1) * n, :] = block[:, i * cols : (i + 1) * cols]
-        out_ref[i] = nn(left[rows, :], right[...]).astype(bf16)
+    like = sc[2] & 1
+    for h in range(2):
+        for out, parity in ((send_ref, 1 - like), (keep_ref, like)):
+            at = pl.multiple_of((2 * h + parity) * cols, 128)
+            for j, block in enumerate(rights):
+                right[j * n : (j + 1) * n, :] = block[:, pl.ds(at, cols)]
+            out[h] = nn(left[rows, :], right[...]).astype(out.dtype)
 
 
 def grad_down(sc, lefts, rights, after):
     n, width = lefts[0].shape
     cols = rights[0].shape[1] // 4
+    block = (2, width // 2, cols)
     return pl.pallas_call(
         grad_down_kernel,
-        out_shape=shape((4, width // 2, cols), bf16),
+        out_shape=(shape(block, bf16), shape(block, bf16)),
         in_specs=[SCALARS] + [WHOLE] * 8 + [LEFT] * len(after),
-        out_specs=WHOLE,
+        out_specs=(WHOLE,) * 2,
         scratch_shapes=[pltpu.VMEM((width, 4 * n), bf16), pltpu.VMEM((4 * n, cols), bf16)],
         cost_estimate=BRIEF,
         compiler_params=pltpu.CompilerParams(vmem_limit_bytes=LIMIT),
@@ -652,52 +678,35 @@
     )(sc, query, key, value, out, gains)
 
 
-def pick_kernel(sc, gate, up, *rest):
-    out_ref, sem = rest[-2:]
-    cols = out_ref.shape[1]
+def pick_kernel(sc, gate, up, down, *rest):
+    out_ref, sems = rest[-2:]
+    rows, cols = out_ref.shape[0] - ROWS, out_ref.shape[1]
+    into = out_ref.at[:rows]
+    start = pl.multiple_of(down_rows(sc[0], sc[1], down.shape[0]), 64)
+    copy = pltpu.make_async_copy(down.at[pl.ds(start, ROWS), :], out_ref.at[rows:], sems.at[1])
+    copy.start()
     at = pl.ds(pl.multiple_of(sc[1] * cols, 128), cols)
     for c, source in ((0, gate), (1, up)):
 
         @pl.when(sc[0] == c)
         def _():
-            pltpu.make_async_copy(source.at[:, at], out_ref, sem).start()
-
-    pltpu.make_async_copy(gate.at[:, at], out_ref, sem).wait()
-
-
-def pick(sc, gate, up, after):
+            pltpu.make_async_copy(source.at[:, at], into, sems.at[0]).start()
+
+    pltpu.make_async_copy(gate.at[:, at], into, sems.at[0]).wait()
+    copy.wait()
+
+
+def pick(sc, gate, up, down, after):
     return pl.pallas_call(
         pick_kernel,
-        out_shape=shape((gate.shape[0], gate.shape[1] // 4), bf16),
-        in_specs=[SCALARS] + [LEFT] * (2 + len(after)),
+        out_shape=shape((gate.shape[0] + ROWS, gate.shape[1] // 4), bf16),
+        in_specs=[SCALARS] + [LEFT] * (3 + len(after)),
         out_specs=WHOLE,
-        scratch_shapes=[pltpu.SemaphoreType.DMA],
+        scratch_shapes=[pltpu.SemaphoreType.DMA((2,))],
         cost_estimate=BRIEF,
         compiler_params=pltpu.CompilerParams(vmem_limit_bytes=16 << 20),
         name="pick",
-    )(sc, gate, up, *after)
-
-
-def pick_down_kernel(sc, down, *rest):
-    out_ref, sem = rest[-2:]
-    half = out_ref.shape[0]
-    copy = pltpu.make_async_copy(down.at[pl.ds(pl.multiple_of(sc[0] * half, half), half), :], out_ref, sem)
-    copy.start()
-    copy.wait()
-
-
-def pick_down(sc, down, after):
-    rows, cols = down.shape
-    return pl.pallas_call(
-        pick_down_kernel,
-        out_shape=shape((rows // 2, cols), bf16),
-        in_specs=[SCALARS] + [LEFT] * (1 + len(after)),
-        out_specs=WHOLE,
-        scratch_shapes=[pltpu.SemaphoreType.DMA],
-        cost_estimate=BRIEF,
-        compiler_params=pltpu.CompilerParams(vmem_limit_bytes=16 << 20),
-        name="pick_down",
-    )(sc, down, *after)
+    )(sc, gate, up, down, *after)
 
 
 def gains_kernel(first_ref, out_ref):
@@ -785,26 +794,27 @@
     def kernel(sc, keep_ref, got_ref, *rest):
         send_ref, own_ref = rest[-2:]
         h = sc[2] >> 1
-        send_ref[...] = (keep_ref[1 - h] + got_ref[1 - h].astype(f32)).astype(bf16)
-        own_ref[...] = keep_ref[h] + got_ref[h].astype(f32)
+        send_ref[...] = (keep_ref[1 - h].astype(f32) + got_ref[1 - h].astype(f32)).astype(bf16)
+        own_ref[...] = keep_ref[h].astype(f32) + got_ref[h].astype(f32)
 
     part = keep.shape[1:]
     return small(kernel, sc, [keep, got], [shape(part, bf16), shape(part, f32)], [], after, "sum_third")
 
 
-def down_split(sc, half, after):
-    def kernel(sc, half_ref, *rest):
+def down_split(sc, own, got, after):
+    def kernel(sc, own_ref, got_ref, *rest):
         send_ref, kept_ref, total = rest[-3:]
         n = total.shape[1]
         for m in range(4):
-            total[m] = half_ref[m * n : (m + 1) * n, :].astype(f32)
+            rows = slice(m * n, (m + 1) * n)
+            total[m] = own_ref[rows, :] + got_ref[rows, :].astype(f32)
         for i, m in enumerate(by_turn(sc[0], sc[1])):
             out = send_ref if i < 2 else kept_ref
             out[i % 2] = total[m].astype(bf16)
 
-    rows, cols = half.shape
+    rows, cols = own.shape
     out = shape((2, rows // 4, cols), bf16)
-    return small(kernel, sc, [half], [out, out], [pltpu.VMEM((4, rows // 4, cols), f32)], after, "down_split")
+    return small(kernel, sc, [own, got], [out, out], [pltpu.VMEM((4, rows // 4, cols), f32)], after, "down_split")
 
 
 def sum_two(sc, own, got, after):
@@ -940,23 +950,23 @@
     parts_a = turns(pick_first(sc, query_weight, key_weight.T, value_weight.T, out_weight, gains))
     ids = jnp.broadcast_to((segment_ids[0] + 1).astype(bf16), (IDS, stretch))
     tokens = home_to_work(jnp.concatenate([tokens[0].T, ids]))
-    piece_b = pick(sc, gate_weight, up_weight, parts_a[1:2])
+    piece_b = pick(sc, gate_weight, up_weight, down_weight.T, parts_a[1:2])
     whole_a = stack(sc, parts_a, [piece_b])
     gains = gains_of(whole_a)
     gain_a, gain_f = gains[:1], gains[1:]
     wa = plane_gather(whole_a.reshape(depth * rows, PIECE))
     far_b = hold(flip_z(piece_b, 2), [wa[0][1], wa[0][2]])
-    parts_b = piece_b, flip_z(piece_b, 1), far_b, flip_z(far_b, 1)
-    whole_b = stack(sc, parts_b).reshape(depth * rows, piece_b.shape[1])
-    wb = plane_gather(whole_b)
-    piece_d = pick_down(sc, down_weight.T, [whole_a])
-    whole_d = lax.all_gather(piece_d, "fsdp", axis=0)
+    whole_b = stack(sc, (piece_b, flip_z(piece_b, 1), far_b, flip_z(far_b, 1)), [wa[0][3]])
+    first_b, second_b = flip(whole_b, SIDE, BACK), flip(whole_b, BACK, SIDE)
 
     h_0, a0, q0, own = pre(sc, tokens, gain_a, cos, sin, *wa, [whole_b])
     kv0 = window(own)
-    o0, lse0 = attend(q0, kv0, [wb[0][1], wb[0][2]])
-    whole_d = hold(whole_d, [o0])
-    weights = wa, wb, (whole_d, flip(whole_d, CORE))
+    first_b = hold(first_b, [kv0[0], second_b])
+    opposite_b = flip(first_b, BACK, SIDE)
+    o0, lse0 = attend(q0, kv0)
+    wb = whole_b, first_b, second_b, hold(opposite_b, [o0])
+    wb = wb, across(wb)
+    weights = wa, wb
     mixed0, h1_0, b0, gate0, up0, z0, h_1, a1, q1, own = post(False, [], sc, o0, h_0, gain_f, gain_a, cos, sin, own, *weights)
     kv1 = window(own)
     across_0 = across((a0, b0, mixed0, z0))
@@ -977,13 +987,13 @@
     away0, gb0_, one1 = across((away0, gb0, one1))
     dq0, three0, far, near, own = attend_back(sc, p0, q0, kv0, lse0, do, cos, sin, [one1, output])
     near, down_far, far = unwindow(sc, far, near)
-    parts_d = grad_down(sc, [gb1, gb0, across_2[0], gb0_], [z1, z0, across_1[3], across_0[3]], [down_far])
-    half_d = lax.psum_scatter(parts_d, "fsdp", scatter_dimension=0, tiled=False)
-    send_b, keep_b = grad_ffn(sc, [b1, b0, across_1[1], across_0[1]], [act1, act0, across_2[1], away0], [parts_d, far])
+    send_b, keep_b = grad_ffn(sc, [b1, b0, across_1[1], across_0[1]], [act1, act0, across_2[1], away0], [down_far])
     got_b = flip(send_b, SIDE, BACK)
+    send_d, keep_d = grad_down(sc, [gb1, gb0, across_2[0], gb0_], [z1, z0, across_1[3], across_0[3]], [send_b])
+    got_d = flip_z(send_d, 1)
     (three0,) = across((three0,))
     tail = [g1, dq0, own, near, far, h_0, gain_a, cos, sin]
-    dk0, dv0, one0, dgain_a0, grad_tokens = back(False, True, sc, weights, tail, None, [send_b, three0])
+    dk0, dv0, one0, dgain_a0, grad_tokens = back(False, True, sc, weights, tail, None, [send_d, three0])
 
     own = [dq1, dq0, dk1, dk0, dv1, dv0, p1, p0]
     got = [three1, three0, one1, flip(one0, CORE)]
@@ -991,18 +1001,19 @@
     got_a = flip(send_a, SIDE, BACK)
     later_b, own_b = sum_first(sc, keep_b, got_b, [send_a])
     more_b = flip(later_b, BACK, SIDE)
-    grad_tokens = home_to_work(hold(grad_tokens, [later_b]), back=True)
-    later_a, own_a = sum_first(sc, keep_a, got_a, [later_b])
+    send_d, keep_d = sum_third(sc, keep_d, got_d, [later_b])
+    got_d = flip_z(send_d, 2)
+    later_a, own_a = sum_first(sc, keep_a, got_a, [send_d])
     more_a = flip(later_a, BACK, SIDE)
     send_b, ring_b = sum_second(sc, own_b, more_b, [later_a])
     got_b = flip_z(send_b, 1)
     send_a, ring_a = sum_second(sc, own_a, more_a, [send_b])
     got_a = flip_z(send_a, 1)
-    send_d, keep_d = down_split(sc, half_d, [send_a])
+    send_b, ring_b = sum_third(sc, ring_b, got_b, [send_a])
+    got_b = flip_z(send_b, 2)
+    send_d, keep_d = down_split(sc, keep_d, got_d, [send_b])
     got_d = flip(send_d, SIDE, BACK)
-    send_b, ring_b = sum_third(sc, ring_b, got_b, [send_d, grad_tokens])
-    got_b = flip_z(send_b, 2)
-    send_a, ring_a = sum_third(sc, ring_a, got_a, [send_b])
+    send_a, ring_a = sum_third(sc, ring_a, got_a, [send_d])
     got_a = flip_z(send_a, 2)
     piece_b = over_groups(sum_two(sc, ring_b, got_b, [send_a]))
     all_b = spread(piece_b)
@@ -1015,6 +1026,7 @@
     all_d = spread(piece_d)
     grad_query, grad_key, grad_value, grad_out, dgains = lay(sc, all_a, across(all_a), (width, KVW, KVW, width), [grad_gate])
     grad_down_ = lay_down(sc, all_d, across(all_d), [grad_query])
+    grad_tokens = home_to_work(hold(grad_tokens, [piece_a]), back=True)
     grad_tokens, output = grad_tokens.astype(f32).T, output.T
     return (output[None], grad_tokens[None], dgains[0], grad_query, grad_key, grad_value, grad_out, dgains[1], grad_gate, grad_up, grad_down_.T)
 

time: 557 us -> 525 us (0.943)
  waiting for transfers between devices: 217 us -> 190 us
  starting transfers between devices: 77.2 us -> 97.7 us
  between operations: 15.5 us -> 1.85 us
  local copies, waits for them, and re-layouts: 39.8 us -> 32 us
    ppermute x62 -> x61, waiting for transfers between devices: 103 us -> 69.7 us  [flip(): lax.ppermute(value, 'dp', [(i, i ^ bits[i & 1]) for i in range(count)])]
    ppermute x10 -> x12, waiting for transfers between devices: 70.7 us -> 95 us  [flip_z(): return lax.ppermute(value, ('dp', 'fsdp'), pairs)]
    ppermute x2, waiting for transfers between devices: 30 us -> 12 us  [unwindow(): lax.ppermute(far, 'fsdp', [(z + 1, z) for z in range(0, depth, 2)])]
    ppermute x62 -> x61, starting transfers between devices: 49.3 us -> 62 us  [flip(): lax.ppermute(value, 'dp', [(i, i ^ bits[i & 1]) for i in range(count)])]
    unnamed x178 -> x168, local copies, waits for them, and re-layouts: 37.2 us -> 29.4 us
    ppermute x10 -> x12, starting transfers between devices: 14.1 us -> 20 us  [flip_z(): return lax.ppermute(value, ('dp', 'fsdp'), pairs)]
    ppermute x2, starting transfers between devices: 3.8 us -> 9.67 us  [window(): far = lax.ppermute(own, 'fsdp', [(z, z + 1) for z in range(0, depth, 2)])]
    pallas_call x14 -> x15, Pallas kernels: 14.7 us -> 13.1 us  [small(): pl.pallas_call(kernel, out_shape=tuple(outs), in_specs=[SCALARS] + [WHOLE...]
  transfers between devices with their start and end apart: 82 -> 81, of which waited for: 37 -> 38; matrix products, arithmetic and copies ran while one was open for 2% -> 1% of each run, Pallas kernels for 27% -> 22%
where the time goes in v10:
time: 525 us; the launch traced here: 520 us
  Pallas kernels  195 us (37%)
  waiting for transfers between devices  190 us (36%)
  starting transfers between devices  97.7 us (19%)
  local copies, waits for them, and re-layouts  32 us (6%)
    ppermute x12, waiting for transfers between devices, flip_z(): return lax.ppermute(value, ('dp', 'fsdp'), pairs)  95 us
    ppermute x61, waiting for transfers between devices, flip(): lax.ppermute(value, 'dp', [(i, i ^ bits[i & 1]) for i in range(count)])  69.7 us
    ppermute x61, starting transfers between devices, flip(): lax.ppermute(value, 'dp', [(i, i ^ bits[i & 1]) for i in range(count)])  62 us
    pallas_call x3, Pallas kernels, back(): pl.pallas_call(functools.partial(back_kernel, start, end, len(after)), ou...  48.4 us
    pallas_call x2, Pallas kernels, post(): pl.pallas_call(functools.partial(post_kernel, last, len(after)), out_shap...  39.3 us
    unnamed x168, local copies, waits for them, and re-layouts  29.4 us
    pallas_call x2, Pallas kernels, attend_back(): pl.pallas_call(attend_back_kernel, out_shape=(shape((3, n, PIECE), bf16),...  25.3 us
    pallas_call x2, Pallas kernels, attend(): pl.pallas_call(attend_kernel, out_shape=(shape((width, n), bf16), shape((...  20.4 us
  transfers between devices with their start and end apart: 81, of which 38 were waited for; matrix products, arithmetic and copies ran while one was open for 1% of the time, Pallas kernels for 22%

profile of v10, /device:TPU:0, one launch (start us, length us, event | category | flops | bytes accessed | tf_op | source)
XLA Modules:
  0.0 520.2 jit_solution(18427515380770371214)
XLA Ops:
  0.7 2.0 copy.39
  8.8 4.1 collective-permute-start.2
  12.9 1.6 collective-permute-start.1
  14.5 7.2 %collective-permute-done.2.rest_2_ = bf16[240,384]{1,0:T(8,128)(2,1)S(1)} collective-permute-done((bf16[240,384]{1,0:T(8,128)(2,1)S(1)}, bf16[240,384]{1,0:T(8,128)(2,1)S(1)}, u32[]{:S(2)}, u32[]{:S(2)}) %collective-permute-start.2) | collective-permute-done | bytes 184352 | tf_op jit(solution)/shard_map/ppermute | solution.py:877
  24.4 3.1 collective-permute-done.3.rest_3_
  27.4 1.5 stack.30.first_ref
  30.3 1.5 collective-permute-start.5
  31.8 3.2 collective-permute-start.12
  35.0 13.6 %collective-permute-done.4.refs_1_.rest_1_ = bf16[960,384]{1,0:T(8,128)(2,1)} collective-permute-done((bf16[960,384]{1,0:T(8,128)(2,1)S(1)}, bf16[960,384]{1,0:T(8,128)(2,1)}, u32[]{:S(2)}, u32[]{:S(2)}) %collective-permute-start.4) | collective-permute-done | bytes 737312 | tf_op jit(solution)/shard_map/ppermute | solution.py:871
  49.8 5.2 %collective-permute-done.12.refs_0_ = bf16[368,640]{1,0:T(8,128)(2,1)S(1)} collective-permute-done((bf16[368,640]{1,0:T(8,128)(2,1)S(1)}, bf16[368,640]{1,0:T(8,128)(2,1)S(1)}, u32[]{:S(2)}, u32[]{:S(2)}) %collective-permute-start.12) | collective-permute-done | bytes 471072 | tf_op jit(solution)/shard_map/ppermute | solution.py:877
  55.8 9.4 %collective-permute-done.11.rest_1_ = bf16[368,640]{1,0:T(8,128)(2,1)S(1)} collective-permute-done((bf16[368,640]{1,0:T(8,128)(2,1)S(1)}, bf16[368,640]{1,0:T(8,128)(2,1)S(1)}, u32[]{:S(2)}, u32[]{:S(2)}) %collective-permute-start.11) | collective-permute-done | bytes 471072 | tf_op jit(solution)/shard_map/ppermute | solution.py:877
  65.2 10.0 %collective-permute-done.13.rest_3_ = bf16[368,640]{1,0:T(8,128)(2,1)S(1)} collective-permute-done((bf16[368,640]{1,0:T(8,128)(2,1)S(1)}, bf16[368,640]{1,0:T(8,128)(2,1)S(1)}, u32[]{:S(2)}, u32[]{:S(2)}) %collective-permute-start.13) | collective-permute-done | bytes 471072 | tf_op jit(solution)/shard_map/ppermute | solution.py:877
  75.2 3.0 stack.31.rest_8_
  80.1 3.0 collective-permute-start.8
  83.1 7.5 %collective-permute-start.9 = (bf16[960,384]{1,0:T(8,128)(2,1)}, bf16[960,384]{1,0:T(8,128)(2,1)}, u32[]{:S(2)}, u32[]{:S(2)}) collective-permute-start(bf16[960,384]{1,0:T(8,128)(2,1)} %collective-permute-done.5.refs_2_.rest_2_), channel_id=1, source_target_pairs={{0,4},{4,0},{8,12},{12,8},{16,20},{20,16},{24,28},{28,24},{1,5},{5... | collective-permute-start | bytes 2211848 | tf_op jit(solution)/shard_map/ppermute | solution.py:871
  94.2 6.8 %pre.1 = (bf16[256,960]{1,0:T(8,128)(2,1)}, bf16[256,960]{1,0:T(8,128)(2,1)}, bf16[960,256]{1,0:T(8,128)(2,1)}, bf16[656,256]{1,0:T(8,128)(2,1)}) custom-call(s32[3]{0:T(128)} %copy-done.46, bf16[976,256]{1,0:T(8,128)(2,1)} %copy-done.76, f32[1,960]{1,0:T(1,128)} %get-tuple-element.201.gain_ref.gain_a.rest_22_.rest_14_, ...), custom_call_target="tpu_custom_call" | custom-call | flops 1024 | bytes 1024 | tf_op jit(solution)/shard_map/pre/pallas_call | solution.py:119
  101.0 8.0 %collective-permute-start.14 = (bf16[656,256]{1,0:T(8,128)(2,1)}, bf16[656,256]{1,0:T(8,128)(2,1)S(1)}, u32[]{:S(2)}, u32[]{:S(2)}) collective-permute-start(bf16[656,256]{1,0:T(8,128)(2,1)} %get-tuple-element.101.kv2.rest_16_), channel_id=1, source_target_pairs={{0,1},{2,3},{4,5},{6,7},{8,9},{10,11},{12,13},{14,15},{16,17},{18,... | collective-permute-start | bytes 1007624 | tf_op jit(solution)/shard_map/ppermute | solution.py:910
  109.1 7.9 %collective-permute-done.14.kv0.refs_1_ = bf16[656,256]{1,0:T(8,128)(2,1)S(1)} collective-permute-done((bf16[656,256]{1,0:T(8,128)(2,1)}, bf16[656,256]{1,0:T(8,128)(2,1)S(1)}, u32[]{:S(2)}, u32[]{:S(2)}) %collective-permute-start.14) | collective-permute-done | bytes 335904 | tf_op jit(solution)/shard_map/ppermute | solution.py:910
  117.0 4.7 collective-permute-done.16.refs_0_
  124.5 10.1 %attend.2 = (bf16[960,256]{1,0:T(8,128)(2,1)S(1)}, f32[15,256]{1,0:T(8,128)S(1)}) custom-call(bf16[960,256]{1,0:T(8,128)(2,1)S(1)} %copy-done.25, bf16[656,256]{1,0:T(8,128)(2,1)S(1)} %collective-permute-done.14.kv0.refs_1_, bf16[656,256]{1,0:T(8,128)(2,1)S(1)} %collective-permute-done.15.kv1, bf16[656,256]{1,0:T(8,128)(2,1)S(1)} %copy-done.5), custom_call_target="tpu_custom_call" | custom-call | flops 1024 | bytes 1024 | tf_op jit(solution)/shard_map/attend/pallas_call | solution.py:172
  135.3 10.6 %collective-permute-done.18.refs_0_ = bf16[4,368,640]{2,1,0:T(8,128)(2,1)} collective-permute-done((bf16[4,368,640]{2,1,0:T(8,128)(2,1)}, bf16[4,368,640]{2,1,0:T(8,128)(2,1)}, u32[]{:S(2)}, u32[]{:S(2)}) %collective-permute-start.18) | collective-permute-done | bytes 1884192 | tf_op jit(solution)/shard_map/ppermute | solution.py:871
  147.2 2.7 collective-permute-done.22.rest_15_
  151.3 21.0 %post.2 = (bf16[256,960]{1,0:T(8,128)(2,1)}, f32[256,960]{1,0:T(8,128)}, bf16[256,960]{1,0:T(8,128)(2,1)}, bf16[256,2560]{1,0:T(8,128)(2,1)}, bf16[256,2560]{1,0...) custom-call(s32[3]{0:T(128)} %copy-done.46, ...), custom_call_target="tpu_custom_call" | custom-call | flops 1024 | bytes 1024 | tf_op jit(solution)/shard_map/post/pallas_call | solution.py:328
  172.3 1.6 collective-permute-start.23
  174.0 5.6 %collective-permute-done.23.kv0 = bf16[656,256]{1,0:T(8,128)(2,1)S(1)} collective-permute-done((bf16[656,256]{1,0:T(8,128)(2,1)}, bf16[656,256]{1,0:T(8,128)(2,1)S(1)}, u32[]{:S(2)}, u32[]{:S(2)}) %collective-permute-start.23) | collective-permute-done | bytes 335904 | tf_op jit(solution)/shard_map/ppermute | solution.py:910
  184.8 10.3 %attend.3 = (bf16[960,256]{1,0:T(8,128)(2,1)S(1)}, f32[15,256]{1,0:T(8,128)S(1)}) custom-call(bf16[960,256]{1,0:T(8,128)(2,1)S(1)} %copy-done.28, bf16[656,256]{1,0:T(8,128)(2,1)S(1)} %collective-permute-done.23.kv0, bf16[656,256]{1,0:T(8,128)(2,1)S(1)} %collective-permute-done.24.kv1.refs_1_, bf16[656,256]{1,0:T(8,128)(2,1)S(1)} %copy-done.3, ...), custom_call_target="tpu_custom_call" | custom-call | flops 1024 | bytes 1024 | tf_op jit(solution)/shard_map/attend/pallas_call | solution.py:172
  196.7 18.3 %post.3 = (bf16[256,960]{1,0:T(8,128)(2,1)}, f32[256,960]{1,0:T(8,128)}, bf16[256,960]{1,0:T(8,128)(2,1)}, bf16[256,2560]{1,0:T(8,128)(2,1)}, bf16[256,2560]{1,0...) custom-call(s32[3]{0:T(128)} %copy-done.46, bf16[960,256]{1,0:T(8,128)(2,1)} %copy-done.54, ...), custom_call_target="tpu_custom_call" | custom-call | flops 1024 | bytes 1024 | tf_op jit(solution)/shard_map/post/pallas_call | solution.py:328
  215.1 1.9 collective-permute-start.33
  217.1 20.8 %back_start.1 = (bf16[256,960]{1,0:T(8,128)(2,1)}, bf16[256,2560]{1,0:T(8,128)(2,1)}, bf16[256,2560]{1,0:T(8,128)(2,1)}, f32[256,960]{1,0:T(8,128)}, bf16[3,256,...) custom-call(s32[3]{0:T(128)} %copy-done.46, bf16[960,384]{1,0:T(8,128)(2,1)} %bitcast.29, ...), custom_call_target="tpu_custom_call" | custom-call | flops 1024 | bytes 1024 | tf_op jit(solution)/shard_map/back_start/pallas_call | solution.py:479
  239.0 3.1 collective-permute-done.30.rest_0_.rest_2_
  243.5 1.5 copy-done.11
  246.0 12.6 %attend_back.2 = (bf16[3,256,384]{2,1,0:T(8,128)(2,1)S(1)}, bf16[3,256,384]{2,1,0:T(8,128)(2,1)S(1)}, f32[640,256]{1,0:T(8,128)S(1)}, bf16[640,256]{1,0:T(8,128)(2,1)S(1)}, f32[640,256]{1,0:T(8,128)S(1)}) custom-call(s32[3]{0:T(128)S(1)} %copy-done.47, bf16[3,256,384]{2,1,0:T(8,128)(2,1)S(1)} %copy-done.11, bf16[960,256]{1,0:T(8,128)(2,1)S(1)} %copy-done.28, ...), custom_call_target="tpu_custom_call" | custom-call | flops 1024 | bytes 1024 | tf_op jit(solution)/shard_map/attend_back/pallas_call | solution.py:225
  263.2 11.4 %collective-permute-done.35.refs_1_.rest_20_ = bf16[640,256]{1,0:T(8,128)(2,1)S(1)} collective-permute-done((bf16[640,256]{1,0:T(8,128)(2,1)S(1)}, bf16[640,256]{1,0:T(8,128)(2,1)S(1)}, u32[]{:S(2)}, u32[]{:S(2)}) %collective-permute-start.35) | collective-permute-done | bytes 327712 | tf_op jit(solution)/shard_map/ppermute | solution.py:919
  275.3 21.1 %back_join.1 = (bf16[256,384]{1,0:T(8,128)(2,1)}, bf16[256,384]{1,0:T(8,128)(2,1)}, bf16[256,384]{1,0:T(8,128)(2,1)}, f32[1,960]{1,0:T(1,128)}, bf16[256,960]{1,...) custom-call(s32[3]{0:T(128)} %copy-done.46, ...), custom_call_target="tpu_custom_call" | custom-call | flops 1024 | bytes 1024 | tf_op jit(solution)/shard_map/back_join/pallas_call | solution.py:479
  299.1 1.5 collective-permute-start.40
  302.8 12.6 %attend_back.3 = (bf16[3,256,384]{2,1,0:T(8,128)(2,1)S(1)}, bf16[3,256,384]{2,1,0:T(8,128)(2,1)S(1)}, f32[640,256]{1,0:T(8,128)S(1)}, bf16[640,256]{1,0:T(8,128)(2,1)S(1)}, f32[640,256]{1,0:T(8,128)S(1)}) custom-call(s32[3]{0:T(128)S(1)} %copy-done.48, bf16[3,256,384]{2,1,0:T(8,128)(2,1)S(1)} %copy-done.12, bf16[960,256]{1,0:T(8,128)(2,1)S(1)} %copy-done.26, ...), custom_call_target="tpu_custom_call" | custom-call | flops 1024 | bytes 1024 | tf_op jit(solution)/shard_map/attend_back/pallas_call | solution.py:225
  316.2 11.0 %collective-permute-start.41 = (bf16[640,256]{1,0:T(8,128)(2,1)S(1)}, bf16[640,256]{1,0:T(8,128)(2,1)S(1)}, u32[]{:S(2)}, u32[]{:S(2)}) collective-permute-start(bf16[640,256]{1,0:T(8,128)(2,1)S(1)} %get-tuple-element.141), channel_id=1, source_target_pairs={{0,4},{4,0},{8,12},{12,8},{16,20},{20,16},{24,28},{28,24},{1,5},{5... | collective-permute-start | bytes 983048 | tf_op jit(solution)/shard_map/ppermute | solution.py:871
  330.9 11.0 %grad_ffn.1 = (bf16[2,960,640]{2,1,0:T(8,128)(2,1)}, bf16[2,960,640]{2,1,0:T(8,128)(2,1)}) custom-call(s32[3]{0:T(128)} %copy-done.46, bf16[256,960]{1,0:T(8,128)(2,1)} %get-tuple-element.120.rest_0_, bf16[256,960]{1,0:T(8,128)(2,1)} %get-tuple-element.107.rest_1_, bf16[256,960]{1,0:T(8,128)(2,1)} %copy-done.24, bf16[256,960]{1,0:T(8,128)(2,1)} %copy-done.23, ...), custom_call_target="tpu_custom_call" | custom-call | flops 1024 | bytes 1024 | tf_op jit(solution)/shard_map/grad_ffn/pallas_call | solution.py:520
  347.6 8.2 %grad_down.1 = (bf16[2,480,640]{2,1,0:T(8,128)(2,1)}, bf16[2,480,640]{2,1,0:T(8,128)(2,1)}) custom-call(s32[3]{0:T(128)} %copy-done.46, bf16[256,960]{1,0:T(8,128)(2,1)} %get-tuple-element.132.rest_0_, bf16[256,960]{1,0:T(8,128)(2,1)} %get-tuple-element.143.rest_1_, bf16[256,960]{1,0:T(8,128)(2,1)} %copy-done.67, bf16[256,960]{1,0:T(8,128)(2,1)} %copy-done.75, ...), custom_call_target="tpu_custom_call" | custom-call | flops 1024 | bytes 1024 | tf_op jit(solution)/shard_map/grad_down/pallas_call | solution.py:551
  357.2 6.4 %back_end.1 = (bf16[256,384]{1,0:T(8,128)(2,1)}, bf16[256,384]{1,0:T(8,128)(2,1)}, bf16[256,384]{1,0:T(8,128)(2,1)}, f32[1,960]{1,0:T(1,128)}, bf16[960,256]{1,0:T(8,128)(2,1)}) custom-call(s32[3]{0:T(128)} %copy-done.46, bf16[960,384]{1,0:T(8,128)(2,1)} %bitcast.31, bf16[960,384]{1,0:T(8,128)(2,1)} %collective-permute-done.4.refs_1_.rest_1_, ...), custom_call_target="tpu_custom_call" | custom-call | flops 1024 | bytes 1024 | tf_op jit(solution)/shard_map/back_end/pallas_call | solution.py:479
  366.5 10.7 %grad_attention.1 = (bf16[2,960,384]{2,1,0:T(8,128)(2,1)}, bf16[2,960,384]{2,1,0:T(8,128)(2,1)}) custom-call(s32[3]{0:T(128)} %copy-done.46, bf16[256,960]{1,0:T(8,128)(2,1)} %get-tuple-element.119.rest_0_, bf16[256,960]{1,0:T(8,128)(2,1)} %get-tuple-element.106.rest_1_, bf16[256,960]{1,0:T(8,128)(2,1)} %copy-done.21, bf16[256,960]{1,0:T(8,128)(2,1)} %copy-done.19, ...), custom_call_target="tpu_custom_call" | custom-call | flops 1024 | bytes 1024 | tf_op jit(solution)/shard_map/grad_attention/pallas_call | solution.py:602
  377.1 2.4 collective-permute-start.47
  379.5 1.6 collective-permute-start.48
  384.5 25.0 %collective-permute-done.48.got_ref = bf16[2,480,640]{2,1,0:T(8,128)(2,1)S(1)} collective-permute-done((bf16[2,480,640]{2,1,0:T(8,128)(2,1)}, bf16[2,480,640]{2,1,0:T(8,128)(2,1)S(1)}, u32[]{:S(2)}, u32[]{:S(2)}) %collective-permute-start.48) | collective-permute-done | bytes 1228832 | tf_op jit(solution)/shard_map/ppermute | solution.py:877
  413.5 2.5 collective-permute-start.54
  416.1 1.5 collective-permute-start.53
  417.6 5.6 %collective-permute-done.50.got_ref = bf16[960,384]{1,0:T(8,128)(2,1)S(1)} collective-permute-done((bf16[960,384]{1,0:T(8,128)(2,1)S(1)}, bf16[960,384]{1,0:T(8,128)(2,1)S(1)}, u32[]{:S(2)}, u32[]{:S(2)}) %collective-permute-start.50) | collective-permute-done | bytes 737312 | tf_op jit(solution)/shard_map/ppermute | solution.py:871
  424.0 1.8 collective-permute-start.52
  425.8 17.8 %collective-permute-done.54.got_ref = bf16[2,240,640]{2,1,0:T(8,128)(2,1)S(1)} collective-permute-done((bf16[2,240,640]{2,1,0:T(8,128)(2,1)S(1)}, bf16[2,240,640]{2,1,0:T(8,128)(2,1)S(1)}, u32[]{:S(2)}, u32[]{:S(2)}) %collective-permute-start.54) | collective-permute-done | bytes 614432 | tf_op jit(solution)/shard_map/ppermute | solution.py:877
  447.1 8.5 %collective-permute-done.52.got_ref = bf16[2,240,384]{2,1,0:T(8,128)(2,1)S(1)} collective-permute-done((bf16[2,240,384]{2,1,0:T(8,128)(2,1)S(1)}, bf16[2,240,384]{2,1,0:T(8,128)(2,1)S(1)}, u32[]{:S(2)}, u32[]{:S(2)}) %collective-permute-start.52) | collective-permute-done | bytes 368672 | tf_op jit(solution)/shard_map/ppermute | solution.py:877
  457.2 1.8 collective-permute-done.57.got_ref
  460.2 6.3 %collective-permute-done.55.got_ref = bf16[240,384]{1,0:T(8,128)(2,1)S(1)} collective-permute-done((bf16[240,384]{1,0:T(8,128)(2,1)S(1)}, bf16[240,384]{1,0:T(8,128)(2,1)S(1)}, u32[]{:S(2)}, u32[]{:S(2)}) %collective-permute-start.55) | collective-permute-done | bytes 184352 | tf_op jit(solution)/shard_map/ppermute | solution.py:877
  467.1 2.1 collective-permute-start.59
  471.8 5.2 collective-permute-done.73.got_ref
  478.6 1.8 collective-permute-start.68
  482.6 3.8 collective-permute-done.66.rest_1_
  487.8 5.6 %collective-permute-done.68.rest_3_ = bf16[240,640]{1,0:T(8,128)(2,1)S(1)} collective-permute-done((bf16[240,640]{1,0:T(8,128)(2,1)S(1)}, bf16[240,640]{1,0:T(8,128)(2,1)S(1)}, u32[]{:S(2)}, u32[]{:S(2)}) %collective-permute-start.68) | collective-permute-done | bytes 307232 | tf_op jit(solution)/shard_map/ppermute | solution.py:871
  494.5 2.5 collective-permute-start.74
  497.1 3.2 collective-permute-done.74.rest_1_
  501.3 2.5 collective-permute-start.76
  505.4 3.1 lay.2
  509.8 1.7 copy-done.10
  511.5 2.4 lay.3
  516.2 2.9 lay_down.1
  (322 shorter events, 89.0 us)
Async XLA Ops:
  8.8 12.8 %collective-permute-start.2 = (bf16[240,384]{1,0:T(8,128)(2,1)S(1)}, bf16[240,384]{1,0:T(8,128)(2,1)S(1)}, u32[]{:S(2)}, u32[]{:S(2)}) collective-permute-start(bf16[240,384]{1,0:T(8,128)(2,1)S(1)} %pick_first.1.rest_0_), channel_id=1, source_target_pairs={{0,2},{1,3},{2,0},{3,1},{4,6},{5,7},{6,4},{7,5},{8,10},{9,11},{10,... | collective-permute-start | bytes 552968 | tf_op jit(solution)/shard_map/ppermute | solution.py:877
  12.9 9.4 %collective-permute-start.1 = (bf16[240,384]{1,0:T(8,128)(2,1)S(1)}, bf16[240,384]{1,0:T(8,128)(2,1)S(1)}, u32[]{:S(2)}, u32[]{:S(2)}) collective-permute-start(bf16[240,384]{1,0:T(8,128)(2,1)S(1)} %pick_first.1.rest_0_), channel_id=1, source_target_pairs={{0,1},{1,0},{2,3},{3,2},{4,5},{5,4},{6,7},{7,6},{8,9},{9,8},{10,11... | collective-permute-start | bytes 552968 | tf_op jit(solution)/shard_map/ppermute | solution.py:877
  21.6 5.8 %collective-permute-start.3 = (bf16[240,384]{1,0:T(8,128)(2,1)S(1)}, bf16[240,384]{1,0:T(8,128)(2,1)S(1)}, u32[]{:S(2)}, u32[]{:S(2)}) collective-permute-start(bf16[240,384]{1,0:T(8,128)(2,1)S(1)} %collective-permute-done.2.rest_2_), channel_id=1, source_target_pairs={{0,1},{1,0},{2,3},{3,2},{4,5},{5,4},{6,7},{7,6},{8,9},{9,8},{10,11... | collective-permute-start | bytes 552968 | tf_op jit(solution)/shard_map/ppermute | solution.py:877
  29.0 19.6 %collective-permute-start.4 = (bf16[960,384]{1,0:T(8,128)(2,1)S(1)}, bf16[960,384]{1,0:T(8,128)(2,1)}, u32[]{:S(2)}, u32[]{:S(2)}) collective-permute-start(bf16[960,384]{1,0:T(8,128)(2,1)S(1)} %bitcast.23), channel_id=1, source_target_pairs={{0,8},{4,20},{8,0},{12,28},{16,24},{20,4},{24,16},{28,12},{1,9},{5... | collective-permute-start | bytes 2211848 | tf_op jit(solution)/shard_map/ppermute | solution.py:871
  30.3 24.8 %collective-permute-start.5 = (bf16[960,384]{1,0:T(8,128)(2,1)S(1)}, bf16[960,384]{1,0:T(8,128)(2,1)}, u32[]{:S(2)}, u32[]{:S(2)}) collective-permute-start(bf16[960,384]{1,0:T(8,128)(2,1)S(1)} %bitcast.24), channel_id=1, source_target_pairs={{0,16},{4,12},{8,24},{12,4},{16,0},{20,28},{24,8},{28,20},{1,17},{... | collective-permute-start | bytes 2211848 | tf_op jit(solution)/shard_map/ppermute | solution.py:871
  31.8 23.3 %collective-permute-start.12 = (bf16[368,640]{1,0:T(8,128)(2,1)S(1)}, bf16[368,640]{1,0:T(8,128)(2,1)S(1)}, u32[]{:S(2)}, u32[]{:S(2)}) collective-permute-start(bf16[368,640]{1,0:T(8,128)(2,1)S(1)} %pick.1.rest_4_.rest_0_), channel_id=1, source_target_pairs={{0,2},{1,3},{2,0},{3,1},{4,6},{5,7},{6,4},{7,5},{8,10},{9,11},{10,... | collective-permute-start | bytes 1413128 | tf_op jit(solution)/shard_map/ppermute | solution.py:877
  48.6 26.6 %collective-permute-start.6 = (bf16[960,384]{1,0:T(8,128)(2,1)}, bf16[960,384]{1,0:T(8,128)(2,1)S(1)}, u32[]{:S(2)}, u32[]{:S(2)}) collective-permute-start(bf16[960,384]{1,0:T(8,128)(2,1)} %collective-permute-done.4.refs_1_.rest_1_), channel_id=1, source_target_pairs={{0,16},{4,12},{8,24},{12,4},{16,0},{20,28},{24,8},{28,20},{1,17},{... | collective-permute-start | bytes 2211848 | tf_op jit(solution)/shard_map/ppermute | solution.py:871
  48.7 16.4 %collective-permute-start.11 = (bf16[368,640]{1,0:T(8,128)(2,1)S(1)}, bf16[368,640]{1,0:T(8,128)(2,1)S(1)}, u32[]{:S(2)}, u32[]{:S(2)}) collective-permute-start(bf16[368,640]{1,0:T(8,128)(2,1)S(1)} %pick.1.rest_4_.rest_0_), channel_id=1, source_target_pairs={{0,1},{1,0},{2,3},{3,2},{4,5},{5,4},{6,7},{7,6},{8,9},{9,8},{10,11... | collective-permute-start | bytes 1413128 | tf_op jit(solution)/shard_map/ppermute | solution.py:877
  55.1 20.1 %collective-permute-start.13 = (bf16[368,640]{1,0:T(8,128)(2,1)S(1)}, bf16[368,640]{1,0:T(8,128)(2,1)S(1)}, u32[]{:S(2)}, u32[]{:S(2)}) collective-permute-start(bf16[368,640]{1,0:T(8,128)(2,1)S(1)} %hold.6.rest_2_), channel_id=1, source_target_pairs={{0,1},{1,0},{2,3},{3,2},{4,5},{5,4},{6,7},{7,6},{8,9},{9,8},{10,11... | collective-permute-start | bytes 1413128 | tf_op jit(solution)/shard_map/ppermute | solution.py:877
  78.2 43.6 %collective-permute-start.16 = (bf16[4,368,640]{2,1,0:T(8,128)(2,1)}, bf16[4,368,640]{2,1,0:T(8,128)(2,1)}, u32[]{:S(2)}, u32[]{:S(2)}) collective-permute-start(bf16[4,368,640]{2,1,0:T(8,128)(2,1)} %stack.31.rest_8_), channel_id=1, source_target_pairs={{0,8},{4,20},{8,0},{12,28},{16,24},{20,4},{24,16},{28,12},{1,9},{5... | collective-permute-start | bytes 5652488 | tf_op jit(solution)/shard_map/ppermute | solution.py:871
  78.8 43.0 %collective-permute-start.17 = (bf16[4,368,640]{2,1,0:T(8,128)(2,1)}, bf16[4,368,640]{2,1,0:T(8,128)(2,1)S(1)}, u32[]{:S(2)}, u32[]{:S(2)}) collective-permute-start(bf16[4,368,640]{2,1,0:T(8,128)(2,1)} %stack.31.rest_8_), channel_id=1, source_target_pairs={{0,16},{4,12},{8,24},{12,4},{16,0},{20,28},{24,8},{28,20},{1,17},{... | collective-permute-start | bytes 5652488 | tf_op jit(solution)/shard_map/ppermute | solution.py:871
  79.3 11.2 %collective-permute-start.7 = (bf16[960,384]{1,0:T(8,128)(2,1)S(1)}, bf16[960,384]{1,0:T(8,128)(2,1)S(1)}, u32[]{:S(2)}, u32[]{:S(2)}) collective-permute-start(bf16[960,384]{1,0:T(8,128)(2,1)S(1)} %bitcast.25), channel_id=1, source_target_pairs={{0,4},{4,0},{8,12},{12,8},{16,20},{20,16},{24,28},{28,24},{1,5},{5... | collective-permute-start | bytes 2211848 | tf_op jit(solution)/shard_map/ppermute | solution.py:871
  80.1 14.1 %collective-permute-start.8 = (bf16[960,384]{1,0:T(8,128)(2,1)}, bf16[960,384]{1,0:T(8,128)(2,1)}, u32[]{:S(2)}, u32[]{:S(2)}) collective-permute-start(bf16[960,384]{1,0:T(8,128)(2,1)} %collective-permute-done.4.refs_1_.rest_1_), channel_id=1, source_target_pairs={{0,4},{4,0},{8,12},{12,8},{16,20},{20,16},{24,28},{28,24},{1,5},{5... | collective-permute-start | bytes 2211848 | tf_op jit(solution)/shard_map/ppermute | solution.py:871
  83.1 11.1 %collective-permute-start.9 = (bf16[960,384]{1,0:T(8,128)(2,1)}, bf16[960,384]{1,0:T(8,128)(2,1)}, u32[]{:S(2)}, u32[]{:S(2)}) collective-permute-start(bf16[960,384]{1,0:T(8,128)(2,1)} %collective-permute-done.5.refs_2_.rest_2_), channel_id=1, source_target_pairs={{0,4},{4,0},{8,12},{12,8},{16,20},{20,16},{24,28},{28,24},{1,5},{5... | collective-permute-start | bytes 2211848 | tf_op jit(solution)/shard_map/ppermute | solution.py:871
  101.0 16.0 %collective-permute-start.14 = (bf16[656,256]{1,0:T(8,128)(2,1)}, bf16[656,256]{1,0:T(8,128)(2,1)S(1)}, u32[]{:S(2)}, u32[]{:S(2)}) collective-permute-start(bf16[656,256]{1,0:T(8,128)(2,1)} %get-tuple-element.101.kv2.rest_16_), channel_id=1, source_target_pairs={{0,1},{2,3},{4,5},{6,7},{8,9},{10,11},{12,13},{14,15},{16,17},{18,... | collective-permute-start | bytes 1007624 | tf_op jit(solution)/shard_map/ppermute | solution.py:910
  121.8 24.1 %collective-permute-start.18 = (bf16[4,368,640]{2,1,0:T(8,128)(2,1)}, bf16[4,368,640]{2,1,0:T(8,128)(2,1)}, u32[]{:S(2)}, u32[]{:S(2)}) collective-permute-start(bf16[4,368,640]{2,1,0:T(8,128)(2,1)} %hold.7.rest_9_), channel_id=1, source_target_pairs={{0,16},{4,12},{8,24},{12,4},{16,0},{20,28},{24,8},{28,20},{1,17},{... | collective-permute-start | bytes 5652488 | tf_op jit(solution)/shard_map/ppermute | solution.py:871
  122.9 23.0 %collective-permute-start.19 = (bf16[4,368,640]{2,1,0:T(8,128)(2,1)}, bf16[4,368,640]{2,1,0:T(8,128)(2,1)S(1)}, u32[]{:S(2)}, u32[]{:S(2)}) collective-permute-start(bf16[4,368,640]{2,1,0:T(8,128)(2,1)} %stack.31.rest_8_), channel_id=1, source_target_pairs={{0,4},{4,0},{8,12},{12,8},{16,20},{20,16},{24,28},{28,24},{1,5},{5... | collective-permute-start | bytes 5652488 | tf_op jit(solution)/shard_map/ppermute | solution.py:871
  134.7 11.3 %collective-permute-start.20 = (bf16[4,368,640]{2,1,0:T(8,128)(2,1)}, bf16[4,368,640]{2,1,0:T(8,128)(2,1)S(1)}, u32[]{:S(2)}, u32[]{:S(2)}) collective-permute-start(bf16[4,368,640]{2,1,0:T(8,128)(2,1)} %hold.7.rest_9_), channel_id=1, source_target_pairs={{0,4},{4,0},{8,12},{12,8},{16,20},{20,16},{24,28},{28,24},{1,5},{5... | collective-permute-start | bytes 5652488 | tf_op jit(solution)/shard_map/ppermute | solution.py:871
  134.9 11.1 %collective-permute-start.21 = (bf16[4,368,640]{2,1,0:T(8,128)(2,1)S(1)}, bf16[4,368,640]{2,1,0:T(8,128)(2,1)S(1)}, u32[]{:S(2)}, u32[]{:S(2)}) collective-permute-start(bf16[4,368,640]{2,1,0:T(8,128)(2,1)S(1)} %collective-permute-done.17.refs_2_.rest_10_), channel_id=1, source_target_pairs={{0,4},{4,0},{8,12},{12,8},{16,20},{20,16},{24,28},{28,24},{1,5},{5... | collective-permute-start | bytes 5652488 | tf_op jit(solution)/shard_map/ppermute | solution.py:871
  172.3 7.3 %collective-permute-start.23 = (bf16[656,256]{1,0:T(8,128)(2,1)}, bf16[656,256]{1,0:T(8,128)(2,1)S(1)}, u32[]{:S(2)}, u32[]{:S(2)}) collective-permute-start(bf16[656,256]{1,0:T(8,128)(2,1)} %get-tuple-element.105.kv2.rest_16_), channel_id=1, source_target_pairs={{0,1},{2,3},{4,5},{6,7},{8,9},{10,11},{12,13},{14,15},{16,17},{18,... | collective-permute-start | bytes 1007624 | tf_op jit(solution)/shard_map/ppermute | solution.py:910
  173.9 10.9 %collective-permute-start.28 = (bf16[256,2560]{1,0:T(8,128)(2,1)}, bf16[256,2560]{1,0:T(8,128)(2,1)S(1)}, u32[]{:S(2)}, u32[]{:S(2)}) collective-permute-start(bf16[256,2560]{1,0:T(8,128)(2,1)} %get-tuple-element.109.rest_5_), channel_id=1, source_target_pairs={{0,4},{4,0},{8,12},{12,8},{16,20},{20,16},{24,28},{28,24},{1,5},{5... | collective-permute-start | bytes 3932168 | tf_op jit(solution)/shard_map/ppermute | solution.py:871
  182.3 13.6 %collective-permute-start.29 = (bf16[960,256]{1,0:T(8,128)(2,1)S(1)}, bf16[960,256]{1,0:T(8,128)(2,1)S(1)}, u32[]{:S(2)}, u32[]{:S(2)}) collective-permute-start(bf16[960,256]{1,0:T(8,128)(2,1)S(1)} %hold.9), channel_id=1, source_target_pairs={{0,0},{1,4},{2,1},{3,5},{4,2},{5,6},{6,3},{7,7},{8,8},{9,12},{10,9... | collective-permute-start | bytes 1474568 | tf_op jit(solution)/shard_map/ppermute | solution.py:888
  215.1 28.4 %collective-permute-start.33 = (bf16[256,2560]{1,0:T(8,128)(2,1)}, bf16[256,2560]{1,0:T(8,128)(2,1)S(1)}, u32[]{:S(2)}, u32[]{:S(2)}) collective-permute-start(bf16[256,2560]{1,0:T(8,128)(2,1)} %get-tuple-element.122.rest_4_), channel_id=1, source_target_pairs={{0,4},{4,0},{8,12},{12,8},{16,20},{20,16},{24,28},{28,24},{1,5},{5... | collective-permute-start | bytes 3932168 | tf_op jit(solution)/shard_map/ppermute | solution.py:871
  237.9 25.3 %collective-permute-start.39 = (bf16[256,2560]{1,0:T(8,128)(2,1)}, bf16[256,2560]{1,0:T(8,128)(2,1)S(1)}, u32[]{:S(2)}, u32[]{:S(2)}) collective-permute-start(bf16[256,2560]{1,0:T(8,128)(2,1)} %get-tuple-element.133), channel_id=1, source_target_pairs={{0,4},{4,0},{8,12},{12,8},{16,20},{20,16},{24,28},{28,24},{1,5},{5... | collective-permute-start | bytes 3932168 | tf_op jit(solution)/shard_map/ppermute | solution.py:871
  238.5 5.0 collective-permute-start.31
  261.8 12.8 %collective-permute-start.35 = (bf16[640,256]{1,0:T(8,128)(2,1)S(1)}, bf16[640,256]{1,0:T(8,128)(2,1)S(1)}, u32[]{:S(2)}, u32[]{:S(2)}) collective-permute-start(bf16[640,256]{1,0:T(8,128)(2,1)S(1)} %far_sum.2), channel_id=1, source_target_pairs={{1,0},{3,2},{5,4},{7,6},{9,8},{11,10},{13,12},{15,14},{17,16},{19,... | collective-permute-start | bytes 983048 | tf_op jit(solution)/shard_map/ppermute | solution.py:919
  296.5 33.4 %collective-permute-start.44 = (bf16[256,2560]{1,0:T(8,128)(2,1)}, bf16[256,2560]{1,0:T(8,128)(2,1)S(1)}, u32[]{:S(2)}, u32[]{:S(2)}) collective-permute-start(bf16[256,2560]{1,0:T(8,128)(2,1)} %get-tuple-element.146), channel_id=1, source_target_pairs={{0,4},{4,0},{8,12},{12,8},{16,20},{20,16},{24,28},{28,24},{1,5},{5... | collective-permute-start | bytes 3932168 | tf_op jit(solution)/shard_map/ppermute | solution.py:871
  316.2 12.3 %collective-permute-start.41 = (bf16[640,256]{1,0:T(8,128)(2,1)S(1)}, bf16[640,256]{1,0:T(8,128)(2,1)S(1)}, u32[]{:S(2)}, u32[]{:S(2)}) collective-permute-start(bf16[640,256]{1,0:T(8,128)(2,1)S(1)} %get-tuple-element.141), channel_id=1, source_target_pairs={{0,4},{4,0},{8,12},{12,8},{16,20},{20,16},{24,28},{28,24},{1,5},{5... | collective-permute-start | bytes 983048 | tf_op jit(solution)/shard_map/ppermute | solution.py:871
  342.0 39.2 %collective-permute-start.49 = (bf16[2,960,640]{2,1,0:T(8,128)(2,1)}, bf16[2,960,640]{2,1,0:T(8,128)(2,1)S(1)}, u32[]{:S(2)}, u32[]{:S(2)}) collective-permute-start(bf16[2,960,640]{2,1,0:T(8,128)(2,1)} %get-tuple-element.147.rest_8_), channel_id=1, source_target_pairs={{0,8},{4,20},{8,0},{12,28},{16,24},{20,4},{24,16},{28,12},{1,9},{5... | collective-permute-start | bytes 7372808 | tf_op jit(solution)/shard_map/ppermute | solution.py:871
  343.0 12.8 %collective-permute-start.45 = (bf16[3,256,384]{2,1,0:T(8,128)(2,1)S(1)}, bf16[3,256,384]{2,1,0:T(8,128)(2,1)S(1)}, u32[]{:S(2)}, u32[]{:S(2)}) collective-permute-start(bf16[3,256,384]{2,1,0:T(8,128)(2,1)S(1)} %get-tuple-element.149), channel_id=1, source_target_pairs={{0,4},{4,0},{8,12},{12,8},{16,20},{20,16},{24,28},{28,24},{1,5},{5... | collective-permute-start | bytes 1769480 | tf_op jit(solution)/shard_map/ppermute | solution.py:871
  344.4 12.0 %collective-permute-start.42 = (bf16[640,256]{1,0:T(8,128)(2,1)S(1)}, bf16[640,256]{1,0:T(8,128)(2,1)S(1)}, u32[]{:S(2)}, u32[]{:S(2)}) collective-permute-start(bf16[640,256]{1,0:T(8,128)(2,1)S(1)} %copy-done.36), channel_id=1, source_target_pairs={{1,0},{3,2},{5,4},{7,6},{9,8},{11,10},{13,12},{15,14},{17,16},{19,... | collective-permute-start | bytes 983048 | tf_op jit(solution)/shard_map/ppermute | solution.py:919
  377.1 33.2 %collective-permute-start.47 = (bf16[2,960,384]{2,1,0:T(8,128)(2,1)}, bf16[2,960,384]{2,1,0:T(8,128)(2,1)S(1)}, u32[]{:S(2)}, u32[]{:S(2)}) collective-permute-start(bf16[2,960,384]{2,1,0:T(8,128)(2,1)} %get-tuple-element.161.rest_0_), channel_id=1, source_target_pairs={{0,8},{4,20},{8,0},{12,28},{16,24},{20,4},{24,16},{28,12},{1,9},{5... | collective-permute-start | bytes 4423688 | tf_op jit(solution)/shard_map/ppermute | solution.py:871
  379.5 30.0 %collective-permute-start.48 = (bf16[2,480,640]{2,1,0:T(8,128)(2,1)}, bf16[2,480,640]{2,1,0:T(8,128)(2,1)S(1)}, u32[]{:S(2)}, u32[]{:S(2)}) collective-permute-start(bf16[2,480,640]{2,1,0:T(8,128)(2,1)} %get-tuple-element.148.rest_17_), channel_id=1, source_target_pairs={{0,1},{1,0},{2,3},{3,2},{4,5},{5,4},{6,7},{7,6},{8,9},{9,8},{10,11... | collective-permute-start | bytes 3686408 | tf_op jit(solution)/shard_map/ppermute | solution.py:877
  383.6 28.9 %collective-permute-start.51 = (bf16[960,640]{1,0:T(8,128)(2,1)S(1)}, bf16[960,640]{1,0:T(8,128)(2,1)S(1)}, u32[]{:S(2)}, u32[]{:S(2)}) collective-permute-start(bf16[960,640]{1,0:T(8,128)(2,1)S(1)} %get-tuple-element.164.rest_0_), channel_id=1, source_target_pairs={{0,16},{4,12},{8,24},{12,4},{16,0},{20,28},{24,8},{28,20},{1,17},{... | collective-permute-start | bytes 3686408 | tf_op jit(solution)/shard_map/ppermute | solution.py:871
  411.7 11.5 %collective-permute-start.50 = (bf16[960,384]{1,0:T(8,128)(2,1)S(1)}, bf16[960,384]{1,0:T(8,128)(2,1)S(1)}, u32[]{:S(2)}, u32[]{:S(2)}) collective-permute-start(bf16[960,384]{1,0:T(8,128)(2,1)S(1)} %get-tuple-element.167.rest_0_), channel_id=1, source_target_pairs={{0,16},{4,12},{8,24},{12,4},{16,0},{20,28},{24,8},{28,20},{1,17},{... | collective-permute-start | bytes 2211848 | tf_op jit(solution)/shard_map/ppermute | solution.py:871
  413.5 30.1 %collective-permute-start.54 = (bf16[2,240,640]{2,1,0:T(8,128)(2,1)S(1)}, bf16[2,240,640]{2,1,0:T(8,128)(2,1)S(1)}, u32[]{:S(2)}, u32[]{:S(2)}) collective-permute-start(bf16[2,240,640]{2,1,0:T(8,128)(2,1)S(1)} %get-tuple-element.169.rest_0_), channel_id=1, source_target_pairs={{0,1},{1,0},{2,3},{3,2},{4,5},{5,4},{6,7},{7,6},{8,9},{9,8},{10,11... | collective-permute-start | bytes 1843208 | tf_op jit(solution)/shard_map/ppermute | solution.py:877
  416.1 29.2 %collective-permute-start.53 = (bf16[480,640]{1,0:T(8,128)(2,1)S(1)}, bf16[480,640]{1,0:T(8,128)(2,1)S(1)}, u32[]{:S(2)}, u32[]{:S(2)}) collective-permute-start(bf16[480,640]{1,0:T(8,128)(2,1)S(1)} %get-tuple-element.165.rest_0_), channel_id=1, source_target_pairs={{0,2},{1,3},{2,0},{3,1},{4,6},{5,7},{6,4},{7,5},{8,10},{9,11},{10,... | collective-permute-start | bytes 1843208 | tf_op jit(solution)/shard_map/ppermute | solution.py:877
  424.0 31.6 %collective-permute-start.52 = (bf16[2,240,384]{2,1,0:T(8,128)(2,1)S(1)}, bf16[2,240,384]{2,1,0:T(8,128)(2,1)S(1)}, u32[]{:S(2)}, u32[]{:S(2)}) collective-permute-start(bf16[2,240,384]{2,1,0:T(8,128)(2,1)S(1)} %get-tuple-element.171.rest_0_), channel_id=1, source_target_pairs={{0,1},{1,0},{2,3},{3,2},{4,5},{5,4},{6,7},{7,6},{8,9},{9,8},{10,11... | collective-permute-start | bytes 1105928 | tf_op jit(solution)/shard_map/ppermute | solution.py:877
  444.3 14.6 %collective-permute-start.57 = (bf16[240,640]{1,0:T(8,128)(2,1)S(1)}, bf16[240,640]{1,0:T(8,128)(2,1)S(1)}, u32[]{:S(2)}, u32[]{:S(2)}) collective-permute-start(bf16[240,640]{1,0:T(8,128)(2,1)S(1)} %get-tuple-element.174.rest_0_), channel_id=1, source_target_pairs={{0,2},{1,3},{2,0},{3,1},{4,6},{5,7},{6,4},{7,5},{8,10},{9,11},{10,... | collective-permute-start | bytes 921608 | tf_op jit(solution)/shard_map/ppermute | solution.py:877
  446.0 13.6 %collective-permute-start.56 = (bf16[2,120,640]{2,1,0:T(8,128)(2,1)S(1)}, bf16[2,120,640]{2,1,0:T(8,128)(2,1)S(1)}, u32[]{:S(2)}, u32[]{:S(2)}) collective-permute-start(bf16[2,120,640]{2,1,0:T(8,128)(2,1)S(1)} %get-tuple-element.175.rest_0_), channel_id=1, source_target_pairs={{0,8},{4,20},{8,0},{12,28},{16,24},{20,4},{24,16},{28,12},{1,9},{5... | collective-permute-start | bytes 921608 | tf_op jit(solution)/shard_map/ppermute | solution.py:871
  456.2 10.3 %collective-permute-start.55 = (bf16[240,384]{1,0:T(8,128)(2,1)S(1)}, bf16[240,384]{1,0:T(8,128)(2,1)S(1)}, u32[]{:S(2)}, u32[]{:S(2)}) collective-permute-start(bf16[240,384]{1,0:T(8,128)(2,1)S(1)} %get-tuple-element.177.rest_0_), channel_id=1, source_target_pairs={{0,2},{1,3},{2,0},{3,1},{4,6},{5,7},{6,4},{7,5},{8,10},{9,11},{10,... | collective-permute-start | bytes 552968 | tf_op jit(solution)/shard_map/ppermute | solution.py:877
  467.1 10.5 %collective-permute-start.59 = (bf16[240,384]{1,0:T(8,128)(2,1)S(1)}, bf16[240,384]{1,0:T(8,128)(2,1)S(1)}, u32[]{:S(2)}, u32[]{:S(2)}) collective-permute-start(bf16[240,384]{1,0:T(8,128)(2,1)S(1)} %sum_two.4.refs_1_.rest_0_), channel_id=1, source_target_pairs={{0,8},{4,20},{8,0},{12,28},{16,24},{20,4},{24,16},{28,12},{1,9},{5... | collective-permute-start | bytes 552968 | tf_op jit(solution)/shard_map/ppermute | solution.py:871
  469.1 9.5 %collective-permute-start.60 = (bf16[240,384]{1,0:T(8,128)(2,1)S(1)}, bf16[240,384]{1,0:T(8,128)(2,1)S(1)}, u32[]{:S(2)}, u32[]{:S(2)}) collective-permute-start(bf16[240,384]{1,0:T(8,128)(2,1)S(1)} %sum_two.4.refs_1_.rest_0_), channel_id=1, source_target_pairs={{0,16},{4,12},{8,24},{12,4},{16,0},{20,28},{24,8},{28,20},{1,17},{... | collective-permute-start | bytes 552968 | tf_op jit(solution)/shard_map/ppermute | solution.py:871
  470.2 6.8 %collective-permute-start.73 = (bf16[120,640]{1,0:T(8,128)(2,1)S(1)}, bf16[120,640]{1,0:T(8,128)(2,1)S(1)}, u32[]{:S(2)}, u32[]{:S(2)}) collective-permute-start(bf16[120,640]{1,0:T(8,128)(2,1)S(1)} %get-tuple-element.180.rest_0_), channel_id=1, source_target_pairs={{0,16},{4,12},{8,24},{12,4},{16,0},{20,28},{24,8},{28,20},{1,17},{... | collective-permute-start | bytes 460808 | tf_op jit(solution)/shard_map/ppermute | solution.py:871
  471.2 9.3 %collective-permute-start.61 = (bf16[240,384]{1,0:T(8,128)(2,1)S(1)}, bf16[240,384]{1,0:T(8,128)(2,1)S(1)}, u32[]{:S(2)}, u32[]{:S(2)}) collective-permute-start(bf16[240,384]{1,0:T(8,128)(2,1)S(1)} %sum_two.4.refs_1_.rest_0_), channel_id=1, source_target_pairs={{0,24},{4,28},{8,16},{12,20},{16,8},{20,12},{24,0},{28,4},{1,25},{... | collective-permute-start | bytes 552968 | tf_op jit(solution)/shard_map/ppermute | solution.py:871
  471.8 9.4 %collective-permute-start.62 = (bf16[240,384]{1,0:T(8,128)(2,1)S(1)}, bf16[240,384]{1,0:T(8,128)(2,1)S(1)}, u32[]{:S(2)}, u32[]{:S(2)}) collective-permute-start(bf16[240,384]{1,0:T(8,128)(2,1)S(1)} %sum_two.4.refs_1_.rest_0_), channel_id=1, source_target_pairs={{0,4},{4,0},{8,12},{12,8},{16,20},{20,16},{24,28},{28,24},{1,5},{5... | collective-permute-start | bytes 552968 | tf_op jit(solution)/shard_map/ppermute | solution.py:871
  476.9 9.5 %collective-permute-start.66 = (bf16[240,640]{1,0:T(8,128)(2,1)S(1)}, bf16[240,640]{1,0:T(8,128)(2,1)S(1)}, u32[]{:S(2)}, u32[]{:S(2)}) collective-permute-start(bf16[240,640]{1,0:T(8,128)(2,1)S(1)} %sum_two.3.rest_0_), channel_id=1, source_target_pairs={{0,8},{4,20},{8,0},{12,28},{16,24},{20,4},{24,16},{28,12},{1,9},{5... | collective-permute-start | bytes 921608 | tf_op jit(solution)/shard_map/ppermute | solution.py:871
  477.6 10.2 %collective-permute-start.67 = (bf16[240,640]{1,0:T(8,128)(2,1)S(1)}, bf16[240,640]{1,0:T(8,128)(2,1)S(1)}, u32[]{:S(2)}, u32[]{:S(2)}) collective-permute-start(bf16[240,640]{1,0:T(8,128)(2,1)S(1)} %sum_two.3.rest_0_), channel_id=1, source_target_pairs={{0,16},{4,12},{8,24},{12,4},{16,0},{20,28},{24,8},{28,20},{1,17},{... | collective-permute-start | bytes 921608 | tf_op jit(solution)/shard_map/ppermute | solution.py:871
  478.6 14.9 %collective-permute-start.68 = (bf16[240,640]{1,0:T(8,128)(2,1)S(1)}, bf16[240,640]{1,0:T(8,128)(2,1)S(1)}, u32[]{:S(2)}, u32[]{:S(2)}) collective-permute-start(bf16[240,640]{1,0:T(8,128)(2,1)S(1)} %sum_two.3.rest_0_), channel_id=1, source_target_pairs={{0,24},{4,28},{8,16},{12,20},{16,8},{20,12},{24,0},{28,4},{1,25},{... | collective-permute-start | bytes 921608 | tf_op jit(solution)/shard_map/ppermute | solution.py:871
  480.4 20.9 %collective-permute-start.58 = (bf16[960,256]{1,0:T(8,128)(2,1)S(1)}, bf16[960,256]{1,0:T(8,128)(2,1)S(1)}, u32[]{:S(2)}, u32[]{:S(2)}) collective-permute-start(bf16[960,256]{1,0:T(8,128)(2,1)S(1)} %hold.11), channel_id=1, source_target_pairs={{0,0},{4,1},{1,2},{5,3},{2,4},{6,5},{3,6},{7,7},{8,8},{12,9},{9,10... | collective-permute-start | bytes 1474568 | tf_op jit(solution)/shard_map/ppermute | solution.py:888
  481.1 13.4 %collective-permute-start.69 = (bf16[240,640]{1,0:T(8,128)(2,1)S(1)}, bf16[240,640]{1,0:T(8,128)(2,1)S(1)}, u32[]{:S(2)}, u32[]{:S(2)}) collective-permute-start(bf16[240,640]{1,0:T(8,128)(2,1)S(1)} %sum_two.3.rest_0_), channel_id=1, source_target_pairs={{0,4},{4,0},{8,12},{12,8},{16,20},{20,16},{24,28},{28,24},{1,5},{5... | collective-permute-start | bytes 921608 | tf_op jit(solution)/shard_map/ppermute | solution.py:871
  486.5 17.3 %collective-permute-start.70 = (bf16[240,640]{1,0:T(8,128)(2,1)S(1)}, bf16[240,640]{1,0:T(8,128)(2,1)S(1)}, u32[]{:S(2)}, u32[]{:S(2)}) collective-permute-start(bf16[240,640]{1,0:T(8,128)(2,1)S(1)} %collective-permute-done.66.rest_1_), channel_id=1, source_target_pairs={{0,4},{4,0},{8,12},{12,8},{16,20},{20,16},{24,28},{28,24},{1,5},{5... | collective-permute-start | bytes 921608 | tf_op jit(solution)/shard_map/ppermute | solution.py:871
  487.7 16.0 %collective-permute-start.71 = (bf16[240,640]{1,0:T(8,128)(2,1)S(1)}, bf16[240,640]{1,0:T(8,128)(2,1)S(1)}, u32[]{:S(2)}, u32[]{:S(2)}) collective-permute-start(bf16[240,640]{1,0:T(8,128)(2,1)S(1)} %collective-permute-done.67.rest_2_), channel_id=1, source_target_pairs={{0,4},{4,0},{8,12},{12,8},{16,20},{20,16},{24,28},{28,24},{1,5},{5... | collective-permute-start | bytes 921608 | tf_op jit(solution)/shard_map/ppermute | solution.py:871
  493.5 10.8 %collective-permute-start.72 = (bf16[240,640]{1,0:T(8,128)(2,1)S(1)}, bf16[240,640]{1,0:T(8,128)(2,1)S(1)}, u32[]{:S(2)}, u32[]{:S(2)}) collective-permute-start(bf16[240,640]{1,0:T(8,128)(2,1)S(1)} %collective-permute-done.68.rest_3_), channel_id=1, source_target_pairs={{0,4},{4,0},{8,12},{12,8},{16,20},{20,16},{24,28},{28,24},{1,5},{5... | collective-permute-start | bytes 921608 | tf_op jit(solution)/shard_map/ppermute | solution.py:871
  494.5 5.7 %collective-permute-start.74 = (bf16[120,640]{1,0:T(8,128)(2,1)S(1)}, bf16[120,640]{1,0:T(8,128)(2,1)S(1)}, u32[]{:S(2)}, u32[]{:S(2)}) collective-permute-start(bf16[120,640]{1,0:T(8,128)(2,1)S(1)} %sum_two.5.rest_8_.rest_0_), channel_id=1, source_target_pairs={{0,8},{4,20},{8,0},{12,28},{16,24},{20,4},{24,16},{28,12},{1,9},{5... | collective-permute-start | bytes 460808 | tf_op jit(solution)/shard_map/ppermute | solution.py:871
  500.3 8.5 %collective-permute-start.75 = (bf16[120,640]{1,0:T(8,128)(2,1)S(1)}, bf16[120,640]{1,0:T(8,128)(2,1)S(1)}, u32[]{:S(2)}, u32[]{:S(2)}) collective-permute-start(bf16[120,640]{1,0:T(8,128)(2,1)S(1)} %sum_two.5.rest_8_.rest_0_), channel_id=1, source_target_pairs={{0,16},{4,12},{8,24},{12,4},{16,0},{20,28},{24,8},{28,20},{1,17},{... | collective-permute-start | bytes 460808 | tf_op jit(solution)/shard_map/ppermute | solution.py:871
  501.3 7.7 %collective-permute-start.76 = (bf16[120,640]{1,0:T(8,128)(2,1)S(1)}, bf16[120,640]{1,0:T(8,128)(2,1)S(1)}, u32[]{:S(2)}, u32[]{:S(2)}) collective-permute-start(bf16[120,640]{1,0:T(8,128)(2,1)S(1)} %sum_two.5.rest_8_.rest_0_), channel_id=1, source_target_pairs={{0,24},{4,28},{8,16},{12,20},{16,8},{20,12},{24,0},{28,4},{1,25},{... | collective-permute-start | bytes 460808 | tf_op jit(solution)/shard_map/ppermute | solution.py:871
  503.8 5.5 %collective-permute-start.63 = (bf16[240,384]{1,0:T(8,128)(2,1)S(1)}, bf16[240,384]{1,0:T(8,128)(2,1)S(1)}, u32[]{:S(2)}, u32[]{:S(2)}) collective-permute-start(bf16[240,384]{1,0:T(8,128)(2,1)S(1)} %collective-permute-done.59.rest_1_), channel_id=1, source_target_pairs={{0,4},{4,0},{8,12},{12,8},{16,20},{20,16},{24,28},{28,24},{1,5},{5... | collective-permute-start | bytes 552968 | tf_op jit(solution)/shard_map/ppermute | solution.py:871
  503.8 5.7 %collective-permute-start.64 = (bf16[240,384]{1,0:T(8,128)(2,1)S(1)}, bf16[240,384]{1,0:T(8,128)(2,1)S(1)}, u32[]{:S(2)}, u32[]{:S(2)}) collective-permute-start(bf16[240,384]{1,0:T(8,128)(2,1)S(1)} %collective-permute-done.60.rest_2_), channel_id=1, source_target_pairs={{0,4},{4,0},{8,12},{12,8},{16,20},{20,16},{24,28},{28,24},{1,5},{5... | collective-permute-start | bytes 552968 | tf_op jit(solution)/shard_map/ppermute | solution.py:871
  504.3 5.5 %collective-permute-start.65 = (bf16[240,384]{1,0:T(8,128)(2,1)S(1)}, bf16[240,384]{1,0:T(8,128)(2,1)S(1)}, u32[]{:S(2)}, u32[]{:S(2)}) collective-permute-start(bf16[240,384]{1,0:T(8,128)(2,1)S(1)} %collective-permute-done.61.rest_3_), channel_id=1, source_target_pairs={{0,4},{4,0},{8,12},{12,8},{16,20},{20,16},{24,28},{28,24},{1,5},{5... | collective-permute-start | bytes 552968 | tf_op jit(solution)/shard_map/ppermute | solution.py:871
  508.8 7.4 %collective-permute-start.77 = (bf16[120,640]{1,0:T(8,128)(2,1)S(1)}, bf16[120,640]{1,0:T(8,128)(2,1)}, u32[]{:S(2)}, u32[]{:S(2)}) collective-permute-start(bf16[120,640]{1,0:T(8,128)(2,1)S(1)} %sum_two.5.rest_8_.rest_0_), channel_id=1, source_target_pairs={{0,4},{4,0},{8,12},{12,8},{16,20},{20,16},{24,28},{28,24},{1,5},{5... | collective-permute-start | bytes 460808 | tf_op jit(solution)/shard_map/ppermute | solution.py:871
  509.0 7.3 %collective-permute-start.78 = (bf16[120,640]{1,0:T(8,128)(2,1)S(1)}, bf16[120,640]{1,0:T(8,128)(2,1)}, u32[]{:S(2)}, u32[]{:S(2)}) collective-permute-start(bf16[120,640]{1,0:T(8,128)(2,1)S(1)} %collective-permute-done.74.rest_1_), channel_id=1, source_target_pairs={{0,4},{4,0},{8,12},{12,8},{16,20},{20,16},{24,28},{28,24},{1,5},{5... | collective-permute-start | bytes 460808 | tf_op jit(solution)/shard_map/ppermute | solution.py:871
  509.3 6.9 %collective-permute-start.79 = (bf16[120,640]{1,0:T(8,128)(2,1)S(1)}, bf16[120,640]{1,0:T(8,128)(2,1)}, u32[]{:S(2)}, u32[]{:S(2)}) collective-permute-start(bf16[120,640]{1,0:T(8,128)(2,1)S(1)} %collective-permute-done.75.rest_2_), channel_id=1, source_target_pairs={{0,4},{4,0},{8,12},{12,8},{16,20},{20,16},{24,28},{28,24},{1,5},{5... | collective-permute-start | bytes 460808 | tf_op jit(solution)/shard_map/ppermute | solution.py:871
  509.5 6.7 %collective-permute-start.80 = (bf16[120,640]{1,0:T(8,128)(2,1)S(1)}, bf16[120,640]{1,0:T(8,128)(2,1)}, u32[]{:S(2)}, u32[]{:S(2)}) collective-permute-start(bf16[120,640]{1,0:T(8,128)(2,1)S(1)} %collective-permute-done.76.rest_3_), channel_id=1, source_target_pairs={{0,4},{4,0},{8,12},{12,8},{16,20},{20,16},{24,28},{28,24},{1,5},{5... | collective-permute-start | bytes 460808 | tf_op jit(solution)/shard_map/ppermute | solution.py:871
  (99 other events, 1021.0 us)

commit v11 on v10

--- a/solution.py
+++ b/solution.py
@@ -419,6 +419,8 @@
         (g_ref,) = take(1)
     else:
         g1_in, dq_ref, own_ref, near_ref, far_ref, h_ref, gain_a, cos_ref, sin_ref = take(9)
+        if end:
+            (last_ref,) = take(1)
     if not end:
         ins = take(4)
     take(after)
@@ -441,7 +443,9 @@
         dgain_a[...] = dgain
         state = g1_in[...] + dx
     if end:
-        g_out[...] = state.astype(bf16).T
+        width = state.shape[1]
+        g_out[:width, :] = last_ref[...]
+        g_out[width:, :] = state.astype(bf16).T
         finish_a(wa, sem_a, (1, 1), (1, 2), (1, 3))
     else:
         ffn_back(state, core, (*ins, *outs), (wa, sem_a, wb, sem_b, wd, sem_d))
@@ -469,7 +473,7 @@
     if not start:
         outs += [shape((n, PIECE), bf16)] * 3 + [shape((1, width), f32)]
     if end:
-        outs += [shape((width, n), bf16)]
+        outs += [shape((2 * width, n), bf16)]
     else:
         hidden = ffn[0].shape[1]
         outs += [shape((n, width), bf16), shape((n, hidden), bf16), shape((n, hidden), bf16)]
@@ -564,7 +568,7 @@
     a_refs, o_refs, rest = rest[:4], rest[4:8], rest[8:]
     queries, keys, values, outs, threes, ones = (rest[i : i + 2] for i in range(0, 12, 2))
     gain_a, gain_f = (rest[i : i + 2] for i in (12, 14))
-    send_ref, keep_ref, left, right = rest[-4:]
+    *sends, keep_ref, left, right = rest[-5:]
     core, chip = sc[0], sc[1]
     n, width = a_refs[0].shape
     turned(left.at[0], a_refs)
@@ -590,20 +594,20 @@
         fill(0, 1, outs, values, 0)
 
     for i, m in enumerate(by_turn(core, chip)):
-        out = send_ref if i < 2 else keep_ref
+        out = sends[i] if i < 2 else keep_ref.at[i - 2]
         which = jnp.where(m > 0, core, 0)
-        out[i % 2] = nn(left[which], right[m]).astype(bf16)
-        out[i % 2, :, KVW:] = gains
+        out[...] = nn(left[which], right[m]).astype(bf16)
+        out[:, KVW:] = gains
 
 
 def grad_attention(sc, a, o, own, got, gains, after):
     n, width = a[0].shape
-    out = shape((2, width, PIECE), bf16)
+    out = shape((width, PIECE), bf16)
     return pl.pallas_call(
         grad_attention_kernel,
-        out_shape=(out, out),
+        out_shape=(out, out, shape((2, width, PIECE), bf16)),
         in_specs=[SCALARS] + [WHOLE] * 24 + [LEFT] * len(after),
-        out_specs=(WHOLE,) * 2,
+        out_specs=(WHOLE,) * 3,
         scratch_shapes=[pltpu.VMEM((2, width, 4 * n), bf16), pltpu.VMEM((4, 4 * n, PIECE), bf16)],
         cost_estimate=BRIEF,
         compiler_params=pltpu.CompilerParams(vmem_limit_bytes=LIMIT),
@@ -762,23 +766,28 @@
     )(sc, *args, *after)
 
 
-def sum_first(sc, keep, got, after):
-    def kernel(sc, keep_ref, got_ref, *rest):
-        later_ref, own_ref = rest[-2:]
-        later_ref[...] = (keep_ref[1].astype(f32) + got_ref[1].astype(f32)).astype(bf16)
-        own_ref[...] = keep_ref[0].astype(f32) + got_ref[0].astype(f32)
-
-    block = keep.shape[1:]
-    return small(kernel, sc, [keep, got], [shape(block, bf16), shape(block, f32)], [], after, "sum_first")
+def sum_first(sc, keep, got, after, parts=1):
+    def kernel(sc, keep_ref, *rest):
+        own_got, later_got = rest[:2] if len(got) == 2 else (rest[0].at[0], rest[0].at[1])
+        own_ref = rest[-1]
+        for i, later_ref in enumerate(rest[-1 - parts : -1]):
+            n = later_ref.shape[0]
+            rows = slice(i * n, (i + 1) * n)
+            later_ref[...] = (keep_ref[1, rows].astype(f32) + later_got[rows].astype(f32)).astype(bf16)
+        own_ref[...] = keep_ref[0].astype(f32) + own_got[...].astype(f32)
+
+    rows, cols = keep.shape[1:]
+    outs = [shape((rows // parts, cols), bf16)] * parts + [shape((rows, cols), f32)]
+    return small(kernel, sc, [keep, *got], outs, [], after, "sum_first")
 
 
 def sum_second(sc, own, got, after):
-    def kernel(sc, own_ref, got_ref, *rest):
-        send_ref, keep_ref, total = rest[-3:]
+    def kernel(sc, own_ref, *rest):
+        gots, (send_ref, keep_ref, total) = rest[: len(got)], rest[-3:]
         n = total.shape[1]
         for j in range(4):
-            rows = slice(j * n, (j + 1) * n)
-            total[j] = own_ref[rows, :] + got_ref[rows, :].astype(f32)
+            part, at = divmod(j * n, gots[0].shape[0])
+            total[j] = own_ref[j * n : (j + 1) * n, :] + gots[part][at : at + n, :].astype(f32)
         like = sc[2] & 1
         for h in range(2):
             send_ref[h] = total[2 * h + 1 - like].astype(bf16)
@@ -787,7 +796,7 @@
     rows, cols = own.shape
     part = (rows // 4, cols)
     outs = [shape((2,) + part, bf16), shape((2,) + part, f32)]
-    return small(kernel, sc, [own, got], outs, [pltpu.VMEM((4,) + part, f32)], after, "sum_second")
+    return small(kernel, sc, [own, *got], outs, [pltpu.VMEM((4,) + part, f32)], after, "sum_second")
 
 
 def sum_third(sc, keep, got, after):
@@ -955,8 +964,9 @@
     gains = gains_of(whole_a)
     gain_a, gain_f = gains[:1], gains[1:]
     wa = plane_gather(whole_a.reshape(depth * rows, PIECE))
-    far_b = hold(flip_z(piece_b, 2), [wa[0][1], wa[0][2]])
-    whole_b = stack(sc, (piece_b, flip_z(piece_b, 1), far_b, flip_z(far_b, 1)), [wa[0][3]])
+    side_b = flip_z(piece_b, 1)
+    far_b = hold(flip_z(piece_b, 2), [wa[0][1], wa[0][2], side_b])
+    whole_b = stack(sc, (piece_b, side_b, far_b, flip_z(far_b, 1)), [wa[0][3]])
     first_b, second_b = flip(whole_b, SIDE, BACK), flip(whole_b, BACK, SIDE)
 
     h_0, a0, q0, own = pre(sc, tokens, gain_a, cos, sin, *wa, [whole_b])
@@ -980,44 +990,42 @@
     dq1, three1, far, near, own = attend_back(sc, p1, q1, kv1, lse1, do, cos, sin, [*across_1])
     near, _, far = unwindow(sc, far, near)
     (three1,) = across((three1,))
-    output = home_to_work(hold(output, [far]), back=True)
     tail = [g1, dq1, own, near, far, h_1, gain_a, cos, sin]
     dk1, dv1, one1, dgain_a1, gb0, act0, away0, g1, p0, dgain_f0, do = back(False, False, sc, weights, tail, [gate0, up0, h1_0, gain_f], [three1, *across_2])
 
     away0, gb0_, one1 = across((away0, gb0, one1))
-    dq0, three0, far, near, own = attend_back(sc, p0, q0, kv0, lse0, do, cos, sin, [one1, output])
-    near, down_far, far = unwindow(sc, far, near)
-    send_b, keep_b = grad_ffn(sc, [b1, b0, across_1[1], across_0[1]], [act1, act0, across_2[1], away0], [down_far])
+    send_b, keep_b = grad_ffn(sc, [b1, b0, across_1[1], across_0[1]], [act1, act0, across_2[1], away0], [])
     got_b = flip(send_b, SIDE, BACK)
     send_d, keep_d = grad_down(sc, [gb1, gb0, across_2[0], gb0_], [z1, z0, across_1[3], across_0[3]], [send_b])
     got_d = flip_z(send_d, 1)
+    dq0, three0, far, near, own = attend_back(sc, p0, q0, kv0, lse0, do, cos, sin, [one1, send_d])
+    near, down_far, far = unwindow(sc, far, near)
     (three0,) = across((three0,))
-    tail = [g1, dq0, own, near, far, h_0, gain_a, cos, sin]
-    dk0, dv0, one0, dgain_a0, grad_tokens = back(False, True, sc, weights, tail, None, [send_d, three0])
-
-    own = [dq1, dq0, dk1, dk0, dv1, dv0, p1, p0]
-    got = [three1, three0, one1, flip(one0, CORE)]
-    send_a, keep_a = grad_attention(sc, [a1, a0, across_1[0], across_0[0]], [mixed1, mixed0, across_1[2], across_0[2]], own, got, [dgain_a1, dgain_a0, dgain_f1, dgain_f0], [])
-    got_a = flip(send_a, SIDE, BACK)
-    later_b, own_b = sum_first(sc, keep_b, got_b, [send_a])
+    later_b, own_b = sum_first(sc, keep_b, [got_b], [far])
     more_b = flip(later_b, BACK, SIDE)
     send_d, keep_d = sum_third(sc, keep_d, got_d, [later_b])
     got_d = flip_z(send_d, 2)
-    later_a, own_a = sum_first(sc, keep_a, got_a, [send_d])
-    more_a = flip(later_a, BACK, SIDE)
-    send_b, ring_b = sum_second(sc, own_b, more_b, [later_a])
+    tail = [g1, dq0, own, near, far, h_0, gain_a, cos, sin, output]
+    dk0, dv0, one0, dgain_a0, leaving = back(False, True, sc, weights, tail, None, [send_d])
+    own = [dq1, dq0, dk1, dk0, dv1, dv0, p1, p0]
+    got = [three1, three0, one1, flip(one0, CORE)]
+    *send_a, keep_a = grad_attention(sc, [a1, a0, across_1[0], across_0[0]], [mixed1, mixed0, across_1[2], across_0[2]], own, got, [dgain_a1, dgain_a0, dgain_f1, dgain_f0], [send_d])
+    got_a = [flip(v, SIDE, BACK) for v in send_a]
+    send_b, ring_b = sum_second(sc, own_b, [more_b], send_a)
     got_b = flip_z(send_b, 1)
+    *later_a, own_a = sum_first(sc, keep_a, got_a, [ring_b], 2)
+    more_a = [flip(v, BACK, SIDE) for v in later_a]
+    send_d, keep_d = down_split(sc, keep_d, got_d, [own_a])
+    got_d = flip(send_d, SIDE, BACK)
+    send_b, ring_b = sum_third(sc, ring_b, got_b, [send_d])
+    got_b = flip_z(send_b, 2)
     send_a, ring_a = sum_second(sc, own_a, more_a, [send_b])
     got_a = flip_z(send_a, 1)
-    send_b, ring_b = sum_third(sc, ring_b, got_b, [send_a])
-    got_b = flip_z(send_b, 2)
-    send_d, keep_d = down_split(sc, keep_d, got_d, [send_b])
-    got_d = flip(send_d, SIDE, BACK)
-    send_a, ring_a = sum_third(sc, ring_a, got_a, [send_d])
-    got_a = flip_z(send_a, 2)
     piece_b = over_groups(sum_two(sc, ring_b, got_b, [send_a]))
     all_b = spread(piece_b)
-    later_d, own_d = sum_first(sc, keep_d, got_d, [piece_b])
+    send_a, ring_a = sum_third(sc, ring_a, got_a, [piece_b])
+    got_a = flip_z(send_a, 2)
+    later_d, own_d = sum_first(sc, keep_d, [got_d], [send_a])
     more_d = flip(later_d, BACK, SIDE)
     piece_a = over_groups(sum_two(sc, ring_a, got_a, [later_d]))
     all_a = spread(piece_a)
@@ -1026,8 +1034,8 @@
     all_d = spread(piece_d)
     grad_query, grad_key, grad_value, grad_out, dgains = lay(sc, all_a, across(all_a), (width, KVW, KVW, width), [grad_gate])
     grad_down_ = lay_down(sc, all_d, across(all_d), [grad_query])
-    grad_tokens = home_to_work(hold(grad_tokens, [piece_a]), back=True)
-    grad_tokens, output = grad_tokens.astype(f32).T, output.T
+    leaving = home_to_work(hold(leaving, [piece_b]), back=True)
+    output, grad_tokens = leaving[:width].T, leaving[width:].astype(f32).T
     return (output[None], grad_tokens[None], dgains[0], grad_query, grad_key, grad_value, grad_out, dgains[1], grad_gate, grad_up, grad_down_.T)
 
 

time: 525 us -> 500 us (0.952)
  waiting for transfers between devices: 190 us -> 176 us
  starting transfers between devices: 97.7 us -> 83.9 us
    ppermute x12, waiting for transfers between devices: 95 us -> 57.9 us  [flip_z(): return lax.ppermute(value, ('dp', 'fsdp'), pairs)]
    ppermute x2, waiting for transfers between devices: 12 us -> 29.2 us  [unwindow(): lax.ppermute(far, 'fsdp', [(z + 1, z) for z in range(0, depth, 2)])]
    ppermute x61 -> x63, starting transfers between devices: 62 us -> 48.4 us  [flip(): lax.ppermute(value, 'dp', [(i, i ^ bits[i & 1]) for i in range(count)])]
    ppermute x61 -> x63, waiting for transfers between devices: 69.7 us -> 75.5 us  [flip(): lax.ppermute(value, 'dp', [(i, i ^ bits[i & 1]) for i in range(count)])]
    unnamed x168 -> x165, local copies, waits for them, and re-layouts: 29.4 us -> 28.5 us
  transfers between devices with their start and end apart: 81 -> 82, of which waited for: 38 -> 38; matrix products, arithmetic and copies ran while one was open for 1% -> 1% of each run, Pallas kernels for 22% -> 24%
where the time goes in v11:
time: 500 us; the launch traced here: 495 us
  Pallas kernels  197 us (39%)
  waiting for transfers between devices  176 us (35%)
  starting transfers between devices  83.9 us (17%)
  local copies, waits for them, and re-layouts  31 us (6%)
    ppermute x63, waiting for transfers between devices, flip(): lax.ppermute(value, 'dp', [(i, i ^ bits[i & 1]) for i in range(count)])  75.5 us
    ppermute x12, waiting for transfers between devices, flip_z(): return lax.ppermute(value, ('dp', 'fsdp'), pairs)  57.9 us
    pallas_call x3, Pallas kernels, back(): pl.pallas_call(functools.partial(back_kernel, start, end, len(after)), ou...  48.6 us
    ppermute x63, starting transfers between devices, flip(): lax.ppermute(value, 'dp', [(i, i ^ bits[i & 1]) for i in range(count)])  48.4 us
    pallas_call x2, Pallas kernels, post(): pl.pallas_call(functools.partial(post_kernel, last, len(after)), out_shap...  39.3 us
    ppermute x2, waiting for transfers between devices, unwindow(): lax.ppermute(far, 'fsdp', [(z + 1, z) for z in range(0, depth, 2)])  29.2 us
    unnamed x165, local copies, waits for them, and re-layouts  28.5 us
    pallas_call x2, Pallas kernels, attend_back(): pl.pallas_call(attend_back_kernel, out_shape=(shape((3, n, PIECE), bf16),...  26.1 us
  transfers between devices with their start and end apart: 82, of which 38 were waited for; matrix products, arithmetic and copies ran while one was open for 1% of the time, Pallas kernels for 24%

profile of v11, /device:TPU:0, one launch (start us, length us, event | category | flops | bytes accessed | tf_op | source)
XLA Modules:
  0.0 494.7 jit_solution(10231645763270638675)
XLA Ops:
  0.7 1.9 copy.36
  8.8 4.1 collective-permute-start.1
  12.9 1.6 collective-permute-start
  14.4 7.2 %collective-permute-done.1.rest_2_ = bf16[240,384]{1,0:T(8,128)(2,1)S(1)} collective-permute-done((bf16[240,384]{1,0:T(8,128)(2,1)S(1)}, bf16[240,384]{1,0:T(8,128)(2,1)S(1)}, u32[]{:S(2)}, u32[]{:S(2)}) %collective-permute-start.1) | collective-permute-done | bytes 184352 | tf_op jit(solution)/shard_map/ppermute | solution.py:886
  24.4 3.1 collective-permute-done.2.rest_3_
  27.4 1.5 stack.30.first_ref
  30.3 1.5 collective-permute-start.4
  31.8 3.2 collective-permute-start.11
  35.0 1.7 collective-permute-start.10
  36.8 11.8 %collective-permute-done.3.refs_1_.rest_1_ = bf16[960,384]{1,0:T(8,128)(2,1)} collective-permute-done((bf16[960,384]{1,0:T(8,128)(2,1)S(1)}, bf16[960,384]{1,0:T(8,128)(2,1)}, u32[]{:S(2)}, u32[]{:S(2)}) %collective-permute-start.3) | collective-permute-done | bytes 737312 | tf_op jit(solution)/shard_map/ppermute | solution.py:880
  48.7 6.4 %collective-permute-done.11.refs_0_ = bf16[368,640]{1,0:T(8,128)(2,1)S(1)} collective-permute-done((bf16[368,640]{1,0:T(8,128)(2,1)S(1)}, bf16[368,640]{1,0:T(8,128)(2,1)S(1)}, u32[]{:S(2)}, u32[]{:S(2)}) %collective-permute-start.11) | collective-permute-done | bytes 471072 | tf_op jit(solution)/shard_map/ppermute | solution.py:886
  56.8 10.0 %collective-permute-done.12.rest_3_ = bf16[368,640]{1,0:T(8,128)(2,1)S(1)} collective-permute-done((bf16[368,640]{1,0:T(8,128)(2,1)S(1)}, bf16[368,640]{1,0:T(8,128)(2,1)S(1)}, u32[]{:S(2)}, u32[]{:S(2)}) %collective-permute-start.12) | collective-permute-done | bytes 471072 | tf_op jit(solution)/shard_map/ppermute | solution.py:886
  66.9 3.0 stack.31.rest_8_
  71.8 4.6 collective-permute-start.8
  76.4 5.9 %collective-permute-start.7 = (bf16[960,384]{1,0:T(8,128)(2,1)}, bf16[960,384]{1,0:T(8,128)(2,1)}, u32[]{:S(2)}, u32[]{:S(2)}) collective-permute-start(bf16[960,384]{1,0:T(8,128)(2,1)} %collective-permute-done.3.refs_1_.rest_1_), channel_id=1, source_target_pairs={{0,4},{4,0},{8,12},{12,8},{16,20},{20,16},{24,28},{28,24},{1,5},{5... | collective-permute-start | bytes 2211848 | tf_op jit(solution)/shard_map/ppermute | solution.py:880
  85.9 6.8 %pre.1 = (bf16[256,960]{1,0:T(8,128)(2,1)}, bf16[256,960]{1,0:T(8,128)(2,1)}, bf16[960,256]{1,0:T(8,128)(2,1)}, bf16[656,256]{1,0:T(8,128)(2,1)}) custom-call(s32[3]{0:T(128)} %copy-done.50, bf16[976,256]{1,0:T(8,128)(2,1)} %copy-done.75, f32[1,960]{1,0:T(1,128)} %get-tuple-element.207.gain_ref.gain_a.rest_22_.rest_14_, ...), custom_call_target="tpu_custom_call" | custom-call | flops 1024 | bytes 1024 | tf_op jit(solution)/shard_map/pre/pallas_call | solution.py:119
  92.8 9.3 %collective-permute-start.15 = (bf16[656,256]{1,0:T(8,128)(2,1)}, bf16[656,256]{1,0:T(8,128)(2,1)S(1)}, u32[]{:S(2)}, u32[]{:S(2)}) collective-permute-start(bf16[656,256]{1,0:T(8,128)(2,1)} %get-tuple-element.102.kv2.rest_16_), channel_id=1, source_target_pairs={{0,1},{2,3},{4,5},{6,7},{8,9},{10,11},{12,13},{14,15},{16,17},{18,... | collective-permute-start | bytes 1007624 | tf_op jit(solution)/shard_map/ppermute | solution.py:919
  102.1 8.3 %collective-permute-done.15.refs_1_.kv0 = bf16[656,256]{1,0:T(8,128)(2,1)S(1)} collective-permute-done((bf16[656,256]{1,0:T(8,128)(2,1)}, bf16[656,256]{1,0:T(8,128)(2,1)S(1)}, u32[]{:S(2)}, u32[]{:S(2)}) %collective-permute-start.15) | collective-permute-done | bytes 335904 | tf_op jit(solution)/shard_map/ppermute | solution.py:919
  113.5 10.1 %attend.2 = (bf16[960,256]{1,0:T(8,128)(2,1)S(1)}, f32[15,256]{1,0:T(8,128)S(1)}) custom-call(bf16[960,256]{1,0:T(8,128)(2,1)S(1)} %copy-done.27, bf16[656,256]{1,0:T(8,128)(2,1)S(1)} %collective-permute-done.15.refs_1_.kv0, bf16[656,256]{1,0:T(8,128)(2,1)S(1)} %collective-permute-done.18.kv1, bf16[656,256]{1,0:T(8,128)(2,1)S(1)} %copy-done.5), custom_call_target="tpu_custom_call" | custom-call | flops 1024 | bytes 1024 | tf_op jit(solution)/shard_map/attend/pallas_call | solution.py:172
  124.2 11.0 %collective-permute-done.17.refs_0_ = bf16[4,368,640]{2,1,0:T(8,128)(2,1)} collective-permute-done((bf16[4,368,640]{2,1,0:T(8,128)(2,1)}, bf16[4,368,640]{2,1,0:T(8,128)(2,1)}, u32[]{:S(2)}, u32[]{:S(2)}) %collective-permute-start.17) | collective-permute-done | bytes 1884192 | tf_op jit(solution)/shard_map/ppermute | solution.py:880
  140.7 20.9 %post.2 = (bf16[256,960]{1,0:T(8,128)(2,1)}, f32[256,960]{1,0:T(8,128)}, bf16[256,960]{1,0:T(8,128)(2,1)}, bf16[256,2560]{1,0:T(8,128)(2,1)}, bf16[256,2560]{1,0...) custom-call(s32[3]{0:T(128)} %copy-done.50, ...), custom_call_target="tpu_custom_call" | custom-call | flops 1024 | bytes 1024 | tf_op jit(solution)/shard_map/post/pallas_call | solution.py:328
  161.6 4.0 collective-permute-start.23
  165.7 5.5 %collective-permute-done.23.kv0 = bf16[656,256]{1,0:T(8,128)(2,1)S(1)} collective-permute-done((bf16[656,256]{1,0:T(8,128)(2,1)}, bf16[656,256]{1,0:T(8,128)(2,1)S(1)}, u32[]{:S(2)}, u32[]{:S(2)}) %collective-permute-start.23) | collective-permute-done | bytes 335904 | tf_op jit(solution)/shard_map/ppermute | solution.py:919
  176.3 10.5 %attend.3 = (bf16[960,256]{1,0:T(8,128)(2,1)S(1)}, f32[15,256]{1,0:T(8,128)S(1)}) custom-call(bf16[960,256]{1,0:T(8,128)(2,1)S(1)} %copy-done.30, bf16[656,256]{1,0:T(8,128)(2,1)S(1)} %collective-permute-done.23.kv0, bf16[656,256]{1,0:T(8,128)(2,1)S(1)} %collective-permute-done.24.refs_1_.kv1, bf16[656,256]{1,0:T(8,128)(2,1)S(1)} %copy-done.3, ...), custom_call_target="tpu_custom_call" | custom-call | flops 1024 | bytes 1024 | tf_op jit(solution)/shard_map/attend/pallas_call | solution.py:172
  188.5 18.3 %post.3 = (bf16[256,960]{1,0:T(8,128)(2,1)}, f32[256,960]{1,0:T(8,128)}, bf16[256,960]{1,0:T(8,128)(2,1)}, bf16[256,2560]{1,0:T(8,128)(2,1)}, bf16[256,2560]{1,0...) custom-call(s32[3]{0:T(128)} %copy-done.50, bf16[960,256]{1,0:T(8,128)(2,1)} %copy-done.56, ...), custom_call_target="tpu_custom_call" | custom-call | flops 1024 | bytes 1024 | tf_op jit(solution)/shard_map/post/pallas_call | solution.py:328
  206.8 2.0 collective-permute-start.33
  208.9 20.7 %back_start.1 = (bf16[256,960]{1,0:T(8,128)(2,1)}, bf16[256,2560]{1,0:T(8,128)(2,1)}, bf16[256,2560]{1,0:T(8,128)(2,1)}, f32[256,960]{1,0:T(8,128)}, bf16[3,256,...) custom-call(s32[3]{0:T(128)} %copy-done.50, bf16[960,384]{1,0:T(8,128)(2,1)} %bitcast.30, ...), custom_call_target="tpu_custom_call" | custom-call | flops 1024 | bytes 1024 | tf_op jit(solution)/shard_map/back_start/pallas_call | solution.py:483
  230.7 3.1 collective-permute-done.30.rest_0_.rest_2_
  237.8 12.6 %attend_back.2 = (bf16[3,256,384]{2,1,0:T(8,128)(2,1)S(1)}, bf16[3,256,384]{2,1,0:T(8,128)(2,1)S(1)}, f32[640,256]{1,0:T(8,128)S(1)}, bf16[640,256]{1,0:T(8,128)(2,1)S(1)}, f32[640,256]{1,0:T(8,128)S(1)}) custom-call(s32[3]{0:T(128)S(1)} %copy-done.51, bf16[3,256,384]{2,1,0:T(8,128)(2,1)S(1)} %copy-done.14, bf16[960,256]{1,0:T(8,128)(2,1)S(1)} %copy-done.30, ...), custom_call_target="tpu_custom_call" | custom-call | flops 1024 | bytes 1024 | tf_op jit(solution)/shard_map/attend_back/pallas_call | solution.py:225
  255.0 11.2 %collective-permute-done.35.rest_20_ = bf16[640,256]{1,0:T(8,128)(2,1)S(1)} collective-permute-done((bf16[640,256]{1,0:T(8,128)(2,1)S(1)}, bf16[640,256]{1,0:T(8,128)(2,1)S(1)}, u32[]{:S(2)}, u32[]{:S(2)}) %collective-permute-start.35) | collective-permute-done | bytes 327712 | tf_op jit(solution)/shard_map/ppermute | solution.py:928
  266.9 21.0 %back_join.1 = (bf16[256,384]{1,0:T(8,128)(2,1)}, bf16[256,384]{1,0:T(8,128)(2,1)}, bf16[256,384]{1,0:T(8,128)(2,1)}, f32[1,960]{1,0:T(1,128)}, bf16[256,960]{1,...) custom-call(s32[3]{0:T(128)} %copy-done.50, ...), custom_call_target="tpu_custom_call" | custom-call | flops 1024 | bytes 1024 | tf_op jit(solution)/shard_map/back_join/pallas_call | solution.py:483
  288.4 2.9 collective-permute-done.41.rest_7_
  292.3 11.4 %grad_ffn.1 = (bf16[2,960,640]{2,1,0:T(8,128)(2,1)}, bf16[2,960,640]{2,1,0:T(8,128)(2,1)}) custom-call(s32[3]{0:T(128)} %copy-done.50, bf16[256,960]{1,0:T(8,128)(2,1)} %get-tuple-element.122.rest_0_, bf16[256,960]{1,0:T(8,128)(2,1)} %get-tuple-element.109.rest_1_, bf16[256,960]{1,0:T(8,128)(2,1)} %copy-done.26, bf16[256,960]{1,0:T(8,128)(2,1)} %copy-done.25, ...), custom_call_target="tpu_custom_call" | custom-call | flops 1024 | bytes 1024 | tf_op jit(solution)/shard_map/grad_ffn/pallas_call | solution.py:524
  303.7 2.1 collective-permute-start.45
  306.4 1.6 collective-permute-done.40.rest_3_
  308.1 8.2 %grad_down.1 = (bf16[2,480,640]{2,1,0:T(8,128)(2,1)}, bf16[2,480,640]{2,1,0:T(8,128)(2,1)}) custom-call(s32[3]{0:T(128)} %copy-done.50, bf16[256,960]{1,0:T(8,128)(2,1)} %get-tuple-element.133.rest_0_, bf16[256,960]{1,0:T(8,128)(2,1)} %get-tuple-element.140.rest_1_, bf16[256,960]{1,0:T(8,128)(2,1)} %copy-done.68, ...), custom_call_target="tpu_custom_call" | custom-call | flops 1024 | bytes 1024 | tf_op jit(solution)/shard_map/grad_down/pallas_call | solution.py:555
  317.6 13.4 %attend_back.3 = (bf16[3,256,384]{2,1,0:T(8,128)(2,1)S(1)}, bf16[3,256,384]{2,1,0:T(8,128)(2,1)}, f32[640,256]{1,0:T(8,128)S(1)}, bf16[640,256]{1,0:T(8,128)(2,1)S(1)}, f32[640,256]{1,0:T(8,128)S(1)}) custom-call(s32[3]{0:T(128)S(1)} %copy-done.52, bf16[3,256,384]{2,1,0:T(8,128)(2,1)S(1)} %copy-done.15, bf16[960,256]{1,0:T(8,128)(2,1)S(1)} %copy-done.28, ...), custom_call_target="tpu_custom_call" | custom-call | flops 1024 | bytes 1024 | tf_op jit(solution)/shard_map/attend_back/pallas_call | solution.py:225
  334.6 18.0 %collective-permute-done.43.rest_1_.rest_12_ = bf16[640,256]{1,0:T(8,128)(2,1)S(1)} collective-permute-done((bf16[640,256]{1,0:T(8,128)(2,1)S(1)}, bf16[640,256]{1,0:T(8,128)(2,1)S(1)}, u32[]{:S(2)}, u32[]{:S(2)}) %collective-permute-start.43) | collective-permute-done | bytes 327712 | tf_op jit(solution)/shard_map/ppermute | solution.py:928
  352.7 2.0 sum_first.3
  354.7 2.1 collective-permute-start.46
  358.6 6.8 %back_end.1 = (bf16[256,384]{1,0:T(8,128)(2,1)}, bf16[256,384]{1,0:T(8,128)(2,1)}, bf16[256,384]{1,0:T(8,128)(2,1)}, f32[1,960]{1,0:T(1,128)}, bf16[1920,256]{1,0:T(8,128)(2,1)}) custom-call(s32[3]{0:T(128)} %copy-done.50, bf16[960,384]{1,0:T(8,128)(2,1)} %bitcast.32, bf16[960,384]{1,0:T(8,128)(2,1)} %collective-permute-done.3.refs_1_.rest_1_, ...), custom_call_target="tpu_custom_call" | custom-call | flops 1024 | bytes 1024 | tf_op jit(solution)/shard_map/back_end/pallas_call | solution.py:483
  368.8 10.5 %grad_attention.1 = (bf16[960,384]{1,0:T(8,128)(2,1)}, bf16[960,384]{1,0:T(8,128)(2,1)}, bf16[2,960,384]{2,1,0:T(8,128)(2,1)}) custom-call(s32[3]{0:T(128)} %copy-done.50, bf16[256,960]{1,0:T(8,128)(2,1)} %get-tuple-element.121.rest_0_, bf16[256,960]{1,0:T(8,128)(2,1)} %get-tuple-element.108.rest_1_, bf16[256,960]{1,0:T(8,128)(2,1)} %copy-done.23, ...), custom_call_target="tpu_custom_call" | custom-call | flops 1024 | bytes 1024 | tf_op jit(solution)/shard_map/grad_attention/pallas_call | solution.py:606
  379.7 1.7 collective-permute-start.52
  381.4 2.4 collective-permute-start.50
  387.1 4.0 collective-permute-done.51.rest_0_
  391.1 7.9 %collective-permute-done.52.rest_1_ = bf16[960,384]{1,0:T(8,128)(2,1)S(1)} collective-permute-done((bf16[960,384]{1,0:T(8,128)(2,1)}, bf16[960,384]{1,0:T(8,128)(2,1)S(1)}, u32[]{:S(2)}, u32[]{:S(2)}) %collective-permute-start.52) | collective-permute-done | bytes 737312 | tf_op jit(solution)/shard_map/ppermute | solution.py:880
  401.9 8.8 %collective-permute-done.50.got_ref = bf16[480,640]{1,0:T(8,128)(2,1)S(1)} collective-permute-done((bf16[480,640]{1,0:T(8,128)(2,1)S(1)}, bf16[480,640]{1,0:T(8,128)(2,1)S(1)}, u32[]{:S(2)}, u32[]{:S(2)}) %collective-permute-start.50) | collective-permute-done | bytes 614432 | tf_op jit(solution)/shard_map/ppermute | solution.py:886
  411.5 4.5 collective-permute-done.49.got_ref
  418.6 15.2 %collective-permute-done.53.got_ref = bf16[240,640]{1,0:T(8,128)(2,1)S(1)} collective-permute-done((bf16[240,640]{1,0:T(8,128)(2,1)S(1)}, bf16[240,640]{1,0:T(8,128)(2,1)S(1)}, u32[]{:S(2)}, u32[]{:S(2)}) %collective-permute-start.53) | collective-permute-done | bytes 307232 | tf_op jit(solution)/shard_map/ppermute | solution.py:886
  436.6 1.9 collective-permute-start.69
  440.7 2.3 collective-permute-done.58.got_ref
  444.1 11.3 %collective-permute-done.74.got_ref = bf16[120,640]{1,0:T(8,128)(2,1)S(1)} collective-permute-done((bf16[120,640]{1,0:T(8,128)(2,1)S(1)}, bf16[120,640]{1,0:T(8,128)(2,1)S(1)}, u32[]{:S(2)}, u32[]{:S(2)}) %collective-permute-start.74) | collective-permute-done | bytes 153632 | tf_op jit(solution)/shard_map/ppermute | solution.py:880
  456.0 2.0 collective-permute-start.77
  459.5 1.9 collective-permute-start.75
  461.5 1.6 collective-permute-start.56
  464.4 5.0 %collective-permute-done.76.rest_2_ = bf16[120,640]{1,0:T(8,128)(2,1)S(1)} collective-permute-done((bf16[120,640]{1,0:T(8,128)(2,1)S(1)}, bf16[120,640]{1,0:T(8,128)(2,1)S(1)}, u32[]{:S(2)}, u32[]{:S(2)}) %collective-permute-start.76) | collective-permute-done | bytes 153632 | tf_op jit(solution)/shard_map/ppermute | solution.py:880
  470.1 2.0 collective-permute-start.60
  472.8 2.9 collective-permute-done.60.rest_1_
  476.3 1.7 collective-permute-done.64.rest_5_
  479.0 3.1 lay.2
  482.2 1.7 copy-done.10
  483.8 2.4 lay.3
  487.5 2.3 lay_down.1
  492.1 2.4 convert_bitcast_fusion
  (320 shorter events, 81.4 us)
Async XLA Ops:
  8.8 12.8 %collective-permute-start.1 = (bf16[240,384]{1,0:T(8,128)(2,1)S(1)}, bf16[240,384]{1,0:T(8,128)(2,1)S(1)}, u32[]{:S(2)}, u32[]{:S(2)}) collective-permute-start(bf16[240,384]{1,0:T(8,128)(2,1)S(1)} %pick_first.1.rest_0_), channel_id=1, source_target_pairs={{0,2},{1,3},{2,0},{3,1},{4,6},{5,7},{6,4},{7,5},{8,10},{9,11},{10,... | collective-permute-start | bytes 552968 | tf_op jit(solution)/shard_map/ppermute | solution.py:886
  12.9 9.4 %collective-permute-start = (bf16[240,384]{1,0:T(8,128)(2,1)S(1)}, bf16[240,384]{1,0:T(8,128)(2,1)S(1)}, u32[]{:S(2)}, u32[]{:S(2)}) collective-permute-start(bf16[240,384]{1,0:T(8,128)(2,1)S(1)} %pick_first.1.rest_0_), channel_id=1, source_target_pairs={{0,1},{1,0},{2,3},{3,2},{4,5},{5,4},{6,7},{7,6},{8,9},{9,8},{10,11... | collective-permute-start | bytes 552968 | tf_op jit(solution)/shard_map/ppermute | solution.py:886
  21.6 5.8 %collective-permute-start.2 = (bf16[240,384]{1,0:T(8,128)(2,1)S(1)}, bf16[240,384]{1,0:T(8,128)(2,1)S(1)}, u32[]{:S(2)}, u32[]{:S(2)}) collective-permute-start(bf16[240,384]{1,0:T(8,128)(2,1)S(1)} %collective-permute-done.1.rest_2_), channel_id=1, source_target_pairs={{0,1},{1,0},{2,3},{3,2},{4,5},{5,4},{6,7},{7,6},{8,9},{9,8},{10,11... | collective-permute-start | bytes 552968 | tf_op jit(solution)/shard_map/ppermute | solution.py:886
  29.0 19.6 %collective-permute-start.3 = (bf16[960,384]{1,0:T(8,128)(2,1)S(1)}, bf16[960,384]{1,0:T(8,128)(2,1)}, u32[]{:S(2)}, u32[]{:S(2)}) collective-permute-start(bf16[960,384]{1,0:T(8,128)(2,1)S(1)} %bitcast.24), channel_id=1, source_target_pairs={{0,8},{4,20},{8,0},{12,28},{16,24},{20,4},{24,16},{28,12},{1,9},{5... | collective-permute-start | bytes 2211848 | tf_op jit(solution)/shard_map/ppermute | solution.py:880
  30.3 25.2 %collective-permute-start.4 = (bf16[960,384]{1,0:T(8,128)(2,1)S(1)}, bf16[960,384]{1,0:T(8,128)(2,1)}, u32[]{:S(2)}, u32[]{:S(2)}) collective-permute-start(bf16[960,384]{1,0:T(8,128)(2,1)S(1)} %bitcast.25), channel_id=1, source_target_pairs={{0,16},{4,12},{8,24},{12,4},{16,0},{20,28},{24,8},{28,20},{1,17},{... | collective-permute-start | bytes 2211848 | tf_op jit(solution)/shard_map/ppermute | solution.py:880
  31.8 23.3 %collective-permute-start.11 = (bf16[368,640]{1,0:T(8,128)(2,1)S(1)}, bf16[368,640]{1,0:T(8,128)(2,1)S(1)}, u32[]{:S(2)}, u32[]{:S(2)}) collective-permute-start(bf16[368,640]{1,0:T(8,128)(2,1)S(1)} %pick.1.rest_4_.rest_0_), channel_id=1, source_target_pairs={{0,2},{1,3},{2,0},{3,1},{4,6},{5,7},{6,4},{7,5},{8,10},{9,11},{10,... | collective-permute-start | bytes 1413128 | tf_op jit(solution)/shard_map/ppermute | solution.py:886
  35.0 20.4 %collective-permute-start.10 = (bf16[368,640]{1,0:T(8,128)(2,1)S(1)}, bf16[368,640]{1,0:T(8,128)(2,1)S(1)}, u32[]{:S(2)}, u32[]{:S(2)}) collective-permute-start(bf16[368,640]{1,0:T(8,128)(2,1)S(1)} %pick.1.rest_4_.rest_0_), channel_id=1, source_target_pairs={{0,1},{1,0},{2,3},{3,2},{4,5},{5,4},{6,7},{7,6},{8,9},{9,8},{10,11... | collective-permute-start | bytes 1413128 | tf_op jit(solution)/shard_map/ppermute | solution.py:886
  48.6 18.3 %collective-permute-start.5 = (bf16[960,384]{1,0:T(8,128)(2,1)}, bf16[960,384]{1,0:T(8,128)(2,1)S(1)}, u32[]{:S(2)}, u32[]{:S(2)}) collective-permute-start(bf16[960,384]{1,0:T(8,128)(2,1)} %collective-permute-done.3.refs_1_.rest_1_), channel_id=1, source_target_pairs={{0,16},{4,12},{8,24},{12,4},{16,0},{20,28},{24,8},{28,20},{1,17},{... | collective-permute-start | bytes 2211848 | tf_op jit(solution)/shard_map/ppermute | solution.py:880
  55.5 11.4 %collective-permute-start.12 = (bf16[368,640]{1,0:T(8,128)(2,1)S(1)}, bf16[368,640]{1,0:T(8,128)(2,1)S(1)}, u32[]{:S(2)}, u32[]{:S(2)}) collective-permute-start(bf16[368,640]{1,0:T(8,128)(2,1)S(1)} %hold.5.rest_2_), channel_id=1, source_target_pairs={{0,1},{1,0},{2,3},{3,2},{4,5},{5,4},{6,7},{7,6},{8,9},{9,8},{10,11... | collective-permute-start | bytes 1413128 | tf_op jit(solution)/shard_map/ppermute | solution.py:886
  69.9 41.3 %collective-permute-start.16 = (bf16[4,368,640]{2,1,0:T(8,128)(2,1)}, bf16[4,368,640]{2,1,0:T(8,128)(2,1)S(1)}, u32[]{:S(2)}, u32[]{:S(2)}) collective-permute-start(bf16[4,368,640]{2,1,0:T(8,128)(2,1)} %stack.31.rest_8_), channel_id=1, source_target_pairs={{0,16},{4,12},{8,24},{12,4},{16,0},{20,28},{24,8},{28,20},{1,17},{... | collective-permute-start | bytes 5652488 | tf_op jit(solution)/shard_map/ppermute | solution.py:880
  70.5 40.7 %collective-permute-start.13 = (bf16[4,368,640]{2,1,0:T(8,128)(2,1)}, bf16[4,368,640]{2,1,0:T(8,128)(2,1)}, u32[]{:S(2)}, u32[]{:S(2)}) collective-permute-start(bf16[4,368,640]{2,1,0:T(8,128)(2,1)} %stack.31.rest_8_), channel_id=1, source_target_pairs={{0,8},{4,20},{8,0},{12,28},{16,24},{20,4},{24,16},{28,12},{1,9},{5... | collective-permute-start | bytes 5652488 | tf_op jit(solution)/shard_map/ppermute | solution.py:880
  71.1 11.2 %collective-permute-start.6 = (bf16[960,384]{1,0:T(8,128)(2,1)S(1)}, bf16[960,384]{1,0:T(8,128)(2,1)S(1)}, u32[]{:S(2)}, u32[]{:S(2)}) collective-permute-start(bf16[960,384]{1,0:T(8,128)(2,1)S(1)} %bitcast.26), channel_id=1, source_target_pairs={{0,4},{4,0},{8,12},{12,8},{16,20},{20,16},{24,28},{28,24},{1,5},{5... | collective-permute-start | bytes 2211848 | tf_op jit(solution)/shard_map/ppermute | solution.py:880
  71.1 5.3 %collective-permute-start.14 = (bf16[976,256]{1,0:T(8,128)(2,1)S(1)}, bf16[976,256]{1,0:T(8,128)(2,1)S(1)}, u32[]{:S(2)}, u32[]{:S(2)}) collective-permute-start(bf16[976,256]{1,0:T(8,128)(2,1)S(1)} %pad_maximum_fusion), channel_id=1, source_target_pairs={{0,0},{1,4},{2,1},{3,5},{4,2},{5,6},{6,3},{7,7},{8,8},{9,12},{10,9... | collective-permute-start | bytes 1499144 | tf_op jit(solution)/shard_map/ppermute | solution.py:897
  71.8 14.1 %collective-permute-start.8 = (bf16[960,384]{1,0:T(8,128)(2,1)}, bf16[960,384]{1,0:T(8,128)(2,1)}, u32[]{:S(2)}, u32[]{:S(2)}) collective-permute-start(bf16[960,384]{1,0:T(8,128)(2,1)} %collective-permute-done.4.refs_2_.rest_2_), channel_id=1, source_target_pairs={{0,4},{4,0},{8,12},{12,8},{16,20},{20,16},{24,28},{28,24},{1,5},{5... | collective-permute-start | bytes 2211848 | tf_op jit(solution)/shard_map/ppermute | solution.py:880
  76.4 9.5 %collective-permute-start.7 = (bf16[960,384]{1,0:T(8,128)(2,1)}, bf16[960,384]{1,0:T(8,128)(2,1)}, u32[]{:S(2)}, u32[]{:S(2)}) collective-permute-start(bf16[960,384]{1,0:T(8,128)(2,1)} %collective-permute-done.3.refs_1_.rest_1_), channel_id=1, source_target_pairs={{0,4},{4,0},{8,12},{12,8},{16,20},{20,16},{24,28},{28,24},{1,5},{5... | collective-permute-start | bytes 2211848 | tf_op jit(solution)/shard_map/ppermute | solution.py:880
  92.8 17.6 %collective-permute-start.15 = (bf16[656,256]{1,0:T(8,128)(2,1)}, bf16[656,256]{1,0:T(8,128)(2,1)S(1)}, u32[]{:S(2)}, u32[]{:S(2)}) collective-permute-start(bf16[656,256]{1,0:T(8,128)(2,1)} %get-tuple-element.102.kv2.rest_16_), channel_id=1, source_target_pairs={{0,1},{2,3},{4,5},{6,7},{8,9},{10,11},{12,13},{14,15},{16,17},{18,... | collective-permute-start | bytes 1007624 | tf_op jit(solution)/shard_map/ppermute | solution.py:919
  111.1 24.1 %collective-permute-start.17 = (bf16[4,368,640]{2,1,0:T(8,128)(2,1)}, bf16[4,368,640]{2,1,0:T(8,128)(2,1)}, u32[]{:S(2)}, u32[]{:S(2)}) collective-permute-start(bf16[4,368,640]{2,1,0:T(8,128)(2,1)} %hold.6.rest_9_), channel_id=1, source_target_pairs={{0,16},{4,12},{8,24},{12,4},{16,0},{20,28},{24,8},{28,20},{1,17},{... | collective-permute-start | bytes 5652488 | tf_op jit(solution)/shard_map/ppermute | solution.py:880
  111.9 23.4 %collective-permute-start.19 = (bf16[4,368,640]{2,1,0:T(8,128)(2,1)}, bf16[4,368,640]{2,1,0:T(8,128)(2,1)S(1)}, u32[]{:S(2)}, u32[]{:S(2)}) collective-permute-start(bf16[4,368,640]{2,1,0:T(8,128)(2,1)} %stack.31.rest_8_), channel_id=1, source_target_pairs={{0,4},{4,0},{8,12},{12,8},{16,20},{20,16},{24,28},{28,24},{1,5},{5... | collective-permute-start | bytes 5652488 | tf_op jit(solution)/shard_map/ppermute | solution.py:880
  123.7 12.9 %collective-permute-start.20 = (bf16[4,368,640]{2,1,0:T(8,128)(2,1)}, bf16[4,368,640]{2,1,0:T(8,128)(2,1)S(1)}, u32[]{:S(2)}, u32[]{:S(2)}) collective-permute-start(bf16[4,368,640]{2,1,0:T(8,128)(2,1)} %hold.6.rest_9_), channel_id=1, source_target_pairs={{0,4},{4,0},{8,12},{12,8},{16,20},{20,16},{24,28},{28,24},{1,5},{5... | collective-permute-start | bytes 5652488 | tf_op jit(solution)/shard_map/ppermute | solution.py:880
  123.9 11.5 %collective-permute-start.21 = (bf16[4,368,640]{2,1,0:T(8,128)(2,1)S(1)}, bf16[4,368,640]{2,1,0:T(8,128)(2,1)S(1)}, u32[]{:S(2)}, u32[]{:S(2)}) collective-permute-start(bf16[4,368,640]{2,1,0:T(8,128)(2,1)S(1)} %collective-permute-done.16.refs_2_.rest_10_), channel_id=1, source_target_pairs={{0,4},{4,0},{8,12},{12,8},{16,20},{20,16},{24,28},{28,24},{1,5},{5... | collective-permute-start | bytes 5652488 | tf_op jit(solution)/shard_map/ppermute | solution.py:880
  135.3 4.1 collective-permute-start.22
  161.6 9.5 %collective-permute-start.23 = (bf16[656,256]{1,0:T(8,128)(2,1)}, bf16[656,256]{1,0:T(8,128)(2,1)S(1)}, u32[]{:S(2)}, u32[]{:S(2)}) collective-permute-start(bf16[656,256]{1,0:T(8,128)(2,1)} %get-tuple-element.106.kv2.rest_16_), channel_id=1, source_target_pairs={{0,1},{2,3},{4,5},{6,7},{8,9},{10,11},{12,13},{14,15},{16,17},{18,... | collective-permute-start | bytes 1007624 | tf_op jit(solution)/shard_map/ppermute | solution.py:919
  165.6 10.7 %collective-permute-start.29 = (bf16[256,2560]{1,0:T(8,128)(2,1)}, bf16[256,2560]{1,0:T(8,128)(2,1)S(1)}, u32[]{:S(2)}, u32[]{:S(2)}) collective-permute-start(bf16[256,2560]{1,0:T(8,128)(2,1)} %get-tuple-element.111.rest_5_), channel_id=1, source_target_pairs={{0,4},{4,0},{8,12},{12,8},{16,20},{20,16},{24,28},{28,24},{1,5},{5... | collective-permute-start | bytes 3932168 | tf_op jit(solution)/shard_map/ppermute | solution.py:880
  173.9 13.8 %collective-permute-start.25 = (bf16[960,256]{1,0:T(8,128)(2,1)S(1)}, bf16[960,256]{1,0:T(8,128)(2,1)S(1)}, u32[]{:S(2)}, u32[]{:S(2)}) collective-permute-start(bf16[960,256]{1,0:T(8,128)(2,1)S(1)} %hold.8), channel_id=1, source_target_pairs={{0,0},{1,4},{2,1},{3,5},{4,2},{5,6},{6,3},{7,7},{8,8},{9,12},{10,9... | collective-permute-start | bytes 1474568 | tf_op jit(solution)/shard_map/ppermute | solution.py:897
  206.8 28.4 %collective-permute-start.33 = (bf16[256,2560]{1,0:T(8,128)(2,1)}, bf16[256,2560]{1,0:T(8,128)(2,1)S(1)}, u32[]{:S(2)}, u32[]{:S(2)}) collective-permute-start(bf16[256,2560]{1,0:T(8,128)(2,1)} %get-tuple-element.124.rest_4_), channel_id=1, source_target_pairs={{0,4},{4,0},{8,12},{12,8},{16,20},{20,16},{24,28},{28,24},{1,5},{5... | collective-permute-start | bytes 3932168 | tf_op jit(solution)/shard_map/ppermute | solution.py:880
  229.7 25.3 %collective-permute-start.38 = (bf16[256,2560]{1,0:T(8,128)(2,1)}, bf16[256,2560]{1,0:T(8,128)(2,1)S(1)}, u32[]{:S(2)}, u32[]{:S(2)}) collective-permute-start(bf16[256,2560]{1,0:T(8,128)(2,1)} %get-tuple-element.134), channel_id=1, source_target_pairs={{0,4},{4,0},{8,12},{12,8},{16,20},{20,16},{24,28},{28,24},{1,5},{5... | collective-permute-start | bytes 3932168 | tf_op jit(solution)/shard_map/ppermute | solution.py:880
  229.7 4.1 collective-permute-start.30
  230.2 4.2 collective-permute-start.31
  230.3 4.9 collective-permute-start.32
  253.6 12.6 %collective-permute-start.35 = (bf16[640,256]{1,0:T(8,128)(2,1)S(1)}, bf16[640,256]{1,0:T(8,128)(2,1)S(1)}, u32[]{:S(2)}, u32[]{:S(2)}) collective-permute-start(bf16[640,256]{1,0:T(8,128)(2,1)S(1)} %far_sum.2), channel_id=1, source_target_pairs={{1,0},{3,2},{5,4},{7,6},{9,8},{11,10},{13,12},{15,14},{17,16},{19,... | collective-permute-start | bytes 983048 | tf_op jit(solution)/shard_map/ppermute | solution.py:928
  303.7 49.0 %collective-permute-start.45 = (bf16[2,960,640]{2,1,0:T(8,128)(2,1)}, bf16[2,960,640]{2,1,0:T(8,128)(2,1)S(1)}, u32[]{:S(2)}, u32[]{:S(2)}) collective-permute-start(bf16[2,960,640]{2,1,0:T(8,128)(2,1)} %get-tuple-element.144.rest_8_), channel_id=1, source_target_pairs={{0,8},{4,20},{8,0},{12,28},{16,24},{20,4},{24,16},{28,12},{1,9},{5... | collective-permute-start | bytes 7372808 | tf_op jit(solution)/shard_map/ppermute | solution.py:880
  306.1 10.1 %collective-permute-start.39 = (bf16[256,384]{1,0:T(8,128)(2,1)S(1)}, bf16[256,384]{1,0:T(8,128)(2,1)S(1)}, u32[]{:S(2)}, u32[]{:S(2)}) collective-permute-start(bf16[256,384]{1,0:T(8,128)(2,1)S(1)} %copy-done.79), channel_id=1, source_target_pairs={{0,4},{4,0},{8,12},{12,8},{16,20},{20,16},{24,28},{28,24},{1,5},{5... | collective-permute-start | bytes 589832 | tf_op jit(solution)/shard_map/ppermute | solution.py:880
  316.2 40.7 %collective-permute-start.44 = (bf16[2,480,640]{2,1,0:T(8,128)(2,1)}, bf16[2,480,640]{2,1,0:T(8,128)(2,1)S(1)}, u32[]{:S(2)}, u32[]{:S(2)}) collective-permute-start(bf16[2,480,640]{2,1,0:T(8,128)(2,1)} %get-tuple-element.145.rest_1_), channel_id=1, source_target_pairs={{0,1},{1,0},{2,3},{3,2},{4,5},{5,4},{6,7},{7,6},{8,9},{9,8},{10,11... | collective-permute-start | bytes 3686408 | tf_op jit(solution)/shard_map/ppermute | solution.py:886
  333.3 19.3 %collective-permute-start.43 = (bf16[640,256]{1,0:T(8,128)(2,1)S(1)}, bf16[640,256]{1,0:T(8,128)(2,1)S(1)}, u32[]{:S(2)}, u32[]{:S(2)}) collective-permute-start(bf16[640,256]{1,0:T(8,128)(2,1)S(1)} %far_sum.3), channel_id=1, source_target_pairs={{1,0},{3,2},{5,4},{7,6},{9,8},{11,10},{13,12},{15,14},{17,16},{19,... | collective-permute-start | bytes 983048 | tf_op jit(solution)/shard_map/ppermute | solution.py:928
  354.7 29.1 %collective-permute-start.46 = (bf16[960,640]{1,0:T(8,128)(2,1)}, bf16[960,640]{1,0:T(8,128)(2,1)S(1)}, u32[]{:S(2)}, u32[]{:S(2)}) collective-permute-start(bf16[960,640]{1,0:T(8,128)(2,1)} %get-tuple-element.153.rest_0_), channel_id=1, source_target_pairs={{0,16},{4,12},{8,24},{12,4},{16,0},{20,28},{24,8},{28,20},{1,17},{... | collective-permute-start | bytes 3686408 | tf_op jit(solution)/shard_map/ppermute | solution.py:880
  356.9 10.0 %collective-permute-start.47 = (bf16[3,256,384]{2,1,0:T(8,128)(2,1)}, bf16[3,256,384]{2,1,0:T(8,128)(2,1)S(1)}, u32[]{:S(2)}, u32[]{:S(2)}) collective-permute-start(bf16[3,256,384]{2,1,0:T(8,128)(2,1)} %get-tuple-element.161), channel_id=1, source_target_pairs={{0,4},{4,0},{8,12},{12,8},{16,20},{20,16},{24,28},{28,24},{1,5},{5... | collective-permute-start | bytes 1769480 | tf_op jit(solution)/shard_map/ppermute | solution.py:880
  379.3 11.7 %collective-permute-start.51 = (bf16[960,384]{1,0:T(8,128)(2,1)}, bf16[960,384]{1,0:T(8,128)(2,1)S(1)}, u32[]{:S(2)}, u32[]{:S(2)}) collective-permute-start(bf16[960,384]{1,0:T(8,128)(2,1)} %get-tuple-element.167.rest_1_), channel_id=1, source_target_pairs={{0,8},{4,20},{8,0},{12,28},{16,24},{20,4},{24,16},{28,12},{1,9},{5... | collective-permute-start | bytes 2211848 | tf_op jit(solution)/shard_map/ppermute | solution.py:880
  379.7 19.3 %collective-permute-start.52 = (bf16[960,384]{1,0:T(8,128)(2,1)}, bf16[960,384]{1,0:T(8,128)(2,1)S(1)}, u32[]{:S(2)}, u32[]{:S(2)}) collective-permute-start(bf16[960,384]{1,0:T(8,128)(2,1)} %get-tuple-element.168.rest_2_), channel_id=1, source_target_pairs={{0,8},{4,20},{8,0},{12,28},{16,24},{20,4},{24,16},{28,12},{1,9},{5... | collective-permute-start | bytes 2211848 | tf_op jit(solution)/shard_map/ppermute | solution.py:880
  381.4 29.3 %collective-permute-start.50 = (bf16[480,640]{1,0:T(8,128)(2,1)S(1)}, bf16[480,640]{1,0:T(8,128)(2,1)S(1)}, u32[]{:S(2)}, u32[]{:S(2)}) collective-permute-start(bf16[480,640]{1,0:T(8,128)(2,1)S(1)} %copy-done.12), channel_id=1, source_target_pairs={{0,2},{1,3},{2,0},{3,1},{4,6},{5,7},{6,4},{7,5},{8,10},{9,11},{10,... | collective-permute-start | bytes 1843208 | tf_op jit(solution)/shard_map/ppermute | solution.py:886
  387.0 29.0 %collective-permute-start.49 = (bf16[2,240,640]{2,1,0:T(8,128)(2,1)S(1)}, bf16[2,240,640]{2,1,0:T(8,128)(2,1)S(1)}, u32[]{:S(2)}, u32[]{:S(2)}) collective-permute-start(bf16[2,240,640]{2,1,0:T(8,128)(2,1)S(1)} %get-tuple-element.170), channel_id=1, source_target_pairs={{0,1},{1,0},{2,3},{3,2},{4,5},{5,4},{6,7},{7,6},{8,9},{9,8},{10,11... | collective-permute-start | bytes 1843208 | tf_op jit(solution)/shard_map/ppermute | solution.py:886
  399.8 16.9 %collective-permute-start.54 = (bf16[480,384]{1,0:T(8,128)(2,1)S(1)}, bf16[480,384]{1,0:T(8,128)(2,1)S(1)}, u32[]{:S(2)}, u32[]{:S(2)}) collective-permute-start(bf16[480,384]{1,0:T(8,128)(2,1)S(1)} %get-tuple-element.177), channel_id=1, source_target_pairs={{0,16},{4,12},{8,24},{12,4},{16,0},{20,28},{24,8},{28,20},{1,17},{... | collective-permute-start | bytes 1105928 | tf_op jit(solution)/shard_map/ppermute | solution.py:880
  400.4 16.3 %collective-permute-start.55 = (bf16[480,384]{1,0:T(8,128)(2,1)S(1)}, bf16[480,384]{1,0:T(8,128)(2,1)S(1)}, u32[]{:S(2)}, u32[]{:S(2)}) collective-permute-start(bf16[480,384]{1,0:T(8,128)(2,1)S(1)} %get-tuple-element.178), channel_id=1, source_target_pairs={{0,16},{4,12},{8,24},{12,4},{16,0},{20,28},{24,8},{28,20},{1,17},{... | collective-permute-start | bytes 1105928 | tf_op jit(solution)/shard_map/ppermute | solution.py:880
  417.5 16.9 %collective-permute-start.57 = (bf16[2,240,384]{2,1,0:T(8,128)(2,1)S(1)}, bf16[2,240,384]{2,1,0:T(8,128)(2,1)S(1)}, u32[]{:S(2)}, u32[]{:S(2)}) collective-permute-start(bf16[2,240,384]{2,1,0:T(8,128)(2,1)S(1)} %get-tuple-element.179.rest_0_), channel_id=1, source_target_pairs={{0,1},{1,0},{2,3},{3,2},{4,5},{5,4},{6,7},{7,6},{8,9},{9,8},{10,11... | collective-permute-start | bytes 1105928 | tf_op jit(solution)/shard_map/ppermute | solution.py:886
  417.6 16.2 %collective-permute-start.53 = (bf16[240,640]{1,0:T(8,128)(2,1)S(1)}, bf16[240,640]{1,0:T(8,128)(2,1)S(1)}, u32[]{:S(2)}, u32[]{:S(2)}) collective-permute-start(bf16[240,640]{1,0:T(8,128)(2,1)S(1)} %get-tuple-element.176.rest_2_), channel_id=1, source_target_pairs={{0,2},{1,3},{2,0},{3,1},{4,6},{5,7},{6,4},{7,5},{8,10},{9,11},{10,... | collective-permute-start | bytes 921608 | tf_op jit(solution)/shard_map/ppermute | solution.py:886
  417.7 21.6 %collective-permute-start.59 = (bf16[2,120,640]{2,1,0:T(8,128)(2,1)S(1)}, bf16[2,120,640]{2,1,0:T(8,128)(2,1)S(1)}, u32[]{:S(2)}, u32[]{:S(2)}) collective-permute-start(bf16[2,120,640]{2,1,0:T(8,128)(2,1)S(1)} %get-tuple-element.174.rest_0_), channel_id=1, source_target_pairs={{0,8},{4,20},{8,0},{12,28},{16,24},{20,4},{24,16},{28,12},{1,9},{5... | collective-permute-start | bytes 921608 | tf_op jit(solution)/shard_map/ppermute | solution.py:880
  435.1 7.9 %collective-permute-start.58 = (bf16[240,384]{1,0:T(8,128)(2,1)S(1)}, bf16[240,384]{1,0:T(8,128)(2,1)S(1)}, u32[]{:S(2)}, u32[]{:S(2)}) collective-permute-start(bf16[240,384]{1,0:T(8,128)(2,1)S(1)} %get-tuple-element.182.rest_1_), channel_id=1, source_target_pairs={{0,2},{1,3},{2,0},{3,1},{4,6},{5,7},{6,4},{7,5},{8,10},{9,11},{10,... | collective-permute-start | bytes 552968 | tf_op jit(solution)/shard_map/ppermute | solution.py:886
  436.6 21.4 %collective-permute-start.70 = (bf16[240,640]{1,0:T(8,128)(2,1)S(1)}, bf16[240,640]{1,0:T(8,128)(2,1)S(1)}, u32[]{:S(2)}, u32[]{:S(2)}) collective-permute-start(bf16[240,640]{1,0:T(8,128)(2,1)S(1)} %sum_two.3.refs_1_.rest_0_), channel_id=1, source_target_pairs={{0,4},{4,0},{8,12},{12,8},{16,20},{20,16},{24,28},{28,24},{1,5},{5... | collective-permute-start | bytes 921608 | tf_op jit(solution)/shard_map/ppermute | solution.py:880
  436.6 22.4 %collective-permute-start.69 = (bf16[240,640]{1,0:T(8,128)(2,1)S(1)}, bf16[240,640]{1,0:T(8,128)(2,1)S(1)}, u32[]{:S(2)}, u32[]{:S(2)}) collective-permute-start(bf16[240,640]{1,0:T(8,128)(2,1)S(1)} %sum_two.3.refs_1_.rest_0_), channel_id=1, source_target_pairs={{0,24},{4,28},{8,16},{12,20},{16,8},{20,12},{24,0},{28,4},{1,25},{... | collective-permute-start | bytes 921608 | tf_op jit(solution)/shard_map/ppermute | solution.py:880
  438.5 21.0 %collective-permute-start.68 = (bf16[240,640]{1,0:T(8,128)(2,1)S(1)}, bf16[240,640]{1,0:T(8,128)(2,1)S(1)}, u32[]{:S(2)}, u32[]{:S(2)}) collective-permute-start(bf16[240,640]{1,0:T(8,128)(2,1)S(1)} %sum_two.3.refs_1_.rest_0_), channel_id=1, source_target_pairs={{0,16},{4,12},{8,24},{12,4},{16,0},{20,28},{24,8},{28,20},{1,17},{... | collective-permute-start | bytes 921608 | tf_op jit(solution)/shard_map/ppermute | solution.py:880
  439.3 22.2 %collective-permute-start.67 = (bf16[240,640]{1,0:T(8,128)(2,1)S(1)}, bf16[240,640]{1,0:T(8,128)(2,1)S(1)}, u32[]{:S(2)}, u32[]{:S(2)}) collective-permute-start(bf16[240,640]{1,0:T(8,128)(2,1)S(1)} %sum_two.3.refs_1_.rest_0_), channel_id=1, source_target_pairs={{0,8},{4,20},{8,0},{12,28},{16,24},{20,4},{24,16},{28,12},{1,9},{5... | collective-permute-start | bytes 921608 | tf_op jit(solution)/shard_map/ppermute | solution.py:880
  442.9 12.4 %collective-permute-start.74 = (bf16[120,640]{1,0:T(8,128)(2,1)S(1)}, bf16[120,640]{1,0:T(8,128)(2,1)S(1)}, u32[]{:S(2)}, u32[]{:S(2)}) collective-permute-start(bf16[120,640]{1,0:T(8,128)(2,1)S(1)} %get-tuple-element.184.rest_0_), channel_id=1, source_target_pairs={{0,16},{4,12},{8,24},{12,4},{16,0},{20,28},{24,8},{28,20},{1,17},{... | collective-permute-start | bytes 460808 | tf_op jit(solution)/shard_map/ppermute | solution.py:880
  456.0 7.8 %collective-permute-start.77 = (bf16[120,640]{1,0:T(8,128)(2,1)S(1)}, bf16[120,640]{1,0:T(8,128)(2,1)S(1)}, u32[]{:S(2)}, u32[]{:S(2)}) collective-permute-start(bf16[120,640]{1,0:T(8,128)(2,1)S(1)} %sum_two.5.rest_8_.rest_0_), channel_id=1, source_target_pairs={{0,24},{4,28},{8,16},{12,20},{16,8},{20,12},{24,0},{28,4},{1,25},{... | collective-permute-start | bytes 460808 | tf_op jit(solution)/shard_map/ppermute | solution.py:880
  458.0 14.2 %collective-permute-start.62 = (bf16[240,384]{1,0:T(8,128)(2,1)S(1)}, bf16[240,384]{1,0:T(8,128)(2,1)S(1)}, u32[]{:S(2)}, u32[]{:S(2)}) collective-permute-start(bf16[240,384]{1,0:T(8,128)(2,1)S(1)} %sum_two.4.rest_0_), channel_id=1, source_target_pairs={{0,24},{4,28},{8,16},{12,20},{16,8},{20,12},{24,0},{28,4},{1,25},{... | collective-permute-start | bytes 552968 | tf_op jit(solution)/shard_map/ppermute | solution.py:880
  459.0 10.4 %collective-permute-start.76 = (bf16[120,640]{1,0:T(8,128)(2,1)S(1)}, bf16[120,640]{1,0:T(8,128)(2,1)S(1)}, u32[]{:S(2)}, u32[]{:S(2)}) collective-permute-start(bf16[120,640]{1,0:T(8,128)(2,1)S(1)} %sum_two.5.rest_8_.rest_0_), channel_id=1, source_target_pairs={{0,16},{4,12},{8,24},{12,4},{16,0},{20,28},{24,8},{28,20},{1,17},{... | collective-permute-start | bytes 460808 | tf_op jit(solution)/shard_map/ppermute | solution.py:880
  459.5 10.6 %collective-permute-start.75 = (bf16[120,640]{1,0:T(8,128)(2,1)S(1)}, bf16[120,640]{1,0:T(8,128)(2,1)S(1)}, u32[]{:S(2)}, u32[]{:S(2)}) collective-permute-start(bf16[120,640]{1,0:T(8,128)(2,1)S(1)} %sum_two.5.rest_8_.rest_0_), channel_id=1, source_target_pairs={{0,8},{4,20},{8,0},{12,28},{16,24},{20,4},{24,16},{28,12},{1,9},{5... | collective-permute-start | bytes 460808 | tf_op jit(solution)/shard_map/ppermute | solution.py:880
  461.5 30.6 %collective-permute-start.56 = (bf16[1920,256]{1,0:T(8,128)(2,1)S(1)}, bf16[1920,256]{1,0:T(8,128)(2,1)}, u32[]{:S(2)}, u32[]{:S(2)}) collective-permute-start(bf16[1920,256]{1,0:T(8,128)(2,1)S(1)} %hold.9), channel_id=1, source_target_pairs={{0,0},{4,1},{1,2},{5,3},{2,4},{6,5},{3,6},{7,7},{8,8},{12,9},{9,10... | collective-permute-start | bytes 2949128 | tf_op jit(solution)/shard_map/ppermute | solution.py:897
  463.7 8.4 %collective-permute-start.61 = (bf16[240,384]{1,0:T(8,128)(2,1)S(1)}, bf16[240,384]{1,0:T(8,128)(2,1)S(1)}, u32[]{:S(2)}, u32[]{:S(2)}) collective-permute-start(bf16[240,384]{1,0:T(8,128)(2,1)S(1)} %sum_two.4.rest_0_), channel_id=1, source_target_pairs={{0,16},{4,12},{8,24},{12,4},{16,0},{20,28},{24,8},{28,20},{1,17},{... | collective-permute-start | bytes 552968 | tf_op jit(solution)/shard_map/ppermute | solution.py:880
  470.1 5.5 %collective-permute-start.60 = (bf16[240,384]{1,0:T(8,128)(2,1)S(1)}, bf16[240,384]{1,0:T(8,128)(2,1)S(1)}, u32[]{:S(2)}, u32[]{:S(2)}) collective-permute-start(bf16[240,384]{1,0:T(8,128)(2,1)S(1)} %sum_two.4.rest_0_), channel_id=1, source_target_pairs={{0,8},{4,20},{8,0},{12,28},{16,24},{20,4},{24,16},{28,12},{1,9},{5... | collective-permute-start | bytes 552968 | tf_op jit(solution)/shard_map/ppermute | solution.py:880
  472.2 4.0 collective-permute-start.65
  472.7 5.4 %collective-permute-start.73 = (bf16[240,640]{1,0:T(8,128)(2,1)S(1)}, bf16[240,640]{1,0:T(8,128)(2,1)S(1)}, u32[]{:S(2)}, u32[]{:S(2)}) collective-permute-start(bf16[240,640]{1,0:T(8,128)(2,1)S(1)} %collective-permute-done.69.rest_3_), channel_id=1, source_target_pairs={{0,4},{4,0},{8,12},{12,8},{16,20},{20,16},{24,28},{28,24},{1,5},{5... | collective-permute-start | bytes 921608 | tf_op jit(solution)/shard_map/ppermute | solution.py:880
  478.0 8.3 %collective-permute-start.78 = (bf16[120,640]{1,0:T(8,128)(2,1)S(1)}, bf16[120,640]{1,0:T(8,128)(2,1)S(1)}, u32[]{:S(2)}, u32[]{:S(2)}) collective-permute-start(bf16[120,640]{1,0:T(8,128)(2,1)S(1)} %sum_two.5.rest_8_.rest_0_), channel_id=1, source_target_pairs={{0,4},{4,0},{8,12},{12,8},{16,20},{20,16},{24,28},{28,24},{1,5},{5... | collective-permute-start | bytes 460808 | tf_op jit(solution)/shard_map/ppermute | solution.py:880
  478.1 8.1 %collective-permute-start.81 = (bf16[120,640]{1,0:T(8,128)(2,1)S(1)}, bf16[120,640]{1,0:T(8,128)(2,1)S(1)}, u32[]{:S(2)}, u32[]{:S(2)}) collective-permute-start(bf16[120,640]{1,0:T(8,128)(2,1)S(1)} %collective-permute-done.77.rest_3_), channel_id=1, source_target_pairs={{0,4},{4,0},{8,12},{12,8},{16,20},{20,16},{24,28},{28,24},{1,5},{5... | collective-permute-start | bytes 460808 | tf_op jit(solution)/shard_map/ppermute | solution.py:880
  478.5 7.7 %collective-permute-start.80 = (bf16[120,640]{1,0:T(8,128)(2,1)S(1)}, bf16[120,640]{1,0:T(8,128)(2,1)S(1)}, u32[]{:S(2)}, u32[]{:S(2)}) collective-permute-start(bf16[120,640]{1,0:T(8,128)(2,1)S(1)} %collective-permute-done.76.rest_2_), channel_id=1, source_target_pairs={{0,4},{4,0},{8,12},{12,8},{16,20},{20,16},{24,28},{28,24},{1,5},{5... | collective-permute-start | bytes 460808 | tf_op jit(solution)/shard_map/ppermute | solution.py:880
  478.6 7.6 %collective-permute-start.79 = (bf16[120,640]{1,0:T(8,128)(2,1)S(1)}, bf16[120,640]{1,0:T(8,128)(2,1)S(1)}, u32[]{:S(2)}, u32[]{:S(2)}) collective-permute-start(bf16[120,640]{1,0:T(8,128)(2,1)S(1)} %collective-permute-done.75.rest_1_), channel_id=1, source_target_pairs={{0,4},{4,0},{8,12},{12,8},{16,20},{20,16},{24,28},{28,24},{1,5},{5... | collective-permute-start | bytes 460808 | tf_op jit(solution)/shard_map/ppermute | solution.py:880
  (99 other events, 1011.2 us)

commit v12 on v11

--- a/solution.py
+++ b/solution.py
@@ -977,10 +977,10 @@
     wb = whole_b, first_b, second_b, hold(opposite_b, [o0])
     wb = wb, across(wb)
     weights = wa, wb
+    cot = home_to_work(cotangent[0].T)
     mixed0, h1_0, b0, gate0, up0, z0, h_1, a1, q1, own = post(False, [], sc, o0, h_0, gain_f, gain_a, cos, sin, own, *weights)
     kv1 = window(own)
     across_0 = across((a0, b0, mixed0, z0))
-    cot = home_to_work(hold(cotangent[0].T, [kv1[1]]))
     o1, lse1 = attend(q1, kv1, across_0)
     mixed1, h1_1, b1, gate1, up1, z1, output = post(True, [cot], sc, o1, h_1, gain_f, gain_a, cos, sin, own, *weights)
     across_1 = across((a1, b1, mixed1, z1))
@@ -996,22 +996,22 @@
     away0, gb0_, one1 = across((away0, gb0, one1))
     send_b, keep_b = grad_ffn(sc, [b1, b0, across_1[1], across_0[1]], [act1, act0, across_2[1], away0], [])
     got_b = flip(send_b, SIDE, BACK)
-    send_d, keep_d = grad_down(sc, [gb1, gb0, across_2[0], gb0_], [z1, z0, across_1[3], across_0[3]], [send_b])
+    dq0, three0, far, near, own = attend_back(sc, p0, q0, kv0, lse0, do, cos, sin, [one1, send_b])
+    near, down_far, far = unwindow(sc, far, near)
+    send_d, keep_d = grad_down(sc, [gb1, gb0, across_2[0], gb0_], [z1, z0, across_1[3], across_0[3]], [down_far])
     got_d = flip_z(send_d, 1)
-    dq0, three0, far, near, own = attend_back(sc, p0, q0, kv0, lse0, do, cos, sin, [one1, send_d])
-    near, down_far, far = unwindow(sc, far, near)
     (three0,) = across((three0,))
-    later_b, own_b = sum_first(sc, keep_b, [got_b], [far])
-    more_b = flip(later_b, BACK, SIDE)
-    send_d, keep_d = sum_third(sc, keep_d, got_d, [later_b])
-    got_d = flip_z(send_d, 2)
     tail = [g1, dq0, own, near, far, h_0, gain_a, cos, sin, output]
     dk0, dv0, one0, dgain_a0, leaving = back(False, True, sc, weights, tail, None, [send_d])
+    later_b, own_b = sum_first(sc, keep_b, [got_b], [one0])
+    more_b = flip(later_b, BACK, SIDE)
     own = [dq1, dq0, dk1, dk0, dv1, dv0, p1, p0]
     got = [three1, three0, one1, flip(one0, CORE)]
-    *send_a, keep_a = grad_attention(sc, [a1, a0, across_1[0], across_0[0]], [mixed1, mixed0, across_1[2], across_0[2]], own, got, [dgain_a1, dgain_a0, dgain_f1, dgain_f0], [send_d])
+    *send_a, keep_a = grad_attention(sc, [a1, a0, across_1[0], across_0[0]], [mixed1, mixed0, across_1[2], across_0[2]], own, got, [dgain_a1, dgain_a0, dgain_f1, dgain_f0], [later_b])
     got_a = [flip(v, SIDE, BACK) for v in send_a]
-    send_b, ring_b = sum_second(sc, own_b, [more_b], send_a)
+    send_d, keep_d = sum_third(sc, keep_d, got_d, send_a)
+    got_d = flip_z(send_d, 2)
+    send_b, ring_b = sum_second(sc, own_b, [more_b], [send_d])
     got_b = flip_z(send_b, 1)
     *later_a, own_a = sum_first(sc, keep_a, got_a, [ring_b], 2)
     more_a = [flip(v, BACK, SIDE) for v in later_a]

time: 500 us -> 485 us (0.970)
  waiting for transfers between devices: 176 us -> 153 us
  starting transfers between devices: 83.9 us -> 89.5 us
    ppermute x2, waiting for transfers between devices: 29.2 us -> 10.3 us  [unwindow(): lax.ppermute(far, 'fsdp', [(z + 1, z) for z in range(0, depth, 2)])]
    ppermute x12, starting transfers between devices: 16.7 us -> 23.1 us  [flip_z(): return lax.ppermute(value, ('dp', 'fsdp'), pairs)]
    unnamed x165 -> x178, local copies, waits for them, and re-layouts: 28.5 us -> 31.6 us
  transfers between devices with their start and end apart: 82 -> 82, of which waited for: 38 -> 36; matrix products, arithmetic and copies ran while one was open for 1% -> 1% of each run, Pallas kernels for 24% -> 25%
where the time goes in v12:
time: 485 us; the launch traced here: 480 us
  Pallas kernels  198 us (41%)
  waiting for transfers between devices  153 us (32%)
  starting transfers between devices  89.5 us (18%)
  local copies, waits for them, and re-layouts  34.3 us (7%)
    ppermute x63, waiting for transfers between devices, flip(): lax.ppermute(value, 'dp', [(i, i ^ bits[i & 1]) for i in range(count)])  72.6 us
    ppermute x12, waiting for transfers between devices, flip_z(): return lax.ppermute(value, ('dp', 'fsdp'), pairs)  60.4 us
    pallas_call x3, Pallas kernels, back(): pl.pallas_call(functools.partial(back_kernel, start, end, len(after)), ou...  48.9 us
    ppermute x63, starting transfers between devices, flip(): lax.ppermute(value, 'dp', [(i, i ^ bits[i & 1]) for i in range(count)])  48.5 us
    pallas_call x2, Pallas kernels, post(): pl.pallas_call(functools.partial(post_kernel, last, len(after)), out_shap...  39.3 us
    unnamed x178, local copies, waits for them, and re-layouts  31.6 us
    pallas_call x2, Pallas kernels, attend_back(): pl.pallas_call(attend_back_kernel, out_shape=(shape((3, n, PIECE), bf16),...  25.3 us
    ppermute x12, starting transfers between devices, flip_z(): return lax.ppermute(value, ('dp', 'fsdp'), pairs)  23.1 us
  transfers between devices with their start and end apart: 82, of which 36 were waited for; matrix products, arithmetic and copies ran while one was open for 1% of the time, Pallas kernels for 25%

profile of v12, /device:TPU:0, one launch (start us, length us, event | category | flops | bytes accessed | tf_op | source)
XLA Modules:
  0.0 480.1 jit_solution(4146002273110556862)
XLA Ops:
  6.8 4.1 collective-permute-start.1
  10.9 1.6 collective-permute-start
  12.5 7.2 %collective-permute-done.1.rest_2_ = bf16[240,384]{1,0:T(8,128)(2,1)S(1)} collective-permute-done((bf16[240,384]{1,0:T(8,128)(2,1)S(1)}, bf16[240,384]{1,0:T(8,128)(2,1)S(1)}, u32[]{:S(2)}, u32[]{:S(2)}) %collective-permute-start.1) | collective-permute-done | bytes 184352 | tf_op jit(solution)/shard_map/ppermute | solution.py:886
  23.7 1.8 collective-permute-done.2.rest_3_
  25.5 1.5 stack.30.first_ref
  28.3 1.5 collective-permute-start.4
  29.9 3.2 collective-permute-start.11
  33.1 1.7 collective-permute-start.10
  34.8 11.8 %collective-permute-done.3.refs_1_.rest_1_ = bf16[960,384]{1,0:T(8,128)(2,1)} collective-permute-done((bf16[960,384]{1,0:T(8,128)(2,1)S(1)}, bf16[960,384]{1,0:T(8,128)(2,1)}, u32[]{:S(2)}, u32[]{:S(2)}) %collective-permute-start.3) | collective-permute-done | bytes 737312 | tf_op jit(solution)/shard_map/ppermute | solution.py:880
  46.8 6.4 %collective-permute-done.11.refs_0_ = bf16[368,640]{1,0:T(8,128)(2,1)S(1)} collective-permute-done((bf16[368,640]{1,0:T(8,128)(2,1)S(1)}, bf16[368,640]{1,0:T(8,128)(2,1)S(1)}, u32[]{:S(2)}, u32[]{:S(2)}) %collective-permute-start.11) | collective-permute-done | bytes 471072 | tf_op jit(solution)/shard_map/ppermute | solution.py:886
  54.9 10.0 %collective-permute-done.12.rest_3_ = bf16[368,640]{1,0:T(8,128)(2,1)S(1)} collective-permute-done((bf16[368,640]{1,0:T(8,128)(2,1)S(1)}, bf16[368,640]{1,0:T(8,128)(2,1)S(1)}, u32[]{:S(2)}, u32[]{:S(2)}) %collective-permute-start.12) | collective-permute-done | bytes 471072 | tf_op jit(solution)/shard_map/ppermute | solution.py:886
  65.0 3.0 stack.31.rest_8_
  69.9 4.6 collective-permute-start.8
  74.5 5.9 %collective-permute-start.7 = (bf16[960,384]{1,0:T(8,128)(2,1)}, bf16[960,384]{1,0:T(8,128)(2,1)}, u32[]{:S(2)}, u32[]{:S(2)}) collective-permute-start(bf16[960,384]{1,0:T(8,128)(2,1)} %collective-permute-done.3.refs_1_.rest_1_), channel_id=1, source_target_pairs={{0,4},{4,0},{8,12},{12,8},{16,20},{20,16},{24,28},{28,24},{1,5},{5... | collective-permute-start | bytes 2211848 | tf_op jit(solution)/shard_map/ppermute | solution.py:880
  84.0 6.8 %pre.1 = (bf16[256,960]{1,0:T(8,128)(2,1)}, bf16[256,960]{1,0:T(8,128)(2,1)}, bf16[960,256]{1,0:T(8,128)(2,1)}, bf16[656,256]{1,0:T(8,128)(2,1)}) custom-call(s32[3]{0:T(128)} %copy-done.49, bf16[976,256]{1,0:T(8,128)(2,1)} %copy-done.80, f32[1,960]{1,0:T(1,128)} %get-tuple-element.207.gain_ref.gain_a.rest_22_.rest_14_, ...), custom_call_target="tpu_custom_call" | custom-call | flops 1024 | bytes 1024 | tf_op jit(solution)/shard_map/pre/pallas_call | solution.py:119
  90.8 9.3 %collective-permute-start.15 = (bf16[656,256]{1,0:T(8,128)(2,1)}, bf16[656,256]{1,0:T(8,128)(2,1)S(1)}, u32[]{:S(2)}, u32[]{:S(2)}) collective-permute-start(bf16[656,256]{1,0:T(8,128)(2,1)} %get-tuple-element.102.kv2.rest_16_), channel_id=1, source_target_pairs={{0,1},{2,3},{4,5},{6,7},{8,9},{10,11},{12,13},{14,15},{16,17},{18,... | collective-permute-start | bytes 1007624 | tf_op jit(solution)/shard_map/ppermute | solution.py:919
  100.2 8.3 %collective-permute-done.15.refs_1_.kv0 = bf16[656,256]{1,0:T(8,128)(2,1)S(1)} collective-permute-done((bf16[656,256]{1,0:T(8,128)(2,1)}, bf16[656,256]{1,0:T(8,128)(2,1)S(1)}, u32[]{:S(2)}, u32[]{:S(2)}) %collective-permute-start.15) | collective-permute-done | bytes 335904 | tf_op jit(solution)/shard_map/ppermute | solution.py:919
  111.6 10.1 %attend.2 = (bf16[960,256]{1,0:T(8,128)(2,1)S(1)}, f32[15,256]{1,0:T(8,128)S(1)}) custom-call(bf16[960,256]{1,0:T(8,128)(2,1)S(1)} %copy-done.29, bf16[656,256]{1,0:T(8,128)(2,1)S(1)} %collective-permute-done.15.refs_1_.kv0, bf16[656,256]{1,0:T(8,128)(2,1)S(1)} %collective-permute-done.18.kv1, bf16[656,256]{1,0:T(8,128)(2,1)S(1)} %copy-done.5), custom_call_target="tpu_custom_call" | custom-call | flops 1024 | bytes 1024 | tf_op jit(solution)/shard_map/attend/pallas_call | solution.py:172
  122.3 11.0 %collective-permute-done.17.refs_0_ = bf16[4,368,640]{2,1,0:T(8,128)(2,1)} collective-permute-done((bf16[4,368,640]{2,1,0:T(8,128)(2,1)}, bf16[4,368,640]{2,1,0:T(8,128)(2,1)}, u32[]{:S(2)}, u32[]{:S(2)}) %collective-permute-start.17) | collective-permute-done | bytes 1884192 | tf_op jit(solution)/shard_map/ppermute | solution.py:880
  134.8 2.8 collective-permute-done.22.rest_15_
  137.6 21.0 %post.2 = (bf16[256,960]{1,0:T(8,128)(2,1)}, f32[256,960]{1,0:T(8,128)}, bf16[256,960]{1,0:T(8,128)(2,1)}, bf16[256,2560]{1,0:T(8,128)(2,1)}, bf16[256,2560]{1,0...) custom-call(s32[3]{0:T(128)} %copy-done.49, ...), custom_call_target="tpu_custom_call" | custom-call | flops 1024 | bytes 1024 | tf_op jit(solution)/shard_map/post/pallas_call | solution.py:328
  158.7 4.0 collective-permute-start.24
  163.5 5.9 %collective-permute-start.27 = (bf16[256,960]{1,0:T(8,128)(2,1)}, bf16[256,960]{1,0:T(8,128)(2,1)S(1)}, u32[]{:S(2)}, u32[]{:S(2)}) collective-permute-start(bf16[256,960]{1,0:T(8,128)(2,1)} %get-tuple-element.109.rest_1_), channel_id=1, source_target_pairs={{0,4},{4,0},{8,12},{12,8},{16,20},{20,16},{24,28},{28,24},{1,5},{5... | collective-permute-start | bytes 1474568 | tf_op jit(solution)/shard_map/ppermute | solution.py:880
  169.4 1.7 collective-permute-done.24.kv0
  175.1 10.5 %attend.3 = (bf16[960,256]{1,0:T(8,128)(2,1)S(1)}, f32[15,256]{1,0:T(8,128)S(1)}) custom-call(bf16[960,256]{1,0:T(8,128)(2,1)S(1)} %copy-done.28, bf16[656,256]{1,0:T(8,128)(2,1)S(1)} %collective-permute-done.24.kv0, bf16[656,256]{1,0:T(8,128)(2,1)S(1)} %collective-permute-done.25.kv1, bf16[656,256]{1,0:T(8,128)(2,1)S(1)} %copy-done.3, ...), custom_call_target="tpu_custom_call" | custom-call | flops 1024 | bytes 1024 | tf_op jit(solution)/shard_map/attend/pallas_call | solution.py:172
  187.3 18.3 %post.3 = (bf16[256,960]{1,0:T(8,128)(2,1)}, f32[256,960]{1,0:T(8,128)}, bf16[256,960]{1,0:T(8,128)(2,1)}, bf16[256,2560]{1,0:T(8,128)(2,1)}, bf16[256,2560]{1,0...) custom-call(s32[3]{0:T(128)} %copy-done.49, bf16[960,256]{1,0:T(8,128)(2,1)} %copy-done.55, ...), custom_call_target="tpu_custom_call" | custom-call | flops 1024 | bytes 1024 | tf_op jit(solution)/shard_map/post/pallas_call | solution.py:328
  205.7 20.9 %back_start.1 = (bf16[256,960]{1,0:T(8,128)(2,1)}, bf16[256,2560]{1,0:T(8,128)(2,1)}, bf16[256,2560]{1,0:T(8,128)(2,1)}, f32[256,960]{1,0:T(8,128)}, bf16[3,256,...) custom-call(s32[3]{0:T(128)} %copy-done.49, bf16[960,384]{1,0:T(8,128)(2,1)} %bitcast.30, ...), custom_call_target="tpu_custom_call" | custom-call | flops 1024 | bytes 1024 | tf_op jit(solution)/shard_map/back_start/pallas_call | solution.py:483
  227.7 2.5 collective-permute-done.30.rest_0_.rest_2_
  232.0 1.5 copy-done.14
  234.6 12.6 %attend_back.2 = (bf16[3,256,384]{2,1,0:T(8,128)(2,1)S(1)}, bf16[3,256,384]{2,1,0:T(8,128)(2,1)S(1)}, f32[640,256]{1,0:T(8,128)S(1)}, bf16[640,256]{1,0:T(8,128)(2,1)S(1)}, f32[640,256]{1,0:T(8,128)S(1)}) custom-call(s32[3]{0:T(128)S(1)} %copy-done.50, bf16[3,256,384]{2,1,0:T(8,128)(2,1)S(1)} %copy-done.14, bf16[960,256]{1,0:T(8,128)(2,1)S(1)} %copy-done.28, ...), custom_call_target="tpu_custom_call" | custom-call | flops 1024 | bytes 1024 | tf_op jit(solution)/shard_map/attend_back/pallas_call | solution.py:225
  251.7 10.3 %collective-permute-done.35.rest_20_ = bf16[640,256]{1,0:T(8,128)(2,1)S(1)} collective-permute-done((bf16[640,256]{1,0:T(8,128)(2,1)S(1)}, bf16[640,256]{1,0:T(8,128)(2,1)S(1)}, u32[]{:S(2)}, u32[]{:S(2)}) %collective-permute-start.35) | collective-permute-done | bytes 327712 | tf_op jit(solution)/shard_map/ppermute | solution.py:928
  262.7 21.1 %back_join.1 = (bf16[256,384]{1,0:T(8,128)(2,1)}, bf16[256,384]{1,0:T(8,128)(2,1)}, bf16[256,384]{1,0:T(8,128)(2,1)}, f32[1,960]{1,0:T(1,128)}, bf16[256,960]{1,...) custom-call(s32[3]{0:T(128)} %copy-done.49, ...), custom_call_target="tpu_custom_call" | custom-call | flops 1024 | bytes 1024 | tf_op jit(solution)/shard_map/back_join/pallas_call | solution.py:483
  284.0 3.2 collective-permute-done.40.rest_7_
  288.3 11.5 %grad_ffn.1 = (bf16[2,960,640]{2,1,0:T(8,128)(2,1)}, bf16[2,960,640]{2,1,0:T(8,128)(2,1)}) custom-call(s32[3]{0:T(128)} %copy-done.49, bf16[256,960]{1,0:T(8,128)(2,1)} %get-tuple-element.122.rest_0_, bf16[256,960]{1,0:T(8,128)(2,1)} %get-tuple-element.109.rest_1_, bf16[256,960]{1,0:T(8,128)(2,1)} %copy-done.27, bf16[256,960]{1,0:T(8,128)(2,1)} %copy-done.26, ...), custom_call_target="tpu_custom_call" | custom-call | flops 1024 | bytes 1024 | tf_op jit(solution)/shard_map/grad_ffn/pallas_call | solution.py:524
  299.8 1.7 collective-permute-start.44
  303.1 1.7 copy-done.10
  304.8 12.6 %attend_back.3 = (bf16[3,256,384]{2,1,0:T(8,128)(2,1)S(1)}, bf16[3,256,384]{2,1,0:T(8,128)(2,1)S(1)}, f32[640,256]{1,0:T(8,128)S(1)}, bf16[640,256]{1,0:T(8,128)(2,1)S(1)}, f32[640,256]{1,0:T(8,128)S(1)}) custom-call(s32[3]{0:T(128)S(1)} %copy-done.51, bf16[3,256,384]{2,1,0:T(8,128)(2,1)S(1)} %copy-done.15, bf16[960,256]{1,0:T(8,128)(2,1)S(1)} %copy-done.30, ...), custom_call_target="tpu_custom_call" | custom-call | flops 1024 | bytes 1024 | tf_op jit(solution)/shard_map/attend_back/pallas_call | solution.py:225
  323.5 8.2 %grad_down.1 = (bf16[2,480,640]{2,1,0:T(8,128)(2,1)}, bf16[2,480,640]{2,1,0:T(8,128)(2,1)}) custom-call(s32[3]{0:T(128)} %copy-done.49, bf16[256,960]{1,0:T(8,128)(2,1)} %get-tuple-element.133.rest_0_, bf16[256,960]{1,0:T(8,128)(2,1)} %get-tuple-element.149.rest_1_, bf16[256,960]{1,0:T(8,128)(2,1)} %copy-done.69, bf16[256,960]{1,0:T(8,128)(2,1)} %copy-done.79, ...), custom_call_target="tpu_custom_call" | custom-call | flops 1024 | bytes 1024 | tf_op jit(solution)/shard_map/grad_down/pallas_call | solution.py:555
  331.7 2.7 collective-permute-start.46
  335.1 7.0 %back_end.1 = (bf16[256,384]{1,0:T(8,128)(2,1)}, bf16[256,384]{1,0:T(8,128)(2,1)}, bf16[256,384]{1,0:T(8,128)(2,1)}, f32[1,960]{1,0:T(1,128)}, bf16[1920,256]{1,0:T(8,128)(2,1)}) custom-call(s32[3]{0:T(128)} %copy-done.49, bf16[960,384]{1,0:T(8,128)(2,1)} %bitcast.32, bf16[960,384]{1,0:T(8,128)(2,1)} %collective-permute-done.3.refs_1_.rest_1_, ...), custom_call_target="tpu_custom_call" | custom-call | flops 1024 | bytes 1024 | tf_op jit(solution)/shard_map/back_end/pallas_call | solution.py:483
  343.0 2.1 sum_first.3
  347.9 1.5 collective-permute-done.47.rest_17_
  350.4 10.6 %grad_attention.1 = (bf16[960,384]{1,0:T(8,128)(2,1)}, bf16[960,384]{1,0:T(8,128)(2,1)}, bf16[2,960,384]{2,1,0:T(8,128)(2,1)}) custom-call(s32[3]{0:T(128)} %copy-done.49, bf16[256,960]{1,0:T(8,128)(2,1)} %get-tuple-element.121.rest_0_, bf16[256,960]{1,0:T(8,128)(2,1)} %get-tuple-element.108.rest_1_, bf16[256,960]{1,0:T(8,128)(2,1)} %copy-done.24, ...), custom_call_target="tpu_custom_call" | custom-call | flops 1024 | bytes 1024 | tf_op jit(solution)/shard_map/grad_attention/pallas_call | solution.py:606
  360.9 2.1 collective-permute-start.51
  365.4 1.7 sum_third.3
  367.1 4.0 collective-permute-start.50
  373.1 7.5 %collective-permute-done.52.rest_1_ = bf16[960,384]{1,0:T(8,128)(2,1)S(1)} collective-permute-done((bf16[960,384]{1,0:T(8,128)(2,1)}, bf16[960,384]{1,0:T(8,128)(2,1)S(1)}, u32[]{:S(2)}, u32[]{:S(2)}) %collective-permute-start.52) | collective-permute-done | bytes 737312 | tf_op jit(solution)/shard_map/ppermute | solution.py:880
  381.4 1.9 collective-permute-start.54
  383.5 15.3 %collective-permute-done.50.got_ref = bf16[480,640]{1,0:T(8,128)(2,1)S(1)} collective-permute-done((bf16[480,640]{1,0:T(8,128)(2,1)S(1)}, bf16[480,640]{1,0:T(8,128)(2,1)S(1)}, u32[]{:S(2)}, u32[]{:S(2)}) %collective-permute-start.50) | collective-permute-done | bytes 614432 | tf_op jit(solution)/shard_map/ppermute | solution.py:886
  399.6 1.9 collective-permute-done.49.got_ref
  405.5 14.1 %collective-permute-done.53.got_ref = bf16[240,640]{1,0:T(8,128)(2,1)S(1)} collective-permute-done((bf16[240,640]{1,0:T(8,128)(2,1)S(1)}, bf16[240,640]{1,0:T(8,128)(2,1)S(1)}, u32[]{:S(2)}, u32[]{:S(2)}) %collective-permute-start.53) | collective-permute-done | bytes 307232 | tf_op jit(solution)/shard_map/ppermute | solution.py:886
  420.8 1.4 collective-permute-start.58
  426.4 3.4 collective-permute-done.58.got_ref
  429.8 2.0 collective-permute-start.74
  432.4 8.6 %collective-permute-done.74.got_ref = bf16[120,640]{1,0:T(8,128)(2,1)S(1)} collective-permute-done((bf16[120,640]{1,0:T(8,128)(2,1)S(1)}, bf16[120,640]{1,0:T(8,128)(2,1)S(1)}, u32[]{:S(2)}, u32[]{:S(2)}) %collective-permute-start.74) | collective-permute-done | bytes 153632 | tf_op jit(solution)/shard_map/ppermute | solution.py:880
  442.8 1.9 collective-permute-start.62
  447.0 2.5 collective-permute-done.77.rest_3_
  451.0 4.8 %collective-permute-done.76.rest_2_ = bf16[120,640]{1,0:T(8,128)(2,1)S(1)} collective-permute-done((bf16[120,640]{1,0:T(8,128)(2,1)S(1)}, bf16[120,640]{1,0:T(8,128)(2,1)S(1)}, u32[]{:S(2)}, u32[]{:S(2)}) %collective-permute-start.76) | collective-permute-done | bytes 153632 | tf_op jit(solution)/shard_map/ppermute | solution.py:880
  458.3 4.0 collective-permute-done.60.rest_1_
  462.8 1.7 collective-permute-done.64.rest_5_
  465.6 3.1 lay.2
  468.7 1.7 copy-done.13
  470.4 2.4 lay.3
  474.0 2.3 lay_down.1
  (332 shorter events, 83.9 us)
Async XLA Ops:
  6.8 12.8 %collective-permute-start.1 = (bf16[240,384]{1,0:T(8,128)(2,1)S(1)}, bf16[240,384]{1,0:T(8,128)(2,1)S(1)}, u32[]{:S(2)}, u32[]{:S(2)}) collective-permute-start(bf16[240,384]{1,0:T(8,128)(2,1)S(1)} %pick_first.1.rest_0_), channel_id=1, source_target_pairs={{0,2},{1,3},{2,0},{3,1},{4,6},{5,7},{6,4},{7,5},{8,10},{9,11},{10,... | collective-permute-start | bytes 552968 | tf_op jit(solution)/shard_map/ppermute | solution.py:886
  10.9 9.4 %collective-permute-start = (bf16[240,384]{1,0:T(8,128)(2,1)S(1)}, bf16[240,384]{1,0:T(8,128)(2,1)S(1)}, u32[]{:S(2)}, u32[]{:S(2)}) collective-permute-start(bf16[240,384]{1,0:T(8,128)(2,1)S(1)} %pick_first.1.rest_0_), channel_id=1, source_target_pairs={{0,1},{1,0},{2,3},{3,2},{4,5},{5,4},{6,7},{7,6},{8,9},{9,8},{10,11... | collective-permute-start | bytes 552968 | tf_op jit(solution)/shard_map/ppermute | solution.py:886
  19.7 5.8 %collective-permute-start.2 = (bf16[240,384]{1,0:T(8,128)(2,1)S(1)}, bf16[240,384]{1,0:T(8,128)(2,1)S(1)}, u32[]{:S(2)}, u32[]{:S(2)}) collective-permute-start(bf16[240,384]{1,0:T(8,128)(2,1)S(1)} %collective-permute-done.1.rest_2_), channel_id=1, source_target_pairs={{0,1},{1,0},{2,3},{3,2},{4,5},{5,4},{6,7},{7,6},{8,9},{9,8},{10,11... | collective-permute-start | bytes 552968 | tf_op jit(solution)/shard_map/ppermute | solution.py:886
  27.1 19.6 %collective-permute-start.3 = (bf16[960,384]{1,0:T(8,128)(2,1)S(1)}, bf16[960,384]{1,0:T(8,128)(2,1)}, u32[]{:S(2)}, u32[]{:S(2)}) collective-permute-start(bf16[960,384]{1,0:T(8,128)(2,1)S(1)} %bitcast.24), channel_id=1, source_target_pairs={{0,8},{4,20},{8,0},{12,28},{16,24},{20,4},{24,16},{28,12},{1,9},{5... | collective-permute-start | bytes 2211848 | tf_op jit(solution)/shard_map/ppermute | solution.py:880
  28.3 25.2 %collective-permute-start.4 = (bf16[960,384]{1,0:T(8,128)(2,1)S(1)}, bf16[960,384]{1,0:T(8,128)(2,1)}, u32[]{:S(2)}, u32[]{:S(2)}) collective-permute-start(bf16[960,384]{1,0:T(8,128)(2,1)S(1)} %bitcast.25), channel_id=1, source_target_pairs={{0,16},{4,12},{8,24},{12,4},{16,0},{20,28},{24,8},{28,20},{1,17},{... | collective-permute-start | bytes 2211848 | tf_op jit(solution)/shard_map/ppermute | solution.py:880
  29.9 23.3 %collective-permute-start.11 = (bf16[368,640]{1,0:T(8,128)(2,1)S(1)}, bf16[368,640]{1,0:T(8,128)(2,1)S(1)}, u32[]{:S(2)}, u32[]{:S(2)}) collective-permute-start(bf16[368,640]{1,0:T(8,128)(2,1)S(1)} %pick.1.rest_4_.rest_0_), channel_id=1, source_target_pairs={{0,2},{1,3},{2,0},{3,1},{4,6},{5,7},{6,4},{7,5},{8,10},{9,11},{10,... | collective-permute-start | bytes 1413128 | tf_op jit(solution)/shard_map/ppermute | solution.py:886
  33.1 20.4 %collective-permute-start.10 = (bf16[368,640]{1,0:T(8,128)(2,1)S(1)}, bf16[368,640]{1,0:T(8,128)(2,1)S(1)}, u32[]{:S(2)}, u32[]{:S(2)}) collective-permute-start(bf16[368,640]{1,0:T(8,128)(2,1)S(1)} %pick.1.rest_4_.rest_0_), channel_id=1, source_target_pairs={{0,1},{1,0},{2,3},{3,2},{4,5},{5,4},{6,7},{7,6},{8,9},{9,8},{10,11... | collective-permute-start | bytes 1413128 | tf_op jit(solution)/shard_map/ppermute | solution.py:886
  46.7 18.3 %collective-permute-start.5 = (bf16[960,384]{1,0:T(8,128)(2,1)}, bf16[960,384]{1,0:T(8,128)(2,1)S(1)}, u32[]{:S(2)}, u32[]{:S(2)}) collective-permute-start(bf16[960,384]{1,0:T(8,128)(2,1)} %collective-permute-done.3.refs_1_.rest_1_), channel_id=1, source_target_pairs={{0,16},{4,12},{8,24},{12,4},{16,0},{20,28},{24,8},{28,20},{1,17},{... | collective-permute-start | bytes 2211848 | tf_op jit(solution)/shard_map/ppermute | solution.py:880
  53.5 11.4 %collective-permute-start.12 = (bf16[368,640]{1,0:T(8,128)(2,1)S(1)}, bf16[368,640]{1,0:T(8,128)(2,1)S(1)}, u32[]{:S(2)}, u32[]{:S(2)}) collective-permute-start(bf16[368,640]{1,0:T(8,128)(2,1)S(1)} %hold.4.rest_2_), channel_id=1, source_target_pairs={{0,1},{1,0},{2,3},{3,2},{4,5},{5,4},{6,7},{7,6},{8,9},{9,8},{10,11... | collective-permute-start | bytes 1413128 | tf_op jit(solution)/shard_map/ppermute | solution.py:886
  67.9 41.3 %collective-permute-start.16 = (bf16[4,368,640]{2,1,0:T(8,128)(2,1)}, bf16[4,368,640]{2,1,0:T(8,128)(2,1)S(1)}, u32[]{:S(2)}, u32[]{:S(2)}) collective-permute-start(bf16[4,368,640]{2,1,0:T(8,128)(2,1)} %stack.31.rest_8_), channel_id=1, source_target_pairs={{0,16},{4,12},{8,24},{12,4},{16,0},{20,28},{24,8},{28,20},{1,17},{... | collective-permute-start | bytes 5652488 | tf_op jit(solution)/shard_map/ppermute | solution.py:880
  68.5 40.7 %collective-permute-start.13 = (bf16[4,368,640]{2,1,0:T(8,128)(2,1)}, bf16[4,368,640]{2,1,0:T(8,128)(2,1)}, u32[]{:S(2)}, u32[]{:S(2)}) collective-permute-start(bf16[4,368,640]{2,1,0:T(8,128)(2,1)} %stack.31.rest_8_), channel_id=1, source_target_pairs={{0,8},{4,20},{8,0},{12,28},{16,24},{20,4},{24,16},{28,12},{1,9},{5... | collective-permute-start | bytes 5652488 | tf_op jit(solution)/shard_map/ppermute | solution.py:880
  69.1 11.2 %collective-permute-start.6 = (bf16[960,384]{1,0:T(8,128)(2,1)S(1)}, bf16[960,384]{1,0:T(8,128)(2,1)S(1)}, u32[]{:S(2)}, u32[]{:S(2)}) collective-permute-start(bf16[960,384]{1,0:T(8,128)(2,1)S(1)} %bitcast.26), channel_id=1, source_target_pairs={{0,4},{4,0},{8,12},{12,8},{16,20},{20,16},{24,28},{28,24},{1,5},{5... | collective-permute-start | bytes 2211848 | tf_op jit(solution)/shard_map/ppermute | solution.py:880
  69.2 5.3 %collective-permute-start.14 = (bf16[976,256]{1,0:T(8,128)(2,1)S(1)}, bf16[976,256]{1,0:T(8,128)(2,1)S(1)}, u32[]{:S(2)}, u32[]{:S(2)}) collective-permute-start(bf16[976,256]{1,0:T(8,128)(2,1)S(1)} %pad_maximum_fusion), channel_id=1, source_target_pairs={{0,0},{1,4},{2,1},{3,5},{4,2},{5,6},{6,3},{7,7},{8,8},{9,12},{10,9... | collective-permute-start | bytes 1499144 | tf_op jit(solution)/shard_map/ppermute | solution.py:897
  69.9 14.1 %collective-permute-start.8 = (bf16[960,384]{1,0:T(8,128)(2,1)}, bf16[960,384]{1,0:T(8,128)(2,1)}, u32[]{:S(2)}, u32[]{:S(2)}) collective-permute-start(bf16[960,384]{1,0:T(8,128)(2,1)} %collective-permute-done.4.refs_2_.rest_2_), channel_id=1, source_target_pairs={{0,4},{4,0},{8,12},{12,8},{16,20},{20,16},{24,28},{28,24},{1,5},{5... | collective-permute-start | bytes 2211848 | tf_op jit(solution)/shard_map/ppermute | solution.py:880
  74.5 9.5 %collective-permute-start.7 = (bf16[960,384]{1,0:T(8,128)(2,1)}, bf16[960,384]{1,0:T(8,128)(2,1)}, u32[]{:S(2)}, u32[]{:S(2)}) collective-permute-start(bf16[960,384]{1,0:T(8,128)(2,1)} %collective-permute-done.3.refs_1_.rest_1_), channel_id=1, source_target_pairs={{0,4},{4,0},{8,12},{12,8},{16,20},{20,16},{24,28},{28,24},{1,5},{5... | collective-permute-start | bytes 2211848 | tf_op jit(solution)/shard_map/ppermute | solution.py:880
  90.8 17.6 %collective-permute-start.15 = (bf16[656,256]{1,0:T(8,128)(2,1)}, bf16[656,256]{1,0:T(8,128)(2,1)S(1)}, u32[]{:S(2)}, u32[]{:S(2)}) collective-permute-start(bf16[656,256]{1,0:T(8,128)(2,1)} %get-tuple-element.102.kv2.rest_16_), channel_id=1, source_target_pairs={{0,1},{2,3},{4,5},{6,7},{8,9},{10,11},{12,13},{14,15},{16,17},{18,... | collective-permute-start | bytes 1007624 | tf_op jit(solution)/shard_map/ppermute | solution.py:919
  109.2 24.1 %collective-permute-start.17 = (bf16[4,368,640]{2,1,0:T(8,128)(2,1)}, bf16[4,368,640]{2,1,0:T(8,128)(2,1)}, u32[]{:S(2)}, u32[]{:S(2)}) collective-permute-start(bf16[4,368,640]{2,1,0:T(8,128)(2,1)} %hold.5.rest_9_), channel_id=1, source_target_pairs={{0,16},{4,12},{8,24},{12,4},{16,0},{20,28},{24,8},{28,20},{1,17},{... | collective-permute-start | bytes 5652488 | tf_op jit(solution)/shard_map/ppermute | solution.py:880
  110.0 23.4 %collective-permute-start.19 = (bf16[4,368,640]{2,1,0:T(8,128)(2,1)}, bf16[4,368,640]{2,1,0:T(8,128)(2,1)S(1)}, u32[]{:S(2)}, u32[]{:S(2)}) collective-permute-start(bf16[4,368,640]{2,1,0:T(8,128)(2,1)} %stack.31.rest_8_), channel_id=1, source_target_pairs={{0,4},{4,0},{8,12},{12,8},{16,20},{20,16},{24,28},{28,24},{1,5},{5... | collective-permute-start | bytes 5652488 | tf_op jit(solution)/shard_map/ppermute | solution.py:880
  121.7 13.0 %collective-permute-start.20 = (bf16[4,368,640]{2,1,0:T(8,128)(2,1)}, bf16[4,368,640]{2,1,0:T(8,128)(2,1)}, u32[]{:S(2)}, u32[]{:S(2)}) collective-permute-start(bf16[4,368,640]{2,1,0:T(8,128)(2,1)} %hold.5.rest_9_), channel_id=1, source_target_pairs={{0,4},{4,0},{8,12},{12,8},{16,20},{20,16},{24,28},{28,24},{1,5},{5... | collective-permute-start | bytes 5652488 | tf_op jit(solution)/shard_map/ppermute | solution.py:880
  121.9 11.4 %collective-permute-start.21 = (bf16[4,368,640]{2,1,0:T(8,128)(2,1)S(1)}, bf16[4,368,640]{2,1,0:T(8,128)(2,1)S(1)}, u32[]{:S(2)}, u32[]{:S(2)}) collective-permute-start(bf16[4,368,640]{2,1,0:T(8,128)(2,1)S(1)} %collective-permute-done.16.refs_2_.rest_10_), channel_id=1, source_target_pairs={{0,4},{4,0},{8,12},{12,8},{16,20},{20,16},{24,28},{28,24},{1,5},{5... | collective-permute-start | bytes 5652488 | tf_op jit(solution)/shard_map/ppermute | solution.py:880
  133.4 4.2 collective-permute-start.22
  158.6 15.3 %collective-permute-start.29 = (bf16[256,2560]{1,0:T(8,128)(2,1)}, bf16[256,2560]{1,0:T(8,128)(2,1)S(1)}, u32[]{:S(2)}, u32[]{:S(2)}) collective-permute-start(bf16[256,2560]{1,0:T(8,128)(2,1)} %get-tuple-element.111.rest_5_), channel_id=1, source_target_pairs={{0,4},{4,0},{8,12},{12,8},{16,20},{20,16},{24,28},{28,24},{1,5},{5... | collective-permute-start | bytes 3932168 | tf_op jit(solution)/shard_map/ppermute | solution.py:880
  158.7 12.5 %collective-permute-start.24 = (bf16[656,256]{1,0:T(8,128)(2,1)}, bf16[656,256]{1,0:T(8,128)(2,1)S(1)}, u32[]{:S(2)}, u32[]{:S(2)}) collective-permute-start(bf16[656,256]{1,0:T(8,128)(2,1)} %get-tuple-element.107.kv2.rest_16_), channel_id=1, source_target_pairs={{0,1},{2,3},{4,5},{6,7},{8,9},{10,11},{12,13},{14,15},{16,17},{18,... | collective-permute-start | bytes 1007624 | tf_op jit(solution)/shard_map/ppermute | solution.py:919
  162.6 9.5 %collective-permute-start.26 = (bf16[256,960]{1,0:T(8,128)(2,1)S(1)}, bf16[256,960]{1,0:T(8,128)(2,1)S(1)}, u32[]{:S(2)}, u32[]{:S(2)}) collective-permute-start(bf16[256,960]{1,0:T(8,128)(2,1)S(1)} %copy-done.73), channel_id=1, source_target_pairs={{0,4},{4,0},{8,12},{12,8},{16,20},{20,16},{24,28},{28,24},{1,5},{5... | collective-permute-start | bytes 1474568 | tf_op jit(solution)/shard_map/ppermute | solution.py:880
  162.8 23.7 %collective-permute-start.23 = (bf16[960,256]{1,0:T(8,128)(2,1)S(1)}, bf16[960,256]{1,0:T(8,128)(2,1)S(1)}, u32[]{:S(2)}, u32[]{:S(2)}) collective-permute-start(bf16[960,256]{1,0:T(8,128)(2,1)S(1)} %bitcast.40), channel_id=1, source_target_pairs={{0,0},{1,4},{2,1},{3,5},{4,2},{5,6},{6,3},{7,7},{8,8},{9,12},{10,9... | collective-permute-start | bytes 1474568 | tf_op jit(solution)/shard_map/ppermute | solution.py:897
  163.5 8.8 %collective-permute-start.27 = (bf16[256,960]{1,0:T(8,128)(2,1)}, bf16[256,960]{1,0:T(8,128)(2,1)S(1)}, u32[]{:S(2)}, u32[]{:S(2)}) collective-permute-start(bf16[256,960]{1,0:T(8,128)(2,1)} %get-tuple-element.109.rest_1_), channel_id=1, source_target_pairs={{0,4},{4,0},{8,12},{12,8},{16,20},{20,16},{24,28},{28,24},{1,5},{5... | collective-permute-start | bytes 1474568 | tf_op jit(solution)/shard_map/ppermute | solution.py:880
  205.6 26.4 %collective-permute-start.33 = (bf16[256,2560]{1,0:T(8,128)(2,1)}, bf16[256,2560]{1,0:T(8,128)(2,1)S(1)}, u32[]{:S(2)}, u32[]{:S(2)}) collective-permute-start(bf16[256,2560]{1,0:T(8,128)(2,1)} %get-tuple-element.124.rest_4_), channel_id=1, source_target_pairs={{0,4},{4,0},{8,12},{12,8},{16,20},{20,16},{24,28},{28,24},{1,5},{5... | collective-permute-start | bytes 3932168 | tf_op jit(solution)/shard_map/ppermute | solution.py:880
  226.6 25.0 %collective-permute-start.38 = (bf16[256,2560]{1,0:T(8,128)(2,1)}, bf16[256,2560]{1,0:T(8,128)(2,1)S(1)}, u32[]{:S(2)}, u32[]{:S(2)}) collective-permute-start(bf16[256,2560]{1,0:T(8,128)(2,1)} %get-tuple-element.134), channel_id=1, source_target_pairs={{0,4},{4,0},{8,12},{12,8},{16,20},{20,16},{24,28},{28,24},{1,5},{5... | collective-permute-start | bytes 3932168 | tf_op jit(solution)/shard_map/ppermute | solution.py:880
  227.2 4.0 collective-permute-start.31
  227.3 4.7 collective-permute-start.32
  250.3 11.7 %collective-permute-start.35 = (bf16[640,256]{1,0:T(8,128)(2,1)S(1)}, bf16[640,256]{1,0:T(8,128)(2,1)S(1)}, u32[]{:S(2)}, u32[]{:S(2)}) collective-permute-start(bf16[640,256]{1,0:T(8,128)(2,1)S(1)} %far_sum.2), channel_id=1, source_target_pairs={{1,0},{3,2},{5,4},{7,6},{9,8},{11,10},{13,12},{15,14},{17,16},{19,... | collective-permute-start | bytes 983048 | tf_op jit(solution)/shard_map/ppermute | solution.py:928
  299.8 42.3 %collective-permute-start.44 = (bf16[2,960,640]{2,1,0:T(8,128)(2,1)}, bf16[2,960,640]{2,1,0:T(8,128)(2,1)S(1)}, u32[]{:S(2)}, u32[]{:S(2)}) collective-permute-start(bf16[2,960,640]{2,1,0:T(8,128)(2,1)} %get-tuple-element.143.rest_1_), channel_id=1, source_target_pairs={{0,8},{4,20},{8,0},{12,28},{16,24},{20,4},{24,16},{28,12},{1,9},{5... | collective-permute-start | bytes 7372808 | tf_op jit(solution)/shard_map/ppermute | solution.py:880
  321.4 13.0 %collective-permute-start.42 = (bf16[640,256]{1,0:T(8,128)(2,1)S(1)}, bf16[640,256]{1,0:T(8,128)(2,1)S(1)}, u32[]{:S(2)}, u32[]{:S(2)}) collective-permute-start(bf16[640,256]{1,0:T(8,128)(2,1)S(1)} %far_sum.3.rest_8_), channel_id=1, source_target_pairs={{1,0},{3,2},{5,4},{7,6},{9,8},{11,10},{13,12},{15,14},{17,16},{19,... | collective-permute-start | bytes 983048 | tf_op jit(solution)/shard_map/ppermute | solution.py:928
  331.7 31.5 %collective-permute-start.46 = (bf16[2,480,640]{2,1,0:T(8,128)(2,1)}, bf16[2,480,640]{2,1,0:T(8,128)(2,1)}, u32[]{:S(2)}, u32[]{:S(2)}) collective-permute-start(bf16[2,480,640]{2,1,0:T(8,128)(2,1)} %get-tuple-element.150.rest_18_), channel_id=1, source_target_pairs={{0,1},{1,0},{2,3},{3,2},{4,5},{5,4},{6,7},{7,6},{8,9},{9,8},{10,11... | collective-permute-start | bytes 3686408 | tf_op jit(solution)/shard_map/ppermute | solution.py:886
  346.6 24.5 %collective-permute-start.45 = (bf16[960,640]{1,0:T(8,128)(2,1)}, bf16[960,640]{1,0:T(8,128)(2,1)S(1)}, u32[]{:S(2)}, u32[]{:S(2)}) collective-permute-start(bf16[960,640]{1,0:T(8,128)(2,1)} %get-tuple-element.155.rest_24_), channel_id=1, source_target_pairs={{0,16},{4,12},{8,24},{12,4},{16,0},{20,28},{24,8},{28,20},{1,17},{... | collective-permute-start | bytes 3686408 | tf_op jit(solution)/shard_map/ppermute | solution.py:880
  360.9 12.2 %collective-permute-start.51 = (bf16[960,384]{1,0:T(8,128)(2,1)}, bf16[960,384]{1,0:T(8,128)(2,1)S(1)}, u32[]{:S(2)}, u32[]{:S(2)}) collective-permute-start(bf16[960,384]{1,0:T(8,128)(2,1)} %get-tuple-element.166.rest_0_), channel_id=1, source_target_pairs={{0,8},{4,20},{8,0},{12,28},{16,24},{20,4},{24,16},{28,12},{1,9},{5... | collective-permute-start | bytes 2211848 | tf_op jit(solution)/shard_map/ppermute | solution.py:880
  363.0 17.6 %collective-permute-start.52 = (bf16[960,384]{1,0:T(8,128)(2,1)}, bf16[960,384]{1,0:T(8,128)(2,1)S(1)}, u32[]{:S(2)}, u32[]{:S(2)}) collective-permute-start(bf16[960,384]{1,0:T(8,128)(2,1)} %get-tuple-element.167.rest_1_), channel_id=1, source_target_pairs={{0,8},{4,20},{8,0},{12,28},{16,24},{20,4},{24,16},{28,12},{1,9},{5... | collective-permute-start | bytes 2211848 | tf_op jit(solution)/shard_map/ppermute | solution.py:880
  367.1 31.8 %collective-permute-start.50 = (bf16[480,640]{1,0:T(8,128)(2,1)S(1)}, bf16[480,640]{1,0:T(8,128)(2,1)S(1)}, u32[]{:S(2)}, u32[]{:S(2)}) collective-permute-start(bf16[480,640]{1,0:T(8,128)(2,1)S(1)} %get-tuple-element.168.rest_1_), channel_id=1, source_target_pairs={{0,2},{1,3},{2,0},{3,1},{4,6},{5,7},{6,4},{7,5},{8,10},{9,11},{10,... | collective-permute-start | bytes 1843208 | tf_op jit(solution)/shard_map/ppermute | solution.py:886
  372.1 29.3 %collective-permute-start.49 = (bf16[2,240,640]{2,1,0:T(8,128)(2,1)S(1)}, bf16[2,240,640]{2,1,0:T(8,128)(2,1)S(1)}, u32[]{:S(2)}, u32[]{:S(2)}) collective-permute-start(bf16[2,240,640]{2,1,0:T(8,128)(2,1)S(1)} %get-tuple-element.170), channel_id=1, source_target_pairs={{0,1},{1,0},{2,3},{3,2},{4,5},{5,4},{6,7},{7,6},{8,9},{9,8},{10,11... | collective-permute-start | bytes 1843208 | tf_op jit(solution)/shard_map/ppermute | solution.py:886
  381.4 20.7 %collective-permute-start.54 = (bf16[480,384]{1,0:T(8,128)(2,1)S(1)}, bf16[480,384]{1,0:T(8,128)(2,1)S(1)}, u32[]{:S(2)}, u32[]{:S(2)}) collective-permute-start(bf16[480,384]{1,0:T(8,128)(2,1)S(1)} %get-tuple-element.177), channel_id=1, source_target_pairs={{0,16},{4,12},{8,24},{12,4},{16,0},{20,28},{24,8},{28,20},{1,17},{... | collective-permute-start | bytes 1105928 | tf_op jit(solution)/shard_map/ppermute | solution.py:880
  383.3 18.8 %collective-permute-start.55 = (bf16[480,384]{1,0:T(8,128)(2,1)S(1)}, bf16[480,384]{1,0:T(8,128)(2,1)S(1)}, u32[]{:S(2)}, u32[]{:S(2)}) collective-permute-start(bf16[480,384]{1,0:T(8,128)(2,1)S(1)} %get-tuple-element.178), channel_id=1, source_target_pairs={{0,16},{4,12},{8,24},{12,4},{16,0},{20,28},{24,8},{28,20},{1,17},{... | collective-permute-start | bytes 1105928 | tf_op jit(solution)/shard_map/ppermute | solution.py:880
  402.9 17.2 %collective-permute-start.57 = (bf16[2,240,384]{2,1,0:T(8,128)(2,1)S(1)}, bf16[2,240,384]{2,1,0:T(8,128)(2,1)S(1)}, u32[]{:S(2)}, u32[]{:S(2)}) collective-permute-start(bf16[2,240,384]{2,1,0:T(8,128)(2,1)S(1)} %get-tuple-element.179.rest_0_), channel_id=1, source_target_pairs={{0,1},{1,0},{2,3},{3,2},{4,5},{5,4},{6,7},{7,6},{8,9},{9,8},{10,11... | collective-permute-start | bytes 1105928 | tf_op jit(solution)/shard_map/ppermute | solution.py:886
  403.0 16.5 %collective-permute-start.53 = (bf16[240,640]{1,0:T(8,128)(2,1)S(1)}, bf16[240,640]{1,0:T(8,128)(2,1)S(1)}, u32[]{:S(2)}, u32[]{:S(2)}) collective-permute-start(bf16[240,640]{1,0:T(8,128)(2,1)S(1)} %get-tuple-element.176.rest_2_), channel_id=1, source_target_pairs={{0,2},{1,3},{2,0},{3,1},{4,6},{5,7},{6,4},{7,5},{8,10},{9,11},{10,... | collective-permute-start | bytes 921608 | tf_op jit(solution)/shard_map/ppermute | solution.py:886
  404.3 20.2 %collective-permute-start.59 = (bf16[2,120,640]{2,1,0:T(8,128)(2,1)S(1)}, bf16[2,120,640]{2,1,0:T(8,128)(2,1)S(1)}, u32[]{:S(2)}, u32[]{:S(2)}) collective-permute-start(bf16[2,120,640]{2,1,0:T(8,128)(2,1)S(1)} %get-tuple-element.174.rest_0_), channel_id=1, source_target_pairs={{0,8},{4,20},{8,0},{12,28},{16,24},{20,4},{24,16},{28,12},{1,9},{5... | collective-permute-start | bytes 921608 | tf_op jit(solution)/shard_map/ppermute | solution.py:880
  420.8 9.0 %collective-permute-start.58 = (bf16[240,384]{1,0:T(8,128)(2,1)S(1)}, bf16[240,384]{1,0:T(8,128)(2,1)S(1)}, u32[]{:S(2)}, u32[]{:S(2)}) collective-permute-start(bf16[240,384]{1,0:T(8,128)(2,1)S(1)} %get-tuple-element.182.rest_1_), channel_id=1, source_target_pairs={{0,2},{1,3},{2,0},{3,1},{4,6},{5,7},{6,4},{7,5},{8,10},{9,11},{10,... | collective-permute-start | bytes 552968 | tf_op jit(solution)/shard_map/ppermute | solution.py:886
  422.3 20.5 %collective-permute-start.70 = (bf16[240,640]{1,0:T(8,128)(2,1)S(1)}, bf16[240,640]{1,0:T(8,128)(2,1)S(1)}, u32[]{:S(2)}, u32[]{:S(2)}) collective-permute-start(bf16[240,640]{1,0:T(8,128)(2,1)S(1)} %sum_two.3.refs_1_.rest_0_), channel_id=1, source_target_pairs={{0,4},{4,0},{8,12},{12,8},{16,20},{20,16},{24,28},{28,24},{1,5},{5... | collective-permute-start | bytes 921608 | tf_op jit(solution)/shard_map/ppermute | solution.py:880
  422.3 22.4 %collective-permute-start.69 = (bf16[240,640]{1,0:T(8,128)(2,1)S(1)}, bf16[240,640]{1,0:T(8,128)(2,1)S(1)}, u32[]{:S(2)}, u32[]{:S(2)}) collective-permute-start(bf16[240,640]{1,0:T(8,128)(2,1)S(1)} %sum_two.3.refs_1_.rest_0_), channel_id=1, source_target_pairs={{0,24},{4,28},{8,16},{12,20},{16,8},{20,12},{24,0},{28,4},{1,25},{... | collective-permute-start | bytes 921608 | tf_op jit(solution)/shard_map/ppermute | solution.py:880
  423.3 22.7 %collective-permute-start.68 = (bf16[240,640]{1,0:T(8,128)(2,1)S(1)}, bf16[240,640]{1,0:T(8,128)(2,1)S(1)}, u32[]{:S(2)}, u32[]{:S(2)}) collective-permute-start(bf16[240,640]{1,0:T(8,128)(2,1)S(1)} %sum_two.3.refs_1_.rest_0_), channel_id=1, source_target_pairs={{0,16},{4,12},{8,24},{12,4},{16,0},{20,28},{24,8},{28,20},{1,17},{... | collective-permute-start | bytes 921608 | tf_op jit(solution)/shard_map/ppermute | solution.py:880
  424.5 21.8 %collective-permute-start.67 = (bf16[240,640]{1,0:T(8,128)(2,1)S(1)}, bf16[240,640]{1,0:T(8,128)(2,1)S(1)}, u32[]{:S(2)}, u32[]{:S(2)}) collective-permute-start(bf16[240,640]{1,0:T(8,128)(2,1)S(1)} %sum_two.3.refs_1_.rest_0_), channel_id=1, source_target_pairs={{0,8},{4,20},{8,0},{12,28},{16,24},{20,4},{24,16},{28,12},{1,9},{5... | collective-permute-start | bytes 921608 | tf_op jit(solution)/shard_map/ppermute | solution.py:880
  429.8 11.3 %collective-permute-start.74 = (bf16[120,640]{1,0:T(8,128)(2,1)S(1)}, bf16[120,640]{1,0:T(8,128)(2,1)S(1)}, u32[]{:S(2)}, u32[]{:S(2)}) collective-permute-start(bf16[120,640]{1,0:T(8,128)(2,1)S(1)} %get-tuple-element.184.rest_0_), channel_id=1, source_target_pairs={{0,16},{4,12},{8,24},{12,4},{16,0},{20,28},{24,8},{28,20},{1,17},{... | collective-permute-start | bytes 460808 | tf_op jit(solution)/shard_map/ppermute | solution.py:880
  441.7 7.9 %collective-permute-start.77 = (bf16[120,640]{1,0:T(8,128)(2,1)S(1)}, bf16[120,640]{1,0:T(8,128)(2,1)S(1)}, u32[]{:S(2)}, u32[]{:S(2)}) collective-permute-start(bf16[120,640]{1,0:T(8,128)(2,1)S(1)} %sum_two.5.rest_8_.rest_0_), channel_id=1, source_target_pairs={{0,24},{4,28},{8,16},{12,20},{16,8},{20,12},{24,0},{28,4},{1,25},{... | collective-permute-start | bytes 460808 | tf_op jit(solution)/shard_map/ppermute | solution.py:880
  442.8 14.2 %collective-permute-start.62 = (bf16[240,384]{1,0:T(8,128)(2,1)S(1)}, bf16[240,384]{1,0:T(8,128)(2,1)S(1)}, u32[]{:S(2)}, u32[]{:S(2)}) collective-permute-start(bf16[240,384]{1,0:T(8,128)(2,1)S(1)} %sum_two.4.rest_0_), channel_id=1, source_target_pairs={{0,24},{4,28},{8,16},{12,20},{16,8},{20,12},{24,0},{28,4},{1,25},{... | collective-permute-start | bytes 552968 | tf_op jit(solution)/shard_map/ppermute | solution.py:880
  444.7 11.1 %collective-permute-start.76 = (bf16[120,640]{1,0:T(8,128)(2,1)S(1)}, bf16[120,640]{1,0:T(8,128)(2,1)S(1)}, u32[]{:S(2)}, u32[]{:S(2)}) collective-permute-start(bf16[120,640]{1,0:T(8,128)(2,1)S(1)} %sum_two.5.rest_8_.rest_0_), channel_id=1, source_target_pairs={{0,16},{4,12},{8,24},{12,4},{16,0},{20,28},{24,8},{28,20},{1,17},{... | collective-permute-start | bytes 460808 | tf_op jit(solution)/shard_map/ppermute | solution.py:880
  446.0 10.7 %collective-permute-start.75 = (bf16[120,640]{1,0:T(8,128)(2,1)S(1)}, bf16[120,640]{1,0:T(8,128)(2,1)S(1)}, u32[]{:S(2)}, u32[]{:S(2)}) collective-permute-start(bf16[120,640]{1,0:T(8,128)(2,1)S(1)} %sum_two.5.rest_8_.rest_0_), channel_id=1, source_target_pairs={{0,8},{4,20},{8,0},{12,28},{16,24},{20,4},{24,16},{28,12},{1,9},{5... | collective-permute-start | bytes 460808 | tf_op jit(solution)/shard_map/ppermute | solution.py:880
  446.3 32.4 %collective-permute-start.56 = (bf16[1920,256]{1,0:T(8,128)(2,1)S(1)}, bf16[1920,256]{1,0:T(8,128)(2,1)S(1)}, u32[]{:S(2)}, u32[]{:S(2)}) collective-permute-start(bf16[1920,256]{1,0:T(8,128)(2,1)S(1)} %hold.7), channel_id=1, source_target_pairs={{0,0},{4,1},{1,2},{5,3},{2,4},{6,5},{3,6},{7,7},{8,8},{12,9},{9,10... | collective-permute-start | bytes 2949128 | tf_op jit(solution)/shard_map/ppermute | solution.py:897
  449.6 8.2 %collective-permute-start.61 = (bf16[240,384]{1,0:T(8,128)(2,1)S(1)}, bf16[240,384]{1,0:T(8,128)(2,1)S(1)}, u32[]{:S(2)}, u32[]{:S(2)}) collective-permute-start(bf16[240,384]{1,0:T(8,128)(2,1)S(1)} %sum_two.4.rest_0_), channel_id=1, source_target_pairs={{0,16},{4,12},{8,24},{12,4},{16,0},{20,28},{24,8},{28,20},{1,17},{... | collective-permute-start | bytes 552968 | tf_op jit(solution)/shard_map/ppermute | solution.py:880
  456.7 5.5 %collective-permute-start.60 = (bf16[240,384]{1,0:T(8,128)(2,1)S(1)}, bf16[240,384]{1,0:T(8,128)(2,1)S(1)}, u32[]{:S(2)}, u32[]{:S(2)}) collective-permute-start(bf16[240,384]{1,0:T(8,128)(2,1)S(1)} %sum_two.4.rest_0_), channel_id=1, source_target_pairs={{0,8},{4,20},{8,0},{12,28},{16,24},{20,4},{24,16},{28,12},{1,9},{5... | collective-permute-start | bytes 552968 | tf_op jit(solution)/shard_map/ppermute | solution.py:880
  456.9 5.3 %collective-permute-start.66 = (bf16[240,384]{1,0:T(8,128)(2,1)S(1)}, bf16[240,384]{1,0:T(8,128)(2,1)S(1)}, u32[]{:S(2)}, u32[]{:S(2)}) collective-permute-start(bf16[240,384]{1,0:T(8,128)(2,1)S(1)} %collective-permute-done.62.rest_3_), channel_id=1, source_target_pairs={{0,4},{4,0},{8,12},{12,8},{16,20},{20,16},{24,28},{28,24},{1,5},{5... | collective-permute-start | bytes 552968 | tf_op jit(solution)/shard_map/ppermute | solution.py:880
  457.8 5.0 %collective-permute-start.65 = (bf16[240,384]{1,0:T(8,128)(2,1)S(1)}, bf16[240,384]{1,0:T(8,128)(2,1)S(1)}, u32[]{:S(2)}, u32[]{:S(2)}) collective-permute-start(bf16[240,384]{1,0:T(8,128)(2,1)S(1)} %collective-permute-done.61.rest_2_), channel_id=1, source_target_pairs={{0,4},{4,0},{8,12},{12,8},{16,20},{20,16},{24,28},{28,24},{1,5},{5... | collective-permute-start | bytes 552968 | tf_op jit(solution)/shard_map/ppermute | solution.py:880
  457.8 6.9 %collective-permute-start.73 = (bf16[240,640]{1,0:T(8,128)(2,1)S(1)}, bf16[240,640]{1,0:T(8,128)(2,1)S(1)}, u32[]{:S(2)}, u32[]{:S(2)}) collective-permute-start(bf16[240,640]{1,0:T(8,128)(2,1)S(1)} %collective-permute-done.69.rest_3_), channel_id=1, source_target_pairs={{0,4},{4,0},{8,12},{12,8},{16,20},{20,16},{24,28},{28,24},{1,5},{5... | collective-permute-start | bytes 921608 | tf_op jit(solution)/shard_map/ppermute | solution.py:880
  464.6 8.3 %collective-permute-start.78 = (bf16[120,640]{1,0:T(8,128)(2,1)S(1)}, bf16[120,640]{1,0:T(8,128)(2,1)S(1)}, u32[]{:S(2)}, u32[]{:S(2)}) collective-permute-start(bf16[120,640]{1,0:T(8,128)(2,1)S(1)} %sum_two.5.rest_8_.rest_0_), channel_id=1, source_target_pairs={{0,4},{4,0},{8,12},{12,8},{16,20},{20,16},{24,28},{28,24},{1,5},{5... | collective-permute-start | bytes 460808 | tf_op jit(solution)/shard_map/ppermute | solution.py:880
  464.7 8.1 %collective-permute-start.81 = (bf16[120,640]{1,0:T(8,128)(2,1)S(1)}, bf16[120,640]{1,0:T(8,128)(2,1)S(1)}, u32[]{:S(2)}, u32[]{:S(2)}) collective-permute-start(bf16[120,640]{1,0:T(8,128)(2,1)S(1)} %collective-permute-done.77.rest_3_), channel_id=1, source_target_pairs={{0,4},{4,0},{8,12},{12,8},{16,20},{20,16},{24,28},{28,24},{1,5},{5... | collective-permute-start | bytes 460808 | tf_op jit(solution)/shard_map/ppermute | solution.py:880
  465.1 7.7 %collective-permute-start.80 = (bf16[120,640]{1,0:T(8,128)(2,1)S(1)}, bf16[120,640]{1,0:T(8,128)(2,1)S(1)}, u32[]{:S(2)}, u32[]{:S(2)}) collective-permute-start(bf16[120,640]{1,0:T(8,128)(2,1)S(1)} %collective-permute-done.76.rest_2_), channel_id=1, source_target_pairs={{0,4},{4,0},{8,12},{12,8},{16,20},{20,16},{24,28},{28,24},{1,5},{5... | collective-permute-start | bytes 460808 | tf_op jit(solution)/shard_map/ppermute | solution.py:880
  465.2 7.6 %collective-permute-start.79 = (bf16[120,640]{1,0:T(8,128)(2,1)S(1)}, bf16[120,640]{1,0:T(8,128)(2,1)S(1)}, u32[]{:S(2)}, u32[]{:S(2)}) collective-permute-start(bf16[120,640]{1,0:T(8,128)(2,1)S(1)} %collective-permute-done.75.rest_1_), channel_id=1, source_target_pairs={{0,4},{4,0},{8,12},{12,8},{16,20},{20,16},{24,28},{28,24},{1,5},{5... | collective-permute-start | bytes 460808 | tf_op jit(solution)/shard_map/ppermute | solution.py:880
  (106 other events, 1015.5 us)

commit v13 on v12

--- a/solution.py
+++ b/solution.py
@@ -39,11 +39,18 @@
     return 0, 1 + core, 2 - core, 3
 
 
-def fetch(mine, other, kept, sems, core, chip):
-    for kind, pieces in ((core, mine), (1 - core, other)):
-        for who, piece in zip(whose(kind), pieces):
-            at = chip ^ who
-            pltpu.make_async_copy(piece, kept.at[kind, at], sems.at[kind, at]).start()
+def fetch(mine, other, kept, sems, core, chip, only=None, turns=range(4)):
+    for j in turns:
+        for kind, pieces in ((core, mine), (1 - core, other)):
+            at = chip ^ whose(kind)[j]
+
+            def copy():
+                pltpu.make_async_copy(pieces[j], kept.at[kind, at], sems.at[kind, at]).start()
+
+            if only is None:
+                copy()
+            else:
+                pl.when(kind == only)(copy)
 
 
 def arrived(kept, sems, *at):
@@ -238,15 +245,11 @@
     return jnp.minimum((kind * 4 + chip) * ROWS, width - ROWS)
 
 
-def fetch_ffn(mine, other, wb, wd, sem_b, sem_d, core, chip):
+def fetch_down(mine, other, wb, wd, sem_d, core, chip):
     rows, width = wb.shape[3], wd.shape[1]
     last = width % ROWS
     for kind, pieces in ((core, mine), (1 - core, other)):
         for who, piece in zip(whose(kind), pieces):
-            at = chip ^ who
-            pltpu.make_async_copy(piece.at[:, :rows], wb.at[kind, at], sem_b.at[kind, at]).start()
-    for kind, pieces in ((core, mine), (1 - core, other)):
-        for who, piece in zip(whose(kind), pieces):
             at = kind * 4 + (chip ^ who)
 
             @pl.when(at < width // ROWS)
@@ -257,6 +260,11 @@
             @pl.when(at == width // ROWS)
             def _():
                 pltpu.make_async_copy(piece.at[:, rows + ROWS - last :], wd.at[:, width - last :], sem_d).start()
+
+
+def fetch_both(mine, other, wb, sem_b, core, chip, turns=range(4)):
+    rows = wb.shape[3]
+    fetch([p.at[:, :rows] for p in mine], [p.at[:, :rows] for p in other], wb, sem_b, core, chip, turns=turns)
 
 
 def whole(wb, c, m):
@@ -284,8 +292,12 @@
     more, rest = rest[7 : 7 + (0 if last else 3)], rest[7 + (0 if last else 3) :]
     wa, sem_a, wb, sem_b, wd, sem_d = rest
     core, chip = sc[0], sc[1]
-    fetch(mine_a, other_a, wa, sem_a, core, chip)
-    fetch_ffn(mine_b, other_b, wb, wd, sem_b, sem_d, core, chip)
+    fetch(mine_a, other_a, wa, sem_a, core, chip, 1)
+    fetch_both(mine_b, other_b, wb, sem_b, core, chip, (0, 1))
+    fetch_down(mine_b, other_b, wb, wd, sem_d, core, chip)
+    fetch_both(mine_b, other_b, wb, sem_b, core, chip, (2, 3))
+    if not last:
+        fetch(mine_a, other_a, wa, sem_a, core, chip, 0)
     o = ot_ref[...].T
     o_ref[...] = o
     for m in range(1, 4):
@@ -296,8 +308,9 @@
     b_ref[...] = b
     n = wb.shape[4]
     total = h1
-    for m in range(4):
-        cols = slice(m * n, (m + 1) * n)
+    for i in range(4):
+        m = chip ^ i
+        cols = pl.ds(pl.multiple_of(m * n, 128), n)
         arrived(wb, sem_b, 0, m)
         gate = nn(b, whole(wb, 0, m))
         arrived(wb, sem_b, 1, m)
@@ -306,14 +319,12 @@
         up_ref[:, cols] = up.astype(bf16)
         z = (gate / (1.0 + jnp.exp(-gate)) * up).astype(bf16)
         z_ref[:, cols] = z
-        if m == 0:
+        if i == 0:
             arrived_down(wd, sem_d)
         total = total + nt(z, wd[m])
     next_ref[...] = total.astype(bf16).T if last else total
     if last:
         arrived(wa, sem_a, 1, 0)
-        for m in range(4):
-            arrived(wa, sem_a, 0, m)
     else:
         project(total, gain_a, cos_ref, sin_ref, ids_ref[2 * KVW :, :], wa, sem_a, *more)
 
@@ -337,7 +348,7 @@
     )(sc, ot, h, gain, gain_a, cos, sin, *wa[0], *wa[1], *wb[0], *wb[1], kv, *after)
 
 
-def ffn_back(state, core, refs, weights):
+def ffn_back(state, core, chip, refs, weights):
     gate_ref, up_ref, h1_ref, gain_ref, gb_ref, keep_ref, send_ref, g1_ref, p_ref, dgain_ref, do_ref = refs
     wa, sem_a, wb, sem_b, wd, sem_d = weights
     gb = state.astype(bf16)
@@ -346,8 +357,9 @@
     first = core == 0
     arrived_down(wd, sem_d)
     db = None
-    for m in range(4):
-        cols = slice(m * n, (m + 1) * n)
+    for i in range(4):
+        m = chip ^ i
+        cols = pl.ds(pl.multiple_of(m * n, 128), n)
         dz = nn(gb, wd[m])
         gate, up = gate_ref[:, cols].astype(f32), up_ref[:, cols].astype(f32)
         sig = 1.0 / (1.0 + jnp.exp(-gate))
@@ -359,7 +371,7 @@
         part = nt(dgate, whole(wb, 0, m))
         arrived(wb, sem_b, 1, m)
         part = part + nt(dup, whole(wb, 1, m))
-        db = part if m == 0 else db + part
+        db = part if i == 0 else db + part
     dx, dgain = norm_back(h1_ref[...], gain_ref[...], db)
     dgain_ref[...] = dgain
     g1 = state + dx
@@ -431,10 +443,15 @@
     else:
         outs = take(7)
     wa, sem_a = take(2)
-    fetch(mine_a, other_a, wa, sem_a, core, chip)
+    if not start:
+        fetch(mine_a, other_a, wa, sem_a, core, chip, 0)
+        fetch(mine_a, other_a, wa, sem_a, core, chip, 1)
     if not end:
         wb, sem_b, wd, sem_d = take(4)
-        fetch_ffn(mine_b, other_b, wb, wd, sem_b, sem_d, core, chip)
+        fetch_down(mine_b, other_b, wb, wd, sem_d, core, chip)
+        fetch_both(mine_b, other_b, wb, sem_b, core, chip)
+    if start:
+        fetch(mine_a, other_a, wa, sem_a, core, chip, 1)
     if start:
         state = g_ref[...].T.astype(f32)
     else:
@@ -448,9 +465,9 @@
         g_out[width:, :] = state.astype(bf16).T
         finish_a(wa, sem_a, (1, 1), (1, 2), (1, 3))
     else:
-        ffn_back(state, core, (*ins, *outs), (wa, sem_a, wb, sem_b, wd, sem_d))
+        ffn_back(state, core, chip, (*ins, *outs), (wa, sem_a, wb, sem_b, wd, sem_d))
         if start:
-            finish_a(wa, sem_a, (1, 0), (0, 0), (0, 1), (0, 2), (0, 3))
+            finish_a(wa, sem_a, (1, 0))
 
 
 def back(start, end, sc, weights, tail, ffn, after=()):
@@ -1015,25 +1032,25 @@
     got_b = flip_z(send_b, 1)
     *later_a, own_a = sum_first(sc, keep_a, got_a, [ring_b], 2)
     more_a = [flip(v, BACK, SIDE) for v in later_a]
-    send_d, keep_d = down_split(sc, keep_d, got_d, [own_a])
-    got_d = flip(send_d, SIDE, BACK)
-    send_b, ring_b = sum_third(sc, ring_b, got_b, [send_d])
+    send_b, ring_b = sum_third(sc, ring_b, got_b, [own_a])
     got_b = flip_z(send_b, 2)
     send_a, ring_a = sum_second(sc, own_a, more_a, [send_b])
     got_a = flip_z(send_a, 1)
-    piece_b = over_groups(sum_two(sc, ring_b, got_b, [send_a]))
+    send_d, keep_d = down_split(sc, keep_d, got_d, [send_a])
+    got_d = flip(send_d, SIDE, BACK)
+    later_d, own_d = sum_first(sc, keep_d, [got_d], [send_d])
+    more_d = flip(later_d, BACK, SIDE)
+    piece_b = over_groups(sum_two(sc, ring_b, got_b, [later_d]))
     all_b = spread(piece_b)
     send_a, ring_a = sum_third(sc, ring_a, got_a, [piece_b])
     got_a = flip_z(send_a, 2)
-    later_d, own_d = sum_first(sc, keep_d, [got_d], [send_a])
-    more_d = flip(later_d, BACK, SIDE)
-    piece_a = over_groups(sum_two(sc, ring_a, got_a, [later_d]))
+    piece_d = over_groups(sum_two(sc, own_d, more_d, [send_a]))
+    all_d = spread(piece_d)
+    piece_a = over_groups(sum_two(sc, ring_a, got_a, [piece_d]))
     all_a = spread(piece_a)
-    piece_d = over_groups(sum_two(sc, own_d, more_d, [piece_a]))
-    grad_gate, grad_up = lay(sc, all_b, across(all_b), (gate_weight.shape[1],) * 2, [piece_d])
-    all_d = spread(piece_d)
-    grad_query, grad_key, grad_value, grad_out, dgains = lay(sc, all_a, across(all_a), (width, KVW, KVW, width), [grad_gate])
-    grad_down_ = lay_down(sc, all_d, across(all_d), [grad_query])
+    grad_gate, grad_up = lay(sc, all_b, across(all_b), (gate_weight.shape[1],) * 2, [piece_a])
+    grad_down_ = lay_down(sc, all_d, across(all_d), [grad_gate])
+    grad_query, grad_key, grad_value, grad_out, dgains = lay(sc, all_a, across(all_a), (width, KVW, KVW, width), [grad_down_])
     leaving = home_to_work(hold(leaving, [piece_b]), back=True)
     output, grad_tokens = leaving[:width].T, leaving[width:].astype(f32).T
     return (output[None], grad_tokens[None], dgains[0], grad_query, grad_key, grad_value, grad_out, dgains[1], grad_gate, grad_up, grad_down_.T)

time: 485 us -> 468 us (0.965)
  waiting for transfers between devices: 153 us -> 138 us
  Pallas kernels: 198 us -> 193 us
    ppermute x63, waiting for transfers between devices: 72.6 us -> 61.4 us  [flip(): lax.ppermute(value, 'dp', [(i, i ^ bits[i & 1]) for i in range(count)])]
  transfers between devices with their start and end apart: 82 -> 82, of which waited for: 36 -> 35; matrix products, arithmetic and copies ran while one was open for 1% -> 1% of each run, Pallas kernels for 25% -> 26%
where the time goes in v13:
time: 468 us; the launch traced here: 463 us
  Pallas kernels  193 us (41%)
  waiting for transfers between devices  138 us (29%)
  starting transfers between devices  92 us (20%)
  local copies, waits for them, and re-layouts  35.1 us (8%)
    ppermute x63, waiting for transfers between devices, flip(): lax.ppermute(value, 'dp', [(i, i ^ bits[i & 1]) for i in range(count)])  61.4 us
    ppermute x12, waiting for transfers between devices, flip_z(): return lax.ppermute(value, ('dp', 'fsdp'), pairs)  56.4 us
    ppermute x63, starting transfers between devices, flip(): lax.ppermute(value, 'dp', [(i, i ^ bits[i & 1]) for i in range(count)])  47.8 us
    pallas_call x3, Pallas kernels, back(): pl.pallas_call(functools.partial(back_kernel, start, end, len(after)), ou...  46.9 us
    pallas_call x2, Pallas kernels, post(): pl.pallas_call(functools.partial(post_kernel, last, len(after)), out_shap...  35.6 us
    unnamed x178, local copies, waits for them, and re-layouts  32.4 us
    ppermute x12, starting transfers between devices, flip_z(): return lax.ppermute(value, ('dp', 'fsdp'), pairs)  26.4 us
    pallas_call x2, Pallas kernels, attend_back(): pl.pallas_call(attend_back_kernel, out_shape=(shape((3, n, PIECE), bf16),...  25.3 us
  transfers between devices with their start and end apart: 82, of which 35 were waited for; matrix products, arithmetic and copies ran while one was open for 1% of the time, Pallas kernels for 26%

profile of v13, /device:TPU:0, one launch (start us, length us, event | category | flops | bytes accessed | tf_op | source)
XLA Modules:
  0.0 463.0 jit_solution(2029185201681148419)
XLA Ops:
  6.8 4.1 collective-permute-start.1
  10.9 1.6 collective-permute-start
  12.5 7.2 %collective-permute-done.1.rest_2_ = bf16[240,384]{1,0:T(8,128)(2,1)S(1)} collective-permute-done((bf16[240,384]{1,0:T(8,128)(2,1)S(1)}, bf16[240,384]{1,0:T(8,128)(2,1)S(1)}, u32[]{:S(2)}, u32[]{:S(2)}) %collective-permute-start.1) | collective-permute-done | bytes 184352 | tf_op jit(solution)/shard_map/ppermute | solution.py:903
  23.7 1.8 collective-permute-done.2.rest_3_
  25.5 1.5 stack.30.first_ref
  28.3 1.5 collective-permute-start.4
  29.9 3.2 collective-permute-start.11
  33.1 1.7 collective-permute-start.10
  34.8 11.8 %collective-permute-done.3.refs_1_.rest_1_ = bf16[960,384]{1,0:T(8,128)(2,1)} collective-permute-done((bf16[960,384]{1,0:T(8,128)(2,1)S(1)}, bf16[960,384]{1,0:T(8,128)(2,1)}, u32[]{:S(2)}, u32[]{:S(2)}) %collective-permute-start.3) | collective-permute-done | bytes 737312 | tf_op jit(solution)/shard_map/ppermute | solution.py:897
  46.8 6.4 %collective-permute-done.11.refs_0_ = bf16[368,640]{1,0:T(8,128)(2,1)S(1)} collective-permute-done((bf16[368,640]{1,0:T(8,128)(2,1)S(1)}, bf16[368,640]{1,0:T(8,128)(2,1)S(1)}, u32[]{:S(2)}, u32[]{:S(2)}) %collective-permute-start.11) | collective-permute-done | bytes 471072 | tf_op jit(solution)/shard_map/ppermute | solution.py:903
  54.9 10.0 %collective-permute-done.12.rest_3_ = bf16[368,640]{1,0:T(8,128)(2,1)S(1)} collective-permute-done((bf16[368,640]{1,0:T(8,128)(2,1)S(1)}, bf16[368,640]{1,0:T(8,128)(2,1)S(1)}, u32[]{:S(2)}, u32[]{:S(2)}) %collective-permute-start.12) | collective-permute-done | bytes 471072 | tf_op jit(solution)/shard_map/ppermute | solution.py:903
  65.0 3.0 stack.31.rest_8_
  69.9 4.6 collective-permute-start.8
  74.5 5.9 %collective-permute-start.7 = (bf16[960,384]{1,0:T(8,128)(2,1)}, bf16[960,384]{1,0:T(8,128)(2,1)}, u32[]{:S(2)}, u32[]{:S(2)}) collective-permute-start(bf16[960,384]{1,0:T(8,128)(2,1)} %collective-permute-done.3.refs_1_.rest_1_), channel_id=1, source_target_pairs={{0,4},{4,0},{8,12},{12,8},{16,20},{20,16},{24,28},{28,24},{1,5},{5... | collective-permute-start | bytes 2211848 | tf_op jit(solution)/shard_map/ppermute | solution.py:897
  84.0 7.5 %pre.1 = (bf16[256,960]{1,0:T(8,128)(2,1)}, bf16[256,960]{1,0:T(8,128)(2,1)}, bf16[960,256]{1,0:T(8,128)(2,1)}, bf16[656,256]{1,0:T(8,128)(2,1)}) custom-call(s32[3]{0:T(128)} %copy-done.49, bf16[976,256]{1,0:T(8,128)(2,1)} %copy-done.80, f32[1,960]{1,0:T(1,128)} %get-tuple-element.207.gain_ref.gain_a.rest_22_.rest_14_, ...), custom_call_target="tpu_custom_call" | custom-call | flops 1024 | bytes 1024 | tf_op jit(solution)/shard_map/pre/pallas_call | solution.py:126
  91.5 9.3 %collective-permute-start.15 = (bf16[656,256]{1,0:T(8,128)(2,1)}, bf16[656,256]{1,0:T(8,128)(2,1)S(1)}, u32[]{:S(2)}, u32[]{:S(2)}) collective-permute-start(bf16[656,256]{1,0:T(8,128)(2,1)} %get-tuple-element.102.kv2.rest_16_), channel_id=1, source_target_pairs={{0,1},{2,3},{4,5},{6,7},{8,9},{10,11},{12,13},{14,15},{16,17},{18,... | collective-permute-start | bytes 1007624 | tf_op jit(solution)/shard_map/ppermute | solution.py:936
  100.8 7.8 %collective-permute-done.15.refs_1_.kv0 = bf16[656,256]{1,0:T(8,128)(2,1)S(1)} collective-permute-done((bf16[656,256]{1,0:T(8,128)(2,1)}, bf16[656,256]{1,0:T(8,128)(2,1)S(1)}, u32[]{:S(2)}, u32[]{:S(2)}) %collective-permute-start.15) | collective-permute-done | bytes 335904 | tf_op jit(solution)/shard_map/ppermute | solution.py:936
  111.6 10.1 %attend.2 = (bf16[960,256]{1,0:T(8,128)(2,1)S(1)}, f32[15,256]{1,0:T(8,128)S(1)}) custom-call(bf16[960,256]{1,0:T(8,128)(2,1)S(1)} %copy-done.30, bf16[656,256]{1,0:T(8,128)(2,1)S(1)} %collective-permute-done.15.refs_1_.kv0, bf16[656,256]{1,0:T(8,128)(2,1)S(1)} %collective-permute-done.18.kv1, bf16[656,256]{1,0:T(8,128)(2,1)S(1)} %copy-done.6), custom_call_target="tpu_custom_call" | custom-call | flops 1024 | bytes 1024 | tf_op jit(solution)/shard_map/attend/pallas_call | solution.py:179
  122.3 11.0 %collective-permute-done.17.refs_0_ = bf16[4,368,640]{2,1,0:T(8,128)(2,1)} collective-permute-done((bf16[4,368,640]{2,1,0:T(8,128)(2,1)}, bf16[4,368,640]{2,1,0:T(8,128)(2,1)}, u32[]{:S(2)}, u32[]{:S(2)}) %collective-permute-start.17) | collective-permute-done | bytes 1884192 | tf_op jit(solution)/shard_map/ppermute | solution.py:897
  134.8 2.8 collective-permute-done.22.rest_15_
  137.6 18.2 %post.2 = (bf16[256,960]{1,0:T(8,128)(2,1)}, f32[256,960]{1,0:T(8,128)}, bf16[256,960]{1,0:T(8,128)(2,1)}, bf16[256,2560]{1,0:T(8,128)(2,1)}, bf16[256,2560]{1,0...) custom-call(s32[3]{0:T(128)} %copy-done.49, ...), custom_call_target="tpu_custom_call" | custom-call | flops 1024 | bytes 1024 | tf_op jit(solution)/shard_map/post/pallas_call | solution.py:339
  156.0 3.8 collective-permute-start.24
  160.7 5.9 %collective-permute-start.27 = (bf16[256,960]{1,0:T(8,128)(2,1)}, bf16[256,960]{1,0:T(8,128)(2,1)S(1)}, u32[]{:S(2)}, u32[]{:S(2)}) collective-permute-start(bf16[256,960]{1,0:T(8,128)(2,1)} %get-tuple-element.109.rest_1_), channel_id=1, source_target_pairs={{0,4},{4,0},{8,12},{12,8},{16,20},{20,16},{24,28},{28,24},{1,5},{5... | collective-permute-start | bytes 1474568 | tf_op jit(solution)/shard_map/ppermute | solution.py:897
  166.6 1.8 collective-permute-done.24.kv0
  172.3 10.5 %attend.3 = (bf16[960,256]{1,0:T(8,128)(2,1)S(1)}, f32[15,256]{1,0:T(8,128)S(1)}) custom-call(bf16[960,256]{1,0:T(8,128)(2,1)S(1)} %copy-done.29, bf16[656,256]{1,0:T(8,128)(2,1)S(1)} %collective-permute-done.24.kv0, bf16[656,256]{1,0:T(8,128)(2,1)S(1)} %collective-permute-done.25.kv1, bf16[656,256]{1,0:T(8,128)(2,1)S(1)} %copy-done.4, ...), custom_call_target="tpu_custom_call" | custom-call | flops 1024 | bytes 1024 | tf_op jit(solution)/shard_map/attend/pallas_call | solution.py:179
  184.5 17.4 %post.3 = (bf16[256,960]{1,0:T(8,128)(2,1)}, f32[256,960]{1,0:T(8,128)}, bf16[256,960]{1,0:T(8,128)(2,1)}, bf16[256,2560]{1,0:T(8,128)(2,1)}, bf16[256,2560]{1,0...) custom-call(s32[3]{0:T(128)} %copy-done.49, bf16[960,256]{1,0:T(8,128)(2,1)} %copy-done.55, ...), custom_call_target="tpu_custom_call" | custom-call | flops 1024 | bytes 1024 | tf_op jit(solution)/shard_map/post/pallas_call | solution.py:339
  202.1 19.1 %back_start.1 = (bf16[256,960]{1,0:T(8,128)(2,1)}, bf16[256,2560]{1,0:T(8,128)(2,1)}, bf16[256,2560]{1,0:T(8,128)(2,1)}, f32[256,960]{1,0:T(8,128)}, bf16[3,256,...) custom-call(s32[3]{0:T(128)} %copy-done.49, bf16[960,384]{1,0:T(8,128)(2,1)} %bitcast.30, ...), custom_call_target="tpu_custom_call" | custom-call | flops 1024 | bytes 1024 | tf_op jit(solution)/shard_map/back_start/pallas_call | solution.py:500
  222.4 2.7 collective-permute-done.30.rest_0_.rest_2_
  226.8 1.5 copy-done.15
  229.3 12.6 %attend_back.2 = (bf16[3,256,384]{2,1,0:T(8,128)(2,1)S(1)}, bf16[3,256,384]{2,1,0:T(8,128)(2,1)S(1)}, f32[640,256]{1,0:T(8,128)S(1)}, bf16[640,256]{1,0:T(8,128)(2,1)S(1)}, f32[640,256]{1,0:T(8,128)S(1)}) custom-call(s32[3]{0:T(128)S(1)} %copy-done.50, bf16[3,256,384]{2,1,0:T(8,128)(2,1)S(1)} %copy-done.15, bf16[960,256]{1,0:T(8,128)(2,1)S(1)} %copy-done.29, ...), custom_call_target="tpu_custom_call" | custom-call | flops 1024 | bytes 1024 | tf_op jit(solution)/shard_map/attend_back/pallas_call | solution.py:232
  246.5 10.5 %collective-permute-done.35.rest_20_ = bf16[640,256]{1,0:T(8,128)(2,1)S(1)} collective-permute-done((bf16[640,256]{1,0:T(8,128)(2,1)S(1)}, bf16[640,256]{1,0:T(8,128)(2,1)S(1)}, u32[]{:S(2)}, u32[]{:S(2)}) %collective-permute-start.35) | collective-permute-done | bytes 327712 | tf_op jit(solution)/shard_map/ppermute | solution.py:945
  257.7 20.8 %back_join.1 = (bf16[256,384]{1,0:T(8,128)(2,1)}, bf16[256,384]{1,0:T(8,128)(2,1)}, bf16[256,384]{1,0:T(8,128)(2,1)}, f32[1,960]{1,0:T(1,128)}, bf16[256,960]{1,...) custom-call(s32[3]{0:T(128)} %copy-done.49, ...), custom_call_target="tpu_custom_call" | custom-call | flops 1024 | bytes 1024 | tf_op jit(solution)/shard_map/back_join/pallas_call | solution.py:500
  278.6 3.2 collective-permute-done.40.rest_7_
  283.0 11.5 %grad_ffn.1 = (bf16[2,960,640]{2,1,0:T(8,128)(2,1)}, bf16[2,960,640]{2,1,0:T(8,128)(2,1)}) custom-call(s32[3]{0:T(128)} %copy-done.49, bf16[256,960]{1,0:T(8,128)(2,1)} %get-tuple-element.122.rest_0_, bf16[256,960]{1,0:T(8,128)(2,1)} %get-tuple-element.109.rest_1_, bf16[256,960]{1,0:T(8,128)(2,1)} %copy-done.28, bf16[256,960]{1,0:T(8,128)(2,1)} %copy-done.27, ...), custom_call_target="tpu_custom_call" | custom-call | flops 1024 | bytes 1024 | tf_op jit(solution)/shard_map/grad_ffn/pallas_call | solution.py:541
  294.5 1.5 collective-permute-start.44
  296.0 1.4 collective-permute-done.39.rest_0_.rest_18_
  297.5 1.7 copy-done.12
  299.2 12.6 %attend_back.3 = (bf16[3,256,384]{2,1,0:T(8,128)(2,1)S(1)}, bf16[3,256,384]{2,1,0:T(8,128)(2,1)S(1)}, f32[640,256]{1,0:T(8,128)S(1)}, bf16[640,256]{1,0:T(8,128)(2,1)S(1)}, f32[640,256]{1,0:T(8,128)S(1)}) custom-call(s32[3]{0:T(128)S(1)} %copy-done.51, bf16[3,256,384]{2,1,0:T(8,128)(2,1)S(1)} %copy-done.16, bf16[960,256]{1,0:T(8,128)(2,1)S(1)} %copy-done.31, ...), custom_call_target="tpu_custom_call" | custom-call | flops 1024 | bytes 1024 | tf_op jit(solution)/shard_map/attend_back/pallas_call | solution.py:232
  318.0 8.2 %grad_down.1 = (bf16[2,480,640]{2,1,0:T(8,128)(2,1)}, bf16[2,480,640]{2,1,0:T(8,128)(2,1)}) custom-call(s32[3]{0:T(128)} %copy-done.49, bf16[256,960]{1,0:T(8,128)(2,1)} %get-tuple-element.133.rest_0_, bf16[256,960]{1,0:T(8,128)(2,1)} %get-tuple-element.149.rest_1_, bf16[256,960]{1,0:T(8,128)(2,1)} %copy-done.69, bf16[256,960]{1,0:T(8,128)(2,1)} %copy-done.79, ...), custom_call_target="tpu_custom_call" | custom-call | flops 1024 | bytes 1024 | tf_op jit(solution)/shard_map/grad_down/pallas_call | solution.py:572
  326.1 2.7 collective-permute-start.46
  329.6 7.0 %back_end.1 = (bf16[256,384]{1,0:T(8,128)(2,1)}, bf16[256,384]{1,0:T(8,128)(2,1)}, bf16[256,384]{1,0:T(8,128)(2,1)}, f32[1,960]{1,0:T(1,128)}, bf16[1920,256]{1,0:T(8,128)(2,1)}) custom-call(s32[3]{0:T(128)} %copy-done.49, bf16[960,384]{1,0:T(8,128)(2,1)} %bitcast.32, bf16[960,384]{1,0:T(8,128)(2,1)} %collective-permute-done.3.refs_1_.rest_1_, ...), custom_call_target="tpu_custom_call" | custom-call | flops 1024 | bytes 1024 | tf_op jit(solution)/shard_map/back_end/pallas_call | solution.py:500
  337.5 2.1 sum_first.3
  342.7 1.5 collective-permute-done.47.rest_17_
  345.2 10.6 %grad_attention.1 = (bf16[960,384]{1,0:T(8,128)(2,1)}, bf16[960,384]{1,0:T(8,128)(2,1)}, bf16[2,960,384]{2,1,0:T(8,128)(2,1)}) custom-call(s32[3]{0:T(128)} %copy-done.49, bf16[256,960]{1,0:T(8,128)(2,1)} %get-tuple-element.121.rest_0_, bf16[256,960]{1,0:T(8,128)(2,1)} %get-tuple-element.108.rest_1_, bf16[256,960]{1,0:T(8,128)(2,1)} %copy-done.25, ...), custom_call_target="tpu_custom_call" | custom-call | flops 1024 | bytes 1024 | tf_op jit(solution)/shard_map/grad_attention/pallas_call | solution.py:623
  360.1 1.7 sum_third.3
  363.3 4.5 collective-permute-start.53
  367.8 7.6 %collective-permute-done.51.rest_1_ = bf16[960,384]{1,0:T(8,128)(2,1)S(1)} collective-permute-done((bf16[960,384]{1,0:T(8,128)(2,1)}, bf16[960,384]{1,0:T(8,128)(2,1)S(1)}, u32[]{:S(2)}, u32[]{:S(2)}) %collective-permute-start.51) | collective-permute-done | bytes 737312 | tf_op jit(solution)/shard_map/ppermute | solution.py:897
  378.4 14.0 %collective-permute-done.49.got_ref = bf16[2,240,640]{2,1,0:T(8,128)(2,1)S(1)} collective-permute-done((bf16[2,240,640]{2,1,0:T(8,128)(2,1)S(1)}, bf16[2,240,640]{2,1,0:T(8,128)(2,1)S(1)}, u32[]{:S(2)}, u32[]{:S(2)}) %collective-permute-start.49) | collective-permute-done | bytes 614432 | tf_op jit(solution)/shard_map/ppermute | solution.py:903
  395.5 5.7 %collective-permute-start.58 = (bf16[2,240,384]{2,1,0:T(8,128)(2,1)S(1)}, bf16[2,240,384]{2,1,0:T(8,128)(2,1)S(1)}, u32[]{:S(2)}, u32[]{:S(2)}) collective-permute-start(bf16[2,240,384]{2,1,0:T(8,128)(2,1)S(1)} %get-tuple-element.178.rest_0_), channel_id=1, source_target_pairs={{0,1},{1,0},{2,3},{3,2},{4,5},{5,4},{6,7},{7,6},{8,9},{9,8},{10,11... | collective-permute-start | bytes 1105928 | tf_op jit(solution)/shard_map/ppermute | solution.py:903
  403.0 8.3 %collective-permute-done.52.got_ref = bf16[240,640]{1,0:T(8,128)(2,1)S(1)} collective-permute-done((bf16[240,640]{1,0:T(8,128)(2,1)S(1)}, bf16[240,640]{1,0:T(8,128)(2,1)S(1)}, u32[]{:S(2)}, u32[]{:S(2)}) %collective-permute-start.52) | collective-permute-done | bytes 307232 | tf_op jit(solution)/shard_map/ppermute | solution.py:903
  412.0 1.6 collective-permute-start.77
  414.2 1.4 collective-permute-start.75
  417.5 8.4 %collective-permute-done.59.got_ref = bf16[240,384]{1,0:T(8,128)(2,1)S(1)} collective-permute-done((bf16[240,384]{1,0:T(8,128)(2,1)S(1)}, bf16[240,384]{1,0:T(8,128)(2,1)S(1)}, u32[]{:S(2)}, u32[]{:S(2)}) %collective-permute-start.59) | collective-permute-done | bytes 184352 | tf_op jit(solution)/shard_map/ppermute | solution.py:903
  425.9 1.5 collective-permute-start.70
  431.1 2.1 collective-permute-start.63
  434.8 2.0 collective-permute-done.69.rest_2_
  437.6 3.3 collective-permute-done.63.rest_3_
  440.9 3.4 collective-permute-done.62.rest_2_
  445.3 1.7 collective-permute-done.72.rest_5_
  448.0 3.1 lay.2
  451.1 1.7 copy-done.10
  452.8 2.3 lay_down.1.rest_8_
  455.2 1.7 copy-done.3
  456.9 2.4 lay.3
  (332 shorter events, 80.9 us)
Async XLA Ops:
  6.8 12.8 %collective-permute-start.1 = (bf16[240,384]{1,0:T(8,128)(2,1)S(1)}, bf16[240,384]{1,0:T(8,128)(2,1)S(1)}, u32[]{:S(2)}, u32[]{:S(2)}) collective-permute-start(bf16[240,384]{1,0:T(8,128)(2,1)S(1)} %pick_first.1.rest_0_), channel_id=1, source_target_pairs={{0,2},{1,3},{2,0},{3,1},{4,6},{5,7},{6,4},{7,5},{8,10},{9,11},{10,... | collective-permute-start | bytes 552968 | tf_op jit(solution)/shard_map/ppermute | solution.py:903
  10.9 9.4 %collective-permute-start = (bf16[240,384]{1,0:T(8,128)(2,1)S(1)}, bf16[240,384]{1,0:T(8,128)(2,1)S(1)}, u32[]{:S(2)}, u32[]{:S(2)}) collective-permute-start(bf16[240,384]{1,0:T(8,128)(2,1)S(1)} %pick_first.1.rest_0_), channel_id=1, source_target_pairs={{0,1},{1,0},{2,3},{3,2},{4,5},{5,4},{6,7},{7,6},{8,9},{9,8},{10,11... | collective-permute-start | bytes 552968 | tf_op jit(solution)/shard_map/ppermute | solution.py:903
  19.7 5.8 %collective-permute-start.2 = (bf16[240,384]{1,0:T(8,128)(2,1)S(1)}, bf16[240,384]{1,0:T(8,128)(2,1)S(1)}, u32[]{:S(2)}, u32[]{:S(2)}) collective-permute-start(bf16[240,384]{1,0:T(8,128)(2,1)S(1)} %collective-permute-done.1.rest_2_), channel_id=1, source_target_pairs={{0,1},{1,0},{2,3},{3,2},{4,5},{5,4},{6,7},{7,6},{8,9},{9,8},{10,11... | collective-permute-start | bytes 552968 | tf_op jit(solution)/shard_map/ppermute | solution.py:903
  27.1 19.6 %collective-permute-start.3 = (bf16[960,384]{1,0:T(8,128)(2,1)S(1)}, bf16[960,384]{1,0:T(8,128)(2,1)}, u32[]{:S(2)}, u32[]{:S(2)}) collective-permute-start(bf16[960,384]{1,0:T(8,128)(2,1)S(1)} %bitcast.24), channel_id=1, source_target_pairs={{0,8},{4,20},{8,0},{12,28},{16,24},{20,4},{24,16},{28,12},{1,9},{5... | collective-permute-start | bytes 2211848 | tf_op jit(solution)/shard_map/ppermute | solution.py:897
  28.3 25.2 %collective-permute-start.4 = (bf16[960,384]{1,0:T(8,128)(2,1)S(1)}, bf16[960,384]{1,0:T(8,128)(2,1)}, u32[]{:S(2)}, u32[]{:S(2)}) collective-permute-start(bf16[960,384]{1,0:T(8,128)(2,1)S(1)} %bitcast.25), channel_id=1, source_target_pairs={{0,16},{4,12},{8,24},{12,4},{16,0},{20,28},{24,8},{28,20},{1,17},{... | collective-permute-start | bytes 2211848 | tf_op jit(solution)/shard_map/ppermute | solution.py:897
  29.9 23.3 %collective-permute-start.11 = (bf16[368,640]{1,0:T(8,128)(2,1)S(1)}, bf16[368,640]{1,0:T(8,128)(2,1)S(1)}, u32[]{:S(2)}, u32[]{:S(2)}) collective-permute-start(bf16[368,640]{1,0:T(8,128)(2,1)S(1)} %pick.1.rest_4_.rest_0_), channel_id=1, source_target_pairs={{0,2},{1,3},{2,0},{3,1},{4,6},{5,7},{6,4},{7,5},{8,10},{9,11},{10,... | collective-permute-start | bytes 1413128 | tf_op jit(solution)/shard_map/ppermute | solution.py:903
  33.1 20.4 %collective-permute-start.10 = (bf16[368,640]{1,0:T(8,128)(2,1)S(1)}, bf16[368,640]{1,0:T(8,128)(2,1)S(1)}, u32[]{:S(2)}, u32[]{:S(2)}) collective-permute-start(bf16[368,640]{1,0:T(8,128)(2,1)S(1)} %pick.1.rest_4_.rest_0_), channel_id=1, source_target_pairs={{0,1},{1,0},{2,3},{3,2},{4,5},{5,4},{6,7},{7,6},{8,9},{9,8},{10,11... | collective-permute-start | bytes 1413128 | tf_op jit(solution)/shard_map/ppermute | solution.py:903
  46.7 18.3 %collective-permute-start.5 = (bf16[960,384]{1,0:T(8,128)(2,1)}, bf16[960,384]{1,0:T(8,128)(2,1)S(1)}, u32[]{:S(2)}, u32[]{:S(2)}) collective-permute-start(bf16[960,384]{1,0:T(8,128)(2,1)} %collective-permute-done.3.refs_1_.rest_1_), channel_id=1, source_target_pairs={{0,16},{4,12},{8,24},{12,4},{16,0},{20,28},{24,8},{28,20},{1,17},{... | collective-permute-start | bytes 2211848 | tf_op jit(solution)/shard_map/ppermute | solution.py:897
  53.5 11.4 %collective-permute-start.12 = (bf16[368,640]{1,0:T(8,128)(2,1)S(1)}, bf16[368,640]{1,0:T(8,128)(2,1)S(1)}, u32[]{:S(2)}, u32[]{:S(2)}) collective-permute-start(bf16[368,640]{1,0:T(8,128)(2,1)S(1)} %hold.4.rest_2_), channel_id=1, source_target_pairs={{0,1},{1,0},{2,3},{3,2},{4,5},{5,4},{6,7},{7,6},{8,9},{9,8},{10,11... | collective-permute-start | bytes 1413128 | tf_op jit(solution)/shard_map/ppermute | solution.py:903
  67.9 41.3 %collective-permute-start.16 = (bf16[4,368,640]{2,1,0:T(8,128)(2,1)}, bf16[4,368,640]{2,1,0:T(8,128)(2,1)S(1)}, u32[]{:S(2)}, u32[]{:S(2)}) collective-permute-start(bf16[4,368,640]{2,1,0:T(8,128)(2,1)} %stack.31.rest_8_), channel_id=1, source_target_pairs={{0,16},{4,12},{8,24},{12,4},{16,0},{20,28},{24,8},{28,20},{1,17},{... | collective-permute-start | bytes 5652488 | tf_op jit(solution)/shard_map/ppermute | solution.py:897
  68.5 40.7 %collective-permute-start.13 = (bf16[4,368,640]{2,1,0:T(8,128)(2,1)}, bf16[4,368,640]{2,1,0:T(8,128)(2,1)}, u32[]{:S(2)}, u32[]{:S(2)}) collective-permute-start(bf16[4,368,640]{2,1,0:T(8,128)(2,1)} %stack.31.rest_8_), channel_id=1, source_target_pairs={{0,8},{4,20},{8,0},{12,28},{16,24},{20,4},{24,16},{28,12},{1,9},{5... | collective-permute-start | bytes 5652488 | tf_op jit(solution)/shard_map/ppermute | solution.py:897
  69.1 11.2 %collective-permute-start.6 = (bf16[960,384]{1,0:T(8,128)(2,1)S(1)}, bf16[960,384]{1,0:T(8,128)(2,1)S(1)}, u32[]{:S(2)}, u32[]{:S(2)}) collective-permute-start(bf16[960,384]{1,0:T(8,128)(2,1)S(1)} %bitcast.26), channel_id=1, source_target_pairs={{0,4},{4,0},{8,12},{12,8},{16,20},{20,16},{24,28},{28,24},{1,5},{5... | collective-permute-start | bytes 2211848 | tf_op jit(solution)/shard_map/ppermute | solution.py:897
  69.2 5.3 %collective-permute-start.14 = (bf16[976,256]{1,0:T(8,128)(2,1)S(1)}, bf16[976,256]{1,0:T(8,128)(2,1)S(1)}, u32[]{:S(2)}, u32[]{:S(2)}) collective-permute-start(bf16[976,256]{1,0:T(8,128)(2,1)S(1)} %pad_maximum_fusion), channel_id=1, source_target_pairs={{0,0},{1,4},{2,1},{3,5},{4,2},{5,6},{6,3},{7,7},{8,8},{9,12},{10,9... | collective-permute-start | bytes 1499144 | tf_op jit(solution)/shard_map/ppermute | solution.py:914
  69.9 14.1 %collective-permute-start.8 = (bf16[960,384]{1,0:T(8,128)(2,1)}, bf16[960,384]{1,0:T(8,128)(2,1)}, u32[]{:S(2)}, u32[]{:S(2)}) collective-permute-start(bf16[960,384]{1,0:T(8,128)(2,1)} %collective-permute-done.4.refs_2_.rest_2_), channel_id=1, source_target_pairs={{0,4},{4,0},{8,12},{12,8},{16,20},{20,16},{24,28},{28,24},{1,5},{5... | collective-permute-start | bytes 2211848 | tf_op jit(solution)/shard_map/ppermute | solution.py:897
  74.5 9.5 %collective-permute-start.7 = (bf16[960,384]{1,0:T(8,128)(2,1)}, bf16[960,384]{1,0:T(8,128)(2,1)}, u32[]{:S(2)}, u32[]{:S(2)}) collective-permute-start(bf16[960,384]{1,0:T(8,128)(2,1)} %collective-permute-done.3.refs_1_.rest_1_), channel_id=1, source_target_pairs={{0,4},{4,0},{8,12},{12,8},{16,20},{20,16},{24,28},{28,24},{1,5},{5... | collective-permute-start | bytes 2211848 | tf_op jit(solution)/shard_map/ppermute | solution.py:897
  91.5 17.2 %collective-permute-start.15 = (bf16[656,256]{1,0:T(8,128)(2,1)}, bf16[656,256]{1,0:T(8,128)(2,1)S(1)}, u32[]{:S(2)}, u32[]{:S(2)}) collective-permute-start(bf16[656,256]{1,0:T(8,128)(2,1)} %get-tuple-element.102.kv2.rest_16_), channel_id=1, source_target_pairs={{0,1},{2,3},{4,5},{6,7},{8,9},{10,11},{12,13},{14,15},{16,17},{18,... | collective-permute-start | bytes 1007624 | tf_op jit(solution)/shard_map/ppermute | solution.py:936
  109.2 24.1 %collective-permute-start.17 = (bf16[4,368,640]{2,1,0:T(8,128)(2,1)}, bf16[4,368,640]{2,1,0:T(8,128)(2,1)}, u32[]{:S(2)}, u32[]{:S(2)}) collective-permute-start(bf16[4,368,640]{2,1,0:T(8,128)(2,1)} %hold.5.rest_9_), channel_id=1, source_target_pairs={{0,16},{4,12},{8,24},{12,4},{16,0},{20,28},{24,8},{28,20},{1,17},{... | collective-permute-start | bytes 5652488 | tf_op jit(solution)/shard_map/ppermute | solution.py:897
  110.0 23.4 %collective-permute-start.19 = (bf16[4,368,640]{2,1,0:T(8,128)(2,1)}, bf16[4,368,640]{2,1,0:T(8,128)(2,1)S(1)}, u32[]{:S(2)}, u32[]{:S(2)}) collective-permute-start(bf16[4,368,640]{2,1,0:T(8,128)(2,1)} %stack.31.rest_8_), channel_id=1, source_target_pairs={{0,4},{4,0},{8,12},{12,8},{16,20},{20,16},{24,28},{28,24},{1,5},{5... | collective-permute-start | bytes 5652488 | tf_op jit(solution)/shard_map/ppermute | solution.py:897
  121.7 13.0 %collective-permute-start.20 = (bf16[4,368,640]{2,1,0:T(8,128)(2,1)}, bf16[4,368,640]{2,1,0:T(8,128)(2,1)}, u32[]{:S(2)}, u32[]{:S(2)}) collective-permute-start(bf16[4,368,640]{2,1,0:T(8,128)(2,1)} %hold.5.rest_9_), channel_id=1, source_target_pairs={{0,4},{4,0},{8,12},{12,8},{16,20},{20,16},{24,28},{28,24},{1,5},{5... | collective-permute-start | bytes 5652488 | tf_op jit(solution)/shard_map/ppermute | solution.py:897
  121.9 11.5 %collective-permute-start.21 = (bf16[4,368,640]{2,1,0:T(8,128)(2,1)S(1)}, bf16[4,368,640]{2,1,0:T(8,128)(2,1)S(1)}, u32[]{:S(2)}, u32[]{:S(2)}) collective-permute-start(bf16[4,368,640]{2,1,0:T(8,128)(2,1)S(1)} %collective-permute-done.16.refs_2_.rest_10_), channel_id=1, source_target_pairs={{0,4},{4,0},{8,12},{12,8},{16,20},{20,16},{24,28},{28,24},{1,5},{5... | collective-permute-start | bytes 5652488 | tf_op jit(solution)/shard_map/ppermute | solution.py:897
  133.4 4.2 collective-permute-start.22
  155.8 15.3 %collective-permute-start.29 = (bf16[256,2560]{1,0:T(8,128)(2,1)}, bf16[256,2560]{1,0:T(8,128)(2,1)S(1)}, u32[]{:S(2)}, u32[]{:S(2)}) collective-permute-start(bf16[256,2560]{1,0:T(8,128)(2,1)} %get-tuple-element.111.rest_5_), channel_id=1, source_target_pairs={{0,4},{4,0},{8,12},{12,8},{16,20},{20,16},{24,28},{28,24},{1,5},{5... | collective-permute-start | bytes 3932168 | tf_op jit(solution)/shard_map/ppermute | solution.py:897
  156.0 12.3 %collective-permute-start.24 = (bf16[656,256]{1,0:T(8,128)(2,1)}, bf16[656,256]{1,0:T(8,128)(2,1)S(1)}, u32[]{:S(2)}, u32[]{:S(2)}) collective-permute-start(bf16[656,256]{1,0:T(8,128)(2,1)} %get-tuple-element.107.kv2.rest_16_), channel_id=1, source_target_pairs={{0,1},{2,3},{4,5},{6,7},{8,9},{10,11},{12,13},{14,15},{16,17},{18,... | collective-permute-start | bytes 1007624 | tf_op jit(solution)/shard_map/ppermute | solution.py:936
  159.8 9.5 %collective-permute-start.26 = (bf16[256,960]{1,0:T(8,128)(2,1)S(1)}, bf16[256,960]{1,0:T(8,128)(2,1)S(1)}, u32[]{:S(2)}, u32[]{:S(2)}) collective-permute-start(bf16[256,960]{1,0:T(8,128)(2,1)S(1)} %copy-done.73), channel_id=1, source_target_pairs={{0,4},{4,0},{8,12},{12,8},{16,20},{20,16},{24,28},{28,24},{1,5},{5... | collective-permute-start | bytes 1474568 | tf_op jit(solution)/shard_map/ppermute | solution.py:897
  160.0 23.7 %collective-permute-start.23 = (bf16[960,256]{1,0:T(8,128)(2,1)S(1)}, bf16[960,256]{1,0:T(8,128)(2,1)S(1)}, u32[]{:S(2)}, u32[]{:S(2)}) collective-permute-start(bf16[960,256]{1,0:T(8,128)(2,1)S(1)} %bitcast.40), channel_id=1, source_target_pairs={{0,0},{1,4},{2,1},{3,5},{4,2},{5,6},{6,3},{7,7},{8,8},{9,12},{10,9... | collective-permute-start | bytes 1474568 | tf_op jit(solution)/shard_map/ppermute | solution.py:914
  160.7 8.8 %collective-permute-start.27 = (bf16[256,960]{1,0:T(8,128)(2,1)}, bf16[256,960]{1,0:T(8,128)(2,1)S(1)}, u32[]{:S(2)}, u32[]{:S(2)}) collective-permute-start(bf16[256,960]{1,0:T(8,128)(2,1)} %get-tuple-element.109.rest_1_), channel_id=1, source_target_pairs={{0,4},{4,0},{8,12},{12,8},{16,20},{20,16},{24,28},{28,24},{1,5},{5... | collective-permute-start | bytes 1474568 | tf_op jit(solution)/shard_map/ppermute | solution.py:897
  201.9 24.8 %collective-permute-start.33 = (bf16[256,2560]{1,0:T(8,128)(2,1)}, bf16[256,2560]{1,0:T(8,128)(2,1)S(1)}, u32[]{:S(2)}, u32[]{:S(2)}) collective-permute-start(bf16[256,2560]{1,0:T(8,128)(2,1)} %get-tuple-element.124.rest_4_), channel_id=1, source_target_pairs={{0,4},{4,0},{8,12},{12,8},{16,20},{20,16},{24,28},{28,24},{1,5},{5... | collective-permute-start | bytes 3932168 | tf_op jit(solution)/shard_map/ppermute | solution.py:897
  221.2 25.2 %collective-permute-start.38 = (bf16[256,2560]{1,0:T(8,128)(2,1)}, bf16[256,2560]{1,0:T(8,128)(2,1)S(1)}, u32[]{:S(2)}, u32[]{:S(2)}) collective-permute-start(bf16[256,2560]{1,0:T(8,128)(2,1)} %get-tuple-element.134), channel_id=1, source_target_pairs={{0,4},{4,0},{8,12},{12,8},{16,20},{20,16},{24,28},{28,24},{1,5},{5... | collective-permute-start | bytes 3932168 | tf_op jit(solution)/shard_map/ppermute | solution.py:897
  221.9 4.1 collective-permute-start.31
  222.3 4.4 collective-permute-start.32
  245.1 11.9 %collective-permute-start.35 = (bf16[640,256]{1,0:T(8,128)(2,1)S(1)}, bf16[640,256]{1,0:T(8,128)(2,1)S(1)}, u32[]{:S(2)}, u32[]{:S(2)}) collective-permute-start(bf16[640,256]{1,0:T(8,128)(2,1)S(1)} %far_sum.2), channel_id=1, source_target_pairs={{1,0},{3,2},{5,4},{7,6},{9,8},{11,10},{13,12},{15,14},{17,16},{19,... | collective-permute-start | bytes 983048 | tf_op jit(solution)/shard_map/ppermute | solution.py:945
  294.5 42.1 %collective-permute-start.44 = (bf16[2,960,640]{2,1,0:T(8,128)(2,1)}, bf16[2,960,640]{2,1,0:T(8,128)(2,1)S(1)}, u32[]{:S(2)}, u32[]{:S(2)}) collective-permute-start(bf16[2,960,640]{2,1,0:T(8,128)(2,1)} %get-tuple-element.143.rest_1_), channel_id=1, source_target_pairs={{0,8},{4,20},{8,0},{12,28},{16,24},{20,4},{24,16},{28,12},{1,9},{5... | collective-permute-start | bytes 7372808 | tf_op jit(solution)/shard_map/ppermute | solution.py:897
  315.8 13.0 %collective-permute-start.42 = (bf16[640,256]{1,0:T(8,128)(2,1)S(1)}, bf16[640,256]{1,0:T(8,128)(2,1)S(1)}, u32[]{:S(2)}, u32[]{:S(2)}) collective-permute-start(bf16[640,256]{1,0:T(8,128)(2,1)S(1)} %far_sum.3.rest_8_), channel_id=1, source_target_pairs={{1,0},{3,2},{5,4},{7,6},{9,8},{11,10},{13,12},{15,14},{17,16},{19,... | collective-permute-start | bytes 983048 | tf_op jit(solution)/shard_map/ppermute | solution.py:945
  326.1 31.7 %collective-permute-start.46 = (bf16[2,480,640]{2,1,0:T(8,128)(2,1)}, bf16[2,480,640]{2,1,0:T(8,128)(2,1)}, u32[]{:S(2)}, u32[]{:S(2)}) collective-permute-start(bf16[2,480,640]{2,1,0:T(8,128)(2,1)} %get-tuple-element.150.rest_18_), channel_id=1, source_target_pairs={{0,1},{1,0},{2,3},{3,2},{4,5},{5,4},{6,7},{7,6},{8,9},{9,8},{10,11... | collective-permute-start | bytes 3686408 | tf_op jit(solution)/shard_map/ppermute | solution.py:903
  341.1 20.8 %collective-permute-start.45 = (bf16[960,640]{1,0:T(8,128)(2,1)}, bf16[960,640]{1,0:T(8,128)(2,1)S(1)}, u32[]{:S(2)}, u32[]{:S(2)}) collective-permute-start(bf16[960,640]{1,0:T(8,128)(2,1)} %get-tuple-element.155.rest_24_), channel_id=1, source_target_pairs={{0,16},{4,12},{8,24},{12,4},{16,0},{20,28},{24,8},{28,20},{1,17},{... | collective-permute-start | bytes 3686408 | tf_op jit(solution)/shard_map/ppermute | solution.py:897
  355.8 12.1 %collective-permute-start.50 = (bf16[960,384]{1,0:T(8,128)(2,1)}, bf16[960,384]{1,0:T(8,128)(2,1)S(1)}, u32[]{:S(2)}, u32[]{:S(2)}) collective-permute-start(bf16[960,384]{1,0:T(8,128)(2,1)} %get-tuple-element.166.rest_0_), channel_id=1, source_target_pairs={{0,8},{4,20},{8,0},{12,28},{16,24},{20,4},{24,16},{28,12},{1,9},{5... | collective-permute-start | bytes 2211848 | tf_op jit(solution)/shard_map/ppermute | solution.py:897
  356.7 18.7 %collective-permute-start.51 = (bf16[960,384]{1,0:T(8,128)(2,1)}, bf16[960,384]{1,0:T(8,128)(2,1)S(1)}, u32[]{:S(2)}, u32[]{:S(2)}) collective-permute-start(bf16[960,384]{1,0:T(8,128)(2,1)} %get-tuple-element.167.rest_1_), channel_id=1, source_target_pairs={{0,8},{4,20},{8,0},{12,28},{16,24},{20,4},{24,16},{28,12},{1,9},{5... | collective-permute-start | bytes 2211848 | tf_op jit(solution)/shard_map/ppermute | solution.py:897
  363.2 29.2 %collective-permute-start.49 = (bf16[2,240,640]{2,1,0:T(8,128)(2,1)S(1)}, bf16[2,240,640]{2,1,0:T(8,128)(2,1)S(1)}, u32[]{:S(2)}, u32[]{:S(2)}) collective-permute-start(bf16[2,240,640]{2,1,0:T(8,128)(2,1)S(1)} %get-tuple-element.170), channel_id=1, source_target_pairs={{0,1},{1,0},{2,3},{3,2},{4,5},{5,4},{6,7},{7,6},{8,9},{9,8},{10,11... | collective-permute-start | bytes 1843208 | tf_op jit(solution)/shard_map/ppermute | solution.py:903
  363.3 30.5 %collective-permute-start.53 = (bf16[480,640]{1,0:T(8,128)(2,1)S(1)}, bf16[480,640]{1,0:T(8,128)(2,1)S(1)}, u32[]{:S(2)}, u32[]{:S(2)}) collective-permute-start(bf16[480,640]{1,0:T(8,128)(2,1)S(1)} %get-tuple-element.168.rest_1_), channel_id=1, source_target_pairs={{0,2},{1,3},{2,0},{3,1},{4,6},{5,7},{6,4},{7,5},{8,10},{9,11},{10,... | collective-permute-start | bytes 1843208 | tf_op jit(solution)/shard_map/ppermute | solution.py:903
  376.3 16.7 %collective-permute-start.54 = (bf16[480,384]{1,0:T(8,128)(2,1)S(1)}, bf16[480,384]{1,0:T(8,128)(2,1)S(1)}, u32[]{:S(2)}, u32[]{:S(2)}) collective-permute-start(bf16[480,384]{1,0:T(8,128)(2,1)S(1)} %get-tuple-element.176), channel_id=1, source_target_pairs={{0,16},{4,12},{8,24},{12,4},{16,0},{20,28},{24,8},{28,20},{1,17},{... | collective-permute-start | bytes 1105928 | tf_op jit(solution)/shard_map/ppermute | solution.py:897
  377.2 15.8 %collective-permute-start.55 = (bf16[480,384]{1,0:T(8,128)(2,1)S(1)}, bf16[480,384]{1,0:T(8,128)(2,1)S(1)}, u32[]{:S(2)}, u32[]{:S(2)}) collective-permute-start(bf16[480,384]{1,0:T(8,128)(2,1)S(1)} %get-tuple-element.177), channel_id=1, source_target_pairs={{0,16},{4,12},{8,24},{12,4},{16,0},{20,28},{24,8},{28,20},{1,17},{... | collective-permute-start | bytes 1105928 | tf_op jit(solution)/shard_map/ppermute | solution.py:897
  394.6 6.9 %collective-permute-start.56 = (bf16[2,120,640]{2,1,0:T(8,128)(2,1)S(1)}, bf16[2,120,640]{2,1,0:T(8,128)(2,1)S(1)}, u32[]{:S(2)}, u32[]{:S(2)}) collective-permute-start(bf16[2,120,640]{2,1,0:T(8,128)(2,1)S(1)} %get-tuple-element.180.rest_1_), channel_id=1, source_target_pairs={{0,8},{4,20},{8,0},{12,28},{16,24},{20,4},{24,16},{28,12},{1,9},{5... | collective-permute-start | bytes 921608 | tf_op jit(solution)/shard_map/ppermute | solution.py:897
  395.5 15.8 %collective-permute-start.52 = (bf16[240,640]{1,0:T(8,128)(2,1)S(1)}, bf16[240,640]{1,0:T(8,128)(2,1)S(1)}, u32[]{:S(2)}, u32[]{:S(2)}) collective-permute-start(bf16[240,640]{1,0:T(8,128)(2,1)S(1)} %get-tuple-element.174.rest_2_), channel_id=1, source_target_pairs={{0,2},{1,3},{2,0},{3,1},{4,6},{5,7},{6,4},{7,5},{8,10},{9,11},{10,... | collective-permute-start | bytes 921608 | tf_op jit(solution)/shard_map/ppermute | solution.py:903
  395.5 18.6 %collective-permute-start.58 = (bf16[2,240,384]{2,1,0:T(8,128)(2,1)S(1)}, bf16[2,240,384]{2,1,0:T(8,128)(2,1)S(1)}, u32[]{:S(2)}, u32[]{:S(2)}) collective-permute-start(bf16[2,240,384]{2,1,0:T(8,128)(2,1)S(1)} %get-tuple-element.178.rest_0_), channel_id=1, source_target_pairs={{0,1},{1,0},{2,3},{3,2},{4,5},{5,4},{6,7},{7,6},{8,9},{9,8},{10,11... | collective-permute-start | bytes 1105928 | tf_op jit(solution)/shard_map/ppermute | solution.py:903
  402.1 14.1 %collective-permute-start.60 = (bf16[120,640]{1,0:T(8,128)(2,1)S(1)}, bf16[120,640]{1,0:T(8,128)(2,1)S(1)}, u32[]{:S(2)}, u32[]{:S(2)}) collective-permute-start(bf16[120,640]{1,0:T(8,128)(2,1)S(1)} %get-tuple-element.181.rest_0_), channel_id=1, source_target_pairs={{0,16},{4,12},{8,24},{12,4},{16,0},{20,28},{24,8},{28,20},{1,17},{... | collective-permute-start | bytes 460808 | tf_op jit(solution)/shard_map/ppermute | solution.py:897
  412.0 13.9 %collective-permute-start.78 = (bf16[240,640]{1,0:T(8,128)(2,1)S(1)}, bf16[240,640]{1,0:T(8,128)(2,1)S(1)}, u32[]{:S(2)}, u32[]{:S(2)}) collective-permute-start(bf16[240,640]{1,0:T(8,128)(2,1)S(1)} %sum_two.3.refs_1_.rest_0_), channel_id=1, source_target_pairs={{0,4},{4,0},{8,12},{12,8},{16,20},{20,16},{24,28},{28,24},{1,5},{5... | collective-permute-start | bytes 921608 | tf_op jit(solution)/shard_map/ppermute | solution.py:897
  412.0 15.3 %collective-permute-start.77 = (bf16[240,640]{1,0:T(8,128)(2,1)S(1)}, bf16[240,640]{1,0:T(8,128)(2,1)S(1)}, u32[]{:S(2)}, u32[]{:S(2)}) collective-permute-start(bf16[240,640]{1,0:T(8,128)(2,1)S(1)} %sum_two.3.refs_1_.rest_0_), channel_id=1, source_target_pairs={{0,24},{4,28},{8,16},{12,20},{16,8},{20,12},{24,0},{28,4},{1,25},{... | collective-permute-start | bytes 921608 | tf_op jit(solution)/shard_map/ppermute | solution.py:897
  413.6 15.6 %collective-permute-start.76 = (bf16[240,640]{1,0:T(8,128)(2,1)S(1)}, bf16[240,640]{1,0:T(8,128)(2,1)S(1)}, u32[]{:S(2)}, u32[]{:S(2)}) collective-permute-start(bf16[240,640]{1,0:T(8,128)(2,1)S(1)} %sum_two.3.refs_1_.rest_0_), channel_id=1, source_target_pairs={{0,16},{4,12},{8,24},{12,4},{16,0},{20,28},{24,8},{28,20},{1,17},{... | collective-permute-start | bytes 921608 | tf_op jit(solution)/shard_map/ppermute | solution.py:897
  414.2 15.6 %collective-permute-start.75 = (bf16[240,640]{1,0:T(8,128)(2,1)S(1)}, bf16[240,640]{1,0:T(8,128)(2,1)S(1)}, u32[]{:S(2)}, u32[]{:S(2)}) collective-permute-start(bf16[240,640]{1,0:T(8,128)(2,1)S(1)} %sum_two.3.refs_1_.rest_0_), channel_id=1, source_target_pairs={{0,8},{4,20},{8,0},{12,28},{16,24},{20,4},{24,16},{28,12},{1,9},{5... | collective-permute-start | bytes 921608 | tf_op jit(solution)/shard_map/ppermute | solution.py:897
  416.2 9.6 %collective-permute-start.59 = (bf16[240,384]{1,0:T(8,128)(2,1)S(1)}, bf16[240,384]{1,0:T(8,128)(2,1)S(1)}, u32[]{:S(2)}, u32[]{:S(2)}) collective-permute-start(bf16[240,384]{1,0:T(8,128)(2,1)S(1)} %get-tuple-element.184.rest_0_), channel_id=1, source_target_pairs={{0,2},{1,3},{2,0},{3,1},{4,6},{5,7},{6,4},{7,5},{8,10},{9,11},{10,... | collective-permute-start | bytes 552968 | tf_op jit(solution)/shard_map/ppermute | solution.py:903
  425.8 5.3 %collective-permute-start.71 = (bf16[120,640]{1,0:T(8,128)(2,1)S(1)}, bf16[120,640]{1,0:T(8,128)(2,1)S(1)}, u32[]{:S(2)}, u32[]{:S(2)}) collective-permute-start(bf16[120,640]{1,0:T(8,128)(2,1)S(1)} %sum_two.4.rest_0_), channel_id=1, source_target_pairs={{0,4},{4,0},{8,12},{12,8},{16,20},{20,16},{24,28},{28,24},{1,5},{5... | collective-permute-start | bytes 460808 | tf_op jit(solution)/shard_map/ppermute | solution.py:897
  425.9 7.7 %collective-permute-start.70 = (bf16[120,640]{1,0:T(8,128)(2,1)S(1)}, bf16[120,640]{1,0:T(8,128)(2,1)S(1)}, u32[]{:S(2)}, u32[]{:S(2)}) collective-permute-start(bf16[120,640]{1,0:T(8,128)(2,1)S(1)} %sum_two.4.rest_0_), channel_id=1, source_target_pairs={{0,24},{4,28},{8,16},{12,20},{16,8},{20,12},{24,0},{28,4},{1,25},{... | collective-permute-start | bytes 460808 | tf_op jit(solution)/shard_map/ppermute | solution.py:897
  427.4 9.4 %collective-permute-start.69 = (bf16[120,640]{1,0:T(8,128)(2,1)S(1)}, bf16[120,640]{1,0:T(8,128)(2,1)S(1)}, u32[]{:S(2)}, u32[]{:S(2)}) collective-permute-start(bf16[120,640]{1,0:T(8,128)(2,1)S(1)} %sum_two.4.rest_0_), channel_id=1, source_target_pairs={{0,16},{4,12},{8,24},{12,4},{16,0},{20,28},{24,8},{28,20},{1,17},{... | collective-permute-start | bytes 460808 | tf_op jit(solution)/shard_map/ppermute | solution.py:897
  429.2 8.4 %collective-permute-start.68 = (bf16[120,640]{1,0:T(8,128)(2,1)S(1)}, bf16[120,640]{1,0:T(8,128)(2,1)S(1)}, u32[]{:S(2)}, u32[]{:S(2)}) collective-permute-start(bf16[120,640]{1,0:T(8,128)(2,1)S(1)} %sum_two.4.rest_0_), channel_id=1, source_target_pairs={{0,8},{4,20},{8,0},{12,28},{16,24},{20,4},{24,16},{28,12},{1,9},{5... | collective-permute-start | bytes 460808 | tf_op jit(solution)/shard_map/ppermute | solution.py:897
  429.8 31.8 %collective-permute-start.57 = (bf16[1920,256]{1,0:T(8,128)(2,1)S(1)}, bf16[1920,256]{1,0:T(8,128)(2,1)S(1)}, u32[]{:S(2)}, u32[]{:S(2)}) collective-permute-start(bf16[1920,256]{1,0:T(8,128)(2,1)S(1)} %hold.7), channel_id=1, source_target_pairs={{0,0},{4,1},{1,2},{5,3},{2,4},{6,5},{3,6},{7,7},{8,8},{12,9},{9,10... | collective-permute-start | bytes 2949128 | tf_op jit(solution)/shard_map/ppermute | solution.py:914
  431.1 9.7 %collective-permute-start.63 = (bf16[240,384]{1,0:T(8,128)(2,1)S(1)}, bf16[240,384]{1,0:T(8,128)(2,1)S(1)}, u32[]{:S(2)}, u32[]{:S(2)}) collective-permute-start(bf16[240,384]{1,0:T(8,128)(2,1)S(1)} %sum_two.5.rest_8_.rest_0_), channel_id=1, source_target_pairs={{0,24},{4,28},{8,16},{12,20},{16,8},{20,12},{24,0},{28,4},{1,25},{... | collective-permute-start | bytes 552968 | tf_op jit(solution)/shard_map/ppermute | solution.py:897
  433.6 10.7 %collective-permute-start.62 = (bf16[240,384]{1,0:T(8,128)(2,1)S(1)}, bf16[240,384]{1,0:T(8,128)(2,1)S(1)}, u32[]{:S(2)}, u32[]{:S(2)}) collective-permute-start(bf16[240,384]{1,0:T(8,128)(2,1)S(1)} %sum_two.5.rest_8_.rest_0_), channel_id=1, source_target_pairs={{0,16},{4,12},{8,24},{12,4},{16,0},{20,28},{24,8},{28,20},{1,17},{... | collective-permute-start | bytes 552968 | tf_op jit(solution)/shard_map/ppermute | solution.py:897
  436.7 7.5 %collective-permute-start.61 = (bf16[240,384]{1,0:T(8,128)(2,1)S(1)}, bf16[240,384]{1,0:T(8,128)(2,1)S(1)}, u32[]{:S(2)}, u32[]{:S(2)}) collective-permute-start(bf16[240,384]{1,0:T(8,128)(2,1)S(1)} %sum_two.5.rest_8_.rest_0_), channel_id=1, source_target_pairs={{0,8},{4,20},{8,0},{12,28},{16,24},{20,4},{24,16},{28,12},{1,9},{5... | collective-permute-start | bytes 552968 | tf_op jit(solution)/shard_map/ppermute | solution.py:897
  437.6 7.2 %collective-permute-start.74 = (bf16[120,640]{1,0:T(8,128)(2,1)S(1)}, bf16[120,640]{1,0:T(8,128)(2,1)S(1)}, u32[]{:S(2)}, u32[]{:S(2)}) collective-permute-start(bf16[120,640]{1,0:T(8,128)(2,1)S(1)} %collective-permute-done.70.rest_3_), channel_id=1, source_target_pairs={{0,4},{4,0},{8,12},{12,8},{16,20},{20,16},{24,28},{28,24},{1,5},{5... | collective-permute-start | bytes 460808 | tf_op jit(solution)/shard_map/ppermute | solution.py:897
  440.9 4.0 collective-permute-start.73
  447.0 8.2 %collective-permute-start.64 = (bf16[240,384]{1,0:T(8,128)(2,1)S(1)}, bf16[240,384]{1,0:T(8,128)(2,1)S(1)}, u32[]{:S(2)}, u32[]{:S(2)}) collective-permute-start(bf16[240,384]{1,0:T(8,128)(2,1)S(1)} %sum_two.5.rest_8_.rest_0_), channel_id=1, source_target_pairs={{0,4},{4,0},{8,12},{12,8},{16,20},{20,16},{24,28},{28,24},{1,5},{5... | collective-permute-start | bytes 552968 | tf_op jit(solution)/shard_map/ppermute | solution.py:897
  447.1 8.0 %collective-permute-start.67 = (bf16[240,384]{1,0:T(8,128)(2,1)S(1)}, bf16[240,384]{1,0:T(8,128)(2,1)S(1)}, u32[]{:S(2)}, u32[]{:S(2)}) collective-permute-start(bf16[240,384]{1,0:T(8,128)(2,1)S(1)} %collective-permute-done.63.rest_3_), channel_id=1, source_target_pairs={{0,4},{4,0},{8,12},{12,8},{16,20},{20,16},{24,28},{28,24},{1,5},{5... | collective-permute-start | bytes 552968 | tf_op jit(solution)/shard_map/ppermute | solution.py:897
  447.5 7.7 %collective-permute-start.66 = (bf16[240,384]{1,0:T(8,128)(2,1)S(1)}, bf16[240,384]{1,0:T(8,128)(2,1)S(1)}, u32[]{:S(2)}, u32[]{:S(2)}) collective-permute-start(bf16[240,384]{1,0:T(8,128)(2,1)S(1)} %collective-permute-done.62.rest_2_), channel_id=1, source_target_pairs={{0,4},{4,0},{8,12},{12,8},{16,20},{20,16},{24,28},{28,24},{1,5},{5... | collective-permute-start | bytes 552968 | tf_op jit(solution)/shard_map/ppermute | solution.py:897
  447.6 7.5 %collective-permute-start.65 = (bf16[240,384]{1,0:T(8,128)(2,1)S(1)}, bf16[240,384]{1,0:T(8,128)(2,1)S(1)}, u32[]{:S(2)}, u32[]{:S(2)}) collective-permute-start(bf16[240,384]{1,0:T(8,128)(2,1)S(1)} %collective-permute-done.61.rest_1_), channel_id=1, source_target_pairs={{0,4},{4,0},{8,12},{12,8},{16,20},{20,16},{24,28},{28,24},{1,5},{5... | collective-permute-start | bytes 552968 | tf_op jit(solution)/shard_map/ppermute | solution.py:897
  (106 other events, 991.6 us)

commit v14 on v13

--- a/solution.py
+++ b/solution.py
@@ -16,6 +16,7 @@
 WHOLE = pl.BlockSpec(memory_space=pltpu.VMEM)
 LEFT = pl.BlockSpec(memory_space=pl.ANY)
 SCALARS = pl.BlockSpec(memory_space=pltpu.SMEM)
+TOKEN = jax.ShapeDtypeStruct((8, 128), f32)
 BRIEF = pl.CostEstimate(flops=1024, bytes_accessed=1024, transcendentals=0)
 
 
@@ -522,7 +523,8 @@
 
 def grad_ffn_kernel(sc, *rest):
     lefts, rights = rest[:4], rest[4:8]
-    send_ref, keep_ref, left, right = rest[-4:]
+    send_ref, keep_ref, token_ref, left, right = rest[-5:]
+    token_ref[...] = jnp.zeros_like(token_ref)
     core, chip = sc[0], sc[1]
     n, cols = rights[0].shape[0], right.shape[1]
     turned(left, lefts)
@@ -540,9 +542,9 @@
     out = shape((2, width, cols), bf16)
     return pl.pallas_call(
         grad_ffn_kernel,
-        out_shape=(out, out),
+        out_shape=(out, out, TOKEN),
         in_specs=[SCALARS] + [WHOLE] * 8 + [LEFT] * len(after),
-        out_specs=(WHOLE,) * 2,
+        out_specs=(WHOLE,) * 3,
         scratch_shapes=[pltpu.VMEM((width, 4 * n), bf16), pltpu.VMEM((4 * n, cols), bf16)],
         cost_estimate=BRIEF,
         compiler_params=pltpu.CompilerParams(vmem_limit_bytes=LIMIT),
@@ -552,7 +554,8 @@
 
 def grad_down_kernel(sc, *rest):
     lefts, rights = rest[:4], rest[4:8]
-    send_ref, keep_ref, left, right = rest[-4:]
+    send_ref, keep_ref, token_ref, left, right = rest[-5:]
+    token_ref[...] = jnp.zeros_like(token_ref)
     n, (_, half, cols) = rights[0].shape[0], send_ref.shape
     turned(left, lefts)
     rows = pl.ds(pl.multiple_of(sc[0] * half, half), half)
@@ -571,9 +574,9 @@
     block = (2, width // 2, cols)
     return pl.pallas_call(
         grad_down_kernel,
-        out_shape=(shape(block, bf16), shape(block, bf16)),
+        out_shape=(shape(block, bf16), shape(block, bf16), TOKEN),
         in_specs=[SCALARS] + [WHOLE] * 8 + [LEFT] * len(after),
-        out_specs=(WHOLE,) * 2,
+        out_specs=(WHOLE,) * 3,
         scratch_shapes=[pltpu.VMEM((width, 4 * n), bf16), pltpu.VMEM((4 * n, cols), bf16)],
         cost_estimate=BRIEF,
         compiler_params=pltpu.CompilerParams(vmem_limit_bytes=LIMIT),
@@ -585,7 +588,8 @@
     a_refs, o_refs, rest = rest[:4], rest[4:8], rest[8:]
     queries, keys, values, outs, threes, ones = (rest[i : i + 2] for i in range(0, 12, 2))
     gain_a, gain_f = (rest[i : i + 2] for i in (12, 14))
-    *sends, keep_ref, left, right = rest[-5:]
+    *sends, keep_ref, token_ref, left, right = rest[-6:]
+    token_ref[...] = jnp.zeros_like(token_ref)
     core, chip = sc[0], sc[1]
     n, width = a_refs[0].shape
     turned(left.at[0], a_refs)
@@ -622,9 +626,9 @@
     out = shape((width, PIECE), bf16)
     return pl.pallas_call(
         grad_attention_kernel,
-        out_shape=(out, out, shape((2, width, PIECE), bf16)),
+        out_shape=(out, out, shape((2, width, PIECE), bf16), TOKEN),
         in_specs=[SCALARS] + [WHOLE] * 24 + [LEFT] * len(after),
-        out_specs=(WHOLE,) * 3,
+        out_specs=(WHOLE,) * 4,
         scratch_shapes=[pltpu.VMEM((2, width, 4 * n), bf16), pltpu.VMEM((4, 4 * n, PIECE), bf16)],
         cost_estimate=BRIEF,
         compiler_params=pltpu.CompilerParams(vmem_limit_bytes=LIMIT),
@@ -669,21 +673,29 @@
     )(sc, *mine, *other, *after)
 
 
-def pick_first_kernel(sc, q_ref, k_ref, v_ref, o_ref, gain_ref, out_ref):
+def pick_first_kernel(sc, q_ref, k_ref, v_ref, o_ref, gain_ref, out_ref, wide, tall, sem):
     rows = out_ref.shape[0]
     which = sc[0] * 4 + sc[1]
+
+    def bring(source, into, first, last):
+        @pl.when((which >= first) & (which <= last))
+        def _():
+            copy = pltpu.make_async_copy(source, into, sem)
+            copy.start()
+            copy.wait()
+
+    bring(q_ref, wide, 0, 2)
+    bring(k_ref, tall, 3, 3)
+    bring(v_ref, tall, 4, 4)
+    bring(o_ref, wide, 5, 7)
     pad = jnp.zeros((6, rows), f32)
     gains = jnp.concatenate([gain_ref[...], pad], axis=0).T.astype(bf16)
     rest = jnp.zeros((rows, PIECE - KVW - 8), bf16)
-    for at in range(8):
-
-        @pl.when(which == at)
+    for m in range(4):
+
+        @pl.when((which == m) | (which == (m + 5 if m < 3 else 4)))
         def _():
-            if at in (3, 4):
-                piece = (k_ref if at == 3 else v_ref)[...].T
-            else:
-                source, m = (q_ref, at) if at < 3 else (o_ref, at - 5)
-                piece = source[:, m * KVW : (m + 1) * KVW]
+            piece = wide[:, m * KVW : (m + 1) * KVW] if m < 3 else tall[...].T
             out_ref[...] = jnp.concatenate([piece, gains, rest], axis=1)
 
 
@@ -691,10 +703,11 @@
     return pl.pallas_call(
         pick_first_kernel,
         out_shape=shape((query.shape[0], PIECE), bf16),
-        in_specs=[SCALARS] + [WHOLE] * 5,
+        in_specs=[SCALARS] + [LEFT] * 4 + [WHOLE],
         out_specs=WHOLE,
-        cost_estimate=BRIEF,
-        compiler_params=pltpu.CompilerParams(vmem_limit_bytes=16 << 20),
+        scratch_shapes=[pltpu.VMEM(query.shape, bf16), pltpu.VMEM(key.shape, bf16), pltpu.SemaphoreType.DMA],
+        cost_estimate=BRIEF,
+        compiler_params=pltpu.CompilerParams(vmem_limit_bytes=LIMIT),
         name="pick_first",
     )(sc, query, key, value, out, gains)
 
@@ -771,11 +784,16 @@
 
 
 def small(kernel, sc, args, outs, scratch, after, name):
-    return pl.pallas_call(
-        kernel,
-        out_shape=tuple(outs),
+    def with_token(*refs):
+        at = len(refs) - len(scratch) - 1
+        refs[at][...] = jnp.zeros_like(refs[at])
+        kernel(*refs[:at], *refs[at + 1 :])
+
+    return pl.pallas_call(
+        with_token,
+        out_shape=(*outs, TOKEN),
         in_specs=[SCALARS] + [WHOLE] * len(args) + [LEFT] * len(after),
-        out_specs=(WHOLE,) * len(outs),
+        out_specs=(WHOLE,) * (len(outs) + 1),
         scratch_shapes=scratch,
         cost_estimate=BRIEF,
         compiler_params=pltpu.CompilerParams(vmem_limit_bytes=32 << 20),
@@ -847,7 +865,7 @@
     def kernel(sc, own_ref, got_ref, *rest):
         rest[-1][...] = (own_ref[...] + got_ref[...].astype(f32)).astype(bf16)
 
-    return small(kernel, sc, [own, got], [shape(own.shape, bf16)], [], after, "sum_two")[0]
+    return small(kernel, sc, [own, got], [shape(own.shape, bf16)], [], after, "sum_two")
 
 
 def lay_down(sc, mine, other, after):
@@ -883,7 +901,7 @@
     def kernel(sc, far_ref, near_ref, *rest):
         rest[-1][...] = (far_ref[...] + jnp.where(sc[0] == 1, near_ref[...].astype(f32), 0.0)).astype(bf16)
 
-    return small(kernel, sc, [far, near], [shape(far.shape, bf16)], [], after, "far_sum")[0]
+    return small(kernel, sc, [far, near], [shape(far.shape, bf16)], [], after, "far_sum")
 
 
 CORE, SIDE, BACK = 1, 2, 4
@@ -938,11 +956,11 @@
     return far, near, own
 
 
-def unwindow(sc, far, near, after=()):
+def unwindow(sc, far, near):
     depth = lax.axis_size("fsdp")
     near = flip(near, CORE)
-    far = far_sum(sc, far, near, after)
-    return near, far, lax.ppermute(far, "fsdp", [(z + 1, z) for z in range(0, depth, 2)])
+    far, token = far_sum(sc, far, near, [])
+    return near, token, lax.ppermute(far, "fsdp", [(z + 1, z) for z in range(0, depth, 2)])
 
 
 def over_groups(value):
@@ -1004,54 +1022,54 @@
 
     gb1, act1, away1, g1, p1, dgain_f1, do = back(True, False, sc, weights, [cot], [gate1, up1, h1_1, gain_f])
     across_2 = across((gb1, away1))
-    dq1, three1, far, near, own = attend_back(sc, p1, q1, kv1, lse1, do, cos, sin, [*across_1])
+    dq1, three1, far, near, own = attend_back(sc, p1, q1, kv1, lse1, do, cos, sin)
     near, _, far = unwindow(sc, far, near)
     (three1,) = across((three1,))
     tail = [g1, dq1, own, near, far, h_1, gain_a, cos, sin]
-    dk1, dv1, one1, dgain_a1, gb0, act0, away0, g1, p0, dgain_f0, do = back(False, False, sc, weights, tail, [gate0, up0, h1_0, gain_f], [three1, *across_2])
+    dk1, dv1, one1, dgain_a1, gb0, act0, away0, g1, p0, dgain_f0, do = back(False, False, sc, weights, tail, [gate0, up0, h1_0, gain_f], [three1, *across_2, *across_1])
 
     away0, gb0_, one1 = across((away0, gb0, one1))
-    send_b, keep_b = grad_ffn(sc, [b1, b0, across_1[1], across_0[1]], [act1, act0, across_2[1], away0], [])
+    send_b, keep_b, done = grad_ffn(sc, [b1, b0, across_1[1], across_0[1]], [act1, act0, across_2[1], away0], [])
     got_b = flip(send_b, SIDE, BACK)
-    dq0, three0, far, near, own = attend_back(sc, p0, q0, kv0, lse0, do, cos, sin, [one1, send_b])
-    near, down_far, far = unwindow(sc, far, near)
-    send_d, keep_d = grad_down(sc, [gb1, gb0, across_2[0], gb0_], [z1, z0, across_1[3], across_0[3]], [down_far])
+    dq0, three0, far, near, own = attend_back(sc, p0, q0, kv0, lse0, do, cos, sin, [one1, done])
+    near, done, far = unwindow(sc, far, near)
+    send_d, keep_d, done = grad_down(sc, [gb1, gb0, across_2[0], gb0_], [z1, z0, across_1[3], across_0[3]], [done])
     got_d = flip_z(send_d, 1)
     (three0,) = across((three0,))
     tail = [g1, dq0, own, near, far, h_0, gain_a, cos, sin, output]
-    dk0, dv0, one0, dgain_a0, leaving = back(False, True, sc, weights, tail, None, [send_d])
-    later_b, own_b = sum_first(sc, keep_b, [got_b], [one0])
+    dk0, dv0, one0, dgain_a0, leaving = back(False, True, sc, weights, tail, None, [done])
+    later_b, own_b, done = sum_first(sc, keep_b, [got_b], [dgain_a0])
     more_b = flip(later_b, BACK, SIDE)
     own = [dq1, dq0, dk1, dk0, dv1, dv0, p1, p0]
     got = [three1, three0, one1, flip(one0, CORE)]
-    *send_a, keep_a = grad_attention(sc, [a1, a0, across_1[0], across_0[0]], [mixed1, mixed0, across_1[2], across_0[2]], own, got, [dgain_a1, dgain_a0, dgain_f1, dgain_f0], [later_b])
+    *send_a, keep_a, done = grad_attention(sc, [a1, a0, across_1[0], across_0[0]], [mixed1, mixed0, across_1[2], across_0[2]], own, got, [dgain_a1, dgain_a0, dgain_f1, dgain_f0], [done])
     got_a = [flip(v, SIDE, BACK) for v in send_a]
-    send_d, keep_d = sum_third(sc, keep_d, got_d, send_a)
+    send_d, keep_d, done = sum_third(sc, keep_d, got_d, [done])
     got_d = flip_z(send_d, 2)
-    send_b, ring_b = sum_second(sc, own_b, [more_b], [send_d])
+    send_b, ring_b, done = sum_second(sc, own_b, [more_b], [done])
     got_b = flip_z(send_b, 1)
-    *later_a, own_a = sum_first(sc, keep_a, got_a, [ring_b], 2)
+    *later_a, own_a, done = sum_first(sc, keep_a, got_a, [done], 2)
     more_a = [flip(v, BACK, SIDE) for v in later_a]
-    send_b, ring_b = sum_third(sc, ring_b, got_b, [own_a])
+    send_b, ring_b, done = sum_third(sc, ring_b, got_b, [done])
     got_b = flip_z(send_b, 2)
-    send_a, ring_a = sum_second(sc, own_a, more_a, [send_b])
+    send_a, ring_a, done = sum_second(sc, own_a, more_a, [done])
     got_a = flip_z(send_a, 1)
-    send_d, keep_d = down_split(sc, keep_d, got_d, [send_a])
+    send_d, keep_d, done = down_split(sc, keep_d, got_d, [done])
     got_d = flip(send_d, SIDE, BACK)
-    later_d, own_d = sum_first(sc, keep_d, [got_d], [send_d])
+    later_d, own_d, done = sum_first(sc, keep_d, [got_d], [done])
     more_d = flip(later_d, BACK, SIDE)
-    piece_b = over_groups(sum_two(sc, ring_b, got_b, [later_d]))
-    all_b = spread(piece_b)
-    send_a, ring_a = sum_third(sc, ring_a, got_a, [piece_b])
+    piece_b, done = sum_two(sc, ring_b, got_b, [done])
+    all_b = spread(over_groups(piece_b))
+    send_a, ring_a, first = sum_third(sc, ring_a, got_a, [done])
     got_a = flip_z(send_a, 2)
-    piece_d = over_groups(sum_two(sc, own_d, more_d, [send_a]))
-    all_d = spread(piece_d)
-    piece_a = over_groups(sum_two(sc, ring_a, got_a, [piece_d]))
-    all_a = spread(piece_a)
-    grad_gate, grad_up = lay(sc, all_b, across(all_b), (gate_weight.shape[1],) * 2, [piece_a])
-    grad_down_ = lay_down(sc, all_d, across(all_d), [grad_gate])
-    grad_query, grad_key, grad_value, grad_out, dgains = lay(sc, all_a, across(all_a), (width, KVW, KVW, width), [grad_down_])
-    leaving = home_to_work(hold(leaving, [piece_b]), back=True)
+    piece_d, done = sum_two(sc, own_d, more_d, [first])
+    all_d = spread(over_groups(piece_d))
+    piece_a, done = sum_two(sc, ring_a, got_a, [done])
+    all_a = spread(over_groups(piece_a))
+    grad_gate, grad_up = lay(sc, all_b, across(all_b), (gate_weight.shape[1],) * 2, [done])
+    grad_down_ = lay_down(sc, all_d, across(all_d), [done])
+    grad_query, grad_key, grad_value, grad_out, dgains = lay(sc, all_a, across(all_a), (width, KVW, KVW, width), [done])
+    leaving = home_to_work(hold(leaving, [first]), back=True)
     output, grad_tokens = leaving[:width].T, leaving[width:].astype(f32).T
     return (output[None], grad_tokens[None], dgains[0], grad_query, grad_key, grad_value, grad_out, dgains[1], grad_gate, grad_up, grad_down_.T)
 

time: 468 us -> 462 us (0.987)
  local copies, waits for them, and re-layouts: 35.1 us -> 27 us
  waiting for transfers between devices: 138 us -> 132 us
    ppermute x12, waiting for transfers between devices: 56.4 us -> 47.1 us  [flip_z(): return lax.ppermute(value, ('dp', 'fsdp'), pairs)]
    unnamed x178 -> x164, local copies, waits for them, and re-layouts: 32.4 us -> 24.3 us
  transfers between devices with their start and end apart: 82 -> 82, of which waited for: 35 -> 32; matrix products, arithmetic and copies ran while one was open for 1% -> 1% of each run, Pallas kernels for 26% -> 30%
where the time goes in v14:
time: 462 us; the launch traced here: 457 us
  Pallas kernels  196 us (42%)
  waiting for transfers between devices  132 us (29%)
  starting transfers between devices  95.3 us (21%)
  local copies, waits for them, and re-layouts  27 us (6%)
  other arithmetic  5.53 us (1%)
    ppermute x63, waiting for transfers between devices, flip(): lax.ppermute(value, 'dp', [(i, i ^ bits[i & 1]) for i in range(count)])  64.6 us
    ppermute x63, starting transfers between devices, flip(): lax.ppermute(value, 'dp', [(i, i ^ bits[i & 1]) for i in range(count)])  48.5 us
    ppermute x12, waiting for transfers between devices, flip_z(): return lax.ppermute(value, ('dp', 'fsdp'), pairs)  47.1 us
    pallas_call x3, Pallas kernels, back(): pl.pallas_call(functools.partial(back_kernel, start, end, len(after)), ou...  46.8 us
    pallas_call x2, Pallas kernels, post(): pl.pallas_call(functools.partial(post_kernel, last, len(after)), out_shap...  35.6 us
    ppermute x12, starting transfers between devices, flip_z(): return lax.ppermute(value, ('dp', 'fsdp'), pairs)  28.2 us
    pallas_call x2, Pallas kernels, attend_back(): pl.pallas_call(attend_back_kernel, out_shape=(shape((3, n, PIECE), bf16),...  25.3 us
    unnamed x164, local copies, waits for them, and re-layouts  24.3 us
  transfers between devices with their start and end apart: 82, of which 32 were waited for; matrix products, arithmetic and copies ran while one was open for 1% of the time, Pallas kernels for 30%

profile of v14, /device:TPU:0, one launch (start us, length us, event | category | flops | bytes accessed | tf_op | source)
XLA Modules:
  0.0 457.0 jit_solution(8957477434429423142)
XLA Ops:
  3.3 2.7 pick_first.1.rest_0_
  6.0 4.1 collective-permute-start.1
  10.1 1.6 collective-permute-start
  11.7 7.3 %collective-permute-done.1.rest_2_ = bf16[240,384]{1,0:T(8,128)(2,1)S(1)} collective-permute-done((bf16[240,384]{1,0:T(8,128)(2,1)}, bf16[240,384]{1,0:T(8,128)(2,1)S(1)}, u32[]{:S(2)}, u32[]{:S(2)}) %collective-permute-start.1) | collective-permute-done | bytes 184352 | tf_op jit(solution)/shard_map/ppermute | solution.py:921
  23.1 1.5 collective-permute-done.2.rest_3_
  24.6 1.5 stack.30.first_ref
  26.2 1.5 collective-permute-start.3
  27.7 1.5 collective-permute-start.4
  29.2 3.2 collective-permute-start.11
  32.5 1.7 collective-permute-start.10
  34.2 11.5 %collective-permute-done.3.refs_1_.rest_1_ = bf16[960,384]{1,0:T(8,128)(2,1)} collective-permute-done((bf16[960,384]{1,0:T(8,128)(2,1)S(1)}, bf16[960,384]{1,0:T(8,128)(2,1)}, u32[]{:S(2)}, u32[]{:S(2)}) %collective-permute-start.3) | collective-permute-done | bytes 737312 | tf_op jit(solution)/shard_map/ppermute | solution.py:915
  45.7 6.8 %collective-permute-done.11.refs_0_ = bf16[368,640]{1,0:T(8,128)(2,1)S(1)} collective-permute-done((bf16[368,640]{1,0:T(8,128)(2,1)S(1)}, bf16[368,640]{1,0:T(8,128)(2,1)S(1)}, u32[]{:S(2)}, u32[]{:S(2)}) %collective-permute-start.11) | collective-permute-done | bytes 471072 | tf_op jit(solution)/shard_map/ppermute | solution.py:921
  54.3 10.0 %collective-permute-done.12.rest_3_ = bf16[368,640]{1,0:T(8,128)(2,1)S(1)} collective-permute-done((bf16[368,640]{1,0:T(8,128)(2,1)S(1)}, bf16[368,640]{1,0:T(8,128)(2,1)S(1)}, u32[]{:S(2)}, u32[]{:S(2)}) %collective-permute-start.12) | collective-permute-done | bytes 471072 | tf_op jit(solution)/shard_map/ppermute | solution.py:921
  64.3 3.0 stack.31.rest_8_
  69.2 4.6 collective-permute-start.8
  73.7 5.9 %collective-permute-start.7 = (bf16[960,384]{1,0:T(8,128)(2,1)}, bf16[960,384]{1,0:T(8,128)(2,1)}, u32[]{:S(2)}, u32[]{:S(2)}) collective-permute-start(bf16[960,384]{1,0:T(8,128)(2,1)} %collective-permute-done.3.refs_1_.rest_1_), channel_id=1, source_target_pairs={{0,4},{4,0},{8,12},{12,8},{16,20},{20,16},{24,28},{28,24},{1,5},{5... | collective-permute-start | bytes 2211848 | tf_op jit(solution)/shard_map/ppermute | solution.py:915
  83.3 7.4 %pre.1 = (bf16[256,960]{1,0:T(8,128)(2,1)}, bf16[256,960]{1,0:T(8,128)(2,1)}, bf16[960,256]{1,0:T(8,128)(2,1)}, bf16[656,256]{1,0:T(8,128)(2,1)}) custom-call(s32[3]{0:T(128)} %pad_add_fusion.sc.refs_0_, bf16[976,256]{1,0:T(8,128)(2,1)} %copy-done.72, f32[1,960]{1,0:T(1,128)} %get-tuple-element.251.gain_ref.gain_a.rest_22_.rest_14_, ...), custom_call_target="tpu_custom_call" | custom-call | flops 1024 | bytes 1024 | tf_op jit(solution)/shard_map/pre/pallas_call | solution.py:127
  90.7 9.3 %collective-permute-start.15 = (bf16[656,256]{1,0:T(8,128)(2,1)}, bf16[656,256]{1,0:T(8,128)(2,1)S(1)}, u32[]{:S(2)}, u32[]{:S(2)}) collective-permute-start(bf16[656,256]{1,0:T(8,128)(2,1)} %get-tuple-element.124.kv2.rest_16_), channel_id=1, source_target_pairs={{0,1},{2,3},{4,5},{6,7},{8,9},{10,11},{12,13},{14,15},{16,17},{18,... | collective-permute-start | bytes 1007624 | tf_op jit(solution)/shard_map/ppermute | solution.py:954
  100.1 7.8 %collective-permute-done.15.refs_1_.kv0 = bf16[656,256]{1,0:T(8,128)(2,1)S(1)} collective-permute-done((bf16[656,256]{1,0:T(8,128)(2,1)}, bf16[656,256]{1,0:T(8,128)(2,1)S(1)}, u32[]{:S(2)}, u32[]{:S(2)}) %collective-permute-start.15) | collective-permute-done | bytes 335904 | tf_op jit(solution)/shard_map/ppermute | solution.py:954
  110.8 10.1 %attend.2 = (bf16[960,256]{1,0:T(8,128)(2,1)S(1)}, f32[15,256]{1,0:T(8,128)S(1)}) custom-call(bf16[960,256]{1,0:T(8,128)(2,1)S(1)} %copy-done.22, bf16[656,256]{1,0:T(8,128)(2,1)S(1)} %collective-permute-done.15.refs_1_.kv0, bf16[656,256]{1,0:T(8,128)(2,1)S(1)} %collective-permute-done.18.kv1, bf16[656,256]{1,0:T(8,128)(2,1)S(1)} %copy-done.5), custom_call_target="tpu_custom_call" | custom-call | flops 1024 | bytes 1024 | tf_op jit(solution)/shard_map/attend/pallas_call | solution.py:180
  121.6 11.2 %collective-permute-done.17.refs_0_ = bf16[4,368,640]{2,1,0:T(8,128)(2,1)} collective-permute-done((bf16[4,368,640]{2,1,0:T(8,128)(2,1)}, bf16[4,368,640]{2,1,0:T(8,128)(2,1)}, u32[]{:S(2)}, u32[]{:S(2)}) %collective-permute-start.17) | collective-permute-done | bytes 1884192 | tf_op jit(solution)/shard_map/ppermute | solution.py:915
  134.2 2.8 collective-permute-done.22.rest_15_
  137.0 18.2 %post.2 = (bf16[256,960]{1,0:T(8,128)(2,1)}, f32[256,960]{1,0:T(8,128)}, bf16[256,960]{1,0:T(8,128)(2,1)}, bf16[256,2560]{1,0:T(8,128)(2,1)}, bf16[256,2560]{1,0...) custom-call(s32[3]{0:T(128)} %pad_add_fusion.sc.refs_0_, ...), custom_call_target="tpu_custom_call" | custom-call | flops 1024 | bytes 1024 | tf_op jit(solution)/shard_map/post/pallas_call | solution.py:340
  155.4 3.7 collective-permute-start.24
  159.9 5.9 %collective-permute-start.27 = (bf16[256,960]{1,0:T(8,128)(2,1)}, bf16[256,960]{1,0:T(8,128)(2,1)S(1)}, u32[]{:S(2)}, u32[]{:S(2)}) collective-permute-start(bf16[256,960]{1,0:T(8,128)(2,1)} %get-tuple-element.131.rest_1_), channel_id=1, source_target_pairs={{0,4},{4,0},{8,12},{12,8},{16,20},{20,16},{24,28},{28,24},{1,5},{5... | collective-permute-start | bytes 1474568 | tf_op jit(solution)/shard_map/ppermute | solution.py:915
  165.9 1.7 collective-permute-done.24.kv0
  171.6 10.5 %attend.3 = (bf16[960,256]{1,0:T(8,128)(2,1)S(1)}, f32[15,256]{1,0:T(8,128)S(1)}) custom-call(bf16[960,256]{1,0:T(8,128)(2,1)S(1)} %copy-done.24, bf16[656,256]{1,0:T(8,128)(2,1)S(1)} %collective-permute-done.24.kv0, bf16[656,256]{1,0:T(8,128)(2,1)S(1)} %collective-permute-done.25.kv1, bf16[656,256]{1,0:T(8,128)(2,1)S(1)} %copy-done.3, ...), custom_call_target="tpu_custom_call" | custom-call | flops 1024 | bytes 1024 | tf_op jit(solution)/shard_map/attend/pallas_call | solution.py:180
  183.7 17.5 %post.3 = (bf16[256,960]{1,0:T(8,128)(2,1)}, f32[256,960]{1,0:T(8,128)}, bf16[256,960]{1,0:T(8,128)(2,1)}, bf16[256,2560]{1,0:T(8,128)(2,1)}, bf16[256,2560]{1,0...) custom-call(s32[3]{0:T(128)} %pad_add_fusion.sc.refs_0_, bf16[960,256]{1,0:T(8,128)(2,1)} %copy-done.47, ...), custom_call_target="tpu_custom_call" | custom-call | flops 1024 | bytes 1024 | tf_op jit(solution)/shard_map/post/pallas_call | solution.py:340
  201.2 19.0 %back_start.1 = (bf16[256,960]{1,0:T(8,128)(2,1)}, bf16[256,2560]{1,0:T(8,128)(2,1)}, bf16[256,2560]{1,0:T(8,128)(2,1)}, f32[256,960]{1,0:T(8,128)}, bf16[3,256,...) custom-call(s32[3]{0:T(128)} %pad_add_fusion.sc.refs_0_, bf16[960,384]{1,0:T(8,128)(2,1)} %bitcast.30, ...), custom_call_target="tpu_custom_call" | custom-call | flops 1024 | bytes 1024 | tf_op jit(solution)/shard_map/back_start/pallas_call | solution.py:501
  223.0 12.6 %attend_back.2 = (bf16[3,256,384]{2,1,0:T(8,128)(2,1)S(1)}, bf16[3,256,384]{2,1,0:T(8,128)(2,1)S(1)}, f32[640,256]{1,0:T(8,128)S(1)}, bf16[640,256]{1,0:T(8,128)(2,1)S(1)}, f32[640,256]{1,0:T(8,128)S(1)}) custom-call(s32[3]{0:T(128)S(1)} %copy-done.41, bf16[3,256,384]{2,1,0:T(8,128)(2,1)S(1)} %copy-done.12, bf16[960,256]{1,0:T(8,128)(2,1)S(1)} %copy-done.24, ...), custom_call_target="tpu_custom_call" | custom-call | flops 1024 | bytes 1024 | tf_op jit(solution)/shard_map/attend_back/pallas_call | solution.py:233
  242.0 10.6 %collective-permute-done.31.rest_20_ = bf16[640,256]{1,0:T(8,128)(2,1)S(1)} collective-permute-done((bf16[640,256]{1,0:T(8,128)(2,1)S(1)}, bf16[640,256]{1,0:T(8,128)(2,1)S(1)}, u32[]{:S(2)}, u32[]{:S(2)}) %collective-permute-start.31) | collective-permute-done | bytes 327712 | tf_op jit(solution)/shard_map/ppermute | solution.py:963
  254.7 20.8 %back_join.1 = (bf16[256,384]{1,0:T(8,128)(2,1)}, bf16[256,384]{1,0:T(8,128)(2,1)}, bf16[256,384]{1,0:T(8,128)(2,1)}, f32[1,960]{1,0:T(1,128)}, bf16[256,960]{1,...) custom-call(s32[3]{0:T(128)} %pad_add_fusion.sc.refs_0_, ...), custom_call_target="tpu_custom_call" | custom-call | flops 1024 | bytes 1024 | tf_op jit(solution)/shard_map/back_join/pallas_call | solution.py:501
  275.6 3.2 collective-permute-done.40.rest_7_
  280.0 11.5 %grad_ffn.1 = (bf16[2,960,640]{2,1,0:T(8,128)(2,1)}, bf16[2,960,640]{2,1,0:T(8,128)(2,1)}, f32[8,128]{1,0:T(8,128)}) custom-call(s32[3]{0:T(128)} %pad_add_fusion.sc.refs_0_, bf16[256,960]{1,0:T(8,128)(2,1)} %get-tuple-element.155.rest_0_, bf16[256,960]{1,0:T(8,128)(2,1)} %get-tuple-element.131.rest_1_, bf16[256,960]{1,0:T(8,128)(2,1)} %copy-done.63, ...), custom_call_target="tpu_custom_call" | custom-call | flops 1024 | bytes 1024 | tf_op jit(solution)/shard_map/grad_ffn/pallas_call | solution.py:543
  291.5 1.6 collective-permute-start.46
  293.1 1.4 collective-permute-done.39.rest_0_.rest_18_
  295.3 12.6 %attend_back.3 = (bf16[3,256,384]{2,1,0:T(8,128)(2,1)S(1)}, bf16[3,256,384]{2,1,0:T(8,128)(2,1)S(1)}, f32[640,256]{1,0:T(8,128)S(1)}, bf16[640,256]{1,0:T(8,128)(2,1)S(1)}, f32[640,256]{1,0:T(8,128)S(1)}) custom-call(s32[3]{0:T(128)S(1)} %copy-done.42, bf16[3,256,384]{2,1,0:T(8,128)(2,1)S(1)} %copy-done.13, bf16[960,256]{1,0:T(8,128)(2,1)S(1)} %copy-done.23, ...), custom_call_target="tpu_custom_call" | custom-call | flops 1024 | bytes 1024 | tf_op jit(solution)/shard_map/attend_back/pallas_call | solution.py:233
  314.6 8.2 %grad_down.1 = (bf16[2,480,640]{2,1,0:T(8,128)(2,1)}, bf16[2,480,640]{2,1,0:T(8,128)(2,1)}, f32[8,128]{1,0:T(8,128)}) custom-call(s32[3]{0:T(128)} %pad_add_fusion.sc.refs_0_, bf16[256,960]{1,0:T(8,128)(2,1)} %get-tuple-element.152.rest_0_, bf16[256,960]{1,0:T(8,128)(2,1)} %get-tuple-element.173.rest_1_, bf16[256,960]{1,0:T(8,128)(2,1)} %copy-done.62, ...), custom_call_target="tpu_custom_call" | custom-call | flops 1024 | bytes 1024 | tf_op jit(solution)/shard_map/grad_down/pallas_call | solution.py:575
  322.7 2.7 collective-permute-start.50
  326.2 7.0 %back_end.1 = (bf16[256,384]{1,0:T(8,128)(2,1)}, bf16[256,384]{1,0:T(8,128)(2,1)}, bf16[256,384]{1,0:T(8,128)(2,1)}, f32[1,960]{1,0:T(1,128)}, bf16[1920,256]{1,0:T(8,128)(2,1)}) custom-call(s32[3]{0:T(128)} %pad_add_fusion.sc.refs_0_, bf16[960,384]{1,0:T(8,128)(2,1)} %bitcast.32, bf16[960,384]{1,0:T(8,128)(2,1)} %collective-permute-done.3.refs_1_.rest_1_, ...), custom_call_target="tpu_custom_call" | custom-call | flops 1024 | bytes 1024 | tf_op jit(solution)/shard_map/back_end/pallas_call | solution.py:501
  333.9 2.1 sum_first.3
  339.1 1.5 collective-permute-done.44.rest_17_
  341.6 10.6 %grad_attention.1 = (bf16[960,384]{1,0:T(8,128)(2,1)}, bf16[960,384]{1,0:T(8,128)(2,1)}, bf16[2,960,384]{2,1,0:T(8,128)(2,1)}, f32[8,128]{1,0:T(8,128)}) custom-call(s32[3]{0:T(128)} %pad_add_fusion.sc.refs_0_, bf16[256,960]{1,0:T(8,128)(2,1)} %get-tuple-element.154.rest_0_, bf16[256,960]{1,0:T(8,128)(2,1)} %get-tuple-element.130.rest_1_, ...), custom_call_target="tpu_custom_call" | custom-call | flops 1024 | bytes 1024 | tf_op jit(solution)/shard_map/grad_attention/pallas_call | solution.py:627
  355.0 1.6 sum_third.3
  357.9 4.5 collective-permute-start.56
  362.4 1.5 collective-permute-done.47.refs_2_
  363.9 7.9 %collective-permute-done.48.refs_3_ = bf16[960,384]{1,0:T(8,128)(2,1)S(1)} collective-permute-done((bf16[960,384]{1,0:T(8,128)(2,1)}, bf16[960,384]{1,0:T(8,128)(2,1)S(1)}, u32[]{:S(2)}, u32[]{:S(2)}) %collective-permute-start.48) | collective-permute-done | bytes 737312 | tf_op jit(solution)/shard_map/ppermute | solution.py:915
  374.8 11.9 %collective-permute-done.53.refs_2_ = bf16[2,240,640]{2,1,0:T(8,128)(2,1)S(1)} collective-permute-done((bf16[2,240,640]{2,1,0:T(8,128)(2,1)S(1)}, bf16[2,240,640]{2,1,0:T(8,128)(2,1)S(1)}, u32[]{:S(2)}, u32[]{:S(2)}) %collective-permute-start.53) | collective-permute-done | bytes 614432 | tf_op jit(solution)/shard_map/ppermute | solution.py:921
  391.2 4.4 collective-permute-start.54
  396.5 9.2 %collective-permute-done.55.refs_2_ = bf16[240,640]{1,0:T(8,128)(2,1)S(1)} collective-permute-done((bf16[240,640]{1,0:T(8,128)(2,1)S(1)}, bf16[240,640]{1,0:T(8,128)(2,1)S(1)}, u32[]{:S(2)}, u32[]{:S(2)}) %collective-permute-start.55) | collective-permute-done | bytes 307232 | tf_op jit(solution)/shard_map/ppermute | solution.py:921
  406.3 1.5 collective-permute-start.70
  408.5 2.2 collective-permute-start.59
  413.2 5.7 %collective-permute-done.60.refs_2_ = bf16[120,640]{1,0:T(8,128)(2,1)S(1)} collective-permute-done((bf16[120,640]{1,0:T(8,128)(2,1)S(1)}, bf16[120,640]{1,0:T(8,128)(2,1)S(1)}, u32[]{:S(2)}, u32[]{:S(2)}) %collective-permute-start.60) | collective-permute-done | bytes 153632 | tf_op jit(solution)/shard_map/ppermute | solution.py:915
  419.6 1.6 collective-permute-start.58
  421.3 1.7 collective-permute-start.77
  425.7 3.3 collective-permute-done.77.refs_4_
  429.0 1.8 collective-permute-start.63
  430.8 1.5 collective-permute-done.76.refs_3_
  434.5 2.9 collective-permute-done.63.rest_3_
  437.4 3.0 collective-permute-done.62.rest_2_
  443.6 2.3 lay_down.1
  445.9 2.4 lay.2
  450.6 3.8 lay.3
  454.4 2.4 convert_bitcast_fusion
  (318 shorter events, 77.8 us)
Async XLA Ops:
  6.0 13.0 %collective-permute-start.1 = (bf16[240,384]{1,0:T(8,128)(2,1)}, bf16[240,384]{1,0:T(8,128)(2,1)S(1)}, u32[]{:S(2)}, u32[]{:S(2)}) collective-permute-start(bf16[240,384]{1,0:T(8,128)(2,1)} %pick_first.1.rest_0_), channel_id=1, source_target_pairs={{0,2},{1,3},{2,0},{3,1},{4,6},{5,7},{6,4},{7,5},{8,10},{9,11},{10,... | collective-permute-start | bytes 552968 | tf_op jit(solution)/shard_map/ppermute | solution.py:921
  10.1 9.6 %collective-permute-start = (bf16[240,384]{1,0:T(8,128)(2,1)}, bf16[240,384]{1,0:T(8,128)(2,1)S(1)}, u32[]{:S(2)}, u32[]{:S(2)}) collective-permute-start(bf16[240,384]{1,0:T(8,128)(2,1)} %pick_first.1.rest_0_), channel_id=1, source_target_pairs={{0,1},{1,0},{2,3},{3,2},{4,5},{5,4},{6,7},{7,6},{8,9},{9,8},{10,11... | collective-permute-start | bytes 552968 | tf_op jit(solution)/shard_map/ppermute | solution.py:921
  18.9 5.7 %collective-permute-start.2 = (bf16[240,384]{1,0:T(8,128)(2,1)S(1)}, bf16[240,384]{1,0:T(8,128)(2,1)S(1)}, u32[]{:S(2)}, u32[]{:S(2)}) collective-permute-start(bf16[240,384]{1,0:T(8,128)(2,1)S(1)} %collective-permute-done.1.rest_2_), channel_id=1, source_target_pairs={{0,1},{1,0},{2,3},{3,2},{4,5},{5,4},{6,7},{7,6},{8,9},{9,8},{10,11... | collective-permute-start | bytes 552968 | tf_op jit(solution)/shard_map/ppermute | solution.py:921
  26.2 19.6 %collective-permute-start.3 = (bf16[960,384]{1,0:T(8,128)(2,1)S(1)}, bf16[960,384]{1,0:T(8,128)(2,1)}, u32[]{:S(2)}, u32[]{:S(2)}) collective-permute-start(bf16[960,384]{1,0:T(8,128)(2,1)S(1)} %bitcast.24), channel_id=1, source_target_pairs={{0,8},{4,20},{8,0},{12,28},{16,24},{20,4},{24,16},{28,12},{1,9},{5... | collective-permute-start | bytes 2211848 | tf_op jit(solution)/shard_map/ppermute | solution.py:915
  27.7 25.2 %collective-permute-start.4 = (bf16[960,384]{1,0:T(8,128)(2,1)S(1)}, bf16[960,384]{1,0:T(8,128)(2,1)}, u32[]{:S(2)}, u32[]{:S(2)}) collective-permute-start(bf16[960,384]{1,0:T(8,128)(2,1)S(1)} %bitcast.25), channel_id=1, source_target_pairs={{0,16},{4,12},{8,24},{12,4},{16,0},{20,28},{24,8},{28,20},{1,17},{... | collective-permute-start | bytes 2211848 | tf_op jit(solution)/shard_map/ppermute | solution.py:915
  29.2 23.3 %collective-permute-start.11 = (bf16[368,640]{1,0:T(8,128)(2,1)S(1)}, bf16[368,640]{1,0:T(8,128)(2,1)S(1)}, u32[]{:S(2)}, u32[]{:S(2)}) collective-permute-start(bf16[368,640]{1,0:T(8,128)(2,1)S(1)} %pick.1.rest_4_.rest_0_), channel_id=1, source_target_pairs={{0,2},{1,3},{2,0},{3,1},{4,6},{5,7},{6,4},{7,5},{8,10},{9,11},{10,... | collective-permute-start | bytes 1413128 | tf_op jit(solution)/shard_map/ppermute | solution.py:921
  32.5 20.5 %collective-permute-start.10 = (bf16[368,640]{1,0:T(8,128)(2,1)S(1)}, bf16[368,640]{1,0:T(8,128)(2,1)S(1)}, u32[]{:S(2)}, u32[]{:S(2)}) collective-permute-start(bf16[368,640]{1,0:T(8,128)(2,1)S(1)} %pick.1.rest_4_.rest_0_), channel_id=1, source_target_pairs={{0,1},{1,0},{2,3},{3,2},{4,5},{5,4},{6,7},{7,6},{8,9},{9,8},{10,11... | collective-permute-start | bytes 1413128 | tf_op jit(solution)/shard_map/ppermute | solution.py:921
  45.7 18.6 %collective-permute-start.5 = (bf16[960,384]{1,0:T(8,128)(2,1)}, bf16[960,384]{1,0:T(8,128)(2,1)S(1)}, u32[]{:S(2)}, u32[]{:S(2)}) collective-permute-start(bf16[960,384]{1,0:T(8,128)(2,1)} %collective-permute-done.3.refs_1_.rest_1_), channel_id=1, source_target_pairs={{0,16},{4,12},{8,24},{12,4},{16,0},{20,28},{24,8},{28,20},{1,17},{... | collective-permute-start | bytes 2211848 | tf_op jit(solution)/shard_map/ppermute | solution.py:915
  52.9 11.4 %collective-permute-start.12 = (bf16[368,640]{1,0:T(8,128)(2,1)S(1)}, bf16[368,640]{1,0:T(8,128)(2,1)S(1)}, u32[]{:S(2)}, u32[]{:S(2)}) collective-permute-start(bf16[368,640]{1,0:T(8,128)(2,1)S(1)} %hold.4.rest_2_), channel_id=1, source_target_pairs={{0,1},{1,0},{2,3},{3,2},{4,5},{5,4},{6,7},{7,6},{8,9},{9,8},{10,11... | collective-permute-start | bytes 1413128 | tf_op jit(solution)/shard_map/ppermute | solution.py:921
  67.3 41.3 %collective-permute-start.16 = (bf16[4,368,640]{2,1,0:T(8,128)(2,1)}, bf16[4,368,640]{2,1,0:T(8,128)(2,1)S(1)}, u32[]{:S(2)}, u32[]{:S(2)}) collective-permute-start(bf16[4,368,640]{2,1,0:T(8,128)(2,1)} %stack.31.rest_8_), channel_id=1, source_target_pairs={{0,16},{4,12},{8,24},{12,4},{16,0},{20,28},{24,8},{28,20},{1,17},{... | collective-permute-start | bytes 5652488 | tf_op jit(solution)/shard_map/ppermute | solution.py:915
  67.9 40.7 %collective-permute-start.13 = (bf16[4,368,640]{2,1,0:T(8,128)(2,1)}, bf16[4,368,640]{2,1,0:T(8,128)(2,1)}, u32[]{:S(2)}, u32[]{:S(2)}) collective-permute-start(bf16[4,368,640]{2,1,0:T(8,128)(2,1)} %stack.31.rest_8_), channel_id=1, source_target_pairs={{0,8},{4,20},{8,0},{12,28},{16,24},{20,4},{24,16},{28,12},{1,9},{5... | collective-permute-start | bytes 5652488 | tf_op jit(solution)/shard_map/ppermute | solution.py:915
  68.4 11.2 %collective-permute-start.6 = (bf16[960,384]{1,0:T(8,128)(2,1)S(1)}, bf16[960,384]{1,0:T(8,128)(2,1)S(1)}, u32[]{:S(2)}, u32[]{:S(2)}) collective-permute-start(bf16[960,384]{1,0:T(8,128)(2,1)S(1)} %bitcast.26), channel_id=1, source_target_pairs={{0,4},{4,0},{8,12},{12,8},{16,20},{20,16},{24,28},{28,24},{1,5},{5... | collective-permute-start | bytes 2211848 | tf_op jit(solution)/shard_map/ppermute | solution.py:915
  68.5 5.3 %collective-permute-start.14 = (bf16[976,256]{1,0:T(8,128)(2,1)S(1)}, bf16[976,256]{1,0:T(8,128)(2,1)S(1)}, u32[]{:S(2)}, u32[]{:S(2)}) collective-permute-start(bf16[976,256]{1,0:T(8,128)(2,1)S(1)} %pad_maximum_fusion), channel_id=1, source_target_pairs={{0,0},{1,4},{2,1},{3,5},{4,2},{5,6},{6,3},{7,7},{8,8},{9,12},{10,9... | collective-permute-start | bytes 1499144 | tf_op jit(solution)/shard_map/ppermute | solution.py:932
  69.2 14.1 %collective-permute-start.8 = (bf16[960,384]{1,0:T(8,128)(2,1)}, bf16[960,384]{1,0:T(8,128)(2,1)}, u32[]{:S(2)}, u32[]{:S(2)}) collective-permute-start(bf16[960,384]{1,0:T(8,128)(2,1)} %collective-permute-done.4.refs_2_.rest_2_), channel_id=1, source_target_pairs={{0,4},{4,0},{8,12},{12,8},{16,20},{20,16},{24,28},{28,24},{1,5},{5... | collective-permute-start | bytes 2211848 | tf_op jit(solution)/shard_map/ppermute | solution.py:915
  73.7 9.5 %collective-permute-start.7 = (bf16[960,384]{1,0:T(8,128)(2,1)}, bf16[960,384]{1,0:T(8,128)(2,1)}, u32[]{:S(2)}, u32[]{:S(2)}) collective-permute-start(bf16[960,384]{1,0:T(8,128)(2,1)} %collective-permute-done.3.refs_1_.rest_1_), channel_id=1, source_target_pairs={{0,4},{4,0},{8,12},{12,8},{16,20},{20,16},{24,28},{28,24},{1,5},{5... | collective-permute-start | bytes 2211848 | tf_op jit(solution)/shard_map/ppermute | solution.py:915
  90.7 17.1 %collective-permute-start.15 = (bf16[656,256]{1,0:T(8,128)(2,1)}, bf16[656,256]{1,0:T(8,128)(2,1)S(1)}, u32[]{:S(2)}, u32[]{:S(2)}) collective-permute-start(bf16[656,256]{1,0:T(8,128)(2,1)} %get-tuple-element.124.kv2.rest_16_), channel_id=1, source_target_pairs={{0,1},{2,3},{4,5},{6,7},{8,9},{10,11},{12,13},{14,15},{16,17},{18,... | collective-permute-start | bytes 1007624 | tf_op jit(solution)/shard_map/ppermute | solution.py:954
  108.6 24.1 %collective-permute-start.17 = (bf16[4,368,640]{2,1,0:T(8,128)(2,1)}, bf16[4,368,640]{2,1,0:T(8,128)(2,1)}, u32[]{:S(2)}, u32[]{:S(2)}) collective-permute-start(bf16[4,368,640]{2,1,0:T(8,128)(2,1)} %hold.5.rest_9_), channel_id=1, source_target_pairs={{0,16},{4,12},{8,24},{12,4},{16,0},{20,28},{24,8},{28,20},{1,17},{... | collective-permute-start | bytes 5652488 | tf_op jit(solution)/shard_map/ppermute | solution.py:915
  109.2 23.6 %collective-permute-start.19 = (bf16[4,368,640]{2,1,0:T(8,128)(2,1)}, bf16[4,368,640]{2,1,0:T(8,128)(2,1)S(1)}, u32[]{:S(2)}, u32[]{:S(2)}) collective-permute-start(bf16[4,368,640]{2,1,0:T(8,128)(2,1)} %stack.31.rest_8_), channel_id=1, source_target_pairs={{0,4},{4,0},{8,12},{12,8},{16,20},{20,16},{24,28},{28,24},{1,5},{5... | collective-permute-start | bytes 5652488 | tf_op jit(solution)/shard_map/ppermute | solution.py:915
  121.0 13.2 %collective-permute-start.20 = (bf16[4,368,640]{2,1,0:T(8,128)(2,1)}, bf16[4,368,640]{2,1,0:T(8,128)(2,1)}, u32[]{:S(2)}, u32[]{:S(2)}) collective-permute-start(bf16[4,368,640]{2,1,0:T(8,128)(2,1)} %hold.5.rest_9_), channel_id=1, source_target_pairs={{0,4},{4,0},{8,12},{12,8},{16,20},{20,16},{24,28},{28,24},{1,5},{5... | collective-permute-start | bytes 5652488 | tf_op jit(solution)/shard_map/ppermute | solution.py:915
  121.2 11.6 %collective-permute-start.21 = (bf16[4,368,640]{2,1,0:T(8,128)(2,1)S(1)}, bf16[4,368,640]{2,1,0:T(8,128)(2,1)S(1)}, u32[]{:S(2)}, u32[]{:S(2)}) collective-permute-start(bf16[4,368,640]{2,1,0:T(8,128)(2,1)S(1)} %collective-permute-done.16.refs_2_.rest_10_), channel_id=1, source_target_pairs={{0,4},{4,0},{8,12},{12,8},{16,20},{20,16},{24,28},{28,24},{1,5},{5... | collective-permute-start | bytes 5652488 | tf_op jit(solution)/shard_map/ppermute | solution.py:915
  132.8 4.2 collective-permute-start.22
  155.2 15.2 %collective-permute-start.29 = (bf16[256,2560]{1,0:T(8,128)(2,1)}, bf16[256,2560]{1,0:T(8,128)(2,1)S(1)}, u32[]{:S(2)}, u32[]{:S(2)}) collective-permute-start(bf16[256,2560]{1,0:T(8,128)(2,1)} %get-tuple-element.133.rest_5_), channel_id=1, source_target_pairs={{0,4},{4,0},{8,12},{12,8},{16,20},{20,16},{24,28},{28,24},{1,5},{5... | collective-permute-start | bytes 3932168 | tf_op jit(solution)/shard_map/ppermute | solution.py:915
  155.4 12.2 %collective-permute-start.24 = (bf16[656,256]{1,0:T(8,128)(2,1)}, bf16[656,256]{1,0:T(8,128)(2,1)S(1)}, u32[]{:S(2)}, u32[]{:S(2)}) collective-permute-start(bf16[656,256]{1,0:T(8,128)(2,1)} %get-tuple-element.129.kv2.rest_16_), channel_id=1, source_target_pairs={{0,1},{2,3},{4,5},{6,7},{8,9},{10,11},{12,13},{14,15},{16,17},{18,... | collective-permute-start | bytes 1007624 | tf_op jit(solution)/shard_map/ppermute | solution.py:954
  159.1 9.5 %collective-permute-start.26 = (bf16[256,960]{1,0:T(8,128)(2,1)S(1)}, bf16[256,960]{1,0:T(8,128)(2,1)S(1)}, u32[]{:S(2)}, u32[]{:S(2)}) collective-permute-start(bf16[256,960]{1,0:T(8,128)(2,1)S(1)} %copy-done.67), channel_id=1, source_target_pairs={{0,4},{4,0},{8,12},{12,8},{16,20},{20,16},{24,28},{28,24},{1,5},{5... | collective-permute-start | bytes 1474568 | tf_op jit(solution)/shard_map/ppermute | solution.py:915
  159.2 23.7 %collective-permute-start.23 = (bf16[960,256]{1,0:T(8,128)(2,1)S(1)}, bf16[960,256]{1,0:T(8,128)(2,1)S(1)}, u32[]{:S(2)}, u32[]{:S(2)}) collective-permute-start(bf16[960,256]{1,0:T(8,128)(2,1)S(1)} %bitcast.40), channel_id=1, source_target_pairs={{0,0},{1,4},{2,1},{3,5},{4,2},{5,6},{6,3},{7,7},{8,8},{9,12},{10,9... | collective-permute-start | bytes 1474568 | tf_op jit(solution)/shard_map/ppermute | solution.py:932
  159.9 8.8 %collective-permute-start.27 = (bf16[256,960]{1,0:T(8,128)(2,1)}, bf16[256,960]{1,0:T(8,128)(2,1)S(1)}, u32[]{:S(2)}, u32[]{:S(2)}) collective-permute-start(bf16[256,960]{1,0:T(8,128)(2,1)} %get-tuple-element.131.rest_1_), channel_id=1, source_target_pairs={{0,4},{4,0},{8,12},{12,8},{16,20},{20,16},{24,28},{28,24},{1,5},{5... | collective-permute-start | bytes 1474568 | tf_op jit(solution)/shard_map/ppermute | solution.py:915
  168.7 68.2 %collective-permute-start.35 = (bf16[256,960]{1,0:T(8,128)(2,1)}, bf16[256,960]{1,0:T(8,128)(2,1)}, u32[]{:S(2)}, u32[]{:S(2)}) collective-permute-start(bf16[256,960]{1,0:T(8,128)(2,1)} %get-tuple-element.154.rest_0_), channel_id=1, source_target_pairs={{0,4},{4,0},{8,12},{12,8},{16,20},{20,16},{24,28},{28,24},{1,5},{5... | collective-permute-start | bytes 1474568 | tf_op jit(solution)/shard_map/ppermute | solution.py:915
  220.2 32.3 %collective-permute-start.34 = (bf16[256,2560]{1,0:T(8,128)(2,1)}, bf16[256,2560]{1,0:T(8,128)(2,1)S(1)}, u32[]{:S(2)}, u32[]{:S(2)}) collective-permute-start(bf16[256,2560]{1,0:T(8,128)(2,1)} %get-tuple-element.153), channel_id=1, source_target_pairs={{0,4},{4,0},{8,12},{12,8},{16,20},{20,16},{24,28},{28,24},{1,5},{5... | collective-permute-start | bytes 3932168 | tf_op jit(solution)/shard_map/ppermute | solution.py:915
  220.3 32.2 %collective-permute-start.38 = (bf16[256,2560]{1,0:T(8,128)(2,1)}, bf16[256,2560]{1,0:T(8,128)(2,1)S(1)}, u32[]{:S(2)}, u32[]{:S(2)}) collective-permute-start(bf16[256,2560]{1,0:T(8,128)(2,1)} %get-tuple-element.157.rest_4_), channel_id=1, source_target_pairs={{0,4},{4,0},{8,12},{12,8},{16,20},{20,16},{24,28},{28,24},{1,5},{5... | collective-permute-start | bytes 3932168 | tf_op jit(solution)/shard_map/ppermute | solution.py:915
  220.8 17.7 %collective-permute-start.36 = (bf16[256,960]{1,0:T(8,128)(2,1)}, bf16[256,960]{1,0:T(8,128)(2,1)S(1)}, u32[]{:S(2)}, u32[]{:S(2)}) collective-permute-start(bf16[256,960]{1,0:T(8,128)(2,1)} %get-tuple-element.155.rest_0_), channel_id=1, source_target_pairs={{0,4},{4,0},{8,12},{12,8},{16,20},{20,16},{24,28},{28,24},{1,5},{5... | collective-permute-start | bytes 1474568 | tf_op jit(solution)/shard_map/ppermute | solution.py:915
  240.6 11.9 %collective-permute-start.31 = (bf16[640,256]{1,0:T(8,128)(2,1)S(1)}, bf16[640,256]{1,0:T(8,128)(2,1)S(1)}, u32[]{:S(2)}, u32[]{:S(2)}) collective-permute-start(bf16[640,256]{1,0:T(8,128)(2,1)S(1)} %get-tuple-element.147), channel_id=1, source_target_pairs={{1,0},{3,2},{5,4},{7,6},{9,8},{11,10},{13,12},{15,14},{17,16},{19,... | collective-permute-start | bytes 983048 | tf_op jit(solution)/shard_map/ppermute | solution.py:963
  291.5 41.7 %collective-permute-start.46 = (bf16[2,960,640]{2,1,0:T(8,128)(2,1)}, bf16[2,960,640]{2,1,0:T(8,128)(2,1)S(1)}, u32[]{:S(2)}, u32[]{:S(2)}) collective-permute-start(bf16[2,960,640]{2,1,0:T(8,128)(2,1)} %get-tuple-element.188), channel_id=1, source_target_pairs={{0,8},{4,20},{8,0},{12,28},{16,24},{20,4},{24,16},{28,12},{1,9},{5... | collective-permute-start | bytes 7372808 | tf_op jit(solution)/shard_map/ppermute | solution.py:915
  309.8 4.0 collective-permute-start.43
  312.5 13.0 %collective-permute-start.42 = (bf16[640,256]{1,0:T(8,128)(2,1)S(1)}, bf16[640,256]{1,0:T(8,128)(2,1)S(1)}, u32[]{:S(2)}, u32[]{:S(2)}) collective-permute-start(bf16[640,256]{1,0:T(8,128)(2,1)S(1)} %get-tuple-element.171), channel_id=1, source_target_pairs={{1,0},{3,2},{5,4},{7,6},{9,8},{11,10},{13,12},{15,14},{17,16},{19,... | collective-permute-start | bytes 983048 | tf_op jit(solution)/shard_map/ppermute | solution.py:963
  322.7 31.6 %collective-permute-start.50 = (bf16[2,480,640]{2,1,0:T(8,128)(2,1)}, bf16[2,480,640]{2,1,0:T(8,128)(2,1)}, u32[]{:S(2)}, u32[]{:S(2)}) collective-permute-start(bf16[2,480,640]{2,1,0:T(8,128)(2,1)} %get-tuple-element.196), channel_id=1, source_target_pairs={{0,1},{1,0},{2,3},{3,2},{4,5},{5,4},{6,7},{7,6},{8,9},{9,8},{10,11... | collective-permute-start | bytes 3686408 | tf_op jit(solution)/shard_map/ppermute | solution.py:921
  337.4 19.1 %collective-permute-start.49 = (bf16[960,640]{1,0:T(8,128)(2,1)}, bf16[960,640]{1,0:T(8,128)(2,1)S(1)}, u32[]{:S(2)}, u32[]{:S(2)}) collective-permute-start(bf16[960,640]{1,0:T(8,128)(2,1)} %get-tuple-element.194), channel_id=1, source_target_pairs={{0,16},{4,12},{8,24},{12,4},{16,0},{20,28},{24,8},{28,20},{1,17},{... | collective-permute-start | bytes 3686408 | tf_op jit(solution)/shard_map/ppermute | solution.py:915
  352.2 11.7 %collective-permute-start.47 = (bf16[960,384]{1,0:T(8,128)(2,1)}, bf16[960,384]{1,0:T(8,128)(2,1)S(1)}, u32[]{:S(2)}, u32[]{:S(2)}) collective-permute-start(bf16[960,384]{1,0:T(8,128)(2,1)} %get-tuple-element.191), channel_id=1, source_target_pairs={{0,8},{4,20},{8,0},{12,28},{16,24},{20,4},{24,16},{28,12},{1,9},{5... | collective-permute-start | bytes 2211848 | tf_op jit(solution)/shard_map/ppermute | solution.py:915
  353.1 18.7 %collective-permute-start.48 = (bf16[960,384]{1,0:T(8,128)(2,1)}, bf16[960,384]{1,0:T(8,128)(2,1)S(1)}, u32[]{:S(2)}, u32[]{:S(2)}) collective-permute-start(bf16[960,384]{1,0:T(8,128)(2,1)} %get-tuple-element.192), channel_id=1, source_target_pairs={{0,8},{4,20},{8,0},{12,28},{16,24},{20,4},{24,16},{28,12},{1,9},{5... | collective-permute-start | bytes 2211848 | tf_op jit(solution)/shard_map/ppermute | solution.py:915
  357.6 29.2 %collective-permute-start.53 = (bf16[2,240,640]{2,1,0:T(8,128)(2,1)S(1)}, bf16[2,240,640]{2,1,0:T(8,128)(2,1)S(1)}, u32[]{:S(2)}, u32[]{:S(2)}) collective-permute-start(bf16[2,240,640]{2,1,0:T(8,128)(2,1)S(1)} %get-tuple-element.204), channel_id=1, source_target_pairs={{0,1},{1,0},{2,3},{3,2},{4,5},{5,4},{6,7},{7,6},{8,9},{9,8},{10,11... | collective-permute-start | bytes 1843208 | tf_op jit(solution)/shard_map/ppermute | solution.py:921
  357.9 30.3 %collective-permute-start.56 = (bf16[480,640]{1,0:T(8,128)(2,1)S(1)}, bf16[480,640]{1,0:T(8,128)(2,1)S(1)}, u32[]{:S(2)}, u32[]{:S(2)}) collective-permute-start(bf16[480,640]{1,0:T(8,128)(2,1)S(1)} %get-tuple-element.212), channel_id=1, source_target_pairs={{0,2},{1,3},{2,0},{3,1},{4,6},{5,7},{6,4},{7,5},{8,10},{9,11},{10,... | collective-permute-start | bytes 1843208 | tf_op jit(solution)/shard_map/ppermute | solution.py:921
  372.7 14.7 %collective-permute-start.51 = (bf16[480,384]{1,0:T(8,128)(2,1)S(1)}, bf16[480,384]{1,0:T(8,128)(2,1)S(1)}, u32[]{:S(2)}, u32[]{:S(2)}) collective-permute-start(bf16[480,384]{1,0:T(8,128)(2,1)S(1)} %get-tuple-element.201), channel_id=1, source_target_pairs={{0,16},{4,12},{8,24},{12,4},{16,0},{20,28},{24,8},{28,20},{1,17},{... | collective-permute-start | bytes 1105928 | tf_op jit(solution)/shard_map/ppermute | solution.py:915
  373.6 13.8 %collective-permute-start.52 = (bf16[480,384]{1,0:T(8,128)(2,1)S(1)}, bf16[480,384]{1,0:T(8,128)(2,1)S(1)}, u32[]{:S(2)}, u32[]{:S(2)}) collective-permute-start(bf16[480,384]{1,0:T(8,128)(2,1)S(1)} %get-tuple-element.202), channel_id=1, source_target_pairs={{0,16},{4,12},{8,24},{12,4},{16,0},{20,28},{24,8},{28,20},{1,17},{... | collective-permute-start | bytes 1105928 | tf_op jit(solution)/shard_map/ppermute | solution.py:915
  389.0 6.9 %collective-permute-start.57 = (bf16[2,120,640]{2,1,0:T(8,128)(2,1)S(1)}, bf16[2,120,640]{2,1,0:T(8,128)(2,1)S(1)}, u32[]{:S(2)}, u32[]{:S(2)}) collective-permute-start(bf16[2,120,640]{2,1,0:T(8,128)(2,1)S(1)} %get-tuple-element.215), channel_id=1, source_target_pairs={{0,8},{4,20},{8,0},{12,28},{16,24},{20,4},{24,16},{28,12},{1,9},{5... | collective-permute-start | bytes 921608 | tf_op jit(solution)/shard_map/ppermute | solution.py:915
  389.9 15.8 %collective-permute-start.55 = (bf16[240,640]{1,0:T(8,128)(2,1)S(1)}, bf16[240,640]{1,0:T(8,128)(2,1)S(1)}, u32[]{:S(2)}, u32[]{:S(2)}) collective-permute-start(bf16[240,640]{1,0:T(8,128)(2,1)S(1)} %get-tuple-element.210), channel_id=1, source_target_pairs={{0,2},{1,3},{2,0},{3,1},{4,6},{5,7},{6,4},{7,5},{8,10},{9,11},{10,... | collective-permute-start | bytes 921608 | tf_op jit(solution)/shard_map/ppermute | solution.py:921
  391.2 16.7 %collective-permute-start.54 = (bf16[2,240,384]{2,1,0:T(8,128)(2,1)S(1)}, bf16[2,240,384]{2,1,0:T(8,128)(2,1)S(1)}, u32[]{:S(2)}, u32[]{:S(2)}) collective-permute-start(bf16[2,240,384]{2,1,0:T(8,128)(2,1)S(1)} %get-tuple-element.208), channel_id=1, source_target_pairs={{0,1},{1,0},{2,3},{3,2},{4,5},{5,4},{6,7},{7,6},{8,9},{9,8},{10,11... | collective-permute-start | bytes 1105928 | tf_op jit(solution)/shard_map/ppermute | solution.py:921
  406.3 14.9 %collective-permute-start.70 = (bf16[240,640]{1,0:T(8,128)(2,1)S(1)}, bf16[240,640]{1,0:T(8,128)(2,1)S(1)}, u32[]{:S(2)}, u32[]{:S(2)}) collective-permute-start(bf16[240,640]{1,0:T(8,128)(2,1)S(1)} %get-tuple-element.232.rest_0_), channel_id=1, source_target_pairs={{0,24},{4,28},{8,16},{12,20},{16,8},{20,12},{24,0},{28,4},{1,25},{... | collective-permute-start | bytes 921608 | tf_op jit(solution)/shard_map/ppermute | solution.py:915
  408.5 11.1 %collective-permute-start.59 = (bf16[240,384]{1,0:T(8,128)(2,1)S(1)}, bf16[240,384]{1,0:T(8,128)(2,1)S(1)}, u32[]{:S(2)}, u32[]{:S(2)}) collective-permute-start(bf16[240,384]{1,0:T(8,128)(2,1)S(1)} %get-tuple-element.221), channel_id=1, source_target_pairs={{0,2},{1,3},{2,0},{3,1},{4,6},{5,7},{6,4},{7,5},{8,10},{9,11},{10,... | collective-permute-start | bytes 552968 | tf_op jit(solution)/shard_map/ppermute | solution.py:921
  410.7 8.3 %collective-permute-start.60 = (bf16[120,640]{1,0:T(8,128)(2,1)S(1)}, bf16[120,640]{1,0:T(8,128)(2,1)S(1)}, u32[]{:S(2)}, u32[]{:S(2)}) collective-permute-start(bf16[120,640]{1,0:T(8,128)(2,1)S(1)} %get-tuple-element.223), channel_id=1, source_target_pairs={{0,16},{4,12},{8,24},{12,4},{16,0},{20,28},{24,8},{28,20},{1,17},{... | collective-permute-start | bytes 460808 | tf_op jit(solution)/shard_map/ppermute | solution.py:915
  411.6 12.0 %collective-permute-start.69 = (bf16[240,640]{1,0:T(8,128)(2,1)S(1)}, bf16[240,640]{1,0:T(8,128)(2,1)S(1)}, u32[]{:S(2)}, u32[]{:S(2)}) collective-permute-start(bf16[240,640]{1,0:T(8,128)(2,1)S(1)} %get-tuple-element.232.rest_0_), channel_id=1, source_target_pairs={{0,16},{4,12},{8,24},{12,4},{16,0},{20,28},{24,8},{28,20},{1,17},{... | collective-permute-start | bytes 921608 | tf_op jit(solution)/shard_map/ppermute | solution.py:915
  412.7 12.0 %collective-permute-start.68 = (bf16[240,640]{1,0:T(8,128)(2,1)S(1)}, bf16[240,640]{1,0:T(8,128)(2,1)S(1)}, u32[]{:S(2)}, u32[]{:S(2)}) collective-permute-start(bf16[240,640]{1,0:T(8,128)(2,1)S(1)} %get-tuple-element.232.rest_0_), channel_id=1, source_target_pairs={{0,8},{4,20},{8,0},{12,28},{16,24},{20,4},{24,16},{28,12},{1,9},{5... | collective-permute-start | bytes 921608 | tf_op jit(solution)/shard_map/ppermute | solution.py:915
  419.5 5.9 %collective-permute-start.78 = (bf16[120,640]{1,0:T(8,128)(2,1)S(1)}, bf16[120,640]{1,0:T(8,128)(2,1)S(1)}, u32[]{:S(2)}, u32[]{:S(2)}) collective-permute-start(bf16[120,640]{1,0:T(8,128)(2,1)S(1)} %get-tuple-element.235.refs_1_), channel_id=1, source_target_pairs={{0,4},{4,0},{8,12},{12,8},{16,20},{20,16},{24,28},{28,24},{1,5},{5... | collective-permute-start | bytes 460808 | tf_op jit(solution)/shard_map/ppermute | solution.py:915
  419.6 34.8 %collective-permute-start.58 = (bf16[1920,256]{1,0:T(8,128)(2,1)S(1)}, bf16[1920,256]{1,0:T(8,128)(2,1)}, u32[]{:S(2)}, u32[]{:S(2)}) collective-permute-start(bf16[1920,256]{1,0:T(8,128)(2,1)S(1)} %hold.7), channel_id=1, source_target_pairs={{0,0},{4,1},{1,2},{5,3},{2,4},{6,5},{3,6},{7,7},{8,8},{12,9},{9,10... | collective-permute-start | bytes 2949128 | tf_op jit(solution)/shard_map/ppermute | solution.py:932
  421.3 7.7 %collective-permute-start.77 = (bf16[120,640]{1,0:T(8,128)(2,1)S(1)}, bf16[120,640]{1,0:T(8,128)(2,1)S(1)}, u32[]{:S(2)}, u32[]{:S(2)}) collective-permute-start(bf16[120,640]{1,0:T(8,128)(2,1)S(1)} %get-tuple-element.235.refs_1_), channel_id=1, source_target_pairs={{0,24},{4,28},{8,16},{12,20},{16,8},{20,12},{24,0},{28,4},{1,25},{... | collective-permute-start | bytes 460808 | tf_op jit(solution)/shard_map/ppermute | solution.py:915
  423.6 8.7 %collective-permute-start.76 = (bf16[120,640]{1,0:T(8,128)(2,1)S(1)}, bf16[120,640]{1,0:T(8,128)(2,1)S(1)}, u32[]{:S(2)}, u32[]{:S(2)}) collective-permute-start(bf16[120,640]{1,0:T(8,128)(2,1)S(1)} %get-tuple-element.235.refs_1_), channel_id=1, source_target_pairs={{0,16},{4,12},{8,24},{12,4},{16,0},{20,28},{24,8},{28,20},{1,17},{... | collective-permute-start | bytes 460808 | tf_op jit(solution)/shard_map/ppermute | solution.py:915
  424.7 8.7 %collective-permute-start.75 = (bf16[120,640]{1,0:T(8,128)(2,1)S(1)}, bf16[120,640]{1,0:T(8,128)(2,1)S(1)}, u32[]{:S(2)}, u32[]{:S(2)}) collective-permute-start(bf16[120,640]{1,0:T(8,128)(2,1)S(1)} %get-tuple-element.235.refs_1_), channel_id=1, source_target_pairs={{0,8},{4,20},{8,0},{12,28},{16,24},{20,4},{24,16},{28,12},{1,9},{5... | collective-permute-start | bytes 460808 | tf_op jit(solution)/shard_map/ppermute | solution.py:915
  425.4 9.1 %collective-permute-start.64 = (bf16[240,384]{1,0:T(8,128)(2,1)S(1)}, bf16[240,384]{1,0:T(8,128)(2,1)S(1)}, u32[]{:S(2)}, u32[]{:S(2)}) collective-permute-start(bf16[240,384]{1,0:T(8,128)(2,1)S(1)} %get-tuple-element.225.rest_0_), channel_id=1, source_target_pairs={{0,4},{4,0},{8,12},{12,8},{16,20},{20,16},{24,28},{28,24},{1,5},{5... | collective-permute-start | bytes 552968 | tf_op jit(solution)/shard_map/ppermute | solution.py:915
  429.0 8.4 %collective-permute-start.63 = (bf16[240,384]{1,0:T(8,128)(2,1)S(1)}, bf16[240,384]{1,0:T(8,128)(2,1)S(1)}, u32[]{:S(2)}, u32[]{:S(2)}) collective-permute-start(bf16[240,384]{1,0:T(8,128)(2,1)S(1)} %get-tuple-element.225.rest_0_), channel_id=1, source_target_pairs={{0,24},{4,28},{8,16},{12,20},{16,8},{20,12},{24,0},{28,4},{1,25},{... | collective-permute-start | bytes 552968 | tf_op jit(solution)/shard_map/ppermute | solution.py:915
  432.3 8.1 %collective-permute-start.62 = (bf16[240,384]{1,0:T(8,128)(2,1)S(1)}, bf16[240,384]{1,0:T(8,128)(2,1)S(1)}, u32[]{:S(2)}, u32[]{:S(2)}) collective-permute-start(bf16[240,384]{1,0:T(8,128)(2,1)S(1)} %get-tuple-element.225.rest_0_), channel_id=1, source_target_pairs={{0,16},{4,12},{8,24},{12,4},{16,0},{20,28},{24,8},{28,20},{1,17},{... | collective-permute-start | bytes 552968 | tf_op jit(solution)/shard_map/ppermute | solution.py:915
  433.5 6.9 %collective-permute-start.61 = (bf16[240,384]{1,0:T(8,128)(2,1)S(1)}, bf16[240,384]{1,0:T(8,128)(2,1)S(1)}, u32[]{:S(2)}, u32[]{:S(2)}) collective-permute-start(bf16[240,384]{1,0:T(8,128)(2,1)S(1)} %get-tuple-element.225.rest_0_), channel_id=1, source_target_pairs={{0,8},{4,20},{8,0},{12,28},{16,24},{20,4},{24,16},{28,12},{1,9},{5... | collective-permute-start | bytes 552968 | tf_op jit(solution)/shard_map/ppermute | solution.py:915
  434.5 6.4 %collective-permute-start.81 = (bf16[120,640]{1,0:T(8,128)(2,1)S(1)}, bf16[120,640]{1,0:T(8,128)(2,1)S(1)}, u32[]{:S(2)}, u32[]{:S(2)}) collective-permute-start(bf16[120,640]{1,0:T(8,128)(2,1)S(1)} %collective-permute-done.77.refs_4_), channel_id=1, source_target_pairs={{0,4},{4,0},{8,12},{12,8},{16,20},{20,16},{24,28},{28,24},{1,5},{5... | collective-permute-start | bytes 460808 | tf_op jit(solution)/shard_map/ppermute | solution.py:915
  442.6 8.0 %collective-permute-start.71 = (bf16[240,640]{1,0:T(8,128)(2,1)S(1)}, bf16[240,640]{1,0:T(8,128)(2,1)S(1)}, u32[]{:S(2)}, u32[]{:S(2)}) collective-permute-start(bf16[240,640]{1,0:T(8,128)(2,1)S(1)} %get-tuple-element.232.rest_0_), channel_id=1, source_target_pairs={{0,4},{4,0},{8,12},{12,8},{16,20},{20,16},{24,28},{28,24},{1,5},{5... | collective-permute-start | bytes 921608 | tf_op jit(solution)/shard_map/ppermute | solution.py:915
  442.8 7.8 %collective-permute-start.74 = (bf16[240,640]{1,0:T(8,128)(2,1)S(1)}, bf16[240,640]{1,0:T(8,128)(2,1)}, u32[]{:S(2)}, u32[]{:S(2)}) collective-permute-start(bf16[240,640]{1,0:T(8,128)(2,1)S(1)} %collective-permute-done.70.rest_3_), channel_id=1, source_target_pairs={{0,4},{4,0},{8,12},{12,8},{16,20},{20,16},{24,28},{28,24},{1,5},{5... | collective-permute-start | bytes 921608 | tf_op jit(solution)/shard_map/ppermute | solution.py:915
  443.1 7.5 %collective-permute-start.73 = (bf16[240,640]{1,0:T(8,128)(2,1)S(1)}, bf16[240,640]{1,0:T(8,128)(2,1)}, u32[]{:S(2)}, u32[]{:S(2)}) collective-permute-start(bf16[240,640]{1,0:T(8,128)(2,1)S(1)} %collective-permute-done.69.rest_2_), channel_id=1, source_target_pairs={{0,4},{4,0},{8,12},{12,8},{16,20},{20,16},{24,28},{28,24},{1,5},{5... | collective-permute-start | bytes 921608 | tf_op jit(solution)/shard_map/ppermute | solution.py:915
  443.3 7.3 %collective-permute-start.72 = (bf16[240,640]{1,0:T(8,128)(2,1)S(1)}, bf16[240,640]{1,0:T(8,128)(2,1)}, u32[]{:S(2)}, u32[]{:S(2)}) collective-permute-start(bf16[240,640]{1,0:T(8,128)(2,1)S(1)} %collective-permute-done.68.rest_1_), channel_id=1, source_target_pairs={{0,4},{4,0},{8,12},{12,8},{16,20},{20,16},{24,28},{28,24},{1,5},{5... | collective-permute-start | bytes 921608 | tf_op jit(solution)/shard_map/ppermute | solution.py:915
  (99 other events, 851.5 us)

commit v15 on v14

--- a/solution.py
+++ b/solution.py
@@ -994,14 +994,14 @@
     parts_a = turns(pick_first(sc, query_weight, key_weight.T, value_weight.T, out_weight, gains))
     ids = jnp.broadcast_to((segment_ids[0] + 1).astype(bf16), (IDS, stretch))
     tokens = home_to_work(jnp.concatenate([tokens[0].T, ids]))
-    piece_b = pick(sc, gate_weight, up_weight, down_weight.T, parts_a[1:2])
-    whole_a = stack(sc, parts_a, [piece_b])
+    piece_b = pick(sc, gate_weight, up_weight, down_weight.T, [])
+    side_b = flip_z(piece_b, 1)
+    far_b = flip_z(piece_b, 2)
+    whole_a = stack(sc, parts_a, [far_b, side_b])
     gains = gains_of(whole_a)
     gain_a, gain_f = gains[:1], gains[1:]
     wa = plane_gather(whole_a.reshape(depth * rows, PIECE))
-    side_b = flip_z(piece_b, 1)
-    far_b = hold(flip_z(piece_b, 2), [wa[0][1], wa[0][2], side_b])
-    whole_b = stack(sc, (piece_b, side_b, far_b, flip_z(far_b, 1)), [wa[0][3]])
+    whole_b = stack(sc, (piece_b, side_b, far_b, flip_z(far_b, 1)), [wa[0][1], wa[0][2]])
     first_b, second_b = flip(whole_b, SIDE, BACK), flip(whole_b, BACK, SIDE)
 
     h_0, a0, q0, own = pre(sc, tokens, gain_a, cos, sin, *wa, [whole_b])
@@ -1009,15 +1009,15 @@
     first_b = hold(first_b, [kv0[0], second_b])
     opposite_b = flip(first_b, BACK, SIDE)
     o0, lse0 = attend(q0, kv0)
-    wb = whole_b, first_b, second_b, hold(opposite_b, [o0])
+    cot = home_to_work(cotangent[0].T)
+    wb = whole_b, first_b, second_b, hold(opposite_b, [o0, cot])
     wb = wb, across(wb)
     weights = wa, wb
-    cot = home_to_work(cotangent[0].T)
     mixed0, h1_0, b0, gate0, up0, z0, h_1, a1, q1, own = post(False, [], sc, o0, h_0, gain_f, gain_a, cos, sin, own, *weights)
     kv1 = window(own)
     across_0 = across((a0, b0, mixed0, z0))
     o1, lse1 = attend(q1, kv1, across_0)
-    mixed1, h1_1, b1, gate1, up1, z1, output = post(True, [cot], sc, o1, h_1, gain_f, gain_a, cos, sin, own, *weights)
+    mixed1, h1_1, b1, gate1, up1, z1, output = post(True, [], sc, o1, h_1, gain_f, gain_a, cos, sin, own, *weights)
     across_1 = across((a1, b1, mixed1, z1))
 
     gb1, act1, away1, g1, p1, dgain_f1, do = back(True, False, sc, weights, [cot], [gate1, up1, h1_1, gain_f])
@@ -1037,7 +1037,7 @@
     got_d = flip_z(send_d, 1)
     (three0,) = across((three0,))
     tail = [g1, dq0, own, near, far, h_0, gain_a, cos, sin, output]
-    dk0, dv0, one0, dgain_a0, leaving = back(False, True, sc, weights, tail, None, [done])
+    dk0, dv0, one0, dgain_a0, leaving = back(False, True, sc, weights, tail, None, [done, three0])
     later_b, own_b, done = sum_first(sc, keep_b, [got_b], [dgain_a0])
     more_b = flip(later_b, BACK, SIDE)
     own = [dq1, dq0, dk1, dk0, dv1, dv0, p1, p0]

time: 462 us -> 490 us (1.061)
  waiting for transfers between devices: 132 us -> 178 us
  starting transfers between devices: 95.3 us -> 77.1 us
    ppermute x63, waiting for transfers between devices: 64.6 us -> 91.8 us  [flip(): lax.ppermute(value, 'dp', [(i, i ^ bits[i & 1]) for i in range(count)])]
    ppermute x12, waiting for transfers between devices: 47.1 us -> 60.6 us  [flip_z(): return lax.ppermute(value, ('dp', 'fsdp'), pairs)]
    ppermute x12, starting transfers between devices: 28.2 us -> 15.8 us  [flip_z(): return lax.ppermute(value, ('dp', 'fsdp'), pairs)]
    ppermute x2, starting transfers between devices: 13 us -> 6.92 us  [window(): far = lax.ppermute(own, 'fsdp', [(z, z + 1) for z in range(0, depth, 2)])]
    ppermute x2, waiting for transfers between devices: 9.5 us -> 15.2 us  [window(): far = lax.ppermute(own, 'fsdp', [(z, z + 1) for z in range(0, depth, 2)])]
    unnamed x164 -> x162, local copies, waits for them, and re-layouts: 24.3 us -> 25.1 us
  transfers between devices with their start and end apart: 82 -> 82, of which waited for: 32 -> 31; matrix products, arithmetic and copies ran while one was open for 1% -> 1% of each run, Pallas kernels for 30% -> 29%
where the time goes in v15:
time: 490 us; the launch traced here: 485 us
  Pallas kernels  196 us (40%)
  waiting for transfers between devices  178 us (36%)
  starting transfers between devices  77.1 us (16%)
  local copies, waits for them, and re-layouts  26.4 us (5%)
  other arithmetic  5.03 us (1%)
    ppermute x63, waiting for transfers between devices, flip(): lax.ppermute(value, 'dp', [(i, i ^ bits[i & 1]) for i in range(count)])  91.8 us
    ppermute x12, waiting for transfers between devices, flip_z(): return lax.ppermute(value, ('dp', 'fsdp'), pairs)  60.6 us
    pallas_call x3, Pallas kernels, back(): pl.pallas_call(functools.partial(back_kernel, start, end, len(after)), ou...  46.7 us
    ppermute x63, starting transfers between devices, flip(): lax.ppermute(value, 'dp', [(i, i ^ bits[i & 1]) for i in range(count)])  44.1 us
    pallas_call x2, Pallas kernels, post(): pl.pallas_call(functools.partial(post_kernel, last, len(after)), out_shap...  35.6 us
    pallas_call x2, Pallas kernels, attend_back(): pl.pallas_call(attend_back_kernel, out_shape=(shape((3, n, PIECE), bf16),...  26.1 us
    unnamed x162, local copies, waits for them, and re-layouts  25.1 us
    pallas_call x2, Pallas kernels, attend(): pl.pallas_call(attend_kernel, out_shape=(shape((width, n), bf16), shape((...  20.7 us
  transfers between devices with their start and end apart: 82, of which 31 were waited for; matrix products, arithmetic and copies ran while one was open for 1% of the time, Pallas kernels for 29%

profile of v15, /device:TPU:0, one launch (start us, length us, event | category | flops | bytes accessed | tf_op | source)
XLA Modules:
  0.0 484.6 jit_solution(7962331079344579260)
XLA Ops:
  5.4 3.1 collective-permute-start.4
  8.5 2.6 collective-permute-start.3
  11.7 2.6 pick_first.1.rest_0_
  15.0 24.8 %collective-permute-done.1.rest_2_ = bf16[240,384]{1,0:T(8,128)(2,1)S(1)} collective-permute-done((bf16[240,384]{1,0:T(8,128)(2,1)}, bf16[240,384]{1,0:T(8,128)(2,1)S(1)}, u32[]{:S(2)}, u32[]{:S(2)}) %collective-permute-start.1) | collective-permute-done | bytes 184352 | tf_op jit(solution)/shard_map/ppermute | solution.py:921
  39.7 5.5 %collective-permute-done.2.rest_3_ = bf16[240,384]{1,0:T(8,128)(2,1)S(1)} collective-permute-done((bf16[240,384]{1,0:T(8,128)(2,1)S(1)}, bf16[240,384]{1,0:T(8,128)(2,1)S(1)}, u32[]{:S(2)}, u32[]{:S(2)}) %collective-permute-start.2) | collective-permute-done | bytes 184352 | tf_op jit(solution)/shard_map/ppermute | solution.py:921
  46.2 1.5 stack.30.first_ref
  47.8 1.6 collective-permute-start.6
  50.8 9.7 %collective-permute-done.12.rest_3_ = bf16[368,640]{1,0:T(8,128)(2,1)S(1)} collective-permute-done((bf16[368,640]{1,0:T(8,128)(2,1)S(1)}, bf16[368,640]{1,0:T(8,128)(2,1)S(1)}, u32[]{:S(2)}, u32[]{:S(2)}) %collective-permute-start.12) | collective-permute-done | bytes 471072 | tf_op jit(solution)/shard_map/ppermute | solution.py:921
  60.5 4.5 collective-permute-done.6.rest_5_.rest_2_
  65.0 3.0 stack.31.rest_8_
  68.0 1.6 collective-permute-start.16
  71.4 11.1 %collective-permute-start.10 = (bf16[960,384]{1,0:T(8,128)(2,1)S(1)}, bf16[960,384]{1,0:T(8,128)(2,1)}, u32[]{:S(2)}, u32[]{:S(2)}) collective-permute-start(bf16[960,384]{1,0:T(8,128)(2,1)S(1)} %collective-permute-done.6.rest_5_.rest_2_), channel_id=1, source_target_pairs={{0,4},{4,0},{8,12},{12,8},{16,20},{20,16},{24,28},{28,24},{1,5},{5... | collective-permute-start | bytes 2211848 | tf_op jit(solution)/shard_map/ppermute | solution.py:915
  83.5 33.7 %collective-permute-done.7.rest_3_ = bf16[960,384]{1,0:T(8,128)(2,1)} collective-permute-done((bf16[960,384]{1,0:T(8,128)(2,1)}, bf16[960,384]{1,0:T(8,128)(2,1)}, u32[]{:S(2)}, u32[]{:S(2)}) %collective-permute-start.7) | collective-permute-done | bytes 737312 | tf_op jit(solution)/shard_map/ppermute | solution.py:915
  119.8 7.4 %pre.1 = (bf16[256,960]{1,0:T(8,128)(2,1)}, bf16[256,960]{1,0:T(8,128)(2,1)}, bf16[960,256]{1,0:T(8,128)(2,1)}, bf16[656,256]{1,0:T(8,128)(2,1)}) custom-call(s32[3]{0:T(128)} %copy-done.40, bf16[976,256]{1,0:T(8,128)(2,1)} %copy-done.70, f32[1,960]{1,0:T(1,128)} %get-tuple-element.251.gain_ref.gain_a.rest_22_.rest_14_, ...), custom_call_target="tpu_custom_call" | custom-call | flops 1024 | bytes 1024 | tf_op jit(solution)/shard_map/pre/pallas_call | solution.py:127
  127.3 2.6 collective-permute-start.15
  129.9 7.9 %collective-permute-done.15.refs_1_.kv0 = bf16[656,256]{1,0:T(8,128)(2,1)S(1)} collective-permute-done((bf16[656,256]{1,0:T(8,128)(2,1)}, bf16[656,256]{1,0:T(8,128)(2,1)S(1)}, u32[]{:S(2)}, u32[]{:S(2)}) %collective-permute-start.15) | collective-permute-done | bytes 335904 | tf_op jit(solution)/shard_map/ppermute | solution.py:954
  138.5 5.4 %collective-permute-start.19 = (bf16[960,256]{1,0:T(8,128)(2,1)}, bf16[960,256]{1,0:T(8,128)(2,1)}, u32[]{:S(2)}, u32[]{:S(2)}) collective-permute-start(bf16[960,256]{1,0:T(8,128)(2,1)} %bitcast.10), channel_id=1, source_target_pairs={{0,0},{1,4},{2,1},{3,5},{4,2},{5,6},{6,3},{7,7},{8,8},{9,12},{10,9... | collective-permute-start | bytes 1474568 | tf_op jit(solution)/shard_map/ppermute | solution.py:932
  145.9 10.1 %attend.2 = (bf16[960,256]{1,0:T(8,128)(2,1)S(1)}, f32[15,256]{1,0:T(8,128)S(1)}) custom-call(bf16[960,256]{1,0:T(8,128)(2,1)S(1)} %copy-done.22, bf16[656,256]{1,0:T(8,128)(2,1)S(1)} %collective-permute-done.15.refs_1_.kv0, bf16[656,256]{1,0:T(8,128)(2,1)S(1)} %collective-permute-done.18.kv1, bf16[656,256]{1,0:T(8,128)(2,1)S(1)} %copy-done.5), custom_call_target="tpu_custom_call" | custom-call | flops 1024 | bytes 1024 | tf_op jit(solution)/shard_map/attend/pallas_call | solution.py:180
  156.0 6.0 %collective-permute-done.17.refs_0_ = bf16[4,368,640]{2,1,0:T(8,128)(2,1)} collective-permute-done((bf16[4,368,640]{2,1,0:T(8,128)(2,1)}, bf16[4,368,640]{2,1,0:T(8,128)(2,1)}, u32[]{:S(2)}, u32[]{:S(2)}) %collective-permute-start.17) | collective-permute-done | bytes 1884192 | tf_op jit(solution)/shard_map/ppermute | solution.py:915
  163.4 2.8 collective-permute-done.23.rest_15_
  166.2 18.1 %post.2 = (bf16[256,960]{1,0:T(8,128)(2,1)}, f32[256,960]{1,0:T(8,128)}, bf16[256,960]{1,0:T(8,128)(2,1)}, bf16[256,2560]{1,0:T(8,128)(2,1)}, bf16[256,2560]{1,0...) custom-call(s32[3]{0:T(128)} %copy-done.40, ...), custom_call_target="tpu_custom_call" | custom-call | flops 1024 | bytes 1024 | tf_op jit(solution)/shard_map/post/pallas_call | solution.py:340
  184.6 4.3 collective-permute-start.24
  189.6 7.3 %collective-permute-done.24.kv0 = bf16[656,256]{1,0:T(8,128)(2,1)S(1)} collective-permute-done((bf16[656,256]{1,0:T(8,128)(2,1)}, bf16[656,256]{1,0:T(8,128)(2,1)S(1)}, u32[]{:S(2)}, u32[]{:S(2)}) %collective-permute-start.24) | collective-permute-done | bytes 335904 | tf_op jit(solution)/shard_map/ppermute | solution.py:954
  200.8 10.5 %attend.3 = (bf16[960,256]{1,0:T(8,128)(2,1)S(1)}, f32[15,256]{1,0:T(8,128)S(1)}) custom-call(bf16[960,256]{1,0:T(8,128)(2,1)S(1)} %copy-done.24, bf16[656,256]{1,0:T(8,128)(2,1)S(1)} %collective-permute-done.24.kv0, bf16[656,256]{1,0:T(8,128)(2,1)S(1)} %collective-permute-done.25.kv1, bf16[656,256]{1,0:T(8,128)(2,1)S(1)} %copy-done.3, ...), custom_call_target="tpu_custom_call" | custom-call | flops 1024 | bytes 1024 | tf_op jit(solution)/shard_map/attend/pallas_call | solution.py:180
  212.1 17.4 %post.3 = (bf16[256,960]{1,0:T(8,128)(2,1)}, f32[256,960]{1,0:T(8,128)}, bf16[256,960]{1,0:T(8,128)(2,1)}, bf16[256,2560]{1,0:T(8,128)(2,1)}, bf16[256,2560]{1,0...) custom-call(s32[3]{0:T(128)} %copy-done.40, bf16[960,256]{1,0:T(8,128)(2,1)} %copy-done.48, ...), custom_call_target="tpu_custom_call" | custom-call | flops 1024 | bytes 1024 | tf_op jit(solution)/shard_map/post/pallas_call | solution.py:340
  229.6 19.0 %back_start.1 = (bf16[256,960]{1,0:T(8,128)(2,1)}, bf16[256,2560]{1,0:T(8,128)(2,1)}, bf16[256,2560]{1,0:T(8,128)(2,1)}, f32[256,960]{1,0:T(8,128)}, bf16[3,256,...) custom-call(s32[3]{0:T(128)} %copy-done.40, bf16[960,384]{1,0:T(8,128)(2,1)} %bitcast.30, ...), custom_call_target="tpu_custom_call" | custom-call | flops 1024 | bytes 1024 | tf_op jit(solution)/shard_map/back_start/pallas_call | solution.py:501
  251.5 12.7 %attend_back.2 = (bf16[3,256,384]{2,1,0:T(8,128)(2,1)S(1)}, bf16[3,256,384]{2,1,0:T(8,128)(2,1)S(1)}, f32[640,256]{1,0:T(8,128)S(1)}, bf16[640,256]{1,0:T(8,128)(2,1)S(1)}, f32[640,256]{1,0:T(8,128)S(1)}) custom-call(s32[3]{0:T(128)S(1)} %copy-done.42, bf16[3,256,384]{2,1,0:T(8,128)(2,1)S(1)} %copy-done.12, bf16[960,256]{1,0:T(8,128)(2,1)S(1)} %copy-done.24, ...), custom_call_target="tpu_custom_call" | custom-call | flops 1024 | bytes 1024 | tf_op jit(solution)/shard_map/attend_back/pallas_call | solution.py:233
  270.4 10.6 %collective-permute-done.31.rest_20_ = bf16[640,256]{1,0:T(8,128)(2,1)S(1)} collective-permute-done((bf16[640,256]{1,0:T(8,128)(2,1)S(1)}, bf16[640,256]{1,0:T(8,128)(2,1)S(1)}, u32[]{:S(2)}, u32[]{:S(2)}) %collective-permute-start.31) | collective-permute-done | bytes 327712 | tf_op jit(solution)/shard_map/ppermute | solution.py:963
  283.2 20.7 %back_join.1 = (bf16[256,384]{1,0:T(8,128)(2,1)}, bf16[256,384]{1,0:T(8,128)(2,1)}, bf16[256,384]{1,0:T(8,128)(2,1)}, f32[1,960]{1,0:T(1,128)}, bf16[256,960]{1,...) custom-call(s32[3]{0:T(128)} %copy-done.40, ...), custom_call_target="tpu_custom_call" | custom-call | flops 1024 | bytes 1024 | tf_op jit(solution)/shard_map/back_join/pallas_call | solution.py:501
  304.0 3.2 collective-permute-done.40.rest_7_
  308.3 11.5 %grad_ffn.1 = (bf16[2,960,640]{2,1,0:T(8,128)(2,1)}, bf16[2,960,640]{2,1,0:T(8,128)(2,1)}, f32[8,128]{1,0:T(8,128)}) custom-call(s32[3]{0:T(128)} %copy-done.40, bf16[256,960]{1,0:T(8,128)(2,1)} %get-tuple-element.155.rest_0_, bf16[256,960]{1,0:T(8,128)(2,1)} %get-tuple-element.131.rest_1_, bf16[256,960]{1,0:T(8,128)(2,1)} %copy-done.63, ...), custom_call_target="tpu_custom_call" | custom-call | flops 1024 | bytes 1024 | tf_op jit(solution)/shard_map/grad_ffn/pallas_call | solution.py:543
  323.4 13.4 %attend_back.3 = (bf16[3,256,384]{2,1,0:T(8,128)(2,1)S(1)}, bf16[3,256,384]{2,1,0:T(8,128)(2,1)}, f32[640,256]{1,0:T(8,128)S(1)}, bf16[640,256]{1,0:T(8,128)(2,1)S(1)}, f32[640,256]{1,0:T(8,128)S(1)}) custom-call(s32[3]{0:T(128)S(1)} %copy-done.43, bf16[3,256,384]{2,1,0:T(8,128)(2,1)S(1)} %copy-done.13, bf16[960,256]{1,0:T(8,128)(2,1)S(1)} %copy-done.23, ...), custom_call_target="tpu_custom_call" | custom-call | flops 1024 | bytes 1024 | tf_op jit(solution)/shard_map/attend_back/pallas_call | solution.py:233
  342.6 8.1 %grad_down.1 = (bf16[2,480,640]{2,1,0:T(8,128)(2,1)}, bf16[2,480,640]{2,1,0:T(8,128)(2,1)}, f32[8,128]{1,0:T(8,128)}) custom-call(s32[3]{0:T(128)} %copy-done.40, bf16[256,960]{1,0:T(8,128)(2,1)} %get-tuple-element.152.rest_0_, bf16[256,960]{1,0:T(8,128)(2,1)} %get-tuple-element.173.rest_1_, bf16[256,960]{1,0:T(8,128)(2,1)} %copy-done.62, ...), custom_call_target="tpu_custom_call" | custom-call | flops 1024 | bytes 1024 | tf_op jit(solution)/shard_map/grad_down/pallas_call | solution.py:575
  350.8 2.7 collective-permute-start.50
  354.4 7.0 %back_end.1 = (bf16[256,384]{1,0:T(8,128)(2,1)}, bf16[256,384]{1,0:T(8,128)(2,1)}, bf16[256,384]{1,0:T(8,128)(2,1)}, f32[1,960]{1,0:T(1,128)}, bf16[1920,256]{1,0:T(8,128)(2,1)}) custom-call(s32[3]{0:T(128)} %copy-done.40, bf16[960,384]{1,0:T(8,128)(2,1)} %bitcast.32, bf16[960,384]{1,0:T(8,128)(2,1)} %collective-permute-done.5.rest_4_.rest_1_, ...), custom_call_target="tpu_custom_call" | custom-call | flops 1024 | bytes 1024 | tf_op jit(solution)/shard_map/back_end/pallas_call | solution.py:501
  362.1 2.1 sum_first.3
  365.6 1.7 collective-permute-start.49
  369.4 10.6 %grad_attention.1 = (bf16[960,384]{1,0:T(8,128)(2,1)}, bf16[960,384]{1,0:T(8,128)(2,1)}, bf16[2,960,384]{2,1,0:T(8,128)(2,1)}, f32[8,128]{1,0:T(8,128)}) custom-call(s32[3]{0:T(128)} %copy-done.40, bf16[256,960]{1,0:T(8,128)(2,1)} %get-tuple-element.154.rest_0_, bf16[256,960]{1,0:T(8,128)(2,1)} %get-tuple-element.130.rest_1_, ...), custom_call_target="tpu_custom_call" | custom-call | flops 1024 | bytes 1024 | tf_op jit(solution)/shard_map/grad_attention/pallas_call | solution.py:627
  380.5 1.6 collective-permute-start.48
  382.8 1.6 sum_third.3
  385.9 2.5 collective-permute-start.56
  388.4 3.3 collective-permute-done.47.refs_2_
  391.8 7.9 %collective-permute-done.48.refs_3_ = bf16[960,384]{1,0:T(8,128)(2,1)S(1)} collective-permute-done((bf16[960,384]{1,0:T(8,128)(2,1)}, bf16[960,384]{1,0:T(8,128)(2,1)S(1)}, u32[]{:S(2)}, u32[]{:S(2)}) %collective-permute-start.48) | collective-permute-done | bytes 737312 | tf_op jit(solution)/shard_map/ppermute | solution.py:915
  400.9 1.7 collective-permute-start.52
  402.6 11.9 %collective-permute-done.53.refs_2_ = bf16[2,240,640]{2,1,0:T(8,128)(2,1)S(1)} collective-permute-done((bf16[2,240,640]{2,1,0:T(8,128)(2,1)S(1)}, bf16[2,240,640]{2,1,0:T(8,128)(2,1)S(1)}, u32[]{:S(2)}, u32[]{:S(2)}) %collective-permute-start.53) | collective-permute-done | bytes 614432 | tf_op jit(solution)/shard_map/ppermute | solution.py:921
  417.3 3.6 collective-permute-start.54
  420.9 2.8 collective-permute-done.57.refs_2_
  424.4 8.7 %collective-permute-done.55.refs_2_ = bf16[240,640]{1,0:T(8,128)(2,1)S(1)} collective-permute-done((bf16[240,640]{1,0:T(8,128)(2,1)S(1)}, bf16[240,640]{1,0:T(8,128)(2,1)S(1)}, u32[]{:S(2)}, u32[]{:S(2)}) %collective-permute-start.55) | collective-permute-done | bytes 307232 | tf_op jit(solution)/shard_map/ppermute | solution.py:921
  433.7 1.5 collective-permute-start.70
  436.0 1.7 collective-permute-start.60
  438.0 1.6 collective-permute-start.68
  439.7 6.9 %collective-permute-done.60.refs_2_ = bf16[120,640]{1,0:T(8,128)(2,1)S(1)} collective-permute-done((bf16[120,640]{1,0:T(8,128)(2,1)S(1)}, bf16[120,640]{1,0:T(8,128)(2,1)S(1)}, u32[]{:S(2)}, u32[]{:S(2)}) %collective-permute-start.60) | collective-permute-done | bytes 153632 | tf_op jit(solution)/shard_map/ppermute | solution.py:915
  447.3 1.6 collective-permute-start.58
  451.5 1.7 collective-permute-start.76
  453.6 3.1 collective-permute-done.77.refs_4_
  456.7 1.5 collective-permute-start.63
  458.2 1.6 collective-permute-done.76.refs_3_
  459.8 1.8 collective-permute-start.62
  461.9 3.2 collective-permute-done.63.rest_3_
  465.1 2.8 collective-permute-done.62.rest_2_
  471.3 2.3 lay_down.1
  473.6 2.4 lay.2
  478.3 3.8 lay.3
  482.1 2.4 convert_bitcast_fusion
  (315 shorter events, 68.4 us)
Async XLA Ops:
  5.4 39.8 %collective-permute-start.4 = (bf16[368,640]{1,0:T(8,128)(2,1)S(1)}, bf16[368,640]{1,0:T(8,128)(2,1)S(1)}, u32[]{:S(2)}, u32[]{:S(2)}) collective-permute-start(bf16[368,640]{1,0:T(8,128)(2,1)S(1)} %pick.1.rest_0_), channel_id=1, source_target_pairs={{0,1},{1,0},{2,3},{3,2},{4,5},{5,4},{6,7},{7,6},{8,9},{9,8},{10,11... | collective-permute-start | bytes 1413128 | tf_op jit(solution)/shard_map/ppermute | solution.py:921
  8.5 36.7 %collective-permute-start.3 = (bf16[368,640]{1,0:T(8,128)(2,1)S(1)}, bf16[368,640]{1,0:T(8,128)(2,1)S(1)}, u32[]{:S(2)}, u32[]{:S(2)}) collective-permute-start(bf16[368,640]{1,0:T(8,128)(2,1)S(1)} %pick.1.rest_0_), channel_id=1, source_target_pairs={{0,2},{1,3},{2,0},{3,1},{4,6},{5,7},{6,4},{7,5},{8,10},{9,11},{10,... | collective-permute-start | bytes 1413128 | tf_op jit(solution)/shard_map/ppermute | solution.py:921
  14.4 25.4 %collective-permute-start.1 = (bf16[240,384]{1,0:T(8,128)(2,1)}, bf16[240,384]{1,0:T(8,128)(2,1)S(1)}, u32[]{:S(2)}, u32[]{:S(2)}) collective-permute-start(bf16[240,384]{1,0:T(8,128)(2,1)} %pick_first.1.rest_0_), channel_id=1, source_target_pairs={{0,2},{1,3},{2,0},{3,1},{4,6},{5,7},{6,4},{7,5},{8,10},{9,11},{10,... | collective-permute-start | bytes 552968 | tf_op jit(solution)/shard_map/ppermute | solution.py:921
  14.8 25.0 %collective-permute-start = (bf16[240,384]{1,0:T(8,128)(2,1)}, bf16[240,384]{1,0:T(8,128)(2,1)S(1)}, u32[]{:S(2)}, u32[]{:S(2)}) collective-permute-start(bf16[240,384]{1,0:T(8,128)(2,1)} %pick_first.1.rest_0_), channel_id=1, source_target_pairs={{0,1},{1,0},{2,3},{3,2},{4,5},{5,4},{6,7},{7,6},{8,9},{9,8},{10,11... | collective-permute-start | bytes 552968 | tf_op jit(solution)/shard_map/ppermute | solution.py:921
  39.7 5.5 %collective-permute-start.2 = (bf16[240,384]{1,0:T(8,128)(2,1)S(1)}, bf16[240,384]{1,0:T(8,128)(2,1)S(1)}, u32[]{:S(2)}, u32[]{:S(2)}) collective-permute-start(bf16[240,384]{1,0:T(8,128)(2,1)S(1)} %collective-permute-done.1.rest_2_), channel_id=1, source_target_pairs={{0,1},{1,0},{2,3},{3,2},{4,5},{5,4},{6,7},{7,6},{8,9},{9,8},{10,11... | collective-permute-start | bytes 552968 | tf_op jit(solution)/shard_map/ppermute | solution.py:921
  47.8 17.2 %collective-permute-start.6 = (bf16[960,384]{1,0:T(8,128)(2,1)S(1)}, bf16[960,384]{1,0:T(8,128)(2,1)S(1)}, u32[]{:S(2)}, u32[]{:S(2)}) collective-permute-start(bf16[960,384]{1,0:T(8,128)(2,1)S(1)} %bitcast.24), channel_id=1, source_target_pairs={{0,16},{4,12},{8,24},{12,4},{16,0},{20,28},{24,8},{28,20},{1,17},{... | collective-permute-start | bytes 2211848 | tf_op jit(solution)/shard_map/ppermute | solution.py:915
  49.4 15.6 %collective-permute-start.5 = (bf16[960,384]{1,0:T(8,128)(2,1)S(1)}, bf16[960,384]{1,0:T(8,128)(2,1)}, u32[]{:S(2)}, u32[]{:S(2)}) collective-permute-start(bf16[960,384]{1,0:T(8,128)(2,1)S(1)} %bitcast.25), channel_id=1, source_target_pairs={{0,8},{4,20},{8,0},{12,28},{16,24},{20,4},{24,16},{28,12},{1,9},{5... | collective-permute-start | bytes 2211848 | tf_op jit(solution)/shard_map/ppermute | solution.py:915
  50.8 9.7 %collective-permute-start.12 = (bf16[368,640]{1,0:T(8,128)(2,1)S(1)}, bf16[368,640]{1,0:T(8,128)(2,1)S(1)}, u32[]{:S(2)}, u32[]{:S(2)}) collective-permute-start(bf16[368,640]{1,0:T(8,128)(2,1)S(1)} %collective-permute-done.3.rest_4_.rest_2_), channel_id=1, source_target_pairs={{0,1},{1,0},{2,3},{3,2},{4,5},{5,4},{6,7},{7,6},{8,9},{9,8},{10,11... | collective-permute-start | bytes 1413128 | tf_op jit(solution)/shard_map/ppermute | solution.py:921
  68.0 69.9 %collective-permute-start.16 = (bf16[4,368,640]{2,1,0:T(8,128)(2,1)}, bf16[4,368,640]{2,1,0:T(8,128)(2,1)S(1)}, u32[]{:S(2)}, u32[]{:S(2)}) collective-permute-start(bf16[4,368,640]{2,1,0:T(8,128)(2,1)} %stack.31.rest_8_), channel_id=1, source_target_pairs={{0,16},{4,12},{8,24},{12,4},{16,0},{20,28},{24,8},{28,20},{1,17},{... | collective-permute-start | bytes 5652488 | tf_op jit(solution)/shard_map/ppermute | solution.py:915
  69.6 68.3 %collective-permute-start.13 = (bf16[4,368,640]{2,1,0:T(8,128)(2,1)}, bf16[4,368,640]{2,1,0:T(8,128)(2,1)}, u32[]{:S(2)}, u32[]{:S(2)}) collective-permute-start(bf16[4,368,640]{2,1,0:T(8,128)(2,1)} %stack.31.rest_8_), channel_id=1, source_target_pairs={{0,8},{4,20},{8,0},{12,28},{16,24},{20,4},{24,16},{28,12},{1,9},{5... | collective-permute-start | bytes 5652488 | tf_op jit(solution)/shard_map/ppermute | solution.py:915
  70.1 12.4 %collective-permute-start.8 = (bf16[960,384]{1,0:T(8,128)(2,1)S(1)}, bf16[960,384]{1,0:T(8,128)(2,1)S(1)}, u32[]{:S(2)}, u32[]{:S(2)}) collective-permute-start(bf16[960,384]{1,0:T(8,128)(2,1)S(1)} %bitcast.26), channel_id=1, source_target_pairs={{0,4},{4,0},{8,12},{12,8},{16,20},{20,16},{24,28},{28,24},{1,5},{5... | collective-permute-start | bytes 2211848 | tf_op jit(solution)/shard_map/ppermute | solution.py:915
  70.1 47.1 %collective-permute-start.7 = (bf16[960,384]{1,0:T(8,128)(2,1)}, bf16[960,384]{1,0:T(8,128)(2,1)}, u32[]{:S(2)}, u32[]{:S(2)}) collective-permute-start(bf16[960,384]{1,0:T(8,128)(2,1)} %collective-permute-done.5.rest_4_.rest_1_), channel_id=1, source_target_pairs={{0,16},{4,12},{8,24},{12,4},{16,0},{20,28},{24,8},{28,20},{1,17},{... | collective-permute-start | bytes 2211848 | tf_op jit(solution)/shard_map/ppermute | solution.py:915
  71.4 47.9 %collective-permute-start.10 = (bf16[960,384]{1,0:T(8,128)(2,1)S(1)}, bf16[960,384]{1,0:T(8,128)(2,1)}, u32[]{:S(2)}, u32[]{:S(2)}) collective-permute-start(bf16[960,384]{1,0:T(8,128)(2,1)S(1)} %collective-permute-done.6.rest_5_.rest_2_), channel_id=1, source_target_pairs={{0,4},{4,0},{8,12},{12,8},{16,20},{20,16},{24,28},{28,24},{1,5},{5... | collective-permute-start | bytes 2211848 | tf_op jit(solution)/shard_map/ppermute | solution.py:915
  83.4 35.8 %collective-permute-start.9 = (bf16[960,384]{1,0:T(8,128)(2,1)}, bf16[960,384]{1,0:T(8,128)(2,1)}, u32[]{:S(2)}, u32[]{:S(2)}) collective-permute-start(bf16[960,384]{1,0:T(8,128)(2,1)} %collective-permute-done.5.rest_4_.rest_1_), channel_id=1, source_target_pairs={{0,4},{4,0},{8,12},{12,8},{16,20},{20,16},{24,28},{28,24},{1,5},{5... | collective-permute-start | bytes 2211848 | tf_op jit(solution)/shard_map/ppermute | solution.py:915
  127.3 10.6 %collective-permute-start.15 = (bf16[656,256]{1,0:T(8,128)(2,1)}, bf16[656,256]{1,0:T(8,128)(2,1)S(1)}, u32[]{:S(2)}, u32[]{:S(2)}) collective-permute-start(bf16[656,256]{1,0:T(8,128)(2,1)} %get-tuple-element.124.kv2.rest_16_), channel_id=1, source_target_pairs={{0,1},{2,3},{4,5},{6,7},{8,9},{10,11},{12,13},{14,15},{16,17},{18,... | collective-permute-start | bytes 1007624 | tf_op jit(solution)/shard_map/ppermute | solution.py:954
  137.8 24.1 %collective-permute-start.17 = (bf16[4,368,640]{2,1,0:T(8,128)(2,1)}, bf16[4,368,640]{2,1,0:T(8,128)(2,1)}, u32[]{:S(2)}, u32[]{:S(2)}) collective-permute-start(bf16[4,368,640]{2,1,0:T(8,128)(2,1)} %hold.3.rest_9_), channel_id=1, source_target_pairs={{0,16},{4,12},{8,24},{12,4},{16,0},{20,28},{24,8},{28,20},{1,17},{... | collective-permute-start | bytes 5652488 | tf_op jit(solution)/shard_map/ppermute | solution.py:915
  138.5 17.5 %collective-permute-start.19 = (bf16[960,256]{1,0:T(8,128)(2,1)}, bf16[960,256]{1,0:T(8,128)(2,1)}, u32[]{:S(2)}, u32[]{:S(2)}) collective-permute-start(bf16[960,256]{1,0:T(8,128)(2,1)} %bitcast.10), channel_id=1, source_target_pairs={{0,0},{1,4},{2,1},{3,5},{4,2},{5,6},{6,3},{7,7},{8,8},{9,12},{10,9... | collective-permute-start | bytes 1474568 | tf_op jit(solution)/shard_map/ppermute | solution.py:932
  144.1 17.9 %collective-permute-start.20 = (bf16[4,368,640]{2,1,0:T(8,128)(2,1)}, bf16[4,368,640]{2,1,0:T(8,128)(2,1)S(1)}, u32[]{:S(2)}, u32[]{:S(2)}) collective-permute-start(bf16[4,368,640]{2,1,0:T(8,128)(2,1)} %stack.31.rest_8_), channel_id=1, source_target_pairs={{0,4},{4,0},{8,12},{12,8},{16,20},{20,16},{24,28},{28,24},{1,5},{5... | collective-permute-start | bytes 5652488 | tf_op jit(solution)/shard_map/ppermute | solution.py:915
  144.6 18.8 %collective-permute-start.21 = (bf16[4,368,640]{2,1,0:T(8,128)(2,1)}, bf16[4,368,640]{2,1,0:T(8,128)(2,1)}, u32[]{:S(2)}, u32[]{:S(2)}) collective-permute-start(bf16[4,368,640]{2,1,0:T(8,128)(2,1)} %hold.3.rest_9_), channel_id=1, source_target_pairs={{0,4},{4,0},{8,12},{12,8},{16,20},{20,16},{24,28},{28,24},{1,5},{5... | collective-permute-start | bytes 5652488 | tf_op jit(solution)/shard_map/ppermute | solution.py:915
  145.7 16.3 %collective-permute-start.22 = (bf16[4,368,640]{2,1,0:T(8,128)(2,1)S(1)}, bf16[4,368,640]{2,1,0:T(8,128)(2,1)S(1)}, u32[]{:S(2)}, u32[]{:S(2)}) collective-permute-start(bf16[4,368,640]{2,1,0:T(8,128)(2,1)S(1)} %collective-permute-done.16.refs_2_.rest_10_), channel_id=1, source_target_pairs={{0,4},{4,0},{8,12},{12,8},{16,20},{20,16},{24,28},{28,24},{1,5},{5... | collective-permute-start | bytes 5652488 | tf_op jit(solution)/shard_map/ppermute | solution.py:915
  162.0 4.2 collective-permute-start.23
  184.4 15.2 %collective-permute-start.29 = (bf16[256,2560]{1,0:T(8,128)(2,1)}, bf16[256,2560]{1,0:T(8,128)(2,1)S(1)}, u32[]{:S(2)}, u32[]{:S(2)}) collective-permute-start(bf16[256,2560]{1,0:T(8,128)(2,1)} %get-tuple-element.133.rest_5_), channel_id=1, source_target_pairs={{0,4},{4,0},{8,12},{12,8},{16,20},{20,16},{24,28},{28,24},{1,5},{5... | collective-permute-start | bytes 3932168 | tf_op jit(solution)/shard_map/ppermute | solution.py:915
  184.6 12.2 %collective-permute-start.24 = (bf16[656,256]{1,0:T(8,128)(2,1)}, bf16[656,256]{1,0:T(8,128)(2,1)S(1)}, u32[]{:S(2)}, u32[]{:S(2)}) collective-permute-start(bf16[656,256]{1,0:T(8,128)(2,1)} %get-tuple-element.129.kv2.rest_16_), channel_id=1, source_target_pairs={{0,1},{2,3},{4,5},{6,7},{8,9},{10,11},{12,13},{14,15},{16,17},{18,... | collective-permute-start | bytes 1007624 | tf_op jit(solution)/shard_map/ppermute | solution.py:954
  188.9 9.0 %collective-permute-start.26 = (bf16[256,960]{1,0:T(8,128)(2,1)S(1)}, bf16[256,960]{1,0:T(8,128)(2,1)S(1)}, u32[]{:S(2)}, u32[]{:S(2)}) collective-permute-start(bf16[256,960]{1,0:T(8,128)(2,1)S(1)} %copy-done.65), channel_id=1, source_target_pairs={{0,4},{4,0},{8,12},{12,8},{16,20},{20,16},{24,28},{28,24},{1,5},{5... | collective-permute-start | bytes 1474568 | tf_op jit(solution)/shard_map/ppermute | solution.py:915
  189.0 9.4 %collective-permute-start.27 = (bf16[256,960]{1,0:T(8,128)(2,1)}, bf16[256,960]{1,0:T(8,128)(2,1)S(1)}, u32[]{:S(2)}, u32[]{:S(2)}) collective-permute-start(bf16[256,960]{1,0:T(8,128)(2,1)} %get-tuple-element.131.rest_1_), channel_id=1, source_target_pairs={{0,4},{4,0},{8,12},{12,8},{16,20},{20,16},{24,28},{28,24},{1,5},{5... | collective-permute-start | bytes 1474568 | tf_op jit(solution)/shard_map/ppermute | solution.py:915
  189.5 9.0 %collective-permute-start.28 = (bf16[256,960]{1,0:T(8,128)(2,1)}, bf16[256,960]{1,0:T(8,128)(2,1)S(1)}, u32[]{:S(2)}, u32[]{:S(2)}) collective-permute-start(bf16[256,960]{1,0:T(8,128)(2,1)} %get-tuple-element.132.rest_5_), channel_id=1, source_target_pairs={{0,4},{4,0},{8,12},{12,8},{16,20},{20,16},{24,28},{28,24},{1,5},{5... | collective-permute-start | bytes 1474568 | tf_op jit(solution)/shard_map/ppermute | solution.py:915
  197.9 67.4 %collective-permute-start.35 = (bf16[256,960]{1,0:T(8,128)(2,1)}, bf16[256,960]{1,0:T(8,128)(2,1)}, u32[]{:S(2)}, u32[]{:S(2)}) collective-permute-start(bf16[256,960]{1,0:T(8,128)(2,1)} %get-tuple-element.154.rest_0_), channel_id=1, source_target_pairs={{0,4},{4,0},{8,12},{12,8},{16,20},{20,16},{24,28},{28,24},{1,5},{5... | collective-permute-start | bytes 1474568 | tf_op jit(solution)/shard_map/ppermute | solution.py:915
  248.7 32.3 %collective-permute-start.34 = (bf16[256,2560]{1,0:T(8,128)(2,1)}, bf16[256,2560]{1,0:T(8,128)(2,1)S(1)}, u32[]{:S(2)}, u32[]{:S(2)}) collective-permute-start(bf16[256,2560]{1,0:T(8,128)(2,1)} %get-tuple-element.153), channel_id=1, source_target_pairs={{0,4},{4,0},{8,12},{12,8},{16,20},{20,16},{24,28},{28,24},{1,5},{5... | collective-permute-start | bytes 3932168 | tf_op jit(solution)/shard_map/ppermute | solution.py:915
  248.8 32.2 %collective-permute-start.38 = (bf16[256,2560]{1,0:T(8,128)(2,1)}, bf16[256,2560]{1,0:T(8,128)(2,1)S(1)}, u32[]{:S(2)}, u32[]{:S(2)}) collective-permute-start(bf16[256,2560]{1,0:T(8,128)(2,1)} %get-tuple-element.157.rest_4_), channel_id=1, source_target_pairs={{0,4},{4,0},{8,12},{12,8},{16,20},{20,16},{24,28},{28,24},{1,5},{5... | collective-permute-start | bytes 3932168 | tf_op jit(solution)/shard_map/ppermute | solution.py:915
  249.3 17.7 %collective-permute-start.36 = (bf16[256,960]{1,0:T(8,128)(2,1)}, bf16[256,960]{1,0:T(8,128)(2,1)S(1)}, u32[]{:S(2)}, u32[]{:S(2)}) collective-permute-start(bf16[256,960]{1,0:T(8,128)(2,1)} %get-tuple-element.155.rest_0_), channel_id=1, source_target_pairs={{0,4},{4,0},{8,12},{12,8},{16,20},{20,16},{24,28},{28,24},{1,5},{5... | collective-permute-start | bytes 1474568 | tf_op jit(solution)/shard_map/ppermute | solution.py:915
  269.1 11.9 %collective-permute-start.31 = (bf16[640,256]{1,0:T(8,128)(2,1)S(1)}, bf16[640,256]{1,0:T(8,128)(2,1)S(1)}, u32[]{:S(2)}, u32[]{:S(2)}) collective-permute-start(bf16[640,256]{1,0:T(8,128)(2,1)S(1)} %get-tuple-element.147), channel_id=1, source_target_pairs={{1,0},{3,2},{5,4},{7,6},{9,8},{11,10},{13,12},{15,14},{17,16},{19,... | collective-permute-start | bytes 983048 | tf_op jit(solution)/shard_map/ppermute | solution.py:963
  319.8 41.5 %collective-permute-start.46 = (bf16[2,960,640]{2,1,0:T(8,128)(2,1)}, bf16[2,960,640]{2,1,0:T(8,128)(2,1)S(1)}, u32[]{:S(2)}, u32[]{:S(2)}) collective-permute-start(bf16[2,960,640]{2,1,0:T(8,128)(2,1)} %get-tuple-element.188), channel_id=1, source_target_pairs={{0,8},{4,20},{8,0},{12,28},{16,24},{20,4},{24,16},{28,12},{1,9},{5... | collective-permute-start | bytes 7372808 | tf_op jit(solution)/shard_map/ppermute | solution.py:915
  337.8 15.7 %collective-permute-start.44 = (bf16[3,256,384]{2,1,0:T(8,128)(2,1)}, bf16[3,256,384]{2,1,0:T(8,128)(2,1)S(1)}, u32[]{:S(2)}, u32[]{:S(2)}) collective-permute-start(bf16[3,256,384]{2,1,0:T(8,128)(2,1)} %get-tuple-element.176), channel_id=1, source_target_pairs={{0,4},{4,0},{8,12},{12,8},{16,20},{20,16},{24,28},{28,24},{1,5},{5... | collective-permute-start | bytes 1769480 | tf_op jit(solution)/shard_map/ppermute | solution.py:915
  340.5 13.0 %collective-permute-start.42 = (bf16[640,256]{1,0:T(8,128)(2,1)S(1)}, bf16[640,256]{1,0:T(8,128)(2,1)S(1)}, u32[]{:S(2)}, u32[]{:S(2)}) collective-permute-start(bf16[640,256]{1,0:T(8,128)(2,1)S(1)} %get-tuple-element.171), channel_id=1, source_target_pairs={{1,0},{3,2},{5,4},{7,6},{9,8},{11,10},{13,12},{15,14},{17,16},{19,... | collective-permute-start | bytes 983048 | tf_op jit(solution)/shard_map/ppermute | solution.py:963
  350.8 31.4 %collective-permute-start.50 = (bf16[2,480,640]{2,1,0:T(8,128)(2,1)}, bf16[2,480,640]{2,1,0:T(8,128)(2,1)}, u32[]{:S(2)}, u32[]{:S(2)}) collective-permute-start(bf16[2,480,640]{2,1,0:T(8,128)(2,1)} %get-tuple-element.196), channel_id=1, source_target_pairs={{0,1},{1,0},{2,3},{3,2},{4,5},{5,4},{6,7},{7,6},{8,9},{9,8},{10,11... | collective-permute-start | bytes 3686408 | tf_op jit(solution)/shard_map/ppermute | solution.py:921
  365.6 18.7 %collective-permute-start.49 = (bf16[960,640]{1,0:T(8,128)(2,1)}, bf16[960,640]{1,0:T(8,128)(2,1)S(1)}, u32[]{:S(2)}, u32[]{:S(2)}) collective-permute-start(bf16[960,640]{1,0:T(8,128)(2,1)} %get-tuple-element.194), channel_id=1, source_target_pairs={{0,16},{4,12},{8,24},{12,4},{16,0},{20,28},{24,8},{28,20},{1,17},{... | collective-permute-start | bytes 3686408 | tf_op jit(solution)/shard_map/ppermute | solution.py:915
  380.0 11.7 %collective-permute-start.47 = (bf16[960,384]{1,0:T(8,128)(2,1)}, bf16[960,384]{1,0:T(8,128)(2,1)S(1)}, u32[]{:S(2)}, u32[]{:S(2)}) collective-permute-start(bf16[960,384]{1,0:T(8,128)(2,1)} %get-tuple-element.191), channel_id=1, source_target_pairs={{0,8},{4,20},{8,0},{12,28},{16,24},{20,4},{24,16},{28,12},{1,9},{5... | collective-permute-start | bytes 2211848 | tf_op jit(solution)/shard_map/ppermute | solution.py:915
  380.5 19.2 %collective-permute-start.48 = (bf16[960,384]{1,0:T(8,128)(2,1)}, bf16[960,384]{1,0:T(8,128)(2,1)S(1)}, u32[]{:S(2)}, u32[]{:S(2)}) collective-permute-start(bf16[960,384]{1,0:T(8,128)(2,1)} %get-tuple-element.192), channel_id=1, source_target_pairs={{0,8},{4,20},{8,0},{12,28},{16,24},{20,4},{24,16},{28,12},{1,9},{5... | collective-permute-start | bytes 2211848 | tf_op jit(solution)/shard_map/ppermute | solution.py:915
  385.4 29.2 %collective-permute-start.53 = (bf16[2,240,640]{2,1,0:T(8,128)(2,1)S(1)}, bf16[2,240,640]{2,1,0:T(8,128)(2,1)S(1)}, u32[]{:S(2)}, u32[]{:S(2)}) collective-permute-start(bf16[2,240,640]{2,1,0:T(8,128)(2,1)S(1)} %get-tuple-element.204), channel_id=1, source_target_pairs={{0,1},{1,0},{2,3},{3,2},{4,5},{5,4},{6,7},{7,6},{8,9},{9,8},{10,11... | collective-permute-start | bytes 1843208 | tf_op jit(solution)/shard_map/ppermute | solution.py:921
  385.9 30.1 %collective-permute-start.56 = (bf16[480,640]{1,0:T(8,128)(2,1)S(1)}, bf16[480,640]{1,0:T(8,128)(2,1)S(1)}, u32[]{:S(2)}, u32[]{:S(2)}) collective-permute-start(bf16[480,640]{1,0:T(8,128)(2,1)S(1)} %get-tuple-element.212), channel_id=1, source_target_pairs={{0,2},{1,3},{2,0},{3,1},{4,6},{5,7},{6,4},{7,5},{8,10},{9,11},{10,... | collective-permute-start | bytes 1843208 | tf_op jit(solution)/shard_map/ppermute | solution.py:921
  400.5 14.7 %collective-permute-start.51 = (bf16[480,384]{1,0:T(8,128)(2,1)S(1)}, bf16[480,384]{1,0:T(8,128)(2,1)S(1)}, u32[]{:S(2)}, u32[]{:S(2)}) collective-permute-start(bf16[480,384]{1,0:T(8,128)(2,1)S(1)} %get-tuple-element.201), channel_id=1, source_target_pairs={{0,16},{4,12},{8,24},{12,4},{16,0},{20,28},{24,8},{28,20},{1,17},{... | collective-permute-start | bytes 1105928 | tf_op jit(solution)/shard_map/ppermute | solution.py:915
  400.9 14.3 %collective-permute-start.52 = (bf16[480,384]{1,0:T(8,128)(2,1)S(1)}, bf16[480,384]{1,0:T(8,128)(2,1)S(1)}, u32[]{:S(2)}, u32[]{:S(2)}) collective-permute-start(bf16[480,384]{1,0:T(8,128)(2,1)S(1)} %get-tuple-element.202), channel_id=1, source_target_pairs={{0,16},{4,12},{8,24},{12,4},{16,0},{20,28},{24,8},{28,20},{1,17},{... | collective-permute-start | bytes 1105928 | tf_op jit(solution)/shard_map/ppermute | solution.py:915
  416.8 6.9 %collective-permute-start.57 = (bf16[2,120,640]{2,1,0:T(8,128)(2,1)S(1)}, bf16[2,120,640]{2,1,0:T(8,128)(2,1)S(1)}, u32[]{:S(2)}, u32[]{:S(2)}) collective-permute-start(bf16[2,120,640]{2,1,0:T(8,128)(2,1)S(1)} %get-tuple-element.215), channel_id=1, source_target_pairs={{0,8},{4,20},{8,0},{12,28},{16,24},{20,4},{24,16},{28,12},{1,9},{5... | collective-permute-start | bytes 921608 | tf_op jit(solution)/shard_map/ppermute | solution.py:915
  417.3 15.8 %collective-permute-start.55 = (bf16[240,640]{1,0:T(8,128)(2,1)S(1)}, bf16[240,640]{1,0:T(8,128)(2,1)S(1)}, u32[]{:S(2)}, u32[]{:S(2)}) collective-permute-start(bf16[240,640]{1,0:T(8,128)(2,1)S(1)} %get-tuple-element.210), channel_id=1, source_target_pairs={{0,2},{1,3},{2,0},{3,1},{4,6},{5,7},{6,4},{7,5},{8,10},{9,11},{10,... | collective-permute-start | bytes 921608 | tf_op jit(solution)/shard_map/ppermute | solution.py:921
  417.3 18.0 %collective-permute-start.54 = (bf16[2,240,384]{2,1,0:T(8,128)(2,1)S(1)}, bf16[2,240,384]{2,1,0:T(8,128)(2,1)S(1)}, u32[]{:S(2)}, u32[]{:S(2)}) collective-permute-start(bf16[2,240,384]{2,1,0:T(8,128)(2,1)S(1)} %get-tuple-element.208), channel_id=1, source_target_pairs={{0,1},{1,0},{2,3},{3,2},{4,5},{5,4},{6,7},{7,6},{8,9},{9,8},{10,11... | collective-permute-start | bytes 1105928 | tf_op jit(solution)/shard_map/ppermute | solution.py:921
  433.7 15.2 %collective-permute-start.70 = (bf16[240,640]{1,0:T(8,128)(2,1)S(1)}, bf16[240,640]{1,0:T(8,128)(2,1)S(1)}, u32[]{:S(2)}, u32[]{:S(2)}) collective-permute-start(bf16[240,640]{1,0:T(8,128)(2,1)S(1)} %get-tuple-element.232.rest_0_), channel_id=1, source_target_pairs={{0,24},{4,28},{8,16},{12,20},{16,8},{20,12},{24,0},{28,4},{1,25},{... | collective-permute-start | bytes 921608 | tf_op jit(solution)/shard_map/ppermute | solution.py:915
  435.9 11.4 %collective-permute-start.59 = (bf16[240,384]{1,0:T(8,128)(2,1)S(1)}, bf16[240,384]{1,0:T(8,128)(2,1)S(1)}, u32[]{:S(2)}, u32[]{:S(2)}) collective-permute-start(bf16[240,384]{1,0:T(8,128)(2,1)S(1)} %get-tuple-element.221), channel_id=1, source_target_pairs={{0,2},{1,3},{2,0},{3,1},{4,6},{5,7},{6,4},{7,5},{8,10},{9,11},{10,... | collective-permute-start | bytes 552968 | tf_op jit(solution)/shard_map/ppermute | solution.py:921
  436.0 10.6 %collective-permute-start.60 = (bf16[120,640]{1,0:T(8,128)(2,1)S(1)}, bf16[120,640]{1,0:T(8,128)(2,1)S(1)}, u32[]{:S(2)}, u32[]{:S(2)}) collective-permute-start(bf16[120,640]{1,0:T(8,128)(2,1)S(1)} %get-tuple-element.223), channel_id=1, source_target_pairs={{0,16},{4,12},{8,24},{12,4},{16,0},{20,28},{24,8},{28,20},{1,17},{... | collective-permute-start | bytes 460808 | tf_op jit(solution)/shard_map/ppermute | solution.py:915
  437.7 13.9 %collective-permute-start.69 = (bf16[240,640]{1,0:T(8,128)(2,1)S(1)}, bf16[240,640]{1,0:T(8,128)(2,1)S(1)}, u32[]{:S(2)}, u32[]{:S(2)}) collective-permute-start(bf16[240,640]{1,0:T(8,128)(2,1)S(1)} %get-tuple-element.232.rest_0_), channel_id=1, source_target_pairs={{0,16},{4,12},{8,24},{12,4},{16,0},{20,28},{24,8},{28,20},{1,17},{... | collective-permute-start | bytes 921608 | tf_op jit(solution)/shard_map/ppermute | solution.py:915
  438.0 15.2 %collective-permute-start.68 = (bf16[240,640]{1,0:T(8,128)(2,1)S(1)}, bf16[240,640]{1,0:T(8,128)(2,1)S(1)}, u32[]{:S(2)}, u32[]{:S(2)}) collective-permute-start(bf16[240,640]{1,0:T(8,128)(2,1)S(1)} %get-tuple-element.232.rest_0_), channel_id=1, source_target_pairs={{0,8},{4,20},{8,0},{12,28},{16,24},{20,4},{24,16},{28,12},{1,9},{5... | collective-permute-start | bytes 921608 | tf_op jit(solution)/shard_map/ppermute | solution.py:915
  447.2 6.4 %collective-permute-start.78 = (bf16[120,640]{1,0:T(8,128)(2,1)S(1)}, bf16[120,640]{1,0:T(8,128)(2,1)S(1)}, u32[]{:S(2)}, u32[]{:S(2)}) collective-permute-start(bf16[120,640]{1,0:T(8,128)(2,1)S(1)} %get-tuple-element.235.refs_1_), channel_id=1, source_target_pairs={{0,4},{4,0},{8,12},{12,8},{16,20},{20,16},{24,28},{28,24},{1,5},{5... | collective-permute-start | bytes 460808 | tf_op jit(solution)/shard_map/ppermute | solution.py:915
  447.3 34.7 %collective-permute-start.58 = (bf16[1920,256]{1,0:T(8,128)(2,1)S(1)}, bf16[1920,256]{1,0:T(8,128)(2,1)}, u32[]{:S(2)}, u32[]{:S(2)}) collective-permute-start(bf16[1920,256]{1,0:T(8,128)(2,1)S(1)} %hold.5), channel_id=1, source_target_pairs={{0,0},{4,1},{1,2},{5,3},{2,4},{6,5},{3,6},{7,7},{8,8},{12,9},{9,10... | collective-permute-start | bytes 2949128 | tf_op jit(solution)/shard_map/ppermute | solution.py:932
  448.9 7.8 %collective-permute-start.77 = (bf16[120,640]{1,0:T(8,128)(2,1)S(1)}, bf16[120,640]{1,0:T(8,128)(2,1)S(1)}, u32[]{:S(2)}, u32[]{:S(2)}) collective-permute-start(bf16[120,640]{1,0:T(8,128)(2,1)S(1)} %get-tuple-element.235.refs_1_), channel_id=1, source_target_pairs={{0,24},{4,28},{8,16},{12,20},{16,8},{20,12},{24,0},{28,4},{1,25},{... | collective-permute-start | bytes 460808 | tf_op jit(solution)/shard_map/ppermute | solution.py:915
  451.5 8.3 %collective-permute-start.76 = (bf16[120,640]{1,0:T(8,128)(2,1)S(1)}, bf16[120,640]{1,0:T(8,128)(2,1)S(1)}, u32[]{:S(2)}, u32[]{:S(2)}) collective-permute-start(bf16[120,640]{1,0:T(8,128)(2,1)S(1)} %get-tuple-element.235.refs_1_), channel_id=1, source_target_pairs={{0,16},{4,12},{8,24},{12,4},{16,0},{20,28},{24,8},{28,20},{1,17},{... | collective-permute-start | bytes 460808 | tf_op jit(solution)/shard_map/ppermute | solution.py:915
  453.3 8.4 %collective-permute-start.75 = (bf16[120,640]{1,0:T(8,128)(2,1)S(1)}, bf16[120,640]{1,0:T(8,128)(2,1)S(1)}, u32[]{:S(2)}, u32[]{:S(2)}) collective-permute-start(bf16[120,640]{1,0:T(8,128)(2,1)S(1)} %get-tuple-element.235.refs_1_), channel_id=1, source_target_pairs={{0,8},{4,20},{8,0},{12,28},{16,24},{20,4},{24,16},{28,12},{1,9},{5... | collective-permute-start | bytes 460808 | tf_op jit(solution)/shard_map/ppermute | solution.py:915
  453.6 8.3 %collective-permute-start.64 = (bf16[240,384]{1,0:T(8,128)(2,1)S(1)}, bf16[240,384]{1,0:T(8,128)(2,1)S(1)}, u32[]{:S(2)}, u32[]{:S(2)}) collective-permute-start(bf16[240,384]{1,0:T(8,128)(2,1)S(1)} %get-tuple-element.225.rest_0_), channel_id=1, source_target_pairs={{0,4},{4,0},{8,12},{12,8},{16,20},{20,16},{24,28},{28,24},{1,5},{5... | collective-permute-start | bytes 552968 | tf_op jit(solution)/shard_map/ppermute | solution.py:915
  456.7 8.4 %collective-permute-start.63 = (bf16[240,384]{1,0:T(8,128)(2,1)S(1)}, bf16[240,384]{1,0:T(8,128)(2,1)S(1)}, u32[]{:S(2)}, u32[]{:S(2)}) collective-permute-start(bf16[240,384]{1,0:T(8,128)(2,1)S(1)} %get-tuple-element.225.rest_0_), channel_id=1, source_target_pairs={{0,24},{4,28},{8,16},{12,20},{16,8},{20,12},{24,0},{28,4},{1,25},{... | collective-permute-start | bytes 552968 | tf_op jit(solution)/shard_map/ppermute | solution.py:915
  459.8 8.2 %collective-permute-start.62 = (bf16[240,384]{1,0:T(8,128)(2,1)S(1)}, bf16[240,384]{1,0:T(8,128)(2,1)S(1)}, u32[]{:S(2)}, u32[]{:S(2)}) collective-permute-start(bf16[240,384]{1,0:T(8,128)(2,1)S(1)} %get-tuple-element.225.rest_0_), channel_id=1, source_target_pairs={{0,16},{4,12},{8,24},{12,4},{16,0},{20,28},{24,8},{28,20},{1,17},{... | collective-permute-start | bytes 552968 | tf_op jit(solution)/shard_map/ppermute | solution.py:915
  461.7 6.7 %collective-permute-start.61 = (bf16[240,384]{1,0:T(8,128)(2,1)S(1)}, bf16[240,384]{1,0:T(8,128)(2,1)S(1)}, u32[]{:S(2)}, u32[]{:S(2)}) collective-permute-start(bf16[240,384]{1,0:T(8,128)(2,1)S(1)} %get-tuple-element.225.rest_0_), channel_id=1, source_target_pairs={{0,8},{4,20},{8,0},{12,28},{16,24},{20,4},{24,16},{28,12},{1,9},{5... | collective-permute-start | bytes 552968 | tf_op jit(solution)/shard_map/ppermute | solution.py:915
  461.9 6.5 %collective-permute-start.81 = (bf16[120,640]{1,0:T(8,128)(2,1)S(1)}, bf16[120,640]{1,0:T(8,128)(2,1)S(1)}, u32[]{:S(2)}, u32[]{:S(2)}) collective-permute-start(bf16[120,640]{1,0:T(8,128)(2,1)S(1)} %collective-permute-done.77.refs_4_), channel_id=1, source_target_pairs={{0,4},{4,0},{8,12},{12,8},{16,20},{20,16},{24,28},{28,24},{1,5},{5... | collective-permute-start | bytes 460808 | tf_op jit(solution)/shard_map/ppermute | solution.py:915
  470.2 8.0 %collective-permute-start.71 = (bf16[240,640]{1,0:T(8,128)(2,1)S(1)}, bf16[240,640]{1,0:T(8,128)(2,1)S(1)}, u32[]{:S(2)}, u32[]{:S(2)}) collective-permute-start(bf16[240,640]{1,0:T(8,128)(2,1)S(1)} %get-tuple-element.232.rest_0_), channel_id=1, source_target_pairs={{0,4},{4,0},{8,12},{12,8},{16,20},{20,16},{24,28},{28,24},{1,5},{5... | collective-permute-start | bytes 921608 | tf_op jit(solution)/shard_map/ppermute | solution.py:915
  470.5 7.8 %collective-permute-start.74 = (bf16[240,640]{1,0:T(8,128)(2,1)S(1)}, bf16[240,640]{1,0:T(8,128)(2,1)}, u32[]{:S(2)}, u32[]{:S(2)}) collective-permute-start(bf16[240,640]{1,0:T(8,128)(2,1)S(1)} %collective-permute-done.70.rest_3_), channel_id=1, source_target_pairs={{0,4},{4,0},{8,12},{12,8},{16,20},{20,16},{24,28},{28,24},{1,5},{5... | collective-permute-start | bytes 921608 | tf_op jit(solution)/shard_map/ppermute | solution.py:915
  470.7 7.5 %collective-permute-start.73 = (bf16[240,640]{1,0:T(8,128)(2,1)S(1)}, bf16[240,640]{1,0:T(8,128)(2,1)}, u32[]{:S(2)}, u32[]{:S(2)}) collective-permute-start(bf16[240,640]{1,0:T(8,128)(2,1)S(1)} %collective-permute-done.69.rest_2_), channel_id=1, source_target_pairs={{0,4},{4,0},{8,12},{12,8},{16,20},{20,16},{24,28},{28,24},{1,5},{5... | collective-permute-start | bytes 921608 | tf_op jit(solution)/shard_map/ppermute | solution.py:915
  471.0 7.3 %collective-permute-start.72 = (bf16[240,640]{1,0:T(8,128)(2,1)S(1)}, bf16[240,640]{1,0:T(8,128)(2,1)}, u32[]{:S(2)}, u32[]{:S(2)}) collective-permute-start(bf16[240,640]{1,0:T(8,128)(2,1)S(1)} %collective-permute-done.68.rest_1_), channel_id=1, source_target_pairs={{0,4},{4,0},{8,12},{12,8},{16,20},{20,16},{24,28},{28,24},{1,5},{5... | collective-permute-start | bytes 921608 | tf_op jit(solution)/shard_map/ppermute | solution.py:915
  (98 other events, 854.7 us)

commit v16 on v14

--- a/solution.py
+++ b/solution.py
@@ -52,6 +52,17 @@
                 copy()
             else:
                 pl.when(kind == only)(copy)
+
+
+def leave(kept, out, sem, cols=None):
+    if cols is not None:
+        kept, out = kept.at[:, cols], out.at[:, cols]
+    pltpu.make_async_copy(kept, out, sem).start()
+
+
+def gone(kepts, outs, sems):
+    for i, (kept, out) in enumerate(zip(kepts, outs)):
+        pltpu.make_async_copy(kept, out, sems.at[i]).wait()
 
 
 def arrived(kept, sems, *at):
@@ -289,9 +300,10 @@
 def post_kernel(last, after, sc, ot_ref, h_ref, gain_ref, gain_a, cos_ref, sin_ref, *rest):
     mine_a, other_a, mine_b, other_b = rest[:4], rest[4:8], rest[8:12], rest[12:16]
     ids_ref, rest = rest[16], rest[17 + after :]
-    o_ref, h1_ref, b_ref, gate_ref, up_ref, z_ref, next_ref = rest[:7]
+    hbm, next_ref = rest[:6], rest[6]
     more, rest = rest[7 : 7 + (0 if last else 3)], rest[7 + (0 if last else 3) :]
-    wa, sem_a, wb, sem_b, wd, sem_d = rest
+    wa, sem_a, wb, sem_b, wd, sem_d, *stage, sem_out = rest
+    o_ref, h1_ref, b_ref, gate_ref, up_ref, z_ref = stage
     core, chip = sc[0], sc[1]
     fetch(mine_a, other_a, wa, sem_a, core, chip, 1)
     fetch_both(mine_b, other_b, wb, sem_b, core, chip, (0, 1))
@@ -301,12 +313,15 @@
         fetch(mine_a, other_a, wa, sem_a, core, chip, 0)
     o = ot_ref[...].T
     o_ref[...] = o
+    leave(o_ref, hbm[0], sem_out.at[0])
     for m in range(1, 4):
         arrived(wa, sem_a, 1, m)
     h1 = h_ref[...].astype(f32) + jnp.concatenate([nn(o, wa[1, m, :, :KVW]) for m in range(1, 4)], axis=1)
     h1_ref[...] = h1
+    leave(h1_ref, hbm[1], sem_out.at[1])
     b = normed(h1, gain_ref[...]).astype(bf16)
     b_ref[...] = b
+    leave(b_ref, hbm[2], sem_out.at[2])
     n = wb.shape[4]
     total = h1
     for i in range(4):
@@ -320,6 +335,8 @@
         up_ref[:, cols] = up.astype(bf16)
         z = (gate / (1.0 + jnp.exp(-gate)) * up).astype(bf16)
         z_ref[:, cols] = z
+        for j in range(3, 6):
+            leave(stage[j], hbm[j], sem_out.at[j], cols)
         if i == 0:
             arrived_down(wd, sem_d)
         total = total + nt(z, wd[m])
@@ -328,6 +345,7 @@
         arrived(wa, sem_a, 1, 0)
     else:
         project(total, gain_a, cos_ref, sin_ref, ids_ref[2 * KVW :, :], wa, sem_a, *more)
+    gone(stage, hbm, sem_out)
 
 
 def post(last, after, sc, ot, h, gain, gain_a, cos, sin, kv, wa, wb):
@@ -341,19 +359,20 @@
         functools.partial(post_kernel, last, len(after)),
         out_shape=tuple(outs),
         in_specs=[SCALARS] + [WHOLE] * 6 + [LEFT] * 16 + [WHOLE] + [LEFT] * len(after),
-        out_specs=(WHOLE,) * len(outs),
-        scratch_shapes=scratch_a(width) + scratch_ffn(width, hidden // 4),
+        out_specs=(LEFT,) * 6 + (WHOLE,) * (len(outs) - 6),
+        scratch_shapes=scratch_a(width) + scratch_ffn(width, hidden // 4) + [pltpu.VMEM(o.shape, o.dtype) for o in outs[:6]] + [pltpu.SemaphoreType.DMA((6,))],
         cost_estimate=BRIEF,
         compiler_params=pltpu.CompilerParams(vmem_limit_bytes=LIMIT),
         name="post",
     )(sc, ot, h, gain, gain_a, cos, sin, *wa[0], *wa[1], *wb[0], *wb[1], kv, *after)
 
 
-def ffn_back(state, core, chip, refs, weights):
+def ffn_back(state, core, chip, refs, weights, stage, sems, hbm):
     gate_ref, up_ref, h1_ref, gain_ref, gb_ref, keep_ref, send_ref, g1_ref, p_ref, dgain_ref, do_ref = refs
     wa, sem_a, wb, sem_b, wd, sem_d = weights
     gb = state.astype(bf16)
     gb_ref[...] = gb
+    leave(gb_ref, hbm[3], sems.at[3])
     n = wb.shape[4]
     first = core == 0
     arrived_down(wd, sem_d)
@@ -362,21 +381,28 @@
         m = chip ^ i
         cols = pl.ds(pl.multiple_of(m * n, 128), n)
         dz = nn(gb, wd[m])
+        if i == 0:
+            for j in range(2):
+                pltpu.make_async_copy(hbm[j], stage[j], sems.at[j]).wait()
         gate, up = gate_ref[:, cols].astype(f32), up_ref[:, cols].astype(f32)
         sig = 1.0 / (1.0 + jnp.exp(-gate))
         dup = (dz * (gate * sig)).astype(bf16)
         dgate = (dz * up * (sig * (1.0 + gate * (1.0 - sig)))).astype(bf16)
         keep_ref[:, cols] = jnp.where(first, dgate, dup)
         send_ref[:, cols] = jnp.where(first, dup, dgate)
+        leave(keep_ref, hbm[4], sems.at[4], cols)
+        leave(send_ref, hbm[5], sems.at[5], cols)
         arrived(wb, sem_b, 0, m)
         part = nt(dgate, whole(wb, 0, m))
         arrived(wb, sem_b, 1, m)
         part = part + nt(dup, whole(wb, 1, m))
         db = part if i == 0 else db + part
+    pltpu.make_async_copy(hbm[2], stage[2], sems.at[2]).wait()
     dx, dgain = norm_back(h1_ref[...], gain_ref[...], db)
     dgain_ref[...] = dgain
     g1 = state + dx
     g1_ref[...] = g1
+    leave(g1_ref, hbm[6], sems.at[6])
     low = g1.astype(bf16)
     do = None
     for p in range(3):
@@ -449,7 +475,11 @@
         fetch(mine_a, other_a, wa, sem_a, core, chip, 1)
     if not end:
         wb, sem_b, wd, sem_d = take(4)
+        stage, (sems,) = take(7), take(1)
+        hbm = [*ins[:3], *outs[:4]]
         fetch_down(mine_b, other_b, wb, wd, sem_d, core, chip)
+        for j in range(3):
+            pltpu.make_async_copy(hbm[j], stage[j], sems.at[j]).start()
         fetch_both(mine_b, other_b, wb, sem_b, core, chip)
     if start:
         fetch(mine_a, other_a, wa, sem_a, core, chip, 1)
@@ -466,7 +496,9 @@
         g_out[width:, :] = state.astype(bf16).T
         finish_a(wa, sem_a, (1, 1), (1, 2), (1, 3))
     else:
-        ffn_back(state, core, chip, (*ins, *outs), (wa, sem_a, wb, sem_b, wd, sem_d))
+        refs = (*stage[:3], ins[3], *stage[3:], *outs[4:])
+        ffn_back(state, core, chip, refs, (wa, sem_a, wb, sem_b, wd, sem_d), stage, sems, hbm)
+        gone(stage[3:], hbm[3:], sems.at[pl.ds(3, 4)])
         if start:
             finish_a(wa, sem_a, (1, 0))
 
@@ -487,7 +519,7 @@
     outs = []
     if not end:
         args += list(ffn)
-        specs += [WHOLE] * len(ffn)
+        specs += [LEFT] * 3 + [WHOLE]
     if not start:
         outs += [shape((n, PIECE), bf16)] * 3 + [shape((1, width), f32)]
     if end:
@@ -496,13 +528,19 @@
         hidden = ffn[0].shape[1]
         outs += [shape((n, width), bf16), shape((n, hidden), bf16), shape((n, hidden), bf16)]
         outs += [shape((n, width), f32), shape((3, n, PIECE), bf16), shape((1, width), f32), shape((width, n), bf16)]
+    out_specs = [WHOLE] * len(outs)
+    if not end:
+        at = 0 if start else 4
+        out_specs[at : at + 4] = [LEFT] * 4
+        scratch += [pltpu.VMEM(x.shape, x.dtype) for x in (*ffn[:3], *outs[at : at + 4])]
+        scratch += [pltpu.SemaphoreType.DMA((7,))]
     args += list(after)
     specs += [LEFT] * len(after)
     return pl.pallas_call(
         functools.partial(back_kernel, start, end, len(after)),
         out_shape=tuple(outs),
         in_specs=specs,
-        out_specs=(WHOLE,) * len(outs),
+        out_specs=tuple(out_specs),
         scratch_shapes=scratch,
         cost_estimate=BRIEF,
         compiler_params=pltpu.CompilerParams(vmem_limit_bytes=LIMIT),

time: 462 us -> 459 us (level)
  transfers between devices with their start and end apart: 82 -> 82, of which waited for: 32 -> 33; matrix products, arithmetic and copies ran while one was open for 1% -> 1% of each run, Pallas kernels for 30% -> 30%
where the time goes in v16:
time: 459 us; the launch traced here: 454 us
  Pallas kernels  193 us (42%)
  waiting for transfers between devices  132 us (29%)
  starting transfers between devices  94.1 us (21%)
  local copies, waits for them, and re-layouts  27 us (6%)
  other arithmetic  5.53 us (1%)
    ppermute x63, waiting for transfers between devices, flip(): lax.ppermute(value, 'dp', [(i, i ^ bits[i & 1]) for i in range(count)])  65.1 us
    ppermute x63, starting transfers between devices, flip(): lax.ppermute(value, 'dp', [(i, i ^ bits[i & 1]) for i in range(count)])  47.5 us
    ppermute x12, waiting for transfers between devices, flip_z(): return lax.ppermute(value, ('dp', 'fsdp'), pairs)  46.7 us
    pallas_call x3, Pallas kernels, back(): pl.pallas_call(functools.partial(back_kernel, start, end, len(after)), ou...  45.7 us
    pallas_call x2, Pallas kernels, post(): pl.pallas_call(functools.partial(post_kernel, last, len(after)), out_shap...  34.7 us
    ppermute x12, starting transfers between devices, flip_z(): return lax.ppermute(value, ('dp', 'fsdp'), pairs)  28 us
    pallas_call x2, Pallas kernels, attend_back(): pl.pallas_call(attend_back_kernel, out_shape=(shape((3, n, PIECE), bf16),...  25.3 us
    unnamed x164, local copies, waits for them, and re-layouts  24.3 us
  transfers between devices with their start and end apart: 82, of which 33 were waited for; matrix products, arithmetic and copies ran while one was open for 1% of the time, Pallas kernels for 30%

profile of v16, /device:TPU:0, one launch (start us, length us, event | category | flops | bytes accessed | tf_op | source)
XLA Modules:
  0.0 453.8 jit_solution(3002837451633340623)
XLA Ops:
  3.3 2.7 pick_first.1.rest_0_
  6.0 4.1 collective-permute-start.1
  10.1 1.6 collective-permute-start
  11.7 7.3 %collective-permute-done.1.rest_2_ = bf16[240,384]{1,0:T(8,128)(2,1)S(1)} collective-permute-done((bf16[240,384]{1,0:T(8,128)(2,1)}, bf16[240,384]{1,0:T(8,128)(2,1)S(1)}, u32[]{:S(2)}, u32[]{:S(2)}) %collective-permute-start.1) | collective-permute-done | bytes 184352 | tf_op jit(solution)/shard_map/ppermute | solution.py:959
  24.6 1.5 stack.30.first_ref
  26.2 1.5 collective-permute-start.3
  29.2 3.2 collective-permute-start.11
  32.5 1.7 collective-permute-start.10
  34.2 11.5 %collective-permute-done.3.refs_1_.rest_1_ = bf16[960,384]{1,0:T(8,128)(2,1)} collective-permute-done((bf16[960,384]{1,0:T(8,128)(2,1)S(1)}, bf16[960,384]{1,0:T(8,128)(2,1)}, u32[]{:S(2)}, u32[]{:S(2)}) %collective-permute-start.3) | collective-permute-done | bytes 737312 | tf_op jit(solution)/shard_map/ppermute | solution.py:953
  45.7 6.8 %collective-permute-done.11.refs_0_ = bf16[368,640]{1,0:T(8,128)(2,1)S(1)} collective-permute-done((bf16[368,640]{1,0:T(8,128)(2,1)S(1)}, bf16[368,640]{1,0:T(8,128)(2,1)S(1)}, u32[]{:S(2)}, u32[]{:S(2)}) %collective-permute-start.11) | collective-permute-done | bytes 471072 | tf_op jit(solution)/shard_map/ppermute | solution.py:959
  54.3 10.0 %collective-permute-done.12.rest_3_ = bf16[368,640]{1,0:T(8,128)(2,1)S(1)} collective-permute-done((bf16[368,640]{1,0:T(8,128)(2,1)S(1)}, bf16[368,640]{1,0:T(8,128)(2,1)S(1)}, u32[]{:S(2)}, u32[]{:S(2)}) %collective-permute-start.12) | collective-permute-done | bytes 471072 | tf_op jit(solution)/shard_map/ppermute | solution.py:959
  64.3 3.0 stack.31.rest_8_
  69.2 4.6 %collective-permute-start.8 = (bf16[960,384]{1,0:T(8,128)(2,1)}, bf16[960,384]{1,0:T(8,128)(2,1)}, u32[]{:S(2)}, u32[]{:S(2)}) collective-permute-start(bf16[960,384]{1,0:T(8,128)(2,1)} %collective-permute-done.4.refs_2_.rest_2_), channel_id=1, source_target_pairs={{0,4},{4,0},{8,12},{12,8},{16,20},{20,16},{24,28},{28,24},{1,5},{5... | collective-permute-start | bytes 2211848 | tf_op jit(solution)/shard_map/ppermute | solution.py:953
  73.7 5.9 %collective-permute-start.7 = (bf16[960,384]{1,0:T(8,128)(2,1)}, bf16[960,384]{1,0:T(8,128)(2,1)}, u32[]{:S(2)}, u32[]{:S(2)}) collective-permute-start(bf16[960,384]{1,0:T(8,128)(2,1)} %collective-permute-done.3.refs_1_.rest_1_), channel_id=1, source_target_pairs={{0,4},{4,0},{8,12},{12,8},{16,20},{20,16},{24,28},{28,24},{1,5},{5... | collective-permute-start | bytes 2211848 | tf_op jit(solution)/shard_map/ppermute | solution.py:953
  83.3 7.4 %pre.1 = (bf16[256,960]{1,0:T(8,128)(2,1)}, bf16[256,960]{1,0:T(8,128)(2,1)}, bf16[960,256]{1,0:T(8,128)(2,1)}, bf16[656,256]{1,0:T(8,128)(2,1)}) custom-call(s32[3]{0:T(128)} %pad_add_fusion.sc.refs_0_, bf16[976,256]{1,0:T(8,128)(2,1)} %copy-done.72, f32[1,960]{1,0:T(1,128)} %get-tuple-element.251.gain_ref.gain_a.rest_22_.rest_14_, ...), custom_call_target="tpu_custom_call" | custom-call | flops 1024 | bytes 1024 | tf_op jit(solution)/shard_map/pre/pallas_call | solution.py:138
  90.7 9.3 %collective-permute-start.15 = (bf16[656,256]{1,0:T(8,128)(2,1)}, bf16[656,256]{1,0:T(8,128)(2,1)S(1)}, u32[]{:S(2)}, u32[]{:S(2)}) collective-permute-start(bf16[656,256]{1,0:T(8,128)(2,1)} %get-tuple-element.124.kv2.rest_16_), channel_id=1, source_target_pairs={{0,1},{2,3},{4,5},{6,7},{8,9},{10,11},{12,13},{14,15},{16,17},{18,... | collective-permute-start | bytes 1007624 | tf_op jit(solution)/shard_map/ppermute | solution.py:992
  100.1 7.8 %collective-permute-done.15.refs_1_.kv0 = bf16[656,256]{1,0:T(8,128)(2,1)S(1)} collective-permute-done((bf16[656,256]{1,0:T(8,128)(2,1)}, bf16[656,256]{1,0:T(8,128)(2,1)S(1)}, u32[]{:S(2)}, u32[]{:S(2)}) %collective-permute-start.15) | collective-permute-done | bytes 335904 | tf_op jit(solution)/shard_map/ppermute | solution.py:992
  110.8 10.1 %attend.2 = (bf16[960,256]{1,0:T(8,128)(2,1)S(1)}, f32[15,256]{1,0:T(8,128)S(1)}) custom-call(bf16[960,256]{1,0:T(8,128)(2,1)S(1)} %copy-done.22, bf16[656,256]{1,0:T(8,128)(2,1)S(1)} %collective-permute-done.15.refs_1_.kv0, bf16[656,256]{1,0:T(8,128)(2,1)S(1)} %collective-permute-done.18.kv1, bf16[656,256]{1,0:T(8,128)(2,1)S(1)} %copy-done.5), custom_call_target="tpu_custom_call" | custom-call | flops 1024 | bytes 1024 | tf_op jit(solution)/shard_map/attend/pallas_call | solution.py:191
  121.6 11.2 %collective-permute-done.17.refs_0_ = bf16[4,368,640]{2,1,0:T(8,128)(2,1)} collective-permute-done((bf16[4,368,640]{2,1,0:T(8,128)(2,1)}, bf16[4,368,640]{2,1,0:T(8,128)(2,1)}, u32[]{:S(2)}, u32[]{:S(2)}) %collective-permute-start.17) | collective-permute-done | bytes 1884192 | tf_op jit(solution)/shard_map/ppermute | solution.py:953
  134.2 2.8 collective-permute-done.22.rest_15_
  137.0 18.0 %post.2 = (bf16[256,960]{1,0:T(8,128)(2,1)}, f32[256,960]{1,0:T(8,128)}, bf16[256,960]{1,0:T(8,128)(2,1)}, bf16[256,2560]{1,0:T(8,128)(2,1)}, bf16[256,2560]{1,0...) custom-call(s32[3]{0:T(128)} %pad_add_fusion.sc.refs_0_, ...), custom_call_target="tpu_custom_call" | custom-call | flops 1024 | bytes 1024 | tf_op jit(solution)/shard_map/post/pallas_call | solution.py:358
  155.2 3.7 collective-permute-start.24
  159.7 5.9 %collective-permute-start.27 = (bf16[256,960]{1,0:T(8,128)(2,1)}, bf16[256,960]{1,0:T(8,128)(2,1)S(1)}, u32[]{:S(2)}, u32[]{:S(2)}) collective-permute-start(bf16[256,960]{1,0:T(8,128)(2,1)} %get-tuple-element.131.rest_1_), channel_id=1, source_target_pairs={{0,4},{4,0},{8,12},{12,8},{16,20},{20,16},{24,28},{28,24},{1,5},{5... | collective-permute-start | bytes 1474568 | tf_op jit(solution)/shard_map/ppermute | solution.py:953
  165.7 1.7 collective-permute-done.24.kv0
  171.4 10.5 %attend.3 = (bf16[960,256]{1,0:T(8,128)(2,1)S(1)}, f32[15,256]{1,0:T(8,128)S(1)}) custom-call(bf16[960,256]{1,0:T(8,128)(2,1)S(1)} %copy-done.24, bf16[656,256]{1,0:T(8,128)(2,1)S(1)} %collective-permute-done.24.kv0, bf16[656,256]{1,0:T(8,128)(2,1)S(1)} %collective-permute-done.25.kv1, bf16[656,256]{1,0:T(8,128)(2,1)S(1)} %copy-done.3, ...), custom_call_target="tpu_custom_call" | custom-call | flops 1024 | bytes 1024 | tf_op jit(solution)/shard_map/attend/pallas_call | solution.py:191
  183.5 16.7 %post.3 = (bf16[256,960]{1,0:T(8,128)(2,1)}, f32[256,960]{1,0:T(8,128)}, bf16[256,960]{1,0:T(8,128)(2,1)}, bf16[256,2560]{1,0:T(8,128)(2,1)}, bf16[256,2560]{1,0...) custom-call(s32[3]{0:T(128)} %pad_add_fusion.sc.refs_0_, bf16[960,256]{1,0:T(8,128)(2,1)} %copy-done.47, ...), custom_call_target="tpu_custom_call" | custom-call | flops 1024 | bytes 1024 | tf_op jit(solution)/shard_map/post/pallas_call | solution.py:358
  200.3 18.3 %back_start.1 = (bf16[256,960]{1,0:T(8,128)(2,1)}, bf16[256,2560]{1,0:T(8,128)(2,1)}, bf16[256,2560]{1,0:T(8,128)(2,1)}, f32[256,960]{1,0:T(8,128)}, bf16[3,256,...) custom-call(s32[3]{0:T(128)} %pad_add_fusion.sc.refs_0_, bf16[960,384]{1,0:T(8,128)(2,1)} %bitcast.30, ...), custom_call_target="tpu_custom_call" | custom-call | flops 1024 | bytes 1024 | tf_op jit(solution)/shard_map/back_start/pallas_call | solution.py:539
  221.3 12.6 %attend_back.2 = (bf16[3,256,384]{2,1,0:T(8,128)(2,1)S(1)}, bf16[3,256,384]{2,1,0:T(8,128)(2,1)S(1)}, f32[640,256]{1,0:T(8,128)S(1)}, bf16[640,256]{1,0:T(8,128)(2,1)S(1)}, f32[640,256]{1,0:T(8,128)S(1)}) custom-call(s32[3]{0:T(128)S(1)} %copy-done.41, bf16[3,256,384]{2,1,0:T(8,128)(2,1)S(1)} %copy-done.12, bf16[960,256]{1,0:T(8,128)(2,1)S(1)} %copy-done.24, ...), custom_call_target="tpu_custom_call" | custom-call | flops 1024 | bytes 1024 | tf_op jit(solution)/shard_map/attend_back/pallas_call | solution.py:244
  240.3 10.6 %collective-permute-done.31.rest_20_ = bf16[640,256]{1,0:T(8,128)(2,1)S(1)} collective-permute-done((bf16[640,256]{1,0:T(8,128)(2,1)S(1)}, bf16[640,256]{1,0:T(8,128)(2,1)S(1)}, u32[]{:S(2)}, u32[]{:S(2)}) %collective-permute-start.31) | collective-permute-done | bytes 327712 | tf_op jit(solution)/shard_map/ppermute | solution.py:1001
  253.0 20.4 %back_join.1 = (bf16[256,384]{1,0:T(8,128)(2,1)}, bf16[256,384]{1,0:T(8,128)(2,1)}, bf16[256,384]{1,0:T(8,128)(2,1)}, f32[1,960]{1,0:T(1,128)}, bf16[256,960]{1,...) custom-call(s32[3]{0:T(128)} %pad_add_fusion.sc.refs_0_, ...), custom_call_target="tpu_custom_call" | custom-call | flops 1024 | bytes 1024 | tf_op jit(solution)/shard_map/back_join/pallas_call | solution.py:539
  273.5 3.2 collective-permute-done.40.rest_7_
  277.9 11.5 %grad_ffn.1 = (bf16[2,960,640]{2,1,0:T(8,128)(2,1)}, bf16[2,960,640]{2,1,0:T(8,128)(2,1)}, f32[8,128]{1,0:T(8,128)}) custom-call(s32[3]{0:T(128)} %pad_add_fusion.sc.refs_0_, bf16[256,960]{1,0:T(8,128)(2,1)} %get-tuple-element.155.rest_0_, bf16[256,960]{1,0:T(8,128)(2,1)} %get-tuple-element.131.rest_1_, bf16[256,960]{1,0:T(8,128)(2,1)} %copy-done.63, ...), custom_call_target="tpu_custom_call" | custom-call | flops 1024 | bytes 1024 | tf_op jit(solution)/shard_map/grad_ffn/pallas_call | solution.py:581
  292.0 12.6 %attend_back.3 = (bf16[3,256,384]{2,1,0:T(8,128)(2,1)S(1)}, bf16[3,256,384]{2,1,0:T(8,128)(2,1)S(1)}, f32[640,256]{1,0:T(8,128)S(1)}, bf16[640,256]{1,0:T(8,128)(2,1)S(1)}, f32[640,256]{1,0:T(8,128)S(1)}) custom-call(s32[3]{0:T(128)S(1)} %copy-done.42, bf16[3,256,384]{2,1,0:T(8,128)(2,1)S(1)} %copy-done.13, bf16[960,256]{1,0:T(8,128)(2,1)S(1)} %copy-done.23, ...), custom_call_target="tpu_custom_call" | custom-call | flops 1024 | bytes 1024 | tf_op jit(solution)/shard_map/attend_back/pallas_call | solution.py:244
  311.3 8.2 %grad_down.1 = (bf16[2,480,640]{2,1,0:T(8,128)(2,1)}, bf16[2,480,640]{2,1,0:T(8,128)(2,1)}, f32[8,128]{1,0:T(8,128)}) custom-call(s32[3]{0:T(128)} %pad_add_fusion.sc.refs_0_, bf16[256,960]{1,0:T(8,128)(2,1)} %get-tuple-element.152.rest_0_, bf16[256,960]{1,0:T(8,128)(2,1)} %get-tuple-element.173.rest_1_, bf16[256,960]{1,0:T(8,128)(2,1)} %copy-done.62, ...), custom_call_target="tpu_custom_call" | custom-call | flops 1024 | bytes 1024 | tf_op jit(solution)/shard_map/grad_down/pallas_call | solution.py:613
  319.4 2.7 collective-permute-start.50
  322.9 7.0 %back_end.1 = (bf16[256,384]{1,0:T(8,128)(2,1)}, bf16[256,384]{1,0:T(8,128)(2,1)}, bf16[256,384]{1,0:T(8,128)(2,1)}, f32[1,960]{1,0:T(1,128)}, bf16[1920,256]{1,0:T(8,128)(2,1)}) custom-call(s32[3]{0:T(128)} %pad_add_fusion.sc.refs_0_, bf16[960,384]{1,0:T(8,128)(2,1)} %bitcast.32, bf16[960,384]{1,0:T(8,128)(2,1)} %collective-permute-done.3.refs_1_.rest_1_, ...), custom_call_target="tpu_custom_call" | custom-call | flops 1024 | bytes 1024 | tf_op jit(solution)/shard_map/back_end/pallas_call | solution.py:539
  330.6 2.1 sum_first.3
  334.1 1.6 collective-permute-start.49
  338.7 10.6 %grad_attention.1 = (bf16[960,384]{1,0:T(8,128)(2,1)}, bf16[960,384]{1,0:T(8,128)(2,1)}, bf16[2,960,384]{2,1,0:T(8,128)(2,1)}, f32[8,128]{1,0:T(8,128)}) custom-call(s32[3]{0:T(128)} %pad_add_fusion.sc.refs_0_, bf16[256,960]{1,0:T(8,128)(2,1)} %get-tuple-element.154.rest_0_, bf16[256,960]{1,0:T(8,128)(2,1)} %get-tuple-element.130.rest_1_, ...), custom_call_target="tpu_custom_call" | custom-call | flops 1024 | bytes 1024 | tf_op jit(solution)/shard_map/grad_attention/pallas_call | solution.py:665
  349.8 1.6 collective-permute-start.48
  352.1 1.6 sum_third.3
  354.7 4.6 %collective-permute-start.56 = (bf16[480,640]{1,0:T(8,128)(2,1)S(1)}, bf16[480,640]{1,0:T(8,128)(2,1)S(1)}, u32[]{:S(2)}, u32[]{:S(2)}) collective-permute-start(bf16[480,640]{1,0:T(8,128)(2,1)S(1)} %get-tuple-element.212), channel_id=1, source_target_pairs={{0,2},{1,3},{2,0},{3,1},{4,6},{5,7},{6,4},{7,5},{8,10},{9,11},{10,... | collective-permute-start | bytes 1843208 | tf_op jit(solution)/shard_map/ppermute | solution.py:959
  359.3 1.7 collective-permute-done.47.refs_2_
  361.0 7.9 %collective-permute-done.48.refs_3_ = bf16[960,384]{1,0:T(8,128)(2,1)S(1)} collective-permute-done((bf16[960,384]{1,0:T(8,128)(2,1)}, bf16[960,384]{1,0:T(8,128)(2,1)S(1)}, u32[]{:S(2)}, u32[]{:S(2)}) %collective-permute-start.48) | collective-permute-done | bytes 737312 | tf_op jit(solution)/shard_map/ppermute | solution.py:953
  370.3 1.6 collective-permute-start.52
  371.9 11.9 %collective-permute-done.53.refs_2_ = bf16[2,240,640]{2,1,0:T(8,128)(2,1)S(1)} collective-permute-done((bf16[2,240,640]{2,1,0:T(8,128)(2,1)S(1)}, bf16[2,240,640]{2,1,0:T(8,128)(2,1)S(1)}, u32[]{:S(2)}, u32[]{:S(2)}) %collective-permute-start.53) | collective-permute-done | bytes 614432 | tf_op jit(solution)/shard_map/ppermute | solution.py:959
  387.9 4.4 collective-permute-start.54
  393.6 8.8 %collective-permute-done.55.refs_2_ = bf16[240,640]{1,0:T(8,128)(2,1)S(1)} collective-permute-done((bf16[240,640]{1,0:T(8,128)(2,1)S(1)}, bf16[240,640]{1,0:T(8,128)(2,1)S(1)}, u32[]{:S(2)}, u32[]{:S(2)}) %collective-permute-start.55) | collective-permute-done | bytes 307232 | tf_op jit(solution)/shard_map/ppermute | solution.py:959
  403.0 1.6 collective-permute-start.70
  405.2 2.2 collective-permute-start.59
  407.4 1.6 collective-permute-start.60
  409.4 1.7 collective-permute-start.68
  411.1 4.5 collective-permute-done.60.refs_2_
  416.3 1.6 collective-permute-start.58
  419.9 2.2 collective-permute-start.76
  422.5 3.3 collective-permute-done.77.refs_4_
  426.9 2.0 collective-permute-done.76.refs_3_
  428.9 1.9 collective-permute-start.62
  430.9 3.2 collective-permute-done.63.rest_3_
  434.1 3.1 collective-permute-done.62.rest_2_
  440.4 2.3 lay_down.1
  442.7 2.4 lay.2
  447.4 3.8 lay.3
  451.2 2.4 convert_bitcast_fusion
  (318 shorter events, 76.2 us)
Async XLA Ops:
  6.0 13.0 %collective-permute-start.1 = (bf16[240,384]{1,0:T(8,128)(2,1)}, bf16[240,384]{1,0:T(8,128)(2,1)S(1)}, u32[]{:S(2)}, u32[]{:S(2)}) collective-permute-start(bf16[240,384]{1,0:T(8,128)(2,1)} %pick_first.1.rest_0_), channel_id=1, source_target_pairs={{0,2},{1,3},{2,0},{3,1},{4,6},{5,7},{6,4},{7,5},{8,10},{9,11},{10,... | collective-permute-start | bytes 552968 | tf_op jit(solution)/shard_map/ppermute | solution.py:959
  10.1 9.6 %collective-permute-start = (bf16[240,384]{1,0:T(8,128)(2,1)}, bf16[240,384]{1,0:T(8,128)(2,1)S(1)}, u32[]{:S(2)}, u32[]{:S(2)}) collective-permute-start(bf16[240,384]{1,0:T(8,128)(2,1)} %pick_first.1.rest_0_), channel_id=1, source_target_pairs={{0,1},{1,0},{2,3},{3,2},{4,5},{5,4},{6,7},{7,6},{8,9},{9,8},{10,11... | collective-permute-start | bytes 552968 | tf_op jit(solution)/shard_map/ppermute | solution.py:959
  18.9 5.7 %collective-permute-start.2 = (bf16[240,384]{1,0:T(8,128)(2,1)S(1)}, bf16[240,384]{1,0:T(8,128)(2,1)S(1)}, u32[]{:S(2)}, u32[]{:S(2)}) collective-permute-start(bf16[240,384]{1,0:T(8,128)(2,1)S(1)} %collective-permute-done.1.rest_2_), channel_id=1, source_target_pairs={{0,1},{1,0},{2,3},{3,2},{4,5},{5,4},{6,7},{7,6},{8,9},{9,8},{10,11... | collective-permute-start | bytes 552968 | tf_op jit(solution)/shard_map/ppermute | solution.py:959
  26.2 19.6 %collective-permute-start.3 = (bf16[960,384]{1,0:T(8,128)(2,1)S(1)}, bf16[960,384]{1,0:T(8,128)(2,1)}, u32[]{:S(2)}, u32[]{:S(2)}) collective-permute-start(bf16[960,384]{1,0:T(8,128)(2,1)S(1)} %bitcast.24), channel_id=1, source_target_pairs={{0,8},{4,20},{8,0},{12,28},{16,24},{20,4},{24,16},{28,12},{1,9},{5... | collective-permute-start | bytes 2211848 | tf_op jit(solution)/shard_map/ppermute | solution.py:953
  27.7 25.2 %collective-permute-start.4 = (bf16[960,384]{1,0:T(8,128)(2,1)S(1)}, bf16[960,384]{1,0:T(8,128)(2,1)}, u32[]{:S(2)}, u32[]{:S(2)}) collective-permute-start(bf16[960,384]{1,0:T(8,128)(2,1)S(1)} %bitcast.25), channel_id=1, source_target_pairs={{0,16},{4,12},{8,24},{12,4},{16,0},{20,28},{24,8},{28,20},{1,17},{... | collective-permute-start | bytes 2211848 | tf_op jit(solution)/shard_map/ppermute | solution.py:953
  29.2 23.3 %collective-permute-start.11 = (bf16[368,640]{1,0:T(8,128)(2,1)S(1)}, bf16[368,640]{1,0:T(8,128)(2,1)S(1)}, u32[]{:S(2)}, u32[]{:S(2)}) collective-permute-start(bf16[368,640]{1,0:T(8,128)(2,1)S(1)} %pick.1.rest_4_.rest_0_), channel_id=1, source_target_pairs={{0,2},{1,3},{2,0},{3,1},{4,6},{5,7},{6,4},{7,5},{8,10},{9,11},{10,... | collective-permute-start | bytes 1413128 | tf_op jit(solution)/shard_map/ppermute | solution.py:959
  32.5 20.5 %collective-permute-start.10 = (bf16[368,640]{1,0:T(8,128)(2,1)S(1)}, bf16[368,640]{1,0:T(8,128)(2,1)S(1)}, u32[]{:S(2)}, u32[]{:S(2)}) collective-permute-start(bf16[368,640]{1,0:T(8,128)(2,1)S(1)} %pick.1.rest_4_.rest_0_), channel_id=1, source_target_pairs={{0,1},{1,0},{2,3},{3,2},{4,5},{5,4},{6,7},{7,6},{8,9},{9,8},{10,11... | collective-permute-start | bytes 1413128 | tf_op jit(solution)/shard_map/ppermute | solution.py:959
  45.7 18.6 %collective-permute-start.5 = (bf16[960,384]{1,0:T(8,128)(2,1)}, bf16[960,384]{1,0:T(8,128)(2,1)S(1)}, u32[]{:S(2)}, u32[]{:S(2)}) collective-permute-start(bf16[960,384]{1,0:T(8,128)(2,1)} %collective-permute-done.3.refs_1_.rest_1_), channel_id=1, source_target_pairs={{0,16},{4,12},{8,24},{12,4},{16,0},{20,28},{24,8},{28,20},{1,17},{... | collective-permute-start | bytes 2211848 | tf_op jit(solution)/shard_map/ppermute | solution.py:953
  52.9 11.4 %collective-permute-start.12 = (bf16[368,640]{1,0:T(8,128)(2,1)S(1)}, bf16[368,640]{1,0:T(8,128)(2,1)S(1)}, u32[]{:S(2)}, u32[]{:S(2)}) collective-permute-start(bf16[368,640]{1,0:T(8,128)(2,1)S(1)} %hold.4.rest_2_), channel_id=1, source_target_pairs={{0,1},{1,0},{2,3},{3,2},{4,5},{5,4},{6,7},{7,6},{8,9},{9,8},{10,11... | collective-permute-start | bytes 1413128 | tf_op jit(solution)/shard_map/ppermute | solution.py:959
  67.3 41.3 %collective-permute-start.16 = (bf16[4,368,640]{2,1,0:T(8,128)(2,1)}, bf16[4,368,640]{2,1,0:T(8,128)(2,1)S(1)}, u32[]{:S(2)}, u32[]{:S(2)}) collective-permute-start(bf16[4,368,640]{2,1,0:T(8,128)(2,1)} %stack.31.rest_8_), channel_id=1, source_target_pairs={{0,16},{4,12},{8,24},{12,4},{16,0},{20,28},{24,8},{28,20},{1,17},{... | collective-permute-start | bytes 5652488 | tf_op jit(solution)/shard_map/ppermute | solution.py:953
  67.9 40.7 %collective-permute-start.13 = (bf16[4,368,640]{2,1,0:T(8,128)(2,1)}, bf16[4,368,640]{2,1,0:T(8,128)(2,1)}, u32[]{:S(2)}, u32[]{:S(2)}) collective-permute-start(bf16[4,368,640]{2,1,0:T(8,128)(2,1)} %stack.31.rest_8_), channel_id=1, source_target_pairs={{0,8},{4,20},{8,0},{12,28},{16,24},{20,4},{24,16},{28,12},{1,9},{5... | collective-permute-start | bytes 5652488 | tf_op jit(solution)/shard_map/ppermute | solution.py:953
  68.4 11.2 %collective-permute-start.6 = (bf16[960,384]{1,0:T(8,128)(2,1)S(1)}, bf16[960,384]{1,0:T(8,128)(2,1)S(1)}, u32[]{:S(2)}, u32[]{:S(2)}) collective-permute-start(bf16[960,384]{1,0:T(8,128)(2,1)S(1)} %bitcast.26), channel_id=1, source_target_pairs={{0,4},{4,0},{8,12},{12,8},{16,20},{20,16},{24,28},{28,24},{1,5},{5... | collective-permute-start | bytes 2211848 | tf_op jit(solution)/shard_map/ppermute | solution.py:953
  68.5 5.3 %collective-permute-start.14 = (bf16[976,256]{1,0:T(8,128)(2,1)S(1)}, bf16[976,256]{1,0:T(8,128)(2,1)S(1)}, u32[]{:S(2)}, u32[]{:S(2)}) collective-permute-start(bf16[976,256]{1,0:T(8,128)(2,1)S(1)} %pad_maximum_fusion), channel_id=1, source_target_pairs={{0,0},{1,4},{2,1},{3,5},{4,2},{5,6},{6,3},{7,7},{8,8},{9,12},{10,9... | collective-permute-start | bytes 1499144 | tf_op jit(solution)/shard_map/ppermute | solution.py:970
  69.2 14.1 %collective-permute-start.8 = (bf16[960,384]{1,0:T(8,128)(2,1)}, bf16[960,384]{1,0:T(8,128)(2,1)}, u32[]{:S(2)}, u32[]{:S(2)}) collective-permute-start(bf16[960,384]{1,0:T(8,128)(2,1)} %collective-permute-done.4.refs_2_.rest_2_), channel_id=1, source_target_pairs={{0,4},{4,0},{8,12},{12,8},{16,20},{20,16},{24,28},{28,24},{1,5},{5... | collective-permute-start | bytes 2211848 | tf_op jit(solution)/shard_map/ppermute | solution.py:953
  73.7 9.5 %collective-permute-start.7 = (bf16[960,384]{1,0:T(8,128)(2,1)}, bf16[960,384]{1,0:T(8,128)(2,1)}, u32[]{:S(2)}, u32[]{:S(2)}) collective-permute-start(bf16[960,384]{1,0:T(8,128)(2,1)} %collective-permute-done.3.refs_1_.rest_1_), channel_id=1, source_target_pairs={{0,4},{4,0},{8,12},{12,8},{16,20},{20,16},{24,28},{28,24},{1,5},{5... | collective-permute-start | bytes 2211848 | tf_op jit(solution)/shard_map/ppermute | solution.py:953
  90.7 17.1 %collective-permute-start.15 = (bf16[656,256]{1,0:T(8,128)(2,1)}, bf16[656,256]{1,0:T(8,128)(2,1)S(1)}, u32[]{:S(2)}, u32[]{:S(2)}) collective-permute-start(bf16[656,256]{1,0:T(8,128)(2,1)} %get-tuple-element.124.kv2.rest_16_), channel_id=1, source_target_pairs={{0,1},{2,3},{4,5},{6,7},{8,9},{10,11},{12,13},{14,15},{16,17},{18,... | collective-permute-start | bytes 1007624 | tf_op jit(solution)/shard_map/ppermute | solution.py:992
  108.6 24.1 %collective-permute-start.17 = (bf16[4,368,640]{2,1,0:T(8,128)(2,1)}, bf16[4,368,640]{2,1,0:T(8,128)(2,1)}, u32[]{:S(2)}, u32[]{:S(2)}) collective-permute-start(bf16[4,368,640]{2,1,0:T(8,128)(2,1)} %hold.5.rest_9_), channel_id=1, source_target_pairs={{0,16},{4,12},{8,24},{12,4},{16,0},{20,28},{24,8},{28,20},{1,17},{... | collective-permute-start | bytes 5652488 | tf_op jit(solution)/shard_map/ppermute | solution.py:953
  109.2 23.6 %collective-permute-start.19 = (bf16[4,368,640]{2,1,0:T(8,128)(2,1)}, bf16[4,368,640]{2,1,0:T(8,128)(2,1)S(1)}, u32[]{:S(2)}, u32[]{:S(2)}) collective-permute-start(bf16[4,368,640]{2,1,0:T(8,128)(2,1)} %stack.31.rest_8_), channel_id=1, source_target_pairs={{0,4},{4,0},{8,12},{12,8},{16,20},{20,16},{24,28},{28,24},{1,5},{5... | collective-permute-start | bytes 5652488 | tf_op jit(solution)/shard_map/ppermute | solution.py:953
  121.0 13.2 %collective-permute-start.20 = (bf16[4,368,640]{2,1,0:T(8,128)(2,1)}, bf16[4,368,640]{2,1,0:T(8,128)(2,1)}, u32[]{:S(2)}, u32[]{:S(2)}) collective-permute-start(bf16[4,368,640]{2,1,0:T(8,128)(2,1)} %hold.5.rest_9_), channel_id=1, source_target_pairs={{0,4},{4,0},{8,12},{12,8},{16,20},{20,16},{24,28},{28,24},{1,5},{5... | collective-permute-start | bytes 5652488 | tf_op jit(solution)/shard_map/ppermute | solution.py:953
  121.2 11.6 %collective-permute-start.21 = (bf16[4,368,640]{2,1,0:T(8,128)(2,1)S(1)}, bf16[4,368,640]{2,1,0:T(8,128)(2,1)S(1)}, u32[]{:S(2)}, u32[]{:S(2)}) collective-permute-start(bf16[4,368,640]{2,1,0:T(8,128)(2,1)S(1)} %collective-permute-done.16.refs_2_.rest_10_), channel_id=1, source_target_pairs={{0,4},{4,0},{8,12},{12,8},{16,20},{20,16},{24,28},{28,24},{1,5},{5... | collective-permute-start | bytes 5652488 | tf_op jit(solution)/shard_map/ppermute | solution.py:953
  132.8 4.2 collective-permute-start.22
  155.0 15.2 %collective-permute-start.29 = (bf16[256,2560]{1,0:T(8,128)(2,1)}, bf16[256,2560]{1,0:T(8,128)(2,1)S(1)}, u32[]{:S(2)}, u32[]{:S(2)}) collective-permute-start(bf16[256,2560]{1,0:T(8,128)(2,1)} %get-tuple-element.133.rest_5_), channel_id=1, source_target_pairs={{0,4},{4,0},{8,12},{12,8},{16,20},{20,16},{24,28},{28,24},{1,5},{5... | collective-permute-start | bytes 3932168 | tf_op jit(solution)/shard_map/ppermute | solution.py:953
  155.2 12.2 %collective-permute-start.24 = (bf16[656,256]{1,0:T(8,128)(2,1)}, bf16[656,256]{1,0:T(8,128)(2,1)S(1)}, u32[]{:S(2)}, u32[]{:S(2)}) collective-permute-start(bf16[656,256]{1,0:T(8,128)(2,1)} %get-tuple-element.129.kv2.rest_16_), channel_id=1, source_target_pairs={{0,1},{2,3},{4,5},{6,7},{8,9},{10,11},{12,13},{14,15},{16,17},{18,... | collective-permute-start | bytes 1007624 | tf_op jit(solution)/shard_map/ppermute | solution.py:992
  158.9 9.5 %collective-permute-start.26 = (bf16[256,960]{1,0:T(8,128)(2,1)S(1)}, bf16[256,960]{1,0:T(8,128)(2,1)S(1)}, u32[]{:S(2)}, u32[]{:S(2)}) collective-permute-start(bf16[256,960]{1,0:T(8,128)(2,1)S(1)} %copy-done.67), channel_id=1, source_target_pairs={{0,4},{4,0},{8,12},{12,8},{16,20},{20,16},{24,28},{28,24},{1,5},{5... | collective-permute-start | bytes 1474568 | tf_op jit(solution)/shard_map/ppermute | solution.py:953
  159.1 23.7 %collective-permute-start.23 = (bf16[960,256]{1,0:T(8,128)(2,1)S(1)}, bf16[960,256]{1,0:T(8,128)(2,1)S(1)}, u32[]{:S(2)}, u32[]{:S(2)}) collective-permute-start(bf16[960,256]{1,0:T(8,128)(2,1)S(1)} %bitcast.40), channel_id=1, source_target_pairs={{0,0},{1,4},{2,1},{3,5},{4,2},{5,6},{6,3},{7,7},{8,8},{9,12},{10,9... | collective-permute-start | bytes 1474568 | tf_op jit(solution)/shard_map/ppermute | solution.py:970
  159.7 8.8 %collective-permute-start.27 = (bf16[256,960]{1,0:T(8,128)(2,1)}, bf16[256,960]{1,0:T(8,128)(2,1)S(1)}, u32[]{:S(2)}, u32[]{:S(2)}) collective-permute-start(bf16[256,960]{1,0:T(8,128)(2,1)} %get-tuple-element.131.rest_1_), channel_id=1, source_target_pairs={{0,4},{4,0},{8,12},{12,8},{16,20},{20,16},{24,28},{28,24},{1,5},{5... | collective-permute-start | bytes 1474568 | tf_op jit(solution)/shard_map/ppermute | solution.py:953
  168.6 66.7 %collective-permute-start.35 = (bf16[256,960]{1,0:T(8,128)(2,1)}, bf16[256,960]{1,0:T(8,128)(2,1)}, u32[]{:S(2)}, u32[]{:S(2)}) collective-permute-start(bf16[256,960]{1,0:T(8,128)(2,1)} %get-tuple-element.154.rest_0_), channel_id=1, source_target_pairs={{0,4},{4,0},{8,12},{12,8},{16,20},{20,16},{24,28},{28,24},{1,5},{5... | collective-permute-start | bytes 1474568 | tf_op jit(solution)/shard_map/ppermute | solution.py:953
  218.6 32.3 %collective-permute-start.34 = (bf16[256,2560]{1,0:T(8,128)(2,1)}, bf16[256,2560]{1,0:T(8,128)(2,1)S(1)}, u32[]{:S(2)}, u32[]{:S(2)}) collective-permute-start(bf16[256,2560]{1,0:T(8,128)(2,1)} %get-tuple-element.153), channel_id=1, source_target_pairs={{0,4},{4,0},{8,12},{12,8},{16,20},{20,16},{24,28},{28,24},{1,5},{5... | collective-permute-start | bytes 3932168 | tf_op jit(solution)/shard_map/ppermute | solution.py:953
  218.7 32.2 %collective-permute-start.38 = (bf16[256,2560]{1,0:T(8,128)(2,1)}, bf16[256,2560]{1,0:T(8,128)(2,1)S(1)}, u32[]{:S(2)}, u32[]{:S(2)}) collective-permute-start(bf16[256,2560]{1,0:T(8,128)(2,1)} %get-tuple-element.157.rest_4_), channel_id=1, source_target_pairs={{0,4},{4,0},{8,12},{12,8},{16,20},{20,16},{24,28},{28,24},{1,5},{5... | collective-permute-start | bytes 3932168 | tf_op jit(solution)/shard_map/ppermute | solution.py:953
  219.2 17.7 %collective-permute-start.36 = (bf16[256,960]{1,0:T(8,128)(2,1)}, bf16[256,960]{1,0:T(8,128)(2,1)S(1)}, u32[]{:S(2)}, u32[]{:S(2)}) collective-permute-start(bf16[256,960]{1,0:T(8,128)(2,1)} %get-tuple-element.155.rest_0_), channel_id=1, source_target_pairs={{0,4},{4,0},{8,12},{12,8},{16,20},{20,16},{24,28},{28,24},{1,5},{5... | collective-permute-start | bytes 1474568 | tf_op jit(solution)/shard_map/ppermute | solution.py:953
  239.0 11.9 %collective-permute-start.31 = (bf16[640,256]{1,0:T(8,128)(2,1)S(1)}, bf16[640,256]{1,0:T(8,128)(2,1)S(1)}, u32[]{:S(2)}, u32[]{:S(2)}) collective-permute-start(bf16[640,256]{1,0:T(8,128)(2,1)S(1)} %get-tuple-element.147), channel_id=1, source_target_pairs={{1,0},{3,2},{5,4},{7,6},{9,8},{11,10},{13,12},{15,14},{17,16},{19,... | collective-permute-start | bytes 983048 | tf_op jit(solution)/shard_map/ppermute | solution.py:1001
  289.4 40.5 %collective-permute-start.46 = (bf16[2,960,640]{2,1,0:T(8,128)(2,1)}, bf16[2,960,640]{2,1,0:T(8,128)(2,1)S(1)}, u32[]{:S(2)}, u32[]{:S(2)}) collective-permute-start(bf16[2,960,640]{2,1,0:T(8,128)(2,1)} %get-tuple-element.188), channel_id=1, source_target_pairs={{0,8},{4,20},{8,0},{12,28},{16,24},{20,4},{24,16},{28,12},{1,9},{5... | collective-permute-start | bytes 7372808 | tf_op jit(solution)/shard_map/ppermute | solution.py:953
  306.5 4.0 collective-permute-start.43
  309.2 13.0 %collective-permute-start.42 = (bf16[640,256]{1,0:T(8,128)(2,1)S(1)}, bf16[640,256]{1,0:T(8,128)(2,1)S(1)}, u32[]{:S(2)}, u32[]{:S(2)}) collective-permute-start(bf16[640,256]{1,0:T(8,128)(2,1)S(1)} %get-tuple-element.171), channel_id=1, source_target_pairs={{1,0},{3,2},{5,4},{7,6},{9,8},{11,10},{13,12},{15,14},{17,16},{19,... | collective-permute-start | bytes 983048 | tf_op jit(solution)/shard_map/ppermute | solution.py:1001
  319.4 31.9 %collective-permute-start.50 = (bf16[2,480,640]{2,1,0:T(8,128)(2,1)}, bf16[2,480,640]{2,1,0:T(8,128)(2,1)}, u32[]{:S(2)}, u32[]{:S(2)}) collective-permute-start(bf16[2,480,640]{2,1,0:T(8,128)(2,1)} %get-tuple-element.196), channel_id=1, source_target_pairs={{0,1},{1,0},{2,3},{3,2},{4,5},{5,4},{6,7},{7,6},{8,9},{9,8},{10,11... | collective-permute-start | bytes 3686408 | tf_op jit(solution)/shard_map/ppermute | solution.py:959
  334.1 19.5 %collective-permute-start.49 = (bf16[960,640]{1,0:T(8,128)(2,1)}, bf16[960,640]{1,0:T(8,128)(2,1)S(1)}, u32[]{:S(2)}, u32[]{:S(2)}) collective-permute-start(bf16[960,640]{1,0:T(8,128)(2,1)} %get-tuple-element.194), channel_id=1, source_target_pairs={{0,16},{4,12},{8,24},{12,4},{16,0},{20,28},{24,8},{28,20},{1,17},{... | collective-permute-start | bytes 3686408 | tf_op jit(solution)/shard_map/ppermute | solution.py:953
  349.3 11.7 %collective-permute-start.47 = (bf16[960,384]{1,0:T(8,128)(2,1)}, bf16[960,384]{1,0:T(8,128)(2,1)S(1)}, u32[]{:S(2)}, u32[]{:S(2)}) collective-permute-start(bf16[960,384]{1,0:T(8,128)(2,1)} %get-tuple-element.191), channel_id=1, source_target_pairs={{0,8},{4,20},{8,0},{12,28},{16,24},{20,4},{24,16},{28,12},{1,9},{5... | collective-permute-start | bytes 2211848 | tf_op jit(solution)/shard_map/ppermute | solution.py:953
  349.8 19.1 %collective-permute-start.48 = (bf16[960,384]{1,0:T(8,128)(2,1)}, bf16[960,384]{1,0:T(8,128)(2,1)S(1)}, u32[]{:S(2)}, u32[]{:S(2)}) collective-permute-start(bf16[960,384]{1,0:T(8,128)(2,1)} %get-tuple-element.192), channel_id=1, source_target_pairs={{0,8},{4,20},{8,0},{12,28},{16,24},{20,4},{24,16},{28,12},{1,9},{5... | collective-permute-start | bytes 2211848 | tf_op jit(solution)/shard_map/ppermute | solution.py:953
  354.7 29.2 %collective-permute-start.53 = (bf16[2,240,640]{2,1,0:T(8,128)(2,1)S(1)}, bf16[2,240,640]{2,1,0:T(8,128)(2,1)S(1)}, u32[]{:S(2)}, u32[]{:S(2)}) collective-permute-start(bf16[2,240,640]{2,1,0:T(8,128)(2,1)S(1)} %get-tuple-element.204), channel_id=1, source_target_pairs={{0,1},{1,0},{2,3},{3,2},{4,5},{5,4},{6,7},{7,6},{8,9},{9,8},{10,11... | collective-permute-start | bytes 1843208 | tf_op jit(solution)/shard_map/ppermute | solution.py:959
  354.7 30.6 %collective-permute-start.56 = (bf16[480,640]{1,0:T(8,128)(2,1)S(1)}, bf16[480,640]{1,0:T(8,128)(2,1)S(1)}, u32[]{:S(2)}, u32[]{:S(2)}) collective-permute-start(bf16[480,640]{1,0:T(8,128)(2,1)S(1)} %get-tuple-element.212), channel_id=1, source_target_pairs={{0,2},{1,3},{2,0},{3,1},{4,6},{5,7},{6,4},{7,5},{8,10},{9,11},{10,... | collective-permute-start | bytes 1843208 | tf_op jit(solution)/shard_map/ppermute | solution.py:959
  369.8 14.7 %collective-permute-start.51 = (bf16[480,384]{1,0:T(8,128)(2,1)S(1)}, bf16[480,384]{1,0:T(8,128)(2,1)S(1)}, u32[]{:S(2)}, u32[]{:S(2)}) collective-permute-start(bf16[480,384]{1,0:T(8,128)(2,1)S(1)} %get-tuple-element.201), channel_id=1, source_target_pairs={{0,16},{4,12},{8,24},{12,4},{16,0},{20,28},{24,8},{28,20},{1,17},{... | collective-permute-start | bytes 1105928 | tf_op jit(solution)/shard_map/ppermute | solution.py:953
  370.3 14.2 %collective-permute-start.52 = (bf16[480,384]{1,0:T(8,128)(2,1)S(1)}, bf16[480,384]{1,0:T(8,128)(2,1)S(1)}, u32[]{:S(2)}, u32[]{:S(2)}) collective-permute-start(bf16[480,384]{1,0:T(8,128)(2,1)S(1)} %get-tuple-element.202), channel_id=1, source_target_pairs={{0,16},{4,12},{8,24},{12,4},{16,0},{20,28},{24,8},{28,20},{1,17},{... | collective-permute-start | bytes 1105928 | tf_op jit(solution)/shard_map/ppermute | solution.py:953
  386.1 6.9 %collective-permute-start.57 = (bf16[2,120,640]{2,1,0:T(8,128)(2,1)S(1)}, bf16[2,120,640]{2,1,0:T(8,128)(2,1)S(1)}, u32[]{:S(2)}, u32[]{:S(2)}) collective-permute-start(bf16[2,120,640]{2,1,0:T(8,128)(2,1)S(1)} %get-tuple-element.215), channel_id=1, source_target_pairs={{0,8},{4,20},{8,0},{12,28},{16,24},{20,4},{24,16},{28,12},{1,9},{5... | collective-permute-start | bytes 921608 | tf_op jit(solution)/shard_map/ppermute | solution.py:953
  386.6 15.8 %collective-permute-start.55 = (bf16[240,640]{1,0:T(8,128)(2,1)S(1)}, bf16[240,640]{1,0:T(8,128)(2,1)S(1)}, u32[]{:S(2)}, u32[]{:S(2)}) collective-permute-start(bf16[240,640]{1,0:T(8,128)(2,1)S(1)} %get-tuple-element.210), channel_id=1, source_target_pairs={{0,2},{1,3},{2,0},{3,1},{4,6},{5,7},{6,4},{7,5},{8,10},{9,11},{10,... | collective-permute-start | bytes 921608 | tf_op jit(solution)/shard_map/ppermute | solution.py:959
  387.9 16.7 %collective-permute-start.54 = (bf16[2,240,384]{2,1,0:T(8,128)(2,1)S(1)}, bf16[2,240,384]{2,1,0:T(8,128)(2,1)S(1)}, u32[]{:S(2)}, u32[]{:S(2)}) collective-permute-start(bf16[2,240,384]{2,1,0:T(8,128)(2,1)S(1)} %get-tuple-element.208), channel_id=1, source_target_pairs={{0,1},{1,0},{2,3},{3,2},{4,5},{5,4},{6,7},{7,6},{8,9},{9,8},{10,11... | collective-permute-start | bytes 1105928 | tf_op jit(solution)/shard_map/ppermute | solution.py:959
  403.0 14.9 %collective-permute-start.70 = (bf16[240,640]{1,0:T(8,128)(2,1)S(1)}, bf16[240,640]{1,0:T(8,128)(2,1)S(1)}, u32[]{:S(2)}, u32[]{:S(2)}) collective-permute-start(bf16[240,640]{1,0:T(8,128)(2,1)S(1)} %get-tuple-element.232.rest_0_), channel_id=1, source_target_pairs={{0,24},{4,28},{8,16},{12,20},{16,8},{20,12},{24,0},{28,4},{1,25},{... | collective-permute-start | bytes 921608 | tf_op jit(solution)/shard_map/ppermute | solution.py:953
  405.2 11.1 %collective-permute-start.59 = (bf16[240,384]{1,0:T(8,128)(2,1)S(1)}, bf16[240,384]{1,0:T(8,128)(2,1)S(1)}, u32[]{:S(2)}, u32[]{:S(2)}) collective-permute-start(bf16[240,384]{1,0:T(8,128)(2,1)S(1)} %get-tuple-element.221), channel_id=1, source_target_pairs={{0,2},{1,3},{2,0},{3,1},{4,6},{5,7},{6,4},{7,5},{8,10},{9,11},{10,... | collective-permute-start | bytes 552968 | tf_op jit(solution)/shard_map/ppermute | solution.py:959
  407.4 8.2 %collective-permute-start.60 = (bf16[120,640]{1,0:T(8,128)(2,1)S(1)}, bf16[120,640]{1,0:T(8,128)(2,1)S(1)}, u32[]{:S(2)}, u32[]{:S(2)}) collective-permute-start(bf16[120,640]{1,0:T(8,128)(2,1)S(1)} %get-tuple-element.223), channel_id=1, source_target_pairs={{0,16},{4,12},{8,24},{12,4},{16,0},{20,28},{24,8},{28,20},{1,17},{... | collective-permute-start | bytes 460808 | tf_op jit(solution)/shard_map/ppermute | solution.py:953
  409.0 10.9 %collective-permute-start.69 = (bf16[240,640]{1,0:T(8,128)(2,1)S(1)}, bf16[240,640]{1,0:T(8,128)(2,1)S(1)}, u32[]{:S(2)}, u32[]{:S(2)}) collective-permute-start(bf16[240,640]{1,0:T(8,128)(2,1)S(1)} %get-tuple-element.232.rest_0_), channel_id=1, source_target_pairs={{0,16},{4,12},{8,24},{12,4},{16,0},{20,28},{24,8},{28,20},{1,17},{... | collective-permute-start | bytes 921608 | tf_op jit(solution)/shard_map/ppermute | solution.py:953
  409.4 12.7 %collective-permute-start.68 = (bf16[240,640]{1,0:T(8,128)(2,1)S(1)}, bf16[240,640]{1,0:T(8,128)(2,1)S(1)}, u32[]{:S(2)}, u32[]{:S(2)}) collective-permute-start(bf16[240,640]{1,0:T(8,128)(2,1)S(1)} %get-tuple-element.232.rest_0_), channel_id=1, source_target_pairs={{0,8},{4,20},{8,0},{12,28},{16,24},{20,4},{24,16},{28,12},{1,9},{5... | collective-permute-start | bytes 921608 | tf_op jit(solution)/shard_map/ppermute | solution.py:953
  416.2 5.9 %collective-permute-start.78 = (bf16[120,640]{1,0:T(8,128)(2,1)S(1)}, bf16[120,640]{1,0:T(8,128)(2,1)S(1)}, u32[]{:S(2)}, u32[]{:S(2)}) collective-permute-start(bf16[120,640]{1,0:T(8,128)(2,1)S(1)} %get-tuple-element.235.refs_1_), channel_id=1, source_target_pairs={{0,4},{4,0},{8,12},{12,8},{16,20},{20,16},{24,28},{28,24},{1,5},{5... | collective-permute-start | bytes 460808 | tf_op jit(solution)/shard_map/ppermute | solution.py:953
  416.3 34.9 %collective-permute-start.58 = (bf16[1920,256]{1,0:T(8,128)(2,1)S(1)}, bf16[1920,256]{1,0:T(8,128)(2,1)}, u32[]{:S(2)}, u32[]{:S(2)}) collective-permute-start(bf16[1920,256]{1,0:T(8,128)(2,1)S(1)} %hold.7), channel_id=1, source_target_pairs={{0,0},{4,1},{1,2},{5,3},{2,4},{6,5},{3,6},{7,7},{8,8},{12,9},{9,10... | collective-permute-start | bytes 2949128 | tf_op jit(solution)/shard_map/ppermute | solution.py:970
  417.9 7.8 %collective-permute-start.77 = (bf16[120,640]{1,0:T(8,128)(2,1)S(1)}, bf16[120,640]{1,0:T(8,128)(2,1)S(1)}, u32[]{:S(2)}, u32[]{:S(2)}) collective-permute-start(bf16[120,640]{1,0:T(8,128)(2,1)S(1)} %get-tuple-element.235.refs_1_), channel_id=1, source_target_pairs={{0,24},{4,28},{8,16},{12,20},{16,8},{20,12},{24,0},{28,4},{1,25},{... | collective-permute-start | bytes 460808 | tf_op jit(solution)/shard_map/ppermute | solution.py:953
  419.9 9.0 %collective-permute-start.76 = (bf16[120,640]{1,0:T(8,128)(2,1)S(1)}, bf16[120,640]{1,0:T(8,128)(2,1)S(1)}, u32[]{:S(2)}, u32[]{:S(2)}) collective-permute-start(bf16[120,640]{1,0:T(8,128)(2,1)S(1)} %get-tuple-element.235.refs_1_), channel_id=1, source_target_pairs={{0,16},{4,12},{8,24},{12,4},{16,0},{20,28},{24,8},{28,20},{1,17},{... | collective-permute-start | bytes 460808 | tf_op jit(solution)/shard_map/ppermute | solution.py:953
  422.1 8.7 %collective-permute-start.75 = (bf16[120,640]{1,0:T(8,128)(2,1)S(1)}, bf16[120,640]{1,0:T(8,128)(2,1)S(1)}, u32[]{:S(2)}, u32[]{:S(2)}) collective-permute-start(bf16[120,640]{1,0:T(8,128)(2,1)S(1)} %get-tuple-element.235.refs_1_), channel_id=1, source_target_pairs={{0,8},{4,20},{8,0},{12,28},{16,24},{20,4},{24,16},{28,12},{1,9},{5... | collective-permute-start | bytes 460808 | tf_op jit(solution)/shard_map/ppermute | solution.py:953
  422.1 8.8 %collective-permute-start.64 = (bf16[240,384]{1,0:T(8,128)(2,1)S(1)}, bf16[240,384]{1,0:T(8,128)(2,1)S(1)}, u32[]{:S(2)}, u32[]{:S(2)}) collective-permute-start(bf16[240,384]{1,0:T(8,128)(2,1)S(1)} %get-tuple-element.225.rest_0_), channel_id=1, source_target_pairs={{0,4},{4,0},{8,12},{12,8},{16,20},{20,16},{24,28},{28,24},{1,5},{5... | collective-permute-start | bytes 552968 | tf_op jit(solution)/shard_map/ppermute | solution.py:953
  425.8 8.4 %collective-permute-start.63 = (bf16[240,384]{1,0:T(8,128)(2,1)S(1)}, bf16[240,384]{1,0:T(8,128)(2,1)S(1)}, u32[]{:S(2)}, u32[]{:S(2)}) collective-permute-start(bf16[240,384]{1,0:T(8,128)(2,1)S(1)} %get-tuple-element.225.rest_0_), channel_id=1, source_target_pairs={{0,24},{4,28},{8,16},{12,20},{16,8},{20,12},{24,0},{28,4},{1,25},{... | collective-permute-start | bytes 552968 | tf_op jit(solution)/shard_map/ppermute | solution.py:953
  428.9 8.3 %collective-permute-start.62 = (bf16[240,384]{1,0:T(8,128)(2,1)S(1)}, bf16[240,384]{1,0:T(8,128)(2,1)S(1)}, u32[]{:S(2)}, u32[]{:S(2)}) collective-permute-start(bf16[240,384]{1,0:T(8,128)(2,1)S(1)} %get-tuple-element.225.rest_0_), channel_id=1, source_target_pairs={{0,16},{4,12},{8,24},{12,4},{16,0},{20,28},{24,8},{28,20},{1,17},{... | collective-permute-start | bytes 552968 | tf_op jit(solution)/shard_map/ppermute | solution.py:953
  430.8 6.7 %collective-permute-start.61 = (bf16[240,384]{1,0:T(8,128)(2,1)S(1)}, bf16[240,384]{1,0:T(8,128)(2,1)S(1)}, u32[]{:S(2)}, u32[]{:S(2)}) collective-permute-start(bf16[240,384]{1,0:T(8,128)(2,1)S(1)} %get-tuple-element.225.rest_0_), channel_id=1, source_target_pairs={{0,8},{4,20},{8,0},{12,28},{16,24},{20,4},{24,16},{28,12},{1,9},{5... | collective-permute-start | bytes 552968 | tf_op jit(solution)/shard_map/ppermute | solution.py:953
  430.9 6.8 %collective-permute-start.81 = (bf16[120,640]{1,0:T(8,128)(2,1)S(1)}, bf16[120,640]{1,0:T(8,128)(2,1)S(1)}, u32[]{:S(2)}, u32[]{:S(2)}) collective-permute-start(bf16[120,640]{1,0:T(8,128)(2,1)S(1)} %collective-permute-done.77.refs_4_), channel_id=1, source_target_pairs={{0,4},{4,0},{8,12},{12,8},{16,20},{20,16},{24,28},{28,24},{1,5},{5... | collective-permute-start | bytes 460808 | tf_op jit(solution)/shard_map/ppermute | solution.py:953
  439.4 8.0 %collective-permute-start.71 = (bf16[240,640]{1,0:T(8,128)(2,1)S(1)}, bf16[240,640]{1,0:T(8,128)(2,1)S(1)}, u32[]{:S(2)}, u32[]{:S(2)}) collective-permute-start(bf16[240,640]{1,0:T(8,128)(2,1)S(1)} %get-tuple-element.232.rest_0_), channel_id=1, source_target_pairs={{0,4},{4,0},{8,12},{12,8},{16,20},{20,16},{24,28},{28,24},{1,5},{5... | collective-permute-start | bytes 921608 | tf_op jit(solution)/shard_map/ppermute | solution.py:953
  439.6 7.8 %collective-permute-start.74 = (bf16[240,640]{1,0:T(8,128)(2,1)S(1)}, bf16[240,640]{1,0:T(8,128)(2,1)}, u32[]{:S(2)}, u32[]{:S(2)}) collective-permute-start(bf16[240,640]{1,0:T(8,128)(2,1)S(1)} %collective-permute-done.70.rest_3_), channel_id=1, source_target_pairs={{0,4},{4,0},{8,12},{12,8},{16,20},{20,16},{24,28},{28,24},{1,5},{5... | collective-permute-start | bytes 921608 | tf_op jit(solution)/shard_map/ppermute | solution.py:953
  439.9 7.5 %collective-permute-start.73 = (bf16[240,640]{1,0:T(8,128)(2,1)S(1)}, bf16[240,640]{1,0:T(8,128)(2,1)}, u32[]{:S(2)}, u32[]{:S(2)}) collective-permute-start(bf16[240,640]{1,0:T(8,128)(2,1)S(1)} %collective-permute-done.69.rest_2_), channel_id=1, source_target_pairs={{0,4},{4,0},{8,12},{12,8},{16,20},{20,16},{24,28},{28,24},{1,5},{5... | collective-permute-start | bytes 921608 | tf_op jit(solution)/shard_map/ppermute | solution.py:953
  440.2 7.3 %collective-permute-start.72 = (bf16[240,640]{1,0:T(8,128)(2,1)S(1)}, bf16[240,640]{1,0:T(8,128)(2,1)}, u32[]{:S(2)}, u32[]{:S(2)}) collective-permute-start(bf16[240,640]{1,0:T(8,128)(2,1)S(1)} %collective-permute-done.68.rest_1_), channel_id=1, source_target_pairs={{0,4},{4,0},{8,12},{12,8},{16,20},{20,16},{24,28},{28,24},{1,5},{5... | collective-permute-start | bytes 921608 | tf_op jit(solution)/shard_map/ppermute | solution.py:953
  (99 other events, 837.9 us)

commit v17 on v16

--- a/solution.py
+++ b/solution.py
@@ -622,11 +622,11 @@
     )(sc, *lefts, *rights, *after)
 
 
-def grad_attention_kernel(sc, *rest):
+def grad_attention_kernel(first, sc, *rest):
     a_refs, o_refs, rest = rest[:4], rest[4:8], rest[8:]
     queries, keys, values, outs, threes, ones = (rest[i : i + 2] for i in range(0, 12, 2))
     gain_a, gain_f = (rest[i : i + 2] for i in (12, 14))
-    *sends, keep_ref, token_ref, left, right = rest[-6:]
+    *outs_of, token_ref, left, right = rest[-5:]
     token_ref[...] = jnp.zeros_like(token_ref)
     core, chip = sc[0], sc[1]
     n, width = a_refs[0].shape
@@ -652,21 +652,20 @@
         turned(left.at[1], o_refs)
         fill(0, 1, outs, values, 0)
 
-    for i, m in enumerate(by_turn(core, chip)):
-        out = sends[i] if i < 2 else keep_ref.at[i - 2]
+    for out, m in zip(outs_of, by_turn(core, chip)[first : first + 2]):
         which = jnp.where(m > 0, core, 0)
         out[...] = nn(left[which], right[m]).astype(bf16)
         out[:, KVW:] = gains
 
 
-def grad_attention(sc, a, o, own, got, gains, after):
+def grad_attention(first, sc, a, o, own, got, gains, after):
     n, width = a[0].shape
     out = shape((width, PIECE), bf16)
     return pl.pallas_call(
-        grad_attention_kernel,
-        out_shape=(out, out, shape((2, width, PIECE), bf16), TOKEN),
+        functools.partial(grad_attention_kernel, first),
+        out_shape=(out, out, TOKEN),
         in_specs=[SCALARS] + [WHOLE] * 24 + [LEFT] * len(after),
-        out_specs=(WHOLE,) * 4,
+        out_specs=(WHOLE,) * 3,
         scratch_shapes=[pltpu.VMEM((2, width, 4 * n), bf16), pltpu.VMEM((4, 4 * n, PIECE), bf16)],
         cost_estimate=BRIEF,
         compiler_params=pltpu.CompilerParams(vmem_limit_bytes=LIMIT),
@@ -675,6 +674,9 @@
 
 
 def lay_kernel(count, sc, *rest):
+    token_ref = rest[-2]
+    token_ref[...] = jnp.zeros_like(token_ref)
+    rest = (*rest[:-2], rest[-1])
     mine, other, outs, kept = rest[:4], rest[4:8], rest[-1 - count : -1], rest[-1]
     core, chip = sc[0], sc[1]
     for kind, pieces in ((core, mine), (1 - core, other)):
@@ -701,9 +703,9 @@
         outs += (shape((2, rows), f32),)
     return pl.pallas_call(
         functools.partial(lay_kernel, len(outs)),
-        out_shape=outs,
+        out_shape=(*outs, TOKEN),
         in_specs=[SCALARS] + [WHOLE] * 8 + [LEFT] * len(after),
-        out_specs=(WHOLE,) * len(outs),
+        out_specs=(WHOLE,) * (len(outs) + 1),
         scratch_shapes=[pltpu.VMEM((2, 4, rows, n), bf16)],
         cost_estimate=BRIEF,
         compiler_params=pltpu.CompilerParams(vmem_limit_bytes=24 << 20),
@@ -840,18 +842,26 @@
 
 
 def sum_first(sc, keep, got, after, parts=1):
-    def kernel(sc, keep_ref, *rest):
-        own_got, later_got = rest[:2] if len(got) == 2 else (rest[0].at[0], rest[0].at[1])
+    def kernel(sc, *refs):
+        rest = list(refs)
+
+        def both(arrays):
+            if len(arrays) == 2:
+                return rest.pop(0), rest.pop(0)
+            ref = rest.pop(0)
+            return ref.at[0], ref.at[1]
+
+        (own_kept, later_kept), (own_got, later_got) = both(keep), both(got)
         own_ref = rest[-1]
         for i, later_ref in enumerate(rest[-1 - parts : -1]):
             n = later_ref.shape[0]
             rows = slice(i * n, (i + 1) * n)
-            later_ref[...] = (keep_ref[1, rows].astype(f32) + later_got[rows].astype(f32)).astype(bf16)
-        own_ref[...] = keep_ref[0].astype(f32) + own_got[...].astype(f32)
-
-    rows, cols = keep.shape[1:]
+            later_ref[...] = (later_kept[rows].astype(f32) + later_got[rows].astype(f32)).astype(bf16)
+        own_ref[...] = own_kept[...].astype(f32) + own_got[...].astype(f32)
+
+    rows, cols = keep[0].shape[-2:]
     outs = [shape((rows // parts, cols), bf16)] * parts + [shape((rows, cols), f32)]
-    return small(kernel, sc, [keep, *got], outs, [], after, "sum_first")
+    return small(kernel, sc, [*keep, *got], outs, [], after, "sum_first")
 
 
 def sum_second(sc, own, got, after):
@@ -919,7 +929,7 @@
                 out_ref[at : at + n, :] = total[c, m]
 
     n, cols = mine[0].shape
-    return small(kernel, sc, [*mine, *other], [shape((8 * n, cols), f32)], [pltpu.VMEM((2, 4, n, cols), f32)], after, "lay_down")[0]
+    return small(kernel, sc, [*mine, *other], [shape((8 * n, cols), f32)], [pltpu.VMEM((2, 4, n, cols), f32)], after, "lay_down")
 
 
 def hold(value, after):
@@ -940,6 +950,17 @@
         rest[-1][...] = (far_ref[...] + jnp.where(sc[0] == 1, near_ref[...].astype(f32), 0.0)).astype(bf16)
 
     return small(kernel, sc, [far, near], [shape(far.shape, bf16)], [], after, "far_sum")
+
+
+def depart(sc, both, after):
+    def kernel(sc, both_ref, *rest):
+        out_ref, grad_ref = rest[-2:]
+        n = out_ref.shape[0]
+        out_ref[...] = both_ref[:n, :]
+        grad_ref[...] = both_ref[n:, :].astype(f32)
+
+    block = (both.shape[0] // 2, both.shape[1])
+    return small(kernel, sc, [both], [shape(block, bf16), shape(block, f32)], [], after, "depart")
 
 
 CORE, SIDE, BACK = 1, 2, 4
@@ -1076,16 +1097,18 @@
     (three0,) = across((three0,))
     tail = [g1, dq0, own, near, far, h_0, gain_a, cos, sin, output]
     dk0, dv0, one0, dgain_a0, leaving = back(False, True, sc, weights, tail, None, [done])
-    later_b, own_b, done = sum_first(sc, keep_b, [got_b], [dgain_a0])
+    later_b, own_b, done = sum_first(sc, [keep_b], [got_b], [dgain_a0])
     more_b = flip(later_b, BACK, SIDE)
     own = [dq1, dq0, dk1, dk0, dv1, dv0, p1, p0]
     got = [three1, three0, one1, flip(one0, CORE)]
-    *send_a, keep_a, done = grad_attention(sc, [a1, a0, across_1[0], across_0[0]], [mixed1, mixed0, across_1[2], across_0[2]], own, got, [dgain_a1, dgain_a0, dgain_f1, dgain_f0], [done])
+    args = [a1, a0, across_1[0], across_0[0]], [mixed1, mixed0, across_1[2], across_0[2]], own, got, [dgain_a1, dgain_a0, dgain_f1, dgain_f0]
+    *send_a, done = grad_attention(0, sc, *args, [done])
     got_a = [flip(v, SIDE, BACK) for v in send_a]
     send_d, keep_d, done = sum_third(sc, keep_d, got_d, [done])
     got_d = flip_z(send_d, 2)
     send_b, ring_b, done = sum_second(sc, own_b, [more_b], [done])
     got_b = flip_z(send_b, 1)
+    *keep_a, done = grad_attention(2, sc, *args, [done])
     *later_a, own_a, done = sum_first(sc, keep_a, got_a, [done], 2)
     more_a = [flip(v, BACK, SIDE) for v in later_a]
     send_b, ring_b, done = sum_third(sc, ring_b, got_b, [done])
@@ -1094,7 +1117,7 @@
     got_a = flip_z(send_a, 1)
     send_d, keep_d, done = down_split(sc, keep_d, got_d, [done])
     got_d = flip(send_d, SIDE, BACK)
-    later_d, own_d, done = sum_first(sc, keep_d, [got_d], [done])
+    later_d, own_d, done = sum_first(sc, [keep_d], [got_d], [done])
     more_d = flip(later_d, BACK, SIDE)
     piece_b, done = sum_two(sc, ring_b, got_b, [done])
     all_b = spread(over_groups(piece_b))
@@ -1104,11 +1127,12 @@
     all_d = spread(over_groups(piece_d))
     piece_a, done = sum_two(sc, ring_a, got_a, [done])
     all_a = spread(over_groups(piece_a))
-    grad_gate, grad_up = lay(sc, all_b, across(all_b), (gate_weight.shape[1],) * 2, [done])
-    grad_down_ = lay_down(sc, all_d, across(all_d), [done])
-    grad_query, grad_key, grad_value, grad_out, dgains = lay(sc, all_a, across(all_a), (width, KVW, KVW, width), [done])
+    grad_gate, grad_up, done = lay(sc, all_b, across(all_b), (gate_weight.shape[1],) * 2, [done])
     leaving = home_to_work(hold(leaving, [first]), back=True)
-    output, grad_tokens = leaving[:width].T, leaving[width:].astype(f32).T
+    output, grad_tokens, done = depart(sc, leaving, [done])
+    grad_down_, done = lay_down(sc, all_d, across(all_d), [done])
+    grad_query, grad_key, grad_value, grad_out, dgains, _ = lay(sc, all_a, across(all_a), (width, KVW, KVW, width), [done])
+    output, grad_tokens = output.T, grad_tokens.T
     return (output[None], grad_tokens[None], dgains[0], grad_query, grad_key, grad_value, grad_out, dgains[1], grad_gate, grad_up, grad_down_.T)
 
 

time: 459 us -> 462 us (level)
  waiting for transfers between devices: 132 us -> 122 us
  Pallas kernels: 193 us -> 202 us
  starting transfers between devices: 94.1 us -> 98.9 us
    ppermute x63, waiting for transfers between devices: 65.1 us -> 55.7 us  [flip(): lax.ppermute(value, 'dp', [(i, i ^ bits[i & 1]) for i in range(count)])]
    pallas_call x3 -> x4, Pallas kernels: 16.7 us -> 21.4 us  [the longest x2 15.8 us: grad_attention(): pl.pallas_call(functools.partial(grad_attention_kernel, first), out_shape...]
    pallas_call x15 -> x16, Pallas kernels: 14.8 us -> 18.5 us  [small(): pl.pallas_call(with_token, out_shape=(*outs, TOKEN), in_specs=[SCALARS] +...]
    unnamed x164 -> x170, local copies, waits for them, and re-layouts: 24.3 us -> 25.6 us
  transfers between devices with their start and end apart: 82 -> 82, of which waited for: 33 -> 33; matrix products, arithmetic and copies ran while one was open for 1% -> 1% of each run, Pallas kernels for 30% -> 31%
where the time goes in v17:
time: 462 us; the launch traced here: 455 us
  Pallas kernels  202 us (44%)
  waiting for transfers between devices  122 us (26%)
  starting transfers between devices  98.9 us (21%)
  local copies, waits for them, and re-layouts  28.2 us (6%)
    ppermute x63, waiting for transfers between devices, flip(): lax.ppermute(value, 'dp', [(i, i ^ bits[i & 1]) for i in range(count)])  55.7 us
    ppermute x63, starting transfers between devices, flip(): lax.ppermute(value, 'dp', [(i, i ^ bits[i & 1]) for i in range(count)])  51.1 us
    ppermute x12, waiting for transfers between devices, flip_z(): return lax.ppermute(value, ('dp', 'fsdp'), pairs)  45.8 us
    pallas_call x3, Pallas kernels, back(): pl.pallas_call(functools.partial(back_kernel, start, end, len(after)), ou...  45.6 us
    pallas_call x2, Pallas kernels, post(): pl.pallas_call(functools.partial(post_kernel, last, len(after)), out_shap...  34.6 us
    ppermute x12, starting transfers between devices, flip_z(): return lax.ppermute(value, ('dp', 'fsdp'), pairs)  30.1 us
    unnamed x170, local copies, waits for them, and re-layouts  25.6 us
    pallas_call x2, Pallas kernels, attend_back(): pl.pallas_call(attend_back_kernel, out_shape=(shape((3, n, PIECE), bf16),...  25.3 us
  transfers between devices with their start and end apart: 82, of which 33 were waited for; matrix products, arithmetic and copies ran while one was open for 1% of the time, Pallas kernels for 31%

profile of v17, /device:TPU:0, one launch (start us, length us, event | category | flops | bytes accessed | tf_op | source)
XLA Modules:
  0.0 455.5 jit_solution(10707264392004404772)
XLA Ops:
  3.3 2.7 pick_first.1.rest_0_
  6.0 4.1 collective-permute-start.1
  10.2 1.6 collective-permute-start
  11.7 7.3 %collective-permute-done.1.rest_2_ = bf16[240,384]{1,0:T(8,128)(2,1)S(1)} collective-permute-done((bf16[240,384]{1,0:T(8,128)(2,1)}, bf16[240,384]{1,0:T(8,128)(2,1)S(1)}, u32[]{:S(2)}, u32[]{:S(2)}) %collective-permute-start.1) | collective-permute-done | bytes 184352 | tf_op jit(solution)/shard_map/ppermute | solution.py:980
  24.7 1.5 stack.30.first_ref
  26.2 1.5 collective-permute-start.3
  29.3 3.2 collective-permute-start.11
  32.5 1.7 collective-permute-start.10
  34.3 11.5 %collective-permute-done.3.refs_1_.rest_1_ = bf16[960,384]{1,0:T(8,128)(2,1)} collective-permute-done((bf16[960,384]{1,0:T(8,128)(2,1)S(1)}, bf16[960,384]{1,0:T(8,128)(2,1)}, u32[]{:S(2)}, u32[]{:S(2)}) %collective-permute-start.3) | collective-permute-done | bytes 737312 | tf_op jit(solution)/shard_map/ppermute | solution.py:974
  45.8 6.8 %collective-permute-done.11.refs_0_ = bf16[368,640]{1,0:T(8,128)(2,1)S(1)} collective-permute-done((bf16[368,640]{1,0:T(8,128)(2,1)S(1)}, bf16[368,640]{1,0:T(8,128)(2,1)S(1)}, u32[]{:S(2)}, u32[]{:S(2)}) %collective-permute-start.11) | collective-permute-done | bytes 471072 | tf_op jit(solution)/shard_map/ppermute | solution.py:980
  54.4 10.0 %collective-permute-done.12.rest_3_ = bf16[368,640]{1,0:T(8,128)(2,1)S(1)} collective-permute-done((bf16[368,640]{1,0:T(8,128)(2,1)S(1)}, bf16[368,640]{1,0:T(8,128)(2,1)S(1)}, u32[]{:S(2)}, u32[]{:S(2)}) %collective-permute-start.12) | collective-permute-done | bytes 471072 | tf_op jit(solution)/shard_map/ppermute | solution.py:980
  64.4 3.0 stack.31.rest_8_
  69.2 4.6 %collective-permute-start.8 = (bf16[960,384]{1,0:T(8,128)(2,1)}, bf16[960,384]{1,0:T(8,128)(2,1)}, u32[]{:S(2)}, u32[]{:S(2)}) collective-permute-start(bf16[960,384]{1,0:T(8,128)(2,1)} %collective-permute-done.4.refs_2_.rest_2_), channel_id=1, source_target_pairs={{0,4},{4,0},{8,12},{12,8},{16,20},{20,16},{24,28},{28,24},{1,5},{5... | collective-permute-start | bytes 2211848 | tf_op jit(solution)/shard_map/ppermute | solution.py:974
  73.8 5.9 %collective-permute-start.7 = (bf16[960,384]{1,0:T(8,128)(2,1)}, bf16[960,384]{1,0:T(8,128)(2,1)}, u32[]{:S(2)}, u32[]{:S(2)}) collective-permute-start(bf16[960,384]{1,0:T(8,128)(2,1)} %collective-permute-done.3.refs_1_.rest_1_), channel_id=1, source_target_pairs={{0,4},{4,0},{8,12},{12,8},{16,20},{20,16},{24,28},{28,24},{1,5},{5... | collective-permute-start | bytes 2211848 | tf_op jit(solution)/shard_map/ppermute | solution.py:974
  83.3 7.5 %pre.1 = (bf16[256,960]{1,0:T(8,128)(2,1)}, bf16[256,960]{1,0:T(8,128)(2,1)}, bf16[960,256]{1,0:T(8,128)(2,1)}, bf16[656,256]{1,0:T(8,128)(2,1)}) custom-call(s32[3]{0:T(128)} %pad_add_fusion.sc.refs_0_, bf16[976,256]{1,0:T(8,128)(2,1)} %copy-done.76, f32[1,960]{1,0:T(1,128)} %get-tuple-element.263.gain_ref.gain_a.rest_22_.rest_14_, ...), custom_call_target="tpu_custom_call" | custom-call | flops 1024 | bytes 1024 | tf_op jit(solution)/shard_map/pre/pallas_call | solution.py:138
  90.8 9.3 %collective-permute-start.15 = (bf16[656,256]{1,0:T(8,128)(2,1)}, bf16[656,256]{1,0:T(8,128)(2,1)S(1)}, u32[]{:S(2)}, u32[]{:S(2)}) collective-permute-start(bf16[656,256]{1,0:T(8,128)(2,1)} %get-tuple-element.131.kv2.rest_16_), channel_id=1, source_target_pairs={{0,1},{2,3},{4,5},{6,7},{8,9},{10,11},{12,13},{14,15},{16,17},{18,... | collective-permute-start | bytes 1007624 | tf_op jit(solution)/shard_map/ppermute | solution.py:1013
  100.2 7.8 %collective-permute-done.15.refs_1_.kv0 = bf16[656,256]{1,0:T(8,128)(2,1)S(1)} collective-permute-done((bf16[656,256]{1,0:T(8,128)(2,1)}, bf16[656,256]{1,0:T(8,128)(2,1)S(1)}, u32[]{:S(2)}, u32[]{:S(2)}) %collective-permute-start.15) | collective-permute-done | bytes 335904 | tf_op jit(solution)/shard_map/ppermute | solution.py:1013
  110.9 10.1 %attend.2 = (bf16[960,256]{1,0:T(8,128)(2,1)S(1)}, f32[15,256]{1,0:T(8,128)S(1)}) custom-call(bf16[960,256]{1,0:T(8,128)(2,1)S(1)} %copy-done.22, bf16[656,256]{1,0:T(8,128)(2,1)S(1)} %collective-permute-done.15.refs_1_.kv0, bf16[656,256]{1,0:T(8,128)(2,1)S(1)} %collective-permute-done.18.kv1, bf16[656,256]{1,0:T(8,128)(2,1)S(1)} %copy-done.5), custom_call_target="tpu_custom_call" | custom-call | flops 1024 | bytes 1024 | tf_op jit(solution)/shard_map/attend/pallas_call | solution.py:191
  121.6 11.2 %collective-permute-done.17.refs_0_ = bf16[4,368,640]{2,1,0:T(8,128)(2,1)} collective-permute-done((bf16[4,368,640]{2,1,0:T(8,128)(2,1)}, bf16[4,368,640]{2,1,0:T(8,128)(2,1)}, u32[]{:S(2)}, u32[]{:S(2)}) %collective-permute-start.17) | collective-permute-done | bytes 1884192 | tf_op jit(solution)/shard_map/ppermute | solution.py:974
  134.2 2.8 collective-permute-done.22.rest_15_
  137.0 17.9 %post.2 = (bf16[256,960]{1,0:T(8,128)(2,1)}, f32[256,960]{1,0:T(8,128)}, bf16[256,960]{1,0:T(8,128)(2,1)}, bf16[256,2560]{1,0:T(8,128)(2,1)}, bf16[256,2560]{1,0...) custom-call(s32[3]{0:T(128)} %pad_add_fusion.sc.refs_0_, ...), custom_call_target="tpu_custom_call" | custom-call | flops 1024 | bytes 1024 | tf_op jit(solution)/shard_map/post/pallas_call | solution.py:358
  155.2 3.7 collective-permute-start.24
  159.7 5.9 %collective-permute-start.27 = (bf16[256,960]{1,0:T(8,128)(2,1)}, bf16[256,960]{1,0:T(8,128)(2,1)S(1)}, u32[]{:S(2)}, u32[]{:S(2)}) collective-permute-start(bf16[256,960]{1,0:T(8,128)(2,1)} %get-tuple-element.138.rest_1_), channel_id=1, source_target_pairs={{0,4},{4,0},{8,12},{12,8},{16,20},{20,16},{24,28},{28,24},{1,5},{5... | collective-permute-start | bytes 1474568 | tf_op jit(solution)/shard_map/ppermute | solution.py:974
  165.6 1.7 collective-permute-done.24.kv0
  171.3 10.5 %attend.3 = (bf16[960,256]{1,0:T(8,128)(2,1)S(1)}, f32[15,256]{1,0:T(8,128)S(1)}) custom-call(bf16[960,256]{1,0:T(8,128)(2,1)S(1)} %copy-done.23, bf16[656,256]{1,0:T(8,128)(2,1)S(1)} %collective-permute-done.24.kv0, bf16[656,256]{1,0:T(8,128)(2,1)S(1)} %collective-permute-done.25.kv1, bf16[656,256]{1,0:T(8,128)(2,1)S(1)} %copy-done.3, ...), custom_call_target="tpu_custom_call" | custom-call | flops 1024 | bytes 1024 | tf_op jit(solution)/shard_map/attend/pallas_call | solution.py:191
  183.5 16.7 %post.3 = (bf16[256,960]{1,0:T(8,128)(2,1)}, f32[256,960]{1,0:T(8,128)}, bf16[256,960]{1,0:T(8,128)(2,1)}, bf16[256,2560]{1,0:T(8,128)(2,1)}, bf16[256,2560]{1,0...) custom-call(s32[3]{0:T(128)} %pad_add_fusion.sc.refs_0_, bf16[960,256]{1,0:T(8,128)(2,1)} %copy-done.48, ...), custom_call_target="tpu_custom_call" | custom-call | flops 1024 | bytes 1024 | tf_op jit(solution)/shard_map/post/pallas_call | solution.py:358
  200.2 18.3 %back_start.1 = (bf16[256,960]{1,0:T(8,128)(2,1)}, bf16[256,2560]{1,0:T(8,128)(2,1)}, bf16[256,2560]{1,0:T(8,128)(2,1)}, f32[256,960]{1,0:T(8,128)}, bf16[3,256,...) custom-call(s32[3]{0:T(128)} %pad_add_fusion.sc.refs_0_, bf16[960,384]{1,0:T(8,128)(2,1)} %bitcast.28, ...), custom_call_target="tpu_custom_call" | custom-call | flops 1024 | bytes 1024 | tf_op jit(solution)/shard_map/back_start/pallas_call | solution.py:539
  221.3 12.6 %attend_back.2 = (bf16[3,256,384]{2,1,0:T(8,128)(2,1)S(1)}, bf16[3,256,384]{2,1,0:T(8,128)(2,1)S(1)}, f32[640,256]{1,0:T(8,128)S(1)}, bf16[640,256]{1,0:T(8,128)(2,1)S(1)}, f32[640,256]{1,0:T(8,128)S(1)}) custom-call(s32[3]{0:T(128)S(1)} %copy-done.41, bf16[3,256,384]{2,1,0:T(8,128)(2,1)S(1)} %copy-done.8, bf16[960,256]{1,0:T(8,128)(2,1)S(1)} %copy-done.23, ...), custom_call_target="tpu_custom_call" | custom-call | flops 1024 | bytes 1024 | tf_op jit(solution)/shard_map/attend_back/pallas_call | solution.py:244
  239.6 10.6 %collective-permute-done.31.rest_20_ = bf16[640,256]{1,0:T(8,128)(2,1)S(1)} collective-permute-done((bf16[640,256]{1,0:T(8,128)(2,1)S(1)}, bf16[640,256]{1,0:T(8,128)(2,1)S(1)}, u32[]{:S(2)}, u32[]{:S(2)}) %collective-permute-start.31) | collective-permute-done | bytes 327712 | tf_op jit(solution)/shard_map/ppermute | solution.py:1022
  250.8 20.4 %back_join.1 = (bf16[256,384]{1,0:T(8,128)(2,1)}, bf16[256,384]{1,0:T(8,128)(2,1)}, bf16[256,384]{1,0:T(8,128)(2,1)}, f32[1,960]{1,0:T(1,128)}, bf16[256,960]{1,...) custom-call(s32[3]{0:T(128)} %pad_add_fusion.sc.refs_0_, ...), custom_call_target="tpu_custom_call" | custom-call | flops 1024 | bytes 1024 | tf_op jit(solution)/shard_map/back_join/pallas_call | solution.py:539
  271.3 3.2 collective-permute-done.40.rest_7_
  275.7 11.5 %grad_ffn.1 = (bf16[2,960,640]{2,1,0:T(8,128)(2,1)}, bf16[2,960,640]{2,1,0:T(8,128)(2,1)}, f32[8,128]{1,0:T(8,128)}) custom-call(s32[3]{0:T(128)} %pad_add_fusion.sc.refs_0_, bf16[256,960]{1,0:T(8,128)(2,1)} %get-tuple-element.162.rest_0_, bf16[256,960]{1,0:T(8,128)(2,1)} %get-tuple-element.138.rest_1_, bf16[256,960]{1,0:T(8,128)(2,1)} %copy-done.66, ...), custom_call_target="tpu_custom_call" | custom-call | flops 1024 | bytes 1024 | tf_op jit(solution)/shard_map/grad_ffn/pallas_call | solution.py:581
  289.7 12.6 %attend_back.3 = (bf16[3,256,384]{2,1,0:T(8,128)(2,1)S(1)}, bf16[3,256,384]{2,1,0:T(8,128)(2,1)S(1)}, f32[640,256]{1,0:T(8,128)S(1)}, bf16[640,256]{1,0:T(8,128)(2,1)S(1)}, f32[640,256]{1,0:T(8,128)S(1)}) custom-call(s32[3]{0:T(128)S(1)} %copy-done.42, bf16[3,256,384]{2,1,0:T(8,128)(2,1)S(1)} %copy-done.9, bf16[960,256]{1,0:T(8,128)(2,1)S(1)} %copy-done.22, ...), custom_call_target="tpu_custom_call" | custom-call | flops 1024 | bytes 1024 | tf_op jit(solution)/shard_map/attend_back/pallas_call | solution.py:244
  309.0 8.2 %grad_down.1 = (bf16[2,480,640]{2,1,0:T(8,128)(2,1)}, bf16[2,480,640]{2,1,0:T(8,128)(2,1)}, f32[8,128]{1,0:T(8,128)}) custom-call(s32[3]{0:T(128)} %pad_add_fusion.sc.refs_0_, bf16[256,960]{1,0:T(8,128)(2,1)} %get-tuple-element.159.rest_0_, bf16[256,960]{1,0:T(8,128)(2,1)} %get-tuple-element.180.rest_1_, bf16[256,960]{1,0:T(8,128)(2,1)} %copy-done.65, ...), custom_call_target="tpu_custom_call" | custom-call | flops 1024 | bytes 1024 | tf_op jit(solution)/shard_map/grad_down/pallas_call | solution.py:613
  317.2 2.7 collective-permute-start.48
  320.6 7.0 %back_end.1 = (bf16[256,384]{1,0:T(8,128)(2,1)}, bf16[256,384]{1,0:T(8,128)(2,1)}, bf16[256,384]{1,0:T(8,128)(2,1)}, f32[1,960]{1,0:T(1,128)}, bf16[1920,256]{1,0:T(8,128)(2,1)}) custom-call(s32[3]{0:T(128)} %pad_add_fusion.sc.refs_0_, bf16[960,384]{1,0:T(8,128)(2,1)} %bitcast.30, bf16[960,384]{1,0:T(8,128)(2,1)} %collective-permute-done.3.refs_1_.rest_1_, ...), custom_call_target="tpu_custom_call" | custom-call | flops 1024 | bytes 1024 | tf_op jit(solution)/shard_map/back_end/pallas_call | solution.py:539
  328.3 2.0 sum_first.3
  331.7 1.7 collective-permute-start.47
  336.4 8.1 %grad_attention.2 = (bf16[960,384]{1,0:T(8,128)(2,1)}, bf16[960,384]{1,0:T(8,128)(2,1)}, f32[8,128]{1,0:T(8,128)}) custom-call(s32[3]{0:T(128)} %pad_add_fusion.sc.refs_0_, bf16[256,960]{1,0:T(8,128)(2,1)} %get-tuple-element.161.rest_0_, bf16[256,960]{1,0:T(8,128)(2,1)} %get-tuple-element.137.rest_1_, bf16[256,960]{1,0:T(8,128)(2,1)} %copy-done.62, ...), custom_call_target="tpu_custom_call" | custom-call | flops 1024 | bytes 1024 | tf_op jit(solution)/shard_map/grad_attention/pallas_call | solution.py:664
  344.9 1.6 collective-permute-start.50
  347.9 2.3 sum_third.3
  350.2 1.8 sum_second.2
  352.6 1.7 collective-permute-start.53
  354.4 4.5 collective-permute-start.56
  358.9 7.8 %grad_attention.3 = (bf16[960,384]{1,0:T(8,128)(2,1)}, bf16[960,384]{1,0:T(8,128)(2,1)}, f32[8,128]{1,0:T(8,128)}) custom-call(s32[3]{0:T(128)} %pad_add_fusion.sc.refs_0_, bf16[256,960]{1,0:T(8,128)(2,1)} %get-tuple-element.161.rest_0_, bf16[256,960]{1,0:T(8,128)(2,1)} %get-tuple-element.137.rest_1_, bf16[256,960]{1,0:T(8,128)(2,1)} %copy-done.62, ...), custom_call_target="tpu_custom_call" | custom-call | flops 1024 | bytes 1024 | tf_op jit(solution)/shard_map/grad_attention/pallas_call | solution.py:664
  372.6 8.8 %collective-permute-done.53.refs_2_ = bf16[2,240,640]{2,1,0:T(8,128)(2,1)} collective-permute-done((bf16[2,240,640]{2,1,0:T(8,128)(2,1)}, bf16[2,240,640]{2,1,0:T(8,128)(2,1)}, u32[]{:S(2)}, u32[]{:S(2)}) %collective-permute-start.53) | collective-permute-done | bytes 614432 | tf_op jit(solution)/shard_map/ppermute | solution.py:980
  384.1 1.6 collective-permute-start.57
  385.7 2.4 collective-permute-start.54
  388.1 2.7 collective-permute-start.55
  391.7 1.5 collective-permute-start.67
  393.2 7.3 %collective-permute-done.55.refs_2_ = bf16[240,640]{1,0:T(8,128)(2,1)S(1)} collective-permute-done((bf16[240,640]{1,0:T(8,128)(2,1)S(1)}, bf16[240,640]{1,0:T(8,128)(2,1)S(1)}, u32[]{:S(2)}, u32[]{:S(2)}) %collective-permute-start.55) | collective-permute-done | bytes 307232 | tf_op jit(solution)/shard_map/ppermute | solution.py:980
  401.9 3.3 collective-permute-start.66
  407.3 1.7 collective-permute-start.60
  409.0 2.9 collective-permute-done.66.refs_2_
  411.8 2.3 collective-permute-start.59
  417.2 7.4 %collective-permute-done.60.rest_2_ = bf16[240,640]{1,0:T(8,128)(2,1)S(1)} collective-permute-done((bf16[240,640]{1,0:T(8,128)(2,1)S(1)}, bf16[240,640]{1,0:T(8,128)(2,1)S(1)}, u32[]{:S(2)}, u32[]{:S(2)}) %collective-permute-start.60) | collective-permute-done | bytes 307232 | tf_op jit(solution)/shard_map/ppermute | solution.py:974
  425.8 2.5 collective-permute-start.70
  429.3 4.6 %collective-permute-done.76.refs_3_ = bf16[120,640]{1,0:T(8,128)(2,1)S(1)} collective-permute-done((bf16[120,640]{1,0:T(8,128)(2,1)S(1)}, bf16[120,640]{1,0:T(8,128)(2,1)S(1)}, u32[]{:S(2)}, u32[]{:S(2)}) %collective-permute-start.76) | collective-permute-done | bytes 153632 | tf_op jit(solution)/shard_map/ppermute | solution.py:974
  433.9 1.7 collective-permute-start.75
  435.7 3.5 collective-permute-done.75.refs_2_
  443.4 3.1 lay.2
  446.5 1.7 depart.1
  448.3 2.3 lay_down.1
  450.6 2.4 lay.3
  (325 shorter events, 80.6 us)
Async XLA Ops:
  6.0 13.0 %collective-permute-start.1 = (bf16[240,384]{1,0:T(8,128)(2,1)}, bf16[240,384]{1,0:T(8,128)(2,1)S(1)}, u32[]{:S(2)}, u32[]{:S(2)}) collective-permute-start(bf16[240,384]{1,0:T(8,128)(2,1)} %pick_first.1.rest_0_), channel_id=1, source_target_pairs={{0,2},{1,3},{2,0},{3,1},{4,6},{5,7},{6,4},{7,5},{8,10},{9,11},{10,... | collective-permute-start | bytes 552968 | tf_op jit(solution)/shard_map/ppermute | solution.py:980
  10.2 9.6 %collective-permute-start = (bf16[240,384]{1,0:T(8,128)(2,1)}, bf16[240,384]{1,0:T(8,128)(2,1)S(1)}, u32[]{:S(2)}, u32[]{:S(2)}) collective-permute-start(bf16[240,384]{1,0:T(8,128)(2,1)} %pick_first.1.rest_0_), channel_id=1, source_target_pairs={{0,1},{1,0},{2,3},{3,2},{4,5},{5,4},{6,7},{7,6},{8,9},{9,8},{10,11... | collective-permute-start | bytes 552968 | tf_op jit(solution)/shard_map/ppermute | solution.py:980
  19.0 5.7 %collective-permute-start.2 = (bf16[240,384]{1,0:T(8,128)(2,1)S(1)}, bf16[240,384]{1,0:T(8,128)(2,1)S(1)}, u32[]{:S(2)}, u32[]{:S(2)}) collective-permute-start(bf16[240,384]{1,0:T(8,128)(2,1)S(1)} %collective-permute-done.1.rest_2_), channel_id=1, source_target_pairs={{0,1},{1,0},{2,3},{3,2},{4,5},{5,4},{6,7},{7,6},{8,9},{9,8},{10,11... | collective-permute-start | bytes 552968 | tf_op jit(solution)/shard_map/ppermute | solution.py:980
  26.2 19.6 %collective-permute-start.3 = (bf16[960,384]{1,0:T(8,128)(2,1)S(1)}, bf16[960,384]{1,0:T(8,128)(2,1)}, u32[]{:S(2)}, u32[]{:S(2)}) collective-permute-start(bf16[960,384]{1,0:T(8,128)(2,1)S(1)} %bitcast.22), channel_id=1, source_target_pairs={{0,8},{4,20},{8,0},{12,28},{16,24},{20,4},{24,16},{28,12},{1,9},{5... | collective-permute-start | bytes 2211848 | tf_op jit(solution)/shard_map/ppermute | solution.py:974
  27.8 25.2 %collective-permute-start.4 = (bf16[960,384]{1,0:T(8,128)(2,1)S(1)}, bf16[960,384]{1,0:T(8,128)(2,1)}, u32[]{:S(2)}, u32[]{:S(2)}) collective-permute-start(bf16[960,384]{1,0:T(8,128)(2,1)S(1)} %bitcast.23), channel_id=1, source_target_pairs={{0,16},{4,12},{8,24},{12,4},{16,0},{20,28},{24,8},{28,20},{1,17},{... | collective-permute-start | bytes 2211848 | tf_op jit(solution)/shard_map/ppermute | solution.py:974
  29.3 23.3 %collective-permute-start.11 = (bf16[368,640]{1,0:T(8,128)(2,1)S(1)}, bf16[368,640]{1,0:T(8,128)(2,1)S(1)}, u32[]{:S(2)}, u32[]{:S(2)}) collective-permute-start(bf16[368,640]{1,0:T(8,128)(2,1)S(1)} %pick.1.rest_4_.rest_0_), channel_id=1, source_target_pairs={{0,2},{1,3},{2,0},{3,1},{4,6},{5,7},{6,4},{7,5},{8,10},{9,11},{10,... | collective-permute-start | bytes 1413128 | tf_op jit(solution)/shard_map/ppermute | solution.py:980
  32.5 20.5 %collective-permute-start.10 = (bf16[368,640]{1,0:T(8,128)(2,1)S(1)}, bf16[368,640]{1,0:T(8,128)(2,1)S(1)}, u32[]{:S(2)}, u32[]{:S(2)}) collective-permute-start(bf16[368,640]{1,0:T(8,128)(2,1)S(1)} %pick.1.rest_4_.rest_0_), channel_id=1, source_target_pairs={{0,1},{1,0},{2,3},{3,2},{4,5},{5,4},{6,7},{7,6},{8,9},{9,8},{10,11... | collective-permute-start | bytes 1413128 | tf_op jit(solution)/shard_map/ppermute | solution.py:980
  45.8 18.6 %collective-permute-start.5 = (bf16[960,384]{1,0:T(8,128)(2,1)}, bf16[960,384]{1,0:T(8,128)(2,1)S(1)}, u32[]{:S(2)}, u32[]{:S(2)}) collective-permute-start(bf16[960,384]{1,0:T(8,128)(2,1)} %collective-permute-done.3.refs_1_.rest_1_), channel_id=1, source_target_pairs={{0,16},{4,12},{8,24},{12,4},{16,0},{20,28},{24,8},{28,20},{1,17},{... | collective-permute-start | bytes 2211848 | tf_op jit(solution)/shard_map/ppermute | solution.py:974
  53.0 11.4 %collective-permute-start.12 = (bf16[368,640]{1,0:T(8,128)(2,1)S(1)}, bf16[368,640]{1,0:T(8,128)(2,1)S(1)}, u32[]{:S(2)}, u32[]{:S(2)}) collective-permute-start(bf16[368,640]{1,0:T(8,128)(2,1)S(1)} %hold.4.rest_2_), channel_id=1, source_target_pairs={{0,1},{1,0},{2,3},{3,2},{4,5},{5,4},{6,7},{7,6},{8,9},{9,8},{10,11... | collective-permute-start | bytes 1413128 | tf_op jit(solution)/shard_map/ppermute | solution.py:980
  67.4 41.3 %collective-permute-start.16 = (bf16[4,368,640]{2,1,0:T(8,128)(2,1)}, bf16[4,368,640]{2,1,0:T(8,128)(2,1)S(1)}, u32[]{:S(2)}, u32[]{:S(2)}) collective-permute-start(bf16[4,368,640]{2,1,0:T(8,128)(2,1)} %stack.31.rest_8_), channel_id=1, source_target_pairs={{0,16},{4,12},{8,24},{12,4},{16,0},{20,28},{24,8},{28,20},{1,17},{... | collective-permute-start | bytes 5652488 | tf_op jit(solution)/shard_map/ppermute | solution.py:974
  68.0 40.7 %collective-permute-start.13 = (bf16[4,368,640]{2,1,0:T(8,128)(2,1)}, bf16[4,368,640]{2,1,0:T(8,128)(2,1)}, u32[]{:S(2)}, u32[]{:S(2)}) collective-permute-start(bf16[4,368,640]{2,1,0:T(8,128)(2,1)} %stack.31.rest_8_), channel_id=1, source_target_pairs={{0,8},{4,20},{8,0},{12,28},{16,24},{20,4},{24,16},{28,12},{1,9},{5... | collective-permute-start | bytes 5652488 | tf_op jit(solution)/shard_map/ppermute | solution.py:974
  68.4 11.2 %collective-permute-start.6 = (bf16[960,384]{1,0:T(8,128)(2,1)S(1)}, bf16[960,384]{1,0:T(8,128)(2,1)S(1)}, u32[]{:S(2)}, u32[]{:S(2)}) collective-permute-start(bf16[960,384]{1,0:T(8,128)(2,1)S(1)} %bitcast.24), channel_id=1, source_target_pairs={{0,4},{4,0},{8,12},{12,8},{16,20},{20,16},{24,28},{28,24},{1,5},{5... | collective-permute-start | bytes 2211848 | tf_op jit(solution)/shard_map/ppermute | solution.py:974
  68.5 5.3 %collective-permute-start.14 = (bf16[976,256]{1,0:T(8,128)(2,1)S(1)}, bf16[976,256]{1,0:T(8,128)(2,1)S(1)}, u32[]{:S(2)}, u32[]{:S(2)}) collective-permute-start(bf16[976,256]{1,0:T(8,128)(2,1)S(1)} %pad_maximum_fusion), channel_id=1, source_target_pairs={{0,0},{1,4},{2,1},{3,5},{4,2},{5,6},{6,3},{7,7},{8,8},{9,12},{10,9... | collective-permute-start | bytes 1499144 | tf_op jit(solution)/shard_map/ppermute | solution.py:991
  69.2 14.1 %collective-permute-start.8 = (bf16[960,384]{1,0:T(8,128)(2,1)}, bf16[960,384]{1,0:T(8,128)(2,1)}, u32[]{:S(2)}, u32[]{:S(2)}) collective-permute-start(bf16[960,384]{1,0:T(8,128)(2,1)} %collective-permute-done.4.refs_2_.rest_2_), channel_id=1, source_target_pairs={{0,4},{4,0},{8,12},{12,8},{16,20},{20,16},{24,28},{28,24},{1,5},{5... | collective-permute-start | bytes 2211848 | tf_op jit(solution)/shard_map/ppermute | solution.py:974
  73.8 9.5 %collective-permute-start.7 = (bf16[960,384]{1,0:T(8,128)(2,1)}, bf16[960,384]{1,0:T(8,128)(2,1)}, u32[]{:S(2)}, u32[]{:S(2)}) collective-permute-start(bf16[960,384]{1,0:T(8,128)(2,1)} %collective-permute-done.3.refs_1_.rest_1_), channel_id=1, source_target_pairs={{0,4},{4,0},{8,12},{12,8},{16,20},{20,16},{24,28},{28,24},{1,5},{5... | collective-permute-start | bytes 2211848 | tf_op jit(solution)/shard_map/ppermute | solution.py:974
  90.8 17.1 %collective-permute-start.15 = (bf16[656,256]{1,0:T(8,128)(2,1)}, bf16[656,256]{1,0:T(8,128)(2,1)S(1)}, u32[]{:S(2)}, u32[]{:S(2)}) collective-permute-start(bf16[656,256]{1,0:T(8,128)(2,1)} %get-tuple-element.131.kv2.rest_16_), channel_id=1, source_target_pairs={{0,1},{2,3},{4,5},{6,7},{8,9},{10,11},{12,13},{14,15},{16,17},{18,... | collective-permute-start | bytes 1007624 | tf_op jit(solution)/shard_map/ppermute | solution.py:1013
  108.7 24.1 %collective-permute-start.17 = (bf16[4,368,640]{2,1,0:T(8,128)(2,1)}, bf16[4,368,640]{2,1,0:T(8,128)(2,1)}, u32[]{:S(2)}, u32[]{:S(2)}) collective-permute-start(bf16[4,368,640]{2,1,0:T(8,128)(2,1)} %hold.5.rest_9_), channel_id=1, source_target_pairs={{0,16},{4,12},{8,24},{12,4},{16,0},{20,28},{24,8},{28,20},{1,17},{... | collective-permute-start | bytes 5652488 | tf_op jit(solution)/shard_map/ppermute | solution.py:974
  109.3 23.6 %collective-permute-start.19 = (bf16[4,368,640]{2,1,0:T(8,128)(2,1)}, bf16[4,368,640]{2,1,0:T(8,128)(2,1)S(1)}, u32[]{:S(2)}, u32[]{:S(2)}) collective-permute-start(bf16[4,368,640]{2,1,0:T(8,128)(2,1)} %stack.31.rest_8_), channel_id=1, source_target_pairs={{0,4},{4,0},{8,12},{12,8},{16,20},{20,16},{24,28},{28,24},{1,5},{5... | collective-permute-start | bytes 5652488 | tf_op jit(solution)/shard_map/ppermute | solution.py:974
  121.0 13.2 %collective-permute-start.20 = (bf16[4,368,640]{2,1,0:T(8,128)(2,1)}, bf16[4,368,640]{2,1,0:T(8,128)(2,1)}, u32[]{:S(2)}, u32[]{:S(2)}) collective-permute-start(bf16[4,368,640]{2,1,0:T(8,128)(2,1)} %hold.5.rest_9_), channel_id=1, source_target_pairs={{0,4},{4,0},{8,12},{12,8},{16,20},{20,16},{24,28},{28,24},{1,5},{5... | collective-permute-start | bytes 5652488 | tf_op jit(solution)/shard_map/ppermute | solution.py:974
  121.3 11.6 %collective-permute-start.21 = (bf16[4,368,640]{2,1,0:T(8,128)(2,1)S(1)}, bf16[4,368,640]{2,1,0:T(8,128)(2,1)S(1)}, u32[]{:S(2)}, u32[]{:S(2)}) collective-permute-start(bf16[4,368,640]{2,1,0:T(8,128)(2,1)S(1)} %collective-permute-done.16.refs_2_.rest_10_), channel_id=1, source_target_pairs={{0,4},{4,0},{8,12},{12,8},{16,20},{20,16},{24,28},{28,24},{1,5},{5... | collective-permute-start | bytes 5652488 | tf_op jit(solution)/shard_map/ppermute | solution.py:974
  132.8 4.2 collective-permute-start.22
  154.9 15.2 %collective-permute-start.29 = (bf16[256,2560]{1,0:T(8,128)(2,1)}, bf16[256,2560]{1,0:T(8,128)(2,1)S(1)}, u32[]{:S(2)}, u32[]{:S(2)}) collective-permute-start(bf16[256,2560]{1,0:T(8,128)(2,1)} %get-tuple-element.140.rest_5_), channel_id=1, source_target_pairs={{0,4},{4,0},{8,12},{12,8},{16,20},{20,16},{24,28},{28,24},{1,5},{5... | collective-permute-start | bytes 3932168 | tf_op jit(solution)/shard_map/ppermute | solution.py:974
  155.2 12.2 %collective-permute-start.24 = (bf16[656,256]{1,0:T(8,128)(2,1)}, bf16[656,256]{1,0:T(8,128)(2,1)S(1)}, u32[]{:S(2)}, u32[]{:S(2)}) collective-permute-start(bf16[656,256]{1,0:T(8,128)(2,1)} %get-tuple-element.136.kv2.rest_16_), channel_id=1, source_target_pairs={{0,1},{2,3},{4,5},{6,7},{8,9},{10,11},{12,13},{14,15},{16,17},{18,... | collective-permute-start | bytes 1007624 | tf_op jit(solution)/shard_map/ppermute | solution.py:1013
  158.9 9.5 %collective-permute-start.26 = (bf16[256,960]{1,0:T(8,128)(2,1)S(1)}, bf16[256,960]{1,0:T(8,128)(2,1)S(1)}, u32[]{:S(2)}, u32[]{:S(2)}) collective-permute-start(bf16[256,960]{1,0:T(8,128)(2,1)S(1)} %copy-done.67), channel_id=1, source_target_pairs={{0,4},{4,0},{8,12},{12,8},{16,20},{20,16},{24,28},{28,24},{1,5},{5... | collective-permute-start | bytes 1474568 | tf_op jit(solution)/shard_map/ppermute | solution.py:974
  159.0 23.7 %collective-permute-start.23 = (bf16[960,256]{1,0:T(8,128)(2,1)S(1)}, bf16[960,256]{1,0:T(8,128)(2,1)S(1)}, u32[]{:S(2)}, u32[]{:S(2)}) collective-permute-start(bf16[960,256]{1,0:T(8,128)(2,1)S(1)} %bitcast.39), channel_id=1, source_target_pairs={{0,0},{1,4},{2,1},{3,5},{4,2},{5,6},{6,3},{7,7},{8,8},{9,12},{10,9... | collective-permute-start | bytes 1474568 | tf_op jit(solution)/shard_map/ppermute | solution.py:991
  159.7 8.8 %collective-permute-start.27 = (bf16[256,960]{1,0:T(8,128)(2,1)}, bf16[256,960]{1,0:T(8,128)(2,1)S(1)}, u32[]{:S(2)}, u32[]{:S(2)}) collective-permute-start(bf16[256,960]{1,0:T(8,128)(2,1)} %get-tuple-element.138.rest_1_), channel_id=1, source_target_pairs={{0,4},{4,0},{8,12},{12,8},{16,20},{20,16},{24,28},{28,24},{1,5},{5... | collective-permute-start | bytes 1474568 | tf_op jit(solution)/shard_map/ppermute | solution.py:974
  168.5 66.7 %collective-permute-start.35 = (bf16[256,960]{1,0:T(8,128)(2,1)}, bf16[256,960]{1,0:T(8,128)(2,1)S(1)}, u32[]{:S(2)}, u32[]{:S(2)}) collective-permute-start(bf16[256,960]{1,0:T(8,128)(2,1)} %get-tuple-element.161.rest_0_), channel_id=1, source_target_pairs={{0,4},{4,0},{8,12},{12,8},{16,20},{20,16},{24,28},{28,24},{1,5},{5... | collective-permute-start | bytes 1474568 | tf_op jit(solution)/shard_map/ppermute | solution.py:974
  218.6 31.6 %collective-permute-start.34 = (bf16[256,2560]{1,0:T(8,128)(2,1)}, bf16[256,2560]{1,0:T(8,128)(2,1)}, u32[]{:S(2)}, u32[]{:S(2)}) collective-permute-start(bf16[256,2560]{1,0:T(8,128)(2,1)} %get-tuple-element.160), channel_id=1, source_target_pairs={{0,4},{4,0},{8,12},{12,8},{16,20},{20,16},{24,28},{28,24},{1,5},{5... | collective-permute-start | bytes 3932168 | tf_op jit(solution)/shard_map/ppermute | solution.py:974
  218.6 31.5 %collective-permute-start.38 = (bf16[256,2560]{1,0:T(8,128)(2,1)}, bf16[256,2560]{1,0:T(8,128)(2,1)}, u32[]{:S(2)}, u32[]{:S(2)}) collective-permute-start(bf16[256,2560]{1,0:T(8,128)(2,1)} %get-tuple-element.164.rest_4_), channel_id=1, source_target_pairs={{0,4},{4,0},{8,12},{12,8},{16,20},{20,16},{24,28},{28,24},{1,5},{5... | collective-permute-start | bytes 3932168 | tf_op jit(solution)/shard_map/ppermute | solution.py:974
  219.1 17.7 %collective-permute-start.36 = (bf16[256,960]{1,0:T(8,128)(2,1)S(1)}, bf16[256,960]{1,0:T(8,128)(2,1)S(1)}, u32[]{:S(2)}, u32[]{:S(2)}) collective-permute-start(bf16[256,960]{1,0:T(8,128)(2,1)S(1)} %copy-done.75), channel_id=1, source_target_pairs={{0,4},{4,0},{8,12},{12,8},{16,20},{20,16},{24,28},{28,24},{1,5},{5... | collective-permute-start | bytes 1474568 | tf_op jit(solution)/shard_map/ppermute | solution.py:974
  238.2 11.9 %collective-permute-start.31 = (bf16[640,256]{1,0:T(8,128)(2,1)S(1)}, bf16[640,256]{1,0:T(8,128)(2,1)S(1)}, u32[]{:S(2)}, u32[]{:S(2)}) collective-permute-start(bf16[640,256]{1,0:T(8,128)(2,1)S(1)} %get-tuple-element.154), channel_id=1, source_target_pairs={{1,0},{3,2},{5,4},{7,6},{9,8},{11,10},{13,12},{15,14},{17,16},{19,... | collective-permute-start | bytes 983048 | tf_op jit(solution)/shard_map/ppermute | solution.py:1022
  287.2 40.4 %collective-permute-start.46 = (bf16[2,960,640]{2,1,0:T(8,128)(2,1)}, bf16[2,960,640]{2,1,0:T(8,128)(2,1)S(1)}, u32[]{:S(2)}, u32[]{:S(2)}) collective-permute-start(bf16[2,960,640]{2,1,0:T(8,128)(2,1)} %get-tuple-element.195), channel_id=1, source_target_pairs={{0,8},{4,20},{8,0},{12,28},{16,24},{20,4},{24,16},{28,12},{1,9},{5... | collective-permute-start | bytes 7372808 | tf_op jit(solution)/shard_map/ppermute | solution.py:974
  304.2 4.0 collective-permute-start.43
  306.9 12.9 %collective-permute-start.42 = (bf16[640,256]{1,0:T(8,128)(2,1)S(1)}, bf16[640,256]{1,0:T(8,128)(2,1)S(1)}, u32[]{:S(2)}, u32[]{:S(2)}) collective-permute-start(bf16[640,256]{1,0:T(8,128)(2,1)S(1)} %get-tuple-element.178), channel_id=1, source_target_pairs={{1,0},{3,2},{5,4},{7,6},{9,8},{11,10},{13,12},{15,14},{17,16},{19,... | collective-permute-start | bytes 983048 | tf_op jit(solution)/shard_map/ppermute | solution.py:1022
  317.2 30.0 %collective-permute-start.48 = (bf16[2,480,640]{2,1,0:T(8,128)(2,1)}, bf16[2,480,640]{2,1,0:T(8,128)(2,1)}, u32[]{:S(2)}, u32[]{:S(2)}) collective-permute-start(bf16[2,480,640]{2,1,0:T(8,128)(2,1)} %get-tuple-element.199), channel_id=1, source_target_pairs={{0,1},{1,0},{2,3},{3,2},{4,5},{5,4},{6,7},{7,6},{8,9},{9,8},{10,11... | collective-permute-start | bytes 3686408 | tf_op jit(solution)/shard_map/ppermute | solution.py:980
  331.7 18.5 %collective-permute-start.47 = (bf16[960,640]{1,0:T(8,128)(2,1)}, bf16[960,640]{1,0:T(8,128)(2,1)S(1)}, u32[]{:S(2)}, u32[]{:S(2)}) collective-permute-start(bf16[960,640]{1,0:T(8,128)(2,1)} %get-tuple-element.197), channel_id=1, source_target_pairs={{0,16},{4,12},{8,24},{12,4},{16,0},{20,28},{24,8},{28,20},{1,17},{... | collective-permute-start | bytes 3686408 | tf_op jit(solution)/shard_map/ppermute | solution.py:974
  344.4 22.3 %collective-permute-start.49 = (bf16[960,384]{1,0:T(8,128)(2,1)}, bf16[960,384]{1,0:T(8,128)(2,1)S(1)}, u32[]{:S(2)}, u32[]{:S(2)}) collective-permute-start(bf16[960,384]{1,0:T(8,128)(2,1)} %get-tuple-element.206), channel_id=1, source_target_pairs={{0,8},{4,20},{8,0},{12,28},{16,24},{20,4},{24,16},{28,12},{1,9},{5... | collective-permute-start | bytes 2211848 | tf_op jit(solution)/shard_map/ppermute | solution.py:974
  344.9 21.8 %collective-permute-start.50 = (bf16[960,384]{1,0:T(8,128)(2,1)}, bf16[960,384]{1,0:T(8,128)(2,1)S(1)}, u32[]{:S(2)}, u32[]{:S(2)}) collective-permute-start(bf16[960,384]{1,0:T(8,128)(2,1)} %get-tuple-element.207), channel_id=1, source_target_pairs={{0,8},{4,20},{8,0},{12,28},{16,24},{20,4},{24,16},{28,12},{1,9},{5... | collective-permute-start | bytes 2211848 | tf_op jit(solution)/shard_map/ppermute | solution.py:974
  352.6 28.7 %collective-permute-start.53 = (bf16[2,240,640]{2,1,0:T(8,128)(2,1)}, bf16[2,240,640]{2,1,0:T(8,128)(2,1)}, u32[]{:S(2)}, u32[]{:S(2)}) collective-permute-start(bf16[2,240,640]{2,1,0:T(8,128)(2,1)} %get-tuple-element.213), channel_id=1, source_target_pairs={{0,1},{1,0},{2,3},{3,2},{4,5},{5,4},{6,7},{7,6},{8,9},{9,8},{10,11... | collective-permute-start | bytes 1843208 | tf_op jit(solution)/shard_map/ppermute | solution.py:980
  354.4 29.0 %collective-permute-start.56 = (bf16[480,640]{1,0:T(8,128)(2,1)}, bf16[480,640]{1,0:T(8,128)(2,1)S(1)}, u32[]{:S(2)}, u32[]{:S(2)}) collective-permute-start(bf16[480,640]{1,0:T(8,128)(2,1)} %get-tuple-element.221), channel_id=1, source_target_pairs={{0,2},{1,3},{2,0},{3,1},{4,6},{5,7},{6,4},{7,5},{8,10},{9,11},{10,... | collective-permute-start | bytes 1843208 | tf_op jit(solution)/shard_map/ppermute | solution.py:980
  370.5 12.1 %collective-permute-start.51 = (bf16[480,384]{1,0:T(8,128)(2,1)S(1)}, bf16[480,384]{1,0:T(8,128)(2,1)S(1)}, u32[]{:S(2)}, u32[]{:S(2)}) collective-permute-start(bf16[480,384]{1,0:T(8,128)(2,1)S(1)} %get-tuple-element.210), channel_id=1, source_target_pairs={{0,16},{4,12},{8,24},{12,4},{16,0},{20,28},{24,8},{28,20},{1,17},{... | collective-permute-start | bytes 1105928 | tf_op jit(solution)/shard_map/ppermute | solution.py:974
  372.0 10.6 %collective-permute-start.52 = (bf16[480,384]{1,0:T(8,128)(2,1)S(1)}, bf16[480,384]{1,0:T(8,128)(2,1)S(1)}, u32[]{:S(2)}, u32[]{:S(2)}) collective-permute-start(bf16[480,384]{1,0:T(8,128)(2,1)S(1)} %get-tuple-element.211), channel_id=1, source_target_pairs={{0,16},{4,12},{8,24},{12,4},{16,0},{20,28},{24,8},{28,20},{1,17},{... | collective-permute-start | bytes 1105928 | tf_op jit(solution)/shard_map/ppermute | solution.py:974
  384.1 6.9 %collective-permute-start.57 = (bf16[2,120,640]{2,1,0:T(8,128)(2,1)S(1)}, bf16[2,120,640]{2,1,0:T(8,128)(2,1)S(1)}, u32[]{:S(2)}, u32[]{:S(2)}) collective-permute-start(bf16[2,120,640]{2,1,0:T(8,128)(2,1)S(1)} %get-tuple-element.224), channel_id=1, source_target_pairs={{0,8},{4,20},{8,0},{12,28},{16,24},{20,4},{24,16},{28,12},{1,9},{5... | collective-permute-start | bytes 921608 | tf_op jit(solution)/shard_map/ppermute | solution.py:974
  385.7 15.5 %collective-permute-start.54 = (bf16[2,240,384]{2,1,0:T(8,128)(2,1)S(1)}, bf16[2,240,384]{2,1,0:T(8,128)(2,1)S(1)}, u32[]{:S(2)}, u32[]{:S(2)}) collective-permute-start(bf16[2,240,384]{2,1,0:T(8,128)(2,1)S(1)} %get-tuple-element.217), channel_id=1, source_target_pairs={{0,1},{1,0},{2,3},{3,2},{4,5},{5,4},{6,7},{7,6},{8,9},{9,8},{10,11... | collective-permute-start | bytes 1105928 | tf_op jit(solution)/shard_map/ppermute | solution.py:980
  388.1 12.4 %collective-permute-start.55 = (bf16[240,640]{1,0:T(8,128)(2,1)S(1)}, bf16[240,640]{1,0:T(8,128)(2,1)S(1)}, u32[]{:S(2)}, u32[]{:S(2)}) collective-permute-start(bf16[240,640]{1,0:T(8,128)(2,1)S(1)} %get-tuple-element.219), channel_id=1, source_target_pairs={{0,2},{1,3},{2,0},{3,1},{4,6},{5,7},{6,4},{7,5},{8,10},{9,11},{10,... | collective-permute-start | bytes 921608 | tf_op jit(solution)/shard_map/ppermute | solution.py:980
  391.7 15.6 %collective-permute-start.67 = (bf16[120,640]{1,0:T(8,128)(2,1)S(1)}, bf16[120,640]{1,0:T(8,128)(2,1)S(1)}, u32[]{:S(2)}, u32[]{:S(2)}) collective-permute-start(bf16[120,640]{1,0:T(8,128)(2,1)S(1)} %get-tuple-element.233), channel_id=1, source_target_pairs={{0,16},{4,12},{8,24},{12,4},{16,0},{20,28},{24,8},{28,20},{1,17},{... | collective-permute-start | bytes 460808 | tf_op jit(solution)/shard_map/ppermute | solution.py:974
  401.9 10.0 %collective-permute-start.66 = (bf16[240,384]{1,0:T(8,128)(2,1)S(1)}, bf16[240,384]{1,0:T(8,128)(2,1)S(1)}, u32[]{:S(2)}, u32[]{:S(2)}) collective-permute-start(bf16[240,384]{1,0:T(8,128)(2,1)S(1)} %get-tuple-element.231), channel_id=1, source_target_pairs={{0,2},{1,3},{2,0},{3,1},{4,6},{5,7},{6,4},{7,5},{8,10},{9,11},{10,... | collective-permute-start | bytes 552968 | tf_op jit(solution)/shard_map/ppermute | solution.py:980
  405.2 9.6 %collective-permute-start.62 = (bf16[240,640]{1,0:T(8,128)(2,1)S(1)}, bf16[240,640]{1,0:T(8,128)(2,1)S(1)}, u32[]{:S(2)}, u32[]{:S(2)}) collective-permute-start(bf16[240,640]{1,0:T(8,128)(2,1)S(1)} %get-tuple-element.229.rest_0_), channel_id=1, source_target_pairs={{0,4},{4,0},{8,12},{12,8},{16,20},{20,16},{24,28},{28,24},{1,5},{5... | collective-permute-start | bytes 921608 | tf_op jit(solution)/shard_map/ppermute | solution.py:974
  405.2 37.9 %collective-permute-start.58 = (bf16[1920,256]{1,0:T(8,128)(2,1)S(1)}, bf16[1920,256]{1,0:T(8,128)(2,1)S(1)}, u32[]{:S(2)}, u32[]{:S(2)}) collective-permute-start(bf16[1920,256]{1,0:T(8,128)(2,1)S(1)} %hold.7), channel_id=1, source_target_pairs={{0,0},{4,1},{1,2},{5,3},{2,4},{6,5},{3,6},{7,7},{8,8},{12,9},{9,10... | collective-permute-start | bytes 2949128 | tf_op jit(solution)/shard_map/ppermute | solution.py:991
  405.9 9.9 %collective-permute-start.61 = (bf16[240,640]{1,0:T(8,128)(2,1)S(1)}, bf16[240,640]{1,0:T(8,128)(2,1)S(1)}, u32[]{:S(2)}, u32[]{:S(2)}) collective-permute-start(bf16[240,640]{1,0:T(8,128)(2,1)S(1)} %get-tuple-element.229.rest_0_), channel_id=1, source_target_pairs={{0,24},{4,28},{8,16},{12,20},{16,8},{20,12},{24,0},{28,4},{1,25},{... | collective-permute-start | bytes 921608 | tf_op jit(solution)/shard_map/ppermute | solution.py:974
  407.3 17.3 %collective-permute-start.60 = (bf16[240,640]{1,0:T(8,128)(2,1)S(1)}, bf16[240,640]{1,0:T(8,128)(2,1)S(1)}, u32[]{:S(2)}, u32[]{:S(2)}) collective-permute-start(bf16[240,640]{1,0:T(8,128)(2,1)S(1)} %get-tuple-element.229.rest_0_), channel_id=1, source_target_pairs={{0,16},{4,12},{8,24},{12,4},{16,0},{20,28},{24,8},{28,20},{1,17},{... | collective-permute-start | bytes 921608 | tf_op jit(solution)/shard_map/ppermute | solution.py:974
  411.8 13.9 %collective-permute-start.59 = (bf16[240,640]{1,0:T(8,128)(2,1)S(1)}, bf16[240,640]{1,0:T(8,128)(2,1)S(1)}, u32[]{:S(2)}, u32[]{:S(2)}) collective-permute-start(bf16[240,640]{1,0:T(8,128)(2,1)S(1)} %get-tuple-element.229.rest_0_), channel_id=1, source_target_pairs={{0,8},{4,20},{8,0},{12,28},{16,24},{20,4},{24,16},{28,12},{1,9},{5... | collective-permute-start | bytes 921608 | tf_op jit(solution)/shard_map/ppermute | solution.py:974
  414.8 13.5 %collective-permute-start.78 = (bf16[120,640]{1,0:T(8,128)(2,1)S(1)}, bf16[120,640]{1,0:T(8,128)(2,1)S(1)}, u32[]{:S(2)}, u32[]{:S(2)}) collective-permute-start(bf16[120,640]{1,0:T(8,128)(2,1)S(1)} %get-tuple-element.240.refs_1_), channel_id=1, source_target_pairs={{0,4},{4,0},{8,12},{12,8},{16,20},{20,16},{24,28},{28,24},{1,5},{5... | collective-permute-start | bytes 460808 | tf_op jit(solution)/shard_map/ppermute | solution.py:974
  415.8 12.4 %collective-permute-start.77 = (bf16[120,640]{1,0:T(8,128)(2,1)S(1)}, bf16[120,640]{1,0:T(8,128)(2,1)S(1)}, u32[]{:S(2)}, u32[]{:S(2)}) collective-permute-start(bf16[120,640]{1,0:T(8,128)(2,1)S(1)} %get-tuple-element.240.refs_1_), channel_id=1, source_target_pairs={{0,24},{4,28},{8,16},{12,20},{16,8},{20,12},{24,0},{28,4},{1,25},{... | collective-permute-start | bytes 460808 | tf_op jit(solution)/shard_map/ppermute | solution.py:974
  424.6 9.4 %collective-permute-start.76 = (bf16[120,640]{1,0:T(8,128)(2,1)S(1)}, bf16[120,640]{1,0:T(8,128)(2,1)S(1)}, u32[]{:S(2)}, u32[]{:S(2)}) collective-permute-start(bf16[120,640]{1,0:T(8,128)(2,1)S(1)} %get-tuple-element.240.refs_1_), channel_id=1, source_target_pairs={{0,16},{4,12},{8,24},{12,4},{16,0},{20,28},{24,8},{28,20},{1,17},{... | collective-permute-start | bytes 460808 | tf_op jit(solution)/shard_map/ppermute | solution.py:974
  425.8 13.5 %collective-permute-start.70 = (bf16[240,384]{1,0:T(8,128)(2,1)S(1)}, bf16[240,384]{1,0:T(8,128)(2,1)S(1)}, u32[]{:S(2)}, u32[]{:S(2)}) collective-permute-start(bf16[240,384]{1,0:T(8,128)(2,1)S(1)} %get-tuple-element.239.rest_0_), channel_id=1, source_target_pairs={{0,24},{4,28},{8,16},{12,20},{16,8},{20,12},{24,0},{28,4},{1,25},{... | collective-permute-start | bytes 552968 | tf_op jit(solution)/shard_map/ppermute | solution.py:974
  428.2 11.4 %collective-permute-start.69 = (bf16[240,384]{1,0:T(8,128)(2,1)S(1)}, bf16[240,384]{1,0:T(8,128)(2,1)S(1)}, u32[]{:S(2)}, u32[]{:S(2)}) collective-permute-start(bf16[240,384]{1,0:T(8,128)(2,1)S(1)} %get-tuple-element.239.rest_0_), channel_id=1, source_target_pairs={{0,16},{4,12},{8,24},{12,4},{16,0},{20,28},{24,8},{28,20},{1,17},{... | collective-permute-start | bytes 552968 | tf_op jit(solution)/shard_map/ppermute | solution.py:974
  428.3 11.5 %collective-permute-start.68 = (bf16[240,384]{1,0:T(8,128)(2,1)S(1)}, bf16[240,384]{1,0:T(8,128)(2,1)S(1)}, u32[]{:S(2)}, u32[]{:S(2)}) collective-permute-start(bf16[240,384]{1,0:T(8,128)(2,1)S(1)} %get-tuple-element.239.rest_0_), channel_id=1, source_target_pairs={{0,8},{4,20},{8,0},{12,28},{16,24},{20,4},{24,16},{28,12},{1,9},{5... | collective-permute-start | bytes 552968 | tf_op jit(solution)/shard_map/ppermute | solution.py:974
  433.9 5.2 %collective-permute-start.75 = (bf16[120,640]{1,0:T(8,128)(2,1)S(1)}, bf16[120,640]{1,0:T(8,128)(2,1)S(1)}, u32[]{:S(2)}, u32[]{:S(2)}) collective-permute-start(bf16[120,640]{1,0:T(8,128)(2,1)S(1)} %get-tuple-element.240.refs_1_), channel_id=1, source_target_pairs={{0,8},{4,20},{8,0},{12,28},{16,24},{20,4},{24,16},{28,12},{1,9},{5... | collective-permute-start | bytes 460808 | tf_op jit(solution)/shard_map/ppermute | solution.py:974
  442.1 8.5 %collective-permute-start.71 = (bf16[240,384]{1,0:T(8,128)(2,1)S(1)}, bf16[240,384]{1,0:T(8,128)(2,1)S(1)}, u32[]{:S(2)}, u32[]{:S(2)}) collective-permute-start(bf16[240,384]{1,0:T(8,128)(2,1)S(1)} %get-tuple-element.239.rest_0_), channel_id=1, source_target_pairs={{0,4},{4,0},{8,12},{12,8},{16,20},{20,16},{24,28},{28,24},{1,5},{5... | collective-permute-start | bytes 552968 | tf_op jit(solution)/shard_map/ppermute | solution.py:974
  442.4 8.2 %collective-permute-start.74 = (bf16[240,384]{1,0:T(8,128)(2,1)S(1)}, bf16[240,384]{1,0:T(8,128)(2,1)S(1)}, u32[]{:S(2)}, u32[]{:S(2)}) collective-permute-start(bf16[240,384]{1,0:T(8,128)(2,1)S(1)} %collective-permute-done.70.rest_3_), channel_id=1, source_target_pairs={{0,4},{4,0},{8,12},{12,8},{16,20},{20,16},{24,28},{28,24},{1,5},{5... | collective-permute-start | bytes 552968 | tf_op jit(solution)/shard_map/ppermute | solution.py:974
  442.6 8.0 %collective-permute-start.73 = (bf16[240,384]{1,0:T(8,128)(2,1)S(1)}, bf16[240,384]{1,0:T(8,128)(2,1)S(1)}, u32[]{:S(2)}, u32[]{:S(2)}) collective-permute-start(bf16[240,384]{1,0:T(8,128)(2,1)S(1)} %collective-permute-done.69.rest_2_), channel_id=1, source_target_pairs={{0,4},{4,0},{8,12},{12,8},{16,20},{20,16},{24,28},{28,24},{1,5},{5... | collective-permute-start | bytes 552968 | tf_op jit(solution)/shard_map/ppermute | solution.py:974
  442.9 7.7 %collective-permute-start.72 = (bf16[240,384]{1,0:T(8,128)(2,1)S(1)}, bf16[240,384]{1,0:T(8,128)(2,1)S(1)}, u32[]{:S(2)}, u32[]{:S(2)}) collective-permute-start(bf16[240,384]{1,0:T(8,128)(2,1)S(1)} %collective-permute-done.68.rest_1_), channel_id=1, source_target_pairs={{0,4},{4,0},{8,12},{12,8},{16,20},{20,16},{24,28},{28,24},{1,5},{5... | collective-permute-start | bytes 552968 | tf_op jit(solution)/shard_map/ppermute | solution.py:974
  443.1 5.2 %collective-permute-start.79 = (bf16[120,640]{1,0:T(8,128)(2,1)S(1)}, bf16[120,640]{1,0:T(8,128)(2,1)S(1)}, u32[]{:S(2)}, u32[]{:S(2)}) collective-permute-start(bf16[120,640]{1,0:T(8,128)(2,1)S(1)} %collective-permute-done.75.refs_2_), channel_id=1, source_target_pairs={{0,4},{4,0},{8,12},{12,8},{16,20},{20,16},{24,28},{28,24},{1,5},{5... | collective-permute-start | bytes 460808 | tf_op jit(solution)/shard_map/ppermute | solution.py:974
  (102 other events, 820.4 us)

commit v18 on v17

--- a/solution.py
+++ b/solution.py
@@ -963,6 +963,36 @@
     return small(kernel, sc, [both], [shape(block, bf16), shape(block, f32)], [], after, "depart")
 
 
+def sum_both(sc, own_b, got_b, own_d, got_d, after):
+    def kernel(sc, b_ref, gb_ref, d_ref, gd_ref, *rest):
+        out_ref = rest[-1]
+        n = b_ref.shape[0]
+        out_ref[:n, :] = (b_ref[...] + gb_ref[...].astype(f32)).astype(bf16)
+        out_ref[n:, :] = (d_ref[...] + gd_ref[...].astype(f32)).astype(bf16)
+
+    rows, cols = own_b.shape[0] + own_d.shape[0], own_b.shape[1]
+    return small(kernel, sc, [own_b, got_b, own_d, got_d], [shape((rows, cols), bf16)], [], after, "sum_both")
+
+
+def lay_both(sc, mine, other, rows, after):
+    def kernel(sc, *rest):
+        gate_ref, up_ref, down_ref, kept = rest[-4:]
+        cols = kept.shape[3]
+        n = kept.shape[2] - rows
+        for kind, pieces in ((sc[0], rest[:4]), (1 - sc[0], rest[4:8])):
+            for who, piece in zip(whose(kind), pieces):
+                kept[kind, sc[1] ^ who] = piece[...].astype(f32)
+        for c, out in enumerate((gate_ref, up_ref)):
+            for m in range(4):
+                out[:, m * cols : (m + 1) * cols] = kept[c, m, :rows]
+                at = (c * 4 + m) * n
+                down_ref[at : at + n, :] = kept[c, m, rows:]
+
+    total, cols = mine[0].shape
+    outs = [shape((rows, 4 * cols), f32)] * 2 + [shape((8 * (total - rows), cols), f32)]
+    return small(kernel, sc, [*mine, *other], outs, [pltpu.VMEM((2, 4, total, cols), f32)], after, "lay_both")
+
+
 CORE, SIDE, BACK = 1, 2, 4
 rope_base = 10000.0
 RUNS = 2
@@ -1119,19 +1149,16 @@
     got_d = flip(send_d, SIDE, BACK)
     later_d, own_d, done = sum_first(sc, [keep_d], [got_d], [done])
     more_d = flip(later_d, BACK, SIDE)
-    piece_b, done = sum_two(sc, ring_b, got_b, [done])
+    send_a, ring_a, done = sum_third(sc, ring_a, got_a, [done])
+    got_a = flip_z(send_a, 2)
+    piece_b, done = sum_both(sc, ring_b, got_b, own_d, more_d, [done])
     all_b = spread(over_groups(piece_b))
-    send_a, ring_a, first = sum_third(sc, ring_a, got_a, [done])
-    got_a = flip_z(send_a, 2)
-    piece_d, done = sum_two(sc, own_d, more_d, [first])
-    all_d = spread(over_groups(piece_d))
     piece_a, done = sum_two(sc, ring_a, got_a, [done])
     all_a = spread(over_groups(piece_a))
-    grad_gate, grad_up, done = lay(sc, all_b, across(all_b), (gate_weight.shape[1],) * 2, [done])
-    leaving = home_to_work(hold(leaving, [first]), back=True)
-    output, grad_tokens, done = depart(sc, leaving, [done])
-    grad_down_, done = lay_down(sc, all_d, across(all_d), [done])
-    grad_query, grad_key, grad_value, grad_out, dgains, _ = lay(sc, all_a, across(all_a), (width, KVW, KVW, width), [done])
+    leaving = home_to_work(hold(leaving, [done]), back=True)
+    grad_gate, grad_up, grad_down_, done = lay_both(sc, all_b, across(all_b), ring_a.shape[0], [done])
+    grad_query, grad_key, grad_value, grad_out, dgains, done = lay(sc, all_a, across(all_a), (width, KVW, KVW, width), [done])
+    output, grad_tokens, _ = depart(sc, leaving, [done])
     output, grad_tokens = output.T, grad_tokens.T
     return (output[None], grad_tokens[None], dgains[0], grad_query, grad_key, grad_value, grad_out, dgains[1], grad_gate, grad_up, grad_down_.T)
 

time: 462 us -> 466 us (level)
  the two profiles are of different devices: /device:TPU:0 before, /device:TPU:24 now
where the time goes in v18:
time: 466 us; the launch traced here: 461 us
  Pallas kernels  200 us (43%)
  waiting for transfers between devices  175 us (38%)
  starting transfers between devices  50 us (11%)
  local copies, waits for them, and re-layouts  30.5 us (7%)
    ppermute x56, waiting for transfers between devices, flip(): lax.ppermute(value, 'dp', [(i, i ^ bits[i & 1]) for i in range(count)])  72.9 us
    ppermute x12, waiting for transfers between devices, flip_z(): return lax.ppermute(value, ('dp', 'fsdp'), pairs)  55.9 us
    pallas_call x3, Pallas kernels, back(): pl.pallas_call(functools.partial(back_kernel, start, end, len(after)), ou...  45.7 us
    pallas_call x2, Pallas kernels, post(): pl.pallas_call(functools.partial(post_kernel, last, len(after)), out_shap...  34.6 us
    ppermute x56, starting transfers between devices, flip(): lax.ppermute(value, 'dp', [(i, i ^ bits[i & 1]) for i in range(count)])  31 us
    unnamed x172, local copies, waits for them, and re-layouts  27.8 us
    pallas_call x2, Pallas kernels, attend_back(): pl.pallas_call(attend_back_kernel, out_shape=(shape((3, n, PIECE), bf16),...  25.3 us
    ppermute x2, waiting for transfers between devices, window(): far = lax.ppermute(own, 'fsdp', [(z, z + 1) for z in range(0, depth, 2)])  23.3 us
  transfers between devices with their start and end apart: 75, of which 36 were waited for; matrix products, arithmetic and copies ran while one was open for 1% of the time, Pallas kernels for 31%

profile of v18, /device:TPU:24, one launch (start us, length us, event | category | flops | bytes accessed | tf_op | source)
XLA Modules:
  0.0 460.9 jit_solution(2287780062982248218)
XLA Ops:
  3.3 2.7 pick_first.1.rest_0_
  6.6 10.7 %collective-permute-done.1.rest_2_ = bf16[240,384]{1,0:T(8,128)(2,1)S(1)} collective-permute-done((bf16[240,384]{1,0:T(8,128)(2,1)}, bf16[240,384]{1,0:T(8,128)(2,1)S(1)}, u32[]{:S(2)}, u32[]{:S(2)}) %collective-permute-start.1) | collective-permute-done | bytes 184352 | tf_op jit(solution)/shard_map/ppermute | solution.py:1010
  20.8 3.1 collective-permute-done.2.rest_3_
  23.9 1.5 stack.30.first_ref
  25.5 1.6 collective-permute-start.3
  27.1 1.5 collective-permute-start.4
  28.9 16.0 %collective-permute-done.3.refs_1_.rest_1_ = bf16[960,384]{1,0:T(8,128)(2,1)} collective-permute-done((bf16[960,384]{1,0:T(8,128)(2,1)S(1)}, bf16[960,384]{1,0:T(8,128)(2,1)}, u32[]{:S(2)}, u32[]{:S(2)}) %collective-permute-start.3) | collective-permute-done | bytes 737312 | tf_op jit(solution)/shard_map/ppermute | solution.py:1004
  44.9 6.0 %collective-permute-done.11.refs_0_ = bf16[368,640]{1,0:T(8,128)(2,1)S(1)} collective-permute-done((bf16[368,640]{1,0:T(8,128)(2,1)S(1)}, bf16[368,640]{1,0:T(8,128)(2,1)S(1)}, u32[]{:S(2)}, u32[]{:S(2)}) %collective-permute-start.11) | collective-permute-done | bytes 471072 | tf_op jit(solution)/shard_map/ppermute | solution.py:1010
  51.0 12.7 %collective-permute-done.12.rest_3_ = bf16[368,640]{1,0:T(8,128)(2,1)S(1)} collective-permute-done((bf16[368,640]{1,0:T(8,128)(2,1)S(1)}, bf16[368,640]{1,0:T(8,128)(2,1)S(1)}, u32[]{:S(2)}, u32[]{:S(2)}) %collective-permute-start.12) | collective-permute-done | bytes 471072 | tf_op jit(solution)/shard_map/ppermute | solution.py:1010
  63.7 3.0 stack.31.rest_8_
  67.8 1.9 collective-permute-start.14
  69.8 8.2 %collective-permute-done.14.ht_ref = bf16[976,256]{1,0:T(8,128)(2,1)S(1)} collective-permute-done((bf16[976,256]{1,0:T(8,128)(2,1)S(1)}, bf16[976,256]{1,0:T(8,128)(2,1)S(1)}, u32[]{:S(2)}, u32[]{:S(2)}) %collective-permute-start.14) | collective-permute-done | bytes 499744 | tf_op jit(solution)/shard_map/ppermute | solution.py:1021
  82.0 7.5 %pre.1 = (bf16[256,960]{1,0:T(8,128)(2,1)}, bf16[256,960]{1,0:T(8,128)(2,1)}, bf16[960,256]{1,0:T(8,128)(2,1)}, bf16[656,256]{1,0:T(8,128)(2,1)}) custom-call(s32[3]{0:T(128)} %pad_add_fusion.sc.refs_0_, bf16[976,256]{1,0:T(8,128)(2,1)} %copy-done.77, f32[1,960]{1,0:T(1,128)} %get-tuple-element.257.gain_ref.gain_a.rest_22_.rest_14_, ...), custom_call_target="tpu_custom_call" | custom-call | flops 1024 | bytes 1024 | tf_op jit(solution)/shard_map/pre/pallas_call | solution.py:138
  89.5 1.6 collective-permute-start.15
  91.1 14.2 %collective-permute-done.15.refs_1_.kv0 = bf16[656,256]{1,0:T(8,128)(2,1)S(1)} collective-permute-done((bf16[656,256]{1,0:T(8,128)(2,1)}, bf16[656,256]{1,0:T(8,128)(2,1)S(1)}, u32[]{:S(2)}, u32[]{:S(2)}) %collective-permute-start.15) | collective-permute-done | bytes 335904 | tf_op jit(solution)/shard_map/ppermute | solution.py:1043
  105.4 4.0 collective-permute-done.16.refs_2_.rest_10_
  111.6 10.1 %attend.2 = (bf16[960,256]{1,0:T(8,128)(2,1)S(1)}, f32[15,256]{1,0:T(8,128)S(1)}) custom-call(bf16[960,256]{1,0:T(8,128)(2,1)S(1)} %copy-done.22, bf16[656,256]{1,0:T(8,128)(2,1)S(1)} %collective-permute-done.15.refs_1_.kv0, bf16[656,256]{1,0:T(8,128)(2,1)S(1)} %collective-permute-done.18.kv1, bf16[656,256]{1,0:T(8,128)(2,1)S(1)} %copy-done.5), custom_call_target="tpu_custom_call" | custom-call | flops 1024 | bytes 1024 | tf_op jit(solution)/shard_map/attend/pallas_call | solution.py:191
  122.3 11.2 %collective-permute-done.17.refs_0_ = bf16[4,368,640]{2,1,0:T(8,128)(2,1)} collective-permute-done((bf16[4,368,640]{2,1,0:T(8,128)(2,1)}, bf16[4,368,640]{2,1,0:T(8,128)(2,1)}, u32[]{:S(2)}, u32[]{:S(2)}) %collective-permute-start.17) | collective-permute-done | bytes 1884192 | tf_op jit(solution)/shard_map/ppermute | solution.py:1004
  134.9 2.8 collective-permute-done.22.rest_15_
  137.7 17.9 %post.2 = (bf16[256,960]{1,0:T(8,128)(2,1)}, f32[256,960]{1,0:T(8,128)}, bf16[256,960]{1,0:T(8,128)(2,1)}, bf16[256,2560]{1,0:T(8,128)(2,1)}, bf16[256,2560]{1,0...) custom-call(s32[3]{0:T(128)} %pad_add_fusion.sc.refs_0_, ...), custom_call_target="tpu_custom_call" | custom-call | flops 1024 | bytes 1024 | tf_op jit(solution)/shard_map/post/pallas_call | solution.py:358
  157.5 1.9 collective-permute-start.23
  159.5 9.1 %collective-permute-done.24.kv0 = bf16[656,256]{1,0:T(8,128)(2,1)S(1)} collective-permute-done((bf16[656,256]{1,0:T(8,128)(2,1)}, bf16[656,256]{1,0:T(8,128)(2,1)S(1)}, u32[]{:S(2)}, u32[]{:S(2)}) %collective-permute-start.24) | collective-permute-done | bytes 335904 | tf_op jit(solution)/shard_map/ppermute | solution.py:1043
  172.6 10.5 %attend.3 = (bf16[960,256]{1,0:T(8,128)(2,1)S(1)}, f32[15,256]{1,0:T(8,128)S(1)}) custom-call(bf16[960,256]{1,0:T(8,128)(2,1)S(1)} %copy-done.23, bf16[656,256]{1,0:T(8,128)(2,1)S(1)} %collective-permute-done.24.kv0, bf16[656,256]{1,0:T(8,128)(2,1)S(1)} %collective-permute-done.25.kv1, bf16[656,256]{1,0:T(8,128)(2,1)S(1)} %copy-done.3, ...), custom_call_target="tpu_custom_call" | custom-call | flops 1024 | bytes 1024 | tf_op jit(solution)/shard_map/attend/pallas_call | solution.py:191
  184.7 16.7 %post.3 = (bf16[256,960]{1,0:T(8,128)(2,1)}, f32[256,960]{1,0:T(8,128)}, bf16[256,960]{1,0:T(8,128)(2,1)}, bf16[256,2560]{1,0:T(8,128)(2,1)}, bf16[256,2560]{1,0...) custom-call(s32[3]{0:T(128)} %pad_add_fusion.sc.refs_0_, bf16[960,256]{1,0:T(8,128)(2,1)} %copy-done.48, ...), custom_call_target="tpu_custom_call" | custom-call | flops 1024 | bytes 1024 | tf_op jit(solution)/shard_map/post/pallas_call | solution.py:358
  201.5 18.4 %back_start.1 = (bf16[256,960]{1,0:T(8,128)(2,1)}, bf16[256,2560]{1,0:T(8,128)(2,1)}, bf16[256,2560]{1,0:T(8,128)(2,1)}, f32[256,960]{1,0:T(8,128)}, bf16[3,256,...) custom-call(s32[3]{0:T(128)} %pad_add_fusion.sc.refs_0_, bf16[960,384]{1,0:T(8,128)(2,1)} %bitcast.28, ...), custom_call_target="tpu_custom_call" | custom-call | flops 1024 | bytes 1024 | tf_op jit(solution)/shard_map/back_start/pallas_call | solution.py:539
  222.7 12.6 %attend_back.2 = (bf16[3,256,384]{2,1,0:T(8,128)(2,1)S(1)}, bf16[3,256,384]{2,1,0:T(8,128)(2,1)S(1)}, f32[640,256]{1,0:T(8,128)S(1)}, bf16[640,256]{1,0:T(8,128)(2,1)S(1)}, f32[640,256]{1,0:T(8,128)S(1)}) custom-call(s32[3]{0:T(128)S(1)} %copy-done.41, bf16[3,256,384]{2,1,0:T(8,128)(2,1)S(1)} %copy-done.8, bf16[960,256]{1,0:T(8,128)(2,1)S(1)} %copy-done.23, ...), custom_call_target="tpu_custom_call" | custom-call | flops 1024 | bytes 1024 | tf_op jit(solution)/shard_map/attend_back/pallas_call | solution.py:244
  239.5 1.6 collective-permute-start.31
  241.2 7.4 %collective-permute-done.31.rest_20_ = bf16[640,256]{1,0:T(8,128)(2,1)S(1)} collective-permute-done((bf16[640,256]{1,0:T(8,128)(2,1)S(1)}, bf16[640,256]{1,0:T(8,128)(2,1)S(1)}, u32[]{:S(2)}, u32[]{:S(2)}) %collective-permute-start.31) | collective-permute-done | bytes 327712 | tf_op jit(solution)/shard_map/ppermute | solution.py:1052
  250.8 20.4 %back_join.1 = (bf16[256,384]{1,0:T(8,128)(2,1)}, bf16[256,384]{1,0:T(8,128)(2,1)}, bf16[256,384]{1,0:T(8,128)(2,1)}, f32[1,960]{1,0:T(1,128)}, bf16[256,960]{1,...) custom-call(s32[3]{0:T(128)} %pad_add_fusion.sc.refs_0_, ...), custom_call_target="tpu_custom_call" | custom-call | flops 1024 | bytes 1024 | tf_op jit(solution)/shard_map/back_join/pallas_call | solution.py:539
  271.3 3.2 collective-permute-done.40.rest_7_
  275.6 11.5 %grad_ffn.1 = (bf16[2,960,640]{2,1,0:T(8,128)(2,1)}, bf16[2,960,640]{2,1,0:T(8,128)(2,1)}, f32[8,128]{1,0:T(8,128)}) custom-call(s32[3]{0:T(128)} %pad_add_fusion.sc.refs_0_, bf16[256,960]{1,0:T(8,128)(2,1)} %get-tuple-element.159.rest_0_, bf16[256,960]{1,0:T(8,128)(2,1)} %get-tuple-element.135.rest_1_, bf16[256,960]{1,0:T(8,128)(2,1)} %copy-done.67, ...), custom_call_target="tpu_custom_call" | custom-call | flops 1024 | bytes 1024 | tf_op jit(solution)/shard_map/grad_ffn/pallas_call | solution.py:581
  287.4 1.4 collective-permute-done.39.rest_0_.rest_18_
  289.7 12.6 %attend_back.3 = (bf16[3,256,384]{2,1,0:T(8,128)(2,1)S(1)}, bf16[3,256,384]{2,1,0:T(8,128)(2,1)S(1)}, f32[640,256]{1,0:T(8,128)S(1)}, bf16[640,256]{1,0:T(8,128)(2,1)S(1)}, f32[640,256]{1,0:T(8,128)S(1)}) custom-call(s32[3]{0:T(128)S(1)} %copy-done.42, bf16[3,256,384]{2,1,0:T(8,128)(2,1)S(1)} %copy-done.9, bf16[960,256]{1,0:T(8,128)(2,1)S(1)} %copy-done.22, ...), custom_call_target="tpu_custom_call" | custom-call | flops 1024 | bytes 1024 | tf_op jit(solution)/shard_map/attend_back/pallas_call | solution.py:244
  306.9 4.4 collective-permute-start.42
  312.1 8.2 %grad_down.1 = (bf16[2,480,640]{2,1,0:T(8,128)(2,1)}, bf16[2,480,640]{2,1,0:T(8,128)(2,1)}, f32[8,128]{1,0:T(8,128)}) custom-call(s32[3]{0:T(128)} %pad_add_fusion.sc.refs_0_, bf16[256,960]{1,0:T(8,128)(2,1)} %get-tuple-element.156.rest_0_, bf16[256,960]{1,0:T(8,128)(2,1)} %get-tuple-element.177.rest_1_, bf16[256,960]{1,0:T(8,128)(2,1)} %copy-done.66, ...), custom_call_target="tpu_custom_call" | custom-call | flops 1024 | bytes 1024 | tf_op jit(solution)/shard_map/grad_down/pallas_call | solution.py:613
  321.0 7.0 %back_end.1 = (bf16[256,384]{1,0:T(8,128)(2,1)}, bf16[256,384]{1,0:T(8,128)(2,1)}, bf16[256,384]{1,0:T(8,128)(2,1)}, f32[1,960]{1,0:T(1,128)}, bf16[1920,256]{1,0:T(8,128)(2,1)}) custom-call(s32[3]{0:T(128)} %pad_add_fusion.sc.refs_0_, bf16[960,384]{1,0:T(8,128)(2,1)} %bitcast.30, bf16[960,384]{1,0:T(8,128)(2,1)} %collective-permute-done.3.refs_1_.rest_1_, ...), custom_call_target="tpu_custom_call" | custom-call | flops 1024 | bytes 1024 | tf_op jit(solution)/shard_map/back_end/pallas_call | solution.py:539
  328.7 2.0 sum_first.3
  330.7 1.4 copy-done.15
  332.2 1.6 collective-permute-start.47
  334.3 1.5 collective-permute-done.44.rest_17_
  336.7 8.1 %grad_attention.2 = (bf16[960,384]{1,0:T(8,128)(2,1)}, bf16[960,384]{1,0:T(8,128)(2,1)}, f32[8,128]{1,0:T(8,128)}) custom-call(s32[3]{0:T(128)} %pad_add_fusion.sc.refs_0_, bf16[256,960]{1,0:T(8,128)(2,1)} %get-tuple-element.158.rest_0_, bf16[256,960]{1,0:T(8,128)(2,1)} %get-tuple-element.134.rest_1_, ...), custom_call_target="tpu_custom_call" | custom-call | flops 1024 | bytes 1024 | tf_op jit(solution)/shard_map/grad_attention/pallas_call | solution.py:664
  345.3 1.6 collective-permute-start.50
  346.9 2.5 collective-permute-done.48.refs_2_
  350.0 2.4 sum_third.3
  352.4 1.8 sum_second.2
  355.1 7.8 %grad_attention.3 = (bf16[960,384]{1,0:T(8,128)(2,1)}, bf16[960,384]{1,0:T(8,128)(2,1)}, f32[8,128]{1,0:T(8,128)}) custom-call(s32[3]{0:T(128)} %pad_add_fusion.sc.refs_0_, bf16[256,960]{1,0:T(8,128)(2,1)} %get-tuple-element.158.rest_0_, bf16[256,960]{1,0:T(8,128)(2,1)} %get-tuple-element.134.rest_1_, ...), custom_call_target="tpu_custom_call" | custom-call | flops 1024 | bytes 1024 | tf_op jit(solution)/shard_map/grad_attention/pallas_call | solution.py:664
  362.9 1.6 collective-permute-done.50.refs_4_
  370.3 9.2 %collective-permute-done.53.refs_2_ = bf16[2,240,640]{2,1,0:T(8,128)(2,1)} collective-permute-done((bf16[2,240,640]{2,1,0:T(8,128)(2,1)}, bf16[2,240,640]{2,1,0:T(8,128)(2,1)}, u32[]{:S(2)}, u32[]{:S(2)}) %collective-permute-start.53) | collective-permute-done | bytes 614432 | tf_op jit(solution)/shard_map/ppermute | solution.py:1010
  382.6 1.8 collective-permute-done.55.refs_2_
  385.1 1.6 collective-permute-start.56
  386.9 5.2 %collective-permute-done.56.refs_2_ = bf16[2,120,640]{2,1,0:T(8,128)(2,1)S(1)} collective-permute-done((bf16[2,120,640]{2,1,0:T(8,128)(2,1)S(1)}, bf16[2,120,640]{2,1,0:T(8,128)(2,1)S(1)}, u32[]{:S(2)}, u32[]{:S(2)}) %collective-permute-start.56) | collective-permute-done | bytes 307232 | tf_op jit(solution)/shard_map/ppermute | solution.py:1004
  392.7 1.6 collective-permute-start.59
  396.0 2.0 collective-permute-start.57
  398.0 8.8 %collective-permute-done.58.refs_2_ = bf16[240,640]{1,0:T(8,128)(2,1)S(1)} collective-permute-done((bf16[240,640]{1,0:T(8,128)(2,1)S(1)}, bf16[240,640]{1,0:T(8,128)(2,1)S(1)}, u32[]{:S(2)}, u32[]{:S(2)}) %collective-permute-start.58) | collective-permute-done | bytes 307232 | tf_op jit(solution)/shard_map/ppermute | solution.py:1010
  408.4 1.4 collective-permute-start.69
  412.5 1.4 collective-permute-start.62
  413.9 16.9 %collective-permute-done.63.rest_3_ = bf16[240,384]{1,0:T(8,128)(2,1)S(1)} collective-permute-done((bf16[240,384]{1,0:T(8,128)(2,1)S(1)}, bf16[240,384]{1,0:T(8,128)(2,1)S(1)}, u32[]{:S(2)}, u32[]{:S(2)}) %collective-permute-start.63) | collective-permute-done | bytes 184352 | tf_op jit(solution)/shard_map/ppermute | solution.py:1004
  430.8 4.3 collective-permute-start.61
  435.1 1.9 collective-permute-start.60
  437.0 1.6 collective-permute-done.61.rest_1_
  442.6 4.2 lay_both.1
  446.8 2.4 lay.1
  451.5 7.5 %collective-permute-done.60.refs_1_ = bf16[1920,256]{1,0:T(8,128)(2,1)S(1)} collective-permute-done((bf16[1920,256]{1,0:T(8,128)(2,1)S(1)}, bf16[1920,256]{1,0:T(8,128)(2,1)S(1)}, u32[]{:S(2)}, u32[]{:S(2)}) %collective-permute-start.60) | collective-permute-done | bytes 983072 | tf_op jit(solution)/shard_map/ppermute | solution.py:1021
  459.0 1.7 depart.1
  (311 shorter events, 68.2 us)
Async XLA Ops:
  6.0 11.3 %collective-permute-start.1 = (bf16[240,384]{1,0:T(8,128)(2,1)}, bf16[240,384]{1,0:T(8,128)(2,1)S(1)}, u32[]{:S(2)}, u32[]{:S(2)}) collective-permute-start(bf16[240,384]{1,0:T(8,128)(2,1)} %pick_first.1.rest_0_), channel_id=1, source_target_pairs={{0,2},{1,3},{2,0},{3,1},{4,6},{5,7},{6,4},{7,5},{8,10},{9,11},{10,... | collective-permute-start | bytes 552968 | tf_op jit(solution)/shard_map/ppermute | solution.py:1010
  6.4 10.9 %collective-permute-start = (bf16[240,384]{1,0:T(8,128)(2,1)}, bf16[240,384]{1,0:T(8,128)(2,1)S(1)}, u32[]{:S(2)}, u32[]{:S(2)}) collective-permute-start(bf16[240,384]{1,0:T(8,128)(2,1)} %pick_first.1.rest_0_), channel_id=1, source_target_pairs={{0,1},{1,0},{2,3},{3,2},{4,5},{5,4},{6,7},{7,6},{8,9},{9,8},{10,11... | collective-permute-start | bytes 552968 | tf_op jit(solution)/shard_map/ppermute | solution.py:1010
  17.3 6.6 %collective-permute-start.2 = (bf16[240,384]{1,0:T(8,128)(2,1)S(1)}, bf16[240,384]{1,0:T(8,128)(2,1)S(1)}, u32[]{:S(2)}, u32[]{:S(2)}) collective-permute-start(bf16[240,384]{1,0:T(8,128)(2,1)S(1)} %collective-permute-done.1.rest_2_), channel_id=1, source_target_pairs={{0,1},{1,0},{2,3},{3,2},{4,5},{5,4},{6,7},{7,6},{8,9},{9,8},{10,11... | collective-permute-start | bytes 552968 | tf_op jit(solution)/shard_map/ppermute | solution.py:1010
  25.5 19.4 %collective-permute-start.3 = (bf16[960,384]{1,0:T(8,128)(2,1)S(1)}, bf16[960,384]{1,0:T(8,128)(2,1)}, u32[]{:S(2)}, u32[]{:S(2)}) collective-permute-start(bf16[960,384]{1,0:T(8,128)(2,1)S(1)} %bitcast.22), channel_id=1, source_target_pairs={{0,8},{4,20},{8,0},{12,28},{16,24},{20,4},{24,16},{28,12},{1,9},{5... | collective-permute-start | bytes 2211848 | tf_op jit(solution)/shard_map/ppermute | solution.py:1004
  27.1 23.8 %collective-permute-start.4 = (bf16[960,384]{1,0:T(8,128)(2,1)S(1)}, bf16[960,384]{1,0:T(8,128)(2,1)}, u32[]{:S(2)}, u32[]{:S(2)}) collective-permute-start(bf16[960,384]{1,0:T(8,128)(2,1)S(1)} %bitcast.23), channel_id=1, source_target_pairs={{0,16},{4,12},{8,24},{12,4},{16,0},{20,28},{24,8},{28,20},{1,17},{... | collective-permute-start | bytes 2211848 | tf_op jit(solution)/shard_map/ppermute | solution.py:1004
  28.6 22.3 %collective-permute-start.11 = (bf16[368,640]{1,0:T(8,128)(2,1)S(1)}, bf16[368,640]{1,0:T(8,128)(2,1)S(1)}, u32[]{:S(2)}, u32[]{:S(2)}) collective-permute-start(bf16[368,640]{1,0:T(8,128)(2,1)S(1)} %pick.1.rest_4_.rest_0_), channel_id=1, source_target_pairs={{0,2},{1,3},{2,0},{3,1},{4,6},{5,7},{6,4},{7,5},{8,10},{9,11},{10,... | collective-permute-start | bytes 1413128 | tf_op jit(solution)/shard_map/ppermute | solution.py:1010
  28.6 22.3 %collective-permute-start.10 = (bf16[368,640]{1,0:T(8,128)(2,1)S(1)}, bf16[368,640]{1,0:T(8,128)(2,1)S(1)}, u32[]{:S(2)}, u32[]{:S(2)}) collective-permute-start(bf16[368,640]{1,0:T(8,128)(2,1)S(1)} %pick.1.rest_4_.rest_0_), channel_id=1, source_target_pairs={{0,1},{1,0},{2,3},{3,2},{4,5},{5,4},{6,7},{7,6},{8,9},{9,8},{10,11... | collective-permute-start | bytes 1413128 | tf_op jit(solution)/shard_map/ppermute | solution.py:1010
  44.9 18.8 %collective-permute-start.5 = (bf16[960,384]{1,0:T(8,128)(2,1)}, bf16[960,384]{1,0:T(8,128)(2,1)S(1)}, u32[]{:S(2)}, u32[]{:S(2)}) collective-permute-start(bf16[960,384]{1,0:T(8,128)(2,1)} %collective-permute-done.3.refs_1_.rest_1_), channel_id=1, source_target_pairs={{0,16},{4,12},{8,24},{12,4},{16,0},{20,28},{24,8},{28,20},{1,17},{... | collective-permute-start | bytes 2211848 | tf_op jit(solution)/shard_map/ppermute | solution.py:1004
  50.9 12.7 %collective-permute-start.12 = (bf16[368,640]{1,0:T(8,128)(2,1)S(1)}, bf16[368,640]{1,0:T(8,128)(2,1)S(1)}, u32[]{:S(2)}, u32[]{:S(2)}) collective-permute-start(bf16[368,640]{1,0:T(8,128)(2,1)S(1)} %hold.4.rest_2_), channel_id=1, source_target_pairs={{0,1},{1,0},{2,3},{3,2},{4,5},{5,4},{6,7},{7,6},{8,9},{9,8},{10,11... | collective-permute-start | bytes 1413128 | tf_op jit(solution)/shard_map/ppermute | solution.py:1010
  66.7 42.7 %collective-permute-start.16 = (bf16[4,368,640]{2,1,0:T(8,128)(2,1)}, bf16[4,368,640]{2,1,0:T(8,128)(2,1)S(1)}, u32[]{:S(2)}, u32[]{:S(2)}) collective-permute-start(bf16[4,368,640]{2,1,0:T(8,128)(2,1)} %stack.31.rest_8_), channel_id=1, source_target_pairs={{0,16},{4,12},{8,24},{12,4},{16,0},{20,28},{24,8},{28,20},{1,17},{... | collective-permute-start | bytes 5652488 | tf_op jit(solution)/shard_map/ppermute | solution.py:1004
  67.2 42.1 %collective-permute-start.13 = (bf16[4,368,640]{2,1,0:T(8,128)(2,1)}, bf16[4,368,640]{2,1,0:T(8,128)(2,1)}, u32[]{:S(2)}, u32[]{:S(2)}) collective-permute-start(bf16[4,368,640]{2,1,0:T(8,128)(2,1)} %stack.31.rest_8_), channel_id=1, source_target_pairs={{0,8},{4,20},{8,0},{12,28},{16,24},{20,4},{24,16},{28,12},{1,9},{5... | collective-permute-start | bytes 5652488 | tf_op jit(solution)/shard_map/ppermute | solution.py:1004
  67.7 10.3 %collective-permute-start.6 = (bf16[960,384]{1,0:T(8,128)(2,1)S(1)}, bf16[960,384]{1,0:T(8,128)(2,1)S(1)}, u32[]{:S(2)}, u32[]{:S(2)}) collective-permute-start(bf16[960,384]{1,0:T(8,128)(2,1)S(1)} %bitcast.24), channel_id=1, source_target_pairs={{0,4},{4,0},{8,12},{12,8},{16,20},{20,16},{24,28},{28,24},{1,5},{5... | collective-permute-start | bytes 2211848 | tf_op jit(solution)/shard_map/ppermute | solution.py:1004
  67.8 10.2 %collective-permute-start.14 = (bf16[976,256]{1,0:T(8,128)(2,1)S(1)}, bf16[976,256]{1,0:T(8,128)(2,1)S(1)}, u32[]{:S(2)}, u32[]{:S(2)}) collective-permute-start(bf16[976,256]{1,0:T(8,128)(2,1)S(1)} %pad_maximum_fusion), channel_id=1, source_target_pairs={{0,0},{1,4},{2,1},{3,5},{4,2},{5,6},{6,3},{7,7},{8,8},{9,12},{10,9... | collective-permute-start | bytes 1499144 | tf_op jit(solution)/shard_map/ppermute | solution.py:1021
  69.7 12.0 %collective-permute-start.8 = (bf16[960,384]{1,0:T(8,128)(2,1)}, bf16[960,384]{1,0:T(8,128)(2,1)}, u32[]{:S(2)}, u32[]{:S(2)}) collective-permute-start(bf16[960,384]{1,0:T(8,128)(2,1)} %collective-permute-done.4.refs_2_.rest_2_), channel_id=1, source_target_pairs={{0,4},{4,0},{8,12},{12,8},{16,20},{20,16},{24,28},{28,24},{1,5},{5... | collective-permute-start | bytes 2211848 | tf_op jit(solution)/shard_map/ppermute | solution.py:1004
  78.0 3.7 collective-permute-start.7
  89.5 15.9 %collective-permute-start.15 = (bf16[656,256]{1,0:T(8,128)(2,1)}, bf16[656,256]{1,0:T(8,128)(2,1)S(1)}, u32[]{:S(2)}, u32[]{:S(2)}) collective-permute-start(bf16[656,256]{1,0:T(8,128)(2,1)} %get-tuple-element.128.kv2.rest_16_), channel_id=1, source_target_pairs={{0,1},{2,3},{4,5},{6,7},{8,9},{10,11},{12,13},{14,15},{16,17},{18,... | collective-permute-start | bytes 1007624 | tf_op jit(solution)/shard_map/ppermute | solution.py:1043
  109.3 24.1 %collective-permute-start.17 = (bf16[4,368,640]{2,1,0:T(8,128)(2,1)}, bf16[4,368,640]{2,1,0:T(8,128)(2,1)}, u32[]{:S(2)}, u32[]{:S(2)}) collective-permute-start(bf16[4,368,640]{2,1,0:T(8,128)(2,1)} %hold.5.rest_9_), channel_id=1, source_target_pairs={{0,16},{4,12},{8,24},{12,4},{16,0},{20,28},{24,8},{28,20},{1,17},{... | collective-permute-start | bytes 5652488 | tf_op jit(solution)/shard_map/ppermute | solution.py:1004
  110.2 23.3 %collective-permute-start.19 = (bf16[4,368,640]{2,1,0:T(8,128)(2,1)}, bf16[4,368,640]{2,1,0:T(8,128)(2,1)S(1)}, u32[]{:S(2)}, u32[]{:S(2)}) collective-permute-start(bf16[4,368,640]{2,1,0:T(8,128)(2,1)} %stack.31.rest_8_), channel_id=1, source_target_pairs={{0,4},{4,0},{8,12},{12,8},{16,20},{20,16},{24,28},{28,24},{1,5},{5... | collective-permute-start | bytes 5652488 | tf_op jit(solution)/shard_map/ppermute | solution.py:1004
  121.7 13.2 %collective-permute-start.20 = (bf16[4,368,640]{2,1,0:T(8,128)(2,1)}, bf16[4,368,640]{2,1,0:T(8,128)(2,1)}, u32[]{:S(2)}, u32[]{:S(2)}) collective-permute-start(bf16[4,368,640]{2,1,0:T(8,128)(2,1)} %hold.5.rest_9_), channel_id=1, source_target_pairs={{0,4},{4,0},{8,12},{12,8},{16,20},{20,16},{24,28},{28,24},{1,5},{5... | collective-permute-start | bytes 5652488 | tf_op jit(solution)/shard_map/ppermute | solution.py:1004
  122.0 11.5 %collective-permute-start.21 = (bf16[4,368,640]{2,1,0:T(8,128)(2,1)S(1)}, bf16[4,368,640]{2,1,0:T(8,128)(2,1)S(1)}, u32[]{:S(2)}, u32[]{:S(2)}) collective-permute-start(bf16[4,368,640]{2,1,0:T(8,128)(2,1)S(1)} %collective-permute-done.16.refs_2_.rest_10_), channel_id=1, source_target_pairs={{0,4},{4,0},{8,12},{12,8},{16,20},{20,16},{24,28},{28,24},{1,5},{5... | collective-permute-start | bytes 5652488 | tf_op jit(solution)/shard_map/ppermute | solution.py:1004
  133.5 4.2 collective-permute-start.22
  155.6 15.8 %collective-permute-start.29 = (bf16[256,2560]{1,0:T(8,128)(2,1)}, bf16[256,2560]{1,0:T(8,128)(2,1)S(1)}, u32[]{:S(2)}, u32[]{:S(2)}) collective-permute-start(bf16[256,2560]{1,0:T(8,128)(2,1)} %get-tuple-element.137.rest_5_), channel_id=1, source_target_pairs={{0,4},{4,0},{8,12},{12,8},{16,20},{20,16},{24,28},{28,24},{1,5},{5... | collective-permute-start | bytes 3932168 | tf_op jit(solution)/shard_map/ppermute | solution.py:1004
  155.8 12.8 %collective-permute-start.24 = (bf16[656,256]{1,0:T(8,128)(2,1)}, bf16[656,256]{1,0:T(8,128)(2,1)S(1)}, u32[]{:S(2)}, u32[]{:S(2)}) collective-permute-start(bf16[656,256]{1,0:T(8,128)(2,1)} %get-tuple-element.133.kv2.rest_16_), channel_id=1, source_target_pairs={{0,1},{2,3},{4,5},{6,7},{8,9},{10,11},{12,13},{14,15},{16,17},{18,... | collective-permute-start | bytes 1007624 | tf_op jit(solution)/shard_map/ppermute | solution.py:1043
  157.1 12.5 %collective-permute-start.26 = (bf16[256,960]{1,0:T(8,128)(2,1)S(1)}, bf16[256,960]{1,0:T(8,128)(2,1)S(1)}, u32[]{:S(2)}, u32[]{:S(2)}) collective-permute-start(bf16[256,960]{1,0:T(8,128)(2,1)S(1)} %copy-done.68), channel_id=1, source_target_pairs={{0,4},{4,0},{8,12},{12,8},{16,20},{20,16},{24,28},{28,24},{1,5},{5... | collective-permute-start | bytes 1474568 | tf_op jit(solution)/shard_map/ppermute | solution.py:1004
  157.5 26.4 %collective-permute-start.23 = (bf16[960,256]{1,0:T(8,128)(2,1)S(1)}, bf16[960,256]{1,0:T(8,128)(2,1)S(1)}, u32[]{:S(2)}, u32[]{:S(2)}) collective-permute-start(bf16[960,256]{1,0:T(8,128)(2,1)S(1)} %bitcast.39), channel_id=1, source_target_pairs={{0,0},{1,4},{2,1},{3,5},{4,2},{5,6},{6,3},{7,7},{8,8},{9,12},{10,9... | collective-permute-start | bytes 1474568 | tf_op jit(solution)/shard_map/ppermute | solution.py:1021
  159.4 10.3 %collective-permute-start.27 = (bf16[256,960]{1,0:T(8,128)(2,1)}, bf16[256,960]{1,0:T(8,128)(2,1)S(1)}, u32[]{:S(2)}, u32[]{:S(2)}) collective-permute-start(bf16[256,960]{1,0:T(8,128)(2,1)} %get-tuple-element.135.rest_1_), channel_id=1, source_target_pairs={{0,4},{4,0},{8,12},{12,8},{16,20},{20,16},{24,28},{28,24},{1,5},{5... | collective-permute-start | bytes 1474568 | tf_op jit(solution)/shard_map/ppermute | solution.py:1004
  169.7 66.8 %collective-permute-start.35 = (bf16[256,960]{1,0:T(8,128)(2,1)}, bf16[256,960]{1,0:T(8,128)(2,1)}, u32[]{:S(2)}, u32[]{:S(2)}) collective-permute-start(bf16[256,960]{1,0:T(8,128)(2,1)} %get-tuple-element.158.rest_0_), channel_id=1, source_target_pairs={{0,4},{4,0},{8,12},{12,8},{16,20},{20,16},{24,28},{28,24},{1,5},{5... | collective-permute-start | bytes 1474568 | tf_op jit(solution)/shard_map/ppermute | solution.py:1004
  219.9 28.7 %collective-permute-start.34 = (bf16[256,2560]{1,0:T(8,128)(2,1)}, bf16[256,2560]{1,0:T(8,128)(2,1)S(1)}, u32[]{:S(2)}, u32[]{:S(2)}) collective-permute-start(bf16[256,2560]{1,0:T(8,128)(2,1)} %get-tuple-element.157), channel_id=1, source_target_pairs={{0,4},{4,0},{8,12},{12,8},{16,20},{20,16},{24,28},{28,24},{1,5},{5... | collective-permute-start | bytes 3932168 | tf_op jit(solution)/shard_map/ppermute | solution.py:1004
  220.0 28.6 %collective-permute-start.38 = (bf16[256,2560]{1,0:T(8,128)(2,1)S(1)}, bf16[256,2560]{1,0:T(8,128)(2,1)S(1)}, u32[]{:S(2)}, u32[]{:S(2)}) collective-permute-start(bf16[256,2560]{1,0:T(8,128)(2,1)S(1)} %copy-done.71), channel_id=1, source_target_pairs={{0,4},{4,0},{8,12},{12,8},{16,20},{20,16},{24,28},{28,24},{1,5},{5... | collective-permute-start | bytes 3932168 | tf_op jit(solution)/shard_map/ppermute | solution.py:1004
  220.5 17.7 %collective-permute-start.36 = (bf16[256,960]{1,0:T(8,128)(2,1)}, bf16[256,960]{1,0:T(8,128)(2,1)S(1)}, u32[]{:S(2)}, u32[]{:S(2)}) collective-permute-start(bf16[256,960]{1,0:T(8,128)(2,1)} %get-tuple-element.159.rest_0_), channel_id=1, source_target_pairs={{0,4},{4,0},{8,12},{12,8},{16,20},{20,16},{24,28},{28,24},{1,5},{5... | collective-permute-start | bytes 1474568 | tf_op jit(solution)/shard_map/ppermute | solution.py:1004
  236.5 3.0 collective-permute-start.37
  237.8 3.3 collective-permute-start.32
  238.2 2.9 collective-permute-start.33
  239.5 9.1 %collective-permute-start.31 = (bf16[640,256]{1,0:T(8,128)(2,1)S(1)}, bf16[640,256]{1,0:T(8,128)(2,1)S(1)}, u32[]{:S(2)}, u32[]{:S(2)}) collective-permute-start(bf16[640,256]{1,0:T(8,128)(2,1)S(1)} %get-tuple-element.151), channel_id=1, source_target_pairs={{1,0},{3,2},{5,4},{7,6},{9,8},{11,10},{13,12},{15,14},{17,16},{19,... | collective-permute-start | bytes 983048 | tf_op jit(solution)/shard_map/ppermute | solution.py:1052
  271.2 3.3 collective-permute-start.40
  287.1 40.9 %collective-permute-start.46 = (bf16[2,960,640]{2,1,0:T(8,128)(2,1)}, bf16[2,960,640]{2,1,0:T(8,128)(2,1)S(1)}, u32[]{:S(2)}, u32[]{:S(2)}) collective-permute-start(bf16[2,960,640]{2,1,0:T(8,128)(2,1)} %get-tuple-element.192), channel_id=1, source_target_pairs={{0,8},{4,20},{8,0},{12,28},{16,24},{20,4},{24,16},{28,12},{1,9},{5... | collective-permute-start | bytes 7372808 | tf_op jit(solution)/shard_map/ppermute | solution.py:1004
  304.1 7.1 %collective-permute-start.43 = (bf16[256,960]{1,0:T(8,128)(2,1)S(1)}, bf16[256,960]{1,0:T(8,128)(2,1)S(1)}, u32[]{:S(2)}, u32[]{:S(2)}) collective-permute-start(bf16[256,960]{1,0:T(8,128)(2,1)S(1)} %copy-done.75), channel_id=1, source_target_pairs={{0,4},{4,0},{8,12},{12,8},{16,20},{20,16},{24,28},{28,24},{1,5},{5... | collective-permute-start | bytes 1474568 | tf_op jit(solution)/shard_map/ppermute | solution.py:1004
  306.9 13.4 %collective-permute-start.42 = (bf16[640,256]{1,0:T(8,128)(2,1)S(1)}, bf16[640,256]{1,0:T(8,128)(2,1)S(1)}, u32[]{:S(2)}, u32[]{:S(2)}) collective-permute-start(bf16[640,256]{1,0:T(8,128)(2,1)S(1)} %get-tuple-element.175), channel_id=1, source_target_pairs={{1,0},{3,2},{5,4},{7,6},{9,8},{11,10},{13,12},{15,14},{17,16},{19,... | collective-permute-start | bytes 983048 | tf_op jit(solution)/shard_map/ppermute | solution.py:1052
  320.3 29.1 %collective-permute-start.48 = (bf16[2,480,640]{2,1,0:T(8,128)(2,1)}, bf16[2,480,640]{2,1,0:T(8,128)(2,1)}, u32[]{:S(2)}, u32[]{:S(2)}) collective-permute-start(bf16[2,480,640]{2,1,0:T(8,128)(2,1)} %get-tuple-element.196), channel_id=1, source_target_pairs={{0,1},{1,0},{2,3},{3,2},{4,5},{5,4},{6,7},{7,6},{8,9},{9,8},{10,11... | collective-permute-start | bytes 3686408 | tf_op jit(solution)/shard_map/ppermute | solution.py:1010
  332.2 20.2 %collective-permute-start.47 = (bf16[960,640]{1,0:T(8,128)(2,1)}, bf16[960,640]{1,0:T(8,128)(2,1)S(1)}, u32[]{:S(2)}, u32[]{:S(2)}) collective-permute-start(bf16[960,640]{1,0:T(8,128)(2,1)} %get-tuple-element.194), channel_id=1, source_target_pairs={{0,16},{4,12},{8,24},{12,4},{16,0},{20,28},{24,8},{28,20},{1,17},{... | collective-permute-start | bytes 3686408 | tf_op jit(solution)/shard_map/ppermute | solution.py:1004
  344.8 18.1 %collective-permute-start.49 = (bf16[960,384]{1,0:T(8,128)(2,1)}, bf16[960,384]{1,0:T(8,128)(2,1)S(1)}, u32[]{:S(2)}, u32[]{:S(2)}) collective-permute-start(bf16[960,384]{1,0:T(8,128)(2,1)} %get-tuple-element.203), channel_id=1, source_target_pairs={{0,8},{4,20},{8,0},{12,28},{16,24},{20,4},{24,16},{28,12},{1,9},{5... | collective-permute-start | bytes 2211848 | tf_op jit(solution)/shard_map/ppermute | solution.py:1004
  345.3 19.1 %collective-permute-start.50 = (bf16[960,384]{1,0:T(8,128)(2,1)}, bf16[960,384]{1,0:T(8,128)(2,1)S(1)}, u32[]{:S(2)}, u32[]{:S(2)}) collective-permute-start(bf16[960,384]{1,0:T(8,128)(2,1)} %get-tuple-element.204), channel_id=1, source_target_pairs={{0,8},{4,20},{8,0},{12,28},{16,24},{20,4},{24,16},{28,12},{1,9},{5... | collective-permute-start | bytes 2211848 | tf_op jit(solution)/shard_map/ppermute | solution.py:1004
  354.8 24.8 %collective-permute-start.53 = (bf16[2,240,640]{2,1,0:T(8,128)(2,1)}, bf16[2,240,640]{2,1,0:T(8,128)(2,1)}, u32[]{:S(2)}, u32[]{:S(2)}) collective-permute-start(bf16[2,240,640]{2,1,0:T(8,128)(2,1)} %get-tuple-element.210), channel_id=1, source_target_pairs={{0,1},{1,0},{2,3},{3,2},{4,5},{5,4},{6,7},{7,6},{8,9},{9,8},{10,11... | collective-permute-start | bytes 1843208 | tf_op jit(solution)/shard_map/ppermute | solution.py:1010
  355.1 29.4 %collective-permute-start.55 = (bf16[480,640]{1,0:T(8,128)(2,1)}, bf16[480,640]{1,0:T(8,128)(2,1)S(1)}, u32[]{:S(2)}, u32[]{:S(2)}) collective-permute-start(bf16[480,640]{1,0:T(8,128)(2,1)} %get-tuple-element.216), channel_id=1, source_target_pairs={{0,2},{1,3},{2,0},{3,1},{4,6},{5,7},{6,4},{7,5},{8,10},{9,11},{10,... | collective-permute-start | bytes 1843208 | tf_op jit(solution)/shard_map/ppermute | solution.py:1010
  368.2 12.5 %collective-permute-start.51 = (bf16[480,384]{1,0:T(8,128)(2,1)S(1)}, bf16[480,384]{1,0:T(8,128)(2,1)S(1)}, u32[]{:S(2)}, u32[]{:S(2)}) collective-permute-start(bf16[480,384]{1,0:T(8,128)(2,1)S(1)} %get-tuple-element.207), channel_id=1, source_target_pairs={{0,16},{4,12},{8,24},{12,4},{16,0},{20,28},{24,8},{28,20},{1,17},{... | collective-permute-start | bytes 1105928 | tf_op jit(solution)/shard_map/ppermute | solution.py:1004
  369.5 11.3 %collective-permute-start.52 = (bf16[480,384]{1,0:T(8,128)(2,1)S(1)}, bf16[480,384]{1,0:T(8,128)(2,1)S(1)}, u32[]{:S(2)}, u32[]{:S(2)}) collective-permute-start(bf16[480,384]{1,0:T(8,128)(2,1)S(1)} %get-tuple-element.208), channel_id=1, source_target_pairs={{0,16},{4,12},{8,24},{12,4},{16,0},{20,28},{24,8},{28,20},{1,17},{... | collective-permute-start | bytes 1105928 | tf_op jit(solution)/shard_map/ppermute | solution.py:1004
  381.6 13.8 %collective-permute-start.54 = (bf16[2,240,384]{2,1,0:T(8,128)(2,1)S(1)}, bf16[2,240,384]{2,1,0:T(8,128)(2,1)S(1)}, u32[]{:S(2)}, u32[]{:S(2)}) collective-permute-start(bf16[2,240,384]{2,1,0:T(8,128)(2,1)S(1)} %get-tuple-element.214), channel_id=1, source_target_pairs={{0,1},{1,0},{2,3},{3,2},{4,5},{5,4},{6,7},{7,6},{8,9},{9,8},{10,11... | collective-permute-start | bytes 1105928 | tf_op jit(solution)/shard_map/ppermute | solution.py:1010
  385.1 6.9 %collective-permute-start.56 = (bf16[2,120,640]{2,1,0:T(8,128)(2,1)S(1)}, bf16[2,120,640]{2,1,0:T(8,128)(2,1)S(1)}, u32[]{:S(2)}, u32[]{:S(2)}) collective-permute-start(bf16[2,120,640]{2,1,0:T(8,128)(2,1)S(1)} %get-tuple-element.219), channel_id=1, source_target_pairs={{0,8},{4,20},{8,0},{12,28},{16,24},{20,4},{24,16},{28,12},{1,9},{5... | collective-permute-start | bytes 921608 | tf_op jit(solution)/shard_map/ppermute | solution.py:1004
  386.7 20.1 %collective-permute-start.58 = (bf16[240,640]{1,0:T(8,128)(2,1)S(1)}, bf16[240,640]{1,0:T(8,128)(2,1)S(1)}, u32[]{:S(2)}, u32[]{:S(2)}) collective-permute-start(bf16[240,640]{1,0:T(8,128)(2,1)S(1)} %get-tuple-element.225), channel_id=1, source_target_pairs={{0,2},{1,3},{2,0},{3,1},{4,6},{5,7},{6,4},{7,5},{8,10},{9,11},{10,... | collective-permute-start | bytes 921608 | tf_op jit(solution)/shard_map/ppermute | solution.py:1010
  392.7 14.2 %collective-permute-start.59 = (bf16[120,640]{1,0:T(8,128)(2,1)S(1)}, bf16[120,640]{1,0:T(8,128)(2,1)S(1)}, u32[]{:S(2)}, u32[]{:S(2)}) collective-permute-start(bf16[120,640]{1,0:T(8,128)(2,1)S(1)} %get-tuple-element.227), channel_id=1, source_target_pairs={{0,16},{4,12},{8,24},{12,4},{16,0},{20,28},{24,8},{28,20},{1,17},{... | collective-permute-start | bytes 460808 | tf_op jit(solution)/shard_map/ppermute | solution.py:1004
  396.0 15.0 %collective-permute-start.57 = (bf16[240,384]{1,0:T(8,128)(2,1)S(1)}, bf16[240,384]{1,0:T(8,128)(2,1)S(1)}, u32[]{:S(2)}, u32[]{:S(2)}) collective-permute-start(bf16[240,384]{1,0:T(8,128)(2,1)S(1)} %get-tuple-element.223), channel_id=1, source_target_pairs={{0,2},{1,3},{2,0},{3,1},{4,6},{5,7},{6,4},{7,5},{8,10},{9,11},{10,... | collective-permute-start | bytes 552968 | tf_op jit(solution)/shard_map/ppermute | solution.py:1010
  407.5 31.1 %collective-permute-start.70 = (bf16[360,640]{1,0:T(8,128)(2,1)S(1)}, bf16[360,640]{1,0:T(8,128)(2,1)S(1)}, u32[]{:S(2)}, u32[]{:S(2)}) collective-permute-start(bf16[360,640]{1,0:T(8,128)(2,1)S(1)} %get-tuple-element.232.refs_1_), channel_id=1, source_target_pairs={{0,24},{4,28},{8,16},{12,20},{16,8},{20,12},{24,0},{28,4},{1,25},{... | collective-permute-start | bytes 1382408 | tf_op jit(solution)/shard_map/ppermute | solution.py:1004
  408.4 30.8 %collective-permute-start.69 = (bf16[360,640]{1,0:T(8,128)(2,1)S(1)}, bf16[360,640]{1,0:T(8,128)(2,1)S(1)}, u32[]{:S(2)}, u32[]{:S(2)}) collective-permute-start(bf16[360,640]{1,0:T(8,128)(2,1)S(1)} %get-tuple-element.232.refs_1_), channel_id=1, source_target_pairs={{0,16},{4,12},{8,24},{12,4},{16,0},{20,28},{24,8},{28,20},{1,17},{... | collective-permute-start | bytes 1382408 | tf_op jit(solution)/shard_map/ppermute | solution.py:1004
  409.8 29.4 %collective-permute-start.68 = (bf16[360,640]{1,0:T(8,128)(2,1)S(1)}, bf16[360,640]{1,0:T(8,128)(2,1)S(1)}, u32[]{:S(2)}, u32[]{:S(2)}) collective-permute-start(bf16[360,640]{1,0:T(8,128)(2,1)S(1)} %get-tuple-element.232.refs_1_), channel_id=1, source_target_pairs={{0,8},{4,20},{8,0},{12,28},{16,24},{20,4},{24,16},{28,12},{1,9},{5... | collective-permute-start | bytes 1382408 | tf_op jit(solution)/shard_map/ppermute | solution.py:1004
  411.6 19.2 %collective-permute-start.63 = (bf16[240,384]{1,0:T(8,128)(2,1)S(1)}, bf16[240,384]{1,0:T(8,128)(2,1)S(1)}, u32[]{:S(2)}, u32[]{:S(2)}) collective-permute-start(bf16[240,384]{1,0:T(8,128)(2,1)S(1)} %get-tuple-element.231.rest_0_), channel_id=1, source_target_pairs={{0,24},{4,28},{8,16},{12,20},{16,8},{20,12},{24,0},{28,4},{1,25},{... | collective-permute-start | bytes 552968 | tf_op jit(solution)/shard_map/ppermute | solution.py:1004
  412.5 22.6 %collective-permute-start.62 = (bf16[240,384]{1,0:T(8,128)(2,1)S(1)}, bf16[240,384]{1,0:T(8,128)(2,1)S(1)}, u32[]{:S(2)}, u32[]{:S(2)}) collective-permute-start(bf16[240,384]{1,0:T(8,128)(2,1)S(1)} %get-tuple-element.231.rest_0_), channel_id=1, source_target_pairs={{0,16},{4,12},{8,24},{12,4},{16,0},{20,28},{24,8},{28,20},{1,17},{... | collective-permute-start | bytes 552968 | tf_op jit(solution)/shard_map/ppermute | solution.py:1004
  430.8 7.8 %collective-permute-start.61 = (bf16[240,384]{1,0:T(8,128)(2,1)S(1)}, bf16[240,384]{1,0:T(8,128)(2,1)S(1)}, u32[]{:S(2)}, u32[]{:S(2)}) collective-permute-start(bf16[240,384]{1,0:T(8,128)(2,1)S(1)} %get-tuple-element.231.rest_0_), channel_id=1, source_target_pairs={{0,8},{4,20},{8,0},{12,28},{16,24},{20,4},{24,16},{28,12},{1,9},{5... | collective-permute-start | bytes 552968 | tf_op jit(solution)/shard_map/ppermute | solution.py:1004
  435.1 23.9 %collective-permute-start.60 = (bf16[1920,256]{1,0:T(8,128)(2,1)S(1)}, bf16[1920,256]{1,0:T(8,128)(2,1)S(1)}, u32[]{:S(2)}, u32[]{:S(2)}) collective-permute-start(bf16[1920,256]{1,0:T(8,128)(2,1)S(1)} %hold.7), channel_id=1, source_target_pairs={{0,0},{4,1},{1,2},{5,3},{2,4},{6,5},{3,6},{7,7},{8,8},{12,9},{9,10... | collective-permute-start | bytes 2949128 | tf_op jit(solution)/shard_map/ppermute | solution.py:1021
  439.1 2.6 collective-permute-start.73
  439.2 3.2 collective-permute-start.72
  440.4 6.4 %collective-permute-start.64 = (bf16[240,384]{1,0:T(8,128)(2,1)S(1)}, bf16[240,384]{1,0:T(8,128)(2,1)S(1)}, u32[]{:S(2)}, u32[]{:S(2)}) collective-permute-start(bf16[240,384]{1,0:T(8,128)(2,1)S(1)} %get-tuple-element.231.rest_0_), channel_id=1, source_target_pairs={{0,4},{4,0},{8,12},{12,8},{16,20},{20,16},{24,28},{28,24},{1,5},{5... | collective-permute-start | bytes 552968 | tf_op jit(solution)/shard_map/ppermute | solution.py:1004
  441.1 5.7 %collective-permute-start.67 = (bf16[240,384]{1,0:T(8,128)(2,1)S(1)}, bf16[240,384]{1,0:T(8,128)(2,1)S(1)}, u32[]{:S(2)}, u32[]{:S(2)}) collective-permute-start(bf16[240,384]{1,0:T(8,128)(2,1)S(1)} %collective-permute-done.63.rest_3_), channel_id=1, source_target_pairs={{0,4},{4,0},{8,12},{12,8},{16,20},{20,16},{24,28},{28,24},{1,5},{5... | collective-permute-start | bytes 552968 | tf_op jit(solution)/shard_map/ppermute | solution.py:1004
  441.8 5.0 %collective-permute-start.66 = (bf16[240,384]{1,0:T(8,128)(2,1)S(1)}, bf16[240,384]{1,0:T(8,128)(2,1)S(1)}, u32[]{:S(2)}, u32[]{:S(2)}) collective-permute-start(bf16[240,384]{1,0:T(8,128)(2,1)S(1)} %collective-permute-done.62.rest_2_), channel_id=1, source_target_pairs={{0,4},{4,0},{8,12},{12,8},{16,20},{20,16},{24,28},{28,24},{1,5},{5... | collective-permute-start | bytes 552968 | tf_op jit(solution)/shard_map/ppermute | solution.py:1004
  442.4 4.4 collective-permute-start.65
  (96 other events, 804.6 us)

commit v19 on v18

--- a/solution.py
+++ b/solution.py
@@ -1149,16 +1149,16 @@
     got_d = flip(send_d, SIDE, BACK)
     later_d, own_d, done = sum_first(sc, [keep_d], [got_d], [done])
     more_d = flip(later_d, BACK, SIDE)
-    send_a, ring_a, done = sum_third(sc, ring_a, got_a, [done])
+    send_a, ring_a, first = sum_third(sc, ring_a, got_a, [done])
     got_a = flip_z(send_a, 2)
-    piece_b, done = sum_both(sc, ring_b, got_b, own_d, more_d, [done])
+    piece_b, done = sum_both(sc, ring_b, got_b, own_d, more_d, [first])
     all_b = spread(over_groups(piece_b))
-    piece_a, done = sum_two(sc, ring_a, got_a, [done])
+    piece_a, done = sum_two(sc, ring_a, got_a, [done, all_b[1]])
     all_a = spread(over_groups(piece_a))
-    leaving = home_to_work(hold(leaving, [done]), back=True)
+    leaving = home_to_work(hold(leaving, [first]), back=True)
+    output, grad_tokens, done = depart(sc, leaving, [done])
     grad_gate, grad_up, grad_down_, done = lay_both(sc, all_b, across(all_b), ring_a.shape[0], [done])
     grad_query, grad_key, grad_value, grad_out, dgains, done = lay(sc, all_a, across(all_a), (width, KVW, KVW, width), [done])
-    output, grad_tokens, _ = depart(sc, leaving, [done])
     output, grad_tokens = output.T, grad_tokens.T
     return (output[None], grad_tokens[None], dgains[0], grad_query, grad_key, grad_value, grad_out, dgains[1], grad_gate, grad_up, grad_down_.T)
 

time: 466 us -> 465 us (level)
  the two profiles are of different devices: /device:TPU:24 before, /device:TPU:0 now
where the time goes in v19:
time: 465 us; the launch traced here: 460 us
  Pallas kernels  200 us (43%)
  waiting for transfers between devices  122 us (26%)
  starting transfers between devices  103 us (22%)
  local copies, waits for them, and re-layouts  29.7 us (6%)
    ppermute x56, starting transfers between devices, flip(): lax.ppermute(value, 'dp', [(i, i ^ bits[i & 1]) for i in range(count)])  56.6 us
    ppermute x56, waiting for transfers between devices, flip(): lax.ppermute(value, 'dp', [(i, i ^ bits[i & 1]) for i in range(count)])  53.6 us
    ppermute x12, waiting for transfers between devices, flip_z(): return lax.ppermute(value, ('dp', 'fsdp'), pairs)  48.3 us
    pallas_call x3, Pallas kernels, back(): pl.pallas_call(functools.partial(back_kernel, start, end, len(after)), ou...  45.7 us
    pallas_call x2, Pallas kernels, post(): pl.pallas_call(functools.partial(post_kernel, last, len(after)), out_shap...  34.6 us
    ppermute x12, starting transfers between devices, flip_z(): return lax.ppermute(value, ('dp', 'fsdp'), pairs)  28.6 us
    unnamed x172, local copies, waits for them, and re-layouts  27.1 us
    pallas_call x2, Pallas kernels, attend_back(): pl.pallas_call(attend_back_kernel, out_shape=(shape((3, n, PIECE), bf16),...  25.3 us
  transfers between devices with their start and end apart: 75, of which 30 were waited for; matrix products, arithmetic and copies ran while one was open for 1% of the time, Pallas kernels for 30%

profile of v19, /device:TPU:0, one launch (start us, length us, event | category | flops | bytes accessed | tf_op | source)
XLA Modules:
  0.0 459.6 jit_solution(17083123302537095523)
XLA Ops:
  3.3 2.7 pick_first.1.rest_0_
  6.0 4.1 collective-permute-start.1
  10.1 1.6 collective-permute-start
  11.7 7.3 %collective-permute-done.1.rest_2_ = bf16[240,384]{1,0:T(8,128)(2,1)S(1)} collective-permute-done((bf16[240,384]{1,0:T(8,128)(2,1)}, bf16[240,384]{1,0:T(8,128)(2,1)S(1)}, u32[]{:S(2)}, u32[]{:S(2)}) %collective-permute-start.1) | collective-permute-done | bytes 184352 | tf_op jit(solution)/shard_map/ppermute | solution.py:1010
  23.1 1.5 collective-permute-done.2.rest_3_
  24.6 1.5 stack.30.first_ref
  26.2 1.5 collective-permute-start.3
  27.7 1.5 collective-permute-start.4
  29.3 3.2 collective-permute-start.11
  32.5 1.7 collective-permute-start.10
  34.2 11.5 %collective-permute-done.3.refs_1_.rest_1_ = bf16[960,384]{1,0:T(8,128)(2,1)} collective-permute-done((bf16[960,384]{1,0:T(8,128)(2,1)S(1)}, bf16[960,384]{1,0:T(8,128)(2,1)}, u32[]{:S(2)}, u32[]{:S(2)}) %collective-permute-start.3) | collective-permute-done | bytes 737312 | tf_op jit(solution)/shard_map/ppermute | solution.py:1004
  45.8 6.8 %collective-permute-done.11.refs_0_ = bf16[368,640]{1,0:T(8,128)(2,1)S(1)} collective-permute-done((bf16[368,640]{1,0:T(8,128)(2,1)S(1)}, bf16[368,640]{1,0:T(8,128)(2,1)S(1)}, u32[]{:S(2)}, u32[]{:S(2)}) %collective-permute-start.11) | collective-permute-done | bytes 471072 | tf_op jit(solution)/shard_map/ppermute | solution.py:1010
  54.3 10.0 %collective-permute-done.12.rest_3_ = bf16[368,640]{1,0:T(8,128)(2,1)S(1)} collective-permute-done((bf16[368,640]{1,0:T(8,128)(2,1)S(1)}, bf16[368,640]{1,0:T(8,128)(2,1)S(1)}, u32[]{:S(2)}, u32[]{:S(2)}) %collective-permute-start.12) | collective-permute-done | bytes 471072 | tf_op jit(solution)/shard_map/ppermute | solution.py:1010
  64.4 3.0 stack.31.rest_8_
  69.2 4.6 collective-permute-start.8
  73.8 5.9 %collective-permute-start.7 = (bf16[960,384]{1,0:T(8,128)(2,1)}, bf16[960,384]{1,0:T(8,128)(2,1)}, u32[]{:S(2)}, u32[]{:S(2)}) collective-permute-start(bf16[960,384]{1,0:T(8,128)(2,1)} %collective-permute-done.3.refs_1_.rest_1_), channel_id=1, source_target_pairs={{0,4},{4,0},{8,12},{12,8},{16,20},{20,16},{24,28},{28,24},{1,5},{5... | collective-permute-start | bytes 2211848 | tf_op jit(solution)/shard_map/ppermute | solution.py:1004
  83.3 7.5 %pre.1 = (bf16[256,960]{1,0:T(8,128)(2,1)}, bf16[256,960]{1,0:T(8,128)(2,1)}, bf16[960,256]{1,0:T(8,128)(2,1)}, bf16[656,256]{1,0:T(8,128)(2,1)}) custom-call(s32[3]{0:T(128)} %pad_add_fusion.sc.refs_0_, bf16[976,256]{1,0:T(8,128)(2,1)} %copy-done.77, f32[1,960]{1,0:T(1,128)} %get-tuple-element.257.gain_ref.gain_a.rest_22_.rest_14_, ...), custom_call_target="tpu_custom_call" | custom-call | flops 1024 | bytes 1024 | tf_op jit(solution)/shard_map/pre/pallas_call | solution.py:138
  90.8 9.3 %collective-permute-start.15 = (bf16[656,256]{1,0:T(8,128)(2,1)}, bf16[656,256]{1,0:T(8,128)(2,1)S(1)}, u32[]{:S(2)}, u32[]{:S(2)}) collective-permute-start(bf16[656,256]{1,0:T(8,128)(2,1)} %get-tuple-element.128.kv2.rest_16_), channel_id=1, source_target_pairs={{0,1},{2,3},{4,5},{6,7},{8,9},{10,11},{12,13},{14,15},{16,17},{18,... | collective-permute-start | bytes 1007624 | tf_op jit(solution)/shard_map/ppermute | solution.py:1043
  100.1 7.8 %collective-permute-done.15.refs_1_.kv0 = bf16[656,256]{1,0:T(8,128)(2,1)S(1)} collective-permute-done((bf16[656,256]{1,0:T(8,128)(2,1)}, bf16[656,256]{1,0:T(8,128)(2,1)S(1)}, u32[]{:S(2)}, u32[]{:S(2)}) %collective-permute-start.15) | collective-permute-done | bytes 335904 | tf_op jit(solution)/shard_map/ppermute | solution.py:1043
  110.9 10.1 %attend.2 = (bf16[960,256]{1,0:T(8,128)(2,1)S(1)}, f32[15,256]{1,0:T(8,128)S(1)}) custom-call(bf16[960,256]{1,0:T(8,128)(2,1)S(1)} %copy-done.22, bf16[656,256]{1,0:T(8,128)(2,1)S(1)} %collective-permute-done.15.refs_1_.kv0, bf16[656,256]{1,0:T(8,128)(2,1)S(1)} %collective-permute-done.18.kv1, bf16[656,256]{1,0:T(8,128)(2,1)S(1)} %copy-done.5), custom_call_target="tpu_custom_call" | custom-call | flops 1024 | bytes 1024 | tf_op jit(solution)/shard_map/attend/pallas_call | solution.py:191
  121.6 11.2 %collective-permute-done.17.refs_0_ = bf16[4,368,640]{2,1,0:T(8,128)(2,1)} collective-permute-done((bf16[4,368,640]{2,1,0:T(8,128)(2,1)}, bf16[4,368,640]{2,1,0:T(8,128)(2,1)}, u32[]{:S(2)}, u32[]{:S(2)}) %collective-permute-start.17) | collective-permute-done | bytes 1884192 | tf_op jit(solution)/shard_map/ppermute | solution.py:1004
  134.2 2.8 collective-permute-done.22.rest_15_
  137.0 17.9 %post.2 = (bf16[256,960]{1,0:T(8,128)(2,1)}, f32[256,960]{1,0:T(8,128)}, bf16[256,960]{1,0:T(8,128)(2,1)}, bf16[256,2560]{1,0:T(8,128)(2,1)}, bf16[256,2560]{1,0...) custom-call(s32[3]{0:T(128)} %pad_add_fusion.sc.refs_0_, ...), custom_call_target="tpu_custom_call" | custom-call | flops 1024 | bytes 1024 | tf_op jit(solution)/shard_map/post/pallas_call | solution.py:358
  155.1 3.7 collective-permute-start.24
  159.6 5.9 %collective-permute-start.27 = (bf16[256,960]{1,0:T(8,128)(2,1)}, bf16[256,960]{1,0:T(8,128)(2,1)S(1)}, u32[]{:S(2)}, u32[]{:S(2)}) collective-permute-start(bf16[256,960]{1,0:T(8,128)(2,1)} %get-tuple-element.135.rest_1_), channel_id=1, source_target_pairs={{0,4},{4,0},{8,12},{12,8},{16,20},{20,16},{24,28},{28,24},{1,5},{5... | collective-permute-start | bytes 1474568 | tf_op jit(solution)/shard_map/ppermute | solution.py:1004
  165.6 1.7 collective-permute-done.24.kv0
  171.3 10.5 %attend.3 = (bf16[960,256]{1,0:T(8,128)(2,1)S(1)}, f32[15,256]{1,0:T(8,128)S(1)}) custom-call(bf16[960,256]{1,0:T(8,128)(2,1)S(1)} %copy-done.23, bf16[656,256]{1,0:T(8,128)(2,1)S(1)} %collective-permute-done.24.kv0, bf16[656,256]{1,0:T(8,128)(2,1)S(1)} %collective-permute-done.25.kv1, bf16[656,256]{1,0:T(8,128)(2,1)S(1)} %copy-done.3, ...), custom_call_target="tpu_custom_call" | custom-call | flops 1024 | bytes 1024 | tf_op jit(solution)/shard_map/attend/pallas_call | solution.py:191
  183.4 16.7 %post.3 = (bf16[256,960]{1,0:T(8,128)(2,1)}, f32[256,960]{1,0:T(8,128)}, bf16[256,960]{1,0:T(8,128)(2,1)}, bf16[256,2560]{1,0:T(8,128)(2,1)}, bf16[256,2560]{1,0...) custom-call(s32[3]{0:T(128)} %pad_add_fusion.sc.refs_0_, bf16[960,256]{1,0:T(8,128)(2,1)} %copy-done.48, ...), custom_call_target="tpu_custom_call" | custom-call | flops 1024 | bytes 1024 | tf_op jit(solution)/shard_map/post/pallas_call | solution.py:358
  200.2 18.4 %back_start.1 = (bf16[256,960]{1,0:T(8,128)(2,1)}, bf16[256,2560]{1,0:T(8,128)(2,1)}, bf16[256,2560]{1,0:T(8,128)(2,1)}, f32[256,960]{1,0:T(8,128)}, bf16[3,256,...) custom-call(s32[3]{0:T(128)} %pad_add_fusion.sc.refs_0_, bf16[960,384]{1,0:T(8,128)(2,1)} %bitcast.28, ...), custom_call_target="tpu_custom_call" | custom-call | flops 1024 | bytes 1024 | tf_op jit(solution)/shard_map/back_start/pallas_call | solution.py:539
  221.3 12.6 %attend_back.2 = (bf16[3,256,384]{2,1,0:T(8,128)(2,1)S(1)}, bf16[3,256,384]{2,1,0:T(8,128)(2,1)S(1)}, f32[640,256]{1,0:T(8,128)S(1)}, bf16[640,256]{1,0:T(8,128)(2,1)S(1)}, f32[640,256]{1,0:T(8,128)S(1)}) custom-call(s32[3]{0:T(128)S(1)} %copy-done.41, bf16[3,256,384]{2,1,0:T(8,128)(2,1)S(1)} %copy-done.8, bf16[960,256]{1,0:T(8,128)(2,1)S(1)} %copy-done.23, ...), custom_call_target="tpu_custom_call" | custom-call | flops 1024 | bytes 1024 | tf_op jit(solution)/shard_map/attend_back/pallas_call | solution.py:244
  239.6 10.6 %collective-permute-done.31.rest_20_ = bf16[640,256]{1,0:T(8,128)(2,1)S(1)} collective-permute-done((bf16[640,256]{1,0:T(8,128)(2,1)S(1)}, bf16[640,256]{1,0:T(8,128)(2,1)S(1)}, u32[]{:S(2)}, u32[]{:S(2)}) %collective-permute-start.31) | collective-permute-done | bytes 327712 | tf_op jit(solution)/shard_map/ppermute | solution.py:1052
  252.3 20.4 %back_join.1 = (bf16[256,384]{1,0:T(8,128)(2,1)}, bf16[256,384]{1,0:T(8,128)(2,1)}, bf16[256,384]{1,0:T(8,128)(2,1)}, f32[1,960]{1,0:T(1,128)}, bf16[256,960]{1,...) custom-call(s32[3]{0:T(128)} %pad_add_fusion.sc.refs_0_, ...), custom_call_target="tpu_custom_call" | custom-call | flops 1024 | bytes 1024 | tf_op jit(solution)/shard_map/back_join/pallas_call | solution.py:539
  272.8 3.2 collective-permute-done.40.rest_7_
  277.1 11.5 %grad_ffn.1 = (bf16[2,960,640]{2,1,0:T(8,128)(2,1)}, bf16[2,960,640]{2,1,0:T(8,128)(2,1)}, f32[8,128]{1,0:T(8,128)}) custom-call(s32[3]{0:T(128)} %pad_add_fusion.sc.refs_0_, bf16[256,960]{1,0:T(8,128)(2,1)} %get-tuple-element.159.rest_0_, bf16[256,960]{1,0:T(8,128)(2,1)} %get-tuple-element.135.rest_1_, bf16[256,960]{1,0:T(8,128)(2,1)} %copy-done.67, ...), custom_call_target="tpu_custom_call" | custom-call | flops 1024 | bytes 1024 | tf_op jit(solution)/shard_map/grad_ffn/pallas_call | solution.py:581
  291.2 12.6 %attend_back.3 = (bf16[3,256,384]{2,1,0:T(8,128)(2,1)S(1)}, bf16[3,256,384]{2,1,0:T(8,128)(2,1)S(1)}, f32[640,256]{1,0:T(8,128)S(1)}, bf16[640,256]{1,0:T(8,128)(2,1)S(1)}, f32[640,256]{1,0:T(8,128)S(1)}) custom-call(s32[3]{0:T(128)S(1)} %copy-done.42, bf16[3,256,384]{2,1,0:T(8,128)(2,1)S(1)} %copy-done.9, bf16[960,256]{1,0:T(8,128)(2,1)S(1)} %copy-done.22, ...), custom_call_target="tpu_custom_call" | custom-call | flops 1024 | bytes 1024 | tf_op jit(solution)/shard_map/attend_back/pallas_call | solution.py:244
  310.5 8.2 %grad_down.1 = (bf16[2,480,640]{2,1,0:T(8,128)(2,1)}, bf16[2,480,640]{2,1,0:T(8,128)(2,1)}, f32[8,128]{1,0:T(8,128)}) custom-call(s32[3]{0:T(128)} %pad_add_fusion.sc.refs_0_, bf16[256,960]{1,0:T(8,128)(2,1)} %get-tuple-element.156.rest_0_, bf16[256,960]{1,0:T(8,128)(2,1)} %get-tuple-element.177.rest_1_, bf16[256,960]{1,0:T(8,128)(2,1)} %copy-done.66, ...), custom_call_target="tpu_custom_call" | custom-call | flops 1024 | bytes 1024 | tf_op jit(solution)/shard_map/grad_down/pallas_call | solution.py:613
  318.7 2.7 collective-permute-start.48
  322.1 7.0 %back_end.1 = (bf16[256,384]{1,0:T(8,128)(2,1)}, bf16[256,384]{1,0:T(8,128)(2,1)}, bf16[256,384]{1,0:T(8,128)(2,1)}, f32[1,960]{1,0:T(1,128)}, bf16[1920,256]{1,0:T(8,128)(2,1)}) custom-call(s32[3]{0:T(128)} %pad_add_fusion.sc.refs_0_, bf16[960,384]{1,0:T(8,128)(2,1)} %bitcast.30, bf16[960,384]{1,0:T(8,128)(2,1)} %collective-permute-done.3.refs_1_.rest_1_, ...), custom_call_target="tpu_custom_call" | custom-call | flops 1024 | bytes 1024 | tf_op jit(solution)/shard_map/back_end/pallas_call | solution.py:539
  329.8 2.0 sum_first.3
  333.2 1.6 collective-permute-start.47
  337.8 8.1 %grad_attention.2 = (bf16[960,384]{1,0:T(8,128)(2,1)}, bf16[960,384]{1,0:T(8,128)(2,1)}, f32[8,128]{1,0:T(8,128)}) custom-call(s32[3]{0:T(128)} %pad_add_fusion.sc.refs_0_, bf16[256,960]{1,0:T(8,128)(2,1)} %get-tuple-element.158.rest_0_, bf16[256,960]{1,0:T(8,128)(2,1)} %get-tuple-element.134.rest_1_, ...), custom_call_target="tpu_custom_call" | custom-call | flops 1024 | bytes 1024 | tf_op jit(solution)/shard_map/grad_attention/pallas_call | solution.py:664
  346.4 1.6 collective-permute-start.50
  349.4 2.3 sum_third.3
  351.7 1.8 sum_second.2
  354.1 1.7 collective-permute-start.53
  355.8 4.5 collective-permute-start.55
  360.4 7.8 %grad_attention.3 = (bf16[960,384]{1,0:T(8,128)(2,1)}, bf16[960,384]{1,0:T(8,128)(2,1)}, f32[8,128]{1,0:T(8,128)}) custom-call(s32[3]{0:T(128)} %pad_add_fusion.sc.refs_0_, bf16[256,960]{1,0:T(8,128)(2,1)} %get-tuple-element.158.rest_0_, bf16[256,960]{1,0:T(8,128)(2,1)} %get-tuple-element.134.rest_1_, ...), custom_call_target="tpu_custom_call" | custom-call | flops 1024 | bytes 1024 | tf_op jit(solution)/shard_map/grad_attention/pallas_call | solution.py:664
  374.1 8.7 %collective-permute-done.53.refs_2_ = bf16[2,240,640]{2,1,0:T(8,128)(2,1)} collective-permute-done((bf16[2,240,640]{2,1,0:T(8,128)(2,1)}, bf16[2,240,640]{2,1,0:T(8,128)(2,1)}, u32[]{:S(2)}, u32[]{:S(2)}) %collective-permute-start.53) | collective-permute-done | bytes 614432 | tf_op jit(solution)/shard_map/ppermute | solution.py:1010
  385.5 1.6 collective-permute-start.56
  387.1 2.4 collective-permute-start.54
  389.6 2.7 collective-permute-start.59
  393.1 1.6 collective-permute-start.60
  394.6 8.1 %collective-permute-done.54.refs_2_ = bf16[2,240,384]{2,1,0:T(8,128)(2,1)S(1)} collective-permute-done((bf16[2,240,384]{2,1,0:T(8,128)(2,1)S(1)}, bf16[2,240,384]{2,1,0:T(8,128)(2,1)S(1)}, u32[]{:S(2)}, u32[]{:S(2)}) %collective-permute-start.54) | collective-permute-done | bytes 368672 | tf_op jit(solution)/shard_map/ppermute | solution.py:1010
  403.3 1.8 collective-permute-start.58
  406.5 1.5 collective-permute-start.61
  410.1 4.8 %collective-permute-done.58.refs_2_ = bf16[240,384]{1,0:T(8,128)(2,1)S(1)} collective-permute-done((bf16[240,384]{1,0:T(8,128)(2,1)S(1)}, bf16[240,384]{1,0:T(8,128)(2,1)S(1)}, u32[]{:S(2)}, u32[]{:S(2)}) %collective-permute-start.58) | collective-permute-done | bytes 184352 | tf_op jit(solution)/shard_map/ppermute | solution.py:1010
  417.9 8.3 %collective-permute-done.70.refs_4_ = bf16[360,640]{1,0:T(8,128)(2,1)S(1)} collective-permute-done((bf16[360,640]{1,0:T(8,128)(2,1)S(1)}, bf16[360,640]{1,0:T(8,128)(2,1)S(1)}, u32[]{:S(2)}, u32[]{:S(2)}) %collective-permute-start.70) | collective-permute-done | bytes 460832 | tf_op jit(solution)/shard_map/ppermute | solution.py:1004
  426.2 10.0 %collective-permute-start.74 = (bf16[360,640]{1,0:T(8,128)(2,1)S(1)}, bf16[360,640]{1,0:T(8,128)(2,1)S(1)}, u32[]{:S(2)}, u32[]{:S(2)}) collective-permute-start(bf16[360,640]{1,0:T(8,128)(2,1)S(1)} %collective-permute-done.70.refs_4_), channel_id=1, source_target_pairs={{0,4},{4,0},{8,12},{12,8},{16,20},{20,16},{24,28},{28,24},{1,5},{5... | collective-permute-start | bytes 1382408 | tf_op jit(solution)/shard_map/ppermute | solution.py:1004
  436.9 3.1 collective-permute-start.72
  440.0 2.1 collective-permute-done.63.rest_2_
  443.1 4.6 collective-permute-done.62.rest_1_
  448.7 1.7 depart.1
  450.4 4.2 lay_both.1
  454.7 2.4 lay.1
  (311 shorter events, 76.0 us)
Async XLA Ops:
  6.0 13.0 %collective-permute-start.1 = (bf16[240,384]{1,0:T(8,128)(2,1)}, bf16[240,384]{1,0:T(8,128)(2,1)S(1)}, u32[]{:S(2)}, u32[]{:S(2)}) collective-permute-start(bf16[240,384]{1,0:T(8,128)(2,1)} %pick_first.1.rest_0_), channel_id=1, source_target_pairs={{0,2},{1,3},{2,0},{3,1},{4,6},{5,7},{6,4},{7,5},{8,10},{9,11},{10,... | collective-permute-start | bytes 552968 | tf_op jit(solution)/shard_map/ppermute | solution.py:1010
  10.1 9.6 %collective-permute-start = (bf16[240,384]{1,0:T(8,128)(2,1)}, bf16[240,384]{1,0:T(8,128)(2,1)S(1)}, u32[]{:S(2)}, u32[]{:S(2)}) collective-permute-start(bf16[240,384]{1,0:T(8,128)(2,1)} %pick_first.1.rest_0_), channel_id=1, source_target_pairs={{0,1},{1,0},{2,3},{3,2},{4,5},{5,4},{6,7},{7,6},{8,9},{9,8},{10,11... | collective-permute-start | bytes 552968 | tf_op jit(solution)/shard_map/ppermute | solution.py:1010
  19.0 5.7 %collective-permute-start.2 = (bf16[240,384]{1,0:T(8,128)(2,1)S(1)}, bf16[240,384]{1,0:T(8,128)(2,1)S(1)}, u32[]{:S(2)}, u32[]{:S(2)}) collective-permute-start(bf16[240,384]{1,0:T(8,128)(2,1)S(1)} %collective-permute-done.1.rest_2_), channel_id=1, source_target_pairs={{0,1},{1,0},{2,3},{3,2},{4,5},{5,4},{6,7},{7,6},{8,9},{9,8},{10,11... | collective-permute-start | bytes 552968 | tf_op jit(solution)/shard_map/ppermute | solution.py:1010
  26.2 19.6 %collective-permute-start.3 = (bf16[960,384]{1,0:T(8,128)(2,1)S(1)}, bf16[960,384]{1,0:T(8,128)(2,1)}, u32[]{:S(2)}, u32[]{:S(2)}) collective-permute-start(bf16[960,384]{1,0:T(8,128)(2,1)S(1)} %bitcast.22), channel_id=1, source_target_pairs={{0,8},{4,20},{8,0},{12,28},{16,24},{20,4},{24,16},{28,12},{1,9},{5... | collective-permute-start | bytes 2211848 | tf_op jit(solution)/shard_map/ppermute | solution.py:1004
  27.7 25.2 %collective-permute-start.4 = (bf16[960,384]{1,0:T(8,128)(2,1)S(1)}, bf16[960,384]{1,0:T(8,128)(2,1)}, u32[]{:S(2)}, u32[]{:S(2)}) collective-permute-start(bf16[960,384]{1,0:T(8,128)(2,1)S(1)} %bitcast.23), channel_id=1, source_target_pairs={{0,16},{4,12},{8,24},{12,4},{16,0},{20,28},{24,8},{28,20},{1,17},{... | collective-permute-start | bytes 2211848 | tf_op jit(solution)/shard_map/ppermute | solution.py:1004
  29.3 23.3 %collective-permute-start.11 = (bf16[368,640]{1,0:T(8,128)(2,1)S(1)}, bf16[368,640]{1,0:T(8,128)(2,1)S(1)}, u32[]{:S(2)}, u32[]{:S(2)}) collective-permute-start(bf16[368,640]{1,0:T(8,128)(2,1)S(1)} %pick.1.rest_4_.rest_0_), channel_id=1, source_target_pairs={{0,2},{1,3},{2,0},{3,1},{4,6},{5,7},{6,4},{7,5},{8,10},{9,11},{10,... | collective-permute-start | bytes 1413128 | tf_op jit(solution)/shard_map/ppermute | solution.py:1010
  32.5 20.5 %collective-permute-start.10 = (bf16[368,640]{1,0:T(8,128)(2,1)S(1)}, bf16[368,640]{1,0:T(8,128)(2,1)S(1)}, u32[]{:S(2)}, u32[]{:S(2)}) collective-permute-start(bf16[368,640]{1,0:T(8,128)(2,1)S(1)} %pick.1.rest_4_.rest_0_), channel_id=1, source_target_pairs={{0,1},{1,0},{2,3},{3,2},{4,5},{5,4},{6,7},{7,6},{8,9},{9,8},{10,11... | collective-permute-start | bytes 1413128 | tf_op jit(solution)/shard_map/ppermute | solution.py:1010
  45.7 18.6 %collective-permute-start.5 = (bf16[960,384]{1,0:T(8,128)(2,1)}, bf16[960,384]{1,0:T(8,128)(2,1)S(1)}, u32[]{:S(2)}, u32[]{:S(2)}) collective-permute-start(bf16[960,384]{1,0:T(8,128)(2,1)} %collective-permute-done.3.refs_1_.rest_1_), channel_id=1, source_target_pairs={{0,16},{4,12},{8,24},{12,4},{16,0},{20,28},{24,8},{28,20},{1,17},{... | collective-permute-start | bytes 2211848 | tf_op jit(solution)/shard_map/ppermute | solution.py:1004
  52.9 11.4 %collective-permute-start.12 = (bf16[368,640]{1,0:T(8,128)(2,1)S(1)}, bf16[368,640]{1,0:T(8,128)(2,1)S(1)}, u32[]{:S(2)}, u32[]{:S(2)}) collective-permute-start(bf16[368,640]{1,0:T(8,128)(2,1)S(1)} %hold.4.rest_2_), channel_id=1, source_target_pairs={{0,1},{1,0},{2,3},{3,2},{4,5},{5,4},{6,7},{7,6},{8,9},{9,8},{10,11... | collective-permute-start | bytes 1413128 | tf_op jit(solution)/shard_map/ppermute | solution.py:1010
  67.3 41.3 %collective-permute-start.16 = (bf16[4,368,640]{2,1,0:T(8,128)(2,1)}, bf16[4,368,640]{2,1,0:T(8,128)(2,1)S(1)}, u32[]{:S(2)}, u32[]{:S(2)}) collective-permute-start(bf16[4,368,640]{2,1,0:T(8,128)(2,1)} %stack.31.rest_8_), channel_id=1, source_target_pairs={{0,16},{4,12},{8,24},{12,4},{16,0},{20,28},{24,8},{28,20},{1,17},{... | collective-permute-start | bytes 5652488 | tf_op jit(solution)/shard_map/ppermute | solution.py:1004
  67.9 40.7 %collective-permute-start.13 = (bf16[4,368,640]{2,1,0:T(8,128)(2,1)}, bf16[4,368,640]{2,1,0:T(8,128)(2,1)}, u32[]{:S(2)}, u32[]{:S(2)}) collective-permute-start(bf16[4,368,640]{2,1,0:T(8,128)(2,1)} %stack.31.rest_8_), channel_id=1, source_target_pairs={{0,8},{4,20},{8,0},{12,28},{16,24},{20,4},{24,16},{28,12},{1,9},{5... | collective-permute-start | bytes 5652488 | tf_op jit(solution)/shard_map/ppermute | solution.py:1004
  68.4 11.2 %collective-permute-start.6 = (bf16[960,384]{1,0:T(8,128)(2,1)S(1)}, bf16[960,384]{1,0:T(8,128)(2,1)S(1)}, u32[]{:S(2)}, u32[]{:S(2)}) collective-permute-start(bf16[960,384]{1,0:T(8,128)(2,1)S(1)} %bitcast.24), channel_id=1, source_target_pairs={{0,4},{4,0},{8,12},{12,8},{16,20},{20,16},{24,28},{28,24},{1,5},{5... | collective-permute-start | bytes 2211848 | tf_op jit(solution)/shard_map/ppermute | solution.py:1004
  68.5 5.3 %collective-permute-start.14 = (bf16[976,256]{1,0:T(8,128)(2,1)S(1)}, bf16[976,256]{1,0:T(8,128)(2,1)S(1)}, u32[]{:S(2)}, u32[]{:S(2)}) collective-permute-start(bf16[976,256]{1,0:T(8,128)(2,1)S(1)} %pad_maximum_fusion), channel_id=1, source_target_pairs={{0,0},{1,4},{2,1},{3,5},{4,2},{5,6},{6,3},{7,7},{8,8},{9,12},{10,9... | collective-permute-start | bytes 1499144 | tf_op jit(solution)/shard_map/ppermute | solution.py:1021
  69.2 14.1 %collective-permute-start.8 = (bf16[960,384]{1,0:T(8,128)(2,1)}, bf16[960,384]{1,0:T(8,128)(2,1)}, u32[]{:S(2)}, u32[]{:S(2)}) collective-permute-start(bf16[960,384]{1,0:T(8,128)(2,1)} %collective-permute-done.4.refs_2_.rest_2_), channel_id=1, source_target_pairs={{0,4},{4,0},{8,12},{12,8},{16,20},{20,16},{24,28},{28,24},{1,5},{5... | collective-permute-start | bytes 2211848 | tf_op jit(solution)/shard_map/ppermute | solution.py:1004
  73.8 9.5 %collective-permute-start.7 = (bf16[960,384]{1,0:T(8,128)(2,1)}, bf16[960,384]{1,0:T(8,128)(2,1)}, u32[]{:S(2)}, u32[]{:S(2)}) collective-permute-start(bf16[960,384]{1,0:T(8,128)(2,1)} %collective-permute-done.3.refs_1_.rest_1_), channel_id=1, source_target_pairs={{0,4},{4,0},{8,12},{12,8},{16,20},{20,16},{24,28},{28,24},{1,5},{5... | collective-permute-start | bytes 2211848 | tf_op jit(solution)/shard_map/ppermute | solution.py:1004
  90.8 17.1 %collective-permute-start.15 = (bf16[656,256]{1,0:T(8,128)(2,1)}, bf16[656,256]{1,0:T(8,128)(2,1)S(1)}, u32[]{:S(2)}, u32[]{:S(2)}) collective-permute-start(bf16[656,256]{1,0:T(8,128)(2,1)} %get-tuple-element.128.kv2.rest_16_), channel_id=1, source_target_pairs={{0,1},{2,3},{4,5},{6,7},{8,9},{10,11},{12,13},{14,15},{16,17},{18,... | collective-permute-start | bytes 1007624 | tf_op jit(solution)/shard_map/ppermute | solution.py:1043
  108.6 24.1 %collective-permute-start.17 = (bf16[4,368,640]{2,1,0:T(8,128)(2,1)}, bf16[4,368,640]{2,1,0:T(8,128)(2,1)}, u32[]{:S(2)}, u32[]{:S(2)}) collective-permute-start(bf16[4,368,640]{2,1,0:T(8,128)(2,1)} %hold.5.rest_9_), channel_id=1, source_target_pairs={{0,16},{4,12},{8,24},{12,4},{16,0},{20,28},{24,8},{28,20},{1,17},{... | collective-permute-start | bytes 5652488 | tf_op jit(solution)/shard_map/ppermute | solution.py:1004
  109.2 23.6 %collective-permute-start.19 = (bf16[4,368,640]{2,1,0:T(8,128)(2,1)}, bf16[4,368,640]{2,1,0:T(8,128)(2,1)S(1)}, u32[]{:S(2)}, u32[]{:S(2)}) collective-permute-start(bf16[4,368,640]{2,1,0:T(8,128)(2,1)} %stack.31.rest_8_), channel_id=1, source_target_pairs={{0,4},{4,0},{8,12},{12,8},{16,20},{20,16},{24,28},{28,24},{1,5},{5... | collective-permute-start | bytes 5652488 | tf_op jit(solution)/shard_map/ppermute | solution.py:1004
  121.0 13.2 %collective-permute-start.20 = (bf16[4,368,640]{2,1,0:T(8,128)(2,1)}, bf16[4,368,640]{2,1,0:T(8,128)(2,1)}, u32[]{:S(2)}, u32[]{:S(2)}) collective-permute-start(bf16[4,368,640]{2,1,0:T(8,128)(2,1)} %hold.5.rest_9_), channel_id=1, source_target_pairs={{0,4},{4,0},{8,12},{12,8},{16,20},{20,16},{24,28},{28,24},{1,5},{5... | collective-permute-start | bytes 5652488 | tf_op jit(solution)/shard_map/ppermute | solution.py:1004
  121.2 11.6 %collective-permute-start.21 = (bf16[4,368,640]{2,1,0:T(8,128)(2,1)S(1)}, bf16[4,368,640]{2,1,0:T(8,128)(2,1)S(1)}, u32[]{:S(2)}, u32[]{:S(2)}) collective-permute-start(bf16[4,368,640]{2,1,0:T(8,128)(2,1)S(1)} %collective-permute-done.16.refs_2_.rest_10_), channel_id=1, source_target_pairs={{0,4},{4,0},{8,12},{12,8},{16,20},{20,16},{24,28},{28,24},{1,5},{5... | collective-permute-start | bytes 5652488 | tf_op jit(solution)/shard_map/ppermute | solution.py:1004
  132.8 4.2 collective-permute-start.22
  154.9 15.2 %collective-permute-start.29 = (bf16[256,2560]{1,0:T(8,128)(2,1)}, bf16[256,2560]{1,0:T(8,128)(2,1)S(1)}, u32[]{:S(2)}, u32[]{:S(2)}) collective-permute-start(bf16[256,2560]{1,0:T(8,128)(2,1)} %get-tuple-element.137.rest_5_), channel_id=1, source_target_pairs={{0,4},{4,0},{8,12},{12,8},{16,20},{20,16},{24,28},{28,24},{1,5},{5... | collective-permute-start | bytes 3932168 | tf_op jit(solution)/shard_map/ppermute | solution.py:1004
  155.1 12.2 %collective-permute-start.24 = (bf16[656,256]{1,0:T(8,128)(2,1)}, bf16[656,256]{1,0:T(8,128)(2,1)S(1)}, u32[]{:S(2)}, u32[]{:S(2)}) collective-permute-start(bf16[656,256]{1,0:T(8,128)(2,1)} %get-tuple-element.133.kv2.rest_16_), channel_id=1, source_target_pairs={{0,1},{2,3},{4,5},{6,7},{8,9},{10,11},{12,13},{14,15},{16,17},{18,... | collective-permute-start | bytes 1007624 | tf_op jit(solution)/shard_map/ppermute | solution.py:1043
  158.8 9.5 %collective-permute-start.26 = (bf16[256,960]{1,0:T(8,128)(2,1)S(1)}, bf16[256,960]{1,0:T(8,128)(2,1)S(1)}, u32[]{:S(2)}, u32[]{:S(2)}) collective-permute-start(bf16[256,960]{1,0:T(8,128)(2,1)S(1)} %copy-done.68), channel_id=1, source_target_pairs={{0,4},{4,0},{8,12},{12,8},{16,20},{20,16},{24,28},{28,24},{1,5},{5... | collective-permute-start | bytes 1474568 | tf_op jit(solution)/shard_map/ppermute | solution.py:1004
  158.9 23.7 %collective-permute-start.23 = (bf16[960,256]{1,0:T(8,128)(2,1)S(1)}, bf16[960,256]{1,0:T(8,128)(2,1)S(1)}, u32[]{:S(2)}, u32[]{:S(2)}) collective-permute-start(bf16[960,256]{1,0:T(8,128)(2,1)S(1)} %bitcast.39), channel_id=1, source_target_pairs={{0,0},{1,4},{2,1},{3,5},{4,2},{5,6},{6,3},{7,7},{8,8},{9,12},{10,9... | collective-permute-start | bytes 1474568 | tf_op jit(solution)/shard_map/ppermute | solution.py:1021
  159.6 8.8 %collective-permute-start.27 = (bf16[256,960]{1,0:T(8,128)(2,1)}, bf16[256,960]{1,0:T(8,128)(2,1)S(1)}, u32[]{:S(2)}, u32[]{:S(2)}) collective-permute-start(bf16[256,960]{1,0:T(8,128)(2,1)} %get-tuple-element.135.rest_1_), channel_id=1, source_target_pairs={{0,4},{4,0},{8,12},{12,8},{16,20},{20,16},{24,28},{28,24},{1,5},{5... | collective-permute-start | bytes 1474568 | tf_op jit(solution)/shard_map/ppermute | solution.py:1004
  168.4 66.8 %collective-permute-start.35 = (bf16[256,960]{1,0:T(8,128)(2,1)}, bf16[256,960]{1,0:T(8,128)(2,1)}, u32[]{:S(2)}, u32[]{:S(2)}) collective-permute-start(bf16[256,960]{1,0:T(8,128)(2,1)} %get-tuple-element.158.rest_0_), channel_id=1, source_target_pairs={{0,4},{4,0},{8,12},{12,8},{16,20},{20,16},{24,28},{28,24},{1,5},{5... | collective-permute-start | bytes 1474568 | tf_op jit(solution)/shard_map/ppermute | solution.py:1004
  218.6 31.6 %collective-permute-start.34 = (bf16[256,2560]{1,0:T(8,128)(2,1)}, bf16[256,2560]{1,0:T(8,128)(2,1)S(1)}, u32[]{:S(2)}, u32[]{:S(2)}) collective-permute-start(bf16[256,2560]{1,0:T(8,128)(2,1)} %get-tuple-element.157), channel_id=1, source_target_pairs={{0,4},{4,0},{8,12},{12,8},{16,20},{20,16},{24,28},{28,24},{1,5},{5... | collective-permute-start | bytes 3932168 | tf_op jit(solution)/shard_map/ppermute | solution.py:1004
  218.7 31.5 %collective-permute-start.38 = (bf16[256,2560]{1,0:T(8,128)(2,1)S(1)}, bf16[256,2560]{1,0:T(8,128)(2,1)S(1)}, u32[]{:S(2)}, u32[]{:S(2)}) collective-permute-start(bf16[256,2560]{1,0:T(8,128)(2,1)S(1)} %copy-done.71), channel_id=1, source_target_pairs={{0,4},{4,0},{8,12},{12,8},{16,20},{20,16},{24,28},{28,24},{1,5},{5... | collective-permute-start | bytes 3932168 | tf_op jit(solution)/shard_map/ppermute | solution.py:1004
  219.1 17.7 %collective-permute-start.36 = (bf16[256,960]{1,0:T(8,128)(2,1)}, bf16[256,960]{1,0:T(8,128)(2,1)S(1)}, u32[]{:S(2)}, u32[]{:S(2)}) collective-permute-start(bf16[256,960]{1,0:T(8,128)(2,1)} %get-tuple-element.159.rest_0_), channel_id=1, source_target_pairs={{0,4},{4,0},{8,12},{12,8},{16,20},{20,16},{24,28},{28,24},{1,5},{5... | collective-permute-start | bytes 1474568 | tf_op jit(solution)/shard_map/ppermute | solution.py:1004
  236.5 3.0 collective-permute-start.32
  238.2 11.9 %collective-permute-start.31 = (bf16[640,256]{1,0:T(8,128)(2,1)S(1)}, bf16[640,256]{1,0:T(8,128)(2,1)S(1)}, u32[]{:S(2)}, u32[]{:S(2)}) collective-permute-start(bf16[640,256]{1,0:T(8,128)(2,1)S(1)} %get-tuple-element.151), channel_id=1, source_target_pairs={{1,0},{3,2},{5,4},{7,6},{9,8},{11,10},{13,12},{15,14},{17,16},{19,... | collective-permute-start | bytes 983048 | tf_op jit(solution)/shard_map/ppermute | solution.py:1052
  272.7 3.3 collective-permute-start.40
  288.6 40.4 %collective-permute-start.46 = (bf16[2,960,640]{2,1,0:T(8,128)(2,1)}, bf16[2,960,640]{2,1,0:T(8,128)(2,1)S(1)}, u32[]{:S(2)}, u32[]{:S(2)}) collective-permute-start(bf16[2,960,640]{2,1,0:T(8,128)(2,1)} %get-tuple-element.192), channel_id=1, source_target_pairs={{0,8},{4,20},{8,0},{12,28},{16,24},{20,4},{24,16},{28,12},{1,9},{5... | collective-permute-start | bytes 7372808 | tf_op jit(solution)/shard_map/ppermute | solution.py:1004
  305.7 4.0 collective-permute-start.43
  308.4 12.9 %collective-permute-start.42 = (bf16[640,256]{1,0:T(8,128)(2,1)S(1)}, bf16[640,256]{1,0:T(8,128)(2,1)S(1)}, u32[]{:S(2)}, u32[]{:S(2)}) collective-permute-start(bf16[640,256]{1,0:T(8,128)(2,1)S(1)} %get-tuple-element.175), channel_id=1, source_target_pairs={{1,0},{3,2},{5,4},{7,6},{9,8},{11,10},{13,12},{15,14},{17,16},{19,... | collective-permute-start | bytes 983048 | tf_op jit(solution)/shard_map/ppermute | solution.py:1052
  318.7 30.0 %collective-permute-start.48 = (bf16[2,480,640]{2,1,0:T(8,128)(2,1)}, bf16[2,480,640]{2,1,0:T(8,128)(2,1)}, u32[]{:S(2)}, u32[]{:S(2)}) collective-permute-start(bf16[2,480,640]{2,1,0:T(8,128)(2,1)} %get-tuple-element.196), channel_id=1, source_target_pairs={{0,1},{1,0},{2,3},{3,2},{4,5},{5,4},{6,7},{7,6},{8,9},{9,8},{10,11... | collective-permute-start | bytes 3686408 | tf_op jit(solution)/shard_map/ppermute | solution.py:1010
  333.2 18.5 %collective-permute-start.47 = (bf16[960,640]{1,0:T(8,128)(2,1)}, bf16[960,640]{1,0:T(8,128)(2,1)S(1)}, u32[]{:S(2)}, u32[]{:S(2)}) collective-permute-start(bf16[960,640]{1,0:T(8,128)(2,1)} %get-tuple-element.194), channel_id=1, source_target_pairs={{0,16},{4,12},{8,24},{12,4},{16,0},{20,28},{24,8},{28,20},{1,17},{... | collective-permute-start | bytes 3686408 | tf_op jit(solution)/shard_map/ppermute | solution.py:1004
  345.8 22.3 %collective-permute-start.49 = (bf16[960,384]{1,0:T(8,128)(2,1)}, bf16[960,384]{1,0:T(8,128)(2,1)S(1)}, u32[]{:S(2)}, u32[]{:S(2)}) collective-permute-start(bf16[960,384]{1,0:T(8,128)(2,1)} %get-tuple-element.203), channel_id=1, source_target_pairs={{0,8},{4,20},{8,0},{12,28},{16,24},{20,4},{24,16},{28,12},{1,9},{5... | collective-permute-start | bytes 2211848 | tf_op jit(solution)/shard_map/ppermute | solution.py:1004
  346.4 21.8 %collective-permute-start.50 = (bf16[960,384]{1,0:T(8,128)(2,1)}, bf16[960,384]{1,0:T(8,128)(2,1)S(1)}, u32[]{:S(2)}, u32[]{:S(2)}) collective-permute-start(bf16[960,384]{1,0:T(8,128)(2,1)} %get-tuple-element.204), channel_id=1, source_target_pairs={{0,8},{4,20},{8,0},{12,28},{16,24},{20,4},{24,16},{28,12},{1,9},{5... | collective-permute-start | bytes 2211848 | tf_op jit(solution)/shard_map/ppermute | solution.py:1004
  354.1 28.7 %collective-permute-start.53 = (bf16[2,240,640]{2,1,0:T(8,128)(2,1)}, bf16[2,240,640]{2,1,0:T(8,128)(2,1)}, u32[]{:S(2)}, u32[]{:S(2)}) collective-permute-start(bf16[2,240,640]{2,1,0:T(8,128)(2,1)} %get-tuple-element.210), channel_id=1, source_target_pairs={{0,1},{1,0},{2,3},{3,2},{4,5},{5,4},{6,7},{7,6},{8,9},{9,8},{10,11... | collective-permute-start | bytes 1843208 | tf_op jit(solution)/shard_map/ppermute | solution.py:1010
  355.8 28.9 %collective-permute-start.55 = (bf16[480,640]{1,0:T(8,128)(2,1)}, bf16[480,640]{1,0:T(8,128)(2,1)S(1)}, u32[]{:S(2)}, u32[]{:S(2)}) collective-permute-start(bf16[480,640]{1,0:T(8,128)(2,1)} %get-tuple-element.216), channel_id=1, source_target_pairs={{0,2},{1,3},{2,0},{3,1},{4,6},{5,7},{6,4},{7,5},{8,10},{9,11},{10,... | collective-permute-start | bytes 1843208 | tf_op jit(solution)/shard_map/ppermute | solution.py:1010
  372.0 12.0 %collective-permute-start.51 = (bf16[480,384]{1,0:T(8,128)(2,1)S(1)}, bf16[480,384]{1,0:T(8,128)(2,1)S(1)}, u32[]{:S(2)}, u32[]{:S(2)}) collective-permute-start(bf16[480,384]{1,0:T(8,128)(2,1)S(1)} %get-tuple-element.207), channel_id=1, source_target_pairs={{0,16},{4,12},{8,24},{12,4},{16,0},{20,28},{24,8},{28,20},{1,17},{... | collective-permute-start | bytes 1105928 | tf_op jit(solution)/shard_map/ppermute | solution.py:1004
  373.5 10.5 %collective-permute-start.52 = (bf16[480,384]{1,0:T(8,128)(2,1)S(1)}, bf16[480,384]{1,0:T(8,128)(2,1)S(1)}, u32[]{:S(2)}, u32[]{:S(2)}) collective-permute-start(bf16[480,384]{1,0:T(8,128)(2,1)S(1)} %get-tuple-element.208), channel_id=1, source_target_pairs={{0,16},{4,12},{8,24},{12,4},{16,0},{20,28},{24,8},{28,20},{1,17},{... | collective-permute-start | bytes 1105928 | tf_op jit(solution)/shard_map/ppermute | solution.py:1004
  385.5 6.9 %collective-permute-start.56 = (bf16[2,120,640]{2,1,0:T(8,128)(2,1)S(1)}, bf16[2,120,640]{2,1,0:T(8,128)(2,1)S(1)}, u32[]{:S(2)}, u32[]{:S(2)}) collective-permute-start(bf16[2,120,640]{2,1,0:T(8,128)(2,1)S(1)} %get-tuple-element.219), channel_id=1, source_target_pairs={{0,8},{4,20},{8,0},{12,28},{16,24},{20,4},{24,16},{28,12},{1,9},{5... | collective-permute-start | bytes 921608 | tf_op jit(solution)/shard_map/ppermute | solution.py:1004
  387.1 15.6 %collective-permute-start.54 = (bf16[2,240,384]{2,1,0:T(8,128)(2,1)S(1)}, bf16[2,240,384]{2,1,0:T(8,128)(2,1)S(1)}, u32[]{:S(2)}, u32[]{:S(2)}) collective-permute-start(bf16[2,240,384]{2,1,0:T(8,128)(2,1)S(1)} %get-tuple-element.214), channel_id=1, source_target_pairs={{0,1},{1,0},{2,3},{3,2},{4,5},{5,4},{6,7},{7,6},{8,9},{9,8},{10,11... | collective-permute-start | bytes 1105928 | tf_op jit(solution)/shard_map/ppermute | solution.py:1010
  389.6 16.3 %collective-permute-start.59 = (bf16[240,640]{1,0:T(8,128)(2,1)S(1)}, bf16[240,640]{1,0:T(8,128)(2,1)S(1)}, u32[]{:S(2)}, u32[]{:S(2)}) collective-permute-start(bf16[240,640]{1,0:T(8,128)(2,1)S(1)} %get-tuple-element.226), channel_id=1, source_target_pairs={{0,2},{1,3},{2,0},{3,1},{4,6},{5,7},{6,4},{7,5},{8,10},{9,11},{10,... | collective-permute-start | bytes 921608 | tf_op jit(solution)/shard_map/ppermute | solution.py:1010
  393.1 12.8 %collective-permute-start.60 = (bf16[120,640]{1,0:T(8,128)(2,1)S(1)}, bf16[120,640]{1,0:T(8,128)(2,1)S(1)}, u32[]{:S(2)}, u32[]{:S(2)}) collective-permute-start(bf16[120,640]{1,0:T(8,128)(2,1)S(1)} %get-tuple-element.228), channel_id=1, source_target_pairs={{0,16},{4,12},{8,24},{12,4},{16,0},{20,28},{24,8},{28,20},{1,17},{... | collective-permute-start | bytes 460808 | tf_op jit(solution)/shard_map/ppermute | solution.py:1004
  403.3 11.5 %collective-permute-start.58 = (bf16[240,384]{1,0:T(8,128)(2,1)S(1)}, bf16[240,384]{1,0:T(8,128)(2,1)S(1)}, u32[]{:S(2)}, u32[]{:S(2)}) collective-permute-start(bf16[240,384]{1,0:T(8,128)(2,1)S(1)} %get-tuple-element.224), channel_id=1, source_target_pairs={{0,2},{1,3},{2,0},{3,1},{4,6},{5,7},{6,4},{7,5},{8,10},{9,11},{10,... | collective-permute-start | bytes 552968 | tf_op jit(solution)/shard_map/ppermute | solution.py:1010
  405.1 42.6 %collective-permute-start.57 = (bf16[1920,256]{1,0:T(8,128)(2,1)S(1)}, bf16[1920,256]{1,0:T(8,128)(2,1)S(1)}, u32[]{:S(2)}, u32[]{:S(2)}) collective-permute-start(bf16[1920,256]{1,0:T(8,128)(2,1)S(1)} %hold.7), channel_id=1, source_target_pairs={{0,0},{4,1},{1,2},{5,3},{2,4},{6,5},{3,6},{7,7},{8,8},{12,9},{9,10... | collective-permute-start | bytes 2949128 | tf_op jit(solution)/shard_map/ppermute | solution.py:1021
  406.5 9.4 %collective-permute-start.61 = (bf16[360,640]{1,0:T(8,128)(2,1)S(1)}, bf16[360,640]{1,0:T(8,128)(2,1)S(1)}, u32[]{:S(2)}, u32[]{:S(2)}) collective-permute-start(bf16[360,640]{1,0:T(8,128)(2,1)S(1)} %get-tuple-element.230.refs_1_), channel_id=1, source_target_pairs={{0,8},{4,20},{8,0},{12,28},{16,24},{20,4},{24,16},{28,12},{1,9},{5... | collective-permute-start | bytes 1382408 | tf_op jit(solution)/shard_map/ppermute | solution.py:1004
  408.0 18.2 %collective-permute-start.70 = (bf16[360,640]{1,0:T(8,128)(2,1)S(1)}, bf16[360,640]{1,0:T(8,128)(2,1)S(1)}, u32[]{:S(2)}, u32[]{:S(2)}) collective-permute-start(bf16[360,640]{1,0:T(8,128)(2,1)S(1)} %get-tuple-element.230.refs_1_), channel_id=1, source_target_pairs={{0,24},{4,28},{8,16},{12,20},{16,8},{20,12},{24,0},{28,4},{1,25},{... | collective-permute-start | bytes 1382408 | tf_op jit(solution)/shard_map/ppermute | solution.py:1004
  408.9 27.3 %collective-permute-start.69 = (bf16[360,640]{1,0:T(8,128)(2,1)S(1)}, bf16[360,640]{1,0:T(8,128)(2,1)S(1)}, u32[]{:S(2)}, u32[]{:S(2)}) collective-permute-start(bf16[360,640]{1,0:T(8,128)(2,1)S(1)} %get-tuple-element.230.refs_1_), channel_id=1, source_target_pairs={{0,16},{4,12},{8,24},{12,4},{16,0},{20,28},{24,8},{28,20},{1,17},{... | collective-permute-start | bytes 1382408 | tf_op jit(solution)/shard_map/ppermute | solution.py:1004
  414.9 21.4 %collective-permute-start.71 = (bf16[360,640]{1,0:T(8,128)(2,1)S(1)}, bf16[360,640]{1,0:T(8,128)(2,1)S(1)}, u32[]{:S(2)}, u32[]{:S(2)}) collective-permute-start(bf16[360,640]{1,0:T(8,128)(2,1)S(1)} %get-tuple-element.230.refs_1_), channel_id=1, source_target_pairs={{0,4},{4,0},{8,12},{12,8},{16,20},{20,16},{24,28},{28,24},{1,5},{5... | collective-permute-start | bytes 1382408 | tf_op jit(solution)/shard_map/ppermute | solution.py:1004
  416.5 20.4 %collective-permute-start.64 = (bf16[240,384]{1,0:T(8,128)(2,1)S(1)}, bf16[240,384]{1,0:T(8,128)(2,1)S(1)}, u32[]{:S(2)}, u32[]{:S(2)}) collective-permute-start(bf16[240,384]{1,0:T(8,128)(2,1)S(1)} %get-tuple-element.234.rest_0_), channel_id=1, source_target_pairs={{0,24},{4,28},{8,16},{12,20},{16,8},{20,12},{24,0},{28,4},{1,25},{... | collective-permute-start | bytes 552968 | tf_op jit(solution)/shard_map/ppermute | solution.py:1004
  426.2 22.0 %collective-permute-start.74 = (bf16[360,640]{1,0:T(8,128)(2,1)S(1)}, bf16[360,640]{1,0:T(8,128)(2,1)S(1)}, u32[]{:S(2)}, u32[]{:S(2)}) collective-permute-start(bf16[360,640]{1,0:T(8,128)(2,1)S(1)} %collective-permute-done.70.refs_4_), channel_id=1, source_target_pairs={{0,4},{4,0},{8,12},{12,8},{16,20},{20,16},{24,28},{28,24},{1,5},{5... | collective-permute-start | bytes 1382408 | tf_op jit(solution)/shard_map/ppermute | solution.py:1004
  436.2 12.1 %collective-permute-start.73 = (bf16[360,640]{1,0:T(8,128)(2,1)S(1)}, bf16[360,640]{1,0:T(8,128)(2,1)S(1)}, u32[]{:S(2)}, u32[]{:S(2)}) collective-permute-start(bf16[360,640]{1,0:T(8,128)(2,1)S(1)} %collective-permute-done.69.refs_3_), channel_id=1, source_target_pairs={{0,4},{4,0},{8,12},{12,8},{16,20},{20,16},{24,28},{28,24},{1,5},{5... | collective-permute-start | bytes 1382408 | tf_op jit(solution)/shard_map/ppermute | solution.py:1004
  436.3 5.9 %collective-permute-start.63 = (bf16[240,384]{1,0:T(8,128)(2,1)S(1)}, bf16[240,384]{1,0:T(8,128)(2,1)S(1)}, u32[]{:S(2)}, u32[]{:S(2)}) collective-permute-start(bf16[240,384]{1,0:T(8,128)(2,1)S(1)} %get-tuple-element.234.rest_0_), channel_id=1, source_target_pairs={{0,16},{4,12},{8,24},{12,4},{16,0},{20,28},{24,8},{28,20},{1,17},{... | collective-permute-start | bytes 552968 | tf_op jit(solution)/shard_map/ppermute | solution.py:1004
  436.9 13.5 %collective-permute-start.72 = (bf16[360,640]{1,0:T(8,128)(2,1)S(1)}, bf16[360,640]{1,0:T(8,128)(2,1)S(1)}, u32[]{:S(2)}, u32[]{:S(2)}) collective-permute-start(bf16[360,640]{1,0:T(8,128)(2,1)S(1)} %collective-permute-done.61.refs_4_.refs_2_), channel_id=1, source_target_pairs={{0,4},{4,0},{8,12},{12,8},{16,20},{20,16},{24,28},{28,24},{1,5},{5... | collective-permute-start | bytes 1382408 | tf_op jit(solution)/shard_map/ppermute | solution.py:1004
  442.2 5.5 %collective-permute-start.62 = (bf16[240,384]{1,0:T(8,128)(2,1)S(1)}, bf16[240,384]{1,0:T(8,128)(2,1)S(1)}, u32[]{:S(2)}, u32[]{:S(2)}) collective-permute-start(bf16[240,384]{1,0:T(8,128)(2,1)S(1)} %get-tuple-element.234.rest_0_), channel_id=1, source_target_pairs={{0,8},{4,20},{8,0},{12,28},{16,24},{20,4},{24,16},{28,12},{1,9},{5... | collective-permute-start | bytes 552968 | tf_op jit(solution)/shard_map/ppermute | solution.py:1004
  447.7 7.0 %collective-permute-start.65 = (bf16[240,384]{1,0:T(8,128)(2,1)S(1)}, bf16[240,384]{1,0:T(8,128)(2,1)S(1)}, u32[]{:S(2)}, u32[]{:S(2)}) collective-permute-start(bf16[240,384]{1,0:T(8,128)(2,1)S(1)} %get-tuple-element.234.rest_0_), channel_id=1, source_target_pairs={{0,4},{4,0},{8,12},{12,8},{16,20},{20,16},{24,28},{28,24},{1,5},{5... | collective-permute-start | bytes 552968 | tf_op jit(solution)/shard_map/ppermute | solution.py:1004
  447.7 7.0 %collective-permute-start.68 = (bf16[240,384]{1,0:T(8,128)(2,1)S(1)}, bf16[240,384]{1,0:T(8,128)(2,1)S(1)}, u32[]{:S(2)}, u32[]{:S(2)}) collective-permute-start(bf16[240,384]{1,0:T(8,128)(2,1)S(1)} %collective-permute-done.64.rest_3_), channel_id=1, source_target_pairs={{0,4},{4,0},{8,12},{12,8},{16,20},{20,16},{24,28},{28,24},{1,5},{5... | collective-permute-start | bytes 552968 | tf_op jit(solution)/shard_map/ppermute | solution.py:1004
  448.2 6.5 %collective-permute-start.67 = (bf16[240,384]{1,0:T(8,128)(2,1)S(1)}, bf16[240,384]{1,0:T(8,128)(2,1)S(1)}, u32[]{:S(2)}, u32[]{:S(2)}) collective-permute-start(bf16[240,384]{1,0:T(8,128)(2,1)S(1)} %collective-permute-done.63.rest_2_), channel_id=1, source_target_pairs={{0,4},{4,0},{8,12},{12,8},{16,20},{20,16},{24,28},{28,24},{1,5},{5... | collective-permute-start | bytes 552968 | tf_op jit(solution)/shard_map/ppermute | solution.py:1004
  448.3 6.4 %collective-permute-start.66 = (bf16[240,384]{1,0:T(8,128)(2,1)S(1)}, bf16[240,384]{1,0:T(8,128)(2,1)S(1)}, u32[]{:S(2)}, u32[]{:S(2)}) collective-permute-start(bf16[240,384]{1,0:T(8,128)(2,1)S(1)} %collective-permute-done.62.rest_1_), channel_id=1, source_target_pairs={{0,4},{4,0},{8,12},{12,8},{16,20},{20,16},{24,28},{28,24},{1,5},{5... | collective-permute-start | bytes 552968 | tf_op jit(solution)/shard_map/ppermute | solution.py:1004
  (96 other events, 800.4 us)
